TPU v7x, 32 devices: a whole 2x2x4 slice. The times are simulated.
32 devices in a mesh: groups: 2 (over x), inst: 4 (over y, core), tp: 4 (over z).
Axes of the slice: x: 2, y: 2, z: 4, core: 2. Of those that a mesh axis runs over, the one named last changes fastest.
Arguments:
- kv_cache: bfloat16 [384, 2, 256, 512], P(('groups', 'inst'), None, None, 'tp'), parts along dimension 0, may hold values from -110 to 110
- hidden: bfloat16 [384, 4096], P(('groups', 'inst')), parts along dimension 0, may hold values from -18 to 18
- lengths: int32 [384], P('groups'), parts along dimension 0, may hold values from 1 to 254, as said below
- source: int32 [384], P('groups'), parts along dimension 0, may hold values from 0 to 191, as said below
- norm_gain: float32 [4096], replicated, may hold values from 0.1 to 1.9
- query_weight: bfloat16 [4096, 2048], P(None, 'tp'), may hold values from -0.09375 to 0.09375
- keyval_weight: bfloat16 [4096, 2, 512], P(None, None, 'tp'), may hold values from -0.09375 to 0.09375
- out_weight: bfloat16 [2048, 4096], P('tp'), may hold values from -0.125 to 0.125
Outputs:
- final_hidden: bfloat16 [384, 4096], P(('groups', 'inst')), parts along dimension 0
- final_cache: bfloat16 [384, 2, 256, 512], P(('groups', 'inst'), None, None, 'tp'), parts along dimension 0
There are 2 independent parts, one for each index of `groups`. A program takes and returns all parts, laid end to end along the dimension named above; an argument that names none is the same for every part. Nothing has to cross between parts.
Inputs may be any that keep to these rules, and one draw needn't show every extreme that they name: `source`: A permutation of the slots. In each instance exactly 4 slots take a request from another instance; from one instance to another exactly 2 requests move or none; the other slots keep their own request. `lengths`: positions from a slot's length on hold stale entries.
All inputs are finite; a program needn't handle non-finite values.
Results may differ from a plain program's by a relative error of at most 0.012.
The roundings to bfloat16 on the way count: a program that leaves them out, or rounds other values in their place, can miss the bound.
Values may be sent and summed in bfloat16 or wider, within the bound.
No kernel may reach another device: no remote copies, remote signals or barrier semaphores. Data moves between devices by JAX's collectives and lax.ppermute only.
A program may use at most 128 MiB of HBM per device.

v0:
```python
import jax
import jax.numpy as jnp
from jax import lax
from jax.sharding import PartitionSpec as P

MOVE = 2


EPS = 1e-05
THETA = 500000.0


def rotate(inputs, position):
    halfway = inputs.shape[-1] // 2
    frequency = THETA ** (-(jnp.arange(halfway, dtype=jnp.float32) * 2.0) / inputs.shape[-1])
    angles = position.astype(jnp.float32)[:, None] * frequency[None, :]
    cosine = jnp.concatenate([jnp.cos(angles), jnp.cos(angles)], axis=-1)
    sine_part = jnp.concatenate([jnp.sin(angles), jnp.sin(angles)], axis=-1)
    target = (inputs.shape[0],) + (1,) * (inputs.ndim - 2) + (inputs.shape[-1],)
    cosine = cosine.reshape(target)
    sine_part = sine_part.reshape(target)
    turned = jnp.concatenate([-inputs[..., halfway:], inputs[..., :halfway]], axis=-1)
    return inputs * cosine + turned * sine_part


def write_rows(stored, new_rows, position):
    placed = (jnp.arange(stored.shape[2], dtype=jnp.int32)[None, :] == position[:, None])[
        :, None, :, None
    ]
    return jnp.where(placed, new_rows[:, :, None, :], stored)


def decode_step(current, stored, position, norm_gain, query_weight, keyval_weight):
    batch_rows = current.shape[0]
    head_dim = stored.shape[-1]
    model_width = current.shape[1]
    widened = current.astype(jnp.float32)
    normed = (
        widened * lax.rsqrt(jnp.mean(widened * widened, axis=-1, keepdims=True) + EPS) * norm_gain
    ).astype(jnp.bfloat16)
    queries = jnp.dot(normed, query_weight, preferred_element_type=jnp.float32).reshape(
        batch_rows, -1, head_dim
    )
    queries = rotate(queries, position).astype(jnp.bfloat16)
    new_rows = jnp.dot(
        normed, keyval_weight.reshape(model_width, 2 * head_dim), preferred_element_type=jnp.float32
    )
    new_rows = new_rows.reshape(batch_rows, 2, head_dim)
    new_rows = jnp.stack([rotate(new_rows[:, 0], position), new_rows[:, 1]], axis=1).astype(
        jnp.bfloat16
    )
    stored = write_rows(stored, new_rows, position)
    scores = jnp.einsum(
        "sjd,scd->sjc", queries, stored[:, 0], preferred_element_type=jnp.float32
    ) * head_dim ** (-0.5)
    visible = (jnp.arange(stored.shape[2], dtype=jnp.int32)[None, :] <= position[:, None])[
        :, None, :
    ]
    scores = jnp.where(visible, scores, -jnp.inf)
    highest = jnp.max(scores, axis=-1, keepdims=True)
    weight = jnp.exp(scores - highest)
    weight16 = (weight / jnp.sum(weight, axis=-1, keepdims=True)).astype(jnp.bfloat16)
    attended = jnp.einsum(
        "sjc,scd->sjd", weight16, stored[:, 1], preferred_element_type=jnp.float32
    )
    attended = attended.astype(jnp.bfloat16).reshape(batch_rows, -1)
    return (widened, attended, stored, new_rows)


def finish(widened, attended, out_weight):
    head_part = jnp.dot(attended, out_weight, preferred_element_type=jnp.float32)
    summed = lax.psum(head_part, "tp")
    return (widened + summed).astype(jnp.bfloat16)


def migration_plan(source, lengths, myself, slot_count, peers, per_pair):
    requests = source.shape[0]
    ordinal = jnp.arange(requests, dtype=jnp.int32)
    destination = jnp.zeros((requests,), jnp.int32).at[source].set(ordinal)
    slot_ids = jnp.arange(slot_count, dtype=jnp.int32)
    my_destination = lax.dynamic_slice_in_dim(destination, myself * slot_count, slot_count)
    my_source = lax.dynamic_slice_in_dim(source, myself * slot_count, slot_count)
    goes_to = my_destination // slot_count
    leaving = goes_to != myself
    earlier = (goes_to[None, :] == goes_to[:, None]) & (
        my_destination[None, :] < my_destination[:, None]
    )
    send_row = goes_to * per_pair + jnp.sum(earlier.astype(jnp.int32), axis=1)
    packet_rows = jnp.arange(peers * per_pair, dtype=jnp.int32)
    packing = ((packet_rows[:, None] == send_row[None, :]) & leaving[None, :]).astype(jnp.bfloat16)
    comes_from = my_source // slot_count
    arriving = comes_from != myself
    before = (comes_from[None, :] == comes_from[:, None]) & (slot_ids[None, :] < slot_ids[:, None])
    receive_row = comes_from * per_pair + jnp.sum(before.astype(jnp.int32), axis=1)
    taking = ((receive_row[:, None] == packet_rows[None, :]) & arriving[:, None]).astype(
        jnp.bfloat16
    )
    keeping = (
        ((my_source - myself * slot_count)[:, None] == slot_ids[None, :]) & ~arriving[:, None]
    ).astype(jnp.bfloat16)
    new_lengths = jnp.take(lengths, my_source, axis=0)
    old_lengths = lax.dynamic_slice_in_dim(lengths, myself * slot_count, slot_count)
    return (packing, taking, keeping, new_lengths, old_lengths)


def select_rows(matrix, rows_in):
    return jnp.dot(matrix, rows_in, preferred_element_type=jnp.float32).astype(jnp.bfloat16)


def relocate(keeping, taking, own_rows, got_rows):
    kept = jnp.dot(keeping, own_rows, preferred_element_type=jnp.float32)
    return (kept + jnp.dot(taking, got_rows, preferred_element_type=jnp.float32)).astype(
        jnp.bfloat16
    )


def local(kv_cache, hidden, lengths, source, norm_gain, query_weight, keyval_weight, out_weight):
    peers = lax.axis_size("inst")
    myself = lax.axis_index("inst")
    slot_count = kv_cache.shape[0]
    packing, taking, keeping, new_lengths, old_lengths = migration_plan(
        source, lengths, myself, slot_count, peers, MOVE
    )
    flat_cache = kv_cache.reshape(slot_count, -1)
    got_cache = lax.all_to_all(
        select_rows(packing, flat_cache), "inst", split_axis=0, concat_axis=0, tiled=True
    )
    widened, attended, scratch, new_rows = decode_step(
        hidden, kv_cache, old_lengths, norm_gain, query_weight, keyval_weight
    )
    current = finish(widened, attended, out_weight)
    flat_rows = new_rows.reshape(slot_count, -1)
    got_rows, got_hidden = (
        lax.all_to_all(
            select_rows(packing, flat_rows), "inst", split_axis=0, concat_axis=0, tiled=True
        ),
        lax.all_to_all(
            select_rows(packing, current), "inst", split_axis=0, concat_axis=0, tiled=True
        ),
    )
    stored = relocate(keeping, taking, flat_cache, got_cache).reshape(kv_cache.shape)
    moved_rows = relocate(keeping, taking, flat_rows, got_rows).reshape(new_rows.shape)
    stored = write_rows(stored, moved_rows, new_lengths)
    current = relocate(keeping, taking, current, got_hidden)
    widened, attended, stored, new_rows = decode_step(
        current, stored, new_lengths + 1, norm_gain, query_weight, keyval_weight
    )
    current = finish(widened, attended, out_weight)
    return (current, stored)


def solution(mesh):
    return jax.shard_map(
        local,
        mesh=mesh,
        in_specs=(
            P(("groups", "inst"), None, None, "tp"),
            P(("groups", "inst"), None),
            P("groups"),
            P("groups"),
            P(),
            P(None, "tp"),
            P(None, None, "tp"),
            P("tp", None),
        ),
        out_specs=(P(("groups", "inst"), None), P(("groups", "inst"), None, None, "tp")),
        check_vma=False,
    )
```

profile of v0, /device:TPU:0, one launch (start us, length us, event | category | flops | bytes accessed | tf_op | source)
XLA Modules:
  0.0 184.5 jit_solution(13558886599698032985)
XLA Ops:
  7.2 0.0 all-reduce.3.cloned.1.call-start
  7.3 1.4 compare_select_fusion.1
  8.6 1.5 gather_fusion
  10.1 0.8 multiply_cosine_fusion
  10.9 0.8 multiply_cosine_fusion.2
  11.7 3.2 %copy.64 = bf16[512,8,2,128]{3,1,2,0:T(8,128)(2,1)} copy(bf16[512,8,2,128]{3,2,1,0:T(2,128)(2,1)} %bitcast.108) | data formatting | bytes 4194304
  14.9 2.9 %copy.21 = bf16[256,4096]{1,0:T(8,128)(2,1)S(1)} copy(bf16[256,4096]{0,1:T(8,128)(2,1)} %bitcast.107) | data formatting | bytes 4194304 | tf_op jit(solution)/shard_map/dot_general | solution.py:45
  17.8 0.2 fusion.28
  18.0 0.8 fusion.34
  18.8 0.1 fusion.61
  18.9 0.1 iota_compare_fusion.4
  18.9 0.1 pad_maximum_fusion
  19.0 0.1 pad_maximum_fusion.1
  19.1 3.1 %fusion.37 = f32[48,512]{1,0:T(8,128)S(1)} fusion(bf16[4096,512]{1,0:T(8,128)(2,1)} %param.13, bf16[48,4096]{1,0:T(8,128)(2,1)S(1)} %copy-done, f32[4096]{0:T(1024)S(1)} %copy-done.3, f32[48]{0:T(128)S(1)} %add_rsqrt_fusion.1), kind=kOutput, calls=%fused_computation.59 | convolution fusion | flops 202113024 | bytes 4702400 | tf_op jit(solution)/shard_map/dot_general | solution.py:41
  22.2 0.1 slice_negate_fusion.1
  22.3 0.1 fusion.62
  22.5 7.6 %copy_select_fusion.1 = bf16[48,2,256,128]{3,2,0,1:T(8,128)(2,1)} fusion(bf16[48,2,256,128]{3,2,1,0:T(8,128)(2,1)} %param.8, pred[48,256]{1,0:T(8,128)(4,1)S(1)} %get-tuple-element.44, bf16[48,2,128]{2,0,1:T(8,128)(2,1)S(1)} %maximum_convert_fusion), kind=kLoop, calls=%fused_computation.12 | loop fusion | flops 3145728 | bytes 12619776 | tf_op jit(solution)/shard_map/jit(_where)/select_n | solution.py:30
  30.0 3.0 %fusion.111 = (f32[48,4]{1,0:T(8,128)S(1)}, f32[48,4,256]{2,1,0:T(4,128)S(1)}) fusion(bf16[48,2,256,128]{3,2,0,1:T(8,128)(2,1)} %copy_select_fusion.1, pred[48,256]{1,0:T(8,128)(4,1)S(1)} %get-tuple-element.43, f32[48,4,64]{2,1,0:T(4,128)S(1)} %get-tuple-element.21, f32[48,4,64]{2,1,0:T(4,128)S(1)} %get-tuple-element.20, f32[48,4,128]{2,1,0:T(4,128)S(1)} %reshape.469, ...), kind=kOutput, calls=%fused_computation.173 | convolution fusion | flops 12902655 | bytes 3601152 | tf_op jit(solution)/shard_map/sub | solution.py:61
  33.1 2.5 %fusion.24 = bf16[48,4,128]{2,1,0:T(4,128)(2,1)S(1)} fusion(bf16[48,2,256,128]{3,2,0,1:T(8,128)(2,1)} %copy_select_fusion.1, f32[48,4,256]{2,1,0:T(4,128)S(1)} %get-tuple-element.46, f32[48,4]{1,0:T(8,128)S(1)} %get-tuple-element.45), kind=kOutput, calls=%fused_computation.40 | convolution fusion | flops 12705792 | bytes 3392256 | tf_op jit(solution)/shard_map/sjc,scd->sjd/dot_general | solution.py:63
  35.6 3.9 %fusion.50 = f32[48,4096]{1,0:T(8,128)} fusion(bf16[512,4096]{1,0:T(8,128)(2,1)} %param.15, bf16[6,8,4,128]{3,2,1,0:T(4,128)(2,1)S(1)} %bitcast.110), kind=kOutput, calls=%fused_computation.73 | convolution fusion | flops 201326592 | bytes 5029888 | tf_op jit(solution)/shard_map/dot_general | solution.py:71
  39.6 1.2 scatter_custom_fusion
  40.8 0.1 broadcast_compare_fusion
  40.9 0.2 convert_reduce_fusion
  41.1 0.1 convolution_convert_fusion.2
  41.2 0.6 all_to_all.27
  41.8 4.2 %all-to-all-start.1 = ((bf16[4,2,256]{2,1,0:T(2,128)(2,1)}), bf16[4,2,256]{2,1,0:T(2,128)(2,1)}, u32[]{:S(2)}, u32[]{:S(2)}) async-start(bf16[4,2,256]{2,1,0:T(2,128)(2,1)} %all_to_all.27), calls=%async_computation.1 | async-start | bytes 8192 | tf_op jit(solution)/shard_map/all_to_all | solution.py:134
  46.0 0.7 fusion.110
  46.7 0.7 iota_compare_fusion
  47.4 0.7 convert_reduce_fusion.1
  48.1 6.2 %convolution_convert_fusion = bf16[8,65536]{1,0:T(8,128)(2,1)S(1)} fusion(bf16[6,8,512,128]{3,2,1,0:T(8,128)(2,1)} %bitcast.102, s32[48]{0:T(128)} %copy-done.23, pred[48]{0:T(512)(128)(4,1)} %copy-done.19), kind=kOutput, calls=%fused_computation.6 | convolution fusion | flops 50856704 | bytes 7340272 | tf_op jit(solution)/shard_map/dot_general | solution.py:107
  54.3 0.7 iota_compare_fusion.2
  55.0 12.5 %fusion.4 = f32[48,65536]{1,0:T(8,128)} fusion(bf16[6,8,512,128]{3,2,1,0:T(8,128)(2,1)} %bitcast.103, s32[48]{0:T(128)} %get-tuple-element.32, pred[48]{0:T(512)(128)(4,1)S(1)} %get-tuple-element.15), kind=kOutput, calls=%fused_computation.8 | convolution fusion | flops 301994496 | bytes 18874608 | tf_op jit(solution)/shard_map/dot_general | solution.py:111
  67.5 0.7 pad_maximum_fusion.2
  68.2 0.7 pad_maximum_fusion.3
  68.8 1.6 all_to_all.30
  70.5 4.0 %all-to-all-start.2 = ((bf16[4,2,65536]{2,1,0:T(2,128)(2,1)}), bf16[4,2,65536]{2,1,0:T(2,128)(2,1)S(1)}, u32[]{:S(2)}, u32[]{:S(2)}) async-start(bf16[4,2,65536]{2,1,0:T(2,128)(2,1)} %all_to_all.30), calls=%async_computation.2 | async-start | bytes 2097152 | tf_op jit(solution)/shard_map/all_to_all | solution.py:125
  74.4 1.2 multiply_add_fusion.1
  75.6 1.5 fusion.58
  77.2 1.3 all_to_all.29
  78.4 1.0 fusion.27
  79.4 0.6 copy.65
  80.1 6.0 %all-reduce.3.cloned.1.call-done = f32[48,4096]{1,0:T(8,128)} async-done(((f32[48,4096]{1,0:T(8,128)}), f32[48,4096]{1,0:T(8,128)}) %all-reduce.3.cloned.1.call-update) | async-done | bytes 786448 | tf_op jit(solution)/shard_map/psum | solution.py:72
  86.1 2.0 %convolution_convert_fusion.1 = bf16[8,4096]{1,0:T(8,128)(2,1)} fusion(s32[48]{0:T(128)} %copy-done.23, pred[48]{0:T(512)(128)(4,1)} %copy-done.19, f32[48,4096]{1,0:T(8,128)} %all-reduce.3.cloned.1.call-done, bf16[48,4096]{1,0:T(8,128)(2,1)S(1)} %copy-done), kind=kOutput, calls=%fused_computation.18 | convolution fusion | flops 3769088 | bytes 1245424 | tf_op jit(solution)/shard_map/dot_general | solution.py:107
  88.0 1.5 all_to_all.24
  89.6 3.9 %all-to-all-start = ((bf16[4,2,4096]{2,1,0:T(2,128)(2,1)}), bf16[4,2,4096]{2,1,0:T(2,128)(2,1)}, u32[]{:S(2)}, u32[]{:S(2)}) async-start(bf16[4,2,4096]{2,1,0:T(2,128)(2,1)} %all_to_all.24), calls=%async_computation | async-start | bytes 131072 | tf_op jit(solution)/shard_map/all_to_all | solution.py:137
  93.5 0.3 all-reduce.5.cloned.1.call-start
  93.7 1.6 all_to_all.32
  95.4 6.5 %fusion.15 = bf16[6,8,512,128]{3,1,2,0:T(8,128)(2,1)S(1)} fusion(f32[48,65536]{1,0:T(8,128)} %fusion.4, bf16[8,65536]{1,0:T(8,128)(2,1)S(1)} %all_to_all.32, s32[48]{0:T(128)} %multiply_add_fusion.1, pred[48]{0:T(512)(128)(4,1)} %get-tuple-element.16), kind=kOutput, calls=%fused_computation.27 | convolution fusion | flops 56623872 | bytes 19923184 | tf_op jit(solution)/shard_map/dot_general | solution.py:112
  101.9 1.2 fusion.68
  103.1 4.3 %copy.32 = bf16[6,8,512,128]{3,2,1,0:T(8,128)(2,1)} copy(bf16[6,8,512,128]{3,1,2,0:T(8,128)(2,1)S(1)} %fusion.15) | data formatting | bytes 12582912
  107.5 0.9 all_to_all.26
  108.4 1.5 multiply_reduce_fusion
  110.0 0.8 fusion.32
  110.8 3.1 %fusion.108 = f32[48,512]{1,0:T(8,128)S(1)} fusion(bf16[4096,512]{1,0:T(8,128)(2,1)} %param.13, f32[48,4096]{1,0:T(8,128)S(1)} %get-tuple-element.48, f32[48]{0:T(128)S(1)} %add_rsqrt_fusion, f32[4096]{0:T(1024)S(1)} %copy-done.3), kind=kOutput, calls=%fused_computation.170 | convolution fusion | flops 201916416 | bytes 5095616 | tf_op jit(solution)/shard_map/dot_general | solution.py:41
  113.9 0.1 fusion.60
  114.0 0.1 slice_negate_fusion
  114.1 0.1 fusion.64
  114.3 6.6 %fusion.6 = bf16[48,2,256,128]{3,2,0,1:T(8,128)(2,1)} fusion(bf16[48,2,256,128]{3,2,1,0:T(8,128)(2,1)} %bitcast.104, pred[48,256]{1,0:T(8,128)(4,1)S(1)} %copy-done.11, pred[48,256]{1,0:T(8,128)(4,1)S(1)} %copy-done.12, bf16[48,2,128]{2,0,1:T(8,128)(2,1)S(1)} %bitcast.109, bf16[48,2,128]{2,0,1:T(8,128)(2,1)S(1)} %pad_maximum_fusion.4), kind=kLoop, calls=%fused_computation.11 | loop fusion | flops 6291456 | bytes 12656640 | tf_op jit(solution)/shard_map/jit(_where)/select_n | solution.py:30
  120.9 3.0 %fusion.112 = (f32[48,4]{1,0:T(8,128)S(1)}, f32[48,4,256]{2,1,0:T(4,128)S(1)}) fusion(bf16[48,2,256,128]{3,2,0,1:T(8,128)(2,1)} %fusion.6, pred[48,256]{1,0:T(8,128)(4,1)S(1)} %copy-done.15, f32[48,4,64]{2,1,0:T(4,128)S(1)} %get-tuple-element.19, f32[48,4,64]{2,1,0:T(4,128)S(1)} %get-tuple-element.18, f32[48,4,128]{2,1,0:T(4,128)S(1)} %reshape.472, ...), kind=kOutput, calls=%fused_computation.174 | convolution fusion | flops 12902655 | bytes 3601152 | tf_op jit(solution)/shard_map/sub | solution.py:61
  123.9 2.5 %fusion.25 = bf16[48,4,128]{2,1,0:T(4,128)(2,1)S(1)} fusion(bf16[48,2,256,128]{3,2,0,1:T(8,128)(2,1)} %fusion.6, f32[48,4,256]{2,1,0:T(4,128)S(1)} %get-tuple-element.50, f32[48,4]{1,0:T(8,128)S(1)} %get-tuple-element.49), kind=kOutput, calls=%fused_computation.41 | convolution fusion | flops 12705792 | bytes 3392256 | tf_op jit(solution)/shard_map/sjc,scd->sjd/dot_general | solution.py:63
  126.4 3.9 %fusion.47 = f32[48,4096]{1,0:T(8,128)} fusion(bf16[512,4096]{1,0:T(8,128)(2,1)} %param.15, bf16[6,8,4,128]{3,2,1,0:T(4,128)(2,1)S(1)} %bitcast.111), kind=kOutput, calls=%fused_computation.70 | convolution fusion | flops 201326592 | bytes 5029888 | tf_op jit(solution)/shard_map/dot_general | solution.py:71
  130.3 6.3 %copy.26 = bf16[48,2,256,128]{3,2,1,0:T(8,128)(2,1)} copy(bf16[48,2,256,128]{3,2,0,1:T(8,128)(2,1)} %fusion.6) | data formatting | bytes 12582912
  136.6 39.1 %all-reduce.5.cloned.1.call-done = f32[48,4096]{1,0:T(8,128)} async-done(((f32[48,4096]{1,0:T(8,128)}), f32[48,4096]{1,0:T(8,128)}) %all-reduce.5.cloned.1.call-update) | async-done | bytes 786448 | tf_op jit(solution)/shard_map/psum | solution.py:72
  175.7 1.9 %add_convert_fusion = bf16[48,4096]{1,0:T(8,128)(2,1)} fusion(f32[48,4096]{1,0:T(8,128)S(1)} %get-tuple-element.48, f32[48,4096]{1,0:T(8,128)} %all-reduce.5.cloned.1.call-done), kind=kLoop, calls=%fused_computation.50 | loop fusion | flops 393216 | bytes 1966080 | tf_op jit(solution)/shard_map/convert_element_type | solution.py:73
  (71 shorter events, 0.3 us)
Async XLA Ops:
  7.2 10.6 %copy-start = (bf16[48,4096]{1,0:T(8,128)(2,1)S(1)}, bf16[48,4096]{1,0:T(8,128)(2,1)}, u32[]{:S(2)}) copy-start(bf16[48,4096]{1,0:T(8,128)(2,1)} %param.9) | copy-start | bytes 1179652
  7.2 10.8 %copy-start.3 = (f32[4096]{0:T(1024)S(1)}, f32[4096]{0:T(1024)}, u32[]{:S(2)}) copy-start(f32[4096]{0:T(1024)} %param.12) | copy-start | bytes 49156
  7.2 78.9 %all-reduce.3.cloned.1.call-start = ((), (), s32[]{:S(2)}) async-start(), calls=%async_computation.3 | async-start | bytes 1572864 | tf_op jit(solution)/shard_map/psum | solution.py:72
  22.4 18.6 %copy-start.9 = (bf16[48,1,128]{2,0,1:T(8,128)(2,1)}, bf16[48,1,128]{2,0,1:T(8,128)(2,1)S(1)}, u32[]{:S(2)}) copy-start(bf16[48,1,128]{2,0,1:T(8,128)(2,1)S(1)} %get-tuple-element.22) | copy-start | bytes 36868
  22.5 18.6 %copy-start.10 = (bf16[48,1,128]{2,0,1:T(8,128)(2,1)}, bf16[48,1,128]{2,0,1:T(8,128)(2,1)S(1)}, u32[]{:S(2)}) copy-start(bf16[48,1,128]{2,0,1:T(8,128)(2,1)S(1)} %get-tuple-element.23) | copy-start | bytes 36868
  30.0 9.5 %copy-start.21 = (s32[192]{0:T(256)S(1)}, s32[192]{0:T(256)}, u32[]{:S(2)}) copy-start(s32[192]{0:T(256)} %param.11) | copy-start | bytes 2308
  40.8 7.2 %copy-start.19 = (pred[48]{0:T(512)(128)(4,1)}, pred[48]{0:T(512)(128)(4,1)S(1)}, u32[]{:S(2)}) copy-start(pred[48]{0:T(512)(128)(4,1)S(1)} %get-tuple-element.10) | copy-start | bytes 148
  41.0 7.0 %copy-start.23 = (s32[48]{0:T(128)}, s32[48]{0:T(128)S(1)}, u32[]{:S(2)}) copy-start(s32[48]{0:T(128)S(1)} %multiply_add_fusion) | copy-start | bytes 580
  41.8 28.7 %all-to-all-start.1 = ((bf16[4,2,256]{2,1,0:T(2,128)(2,1)}), bf16[4,2,256]{2,1,0:T(2,128)(2,1)}, u32[]{:S(2)}, u32[]{:S(2)}) async-start(bf16[4,2,256]{2,1,0:T(2,128)(2,1)} %all_to_all.27), calls=%async_computation.1 | async-start | bytes 8192 | tf_op jit(solution)/shard_map/all_to_all | solution.py:134
  46.7 1.4 copy-start.24
  46.7 20.8 %copy-start.17 = (pred[48]{0:T(512)(128)(4,1)}, pred[48]{0:T(512)(128)(4,1)S(1)}, u32[]{:S(2)}) copy-start(pred[48]{0:T(512)(128)(4,1)S(1)} %get-tuple-element.15) | copy-start | bytes 148
  55.0 12.5 %copy-start.5 = (f32[48,64]{1,0:T(8,128)S(1)}, f32[48,64]{1,0:T(8,128)}, u32[]{:S(2)}) copy-start(f32[48,64]{1,0:T(8,128)} %get-tuple-element.28) | copy-start | bytes 36868
  55.0 13.1 %copy-start.4 = (f32[48,64]{1,0:T(8,128)S(1)}, f32[48,64]{1,0:T(8,128)}, u32[]{:S(2)}) copy-start(f32[48,64]{1,0:T(8,128)} %get-tuple-element.30) | copy-start | bytes 36868
  70.5 19.1 %all-to-all-start.2 = ((bf16[4,2,65536]{2,1,0:T(2,128)(2,1)}), bf16[4,2,65536]{2,1,0:T(2,128)(2,1)S(1)}, u32[]{:S(2)}, u32[]{:S(2)}) async-start(bf16[4,2,65536]{2,1,0:T(2,128)(2,1)} %all_to_all.30), calls=%async_computation.2 | async-start | bytes 2097152 | tf_op jit(solution)/shard_map/all_to_all | solution.py:125
  89.6 3.9 %copy-start.1 = (bf16[4,2,65536]{2,1,0:T(2,128)(2,1)}, bf16[4,2,65536]{2,1,0:T(2,128)(2,1)S(1)}, u32[]{:S(2)}) copy-start(bf16[4,2,65536]{2,1,0:T(2,128)(2,1)S(1)} %all-to-all-done.2) | copy-start | bytes 3145732
  89.6 17.9 %all-to-all-start = ((bf16[4,2,4096]{2,1,0:T(2,128)(2,1)}), bf16[4,2,4096]{2,1,0:T(2,128)(2,1)}, u32[]{:S(2)}, u32[]{:S(2)}) async-start(bf16[4,2,4096]{2,1,0:T(2,128)(2,1)} %all_to_all.24), calls=%async_computation | async-start | bytes 131072 | tf_op jit(solution)/shard_map/all_to_all | solution.py:137
  93.5 82.3 %all-reduce.5.cloned.1.call-start = ((), (), s32[]{:S(2)}) async-start(), calls=%async_computation.4 | async-start | bytes 1572864 | tf_op jit(solution)/shard_map/psum | solution.py:72
  95.4 6.5 %copy-start.2 = (f32[48,4096]{1,0:T(8,128)S(1)}, f32[48,4096]{1,0:T(8,128)}, u32[]{:S(2)}) copy-start(f32[48,4096]{1,0:T(8,128)} %all-reduce.3.cloned.1.call-done) | copy-start | bytes 2359300
  95.4 6.5 %copy-start.18 = (pred[48]{0:T(512)(128)(4,1)S(1)}, pred[48]{0:T(512)(128)(4,1)}, u32[]{:S(2)}) copy-start(pred[48]{0:T(512)(128)(4,1)} %copy-done.17) | copy-start | bytes 148
  95.4 6.5 %copy-start.20 = (s32[48]{0:T(128)S(1)}, s32[48]{0:T(128)}, u32[]{:S(2)}) copy-start(s32[48]{0:T(128)} %get-tuple-element.32) | copy-start | bytes 580
  103.1 5.3 %copy-start.16 = (pred[48]{0:T(512)(128)(4,1)S(1)}, pred[48]{0:T(512)(128)(4,1)}, u32[]{:S(2)}) copy-start(pred[48]{0:T(512)(128)(4,1)} %get-tuple-element.16) | copy-start | bytes 148
  103.1 5.3 %copy-start.22 = (s32[48]{0:T(128)S(1)}, s32[48]{0:T(128)}, u32[]{:S(2)}) copy-start(s32[48]{0:T(128)} %multiply_add_fusion.1) | copy-start | bytes 580
  107.5 6.7 %copy-start.6 = (f32[48,1,64]{2,0,1:T(8,128)S(1)}, f32[48,1,64]{2,0,1:T(8,128)}, u32[]{:S(2)}) copy-start(f32[48,1,64]{2,0,1:T(8,128)} %get-tuple-element.29) | copy-start | bytes 36868
  107.5 6.7 %copy-start.7 = (f32[48,1,64]{2,0,1:T(8,128)S(1)}, f32[48,1,64]{2,0,1:T(8,128)}, u32[]{:S(2)}) copy-start(f32[48,1,64]{2,0,1:T(8,128)} %get-tuple-element.41) | copy-start | bytes 36868
  107.5 6.8 %copy-start.8 = (bf16[6,2,8,128]{3,2,0,1:T(8,128)(2,1)S(1)}, bf16[6,2,8,128]{3,2,0,1:T(8,128)(2,1)}, u32[]{:S(2)}) copy-start(bf16[6,2,8,128]{3,2,0,1:T(8,128)(2,1)} %copy.65) | copy-start | bytes 73732
  107.5 6.8 %copy-start.11 = (pred[48,256]{1,0:T(8,128)(4,1)S(1)}, pred[48,256]{1,0:T(8,128)(4,1)}, u32[]{:S(2)}) copy-start(pred[48,256]{1,0:T(8,128)(4,1)} %iota_compare_fusion) | copy-start | bytes 36868
  107.5 6.8 %copy-start.12 = (pred[48,256]{1,0:T(8,128)(4,1)S(1)}, pred[48,256]{1,0:T(8,128)(4,1)}, u32[]{:S(2)}) copy-start(pred[48,256]{1,0:T(8,128)(4,1)} %get-tuple-element.40) | copy-start | bytes 36868
  114.3 6.6 %copy-start.13 = (f32[48,128]{1,0:T(8,128)S(1)}, f32[48,128]{1,0:T(8,128)}, u32[]{:S(2)}) copy-start(f32[48,128]{1,0:T(8,128)} %pad_maximum_fusion.2) | copy-start | bytes 73732
  114.3 6.6 %copy-start.14 = (f32[48,128]{1,0:T(8,128)S(1)}, f32[48,128]{1,0:T(8,128)}, u32[]{:S(2)}) copy-start(f32[48,128]{1,0:T(8,128)} %pad_maximum_fusion.3) | copy-start | bytes 73732
  114.3 6.6 %copy-start.15 = (pred[48,256]{1,0:T(8,128)(4,1)S(1)}, pred[48,256]{1,0:T(8,128)(4,1)}, u32[]{:S(2)}) copy-start(pred[48,256]{1,0:T(8,128)(4,1)} %get-tuple-element.39) | copy-start | bytes 36868
Sparse Core Ops, SparseCore 0:
  39.6 46.3 all-reduce.2
  130.5 45.2 all-reduce.4
where the time goes:
time: 186 us; the launch traced here: 185 us
  matrix products  59.1 us (32%)
  waiting for transfers between devices  45.2 us (24%)
  local copies, waits for them, and re-layouts  27.7 us (15%)
  other arithmetic  25.6 us (14%)
  between operations  14.5 us (8%)
  starting transfers between devices  12.4 us (7%)
    psum x2, waiting for transfers between devices, finish(): summed = lax.psum(head_part, 'tp')  45.1 us
    dot_general x3, matrix products, relocate(): kept = jnp.dot(keeping, own_rows, preferred_element_type=jnp.float32)  15.2 us
    select_n x2, other arithmetic, write_rows(): return jnp.where(placed, new_rows[:, :, None, :], stored)  14.1 us
    unnamed x53, local copies, waits for them, and re-layouts  13.9 us
    dot_general x3, matrix products, relocate(): jnp.dot(taking, got_rows, preferred_element_type=jnp.float32)  9.03 us
    dot_general x3, matrix products, select_rows(): jnp.dot(matrix, rows_in, preferred_element_type=jnp.float32)  8.32 us
    dot_general x2, matrix products, finish(): jnp.dot(attended, out_weight, preferred_element_type=jnp.float32)  7.87 us
    dot_general x2, matrix products, decode_step(): jnp.dot(normed, query_weight, preferred_element_type=jnp.float32)  6.14 us
  transfers between devices with their start and end apart: 5, of which 2 were waited for; matrix products, arithmetic and copies ran while one was open for 27% of the time, Pallas kernels for 0%

commit v1 on v0

v1 whole, which is shorter than its diff:
```python
import functools

import jax
import jax.numpy as jnp
import numpy as np
from jax import lax
from jax.experimental import pallas as pl
from jax.experimental.pallas import tpu as pltpu
from jax.sharding import PartitionSpec as P

MOVE = 2
EPS = 1e-05
THETA = 500000.0
HD = 128
GROUP = 8
PIECE = 16
CHUNK = 8

F32 = jnp.float32
BF16 = jnp.bfloat16
I32 = jnp.int32

ANY = pl.BlockSpec(memory_space=pl.ANY)
VMEM = pl.BlockSpec(memory_space=pltpu.VMEM)
SMEM = pl.BlockSpec(memory_space=pltpu.SMEM)


def params(mib):
    return pltpu.CompilerParams(vmem_limit_bytes=mib * 1024 * 1024)


def cost(flops, nbytes):
    return pl.CostEstimate(flops=flops, bytes_accessed=nbytes, transcendentals=0)


def angle_tables(positions):
    frequency = THETA ** (-(np.arange(HD // 2, dtype=np.float64) * 2.0) / HD)
    angles = np.arange(positions, dtype=np.float64)[:, None] * frequency[None, :]
    cosine = np.concatenate([np.cos(angles), np.cos(angles)], axis=-1)
    sine = np.concatenate([-np.sin(angles), np.sin(angles)], axis=-1)
    return cosine.astype(np.float32), sine.astype(np.float32)


def turn(x, cosine, sine):
    return x * cosine + pltpu.roll(x, HD // 2, 1) * sine


def gather_angles(position_of, slots, cos_ref, sin_ref, cos_rows, sin_rows):
    for s in range(slots):
        p = position_of(s)
        cos_rows[s : s + 1, :] = cos_ref[pl.ds(p, 1), :]
        sin_rows[s : s + 1, :] = sin_ref[pl.ds(p, 1), :]


def spread_normed(normed3, spread, slots, width):
    blocks = width // HD
    row = lax.broadcasted_iota(I32, (HD, 4 * HD), 0)
    col = lax.broadcasted_iota(I32, (HD, 4 * HD), 1)
    goal = jnp.where(col < 2 * HD, 2 * row, 2 * row + 1 + 2 * HD)
    places = jnp.where(col == goal, 1.0, 0.0).astype(BF16)
    spread_all = jnp.dot(
        normed3[...].reshape(blocks * slots, HD), places, preferred_element_type=F32
    ).astype(BF16)
    spread[:, 0:slots, :] = spread_all[:, : 2 * HD].reshape(blocks, slots, 2 * HD)
    spread[:, slots:, :] = spread_all[:, 2 * HD :].reshape(blocks, slots, 2 * HD)


def project(normed3, spread, wq, wkv, wq_copies, wkv_copies, slots, width):
    pieces = len(wq_copies)
    depth = width // pieces
    query = None
    pair = None
    for c in range(pieces):
        wkv_copies[c].wait()
        for b in range(c * depth // HD, (c + 1) * depth // HD):
            part = jnp.dot(
                spread[b], wkv[b * 2 * HD : (b + 1) * 2 * HD, :], preferred_element_type=F32
            )
            pair = part if pair is None else pair + part
    for c in range(pieces):
        wq_copies[c].wait()
        for b in range(c * depth // (2 * HD), (c + 1) * depth // (2 * HD)):
            block = jnp.concatenate([normed3[2 * b], normed3[2 * b + 1]], axis=1)
            part = jnp.dot(
                block, wq[b * 2 * HD : (b + 1) * 2 * HD, :], preferred_element_type=F32
            )
            query = part if query is None else query + part
    return query, pair[:slots], pair[slots:]


def weight_copies(src, dst, sem, pieces):
    depth = src.shape[0] // pieces
    copies = [
        pltpu.make_async_copy(
            src.at[pl.ds(c * depth, depth)], dst.at[pl.ds(c * depth, depth)], sem.at[c]
        )
        for c in range(pieces)
    ]
    return copies


def put_row(cache, place, p, key_row, value_row):
    base = pl.multiple_of((jnp.maximum(p, 0) // PIECE) * PIECE, PIECE)
    hit = lax.broadcasted_iota(I32, (PIECE, HD), 0) + base == p
    for which, new in ((0, key_row), (1, value_row)):
        old = cache[place, which, pl.ds(base, PIECE), :].astype(F32)
        cache[place, which, pl.ds(base, PIECE), :] = jnp.where(hit, new, old).astype(BF16)


def attend(cache, places, positions, query_rows):
    cap = cache.shape[2]
    col = lax.broadcasted_iota(I32, (GROUP, cap), 1)
    scores = [
        lax.dot_general(
            rows.astype(BF16),
            cache[place, 0],
            (((1,), (1,)), ((), ())),
            preferred_element_type=F32,
        )
        for place, rows in zip(places, query_rows)
    ]
    probs = []
    for score, p in zip(scores, positions):
        score = jnp.where(col <= p, score * HD**-0.5, -jnp.inf)
        weight = jnp.exp(score - jnp.max(score, axis=-1, keepdims=True))
        weight = weight / jnp.sum(weight, axis=-1, keepdims=True)
        probs.append(weight.astype(BF16))
    return [
        jnp.dot(prob, cache[place, 1], preferred_element_type=F32)
        for place, prob in zip(places, probs)
    ]


def norm_into(normed3, pieces, gains, firsts, total_width):
    square = None
    for piece in pieces:
        part = jnp.sum(piece * piece, axis=-1, keepdims=True)
        square = part if square is None else square + part
    factor = lax.rsqrt(square / total_width + EPS)
    for piece, gain, first in zip(pieces, gains, firsts):
        normed = (piece * factor * gain).astype(BF16)
        for i in range(piece.shape[1] // HD):
            normed3[first + i] = normed[:, i * HD : (i + 1) * HD]


def first_kernel(
    peers, slots, heads, shard,
    meta, source_s, lengths_s, source_v, hidden, gain, cos_ref, sin_ref, wq_hbm, wkv_hbm, cache_hbm,
    query_out, newkey_out, newvalue_out, plan, *rest,
):
    others = peers - 1
    moving = others * MOVE
    boxes, notes = rest[:others], rest[others : 2 * others]
    (wq, wkv, normed3, spread, cos_rows, sin_rows, leaving, hidden32,
     wq_sem, wkv_sem, in_sem, out_sem) = rest[2 * others :]
    width = hidden.shape[1]
    me, me_tp = meta[0], meta[1]
    wq_copies = weight_copies(wq_hbm, wq, wq_sem, 4)
    wkv_copies = weight_copies(wkv_hbm, wkv, wkv_sem, 4)
    for copy in wkv_copies + wq_copies:
        copy.start()

    low = me * slots
    src = source_v[...]
    index = lax.broadcasted_iota(I32, src.shape, 1)
    mine_goes = (src >= low) & (src < low + slots)
    mine_comes = (index >= low) & (index < low + slots)
    index_f = index.astype(F32)
    send_slots = []
    for k in range(1, peers):
        to = lax.rem(me + k, peers) * slots
        sent = mine_goes & (index >= to) & (index < to + slots)
        origin = lax.rem(me + peers - k, peers) * slots
        taken = mine_comes & (src >= origin) & (src < origin + slots)
        for m in range(MOVE):
            at = (k - 1) * MOVE + m
            if m == 0:
                j = jnp.min(jnp.where(sent, index_f, 1e6)).astype(I32)
                r = jnp.min(jnp.where(taken, index_f, 1e6)).astype(I32)
            else:
                j = jnp.max(jnp.where(sent, index_f, -1.0)).astype(I32)
                r = jnp.max(jnp.where(taken, index_f, -1.0)).astype(I32)
            known = (j >= 0) & (j < src.shape[1])
            slot = source_s[jnp.where(known, j, 0)] - low
            slot = jnp.where(known, slot, 0)
            send_slots.append(slot)
            plan[at] = jnp.where((r >= 0) & (r < src.shape[1]), r - low, -1)
            pltpu.make_async_copy(cache_hbm.at[slot], leaving.at[at], in_sem.at[at]).start()

    wide = hidden[...].astype(F32)
    hidden32[...] = wide
    norm_into(normed3, [wide], [gain[...]], [0], width)
    spread_normed(normed3, spread, slots, width)
    gather_angles(lambda s: lengths_s[low + s], slots, cos_ref, sin_ref, cos_rows, sin_rows)
    query, key, value = project(normed3, spread, wq, wkv, wq_copies, wkv_copies, slots, width)
    cosine, sine = cos_rows[...], sin_rows[...]
    query_out[...] = jnp.zeros(query_out.shape, F32)
    for g in range(heads):
        turned = turn(query[:, g * HD : (g + 1) * HD], cosine, sine)
        query_out[pl.ds(g, slots, stride=GROUP), :] = turned.astype(BF16).astype(F32)
    newkey_out[...] = turn(key, cosine, sine).astype(BF16).astype(F32)
    newvalue_out[...] = value.astype(BF16).astype(F32)

    positions = [lengths_s[low + slot] for slot in send_slots]
    for at, slot in enumerate(send_slots):
        pltpu.make_async_copy(cache_hbm.at[slot], leaving.at[at], in_sem.at[at]).wait()
        put_row(
            leaving, at, positions[at],
            newkey_out[pl.ds(slot, 1), :], newvalue_out[pl.ds(slot, 1), :],
        )
    for k in range(others):
        pltpu.make_async_copy(
            leaving.at[pl.ds(k * MOVE, MOVE)], boxes[k], out_sem.at[k]
        ).start()
    rows = [query_out[pl.ds(pl.multiple_of(slot * GROUP, GROUP), GROUP), :] for slot in send_slots]
    attended = attend(leaving, list(range(moving)), positions, rows)
    column = pl.multiple_of(me_tp * shard, shard)
    for at, slot in enumerate(send_slots):
        note = notes[at // MOVE]
        m = at % MOVE
        for g in range(heads):
            note[m : m + 1, g * HD : (g + 1) * HD] = attended[at][g : g + 1, :]
        note[m : m + 1, heads * HD :] = hidden32[pl.ds(slot, 1), pl.ds(column, shard)]
    for k in range(others):
        pltpu.make_async_copy(
            leaving.at[pl.ds(k * MOVE, MOVE)], boxes[k], out_sem.at[k]
        ).wait()


def attend_all(buffer, places, positions, query_of, attended_rows, slots):
    for c in range(slots // CHUNK):
        span = range(c * CHUNK, (c + 1) * CHUNK)
        got = attend(
            buffer,
            [places[s] for s in span],
            [positions[s] for s in span],
            [query_of(s) for s in span],
        )
        for s, rows in zip(span, got):
            attended_rows[s * GROUP : (s + 1) * GROUP, :] = rows


def attend_kernel(
    slots, heads, meta, lengths_s, query, newkey, newvalue, cache_hbm, out,
    buffer, attended_rows, in_sem,
):
    low = meta[0] * slots

    def copy_in(c):
        span = pl.ds(c * CHUNK, CHUNK)
        return pltpu.make_async_copy(cache_hbm.at[span], buffer.at[span], in_sem.at[c])

    for c in range(slots // CHUNK):
        copy_in(c).start()
    for c in range(slots // CHUNK):
        copy_in(c).wait()
        span = list(range(c * CHUNK, (c + 1) * CHUNK))
        positions = [lengths_s[low + s] for s in span]
        for s, p in zip(span, positions):
            put_row(buffer, s, p, newkey[s : s + 1, :], newvalue[s : s + 1, :])
        got = attend(
            buffer, span, positions, [query[s * GROUP : (s + 1) * GROUP, :] for s in span]
        )
        for s, rows in zip(span, got):
            attended_rows[s * GROUP : (s + 1) * GROUP, :] = rows
    for g in range(heads):
        out[:, g * HD : (g + 1) * HD] = attended_rows[pl.ds(g, slots, stride=GROUP), :].astype(BF16)


def project_out(attended, wo, wo_hbm, wo_sem, own, sends, me_tp, peers_tp):
    shard = own.shape[1]
    for k in list(range(1, peers_tp)) + [0]:
        out_copy(wo, wo_hbm, wo_sem, me_tp, peers_tp, shard, k).wait()
        part = jnp.dot(attended, wo[k], preferred_element_type=F32)
        if k == 0:
            own[...] = part
        else:
            sends[k - 1][...] = part.astype(BF16)


def out_copy(wo, wo_hbm, wo_sem, me_tp, peers_tp, shard, k):
    column = pl.multiple_of(lax.rem(me_tp + k, peers_tp) * shard, shard)
    return pltpu.make_async_copy(wo_hbm.at[:, pl.ds(column, shard)], wo.at[k], wo_sem.at[k])


def out_kernel(peers, peers_tp, meta, plan, attended, wo_hbm, *rest):
    notes = rest[: peers - 1]
    own = rest[peers - 1]
    sends = rest[peers : peers + peers_tp - 1]
    wo, wo_sem = rest[peers + peers_tp - 1 :]
    me_tp = meta[1]
    shard = own.shape[1]
    for k in list(range(1, peers_tp)) + [0]:
        out_copy(wo, wo_hbm, wo_sem, me_tp, peers_tp, shard, k).start()
    rows = attended[...].astype(F32)
    index = lax.broadcasted_iota(I32, rows.shape, 0)
    for at in range((peers - 1) * MOVE):
        note = notes[at // MOVE][at % MOVE : at % MOVE + 1, : rows.shape[1]]
        rows = jnp.where(index == plan[at], note, rows)
    project_out(rows.astype(BF16), wo, wo_hbm, wo_sem, own, sends, me_tp, peers_tp)


def sum_kernel(peers, peers_tp, heads, meta, plan, hidden, own, *rest):
    got, notes, out = rest[: peers_tp - 1], rest[peers_tp - 1 : -1], rest[-1]
    shard = own.shape[1]
    total = own[...]
    for part in got:
        total = total + part[...].astype(F32)
    if notes:
        column = pl.multiple_of(meta[1] * shard, shard)
        residual = hidden[:, pl.ds(column, shard)].astype(F32)
        index = lax.broadcasted_iota(I32, residual.shape, 0)
        for at in range((peers - 1) * MOVE):
            note = notes[at // MOVE][at % MOVE : at % MOVE + 1, heads * HD :]
            residual = jnp.where(index == plan[at], note, residual)
    else:
        residual = hidden[...].astype(F32)
    out[...] = (residual + total).astype(BF16)


def load_slots(slots, peers, cache_hbm, box_hbm, buffer, in_sem):
    copies = []
    for c in range(slots // CHUNK):
        span = pl.ds(c * CHUNK, CHUNK)
        copies.append(pltpu.make_async_copy(cache_hbm.at[span], buffer.at[span], in_sem.at[c]))
    for k in range(peers - 1):
        copies.append(
            pltpu.make_async_copy(
                box_hbm[k],
                buffer.at[pl.ds(slots + k * MOVE, MOVE)],
                in_sem.at[slots // CHUNK + k],
            )
        )
    return copies


def map_places(slots, peers, plan, place):
    for s in range(slots):
        place[s] = s
    for at in range((peers - 1) * MOVE):
        taker = plan[at]

        @pl.when(taker >= 0)
        def _():
            place[taker] = slots + at


def second_kernel(
    peers, peers_tp, slots, heads,
    meta, source_s, lengths_s, plan, gain, cos_ref, sin_ref, newkey1, newvalue1,
    wq_hbm, wkv_hbm, wo_hbm, cache_hbm, *rest,
):
    blocks, rest = rest[:peers_tp], rest[peers_tp:]
    box_hbm, rest = rest[: peers - 1], rest[peers - 1 :]
    newkey, newvalue, own = rest[:3]
    sends, rest = rest[3 : 2 + peers_tp], rest[2 + peers_tp :]
    (wq, wkv, wo, normed3, spread, cos_rows, sin_rows, buffer, query_rows, attended_rows, place,
     wq_sem, wkv_sem, wo_sem, in_sem) = rest
    me, me_tp = meta[0], meta[1]
    low = me * slots
    width = gain.shape[1]
    shard = own.shape[1]
    wq_copies = weight_copies(wq_hbm, wq, wq_sem, 4)
    wkv_copies = weight_copies(wkv_hbm, wkv, wkv_sem, 4)
    cache_copies = load_slots(slots, peers, cache_hbm, box_hbm, buffer, in_sem)
    for copy in wkv_copies + wq_copies + cache_copies[::-1]:
        copy.start()
    for k in list(range(1, peers_tp)) + [0]:
        out_copy(wo, wo_hbm, wo_sem, me_tp, peers_tp, shard, k).start()

    map_places(slots, peers, plan, place)
    firsts = [lax.rem(me_tp + peers_tp - k, peers_tp) for k in range(peers_tp)]
    norm_into(
        normed3,
        [block[...].astype(F32) for block in blocks],
        [gain[:, pl.ds(pl.multiple_of(first * shard, shard), shard)] for first in firsts],
        [first * (shard // HD) for first in firsts],
        width,
    )
    spread_normed(normed3, spread, slots, width)
    lengths = [lengths_s[source_s[low + s]] for s in range(slots)]
    gather_angles(lambda s: lengths[s] + 1, slots, cos_ref, sin_ref, cos_rows, sin_rows)
    query, key, value = project(normed3, spread, wq, wkv, wq_copies, wkv_copies, slots, width)
    cosine, sine = cos_rows[...], sin_rows[...]
    query_rows[...] = jnp.zeros(query_rows.shape, F32)
    for g in range(heads):
        turned = turn(query[:, g * HD : (g + 1) * HD], cosine, sine)
        query_rows[pl.ds(g, slots, stride=GROUP), :] = turned.astype(BF16).astype(F32)
    newkey[...] = turn(key, cosine, sine).astype(BF16).astype(F32)
    newvalue[...] = value.astype(BF16).astype(F32)

    for copy in cache_copies[::-1]:
        copy.wait()
    for c in range(slots // CHUNK):
        span = list(range(c * CHUNK, (c + 1) * CHUNK))
        places = [place[s] for s in span]
        for s, at in zip(span, places):
            first = jnp.where(at < slots, lengths[s], -1)
            put_row(buffer, at, first, newkey1[s : s + 1, :], newvalue1[s : s + 1, :])
            put_row(buffer, at, lengths[s] + 1, newkey[s : s + 1, :], newvalue[s : s + 1, :])
        got = attend(
            buffer, places, [lengths[s] + 1 for s in span],
            [query_rows[s * GROUP : (s + 1) * GROUP, :] for s in span],
        )
        for s, rows in zip(span, got):
            attended_rows[s * GROUP : (s + 1) * GROUP, :] = rows
    attended = jnp.concatenate(
        [attended_rows[pl.ds(g, slots, stride=GROUP), :].astype(BF16) for g in range(heads)], axis=1
    )
    project_out(attended, wo, wo_hbm, wo_sem, own, sends, me_tp, peers_tp)


def cache_kernel(
    peers, slots, meta, source_s, lengths_s, plan, newkey1, newvalue1, newkey2, newvalue2,
    cache_hbm, *rest,
):
    box_hbm, rest = rest[: peers - 1], rest[peers - 1 :]
    out_hbm, buffer, place, in_sem, out_sem = rest
    low = meta[0] * slots
    cache_copies = load_slots(slots, peers, cache_hbm, box_hbm, buffer, in_sem)
    for copy in cache_copies:
        copy.start()
    map_places(slots, peers, plan, place)
    chunks = slots // CHUNK
    for copy in cache_copies[chunks:]:
        copy.wait()
    outs = []
    for c in range(chunks):
        cache_copies[c].wait()
        for s in range(c * CHUNK, (c + 1) * CHUNK):
            at = place[s]
            length = lengths_s[source_s[low + s]]
            first = jnp.where(at < slots, length, -1)
            put_row(buffer, at, first, newkey1[s : s + 1, :], newvalue1[s : s + 1, :])
            put_row(buffer, at, length + 1, newkey2[s : s + 1, :], newvalue2[s : s + 1, :])
            copy = pltpu.make_async_copy(buffer.at[at], out_hbm.at[s], out_sem.at[s])
            copy.start()
            outs.append(copy)
    for copy in outs:
        copy.wait()


def join_kernel(peers_tp, meta, *rest):
    blocks, out = rest[:-1], rest[-1]
    shard = blocks[0].shape[1]
    for k, block in enumerate(blocks):
        first = lax.rem(meta[1] + peers_tp - k, peers_tp)
        out[:, pl.ds(pl.multiple_of(first * shard, shard), shard)] = block[...]


def shifted(x, axis, size, k):
    return lax.ppermute(x, axis, [(i, (i + k) % size) for i in range(size)])


def local(
    tables, kv_cache, hidden, lengths, source, norm_gain, query_weight, keyval_weight, out_weight
):
    peers, peers_tp = lax.axis_size("inst"), lax.axis_size("tp")
    slots, cap = kv_cache.shape[0], kv_cache.shape[2]
    width = hidden.shape[1]
    heads = query_weight.shape[1] // HD
    shard = width // peers_tp
    others, moving = peers - 1, (peers - 1) * MOVE
    blocks = width // HD
    meta = jnp.stack([lax.axis_index("inst"), lax.axis_index("tp")]).astype(I32)
    gain = norm_gain.reshape(1, width)
    wkv = keyval_weight.reshape(2 * width, HD)
    cosine, sine = (jnp.asarray(table) for table in tables)
    row32 = jax.ShapeDtypeStruct((slots, HD), F32)
    note_width = heads * HD + shard
    dma = pltpu.SemaphoreType.DMA
    weights = [
        pltpu.VMEM(query_weight.shape, BF16),
        pltpu.VMEM(wkv.shape, BF16),
    ]
    stages = [
        pltpu.VMEM((blocks, slots, HD), BF16),
        pltpu.VMEM((blocks, 2 * slots, 2 * HD), BF16),
        pltpu.VMEM((slots, HD), F32),
        pltpu.VMEM((slots, HD), F32),
    ]
    flops = 2 * slots * width * (heads + 2) * HD
    cache_bytes = kv_cache.size * 2

    query, newkey1, newvalue1, plan, *rest = pl.pallas_call(
        functools.partial(first_kernel, peers, slots, heads, shard),
        out_shape=[
            jax.ShapeDtypeStruct((slots * GROUP, HD), F32),
            row32,
            row32,
            jax.ShapeDtypeStruct((moving,), I32),
        ]
        + [jax.ShapeDtypeStruct((MOVE,) + kv_cache.shape[1:], BF16)] * others
        + [jax.ShapeDtypeStruct((MOVE, note_width), F32)] * others,
        in_specs=[SMEM] * 3 + [VMEM] * 5 + [ANY] * 3,
        out_specs=[VMEM] * 3 + [SMEM] + [ANY] * others + [VMEM] * others,
        scratch_shapes=weights
        + stages
        + [
            pltpu.VMEM((moving,) + kv_cache.shape[1:], BF16),
            pltpu.VMEM((slots, width), F32),
            dma((4,)),
            dma((4,)),
            dma((moving,)),
            dma((others,)),
        ],
        compiler_params=params(40),
        cost_estimate=cost(flops, (query_weight.size + wkv.size) * 2),
        name="first_step",
    )(meta, source, lengths, source.reshape(1, -1), hidden, gain, cosine, sine, query_weight, wkv,
      kv_cache)
    boxes, notes = rest[:others], rest[others:]
    got_notes = [shifted(note, "inst", peers, k + 1) for k, note in enumerate(notes)]
    got_boxes = [shifted(box, "inst", peers, k + 1) for k, box in enumerate(boxes)]

    attended = pl.pallas_call(
        functools.partial(attend_kernel, slots, heads),
        out_shape=jax.ShapeDtypeStruct((slots, heads * HD), BF16),
        in_specs=[SMEM] * 2 + [VMEM] * 3 + [ANY],
        out_specs=VMEM,
        scratch_shapes=[
            pltpu.VMEM(kv_cache.shape, BF16),
            pltpu.VMEM((slots * GROUP, HD), F32),
            dma((slots // CHUNK,)),
        ],
        compiler_params=params(24),
        cost_estimate=cost(4 * slots * cap * HD * heads, cache_bytes),
        name="attention",
    )(meta, lengths, query, newkey1, newvalue1, kv_cache)

    sent = [jax.ShapeDtypeStruct((slots, shard), F32)]
    sent += [jax.ShapeDtypeStruct((slots, shard), BF16)] * (peers_tp - 1)
    wo_scratch = pltpu.VMEM((peers_tp, heads * HD, shard), BF16)
    own, *sends = pl.pallas_call(
        functools.partial(out_kernel, peers, peers_tp),
        out_shape=sent,
        in_specs=[SMEM] * 2 + [VMEM, ANY] + [VMEM] * others,
        out_specs=[VMEM] * peers_tp,
        scratch_shapes=[wo_scratch, dma((peers_tp,))],
        compiler_params=params(24),
        cost_estimate=cost(2 * slots * width * heads * HD, out_weight.size * 2),
        name="out_projection",
    )(meta, plan, attended, out_weight, *got_notes)

    def summed(residual, own, sends, notes):
        got = [shifted(part, "tp", peers_tp, k + 1) for k, part in enumerate(sends)]
        shard_rows = pl.pallas_call(
            functools.partial(sum_kernel, peers, peers_tp, heads),
            out_shape=jax.ShapeDtypeStruct((slots, shard), BF16),
            in_specs=[SMEM] * 2 + [VMEM] * (2 + len(got) + len(notes)),
            out_specs=VMEM,
            compiler_params=params(16),
            name="sum_terms",
        )(meta, plan, residual, own, *got, *notes)
        return [shard_rows] + [
            shifted(shard_rows, "tp", peers_tp, k) for k in range(1, peers_tp)
        ]

    pieces = summed(hidden, own, sends, got_notes)

    newkey2, newvalue2, own, *sends = pl.pallas_call(
        functools.partial(second_kernel, peers, peers_tp, slots, heads),
        out_shape=[row32, row32] + sent,
        in_specs=[SMEM] * 4 + [VMEM] * 5 + [ANY] * 4 + [VMEM] * peers_tp + [ANY] * others,
        out_specs=[VMEM] * (2 + peers_tp),
        scratch_shapes=weights
        + [wo_scratch]
        + stages
        + [
            pltpu.VMEM((slots + moving,) + kv_cache.shape[1:], BF16),
            pltpu.VMEM((slots * GROUP, HD), F32),
            pltpu.VMEM((slots * GROUP, HD), F32),
            pltpu.SMEM((slots,), I32),
            dma((4,)),
            dma((4,)),
            dma((peers_tp,)),
            dma((slots // CHUNK + others,)),
        ],
        compiler_params=params(48),
        cost_estimate=cost(3 * flops, cache_bytes + (query_weight.size + wkv.size) * 4),
        name="second_step",
    )(meta, source, lengths, plan, gain, cosine, sine, newkey1, newvalue1, query_weight, wkv,
      out_weight, kv_cache, *pieces, *got_boxes)

    pieces = summed(pieces[0], own, sends, [])
    final_cache = pl.pallas_call(
        functools.partial(cache_kernel, peers, slots),
        out_shape=jax.ShapeDtypeStruct(kv_cache.shape, BF16),
        in_specs=[SMEM] * 4 + [VMEM] * 4 + [ANY] * peers,
        out_specs=ANY,
        scratch_shapes=[
            pltpu.VMEM((slots + moving,) + kv_cache.shape[1:], BF16),
            pltpu.SMEM((slots,), I32),
            dma((slots // CHUNK + others,)),
            dma((slots,)),
        ],
        compiler_params=params(24),
        cost_estimate=cost(0, 2 * cache_bytes),
        name="write_cache",
    )(meta, source, lengths, plan, newkey1, newvalue1, newkey2, newvalue2, kv_cache, *got_boxes)
    final_hidden = pl.pallas_call(
        functools.partial(join_kernel, peers_tp),
        out_shape=jax.ShapeDtypeStruct(hidden.shape, BF16),
        in_specs=[SMEM] + [VMEM] * peers_tp,
        out_specs=VMEM,
        compiler_params=params(16),
        name="join",
    )(meta, *pieces)
    return (final_hidden, final_cache)


def solution(mesh):
    def whole(kv_cache, *rest):
        tables = angle_tables(kv_cache.shape[2])
        return jax.shard_map(
            functools.partial(local, tables),
            mesh=mesh,
            in_specs=(
                P(("groups", "inst"), None, None, "tp"),
                P(("groups", "inst"), None),
                P("groups"),
                P("groups"),
                P(),
                P(None, "tp"),
                P(None, None, "tp"),
                P("tp", None),
            ),
            out_specs=(P(("groups", "inst"), None), P(("groups", "inst"), None, None, "tp")),
            check_vma=False,
        )(kv_cache, *rest)

    return whole
```

time: 186 us -> 89.5 us (0.48)
  matrix products: 59.1 us -> 0 us
  Pallas kernels: 0 us -> 31 us
  waiting for transfers between devices: 45.2 us -> 14.8 us
  other arithmetic: 25.6 us -> 0.08 us
  starting transfers between devices: 12.4 us -> 31 us
  local copies, waits for them, and re-layouts: 27.7 us -> 11.5 us
  between operations: 14.5 us -> 0.87 us
    dot_general x17 -> x0, matrix products: 53 us -> none  [the longest x3 15.2 us: relocate(): kept = jnp.dot(keeping, own_rows, preferred_element_type=jnp.float32)]
    psum x2 -> x0, waiting for transfers between devices: 45.1 us -> none  [finish(): summed = lax.psum(head_part, 'tp')]
    pallas_call x0 -> x8, Pallas kernels: none -> 31 us  [the longest x1 10.1 us: local(): pl.pallas_call(functools.partial(second_kernel, peers, peers_tp, slots, h...]
    ppermute x0 -> x18, starting transfers between devices: none -> 31 us  [shifted(): return lax.ppermute(x, axis, [(i, (i + k) % size) for i in range(size)])]
    select_n x4 -> x0, other arithmetic: 15.5 us -> none  [the longest x2 14.1 us: write_rows(): return jnp.where(placed, new_rows[:, :, None, :], stored)]
    ppermute x0 -> x18, waiting for transfers between devices: none -> 14.8 us  [shifted(): return lax.ppermute(x, axis, [(i, (i + k) % size) for i in range(size)])]
    all_to_all x3 -> x0, starting transfers between devices: 12.1 us -> none  [the longest x1 4.24 us: local(): lax.all_to_all(select_rows(packing, flat_rows), 'inst', split_axis=0, con...]
    all_to_all x6 -> x0, local copies, waits for them, and re-layouts: 7.55 us -> none  [the longest x2 3.25 us: local(): lax.all_to_all(select_rows(packing, flat_cache), 'inst', split_axis=0, co...]
  transfers between devices with their start and end apart: 5 -> 18, of which waited for: 2 -> 10; matrix products, arithmetic and copies ran while one was open for 27% -> 0% of each run, Pallas kernels for 0% -> 11%
where the time goes in v1:
time: 89.5 us; the launch traced here: 89.1 us
  Pallas kernels  31 us (35%)
  starting transfers between devices  31 us (35%)
  waiting for transfers between devices  14.8 us (17%)
  local copies, waits for them, and re-layouts  11.5 us (13%)
    ppermute x18, starting transfers between devices, shifted(): return lax.ppermute(x, axis, [(i, (i + k) % size) for i in range(size)])  31 us
    ppermute x18, waiting for transfers between devices, shifted(): return lax.ppermute(x, axis, [(i, (i + k) % size) for i in range(size)])  14.8 us
    unnamed x36, local copies, waits for them, and re-layouts  11.5 us
    pallas_call x1, Pallas kernels, local(): pl.pallas_call(functools.partial(second_kernel, peers, peers_tp, slots, h...  10.1 us
    pallas_call x1, Pallas kernels, local(): pl.pallas_call(functools.partial(first_kernel, peers, slots, heads, shard...  6.94 us
    pallas_call x1, Pallas kernels, local(): pl.pallas_call(functools.partial(attend_kernel, slots, heads), out_shape=...  4.56 us
    pallas_call x1, Pallas kernels, local(): pl.pallas_call(functools.partial(cache_kernel, peers, slots), out_shape=j...  4.24 us
    pallas_call x1, Pallas kernels, local(): pl.pallas_call(functools.partial(out_kernel, peers, peers_tp), out_shape=...  2.59 us
  transfers between devices with their start and end apart: 18, of which 10 were waited for; matrix products, arithmetic and copies ran while one was open for 0% of the time, Pallas kernels for 11%

profile of v1, /device:TPU:0, one launch (start us, length us, event | category | flops | bytes accessed | tf_op | source)
XLA Modules:
  0.0 89.1 jit_solution(10221624158579247404)
XLA Ops:
  0.6 0.1 pad_add_fusion.meta
  0.7 2.8 %copy-done = bf16[48,2,256,128]{3,2,1,0:T(8,128)(2,1)S(1)} copy-done((bf16[48,2,256,128]{3,2,1,0:T(8,128)(2,1)S(1)}, bf16[48,2,256,128]{3,2,1,0:T(8,128)(2,1)}, u32[]{:S(2)}) %copy-start) | copy-done | bytes 6291480
  3.5 2.2 %copy-done.1 = bf16[4096,512]{1,0:T(8,128)(2,1)S(1)} copy-done((bf16[4096,512]{1,0:T(8,128)(2,1)S(1)}, bf16[4096,512]{1,0:T(8,128)(2,1)}, u32[]{:S(2)}) %copy-start.1) | copy-done | bytes 4194328
  5.7 1.6 %copy-done.3 = bf16[4096,2,128]{2,1,0:T(2,128)(2,1)S(1)} copy-done((bf16[4096,2,128]{2,1,0:T(2,128)(2,1)S(1)}, bf16[4096,2,128]{2,1,0:T(2,128)(2,1)}, u32[]{:S(2)}) %copy-start.3) | copy-done | bytes 2097176
  7.3 1.0 %copy-done.5 = bf16[48,4096]{1,0:T(8,128)(2,1)S(1)} copy-done((bf16[48,4096]{1,0:T(8,128)(2,1)S(1)}, bf16[48,4096]{1,0:T(8,128)(2,1)}, u32[]{:S(2)}) %copy-start.5) | copy-done | bytes 393240
  8.3 0.9 %copy-done.6 = f32[256,128]{1,0:T(8,128)S(1)} copy-done((f32[256,128]{1,0:T(8,128)S(1)}, f32[256,128]{1,0:T(8,128)}, u32[]{:S(2)}) %copy-start.6) | copy-done | bytes 131096
  9.2 0.9 %copy-done.8 = f32[256,128]{1,0:T(8,128)S(1)} copy-done((f32[256,128]{1,0:T(8,128)S(1)}, f32[256,128]{1,0:T(8,128)}, u32[]{:S(2)}) %copy-start.8) | copy-done | bytes 131096
  10.1 0.7 copy-done.10
  10.8 0.7 copy-done.12
  11.5 0.7 copy-done.14
  12.2 6.9 %first_step.1 = (f32[384,128]{1,0:T(8,128)S(1)}, f32[48,128]{1,0:T(8,128)S(1)}, f32[48,128]{1,0:T(8,128)S(1)}, s32[6]{0:T(128)S(1)}, bf16[2,2,256,128]{3,2,1,0:T...) custom-call(s32[2]{0:T(128)S(1)} %pad_add_fusion.meta, ...), custom_call_target="tpu_custom_call" | custom-call | flops 301989888 | bytes 6291456 | tf_op jit(solution)/shard_map/first_step/pallas_call | solution.py:485
  19.1 0.0 copy-start.2
  19.1 0.5 collective-permute-start
  19.6 2.6 %collective-permute-start.1 = (f32[2,1536]{1,0:T(2,128)S(1)}, f32[2,1536]{1,0:T(2,128)S(1)}, u32[]{:S(2)}, u32[]{:S(2)}) collective-permute-start(f32[2,1536]{1,0:T(2,128)S(1)} %get-tuple-element.27), channel_id=1, source_target_pairs={{0,8},{4,12},{8,0},{12,4},{1,9},{5,13},{9,1},{13,5},{2,10},{6,14},... | collective-permute-start | bytes 36872 | tf_op jit(solution)/shard_map/ppermute | solution.py:452
  22.2 1.4 %collective-permute-start.2 = (f32[2,1536]{1,0:T(2,128)S(1)}, f32[2,1536]{1,0:T(2,128)S(1)}, u32[]{:S(2)}, u32[]{:S(2)}) collective-permute-start(f32[2,1536]{1,0:T(2,128)S(1)} %get-tuple-element.28), channel_id=1, source_target_pairs={{0,12},{4,0},{8,4},{12,8},{1,13},{5,1},{9,5},{13,9},{2,14},{6,2},{... | collective-permute-start | bytes 36872 | tf_op jit(solution)/shard_map/ppermute | solution.py:452
  23.6 4.6 %attention.1.attended = bf16[48,512]{1,0:T(8,128)(2,1)S(1)} custom-call(s32[2]{0:T(128)S(1)} %pad_add_fusion.meta, s32[192]{0:T(256)S(1)} %copy-done.14, f32[384,128]{1,0:T(8,128)S(1)} %get-tuple-element.23.query, f32[48,128]{1,0:T(8,128)S(1)} %get-tuple-element.24.newkey.newkey1, f32[48,128]{1,0:T(8,128)S(1)} %get-tuple-element.25.newvalue.newvalue1, ...), custom_call_target="tpu_custom_call" | custom-call | flops 25165824 | bytes 6291456 | tf_op jit(solution)/shard_map/attention/pallas_call | solution.py:516
  28.2 0.0 copy-start.4
  28.2 0.0 copy-start.7
  28.2 0.0 copy-start.9
  28.2 0.0 copy-start.11
  28.2 0.0 copy-start.13
  28.2 0.0 copy-start.15
  28.2 0.0 collective-permute-done.rest_0_.rest_3_
  28.3 0.0 collective-permute-done.1.rest_1_.rest_4_
  28.3 0.0 collective-permute-done.2.rest_2_.rest_5_
  28.3 2.6 %out_projection.1 = (f32[48,1024]{1,0:T(8,128)S(1)}, bf16[48,1024]{1,0:T(8,128)(2,1)S(1)}, bf16[48,1024]{1,0:T(8,128)(2,1)S(1)}, bf16[48,1024]{1,0:T(8,128)(2,1)S(1)}) custom-call(s32[2]{0:T(128)S(1)} %pad_add_fusion.meta, s32[6]{0:T(128)S(1)} %get-tuple-element.22.plan, bf16[48,512]{1,0:T(8,128)(2,1)S(1)} %attention.1.attended, ...), custom_call_target="tpu_custom_call" | custom-call | flops 201326592 | bytes 4194304 | tf_op jit(solution)/shard_map/out_projection/pallas_call | solution.py:534
  30.9 1.6 %collective-permute-start.3 = (bf16[48,1024]{1,0:T(8,128)(2,1)S(1)}, bf16[48,1024]{1,0:T(8,128)(2,1)S(1)}, u32[]{:S(2)}, u32[]{:S(2)}) collective-permute-start(bf16[48,1024]{1,0:T(8,128)(2,1)S(1)} %get-tuple-element.30), channel_id=1, source_target_pairs={{0,1},{1,2},{2,3},{3,0},{4,5},{5,6},{6,7},{7,4},{8,9},{9,10},{10,1... | collective-permute-start | bytes 294920 | tf_op jit(solution)/shard_map/ppermute | solution.py:452
  32.5 2.6 %collective-permute-start.4 = (bf16[48,1024]{1,0:T(8,128)(2,1)S(1)}, bf16[48,1024]{1,0:T(8,128)(2,1)S(1)}, u32[]{:S(2)}, u32[]{:S(2)}) collective-permute-start(bf16[48,1024]{1,0:T(8,128)(2,1)S(1)} %get-tuple-element.31), channel_id=1, source_target_pairs={{0,2},{1,3},{2,0},{3,1},{4,6},{5,7},{6,4},{7,5},{8,10},{9,11},{10,... | collective-permute-start | bytes 294920 | tf_op jit(solution)/shard_map/ppermute | solution.py:452
  35.1 1.3 %collective-permute-start.5 = (bf16[48,1024]{1,0:T(8,128)(2,1)S(1)}, bf16[48,1024]{1,0:T(8,128)(2,1)S(1)}, u32[]{:S(2)}, u32[]{:S(2)}) collective-permute-start(bf16[48,1024]{1,0:T(8,128)(2,1)S(1)} %get-tuple-element.32), channel_id=1, source_target_pairs={{0,3},{1,0},{2,1},{3,2},{4,7},{5,4},{6,5},{7,6},{8,11},{9,8},{10,9... | collective-permute-start | bytes 294920 | tf_op jit(solution)/shard_map/ppermute | solution.py:452
  36.4 0.0 collective-permute-start.9
  36.4 0.5 collective-permute-start.10
  37.0 1.4 %collective-permute-done.3.rest_0_ = bf16[48,1024]{1,0:T(8,128)(2,1)S(1)} collective-permute-done((bf16[48,1024]{1,0:T(8,128)(2,1)S(1)}, bf16[48,1024]{1,0:T(8,128)(2,1)S(1)}, u32[]{:S(2)}, u32[]{:S(2)}) %collective-permute-start.3) | collective-permute-done | bytes 98336 | tf_op jit(solution)/shard_map/ppermute | solution.py:452
  38.4 0.1 collective-permute-start.11
  38.4 2.7 %collective-permute-done.4.rest_1_ = bf16[48,1024]{1,0:T(8,128)(2,1)S(1)} collective-permute-done((bf16[48,1024]{1,0:T(8,128)(2,1)S(1)}, bf16[48,1024]{1,0:T(8,128)(2,1)S(1)}, u32[]{:S(2)}, u32[]{:S(2)}) %collective-permute-start.4) | collective-permute-done | bytes 98336 | tf_op jit(solution)/shard_map/ppermute | solution.py:452
  41.1 0.1 collective-permute-done.5.rest_2_
  41.2 0.7 sum_terms.2.rest_0_.hidden
  41.9 0.0 slice-start.1
  41.9 3.4 %collective-permute-start.8 = (bf16[48,1024]{1,0:T(8,128)(2,1)S(1)}, bf16[48,1024]{1,0:T(8,128)(2,1)S(1)}, u32[]{:S(2)}, u32[]{:S(2)}) collective-permute-start(bf16[48,1024]{1,0:T(8,128)(2,1)S(1)} %sum_terms.2.rest_0_.hidden), channel_id=1, source_target_pairs={{0,3},{1,0},{2,1},{3,2},{4,7},{5,4},{6,5},{7,6},{8,11},{9,8},{10,9... | collective-permute-start | bytes 294920 | tf_op jit(solution)/shard_map/ppermute | solution.py:452
  45.3 0.4 collective-permute-start.7
  45.7 1.9 %collective-permute-done.8.rest_3_ = bf16[48,1024]{1,0:T(8,128)(2,1)S(1)} collective-permute-done((bf16[48,1024]{1,0:T(8,128)(2,1)S(1)}, bf16[48,1024]{1,0:T(8,128)(2,1)S(1)}, u32[]{:S(2)}, u32[]{:S(2)}) %collective-permute-start.8) | collective-permute-done | bytes 98336 | tf_op jit(solution)/shard_map/ppermute | solution.py:452
  47.5 5.4 %collective-permute-start.6 = (bf16[48,1024]{1,0:T(8,128)(2,1)S(1)}, bf16[48,1024]{1,0:T(8,128)(2,1)S(1)}, u32[]{:S(2)}, u32[]{:S(2)}) collective-permute-start(bf16[48,1024]{1,0:T(8,128)(2,1)S(1)} %sum_terms.2.rest_0_.hidden), channel_id=1, source_target_pairs={{0,1},{1,2},{2,3},{3,0},{4,5},{5,6},{6,7},{7,4},{8,9},{9,10},{10,1... | collective-permute-start | bytes 294920 | tf_op jit(solution)/shard_map/ppermute | solution.py:452
  53.0 0.5 collective-permute-done.7.rest_2_
  53.5 1.7 %collective-permute-done.6.rest_1_ = bf16[48,1024]{1,0:T(8,128)(2,1)S(1)} collective-permute-done((bf16[48,1024]{1,0:T(8,128)(2,1)S(1)}, bf16[48,1024]{1,0:T(8,128)(2,1)S(1)}, u32[]{:S(2)}, u32[]{:S(2)}) %collective-permute-start.6) | collective-permute-done | bytes 98336 | tf_op jit(solution)/shard_map/ppermute | solution.py:452
  55.2 0.0 collective-permute-done.9.rest_4_.rest_0_
  55.2 0.0 collective-permute-done.10.rest_5_.rest_1_
  55.2 0.0 collective-permute-done.11.rest_6_.rest_2_
  55.2 0.0 copy-done.4
  55.2 0.0 copy-done.7
  55.2 10.1 %second_step.1 = (f32[48,128]{1,0:T(8,128)S(1)}, f32[48,128]{1,0:T(8,128)S(1)}, f32[48,1024]{1,0:T(8,128)S(1)}, bf16[48,1024]{1,0:T(8,128)(2,1)S(1)}, bf16[48,10...) custom-call(s32[2]{0:T(128)S(1)} %pad_add_fusion.meta, s32[192]{0:T(256)S(1)} %copy-done.13, s32[192]{0:T(256)S(1)} %copy-done.15, ...), custom_call_target="tpu_custom_call" | custom-call | flops 905969664 | bytes 18874368 | tf_op jit(solution)/shard_map/second_step/pallas_call | solution.py:561
  65.3 2.5 %collective-permute-start.12 = (bf16[48,1024]{1,0:T(8,128)(2,1)S(1)}, bf16[48,1024]{1,0:T(8,128)(2,1)S(1)}, u32[]{:S(2)}, u32[]{:S(2)}) collective-permute-start(bf16[48,1024]{1,0:T(8,128)(2,1)S(1)} %get-tuple-element.37), channel_id=1, source_target_pairs={{0,1},{1,2},{2,3},{3,0},{4,5},{5,6},{6,7},{7,4},{8,9},{9,10},{10,1... | collective-permute-start | bytes 294920 | tf_op jit(solution)/shard_map/ppermute | solution.py:452
  67.8 0.0 collective-permute-start.13
  67.8 2.4 %collective-permute-start.14 = (bf16[48,1024]{1,0:T(8,128)(2,1)S(1)}, bf16[48,1024]{1,0:T(8,128)(2,1)S(1)}, u32[]{:S(2)}, u32[]{:S(2)}) collective-permute-start(bf16[48,1024]{1,0:T(8,128)(2,1)S(1)} %get-tuple-element.39), channel_id=1, source_target_pairs={{0,3},{1,0},{2,1},{3,2},{4,7},{5,4},{6,5},{7,6},{8,11},{9,8},{10,9... | collective-permute-start | bytes 294920 | tf_op jit(solution)/shard_map/ppermute | solution.py:452
  70.2 1.6 %collective-permute-done.12.rest_0_ = bf16[48,1024]{1,0:T(8,128)(2,1)S(1)} collective-permute-done((bf16[48,1024]{1,0:T(8,128)(2,1)S(1)}, bf16[48,1024]{1,0:T(8,128)(2,1)S(1)}, u32[]{:S(2)}, u32[]{:S(2)}) %collective-permute-start.12) | collective-permute-done | bytes 98336 | tf_op jit(solution)/shard_map/ppermute | solution.py:452
  71.8 2.7 %collective-permute-done.13.rest_1_ = bf16[48,1024]{1,0:T(8,128)(2,1)S(1)} collective-permute-done((bf16[48,1024]{1,0:T(8,128)(2,1)S(1)}, bf16[48,1024]{1,0:T(8,128)(2,1)S(1)}, u32[]{:S(2)}, u32[]{:S(2)}) %collective-permute-start.13) | collective-permute-done | bytes 98336 | tf_op jit(solution)/shard_map/ppermute | solution.py:452
  74.6 0.0 collective-permute-done.14.rest_2_
  74.6 0.6 sum_terms.3.rest_0_
  75.2 4.5 %collective-permute-start.17 = (bf16[48,1024]{1,0:T(8,128)(2,1)S(1)}, bf16[48,1024]{1,0:T(8,128)(2,1)S(1)}, u32[]{:S(2)}, u32[]{:S(2)}) collective-permute-start(bf16[48,1024]{1,0:T(8,128)(2,1)S(1)} %sum_terms.3.rest_0_), channel_id=1, source_target_pairs={{0,3},{1,0},{2,1},{3,2},{4,7},{5,4},{6,5},{7,6},{8,11},{9,8},{10,9... | collective-permute-start | bytes 294920 | tf_op jit(solution)/shard_map/ppermute | solution.py:452
  79.7 1.7 %collective-permute-start.16 = (bf16[48,1024]{1,0:T(8,128)(2,1)S(1)}, bf16[48,1024]{1,0:T(8,128)(2,1)S(1)}, u32[]{:S(2)}, u32[]{:S(2)}) collective-permute-start(bf16[48,1024]{1,0:T(8,128)(2,1)S(1)} %sum_terms.3.rest_0_), channel_id=1, source_target_pairs={{0,2},{1,3},{2,0},{3,1},{4,6},{5,7},{6,4},{7,5},{8,10},{9,11},{10,... | collective-permute-start | bytes 294920 | tf_op jit(solution)/shard_map/ppermute | solution.py:452
  81.4 0.0 collective-permute-start.15
  81.4 4.2 %write_cache.1 = bf16[48,2,256,128]{3,2,1,0:T(8,128)(2,1)} custom-call(s32[2]{0:T(128)S(1)} %pad_add_fusion.meta, s32[192]{0:T(256)S(1)} %copy-done.13, s32[192]{0:T(256)S(1)} %copy-done.15, s32[6]{0:T(128)S(1)} %get-tuple-element.22.plan, f32[48,128]{1,0:T(8,128)S(1)} %get-tuple-element.24.newkey.newkey1, ...), custom_call_target="tpu_custom_call" | custom-call | bytes 12582912 | tf_op jit(solution)/shard_map/write_cache/pallas_call | solution.py:586
  85.7 0.0 collective-permute-done.17.rest_3_
  85.7 0.4 collective-permute-done.16.rest_2_
  86.1 1.7 %collective-permute-done.15.rest_1_ = bf16[48,1024]{1,0:T(8,128)(2,1)S(1)} collective-permute-done((bf16[48,1024]{1,0:T(8,128)(2,1)S(1)}, bf16[48,1024]{1,0:T(8,128)(2,1)S(1)}, u32[]{:S(2)}, u32[]{:S(2)}) %collective-permute-start.15) | collective-permute-done | bytes 98336 | tf_op jit(solution)/shard_map/ppermute | solution.py:452
  87.8 1.3 %join.1 = bf16[48,4096]{1,0:T(8,128)(2,1)} custom-call(s32[2]{0:T(128)S(1)} %pad_add_fusion.meta, bf16[48,1024]{1,0:T(8,128)(2,1)S(1)} %sum_terms.3.rest_0_, bf16[48,1024]{1,0:T(8,128)(2,1)S(1)} %collective-permute-done.15.rest_1_, bf16[48,1024]{1,0:T(8,128)(2,1)S(1)} %collective-permute-done.16.rest_2_, bf16[48,1024]{1,0:T(8,128)(2,1)S(1)} %collective-permute-done.17.rest_3_), custom_call_target="tpu_custom_call" | custom-call | tf_op jit(solution)/shard_map/join/pallas_call | solution.py:601
  (18 shorter events, 0.0 us)
Async XLA Ops:
  0.7 2.8 %copy-start = (bf16[48,2,256,128]{3,2,1,0:T(8,128)(2,1)S(1)}, bf16[48,2,256,128]{3,2,1,0:T(8,128)(2,1)}, u32[]{:S(2)}) copy-start(bf16[48,2,256,128]{3,2,1,0:T(8,128)(2,1)} %cache_hbm.7) | copy-start | bytes 18874372
  3.5 2.2 %copy-start.1 = (bf16[4096,512]{1,0:T(8,128)(2,1)S(1)}, bf16[4096,512]{1,0:T(8,128)(2,1)}, u32[]{:S(2)}) copy-start(bf16[4096,512]{1,0:T(8,128)(2,1)} %wq_hbm.3) | copy-start | bytes 12582916
  5.7 1.6 %copy-start.3 = (bf16[4096,2,128]{2,1,0:T(2,128)(2,1)S(1)}, bf16[4096,2,128]{2,1,0:T(2,128)(2,1)}, u32[]{:S(2)}) copy-start(bf16[4096,2,128]{2,1,0:T(2,128)(2,1)} %param.16) | copy-start | bytes 6291460
  7.3 1.0 %copy-start.5 = (bf16[48,4096]{1,0:T(8,128)(2,1)S(1)}, bf16[48,4096]{1,0:T(8,128)(2,1)}, u32[]{:S(2)}) copy-start(bf16[48,4096]{1,0:T(8,128)(2,1)} %hidden.3) | copy-start | bytes 1179652
  8.3 0.9 %copy-start.6 = (f32[256,128]{1,0:T(8,128)S(1)}, f32[256,128]{1,0:T(8,128)}, u32[]{:S(2)}) copy-start(f32[256,128]{1,0:T(8,128)} %constant.12.clone.sin_ref) | copy-start | bytes 393220
  9.2 0.9 %copy-start.8 = (f32[256,128]{1,0:T(8,128)S(1)}, f32[256,128]{1,0:T(8,128)}, u32[]{:S(2)}) copy-start(f32[256,128]{1,0:T(8,128)} %constant.11.clone.cos_ref) | copy-start | bytes 393220
  10.1 0.7 copy-start.10
  10.8 0.7 copy-start.12
  11.5 0.7 copy-start.14
  19.1 9.2 %copy-start.2 = (bf16[512,4096]{1,0:T(8,128)(2,1)S(1)}, bf16[512,4096]{1,0:T(8,128)(2,1)}, u32[]{:S(2)}) copy-start(bf16[512,4096]{1,0:T(8,128)(2,1)} %wo_hbm.3) | copy-start | bytes 12582916
  19.1 9.1 %collective-permute-start = (f32[2,1536]{1,0:T(2,128)S(1)}, f32[2,1536]{1,0:T(2,128)S(1)}, u32[]{:S(2)}, u32[]{:S(2)}) collective-permute-start(f32[2,1536]{1,0:T(2,128)S(1)} %get-tuple-element.26), channel_id=1, source_target_pairs={{0,4},{4,8},{8,12},{12,0},{1,5},{5,9},{9,13},{13,1},{2,6},{6,10},{... | collective-permute-start | bytes 36872 | tf_op jit(solution)/shard_map/ppermute | solution.py:452
  19.6 8.6 %collective-permute-start.1 = (f32[2,1536]{1,0:T(2,128)S(1)}, f32[2,1536]{1,0:T(2,128)S(1)}, u32[]{:S(2)}, u32[]{:S(2)}) collective-permute-start(f32[2,1536]{1,0:T(2,128)S(1)} %get-tuple-element.27), channel_id=1, source_target_pairs={{0,8},{4,12},{8,0},{12,4},{1,9},{5,13},{9,1},{13,5},{2,10},{6,14},... | collective-permute-start | bytes 36872 | tf_op jit(solution)/shard_map/ppermute | solution.py:452
  22.2 6.0 %collective-permute-start.2 = (f32[2,1536]{1,0:T(2,128)S(1)}, f32[2,1536]{1,0:T(2,128)S(1)}, u32[]{:S(2)}, u32[]{:S(2)}) collective-permute-start(f32[2,1536]{1,0:T(2,128)S(1)} %get-tuple-element.28), channel_id=1, source_target_pairs={{0,12},{4,0},{8,4},{12,8},{1,13},{5,1},{9,5},{13,9},{2,14},{6,2},{... | collective-permute-start | bytes 36872 | tf_op jit(solution)/shard_map/ppermute | solution.py:452
  28.2 27.0 %copy-start.4 = (bf16[4096,2,128]{2,1,0:T(2,128)(2,1)S(1)}, bf16[4096,2,128]{2,1,0:T(2,128)(2,1)}, u32[]{:S(2)}) copy-start(bf16[4096,2,128]{2,1,0:T(2,128)(2,1)} %param.16) | copy-start | bytes 6291460
  28.2 27.0 %copy-start.7 = (f32[256,128]{1,0:T(8,128)S(1)}, f32[256,128]{1,0:T(8,128)}, u32[]{:S(2)}) copy-start(f32[256,128]{1,0:T(8,128)} %constant.12.clone.sin_ref) | copy-start | bytes 393220
  28.2 27.0 %copy-start.9 = (f32[256,128]{1,0:T(8,128)S(1)}, f32[256,128]{1,0:T(8,128)}, u32[]{:S(2)}) copy-start(f32[256,128]{1,0:T(8,128)} %constant.11.clone.cos_ref) | copy-start | bytes 393220
  28.2 27.0 %copy-start.11 = (f32[4096]{0:T(1024)S(1)}, f32[4096]{0:T(1024)}, u32[]{:S(2)}) copy-start(f32[4096]{0:T(1024)} %param.14) | copy-start | bytes 49156
  28.2 27.0 %copy-start.13 = (s32[192]{0:T(256)S(1)}, s32[192]{0:T(256)}, u32[]{:S(2)}) copy-start(s32[192]{0:T(256)} %source_s.5) | copy-start | bytes 2308
  28.2 27.0 %copy-start.15 = (s32[192]{0:T(256)S(1)}, s32[192]{0:T(256)}, u32[]{:S(2)}) copy-start(s32[192]{0:T(256)} %lengths_s.7) | copy-start | bytes 2308
  30.9 7.5 %collective-permute-start.3 = (bf16[48,1024]{1,0:T(8,128)(2,1)S(1)}, bf16[48,1024]{1,0:T(8,128)(2,1)S(1)}, u32[]{:S(2)}, u32[]{:S(2)}) collective-permute-start(bf16[48,1024]{1,0:T(8,128)(2,1)S(1)} %get-tuple-element.30), channel_id=1, source_target_pairs={{0,1},{1,2},{2,3},{3,0},{4,5},{5,6},{6,7},{7,4},{8,9},{9,10},{10,1... | collective-permute-start | bytes 294920 | tf_op jit(solution)/shard_map/ppermute | solution.py:452
  32.5 8.6 %collective-permute-start.4 = (bf16[48,1024]{1,0:T(8,128)(2,1)S(1)}, bf16[48,1024]{1,0:T(8,128)(2,1)S(1)}, u32[]{:S(2)}, u32[]{:S(2)}) collective-permute-start(bf16[48,1024]{1,0:T(8,128)(2,1)S(1)} %get-tuple-element.31), channel_id=1, source_target_pairs={{0,2},{1,3},{2,0},{3,1},{4,6},{5,7},{6,4},{7,5},{8,10},{9,11},{10,... | collective-permute-start | bytes 294920 | tf_op jit(solution)/shard_map/ppermute | solution.py:452
  35.1 6.1 %collective-permute-start.5 = (bf16[48,1024]{1,0:T(8,128)(2,1)S(1)}, bf16[48,1024]{1,0:T(8,128)(2,1)S(1)}, u32[]{:S(2)}, u32[]{:S(2)}) collective-permute-start(bf16[48,1024]{1,0:T(8,128)(2,1)S(1)} %get-tuple-element.32), channel_id=1, source_target_pairs={{0,3},{1,0},{2,1},{3,2},{4,7},{5,4},{6,5},{7,6},{8,11},{9,8},{10,9... | collective-permute-start | bytes 294920 | tf_op jit(solution)/shard_map/ppermute | solution.py:452
  36.4 18.7 %collective-permute-start.9 = (bf16[2,2,256,128]{3,2,1,0:T(8,128)(2,1)S(1)}, bf16[2,2,256,128]{3,2,1,0:T(8,128)(2,1)S(1)}, u32[]{:S(2)}, u32[]{:S(2)}) collective-permute-start(bf16[2,2,256,128]{3,2,1,0:T(8,128)(2,1)S(1)} %get-tuple-element.33), channel_id=1, source_target_pairs={{0,4},{4,8},{8,12},{12,0},{1,5},{5,9},{9,13},{13,1},{2,6},{6,10},{... | collective-permute-start | bytes 786440 | tf_op jit(solution)/shard_map/ppermute | solution.py:452
  36.4 18.7 %collective-permute-start.10 = (bf16[2,2,256,128]{3,2,1,0:T(8,128)(2,1)S(1)}, bf16[2,2,256,128]{3,2,1,0:T(8,128)(2,1)S(1)}, u32[]{:S(2)}, u32[]{:S(2)}) collective-permute-start(bf16[2,2,256,128]{3,2,1,0:T(8,128)(2,1)S(1)} %get-tuple-element.34), channel_id=1, source_target_pairs={{0,8},{4,12},{8,0},{12,4},{1,9},{5,13},{9,1},{13,5},{2,10},{6,14},... | collective-permute-start | bytes 786440 | tf_op jit(solution)/shard_map/ppermute | solution.py:452
  38.4 16.8 %collective-permute-start.11 = (bf16[2,2,256,128]{3,2,1,0:T(8,128)(2,1)S(1)}, bf16[2,2,256,128]{3,2,1,0:T(8,128)(2,1)S(1)}, u32[]{:S(2)}, u32[]{:S(2)}) collective-permute-start(bf16[2,2,256,128]{3,2,1,0:T(8,128)(2,1)S(1)} %get-tuple-element.35), channel_id=1, source_target_pairs={{0,12},{4,0},{8,4},{12,8},{1,13},{5,1},{9,5},{13,9},{2,14},{6,2},{... | collective-permute-start | bytes 786440 | tf_op jit(solution)/shard_map/ppermute | solution.py:452
  41.2 40.2 %slice-start = ((s8[6291456]{0:T(1024)(128)(4,1)}), s8[4194304]{0:T(1024)(128)(4,1)S(1)}, s32[]{:S(2)}) async-start(s8[6291456]{0:T(1024)(128)(4,1)} %bitcast.5), calls=%async_computation | async-start | bytes 8388608
  41.9 39.5 %slice-start.1 = ((s8[6291456]{0:T(1024)(128)(4,1)}), s8[2097152]{0:T(1024)(128)(4,1)S(1)}, s32[]{:S(2)}) async-start(s8[6291456]{0:T(1024)(128)(4,1)} %bitcast.5), calls=%async_computation.1 | async-start | bytes 4194304
  41.9 5.6 %collective-permute-start.8 = (bf16[48,1024]{1,0:T(8,128)(2,1)S(1)}, bf16[48,1024]{1,0:T(8,128)(2,1)S(1)}, u32[]{:S(2)}, u32[]{:S(2)}) collective-permute-start(bf16[48,1024]{1,0:T(8,128)(2,1)S(1)} %sum_terms.2.rest_0_.hidden), channel_id=1, source_target_pairs={{0,3},{1,0},{2,1},{3,2},{4,7},{5,4},{6,5},{7,6},{8,11},{9,8},{10,9... | collective-permute-start | bytes 294920 | tf_op jit(solution)/shard_map/ppermute | solution.py:452
  45.3 8.1 %collective-permute-start.7 = (bf16[48,1024]{1,0:T(8,128)(2,1)S(1)}, bf16[48,1024]{1,0:T(8,128)(2,1)S(1)}, u32[]{:S(2)}, u32[]{:S(2)}) collective-permute-start(bf16[48,1024]{1,0:T(8,128)(2,1)S(1)} %sum_terms.2.rest_0_.hidden), channel_id=1, source_target_pairs={{0,2},{1,3},{2,0},{3,1},{4,6},{5,7},{6,4},{7,5},{8,10},{9,11},{10,... | collective-permute-start | bytes 294920 | tf_op jit(solution)/shard_map/ppermute | solution.py:452
  47.5 7.6 %collective-permute-start.6 = (bf16[48,1024]{1,0:T(8,128)(2,1)S(1)}, bf16[48,1024]{1,0:T(8,128)(2,1)S(1)}, u32[]{:S(2)}, u32[]{:S(2)}) collective-permute-start(bf16[48,1024]{1,0:T(8,128)(2,1)S(1)} %sum_terms.2.rest_0_.hidden), channel_id=1, source_target_pairs={{0,1},{1,2},{2,3},{3,0},{4,5},{5,6},{6,7},{7,4},{8,9},{9,10},{10,1... | collective-permute-start | bytes 294920 | tf_op jit(solution)/shard_map/ppermute | solution.py:452
  65.3 6.5 %collective-permute-start.12 = (bf16[48,1024]{1,0:T(8,128)(2,1)S(1)}, bf16[48,1024]{1,0:T(8,128)(2,1)S(1)}, u32[]{:S(2)}, u32[]{:S(2)}) collective-permute-start(bf16[48,1024]{1,0:T(8,128)(2,1)S(1)} %get-tuple-element.37), channel_id=1, source_target_pairs={{0,1},{1,2},{2,3},{3,0},{4,5},{5,6},{6,7},{7,4},{8,9},{9,10},{10,1... | collective-permute-start | bytes 294920 | tf_op jit(solution)/shard_map/ppermute | solution.py:452
  67.8 6.8 %collective-permute-start.13 = (bf16[48,1024]{1,0:T(8,128)(2,1)S(1)}, bf16[48,1024]{1,0:T(8,128)(2,1)S(1)}, u32[]{:S(2)}, u32[]{:S(2)}) collective-permute-start(bf16[48,1024]{1,0:T(8,128)(2,1)S(1)} %get-tuple-element.38), channel_id=1, source_target_pairs={{0,2},{1,3},{2,0},{3,1},{4,6},{5,7},{6,4},{7,5},{8,10},{9,11},{10,... | collective-permute-start | bytes 294920 | tf_op jit(solution)/shard_map/ppermute | solution.py:452
  67.8 6.8 %collective-permute-start.14 = (bf16[48,1024]{1,0:T(8,128)(2,1)S(1)}, bf16[48,1024]{1,0:T(8,128)(2,1)S(1)}, u32[]{:S(2)}, u32[]{:S(2)}) collective-permute-start(bf16[48,1024]{1,0:T(8,128)(2,1)S(1)} %get-tuple-element.39), channel_id=1, source_target_pairs={{0,3},{1,0},{2,1},{3,2},{4,7},{5,4},{6,5},{7,6},{8,11},{9,8},{10,9... | collective-permute-start | bytes 294920 | tf_op jit(solution)/shard_map/ppermute | solution.py:452
  75.2 10.5 %collective-permute-start.17 = (bf16[48,1024]{1,0:T(8,128)(2,1)S(1)}, bf16[48,1024]{1,0:T(8,128)(2,1)S(1)}, u32[]{:S(2)}, u32[]{:S(2)}) collective-permute-start(bf16[48,1024]{1,0:T(8,128)(2,1)S(1)} %sum_terms.3.rest_0_), channel_id=1, source_target_pairs={{0,3},{1,0},{2,1},{3,2},{4,7},{5,4},{6,5},{7,6},{8,11},{9,8},{10,9... | collective-permute-start | bytes 294920 | tf_op jit(solution)/shard_map/ppermute | solution.py:452
  79.7 6.4 %collective-permute-start.16 = (bf16[48,1024]{1,0:T(8,128)(2,1)S(1)}, bf16[48,1024]{1,0:T(8,128)(2,1)S(1)}, u32[]{:S(2)}, u32[]{:S(2)}) collective-permute-start(bf16[48,1024]{1,0:T(8,128)(2,1)S(1)} %sum_terms.3.rest_0_), channel_id=1, source_target_pairs={{0,2},{1,3},{2,0},{3,1},{4,6},{5,7},{6,4},{7,5},{8,10},{9,11},{10,... | collective-permute-start | bytes 294920 | tf_op jit(solution)/shard_map/ppermute | solution.py:452
  81.4 6.4 %collective-permute-start.15 = (bf16[48,1024]{1,0:T(8,128)(2,1)S(1)}, bf16[48,1024]{1,0:T(8,128)(2,1)S(1)}, u32[]{:S(2)}, u32[]{:S(2)}) collective-permute-start(bf16[48,1024]{1,0:T(8,128)(2,1)S(1)} %sum_terms.3.rest_0_), channel_id=1, source_target_pairs={{0,1},{1,2},{2,3},{3,0},{4,5},{5,6},{6,7},{7,4},{8,9},{9,10},{10,1... | collective-permute-start | bytes 294920 | tf_op jit(solution)/shard_map/ppermute | solution.py:452

commit v2 on v1

--- a/solution.py
+++ b/solution.py
@@ -23,6 +23,7 @@
 ANY = pl.BlockSpec(memory_space=pl.ANY)
 VMEM = pl.BlockSpec(memory_space=pltpu.VMEM)
 SMEM = pl.BlockSpec(memory_space=pltpu.SMEM)
+HBM = pl.BlockSpec(memory_space=pltpu.HBM)
 
 
 def params(mib):
@@ -65,20 +66,22 @@
     spread[:, slots:, :] = spread_all[:, 2 * HD :].reshape(blocks, slots, 2 * HD)
 
 
-def project(normed3, spread, wq, wkv, wq_copies, wkv_copies, slots, width):
-    pieces = len(wq_copies)
+def project(normed3, spread, wq, wkv, slots, width, wq_copies=(), wkv_copies=()):
+    pieces = max(len(wq_copies), 1)
     depth = width // pieces
     query = None
     pair = None
     for c in range(pieces):
-        wkv_copies[c].wait()
+        for copy in wkv_copies[c : c + 1]:
+            copy.wait()
         for b in range(c * depth // HD, (c + 1) * depth // HD):
             part = jnp.dot(
                 spread[b], wkv[b * 2 * HD : (b + 1) * 2 * HD, :], preferred_element_type=F32
             )
             pair = part if pair is None else pair + part
     for c in range(pieces):
-        wq_copies[c].wait()
+        for copy in wq_copies[c : c + 1]:
+            copy.wait()
         for b in range(c * depth // (2 * HD), (c + 1) * depth // (2 * HD)):
             block = jnp.concatenate([normed3[2 * b], normed3[2 * b + 1]], axis=1)
             part = jnp.dot(
@@ -145,20 +148,29 @@
 
 def first_kernel(
     peers, slots, heads, shard,
-    meta, source_s, lengths_s, source_v, hidden, gain, cos_ref, sin_ref, wq_hbm, wkv_hbm, cache_hbm,
-    query_out, newkey_out, newvalue_out, plan, *rest,
+    meta, source_hbm, lengths_hbm, hidden_hbm, gain_hbm, cos_hbm, sin_hbm, wq_hbm, wkv_hbm,
+    cache_hbm, query_out, newkey_out, newvalue_out, plan, *rest,
 ):
     others = peers - 1
     moving = others * MOVE
     boxes, notes = rest[:others], rest[others : 2 * others]
-    (wq, wkv, normed3, spread, cos_rows, sin_rows, leaving, hidden32,
-     wq_sem, wkv_sem, in_sem, out_sem) = rest[2 * others :]
+    (wq, wkv, normed3, spread, cos_rows, sin_rows, leaving, hidden32, source_s, lengths_s, source_v,
+     hidden, gain, cos_ref, sin_ref, small_sem, wq_sem, wkv_sem, in_sem, out_sem) = rest[2 * others :]
     width = hidden.shape[1]
     me, me_tp = meta[0], meta[1]
     wq_copies = weight_copies(wq_hbm, wq, wq_sem, 4)
     wkv_copies = weight_copies(wkv_hbm, wkv, wkv_sem, 4)
-    for copy in wkv_copies + wq_copies:
+    small = [
+        pltpu.make_async_copy(src, dst, small_sem.at[i])
+        for i, (src, dst) in enumerate((
+            (source_hbm, source_v), (source_hbm, source_s), (lengths_hbm, lengths_s),
+            (hidden_hbm, hidden), (gain_hbm, gain), (cos_hbm, cos_ref), (sin_hbm, sin_ref),
+        ))
+    ]
+    for copy in small + wkv_copies + wq_copies:
         copy.start()
+    small[0].wait()
+    small[1].wait()
 
     low = me * slots
     src = source_v[...]
@@ -168,10 +180,9 @@
     index_f = index.astype(F32)
     send_slots = []
     for k in range(1, peers):
-        to = lax.rem(me + k, peers) * slots
-        sent = mine_goes & (index >= to) & (index < to + slots)
-        origin = lax.rem(me + peers - k, peers) * slots
-        taken = mine_comes & (src >= origin) & (src < origin + slots)
+        other = jnp.bitwise_xor(me, k) * slots
+        sent = mine_goes & (index >= other) & (index < other + slots)
+        taken = mine_comes & (src >= other) & (src < other + slots)
         for m in range(MOVE):
             at = (k - 1) * MOVE + m
             if m == 0:
@@ -181,18 +192,22 @@
                 j = jnp.max(jnp.where(sent, index_f, -1.0)).astype(I32)
                 r = jnp.max(jnp.where(taken, index_f, -1.0)).astype(I32)
             known = (j >= 0) & (j < src.shape[1])
-            slot = source_s[jnp.where(known, j, 0)] - low
+            slot = source_s[0, jnp.where(known, j, 0)] - low
             slot = jnp.where(known, slot, 0)
             send_slots.append(slot)
             plan[at] = jnp.where((r >= 0) & (r < src.shape[1]), r - low, -1)
             pltpu.make_async_copy(cache_hbm.at[slot], leaving.at[at], in_sem.at[at]).start()
 
+    for copy in small[2:]:
+        copy.wait()
     wide = hidden[...].astype(F32)
     hidden32[...] = wide
     norm_into(normed3, [wide], [gain[...]], [0], width)
     spread_normed(normed3, spread, slots, width)
-    gather_angles(lambda s: lengths_s[low + s], slots, cos_ref, sin_ref, cos_rows, sin_rows)
-    query, key, value = project(normed3, spread, wq, wkv, wq_copies, wkv_copies, slots, width)
+    gather_angles(lambda s: lengths_s[0, low + s], slots, cos_ref, sin_ref, cos_rows, sin_rows)
+    query, key, value = project(
+        normed3, spread, wq, wkv, slots, width, wq_copies, wkv_copies
+    )
     cosine, sine = cos_rows[...], sin_rows[...]
     query_out[...] = jnp.zeros(query_out.shape, F32)
     for g in range(heads):
@@ -201,7 +216,7 @@
     newkey_out[...] = turn(key, cosine, sine).astype(BF16).astype(F32)
     newvalue_out[...] = value.astype(BF16).astype(F32)
 
-    positions = [lengths_s[low + slot] for slot in send_slots]
+    positions = [lengths_s[0, low + slot] for slot in send_slots]
     for at, slot in enumerate(send_slots):
         pltpu.make_async_copy(cache_hbm.at[slot], leaving.at[at], in_sem.at[at]).wait()
         put_row(
@@ -227,19 +242,6 @@
         ).wait()
 
 
-def attend_all(buffer, places, positions, query_of, attended_rows, slots):
-    for c in range(slots // CHUNK):
-        span = range(c * CHUNK, (c + 1) * CHUNK)
-        got = attend(
-            buffer,
-            [places[s] for s in span],
-            [positions[s] for s in span],
-            [query_of(s) for s in span],
-        )
-        for s, rows in zip(span, got):
-            attended_rows[s * GROUP : (s + 1) * GROUP, :] = rows
-
-
 def attend_kernel(
     slots, heads, meta, lengths_s, query, newkey, newvalue, cache_hbm, out,
     buffer, attended_rows, in_sem,
@@ -267,37 +269,27 @@
         out[:, g * HD : (g + 1) * HD] = attended_rows[pl.ds(g, slots, stride=GROUP), :].astype(BF16)
 
 
-def project_out(attended, wo, wo_hbm, wo_sem, own, sends, me_tp, peers_tp):
+def project_out(attended, wo, own, sends, me_tp, peers_tp):
     shard = own.shape[1]
-    for k in list(range(1, peers_tp)) + [0]:
-        out_copy(wo, wo_hbm, wo_sem, me_tp, peers_tp, shard, k).wait()
-        part = jnp.dot(attended, wo[k], preferred_element_type=F32)
+    for k in list(range(peers_tp - 1, 0, -1)) + [0]:
+        column = pl.multiple_of(jnp.bitwise_xor(me_tp, k) * shard, shard)
+        part = jnp.dot(attended, wo[:, pl.ds(column, shard)], preferred_element_type=F32)
         if k == 0:
             own[...] = part
         else:
             sends[k - 1][...] = part.astype(BF16)
 
 
-def out_copy(wo, wo_hbm, wo_sem, me_tp, peers_tp, shard, k):
-    column = pl.multiple_of(lax.rem(me_tp + k, peers_tp) * shard, shard)
-    return pltpu.make_async_copy(wo_hbm.at[:, pl.ds(column, shard)], wo.at[k], wo_sem.at[k])
-
-
-def out_kernel(peers, peers_tp, meta, plan, attended, wo_hbm, *rest):
+def out_kernel(peers, peers_tp, meta, plan, attended, wo, *rest):
     notes = rest[: peers - 1]
     own = rest[peers - 1]
-    sends = rest[peers : peers + peers_tp - 1]
-    wo, wo_sem = rest[peers + peers_tp - 1 :]
-    me_tp = meta[1]
-    shard = own.shape[1]
-    for k in list(range(1, peers_tp)) + [0]:
-        out_copy(wo, wo_hbm, wo_sem, me_tp, peers_tp, shard, k).start()
+    sends = rest[peers:]
     rows = attended[...].astype(F32)
     index = lax.broadcasted_iota(I32, rows.shape, 0)
     for at in range((peers - 1) * MOVE):
         note = notes[at // MOVE][at % MOVE : at % MOVE + 1, : rows.shape[1]]
         rows = jnp.where(index == plan[at], note, rows)
-    project_out(rows.astype(BF16), wo, wo_hbm, wo_sem, own, sends, me_tp, peers_tp)
+    project_out(rows.astype(BF16), wo, own, sends, meta[1], peers_tp)
 
 
 def sum_kernel(peers, peers_tp, heads, meta, plan, hidden, own, *rest):
@@ -348,28 +340,24 @@
 def second_kernel(
     peers, peers_tp, slots, heads,
     meta, source_s, lengths_s, plan, gain, cos_ref, sin_ref, newkey1, newvalue1,
-    wq_hbm, wkv_hbm, wo_hbm, cache_hbm, *rest,
+    wq, wkv, wo, cache_hbm, *rest,
 ):
     blocks, rest = rest[:peers_tp], rest[peers_tp:]
     box_hbm, rest = rest[: peers - 1], rest[peers - 1 :]
     newkey, newvalue, own = rest[:3]
     sends, rest = rest[3 : 2 + peers_tp], rest[2 + peers_tp :]
-    (wq, wkv, wo, normed3, spread, cos_rows, sin_rows, buffer, query_rows, attended_rows, place,
-     wq_sem, wkv_sem, wo_sem, in_sem) = rest
+    (normed3, spread, cos_rows, sin_rows, buffer, query_rows, attended_rows, place,
+     in_sem) = rest
     me, me_tp = meta[0], meta[1]
     low = me * slots
     width = gain.shape[1]
     shard = own.shape[1]
-    wq_copies = weight_copies(wq_hbm, wq, wq_sem, 4)
-    wkv_copies = weight_copies(wkv_hbm, wkv, wkv_sem, 4)
     cache_copies = load_slots(slots, peers, cache_hbm, box_hbm, buffer, in_sem)
-    for copy in wkv_copies + wq_copies + cache_copies[::-1]:
+    for copy in cache_copies[::-1]:
         copy.start()
-    for k in list(range(1, peers_tp)) + [0]:
-        out_copy(wo, wo_hbm, wo_sem, me_tp, peers_tp, shard, k).start()
 
     map_places(slots, peers, plan, place)
-    firsts = [lax.rem(me_tp + peers_tp - k, peers_tp) for k in range(peers_tp)]
+    firsts = [jnp.bitwise_xor(me_tp, k) for k in range(peers_tp)]
     norm_into(
         normed3,
         [block[...].astype(F32) for block in blocks],
@@ -380,7 +368,7 @@
     spread_normed(normed3, spread, slots, width)
     lengths = [lengths_s[source_s[low + s]] for s in range(slots)]
     gather_angles(lambda s: lengths[s] + 1, slots, cos_ref, sin_ref, cos_rows, sin_rows)
-    query, key, value = project(normed3, spread, wq, wkv, wq_copies, wkv_copies, slots, width)
+    query, key, value = project(normed3, spread, wq, wkv, slots, width)
     cosine, sine = cos_rows[...], sin_rows[...]
     query_rows[...] = jnp.zeros(query_rows.shape, F32)
     for g in range(heads):
@@ -407,7 +395,7 @@
     attended = jnp.concatenate(
         [attended_rows[pl.ds(g, slots, stride=GROUP), :].astype(BF16) for g in range(heads)], axis=1
     )
-    project_out(attended, wo, wo_hbm, wo_sem, own, sends, me_tp, peers_tp)
+    project_out(attended, wo, own, sends, me_tp, peers_tp)
 
 
 def cache_kernel(
@@ -441,15 +429,19 @@
 
 
 def join_kernel(peers_tp, meta, *rest):
-    blocks, out = rest[:-1], rest[-1]
+    blocks, out, sem = rest[:-2], rest[-2], rest[-1]
     shard = blocks[0].shape[1]
+    copies = []
     for k, block in enumerate(blocks):
-        first = lax.rem(meta[1] + peers_tp - k, peers_tp)
-        out[:, pl.ds(pl.multiple_of(first * shard, shard), shard)] = block[...]
-
-
-def shifted(x, axis, size, k):
-    return lax.ppermute(x, axis, [(i, (i + k) % size) for i in range(size)])
+        column = pl.multiple_of(jnp.bitwise_xor(meta[1], k) * shard, shard)
+        copies.append(pltpu.make_async_copy(block, out.at[:, pl.ds(column, shard)], sem.at[k]))
+        copies[-1].start()
+    for copy in copies:
+        copy.wait()
+
+
+def swapped(x, axis, size, k):
+    return lax.ppermute(x, axis, [(i, i ^ k) for i in range(size)])
 
 
 def local(
@@ -492,26 +484,34 @@
         ]
         + [jax.ShapeDtypeStruct((MOVE,) + kv_cache.shape[1:], BF16)] * others
         + [jax.ShapeDtypeStruct((MOVE, note_width), F32)] * others,
-        in_specs=[SMEM] * 3 + [VMEM] * 5 + [ANY] * 3,
+        in_specs=[SMEM] + [HBM] * 9,
         out_specs=[VMEM] * 3 + [SMEM] + [ANY] * others + [VMEM] * others,
         scratch_shapes=weights
         + stages
         + [
             pltpu.VMEM((moving,) + kv_cache.shape[1:], BF16),
             pltpu.VMEM((slots, width), F32),
+            pltpu.SMEM((1, source.shape[0]), I32),
+            pltpu.SMEM((1, source.shape[0]), I32),
+            pltpu.VMEM((1, source.shape[0]), I32),
+            pltpu.VMEM(hidden.shape, BF16),
+            pltpu.VMEM((1, width), F32),
+            pltpu.VMEM(cosine.shape, F32),
+            pltpu.VMEM(cosine.shape, F32),
+            dma((7,)),
             dma((4,)),
             dma((4,)),
             dma((moving,)),
             dma((others,)),
         ],
-        compiler_params=params(40),
+        compiler_params=params(24),
         cost_estimate=cost(flops, (query_weight.size + wkv.size) * 2),
         name="first_step",
-    )(meta, source, lengths, source.reshape(1, -1), hidden, gain, cosine, sine, query_weight, wkv,
-      kv_cache)
+    )(meta, source.reshape(1, -1), lengths.reshape(1, -1), hidden, gain, cosine, sine, query_weight,
+      wkv, kv_cache)
     boxes, notes = rest[:others], rest[others:]
-    got_notes = [shifted(note, "inst", peers, k + 1) for k, note in enumerate(notes)]
-    got_boxes = [shifted(box, "inst", peers, k + 1) for k, box in enumerate(boxes)]
+    got_notes = [swapped(note, "inst", peers, k + 1) for k, note in enumerate(notes)]
+    got_boxes = [swapped(box, "inst", peers, k + 1) for k, box in enumerate(boxes)]
 
     attended = pl.pallas_call(
         functools.partial(attend_kernel, slots, heads),
@@ -530,20 +530,18 @@
 
     sent = [jax.ShapeDtypeStruct((slots, shard), F32)]
     sent += [jax.ShapeDtypeStruct((slots, shard), BF16)] * (peers_tp - 1)
-    wo_scratch = pltpu.VMEM((peers_tp, heads * HD, shard), BF16)
     own, *sends = pl.pallas_call(
         functools.partial(out_kernel, peers, peers_tp),
         out_shape=sent,
-        in_specs=[SMEM] * 2 + [VMEM, ANY] + [VMEM] * others,
+        in_specs=[SMEM] * 2 + [VMEM] * (2 + others),
         out_specs=[VMEM] * peers_tp,
-        scratch_shapes=[wo_scratch, dma((peers_tp,))],
-        compiler_params=params(24),
+        compiler_params=params(16),
         cost_estimate=cost(2 * slots * width * heads * HD, out_weight.size * 2),
         name="out_projection",
     )(meta, plan, attended, out_weight, *got_notes)
 
     def summed(residual, own, sends, notes):
-        got = [shifted(part, "tp", peers_tp, k + 1) for k, part in enumerate(sends)]
+        got = [swapped(sends[k - 1], "tp", peers_tp, k) for k in range(peers_tp - 1, 0, -1)]
         shard_rows = pl.pallas_call(
             functools.partial(sum_kernel, peers, peers_tp, heads),
             out_shape=jax.ShapeDtypeStruct((slots, shard), BF16),
@@ -553,7 +551,7 @@
             name="sum_terms",
         )(meta, plan, residual, own, *got, *notes)
         return [shard_rows] + [
-            shifted(shard_rows, "tp", peers_tp, k) for k in range(1, peers_tp)
+            swapped(shard_rows, "tp", peers_tp, k) for k in range(1, peers_tp)
         ]
 
     pieces = summed(hidden, own, sends, got_notes)
@@ -561,22 +559,17 @@
     newkey2, newvalue2, own, *sends = pl.pallas_call(
         functools.partial(second_kernel, peers, peers_tp, slots, heads),
         out_shape=[row32, row32] + sent,
-        in_specs=[SMEM] * 4 + [VMEM] * 5 + [ANY] * 4 + [VMEM] * peers_tp + [ANY] * others,
+        in_specs=[SMEM] * 4 + [VMEM] * 8 + [ANY] + [VMEM] * peers_tp + [ANY] * others,
         out_specs=[VMEM] * (2 + peers_tp),
-        scratch_shapes=weights
-        + [wo_scratch]
-        + stages
+        scratch_shapes=stages
         + [
             pltpu.VMEM((slots + moving,) + kv_cache.shape[1:], BF16),
             pltpu.VMEM((slots * GROUP, HD), F32),
             pltpu.VMEM((slots * GROUP, HD), F32),
             pltpu.SMEM((slots,), I32),
-            dma((4,)),
-            dma((4,)),
-            dma((peers_tp,)),
             dma((slots // CHUNK + others,)),
         ],
-        compiler_params=params(48),
+        compiler_params=params(32),
         cost_estimate=cost(3 * flops, cache_bytes + (query_weight.size + wkv.size) * 4),
         name="second_step",
     )(meta, source, lengths, plan, gain, cosine, sine, newkey1, newvalue1, query_weight, wkv,
@@ -601,8 +594,9 @@
     final_hidden = pl.pallas_call(
         functools.partial(join_kernel, peers_tp),
         out_shape=jax.ShapeDtypeStruct(hidden.shape, BF16),
-        in_specs=[SMEM] + [VMEM] * peers_tp,
-        out_specs=VMEM,
+        in_specs=[SMEM] + [ANY] * peers_tp,
+        out_specs=ANY,
+        scratch_shapes=[dma((peers_tp,))],
         compiler_params=params(16),
         name="join",
     )(meta, *pieces)

time: 89.5 us -> 85.4 us (0.954)
  starting transfers between devices: 31 us -> 24.4 us
  waiting for transfers between devices: 14.8 us -> 21 us
  Pallas kernels: 31 us -> 27.2 us
    ppermute x18, starting transfers between devices: 31 us -> 24.4 us  [swapped(): return lax.ppermute(x, axis, [(i, i ^ k) for i in range(size)])]
    ppermute x18, waiting for transfers between devices: 14.8 us -> 21 us  [swapped(): return lax.ppermute(x, axis, [(i, i ^ k) for i in range(size)])]
    pallas_call x1, Pallas kernels: 10.1 us -> 6.79 us  [local(): pl.pallas_call(functools.partial(second_kernel, peers, peers_tp, slots, h...]
    pallas_call x1, Pallas kernels: 2.59 us -> 1.4 us  [local(): pl.pallas_call(functools.partial(out_kernel, peers, peers_tp), out_shape=...]
    unnamed x36 -> x38, local copies, waits for them, and re-layouts: 11.5 us -> 11.5 us
  transfers between devices with their start and end apart: 18 -> 18, of which waited for: 10 -> 8; matrix products, arithmetic and copies ran while one was open for 0% -> 0% of each run, Pallas kernels for 11% -> 11%
where the time goes in v2:
time: 85.4 us; the launch traced here: 85 us
  Pallas kernels  27.2 us (32%)
  starting transfers between devices  24.4 us (29%)
  waiting for transfers between devices  21 us (25%)
  local copies, waits for them, and re-layouts  11.5 us (13%)
  between operations  0.88 us (1%)
    ppermute x18, starting transfers between devices, swapped(): return lax.ppermute(x, axis, [(i, i ^ k) for i in range(size)])  24.4 us
    ppermute x18, waiting for transfers between devices, swapped(): return lax.ppermute(x, axis, [(i, i ^ k) for i in range(size)])  21 us
    unnamed x38, local copies, waits for them, and re-layouts  11.5 us
    pallas_call x1, Pallas kernels, local(): pl.pallas_call(functools.partial(first_kernel, peers, slots, heads, shard...  7.61 us
    pallas_call x1, Pallas kernels, local(): pl.pallas_call(functools.partial(second_kernel, peers, peers_tp, slots, h...  6.79 us
    pallas_call x1, Pallas kernels, local(): pl.pallas_call(functools.partial(attend_kernel, slots, heads), out_shape=...  4.56 us
    pallas_call x1, Pallas kernels, local(): pl.pallas_call(functools.partial(cache_kernel, peers, slots), out_shape=j...  4.23 us
  transfers between devices with their start and end apart: 18, of which 8 were waited for; matrix products, arithmetic and copies ran while one was open for 0% of the time, Pallas kernels for 11%

profile of v2, /device:TPU:0, one launch (start us, length us, event | category | flops | bytes accessed | tf_op | source)
XLA Modules:
  0.0 85.0 jit_solution(4278008497336956747)
XLA Ops:
  0.6 0.1 pad_add_fusion.meta
  0.7 2.8 %copy-done = bf16[48,2,256,128]{3,2,1,0:T(8,128)(2,1)S(1)} copy-done((bf16[48,2,256,128]{3,2,1,0:T(8,128)(2,1)S(1)}, bf16[48,2,256,128]{3,2,1,0:T(8,128)(2,1)}, u32[]{:S(2)}) %copy-start) | copy-done | bytes 6291480
  3.5 2.2 %copy-done.1 = bf16[4096,512]{1,0:T(8,128)(2,1)S(1)} copy-done((bf16[4096,512]{1,0:T(8,128)(2,1)S(1)}, bf16[4096,512]{1,0:T(8,128)(2,1)}, u32[]{:S(2)}) %copy-start.1) | copy-done | bytes 4194328
  5.7 1.6 %copy-done.4 = bf16[4096,2,128]{2,1,0:T(2,128)(2,1)S(1)} copy-done((bf16[4096,2,128]{2,1,0:T(2,128)(2,1)S(1)}, bf16[4096,2,128]{2,1,0:T(2,128)(2,1)}, u32[]{:S(2)}) %copy-start.4) | copy-done | bytes 2097176
  7.3 1.0 %copy-done.6 = bf16[48,4096]{1,0:T(8,128)(2,1)S(1)} copy-done((bf16[48,4096]{1,0:T(8,128)(2,1)S(1)}, bf16[48,4096]{1,0:T(8,128)(2,1)}, u32[]{:S(2)}) %copy-start.6) | copy-done | bytes 393240
  8.3 0.9 %copy-done.7 = f32[256,128]{1,0:T(8,128)S(1)} copy-done((f32[256,128]{1,0:T(8,128)S(1)}, f32[256,128]{1,0:T(8,128)}, u32[]{:S(2)}) %copy-start.7) | copy-done | bytes 131096
  9.2 0.9 %copy-done.9 = f32[256,128]{1,0:T(8,128)S(1)} copy-done((f32[256,128]{1,0:T(8,128)S(1)}, f32[256,128]{1,0:T(8,128)}, u32[]{:S(2)}) %copy-start.9) | copy-done | bytes 131096
  10.1 0.7 copy-done.11
  10.8 0.7 copy-done.13
  11.5 0.7 copy-done.15
  12.2 7.6 %first_step.1 = (f32[384,128]{1,0:T(8,128)S(1)}, f32[48,128]{1,0:T(8,128)S(1)}, f32[48,128]{1,0:T(8,128)S(1)}, s32[6]{0:T(128)S(1)}, bf16[2,2,256,128]{3,2,1,0:T...) custom-call(s32[2]{0:T(128)S(1)} %pad_add_fusion.meta, ...), custom_call_target="tpu_custom_call" | custom-call | flops 301989888 | bytes 6291456 | tf_op jit(solution)/shard_map/first_step/pallas_call | solution.py:477
  19.8 0.5 collective-permute-start
  20.3 2.6 %collective-permute-start.1 = (f32[2,1536]{1,0:T(2,128)S(1)}, f32[2,1536]{1,0:T(2,128)S(1)}, u32[]{:S(2)}, u32[]{:S(2)}) collective-permute-start(f32[2,1536]{1,0:T(2,128)S(1)} %get-tuple-element.27), channel_id=1, source_target_pairs={{0,8},{4,12},{8,0},{12,4},{1,9},{5,13},{9,1},{13,5},{2,10},{6,14},... | collective-permute-start | bytes 36872 | tf_op jit(solution)/shard_map/ppermute | solution.py:444
  22.9 0.1 collective-permute-start.2
  23.0 4.6 %attention.1.attended = bf16[48,512]{1,0:T(8,128)(2,1)S(1)} custom-call(s32[2]{0:T(128)S(1)} %pad_add_fusion.meta, s32[192]{0:T(256)S(1)} %copy-done.13, f32[384,128]{1,0:T(8,128)S(1)} %get-tuple-element.23.query, f32[48,128]{1,0:T(8,128)S(1)} %get-tuple-element.24.newkey.newkey1, f32[48,128]{1,0:T(8,128)S(1)} %get-tuple-element.25.newvalue.newvalue1, ...), custom_call_target="tpu_custom_call" | custom-call | flops 25165824 | bytes 6291456 | tf_op jit(solution)/shard_map/attention/pallas_call | solution.py:516
  27.5 0.0 copy-start.2
  27.5 0.0 copy-start.8
  27.6 0.0 copy-start.10
  27.6 0.0 copy-start.12
  27.6 0.0 copy-start.14
  27.6 0.0 copy-start.16
  27.6 0.0 collective-permute-done.rest_0_.rest_3_
  27.6 0.0 collective-permute-done.1.rest_1_.rest_4_
  27.6 0.0 collective-permute-done.2.rest_2_.rest_5_
  27.6 0.0 copy-done.3
  27.6 1.4 %out_projection.1 = (f32[48,1024]{1,0:T(8,128)S(1)}, bf16[48,1024]{1,0:T(8,128)(2,1)S(1)}, bf16[48,1024]{1,0:T(8,128)(2,1)S(1)}, bf16[48,1024]{1,0:T(8,128)(2,1)S(1)}) custom-call(s32[2]{0:T(128)S(1)} %pad_add_fusion.meta, s32[6]{0:T(128)S(1)} %get-tuple-element.22.plan, bf16[48,512]{1,0:T(8,128)(2,1)S(1)} %attention.1.attended, ...), custom_call_target="tpu_custom_call" | custom-call | flops 201326592 | bytes 4194304 | tf_op jit(solution)/shard_map/out_projection/pallas_call | solution.py:533
  29.1 3.9 %collective-permute-start.3 = (bf16[48,1024]{1,0:T(8,128)(2,1)S(1)}, bf16[48,1024]{1,0:T(8,128)(2,1)S(1)}, u32[]{:S(2)}, u32[]{:S(2)}) collective-permute-start(bf16[48,1024]{1,0:T(8,128)(2,1)S(1)} %get-tuple-element.30), channel_id=1, source_target_pairs={{0,3},{1,2},{2,1},{3,0},{4,7},{5,6},{6,5},{7,4},{8,11},{9,10},{10,... | collective-permute-start | bytes 294920 | tf_op jit(solution)/shard_map/ppermute | solution.py:444
  32.9 0.0 collective-permute-start.4
  32.9 0.6 collective-permute-start.5
  33.6 0.0 collective-permute-start.9
  33.6 1.7 %collective-permute-start.10 = (bf16[2,2,256,128]{3,2,1,0:T(8,128)(2,1)S(1)}, bf16[2,2,256,128]{3,2,1,0:T(8,128)(2,1)S(1)}, u32[]{:S(2)}, u32[]{:S(2)}) collective-permute-start(bf16[2,2,256,128]{3,2,1,0:T(8,128)(2,1)S(1)} %get-tuple-element.34), channel_id=1, source_target_pairs={{0,8},{4,12},{8,0},{12,4},{1,9},{5,13},{9,1},{13,5},{2,10},{6,14},... | collective-permute-start | bytes 786440 | tf_op jit(solution)/shard_map/ppermute | solution.py:444
  35.2 1.4 %collective-permute-done.3.rest_0_ = bf16[48,1024]{1,0:T(8,128)(2,1)S(1)} collective-permute-done((bf16[48,1024]{1,0:T(8,128)(2,1)S(1)}, bf16[48,1024]{1,0:T(8,128)(2,1)S(1)}, u32[]{:S(2)}, u32[]{:S(2)}) %collective-permute-start.3) | collective-permute-done | bytes 98336 | tf_op jit(solution)/shard_map/ppermute | solution.py:444
  36.6 0.4 collective-permute-start.11
  37.0 4.7 %collective-permute-done.4.rest_1_ = bf16[48,1024]{1,0:T(8,128)(2,1)S(1)} collective-permute-done((bf16[48,1024]{1,0:T(8,128)(2,1)S(1)}, bf16[48,1024]{1,0:T(8,128)(2,1)S(1)}, u32[]{:S(2)}, u32[]{:S(2)}) %collective-permute-start.4) | collective-permute-done | bytes 98336 | tf_op jit(solution)/shard_map/ppermute | solution.py:444
  41.7 0.0 collective-permute-done.5.rest_2_
  41.7 0.7 sum_terms.2.rest_0_.hidden
  42.4 2.5 %collective-permute-start.8 = (bf16[48,1024]{1,0:T(8,128)(2,1)S(1)}, bf16[48,1024]{1,0:T(8,128)(2,1)S(1)}, u32[]{:S(2)}, u32[]{:S(2)}) collective-permute-start(bf16[48,1024]{1,0:T(8,128)(2,1)S(1)} %sum_terms.2.rest_0_.hidden), channel_id=1, source_target_pairs={{0,3},{1,2},{2,1},{3,0},{4,7},{5,6},{6,5},{7,4},{8,11},{9,10},{10,... | collective-permute-start | bytes 294920 | tf_op jit(solution)/shard_map/ppermute | solution.py:444
  44.9 0.0 collective-permute-start.7
  44.9 4.7 %collective-permute-done.8.rest_3_ = bf16[48,1024]{1,0:T(8,128)(2,1)S(1)} collective-permute-done((bf16[48,1024]{1,0:T(8,128)(2,1)S(1)}, bf16[48,1024]{1,0:T(8,128)(2,1)S(1)}, u32[]{:S(2)}, u32[]{:S(2)}) %collective-permute-start.8) | collective-permute-done | bytes 98336 | tf_op jit(solution)/shard_map/ppermute | solution.py:444
  49.6 3.1 %collective-permute-start.6 = (bf16[48,1024]{1,0:T(8,128)(2,1)S(1)}, bf16[48,1024]{1,0:T(8,128)(2,1)S(1)}, u32[]{:S(2)}, u32[]{:S(2)}) collective-permute-start(bf16[48,1024]{1,0:T(8,128)(2,1)S(1)} %sum_terms.2.rest_0_.hidden), channel_id=1, source_target_pairs={{0,1},{1,0},{2,3},{3,2},{4,5},{5,4},{6,7},{7,6},{8,9},{9,8},{10,11... | collective-permute-start | bytes 294920 | tf_op jit(solution)/shard_map/ppermute | solution.py:444
  52.8 0.8 collective-permute-done.7.rest_2_
  53.6 1.8 %collective-permute-done.6.rest_1_ = bf16[48,1024]{1,0:T(8,128)(2,1)S(1)} collective-permute-done((bf16[48,1024]{1,0:T(8,128)(2,1)S(1)}, bf16[48,1024]{1,0:T(8,128)(2,1)S(1)}, u32[]{:S(2)}, u32[]{:S(2)}) %collective-permute-start.6) | collective-permute-done | bytes 98336 | tf_op jit(solution)/shard_map/ppermute | solution.py:444
  55.4 0.0 collective-permute-done.9.rest_4_.rest_0_
  55.4 0.0 collective-permute-done.10.rest_5_.rest_1_
  55.4 0.0 collective-permute-done.11.rest_6_.rest_2_
  55.4 0.0 copy-done.5
  55.4 0.0 slice-done
  55.4 0.0 slice-done.1
  55.5 6.8 %second_step.1 = (f32[48,128]{1,0:T(8,128)S(1)}, f32[48,128]{1,0:T(8,128)S(1)}, f32[48,1024]{1,0:T(8,128)S(1)}, bf16[48,1024]{1,0:T(8,128)(2,1)S(1)}, bf16[48,10...) custom-call(s32[2]{0:T(128)S(1)} %pad_add_fusion.meta, s32[192]{0:T(256)S(1)} %copy-done.16, s32[192]{0:T(256)S(1)} %copy-done.14, ...), custom_call_target="tpu_custom_call" | custom-call | flops 905969664 | bytes 18874368 | tf_op jit(solution)/shard_map/second_step/pallas_call | solution.py:559
  62.3 2.1 %collective-permute-start.12 = (bf16[48,1024]{1,0:T(8,128)(2,1)S(1)}, bf16[48,1024]{1,0:T(8,128)(2,1)S(1)}, u32[]{:S(2)}, u32[]{:S(2)}) collective-permute-start(bf16[48,1024]{1,0:T(8,128)(2,1)S(1)} %get-tuple-element.37), channel_id=1, source_target_pairs={{0,3},{1,2},{2,1},{3,0},{4,7},{5,6},{6,5},{7,4},{8,11},{9,10},{10,... | collective-permute-start | bytes 294920 | tf_op jit(solution)/shard_map/ppermute | solution.py:444
  64.4 1.4 %collective-permute-start.13 = (bf16[48,1024]{1,0:T(8,128)(2,1)S(1)}, bf16[48,1024]{1,0:T(8,128)(2,1)S(1)}, u32[]{:S(2)}, u32[]{:S(2)}) collective-permute-start(bf16[48,1024]{1,0:T(8,128)(2,1)S(1)} %get-tuple-element.38), channel_id=1, source_target_pairs={{0,2},{1,3},{2,0},{3,1},{4,6},{5,7},{6,4},{7,5},{8,10},{9,11},{10,... | collective-permute-start | bytes 294920 | tf_op jit(solution)/shard_map/ppermute | solution.py:444
  65.8 0.9 %collective-permute-start.14 = (bf16[48,1024]{1,0:T(8,128)(2,1)S(1)}, bf16[48,1024]{1,0:T(8,128)(2,1)S(1)}, u32[]{:S(2)}, u32[]{:S(2)}) collective-permute-start(bf16[48,1024]{1,0:T(8,128)(2,1)S(1)} %get-tuple-element.39), channel_id=1, source_target_pairs={{0,1},{1,0},{2,3},{3,2},{4,5},{5,4},{6,7},{7,6},{8,9},{9,8},{10,11... | collective-permute-start | bytes 294920 | tf_op jit(solution)/shard_map/ppermute | solution.py:444
  66.7 2.3 %collective-permute-done.12.rest_0_ = bf16[48,1024]{1,0:T(8,128)(2,1)S(1)} collective-permute-done((bf16[48,1024]{1,0:T(8,128)(2,1)S(1)}, bf16[48,1024]{1,0:T(8,128)(2,1)S(1)}, u32[]{:S(2)}, u32[]{:S(2)}) %collective-permute-start.12) | collective-permute-done | bytes 98336 | tf_op jit(solution)/shard_map/ppermute | solution.py:444
  69.1 3.5 %collective-permute-done.13.rest_1_ = bf16[48,1024]{1,0:T(8,128)(2,1)S(1)} collective-permute-done((bf16[48,1024]{1,0:T(8,128)(2,1)S(1)}, bf16[48,1024]{1,0:T(8,128)(2,1)S(1)}, u32[]{:S(2)}, u32[]{:S(2)}) %collective-permute-start.13) | collective-permute-done | bytes 98336 | tf_op jit(solution)/shard_map/ppermute | solution.py:444
  72.6 0.0 collective-permute-done.14.rest_2_
  72.6 0.6 sum_terms.3.rest_0_
  73.2 2.5 %collective-permute-start.17 = (bf16[48,1024]{1,0:T(8,128)(2,1)S(1)}, bf16[48,1024]{1,0:T(8,128)(2,1)S(1)}, u32[]{:S(2)}, u32[]{:S(2)}) collective-permute-start(bf16[48,1024]{1,0:T(8,128)(2,1)S(1)} %sum_terms.3.rest_0_), channel_id=1, source_target_pairs={{0,3},{1,2},{2,1},{3,0},{4,7},{5,6},{6,5},{7,4},{8,11},{9,10},{10,... | collective-permute-start | bytes 294920 | tf_op jit(solution)/shard_map/ppermute | solution.py:444
  75.7 0.0 collective-permute-start.16
  75.7 1.9 %collective-permute-start.15 = (bf16[48,1024]{1,0:T(8,128)(2,1)S(1)}, bf16[48,1024]{1,0:T(8,128)(2,1)S(1)}, u32[]{:S(2)}, u32[]{:S(2)}) collective-permute-start(bf16[48,1024]{1,0:T(8,128)(2,1)S(1)} %sum_terms.3.rest_0_), channel_id=1, source_target_pairs={{0,1},{1,0},{2,3},{3,2},{4,5},{5,4},{6,7},{7,6},{8,9},{9,8},{10,11... | collective-permute-start | bytes 294920 | tf_op jit(solution)/shard_map/ppermute | solution.py:444
  77.6 4.2 %write_cache.1 = bf16[48,2,256,128]{3,2,1,0:T(8,128)(2,1)} custom-call(s32[2]{0:T(128)S(1)} %pad_add_fusion.meta, s32[192]{0:T(256)S(1)} %copy-done.16, s32[192]{0:T(256)S(1)} %copy-done.14, s32[6]{0:T(128)S(1)} %get-tuple-element.22.plan, f32[48,128]{1,0:T(8,128)S(1)} %get-tuple-element.24.newkey.newkey1, ...), custom_call_target="tpu_custom_call" | custom-call | bytes 12582912 | tf_op jit(solution)/shard_map/write_cache/pallas_call | solution.py:579
  81.9 0.0 collective-permute-done.17.rest_3_
  81.9 1.8 %collective-permute-done.16.rest_2_ = bf16[48,1024]{1,0:T(8,128)(2,1)S(1)} collective-permute-done((bf16[48,1024]{1,0:T(8,128)(2,1)S(1)}, bf16[48,1024]{1,0:T(8,128)(2,1)S(1)}, u32[]{:S(2)}, u32[]{:S(2)}) %collective-permute-start.16) | collective-permute-done | bytes 98336 | tf_op jit(solution)/shard_map/ppermute | solution.py:444
  83.7 0.0 collective-permute-done.15.rest_1_
  83.7 1.3 %join.1 = bf16[48,4096]{1,0:T(8,128)(2,1)} custom-call(s32[2]{0:T(128)S(1)} %pad_add_fusion.meta, bf16[48,1024]{1,0:T(8,128)(2,1)S(1)} %sum_terms.3.rest_0_, bf16[48,1024]{1,0:T(8,128)(2,1)S(1)} %collective-permute-done.15.rest_1_, bf16[48,1024]{1,0:T(8,128)(2,1)S(1)} %collective-permute-done.16.rest_2_, bf16[48,1024]{1,0:T(8,128)(2,1)S(1)} %collective-permute-done.17.rest_3_), custom_call_target="tpu_custom_call" | custom-call | tf_op jit(solution)/shard_map/join/pallas_call | solution.py:594
  (20 shorter events, 0.0 us)
Async XLA Ops:
  0.7 2.8 %copy-start = (bf16[48,2,256,128]{3,2,1,0:T(8,128)(2,1)S(1)}, bf16[48,2,256,128]{3,2,1,0:T(8,128)(2,1)}, u32[]{:S(2)}) copy-start(bf16[48,2,256,128]{3,2,1,0:T(8,128)(2,1)} %cache_hbm.7) | copy-start | bytes 18874372
  3.5 2.2 %copy-start.1 = (bf16[4096,512]{1,0:T(8,128)(2,1)S(1)}, bf16[4096,512]{1,0:T(8,128)(2,1)}, u32[]{:S(2)}) copy-start(bf16[4096,512]{1,0:T(8,128)(2,1)} %wq.1) | copy-start | bytes 12582916
  5.7 1.6 %copy-start.4 = (bf16[4096,2,128]{2,1,0:T(2,128)(2,1)S(1)}, bf16[4096,2,128]{2,1,0:T(2,128)(2,1)}, u32[]{:S(2)}) copy-start(bf16[4096,2,128]{2,1,0:T(2,128)(2,1)} %param.16) | copy-start | bytes 6291460
  7.3 1.0 %copy-start.6 = (bf16[48,4096]{1,0:T(8,128)(2,1)S(1)}, bf16[48,4096]{1,0:T(8,128)(2,1)}, u32[]{:S(2)}) copy-start(bf16[48,4096]{1,0:T(8,128)(2,1)} %hidden.1) | copy-start | bytes 1179652
  8.3 0.9 %copy-start.7 = (f32[256,128]{1,0:T(8,128)S(1)}, f32[256,128]{1,0:T(8,128)}, u32[]{:S(2)}) copy-start(f32[256,128]{1,0:T(8,128)} %constant.12.clone.sin_hbm.sin_ref) | copy-start | bytes 393220
  9.2 0.9 %copy-start.9 = (f32[256,128]{1,0:T(8,128)S(1)}, f32[256,128]{1,0:T(8,128)}, u32[]{:S(2)}) copy-start(f32[256,128]{1,0:T(8,128)} %constant.11.clone.cos_hbm.cos_ref) | copy-start | bytes 393220
  10.1 0.7 copy-start.11
  10.8 0.7 copy-start.13
  11.5 0.7 copy-start.15
  12.2 15.5 %copy-start.3 = (bf16[512,4096]{1,0:T(8,128)(2,1)S(1)}, bf16[512,4096]{1,0:T(8,128)(2,1)}, u32[]{:S(2)}) copy-start(bf16[512,4096]{1,0:T(8,128)(2,1)} %wo.3) | copy-start | bytes 12582916
  12.2 43.2 %copy-start.5 = (bf16[4096,2,128]{2,1,0:T(2,128)(2,1)S(1)}, bf16[4096,2,128]{2,1,0:T(2,128)(2,1)}, u32[]{:S(2)}) copy-start(bf16[4096,2,128]{2,1,0:T(2,128)(2,1)} %param.16) | copy-start | bytes 6291460
  19.8 7.8 %collective-permute-start = (f32[2,1536]{1,0:T(2,128)S(1)}, f32[2,1536]{1,0:T(2,128)S(1)}, u32[]{:S(2)}, u32[]{:S(2)}) collective-permute-start(f32[2,1536]{1,0:T(2,128)S(1)} %get-tuple-element.26), channel_id=1, source_target_pairs={{0,4},{4,0},{8,12},{12,8},{1,5},{5,1},{9,13},{13,9},{2,6},{6,2},{1... | collective-permute-start | bytes 36872 | tf_op jit(solution)/shard_map/ppermute | solution.py:444
  20.3 7.3 %collective-permute-start.1 = (f32[2,1536]{1,0:T(2,128)S(1)}, f32[2,1536]{1,0:T(2,128)S(1)}, u32[]{:S(2)}, u32[]{:S(2)}) collective-permute-start(f32[2,1536]{1,0:T(2,128)S(1)} %get-tuple-element.27), channel_id=1, source_target_pairs={{0,8},{4,12},{8,0},{12,4},{1,9},{5,13},{9,1},{13,5},{2,10},{6,14},... | collective-permute-start | bytes 36872 | tf_op jit(solution)/shard_map/ppermute | solution.py:444
  22.9 4.7 %collective-permute-start.2 = (f32[2,1536]{1,0:T(2,128)S(1)}, f32[2,1536]{1,0:T(2,128)S(1)}, u32[]{:S(2)}, u32[]{:S(2)}) collective-permute-start(f32[2,1536]{1,0:T(2,128)S(1)} %get-tuple-element.28), channel_id=1, source_target_pairs={{0,12},{4,8},{8,4},{12,0},{1,13},{5,9},{9,5},{13,1},{2,14},{6,10},... | collective-permute-start | bytes 36872 | tf_op jit(solution)/shard_map/ppermute | solution.py:444
  23.0 32.4 %slice-start = ((s8[6291456]{0:T(1024)(128)(4,1)}), s8[4194304]{0:T(1024)(128)(4,1)S(1)}, s32[]{:S(2)}) async-start(s8[6291456]{0:T(1024)(128)(4,1)} %bitcast.6), calls=%async_computation | async-start | bytes 8388608
  23.0 32.4 %slice-start.1 = ((s8[6291456]{0:T(1024)(128)(4,1)}), s8[2097152]{0:T(1024)(128)(4,1)S(1)}, s32[]{:S(2)}) async-start(s8[6291456]{0:T(1024)(128)(4,1)} %bitcast.6), calls=%async_computation.1 | async-start | bytes 4194304
  27.5 27.9 %copy-start.2 = (bf16[4096,512]{1,0:T(8,128)(2,1)S(1)}, bf16[4096,512]{1,0:T(8,128)(2,1)}, u32[]{:S(2)}) copy-start(bf16[4096,512]{1,0:T(8,128)(2,1)} %wq.1) | copy-start | bytes 12582916
  27.5 27.9 %copy-start.8 = (f32[256,128]{1,0:T(8,128)S(1)}, f32[256,128]{1,0:T(8,128)}, u32[]{:S(2)}) copy-start(f32[256,128]{1,0:T(8,128)} %constant.12.clone.sin_hbm.sin_ref) | copy-start | bytes 393220
  27.6 27.9 %copy-start.10 = (f32[256,128]{1,0:T(8,128)S(1)}, f32[256,128]{1,0:T(8,128)}, u32[]{:S(2)}) copy-start(f32[256,128]{1,0:T(8,128)} %constant.11.clone.cos_hbm.cos_ref) | copy-start | bytes 393220
  27.6 27.9 %copy-start.12 = (f32[4096]{0:T(1024)S(1)}, f32[4096]{0:T(1024)}, u32[]{:S(2)}) copy-start(f32[4096]{0:T(1024)} %param.14) | copy-start | bytes 49156
  27.6 27.9 %copy-start.14 = (s32[192]{0:T(256)S(1)}, s32[192]{0:T(256)}, u32[]{:S(2)}) copy-start(s32[192]{0:T(256)} %lengths_s.5) | copy-start | bytes 2308
  27.6 27.9 %copy-start.16 = (s32[192]{0:T(256)S(1)}, s32[192]{0:T(256)}, u32[]{:S(2)}) copy-start(s32[192]{0:T(256)} %source_s.3) | copy-start | bytes 2308
  29.1 7.5 %collective-permute-start.3 = (bf16[48,1024]{1,0:T(8,128)(2,1)S(1)}, bf16[48,1024]{1,0:T(8,128)(2,1)S(1)}, u32[]{:S(2)}, u32[]{:S(2)}) collective-permute-start(bf16[48,1024]{1,0:T(8,128)(2,1)S(1)} %get-tuple-element.30), channel_id=1, source_target_pairs={{0,3},{1,2},{2,1},{3,0},{4,7},{5,6},{6,5},{7,4},{8,11},{9,10},{10,... | collective-permute-start | bytes 294920 | tf_op jit(solution)/shard_map/ppermute | solution.py:444
  32.9 8.8 %collective-permute-start.4 = (bf16[48,1024]{1,0:T(8,128)(2,1)S(1)}, bf16[48,1024]{1,0:T(8,128)(2,1)S(1)}, u32[]{:S(2)}, u32[]{:S(2)}) collective-permute-start(bf16[48,1024]{1,0:T(8,128)(2,1)S(1)} %get-tuple-element.31), channel_id=1, source_target_pairs={{0,2},{1,3},{2,0},{3,1},{4,6},{5,7},{6,4},{7,5},{8,10},{9,11},{10,... | collective-permute-start | bytes 294920 | tf_op jit(solution)/shard_map/ppermute | solution.py:444
  32.9 8.8 %collective-permute-start.5 = (bf16[48,1024]{1,0:T(8,128)(2,1)S(1)}, bf16[48,1024]{1,0:T(8,128)(2,1)S(1)}, u32[]{:S(2)}, u32[]{:S(2)}) collective-permute-start(bf16[48,1024]{1,0:T(8,128)(2,1)S(1)} %get-tuple-element.32), channel_id=1, source_target_pairs={{0,1},{1,0},{2,3},{3,2},{4,5},{5,4},{6,7},{7,6},{8,9},{9,8},{10,11... | collective-permute-start | bytes 294920 | tf_op jit(solution)/shard_map/ppermute | solution.py:444
  33.6 21.8 %collective-permute-start.9 = (bf16[2,2,256,128]{3,2,1,0:T(8,128)(2,1)S(1)}, bf16[2,2,256,128]{3,2,1,0:T(8,128)(2,1)S(1)}, u32[]{:S(2)}, u32[]{:S(2)}) collective-permute-start(bf16[2,2,256,128]{3,2,1,0:T(8,128)(2,1)S(1)} %get-tuple-element.33), channel_id=1, source_target_pairs={{0,4},{4,0},{8,12},{12,8},{1,5},{5,1},{9,13},{13,9},{2,6},{6,2},{1... | collective-permute-start | bytes 786440 | tf_op jit(solution)/shard_map/ppermute | solution.py:444
  33.6 21.8 %collective-permute-start.10 = (bf16[2,2,256,128]{3,2,1,0:T(8,128)(2,1)S(1)}, bf16[2,2,256,128]{3,2,1,0:T(8,128)(2,1)S(1)}, u32[]{:S(2)}, u32[]{:S(2)}) collective-permute-start(bf16[2,2,256,128]{3,2,1,0:T(8,128)(2,1)S(1)} %get-tuple-element.34), channel_id=1, source_target_pairs={{0,8},{4,12},{8,0},{12,4},{1,9},{5,13},{9,1},{13,5},{2,10},{6,14},... | collective-permute-start | bytes 786440 | tf_op jit(solution)/shard_map/ppermute | solution.py:444
  36.6 18.8 %collective-permute-start.11 = (bf16[2,2,256,128]{3,2,1,0:T(8,128)(2,1)S(1)}, bf16[2,2,256,128]{3,2,1,0:T(8,128)(2,1)S(1)}, u32[]{:S(2)}, u32[]{:S(2)}) collective-permute-start(bf16[2,2,256,128]{3,2,1,0:T(8,128)(2,1)S(1)} %get-tuple-element.35), channel_id=1, source_target_pairs={{0,12},{4,8},{8,4},{12,0},{1,13},{5,9},{9,5},{13,1},{2,14},{6,10},... | collective-permute-start | bytes 786440 | tf_op jit(solution)/shard_map/ppermute | solution.py:444
  42.4 7.3 %collective-permute-start.8 = (bf16[48,1024]{1,0:T(8,128)(2,1)S(1)}, bf16[48,1024]{1,0:T(8,128)(2,1)S(1)}, u32[]{:S(2)}, u32[]{:S(2)}) collective-permute-start(bf16[48,1024]{1,0:T(8,128)(2,1)S(1)} %sum_terms.2.rest_0_.hidden), channel_id=1, source_target_pairs={{0,3},{1,2},{2,1},{3,0},{4,7},{5,6},{6,5},{7,4},{8,11},{9,10},{10,... | collective-permute-start | bytes 294920 | tf_op jit(solution)/shard_map/ppermute | solution.py:444
  44.9 8.6 %collective-permute-start.7 = (bf16[48,1024]{1,0:T(8,128)(2,1)S(1)}, bf16[48,1024]{1,0:T(8,128)(2,1)S(1)}, u32[]{:S(2)}, u32[]{:S(2)}) collective-permute-start(bf16[48,1024]{1,0:T(8,128)(2,1)S(1)} %sum_terms.2.rest_0_.hidden), channel_id=1, source_target_pairs={{0,2},{1,3},{2,0},{3,1},{4,6},{5,7},{6,4},{7,5},{8,10},{9,11},{10,... | collective-permute-start | bytes 294920 | tf_op jit(solution)/shard_map/ppermute | solution.py:444
  49.6 5.7 %collective-permute-start.6 = (bf16[48,1024]{1,0:T(8,128)(2,1)S(1)}, bf16[48,1024]{1,0:T(8,128)(2,1)S(1)}, u32[]{:S(2)}, u32[]{:S(2)}) collective-permute-start(bf16[48,1024]{1,0:T(8,128)(2,1)S(1)} %sum_terms.2.rest_0_.hidden), channel_id=1, source_target_pairs={{0,1},{1,0},{2,3},{3,2},{4,5},{5,4},{6,7},{7,6},{8,9},{9,8},{10,11... | collective-permute-start | bytes 294920 | tf_op jit(solution)/shard_map/ppermute | solution.py:444
  62.3 6.8 %collective-permute-start.12 = (bf16[48,1024]{1,0:T(8,128)(2,1)S(1)}, bf16[48,1024]{1,0:T(8,128)(2,1)S(1)}, u32[]{:S(2)}, u32[]{:S(2)}) collective-permute-start(bf16[48,1024]{1,0:T(8,128)(2,1)S(1)} %get-tuple-element.37), channel_id=1, source_target_pairs={{0,3},{1,2},{2,1},{3,0},{4,7},{5,6},{6,5},{7,4},{8,11},{9,10},{10,... | collective-permute-start | bytes 294920 | tf_op jit(solution)/shard_map/ppermute | solution.py:444
  64.4 8.2 %collective-permute-start.13 = (bf16[48,1024]{1,0:T(8,128)(2,1)S(1)}, bf16[48,1024]{1,0:T(8,128)(2,1)S(1)}, u32[]{:S(2)}, u32[]{:S(2)}) collective-permute-start(bf16[48,1024]{1,0:T(8,128)(2,1)S(1)} %get-tuple-element.38), channel_id=1, source_target_pairs={{0,2},{1,3},{2,0},{3,1},{4,6},{5,7},{6,4},{7,5},{8,10},{9,11},{10,... | collective-permute-start | bytes 294920 | tf_op jit(solution)/shard_map/ppermute | solution.py:444
  65.8 6.7 %collective-permute-start.14 = (bf16[48,1024]{1,0:T(8,128)(2,1)S(1)}, bf16[48,1024]{1,0:T(8,128)(2,1)S(1)}, u32[]{:S(2)}, u32[]{:S(2)}) collective-permute-start(bf16[48,1024]{1,0:T(8,128)(2,1)S(1)} %get-tuple-element.39), channel_id=1, source_target_pairs={{0,1},{1,0},{2,3},{3,2},{4,5},{5,4},{6,7},{7,6},{8,9},{9,8},{10,11... | collective-permute-start | bytes 294920 | tf_op jit(solution)/shard_map/ppermute | solution.py:444
  73.2 8.7 %collective-permute-start.17 = (bf16[48,1024]{1,0:T(8,128)(2,1)S(1)}, bf16[48,1024]{1,0:T(8,128)(2,1)S(1)}, u32[]{:S(2)}, u32[]{:S(2)}) collective-permute-start(bf16[48,1024]{1,0:T(8,128)(2,1)S(1)} %sum_terms.3.rest_0_), channel_id=1, source_target_pairs={{0,3},{1,2},{2,1},{3,0},{4,7},{5,6},{6,5},{7,4},{8,11},{9,10},{10,... | collective-permute-start | bytes 294920 | tf_op jit(solution)/shard_map/ppermute | solution.py:444
  75.7 8.0 %collective-permute-start.16 = (bf16[48,1024]{1,0:T(8,128)(2,1)S(1)}, bf16[48,1024]{1,0:T(8,128)(2,1)S(1)}, u32[]{:S(2)}, u32[]{:S(2)}) collective-permute-start(bf16[48,1024]{1,0:T(8,128)(2,1)S(1)} %sum_terms.3.rest_0_), channel_id=1, source_target_pairs={{0,2},{1,3},{2,0},{3,1},{4,6},{5,7},{6,4},{7,5},{8,10},{9,11},{10,... | collective-permute-start | bytes 294920 | tf_op jit(solution)/shard_map/ppermute | solution.py:444
  75.7 8.0 %collective-permute-start.15 = (bf16[48,1024]{1,0:T(8,128)(2,1)S(1)}, bf16[48,1024]{1,0:T(8,128)(2,1)S(1)}, u32[]{:S(2)}, u32[]{:S(2)}) collective-permute-start(bf16[48,1024]{1,0:T(8,128)(2,1)S(1)} %sum_terms.3.rest_0_), channel_id=1, source_target_pairs={{0,1},{1,0},{2,3},{3,2},{4,5},{5,4},{6,7},{7,6},{8,9},{9,8},{10,11... | collective-permute-start | bytes 294920 | tf_op jit(solution)/shard_map/ppermute | solution.py:444

commit v3 on v2

--- a/solution.py
+++ b/solution.py
@@ -280,7 +280,7 @@
             sends[k - 1][...] = part.astype(BF16)
 
 
-def out_kernel(peers, peers_tp, meta, plan, attended, wo, *rest):
+def out_kernel(peers, peers_tp, meta, plan, attended, wo, _box, *rest):
     notes = rest[: peers - 1]
     own = rest[peers - 1]
     sends = rest[peers:]
@@ -507,8 +507,11 @@
         compiler_params=params(24),
         cost_estimate=cost(flops, (query_weight.size + wkv.size) * 2),
         name="first_step",
-    )(meta, source.reshape(1, -1), lengths.reshape(1, -1), hidden, gain, cosine, sine, query_weight,
-      wkv, kv_cache)
+    )(meta, *(
+        pltpu.with_memory_space_constraint(x, pltpu.HBM)
+        for x in (source.reshape(1, -1), lengths.reshape(1, -1), hidden, gain, cosine, sine,
+                  query_weight, wkv, kv_cache)
+    ))
     boxes, notes = rest[:others], rest[others:]
     got_notes = [swapped(note, "inst", peers, k + 1) for k, note in enumerate(notes)]
     got_boxes = [swapped(box, "inst", peers, k + 1) for k, box in enumerate(boxes)]
@@ -533,12 +536,12 @@
     own, *sends = pl.pallas_call(
         functools.partial(out_kernel, peers, peers_tp),
         out_shape=sent,
-        in_specs=[SMEM] * 2 + [VMEM] * (2 + others),
+        in_specs=[SMEM] * 2 + [VMEM] * 2 + [ANY] + [VMEM] * others,
         out_specs=[VMEM] * peers_tp,
         compiler_params=params(16),
         cost_estimate=cost(2 * slots * width * heads * HD, out_weight.size * 2),
         name="out_projection",
-    )(meta, plan, attended, out_weight, *got_notes)
+    )(meta, plan, attended, out_weight, got_boxes[0], *got_notes)
 
     def summed(residual, own, sends, notes):
         got = [swapped(sends[k - 1], "tp", peers_tp, k) for k in range(peers_tp - 1, 0, -1)]

time: 85.4 us -> 79.9 us (0.936)
  local copies, waits for them, and re-layouts: 11.5 us -> 0.06 us
  waiting for transfers between devices: 21 us -> 27.7 us
    unnamed x38 -> x22, local copies, waits for them, and re-layouts: 11.5 us -> 0.06 us
    ppermute x18, waiting for transfers between devices: 21 us -> 27.7 us  [swapped(): return lax.ppermute(x, axis, [(i, i ^ k) for i in range(size)])]
  transfers between devices with their start and end apart: 18 -> 18, of which waited for: 8 -> 8; matrix products, arithmetic and copies ran while one was open for 0% -> 0% of each run, Pallas kernels for 11% -> 14%
where the time goes in v3:
time: 79.9 us; the launch traced here: 79.7 us
  waiting for transfers between devices  27.7 us (35%)
  Pallas kernels  27.1 us (34%)
  starting transfers between devices  23.9 us (30%)
  between operations  0.81 us (1%)
    ppermute x18, waiting for transfers between devices, swapped(): return lax.ppermute(x, axis, [(i, i ^ k) for i in range(size)])  27.7 us
    ppermute x18, starting transfers between devices, swapped(): return lax.ppermute(x, axis, [(i, i ^ k) for i in range(size)])  23.9 us
    pallas_call x1, Pallas kernels, local(): pl.pallas_call(functools.partial(first_kernel, peers, slots, heads, shard...  7.52 us
    pallas_call x1, Pallas kernels, local(): pl.pallas_call(functools.partial(second_kernel, peers, peers_tp, slots, h...  6.83 us
    pallas_call x1, Pallas kernels, local(): pl.pallas_call(functools.partial(attend_kernel, slots, heads), out_shape=...  4.56 us
    pallas_call x1, Pallas kernels, local(): pl.pallas_call(functools.partial(cache_kernel, peers, slots), out_shape=j...  4.23 us
  transfers between devices with their start and end apart: 18, of which 8 were waited for; matrix products, arithmetic and copies ran while one was open for 0% of the time, Pallas kernels for 14%

profile of v3, /device:TPU:0, one launch (start us, length us, event | category | flops | bytes accessed | tf_op | source)
XLA Modules:
  0.0 79.7 jit_solution(11786670538878946820)
XLA Ops:
  0.6 0.1 pad_add_fusion.meta
  0.7 7.5 %first_step.1 = (f32[384,128]{1,0:T(8,128)S(1)}, f32[48,128]{1,0:T(8,128)S(1)}, f32[48,128]{1,0:T(8,128)S(1)}, s32[6]{0:T(128)S(1)}, bf16[2,2,256,128]{3,2,1,0:T...) custom-call(s32[2]{0:T(128)S(1)} %pad_add_fusion.meta, ...), custom_call_target="tpu_custom_call" | custom-call | flops 301989888 | bytes 6291456 | tf_op jit(solution)/shard_map/first_step/pallas_call | solution.py:477
  8.2 0.0 copy-start.1
  8.3 0.5 collective-permute-start
  8.8 2.6 %collective-permute-start.10 = (bf16[2,2,256,128]{3,2,1,0:T(8,128)(2,1)S(1)}, bf16[2,2,256,128]{3,2,1,0:T(8,128)(2,1)S(1)}, u32[]{:S(2)}, u32[]{:S(2)}) collective-permute-start(bf16[2,2,256,128]{3,2,1,0:T(8,128)(2,1)S(1)} %get-tuple-element.34), channel_id=1, source_target_pairs={{0,8},{4,12},{8,0},{12,4},{1,9},{5,13},{9,1},{13,5},{2,10},{6,14},... | collective-permute-start | bytes 786440 | tf_op jit(solution)/shard_map/ppermute | solution.py:444
  11.4 0.1 collective-permute-start.11
  11.4 0.1 collective-permute-start.1
  11.6 1.9 %collective-permute-start.2 = (f32[2,1536]{1,0:T(2,128)S(1)}, f32[2,1536]{1,0:T(2,128)S(1)}, u32[]{:S(2)}, u32[]{:S(2)}) collective-permute-start(f32[2,1536]{1,0:T(2,128)S(1)} %get-tuple-element.28), channel_id=1, source_target_pairs={{0,8},{4,12},{8,0},{12,4},{1,9},{5,13},{9,1},{13,5},{2,10},{6,14},... | collective-permute-start | bytes 36872 | tf_op jit(solution)/shard_map/ppermute | solution.py:444
  13.5 0.0 collective-permute-done.1.rest_0_.rest_3_
  13.5 0.8 collective-permute-start.3
  14.3 0.0 slice-done
  14.3 0.0 slice-done.1
  14.3 0.0 copy-done.7
  14.3 0.0 copy-start.3
  14.3 0.0 copy-start.2
  14.3 4.6 %attention.1.attended = bf16[48,512]{1,0:T(8,128)(2,1)S(1)} custom-call(s32[2]{0:T(128)S(1)} %pad_add_fusion.meta, s32[192]{0:T(256)S(1)} %copy-done.7, f32[384,128]{1,0:T(8,128)S(1)} %get-tuple-element.23.query, f32[48,128]{1,0:T(8,128)S(1)} %get-tuple-element.24.newkey.newkey1, f32[48,128]{1,0:T(8,128)S(1)} %get-tuple-element.25.newvalue.newvalue1, ...), custom_call_target="tpu_custom_call" | custom-call | flops 25165824 | bytes 6291456 | tf_op jit(solution)/shard_map/attention/pallas_call | solution.py:519
  18.9 0.0 copy-start
  18.9 0.0 copy-start.4
  18.9 0.0 copy-start.5
  18.9 0.0 copy-start.6
  18.9 0.0 copy-start.8
  19.0 5.3 %collective-permute-done.2.rest_1_.rest_4_ = f32[2,1536]{1,0:T(2,128)S(1)} collective-permute-done((f32[2,1536]{1,0:T(2,128)S(1)}, f32[2,1536]{1,0:T(2,128)S(1)}, u32[]{:S(2)}, u32[]{:S(2)}) %collective-permute-start.2) | collective-permute-done | bytes 12320 | tf_op jit(solution)/shard_map/ppermute | solution.py:444
  24.3 0.0 collective-permute-done.3.rest_2_.rest_5_
  24.3 0.0 collective-permute-done._box.rest_4_.rest_0_
  24.3 0.0 copy-done.1
  24.3 1.4 %out_projection.1 = (f32[48,1024]{1,0:T(8,128)S(1)}, bf16[48,1024]{1,0:T(8,128)(2,1)S(1)}, bf16[48,1024]{1,0:T(8,128)(2,1)S(1)}, bf16[48,1024]{1,0:T(8,128)(2,1)S(1)}) custom-call(s32[2]{0:T(128)S(1)} %pad_add_fusion.meta, s32[6]{0:T(128)S(1)} %get-tuple-element.22.plan, bf16[48,512]{1,0:T(8,128)(2,1)S(1)} %attention.1.attended, ...), custom_call_target="tpu_custom_call" | custom-call | flops 201326592 | bytes 4194304 | tf_op jit(solution)/shard_map/out_projection/pallas_call | solution.py:536
  25.7 3.9 %collective-permute-start.4 = (bf16[48,1024]{1,0:T(8,128)(2,1)S(1)}, bf16[48,1024]{1,0:T(8,128)(2,1)S(1)}, u32[]{:S(2)}, u32[]{:S(2)}) collective-permute-start(bf16[48,1024]{1,0:T(8,128)(2,1)S(1)} %get-tuple-element.31), channel_id=1, source_target_pairs={{0,3},{1,2},{2,1},{3,0},{4,7},{5,6},{6,5},{7,4},{8,11},{9,10},{10,... | collective-permute-start | bytes 294920 | tf_op jit(solution)/shard_map/ppermute | solution.py:444
  29.6 0.0 collective-permute-start.5
  29.6 0.6 collective-permute-start.6
  30.2 3.0 %collective-permute-done.4.rest_0_ = bf16[48,1024]{1,0:T(8,128)(2,1)S(1)} collective-permute-done((bf16[48,1024]{1,0:T(8,128)(2,1)S(1)}, bf16[48,1024]{1,0:T(8,128)(2,1)S(1)}, u32[]{:S(2)}, u32[]{:S(2)}) %collective-permute-start.4) | collective-permute-done | bytes 98336 | tf_op jit(solution)/shard_map/ppermute | solution.py:444
  33.3 4.8 %collective-permute-done.5.rest_1_ = bf16[48,1024]{1,0:T(8,128)(2,1)S(1)} collective-permute-done((bf16[48,1024]{1,0:T(8,128)(2,1)S(1)}, bf16[48,1024]{1,0:T(8,128)(2,1)S(1)}, u32[]{:S(2)}, u32[]{:S(2)}) %collective-permute-start.5) | collective-permute-done | bytes 98336 | tf_op jit(solution)/shard_map/ppermute | solution.py:444
  38.1 0.0 collective-permute-done.6.rest_2_
  38.1 0.0 copy-done.3
  38.1 0.7 sum_terms.2.rest_0_.hidden
  38.8 2.5 %collective-permute-start.9 = (bf16[48,1024]{1,0:T(8,128)(2,1)S(1)}, bf16[48,1024]{1,0:T(8,128)(2,1)S(1)}, u32[]{:S(2)}, u32[]{:S(2)}) collective-permute-start(bf16[48,1024]{1,0:T(8,128)(2,1)S(1)} %sum_terms.2.rest_0_.hidden), channel_id=1, source_target_pairs={{0,3},{1,2},{2,1},{3,0},{4,7},{5,6},{6,5},{7,4},{8,11},{9,10},{10,... | collective-permute-start | bytes 294920 | tf_op jit(solution)/shard_map/ppermute | solution.py:444
  41.3 0.0 collective-permute-start.8
  41.3 1.9 %collective-permute-start.7 = (bf16[48,1024]{1,0:T(8,128)(2,1)S(1)}, bf16[48,1024]{1,0:T(8,128)(2,1)S(1)}, u32[]{:S(2)}, u32[]{:S(2)}) collective-permute-start(bf16[48,1024]{1,0:T(8,128)(2,1)S(1)} %sum_terms.2.rest_0_.hidden), channel_id=1, source_target_pairs={{0,1},{1,0},{2,3},{3,2},{4,5},{5,4},{6,7},{7,6},{8,9},{9,8},{10,11... | collective-permute-start | bytes 294920 | tf_op jit(solution)/shard_map/ppermute | solution.py:444
  43.3 0.0 collective-permute-done.10.rest_5_.rest_1_
  43.3 0.0 collective-permute-done.11.rest_6_.rest_2_
  43.3 3.1 %collective-permute-done.9.rest_3_ = bf16[48,1024]{1,0:T(8,128)(2,1)S(1)} collective-permute-done((bf16[48,1024]{1,0:T(8,128)(2,1)S(1)}, bf16[48,1024]{1,0:T(8,128)(2,1)S(1)}, u32[]{:S(2)}, u32[]{:S(2)}) %collective-permute-start.9) | collective-permute-done | bytes 98336 | tf_op jit(solution)/shard_map/ppermute | solution.py:444
  46.4 3.4 %collective-permute-done.8.rest_2_ = bf16[48,1024]{1,0:T(8,128)(2,1)S(1)} collective-permute-done((bf16[48,1024]{1,0:T(8,128)(2,1)S(1)}, bf16[48,1024]{1,0:T(8,128)(2,1)S(1)}, u32[]{:S(2)}, u32[]{:S(2)}) %collective-permute-start.8) | collective-permute-done | bytes 98336 | tf_op jit(solution)/shard_map/ppermute | solution.py:444
  49.8 0.0 collective-permute-done.7.rest_1_
  49.8 0.0 copy-done.2
  49.8 0.0 copy-done
  49.8 0.0 copy-done.4
  49.8 0.0 copy-done.5
  49.8 0.0 copy-done.6
  49.8 0.0 copy-done.8
  49.8 6.8 %second_step.1 = (f32[48,128]{1,0:T(8,128)S(1)}, f32[48,128]{1,0:T(8,128)S(1)}, f32[48,1024]{1,0:T(8,128)S(1)}, bf16[48,1024]{1,0:T(8,128)(2,1)S(1)}, bf16[48,10...) custom-call(s32[2]{0:T(128)S(1)} %pad_add_fusion.meta, s32[192]{0:T(256)S(1)} %copy-done.8, s32[192]{0:T(256)S(1)} %copy-done.7, ...), custom_call_target="tpu_custom_call" | custom-call | flops 905969664 | bytes 18874368 | tf_op jit(solution)/shard_map/second_step/pallas_call | solution.py:562
  56.7 1.7 %collective-permute-start.12 = (bf16[48,1024]{1,0:T(8,128)(2,1)S(1)}, bf16[48,1024]{1,0:T(8,128)(2,1)S(1)}, u32[]{:S(2)}, u32[]{:S(2)}) collective-permute-start(bf16[48,1024]{1,0:T(8,128)(2,1)S(1)} %get-tuple-element.37), channel_id=1, source_target_pairs={{0,3},{1,2},{2,1},{3,0},{4,7},{5,6},{6,5},{7,4},{8,11},{9,10},{10,... | collective-permute-start | bytes 294920 | tf_op jit(solution)/shard_map/ppermute | solution.py:444
  58.3 0.0 collective-permute-start.13
  58.3 2.8 %collective-permute-start.14 = (bf16[48,1024]{1,0:T(8,128)(2,1)S(1)}, bf16[48,1024]{1,0:T(8,128)(2,1)S(1)}, u32[]{:S(2)}, u32[]{:S(2)}) collective-permute-start(bf16[48,1024]{1,0:T(8,128)(2,1)S(1)} %get-tuple-element.39), channel_id=1, source_target_pairs={{0,1},{1,0},{2,3},{3,2},{4,5},{5,4},{6,7},{7,6},{8,9},{9,8},{10,11... | collective-permute-start | bytes 294920 | tf_op jit(solution)/shard_map/ppermute | solution.py:444
  61.1 3.2 %collective-permute-done.12.rest_0_ = bf16[48,1024]{1,0:T(8,128)(2,1)S(1)} collective-permute-done((bf16[48,1024]{1,0:T(8,128)(2,1)S(1)}, bf16[48,1024]{1,0:T(8,128)(2,1)S(1)}, u32[]{:S(2)}, u32[]{:S(2)}) %collective-permute-start.12) | collective-permute-done | bytes 98336 | tf_op jit(solution)/shard_map/ppermute | solution.py:444
  64.3 2.6 %collective-permute-done.13.rest_1_ = bf16[48,1024]{1,0:T(8,128)(2,1)S(1)} collective-permute-done((bf16[48,1024]{1,0:T(8,128)(2,1)S(1)}, bf16[48,1024]{1,0:T(8,128)(2,1)S(1)}, u32[]{:S(2)}, u32[]{:S(2)}) %collective-permute-start.13) | collective-permute-done | bytes 98336 | tf_op jit(solution)/shard_map/ppermute | solution.py:444
  66.9 0.0 collective-permute-done.14.rest_2_
  66.9 0.6 sum_terms.3.rest_0_
  67.5 2.2 %collective-permute-start.17 = (bf16[48,1024]{1,0:T(8,128)(2,1)S(1)}, bf16[48,1024]{1,0:T(8,128)(2,1)S(1)}, u32[]{:S(2)}, u32[]{:S(2)}) collective-permute-start(bf16[48,1024]{1,0:T(8,128)(2,1)S(1)} %sum_terms.3.rest_0_), channel_id=1, source_target_pairs={{0,3},{1,2},{2,1},{3,0},{4,7},{5,6},{6,5},{7,4},{8,11},{9,10},{10,... | collective-permute-start | bytes 294920 | tf_op jit(solution)/shard_map/ppermute | solution.py:444
  69.7 0.0 collective-permute-start.16
  69.7 2.2 %collective-permute-start.15 = (bf16[48,1024]{1,0:T(8,128)(2,1)S(1)}, bf16[48,1024]{1,0:T(8,128)(2,1)S(1)}, u32[]{:S(2)}, u32[]{:S(2)}) collective-permute-start(bf16[48,1024]{1,0:T(8,128)(2,1)S(1)} %sum_terms.3.rest_0_), channel_id=1, source_target_pairs={{0,1},{1,0},{2,3},{3,2},{4,5},{5,4},{6,7},{7,6},{8,9},{9,8},{10,11... | collective-permute-start | bytes 294920 | tf_op jit(solution)/shard_map/ppermute | solution.py:444
  71.9 4.2 %write_cache.1 = bf16[48,2,256,128]{3,2,1,0:T(8,128)(2,1)} custom-call(s32[2]{0:T(128)S(1)} %pad_add_fusion.meta, s32[192]{0:T(256)S(1)} %copy-done.8, s32[192]{0:T(256)S(1)} %copy-done.7, s32[6]{0:T(128)S(1)} %get-tuple-element.22.plan, f32[48,128]{1,0:T(8,128)S(1)} %get-tuple-element.24.newkey.newkey1, f32[48,128]{1,0:T(8,128)S(1)} %get-tuple-element.25.newvalue.newvalue1, ...), custom_call_target="tpu_custom_call" | custom-call | bytes 12582912 | tf_op jit(solution)/shard_map/write_cache/pallas_call | solution.py:582
  76.2 0.0 collective-permute-done.17.rest_3_
  76.2 2.2 %collective-permute-done.16.rest_2_ = bf16[48,1024]{1,0:T(8,128)(2,1)S(1)} collective-permute-done((bf16[48,1024]{1,0:T(8,128)(2,1)S(1)}, bf16[48,1024]{1,0:T(8,128)(2,1)S(1)}, u32[]{:S(2)}, u32[]{:S(2)}) %collective-permute-start.16) | collective-permute-done | bytes 98336 | tf_op jit(solution)/shard_map/ppermute | solution.py:444
  78.4 0.0 collective-permute-done.15.rest_1_
  78.4 1.3 %join.1 = bf16[48,4096]{1,0:T(8,128)(2,1)} custom-call(s32[2]{0:T(128)S(1)} %pad_add_fusion.meta, bf16[48,1024]{1,0:T(8,128)(2,1)S(1)} %sum_terms.3.rest_0_, bf16[48,1024]{1,0:T(8,128)(2,1)S(1)} %collective-permute-done.15.rest_1_, bf16[48,1024]{1,0:T(8,128)(2,1)S(1)} %collective-permute-done.16.rest_2_, bf16[48,1024]{1,0:T(8,128)(2,1)S(1)} %collective-permute-done.17.rest_3_), custom_call_target="tpu_custom_call" | custom-call | tf_op jit(solution)/shard_map/join/pallas_call | solution.py:597
  (4 shorter events, 0.0 us)
Async XLA Ops:
  0.7 13.6 %slice-start = ((s8[6291456]{0:T(1024)(128)(4,1)}), s8[4194304]{0:T(1024)(128)(4,1)S(1)}, s32[]{:S(2)}) async-start(s8[6291456]{0:T(1024)(128)(4,1)} %bitcast.6), calls=%async_computation | async-start | bytes 8388608
  0.7 13.6 %slice-start.1 = ((s8[6291456]{0:T(1024)(128)(4,1)}), s8[2097152]{0:T(1024)(128)(4,1)S(1)}, s32[]{:S(2)}) async-start(s8[6291456]{0:T(1024)(128)(4,1)} %bitcast.6), calls=%async_computation.1 | async-start | bytes 4194304
  0.7 13.6 %copy-start.7 = (s32[192]{0:T(256)S(1)}, s32[192]{0:T(256)}, u32[]{:S(2)}) copy-start(s32[192]{0:T(256)} %lengths_s.5) | copy-start | bytes 2308
  8.2 16.0 %copy-start.1 = (bf16[512,4096]{1,0:T(8,128)(2,1)S(1)}, bf16[512,4096]{1,0:T(8,128)(2,1)}, u32[]{:S(2)}) copy-start(bf16[512,4096]{1,0:T(8,128)(2,1)} %wo.3) | copy-start | bytes 12582916
  8.3 16.0 %collective-permute-start = (bf16[2,2,256,128]{3,2,1,0:T(8,128)(2,1)S(1)}, bf16[2,2,256,128]{3,2,1,0:T(8,128)(2,1)S(1)}, u32[]{:S(2)}, u32[]{:S(2)}) collective-permute-start(bf16[2,2,256,128]{3,2,1,0:T(8,128)(2,1)S(1)} %get-tuple-element.26), channel_id=1, source_target_pairs={{0,4},{4,0},{8,12},{12,8},{1,5},{5,1},{9,13},{13,9},{2,6},{6,2},{1... | collective-permute-start | bytes 786440 | tf_op jit(solution)/shard_map/ppermute | solution.py:444
  8.8 34.5 %collective-permute-start.10 = (bf16[2,2,256,128]{3,2,1,0:T(8,128)(2,1)S(1)}, bf16[2,2,256,128]{3,2,1,0:T(8,128)(2,1)S(1)}, u32[]{:S(2)}, u32[]{:S(2)}) collective-permute-start(bf16[2,2,256,128]{3,2,1,0:T(8,128)(2,1)S(1)} %get-tuple-element.34), channel_id=1, source_target_pairs={{0,8},{4,12},{8,0},{12,4},{1,9},{5,13},{9,1},{13,5},{2,10},{6,14},... | collective-permute-start | bytes 786440 | tf_op jit(solution)/shard_map/ppermute | solution.py:444
  11.4 31.9 %collective-permute-start.11 = (bf16[2,2,256,128]{3,2,1,0:T(8,128)(2,1)S(1)}, bf16[2,2,256,128]{3,2,1,0:T(8,128)(2,1)S(1)}, u32[]{:S(2)}, u32[]{:S(2)}) collective-permute-start(bf16[2,2,256,128]{3,2,1,0:T(8,128)(2,1)S(1)} %get-tuple-element.35), channel_id=1, source_target_pairs={{0,12},{4,8},{8,4},{12,0},{1,13},{5,9},{9,5},{13,1},{2,14},{6,10},... | collective-permute-start | bytes 786440 | tf_op jit(solution)/shard_map/ppermute | solution.py:444
  11.4 2.1 %collective-permute-start.1 = (f32[2,1536]{1,0:T(2,128)S(1)}, f32[2,1536]{1,0:T(2,128)S(1)}, u32[]{:S(2)}, u32[]{:S(2)}) collective-permute-start(f32[2,1536]{1,0:T(2,128)S(1)} %get-tuple-element.27), channel_id=1, source_target_pairs={{0,4},{4,0},{8,12},{12,8},{1,5},{5,1},{9,13},{13,9},{2,6},{6,2},{1... | collective-permute-start | bytes 36872 | tf_op jit(solution)/shard_map/ppermute | solution.py:444
  11.6 12.7 %collective-permute-start.2 = (f32[2,1536]{1,0:T(2,128)S(1)}, f32[2,1536]{1,0:T(2,128)S(1)}, u32[]{:S(2)}, u32[]{:S(2)}) collective-permute-start(f32[2,1536]{1,0:T(2,128)S(1)} %get-tuple-element.28), channel_id=1, source_target_pairs={{0,8},{4,12},{8,0},{12,4},{1,9},{5,13},{9,1},{13,5},{2,10},{6,14},... | collective-permute-start | bytes 36872 | tf_op jit(solution)/shard_map/ppermute | solution.py:444
  13.5 10.8 %collective-permute-start.3 = (f32[2,1536]{1,0:T(2,128)S(1)}, f32[2,1536]{1,0:T(2,128)S(1)}, u32[]{:S(2)}, u32[]{:S(2)}) collective-permute-start(f32[2,1536]{1,0:T(2,128)S(1)} %get-tuple-element.29), channel_id=1, source_target_pairs={{0,12},{4,8},{8,4},{12,0},{1,13},{5,9},{9,5},{13,1},{2,14},{6,10},... | collective-permute-start | bytes 36872 | tf_op jit(solution)/shard_map/ppermute | solution.py:444
  14.3 23.8 %copy-start.3 = (bf16[48,4096]{1,0:T(8,128)(2,1)S(1)}, bf16[48,4096]{1,0:T(8,128)(2,1)}, u32[]{:S(2)}) copy-start(bf16[48,4096]{1,0:T(8,128)(2,1)} %hidden.1) | copy-start | bytes 1179652
  14.3 35.5 %copy-start.2 = (bf16[4096,2,128]{2,1,0:T(2,128)(2,1)S(1)}, bf16[4096,2,128]{2,1,0:T(2,128)(2,1)}, u32[]{:S(2)}) copy-start(bf16[4096,2,128]{2,1,0:T(2,128)(2,1)} %param.16) | copy-start | bytes 6291460
  18.9 30.9 %copy-start = (bf16[4096,512]{1,0:T(8,128)(2,1)S(1)}, bf16[4096,512]{1,0:T(8,128)(2,1)}, u32[]{:S(2)}) copy-start(bf16[4096,512]{1,0:T(8,128)(2,1)} %wq.1) | copy-start | bytes 12582916
  18.9 30.9 %copy-start.4 = (f32[256,128]{1,0:T(8,128)S(1)}, f32[256,128]{1,0:T(8,128)}, u32[]{:S(2)}) copy-start(f32[256,128]{1,0:T(8,128)} %constant.12.clone.sin_hbm.sin_ref) | copy-start | bytes 393220
  18.9 30.9 %copy-start.5 = (f32[256,128]{1,0:T(8,128)S(1)}, f32[256,128]{1,0:T(8,128)}, u32[]{:S(2)}) copy-start(f32[256,128]{1,0:T(8,128)} %constant.11.clone.cos_hbm.cos_ref) | copy-start | bytes 393220
  18.9 30.9 %copy-start.6 = (f32[4096]{0:T(1024)S(1)}, f32[4096]{0:T(1024)}, u32[]{:S(2)}) copy-start(f32[4096]{0:T(1024)} %param.14) | copy-start | bytes 49156
  18.9 30.9 %copy-start.8 = (s32[192]{0:T(256)S(1)}, s32[192]{0:T(256)}, u32[]{:S(2)}) copy-start(s32[192]{0:T(256)} %source_s.3) | copy-start | bytes 2308
  25.7 7.6 %collective-permute-start.4 = (bf16[48,1024]{1,0:T(8,128)(2,1)S(1)}, bf16[48,1024]{1,0:T(8,128)(2,1)S(1)}, u32[]{:S(2)}, u32[]{:S(2)}) collective-permute-start(bf16[48,1024]{1,0:T(8,128)(2,1)S(1)} %get-tuple-element.31), channel_id=1, source_target_pairs={{0,3},{1,2},{2,1},{3,0},{4,7},{5,6},{6,5},{7,4},{8,11},{9,10},{10,... | collective-permute-start | bytes 294920 | tf_op jit(solution)/shard_map/ppermute | solution.py:444
  29.6 8.5 %collective-permute-start.5 = (bf16[48,1024]{1,0:T(8,128)(2,1)S(1)}, bf16[48,1024]{1,0:T(8,128)(2,1)S(1)}, u32[]{:S(2)}, u32[]{:S(2)}) collective-permute-start(bf16[48,1024]{1,0:T(8,128)(2,1)S(1)} %get-tuple-element.32), channel_id=1, source_target_pairs={{0,2},{1,3},{2,0},{3,1},{4,6},{5,7},{6,4},{7,5},{8,10},{9,11},{10,... | collective-permute-start | bytes 294920 | tf_op jit(solution)/shard_map/ppermute | solution.py:444
  29.6 8.5 %collective-permute-start.6 = (bf16[48,1024]{1,0:T(8,128)(2,1)S(1)}, bf16[48,1024]{1,0:T(8,128)(2,1)S(1)}, u32[]{:S(2)}, u32[]{:S(2)}) collective-permute-start(bf16[48,1024]{1,0:T(8,128)(2,1)S(1)} %get-tuple-element.33), channel_id=1, source_target_pairs={{0,1},{1,0},{2,3},{3,2},{4,5},{5,4},{6,7},{7,6},{8,9},{9,8},{10,11... | collective-permute-start | bytes 294920 | tf_op jit(solution)/shard_map/ppermute | solution.py:444
  38.8 7.6 %collective-permute-start.9 = (bf16[48,1024]{1,0:T(8,128)(2,1)S(1)}, bf16[48,1024]{1,0:T(8,128)(2,1)S(1)}, u32[]{:S(2)}, u32[]{:S(2)}) collective-permute-start(bf16[48,1024]{1,0:T(8,128)(2,1)S(1)} %sum_terms.2.rest_0_.hidden), channel_id=1, source_target_pairs={{0,3},{1,2},{2,1},{3,0},{4,7},{5,6},{6,5},{7,4},{8,11},{9,10},{10,... | collective-permute-start | bytes 294920 | tf_op jit(solution)/shard_map/ppermute | solution.py:444
  41.3 8.4 %collective-permute-start.8 = (bf16[48,1024]{1,0:T(8,128)(2,1)S(1)}, bf16[48,1024]{1,0:T(8,128)(2,1)S(1)}, u32[]{:S(2)}, u32[]{:S(2)}) collective-permute-start(bf16[48,1024]{1,0:T(8,128)(2,1)S(1)} %sum_terms.2.rest_0_.hidden), channel_id=1, source_target_pairs={{0,2},{1,3},{2,0},{3,1},{4,6},{5,7},{6,4},{7,5},{8,10},{9,11},{10,... | collective-permute-start | bytes 294920 | tf_op jit(solution)/shard_map/ppermute | solution.py:444
  41.3 8.4 %collective-permute-start.7 = (bf16[48,1024]{1,0:T(8,128)(2,1)S(1)}, bf16[48,1024]{1,0:T(8,128)(2,1)S(1)}, u32[]{:S(2)}, u32[]{:S(2)}) collective-permute-start(bf16[48,1024]{1,0:T(8,128)(2,1)S(1)} %sum_terms.2.rest_0_.hidden), channel_id=1, source_target_pairs={{0,1},{1,0},{2,3},{3,2},{4,5},{5,4},{6,7},{7,6},{8,9},{9,8},{10,11... | collective-permute-start | bytes 294920 | tf_op jit(solution)/shard_map/ppermute | solution.py:444
  56.7 7.7 %collective-permute-start.12 = (bf16[48,1024]{1,0:T(8,128)(2,1)S(1)}, bf16[48,1024]{1,0:T(8,128)(2,1)S(1)}, u32[]{:S(2)}, u32[]{:S(2)}) collective-permute-start(bf16[48,1024]{1,0:T(8,128)(2,1)S(1)} %get-tuple-element.37), channel_id=1, source_target_pairs={{0,3},{1,2},{2,1},{3,0},{4,7},{5,6},{6,5},{7,4},{8,11},{9,10},{10,... | collective-permute-start | bytes 294920 | tf_op jit(solution)/shard_map/ppermute | solution.py:444
  58.3 8.6 %collective-permute-start.13 = (bf16[48,1024]{1,0:T(8,128)(2,1)S(1)}, bf16[48,1024]{1,0:T(8,128)(2,1)S(1)}, u32[]{:S(2)}, u32[]{:S(2)}) collective-permute-start(bf16[48,1024]{1,0:T(8,128)(2,1)S(1)} %get-tuple-element.38), channel_id=1, source_target_pairs={{0,2},{1,3},{2,0},{3,1},{4,6},{5,7},{6,4},{7,5},{8,10},{9,11},{10,... | collective-permute-start | bytes 294920 | tf_op jit(solution)/shard_map/ppermute | solution.py:444
  58.3 8.6 %collective-permute-start.14 = (bf16[48,1024]{1,0:T(8,128)(2,1)S(1)}, bf16[48,1024]{1,0:T(8,128)(2,1)S(1)}, u32[]{:S(2)}, u32[]{:S(2)}) collective-permute-start(bf16[48,1024]{1,0:T(8,128)(2,1)S(1)} %get-tuple-element.39), channel_id=1, source_target_pairs={{0,1},{1,0},{2,3},{3,2},{4,5},{5,4},{6,7},{7,6},{8,9},{9,8},{10,11... | collective-permute-start | bytes 294920 | tf_op jit(solution)/shard_map/ppermute | solution.py:444
  67.5 8.7 %collective-permute-start.17 = (bf16[48,1024]{1,0:T(8,128)(2,1)S(1)}, bf16[48,1024]{1,0:T(8,128)(2,1)S(1)}, u32[]{:S(2)}, u32[]{:S(2)}) collective-permute-start(bf16[48,1024]{1,0:T(8,128)(2,1)S(1)} %sum_terms.3.rest_0_), channel_id=1, source_target_pairs={{0,3},{1,2},{2,1},{3,0},{4,7},{5,6},{6,5},{7,4},{8,11},{9,10},{10,... | collective-permute-start | bytes 294920 | tf_op jit(solution)/shard_map/ppermute | solution.py:444
  69.7 8.7 %collective-permute-start.16 = (bf16[48,1024]{1,0:T(8,128)(2,1)S(1)}, bf16[48,1024]{1,0:T(8,128)(2,1)S(1)}, u32[]{:S(2)}, u32[]{:S(2)}) collective-permute-start(bf16[48,1024]{1,0:T(8,128)(2,1)S(1)} %sum_terms.3.rest_0_), channel_id=1, source_target_pairs={{0,2},{1,3},{2,0},{3,1},{4,6},{5,7},{6,4},{7,5},{8,10},{9,11},{10,... | collective-permute-start | bytes 294920 | tf_op jit(solution)/shard_map/ppermute | solution.py:444
  69.7 8.7 %collective-permute-start.15 = (bf16[48,1024]{1,0:T(8,128)(2,1)S(1)}, bf16[48,1024]{1,0:T(8,128)(2,1)S(1)}, u32[]{:S(2)}, u32[]{:S(2)}) collective-permute-start(bf16[48,1024]{1,0:T(8,128)(2,1)S(1)} %sum_terms.3.rest_0_), channel_id=1, source_target_pairs={{0,1},{1,0},{2,3},{3,2},{4,5},{5,4},{6,7},{7,6},{8,9},{9,8},{10,11... | collective-permute-start | bytes 294920 | tf_op jit(solution)/shard_map/ppermute | solution.py:444

commit v4 on v3

--- a/solution.py
+++ b/solution.py
@@ -15,6 +15,7 @@
 GROUP = 8
 PIECE = 16
 CHUNK = 8
+NOTE = 16
 
 F32 = jnp.float32
 BF16 = jnp.bfloat16
@@ -153,9 +154,10 @@
 ):
     others = peers - 1
     moving = others * MOVE
-    boxes, notes = rest[:others], rest[others : 2 * others]
+    box, notes = rest[0], (None,) + rest[1:others]
     (wq, wkv, normed3, spread, cos_rows, sin_rows, leaving, hidden32, source_s, lengths_s, source_v,
-     hidden, gain, cos_ref, sin_ref, small_sem, wq_sem, wkv_sem, in_sem, out_sem) = rest[2 * others :]
+     hidden, gain, cos_ref, sin_ref, tail, small_sem, wq_sem, wkv_sem, in_sem,
+     box_sem) = rest[others:]
     width = hidden.shape[1]
     me, me_tp = meta[0], meta[1]
     wq_copies = weight_copies(wq_hbm, wq, wq_sem, 4)
@@ -196,6 +198,7 @@
             slot = jnp.where(known, slot, 0)
             send_slots.append(slot)
             plan[at] = jnp.where((r >= 0) & (r < src.shape[1]), r - low, -1)
+            plan[moving + at] = slot
             pltpu.make_async_copy(cache_hbm.at[slot], leaving.at[at], in_sem.at[at]).start()
 
     for copy in small[2:]:
@@ -223,23 +226,37 @@
             leaving, at, positions[at],
             newkey_out[pl.ds(slot, 1), :], newvalue_out[pl.ds(slot, 1), :],
         )
-    for k in range(others):
+    cap = leaving.shape[2]
+    copies = [
         pltpu.make_async_copy(
-            leaving.at[pl.ds(k * MOVE, MOVE)], boxes[k], out_sem.at[k]
-        ).start()
+            leaving.at[pl.ds(0, MOVE)], box.at[:, :, pl.ds(0, cap), :], box_sem.at[0]
+        )
+    ]
+    copies[0].start()
     rows = [query_out[pl.ds(pl.multiple_of(slot * GROUP, GROUP), GROUP), :] for slot in send_slots]
     attended = attend(leaving, list(range(moving)), positions, rows)
     column = pl.multiple_of(me_tp * shard, shard)
     for at, slot in enumerate(send_slots):
-        note = notes[at // MOVE]
         m = at % MOVE
-        for g in range(heads):
-            note[m : m + 1, g * HD : (g + 1) * HD] = attended[at][g : g + 1, :]
-        note[m : m + 1, heads * HD :] = hidden32[pl.ds(slot, 1), pl.ds(column, shard)]
-    for k in range(others):
-        pltpu.make_async_copy(
-            leaving.at[pl.ds(k * MOVE, MOVE)], boxes[k], out_sem.at[k]
-        ).wait()
+        residual = hidden32[pl.ds(slot, 1), pl.ds(column, shard)]
+        if at < MOVE:
+            blocks = [attended[at][g : g + 1, :] for g in range(heads)]
+            blocks += [residual[:, b * HD : (b + 1) * HD] for b in range(shard // HD)]
+            blocks += [jnp.zeros((1, HD), F32)] * (NOTE - len(blocks))
+            tail[m] = jnp.concatenate(blocks, axis=0).astype(BF16)
+            copies.append(
+                pltpu.make_async_copy(
+                    tail.at[m], box.at[m, 0, pl.ds(cap, NOTE), :], box_sem.at[1 + m]
+                )
+            )
+            copies[-1].start()
+        else:
+            note = notes[at // MOVE]
+            for g in range(heads):
+                note[m : m + 1, g * HD : (g + 1) * HD] = attended[at][g : g + 1, :]
+            note[m : m + 1, heads * HD :] = residual
+    for copy in copies:
+        copy.wait()
 
 
 def attend_kernel(
@@ -269,45 +286,76 @@
         out[:, g * HD : (g + 1) * HD] = attended_rows[pl.ds(g, slots, stride=GROUP), :].astype(BF16)
 
 
-def project_out(attended, wo, own, sends, me_tp, peers_tp):
+def project_out(attended, wo, residual, own, sends, me_tp, peers_tp):
     shard = own.shape[1]
     for k in list(range(peers_tp - 1, 0, -1)) + [0]:
         column = pl.multiple_of(jnp.bitwise_xor(me_tp, k) * shard, shard)
         part = jnp.dot(attended, wo[:, pl.ds(column, shard)], preferred_element_type=F32)
         if k == 0:
-            own[...] = part
+            own[...] = residual + part
         else:
             sends[k - 1][...] = part.astype(BF16)
 
 
-def out_kernel(peers, peers_tp, meta, plan, attended, wo, _box, *rest):
-    notes = rest[: peers - 1]
-    own = rest[peers - 1]
-    sends = rest[peers:]
+def out_kernel(
+    peers, peers_tp, slots, meta, lengths_s, plan, attended, wo, hidden, newkey, newvalue, box_hbm,
+    cache_hbm, *rest,
+):
+    notes, rest = rest[: peers - 2], rest[peers - 2 :]
+    own, sends, boxes = rest[0], rest[1:peers_tp], rest[peers_tp : peers_tp + peers - 2]
+    leaving, tail, sem, in_sem, out_sem = rest[peers_tp + peers - 2 :]
+    moving = (peers - 1) * MOVE
+    send_slots = [plan[moving + at] for at in range(MOVE, moving)]
+    packs = [
+        pltpu.make_async_copy(cache_hbm.at[slot], leaving.at[i], in_sem.at[i])
+        for i, slot in enumerate(send_slots)
+    ]
+    for pack in packs:
+        pack.start()
+    shard = own.shape[1]
+    cap = box_hbm.shape[2] - NOTE
+    copy = pltpu.make_async_copy(box_hbm.at[:, 0, pl.ds(cap, NOTE), :], tail, sem.at[0])
+    copy.start()
     rows = attended[...].astype(F32)
-    index = lax.broadcasted_iota(I32, rows.shape, 0)
+    heads = rows.shape[1] // HD
+    column = pl.multiple_of(meta[1] * shard, shard)
+    residual = hidden[:, pl.ds(column, shard)].astype(F32)
+    row_index = lax.broadcasted_iota(I32, rows.shape, 0)
+    residual_index = lax.broadcasted_iota(I32, residual.shape, 0)
+    copy.wait()
     for at in range((peers - 1) * MOVE):
-        note = notes[at // MOVE][at % MOVE : at % MOVE + 1, : rows.shape[1]]
-        rows = jnp.where(index == plan[at], note, rows)
-    project_out(rows.astype(BF16), wo, own, sends, meta[1], peers_tp)
-
-
-def sum_kernel(peers, peers_tp, heads, meta, plan, hidden, own, *rest):
-    got, notes, out = rest[: peers_tp - 1], rest[peers_tp - 1 : -1], rest[-1]
-    shard = own.shape[1]
+        m = at % MOVE
+        if at < MOVE:
+            blocks = tail[m].astype(F32)
+            blocks = [blocks[b : b + 1, :] for b in range(heads + shard // HD)]
+            note = jnp.concatenate(blocks, axis=1)
+        else:
+            note = notes[at // MOVE - 1][m : m + 1, :]
+        rows = jnp.where(row_index == plan[at], note[:, : heads * HD], rows)
+        residual = jnp.where(residual_index == plan[at], note[:, heads * HD :], residual)
+    for pack in packs:
+        pack.wait()
+    for i, slot in enumerate(send_slots):
+        put_row(
+            leaving, i, lengths_s[meta[0] * slots + slot],
+            newkey[pl.ds(slot, 1), :], newvalue[pl.ds(slot, 1), :],
+        )
+    outs = [
+        pltpu.make_async_copy(leaving.at[pl.ds(k * MOVE, MOVE)], out, out_sem.at[k])
+        for k, out in enumerate(boxes)
+    ]
+    for out in outs:
+        out.start()
+    project_out(rows.astype(BF16), wo, residual, own, sends, meta[1], peers_tp)
+    for out in outs:
+        out.wait()
+
+
+def sum_kernel(own, *rest):
     total = own[...]
-    for part in got:
+    for part in rest[:-1]:
         total = total + part[...].astype(F32)
-    if notes:
-        column = pl.multiple_of(meta[1] * shard, shard)
-        residual = hidden[:, pl.ds(column, shard)].astype(F32)
-        index = lax.broadcasted_iota(I32, residual.shape, 0)
-        for at in range((peers - 1) * MOVE):
-            note = notes[at // MOVE][at % MOVE : at % MOVE + 1, heads * HD :]
-            residual = jnp.where(index == plan[at], note, residual)
-    else:
-        residual = hidden[...].astype(F32)
-    out[...] = (residual + total).astype(BF16)
+    rest[-1][...] = total.astype(BF16)
 
 
 def load_slots(slots, peers, cache_hbm, box_hbm, buffer, in_sem):
@@ -318,7 +366,7 @@
     for k in range(peers - 1):
         copies.append(
             pltpu.make_async_copy(
-                box_hbm[k],
+                box_hbm[k].at[:, :, pl.ds(0, cache_hbm.shape[2]), :],
                 buffer.at[pl.ds(slots + k * MOVE, MOVE)],
                 in_sem.at[slots // CHUNK + k],
             )
@@ -395,7 +443,7 @@
     attended = jnp.concatenate(
         [attended_rows[pl.ds(g, slots, stride=GROUP), :].astype(BF16) for g in range(heads)], axis=1
     )
-    project_out(attended, wo, own, sends, me_tp, peers_tp)
+    project_out(attended, wo, blocks[0][...].astype(F32), own, sends, me_tp, peers_tp)
 
 
 def cache_kernel(
@@ -474,18 +522,18 @@
     flops = 2 * slots * width * (heads + 2) * HD
     cache_bytes = kv_cache.size * 2
 
-    query, newkey1, newvalue1, plan, *rest = pl.pallas_call(
+    query, newkey1, newvalue1, plan, *notes = pl.pallas_call(
         functools.partial(first_kernel, peers, slots, heads, shard),
         out_shape=[
             jax.ShapeDtypeStruct((slots * GROUP, HD), F32),
             row32,
             row32,
-            jax.ShapeDtypeStruct((moving,), I32),
+            jax.ShapeDtypeStruct((2 * moving,), I32),
         ]
-        + [jax.ShapeDtypeStruct((MOVE,) + kv_cache.shape[1:], BF16)] * others
-        + [jax.ShapeDtypeStruct((MOVE, note_width), F32)] * others,
+        + [jax.ShapeDtypeStruct((MOVE, 2, cap + NOTE, HD), BF16)]
+        + [jax.ShapeDtypeStruct((MOVE, note_width), F32)] * (others - 1),
         in_specs=[SMEM] + [HBM] * 9,
-        out_specs=[VMEM] * 3 + [SMEM] + [ANY] * others + [VMEM] * others,
+        out_specs=[VMEM] * 3 + [SMEM, ANY] + [VMEM] * (others - 1),
         scratch_shapes=weights
         + stages
         + [
@@ -498,11 +546,12 @@
             pltpu.VMEM((1, width), F32),
             pltpu.VMEM(cosine.shape, F32),
             pltpu.VMEM(cosine.shape, F32),
+            pltpu.VMEM((MOVE, NOTE, HD), BF16),
             dma((7,)),
             dma((4,)),
             dma((4,)),
             dma((moving,)),
-            dma((others,)),
+            dma((1 + MOVE,)),
         ],
         compiler_params=params(24),
         cost_estimate=cost(flops, (query_weight.size + wkv.size) * 2),
@@ -512,9 +561,7 @@
         for x in (source.reshape(1, -1), lengths.reshape(1, -1), hidden, gain, cosine, sine,
                   query_weight, wkv, kv_cache)
     ))
-    boxes, notes = rest[:others], rest[others:]
     got_notes = [swapped(note, "inst", peers, k + 1) for k, note in enumerate(notes)]
-    got_boxes = [swapped(box, "inst", peers, k + 1) for k, box in enumerate(boxes)]
 
     attended = pl.pallas_call(
         functools.partial(attend_kernel, slots, heads),
@@ -533,31 +580,42 @@
 
     sent = [jax.ShapeDtypeStruct((slots, shard), F32)]
     sent += [jax.ShapeDtypeStruct((slots, shard), BF16)] * (peers_tp - 1)
-    own, *sends = pl.pallas_call(
-        functools.partial(out_kernel, peers, peers_tp),
-        out_shape=sent,
-        in_specs=[SMEM] * 2 + [VMEM] * 2 + [ANY] + [VMEM] * others,
-        out_specs=[VMEM] * peers_tp,
-        compiler_params=params(16),
+    own, *rest = pl.pallas_call(
+        functools.partial(out_kernel, peers, peers_tp, slots),
+        out_shape=sent
+        + [jax.ShapeDtypeStruct((MOVE,) + kv_cache.shape[1:], BF16)] * (others - 1),
+        in_specs=[SMEM] * 3 + [VMEM] * 5 + [ANY] * 2 + [VMEM] * (others - 1),
+        out_specs=[VMEM] * peers_tp + [ANY] * (others - 1),
+        scratch_shapes=[
+            pltpu.VMEM((moving - MOVE,) + kv_cache.shape[1:], BF16),
+            pltpu.VMEM((MOVE, NOTE, HD), BF16),
+            dma((1,)),
+            dma((moving - MOVE,)),
+            dma((others - 1,)),
+        ],
+        compiler_params=params(20),
         cost_estimate=cost(2 * slots * width * heads * HD, out_weight.size * 2),
         name="out_projection",
-    )(meta, plan, attended, out_weight, got_boxes[0], *got_notes)
-
-    def summed(residual, own, sends, notes):
+    )(meta, lengths, plan, attended, out_weight, hidden, newkey1, newvalue1, got_notes[0], kv_cache,
+      *got_notes[1:])
+    sends, boxes = rest[: peers_tp - 1], rest[peers_tp - 1 :]
+    got_boxes = got_notes[:1] + [swapped(box, "inst", peers, k + 2) for k, box in enumerate(boxes)]
+
+    def summed(own, sends):
         got = [swapped(sends[k - 1], "tp", peers_tp, k) for k in range(peers_tp - 1, 0, -1)]
         shard_rows = pl.pallas_call(
-            functools.partial(sum_kernel, peers, peers_tp, heads),
+            sum_kernel,
             out_shape=jax.ShapeDtypeStruct((slots, shard), BF16),
-            in_specs=[SMEM] * 2 + [VMEM] * (2 + len(got) + len(notes)),
+            in_specs=[VMEM] * peers_tp,
             out_specs=VMEM,
             compiler_params=params(16),
             name="sum_terms",
-        )(meta, plan, residual, own, *got, *notes)
+        )(own, *got)
         return [shard_rows] + [
             swapped(shard_rows, "tp", peers_tp, k) for k in range(1, peers_tp)
         ]
 
-    pieces = summed(hidden, own, sends, got_notes)
+    pieces = summed(own, sends)
 
     newkey2, newvalue2, own, *sends = pl.pallas_call(
         functools.partial(second_kernel, peers, peers_tp, slots, heads),
@@ -578,7 +636,7 @@
     )(meta, source, lengths, plan, gain, cosine, sine, newkey1, newvalue1, query_weight, wkv,
       out_weight, kv_cache, *pieces, *got_boxes)
 
-    pieces = summed(pieces[0], own, sends, [])
+    pieces = summed(own, sends)
     final_cache = pl.pallas_call(
         functools.partial(cache_kernel, peers, slots),
         out_shape=jax.ShapeDtypeStruct(kv_cache.shape, BF16),

time: 79.9 us -> 73.9 us (0.925)
  waiting for transfers between devices: 27.7 us -> 23 us
  starting transfers between devices: 23.9 us -> 22.8 us
    ppermute x18 -> x17, waiting for transfers between devices: 27.7 us -> 23 us  [swapped(): return lax.ppermute(x, axis, [(i, i ^ k) for i in range(size)])]
    ppermute x18 -> x17, starting transfers between devices: 23.9 us -> 22.8 us  [swapped(): return lax.ppermute(x, axis, [(i, i ^ k) for i in range(size)])]
  transfers between devices with their start and end apart: 18 -> 17, of which waited for: 8 -> 7; matrix products, arithmetic and copies ran while one was open for 0% -> 0% of each run, Pallas kernels for 14% -> 12%
where the time goes in v4:
time: 73.9 us; the launch traced here: 73.7 us
  Pallas kernels  26.9 us (36%)
  waiting for transfers between devices  23 us (31%)
  starting transfers between devices  22.8 us (31%)
  between operations  0.87 us (1%)
    ppermute x17, waiting for transfers between devices, swapped(): return lax.ppermute(x, axis, [(i, i ^ k) for i in range(size)])  23 us
    ppermute x17, starting transfers between devices, swapped(): return lax.ppermute(x, axis, [(i, i ^ k) for i in range(size)])  22.8 us
    pallas_call x1, Pallas kernels, local(): pl.pallas_call(functools.partial(first_kernel, peers, slots, heads, shard...  7.51 us
    pallas_call x1, Pallas kernels, local(): pl.pallas_call(functools.partial(second_kernel, peers, peers_tp, slots, h...  6.83 us
    pallas_call x1, Pallas kernels, local(): pl.pallas_call(functools.partial(attend_kernel, slots, heads), out_shape=...  4.56 us
    pallas_call x1, Pallas kernels, local(): pl.pallas_call(functools.partial(cache_kernel, peers, slots), out_shape=j...  4.23 us
    pallas_call x1, Pallas kernels, local(): pl.pallas_call(functools.partial(out_kernel, peers, peers_tp, slots), out...  2.34 us
  transfers between devices with their start and end apart: 17, of which 7 were waited for; matrix products, arithmetic and copies ran while one was open for 0% of the time, Pallas kernels for 12%

profile of v4, /device:TPU:0, one launch (start us, length us, event | category | flops | bytes accessed | tf_op | source)
XLA Modules:
  0.0 73.7 jit_solution(3162861903350154813)
XLA Ops:
  0.6 0.1 pad_add_fusion.meta
  0.7 0.0 slice-start
  0.7 0.0 slice-start.1
  0.7 0.0 copy-start.7
  0.7 7.5 %first_step.1 = (f32[384,128]{1,0:T(8,128)S(1)}, f32[48,128]{1,0:T(8,128)S(1)}, f32[48,128]{1,0:T(8,128)S(1)}, s32[12]{0:T(128)S(1)}, bf16[2,2,272,128]{3,2,1,0:...) custom-call(s32[2]{0:T(128)S(1)} %pad_add_fusion.meta, s32[1,192]{1,0:T(1,128)} %bitcast.13, ...), custom_call_target="tpu_custom_call" | custom-call | flops 301989888 | bytes 6291456 | tf_op jit(solution)/shard_map/first_step/pallas_call | solution.py:525
  8.2 0.0 copy-start.1
  8.2 0.0 copy-start.3
  8.3 0.5 collective-permute-start
  8.8 2.6 %collective-permute-start.1 = (f32[2,1536]{1,0:T(2,128)S(1)}, f32[2,1536]{1,0:T(2,128)S(1)}, u32[]{:S(2)}, u32[]{:S(2)}) collective-permute-start(f32[2,1536]{1,0:T(2,128)S(1)} %get-tuple-element.26), channel_id=1, source_target_pairs={{0,8},{4,12},{8,0},{12,4},{1,9},{5,13},{9,1},{13,5},{2,10},{6,14},... | collective-permute-start | bytes 36872 | tf_op jit(solution)/shard_map/ppermute | solution.py:492
  11.4 0.1 collective-permute-start.2
  11.4 0.0 slice-done
  11.4 0.0 slice-done.1
  11.4 0.0 copy-done.7
  11.4 4.6 %attention.1.attended = bf16[48,512]{1,0:T(8,128)(2,1)S(1)} custom-call(s32[2]{0:T(128)S(1)} %pad_add_fusion.meta, s32[192]{0:T(256)S(1)} %copy-done.7, f32[384,128]{1,0:T(8,128)S(1)} %get-tuple-element.24.query, f32[48,128]{1,0:T(8,128)S(1)} %get-tuple-element.22.newkey.newkey1, f32[48,128]{1,0:T(8,128)S(1)} %get-tuple-element.23.newvalue.newvalue1, ...), custom_call_target="tpu_custom_call" | custom-call | flops 25165824 | bytes 6291456 | tf_op jit(solution)/shard_map/attention/pallas_call | solution.py:566
  16.0 0.0 collective-permute-done.1.rest_0_
  16.0 0.0 collective-permute-done.2.rest_1_
  16.0 0.0 collective-permute-done.box_hbm.rest_4_.rest_0_
  16.0 0.0 copy-done.1
  16.0 0.0 copy-done.3
  16.1 0.0 copy-start
  16.1 0.0 copy-start.2
  16.1 0.0 copy-start.4
  16.1 0.0 copy-start.5
  16.1 0.0 copy-start.6
  16.1 0.0 copy-start.8
  16.1 2.3 %out_projection.1 = (f32[48,1024]{1,0:T(8,128)S(1)}, bf16[48,1024]{1,0:T(8,128)(2,1)S(1)}, bf16[48,1024]{1,0:T(8,128)(2,1)S(1)}, bf16[48,1024]{1,0:T(8,128)(2,1)...) custom-call(s32[2]{0:T(128)S(1)} %pad_add_fusion.meta, s32[192]{0:T(256)S(1)} %copy-done.7, ...), custom_call_target="tpu_custom_call" | custom-call | flops 201326592 | bytes 4194304 | tf_op jit(solution)/shard_map/out_projection/pallas_call | solution.py:583
  18.5 1.8 %collective-permute-start.9 = (bf16[2,2,256,128]{3,2,1,0:T(8,128)(2,1)S(1)}, bf16[2,2,256,128]{3,2,1,0:T(8,128)(2,1)S(1)}, u32[]{:S(2)}, u32[]{:S(2)}) collective-permute-start(bf16[2,2,256,128]{3,2,1,0:T(8,128)(2,1)S(1)} %get-tuple-element.32), channel_id=1, source_target_pairs={{0,8},{4,12},{8,0},{12,4},{1,9},{5,13},{9,1},{13,5},{2,10},{6,14},... | collective-permute-start | bytes 786440 | tf_op jit(solution)/shard_map/ppermute | solution.py:492
  20.3 0.0 collective-permute-start.10
  20.3 3.7 %collective-permute-start.3 = (bf16[48,1024]{1,0:T(8,128)(2,1)S(1)}, bf16[48,1024]{1,0:T(8,128)(2,1)S(1)}, u32[]{:S(2)}, u32[]{:S(2)}) collective-permute-start(bf16[48,1024]{1,0:T(8,128)(2,1)S(1)} %get-tuple-element.29), channel_id=1, source_target_pairs={{0,3},{1,2},{2,1},{3,0},{4,7},{5,6},{6,5},{7,4},{8,11},{9,10},{10,... | collective-permute-start | bytes 294920 | tf_op jit(solution)/shard_map/ppermute | solution.py:492
  24.1 0.0 collective-permute-start.4
  24.1 0.7 collective-permute-start.5
  24.7 3.2 %collective-permute-done.3.rest_0_ = bf16[48,1024]{1,0:T(8,128)(2,1)S(1)} collective-permute-done((bf16[48,1024]{1,0:T(8,128)(2,1)S(1)}, bf16[48,1024]{1,0:T(8,128)(2,1)S(1)}, u32[]{:S(2)}, u32[]{:S(2)}) %collective-permute-start.3) | collective-permute-done | bytes 98336 | tf_op jit(solution)/shard_map/ppermute | solution.py:492
  27.9 5.0 %collective-permute-done.4.rest_1_ = bf16[48,1024]{1,0:T(8,128)(2,1)S(1)} collective-permute-done((bf16[48,1024]{1,0:T(8,128)(2,1)S(1)}, bf16[48,1024]{1,0:T(8,128)(2,1)S(1)}, u32[]{:S(2)}, u32[]{:S(2)}) %collective-permute-start.4) | collective-permute-done | bytes 98336 | tf_op jit(solution)/shard_map/ppermute | solution.py:492
  32.9 0.0 collective-permute-done.5.rest_2_
  32.9 0.1 sum_terms.2.rest_0_
  33.0 2.5 %collective-permute-start.8 = (bf16[48,1024]{1,0:T(8,128)(2,1)S(1)}, bf16[48,1024]{1,0:T(8,128)(2,1)S(1)}, u32[]{:S(2)}, u32[]{:S(2)}) collective-permute-start(bf16[48,1024]{1,0:T(8,128)(2,1)S(1)} %sum_terms.2.rest_0_), channel_id=1, source_target_pairs={{0,3},{1,2},{2,1},{3,0},{4,7},{5,6},{6,5},{7,4},{8,11},{9,10},{10,... | collective-permute-start | bytes 294920 | tf_op jit(solution)/shard_map/ppermute | solution.py:492
  35.5 0.0 collective-permute-start.7
  35.5 1.9 %collective-permute-start.6 = (bf16[48,1024]{1,0:T(8,128)(2,1)S(1)}, bf16[48,1024]{1,0:T(8,128)(2,1)S(1)}, u32[]{:S(2)}, u32[]{:S(2)}) collective-permute-start(bf16[48,1024]{1,0:T(8,128)(2,1)S(1)} %sum_terms.2.rest_0_), channel_id=1, source_target_pairs={{0,1},{1,0},{2,3},{3,2},{4,5},{5,4},{6,7},{7,6},{8,9},{9,8},{10,11... | collective-permute-start | bytes 294920 | tf_op jit(solution)/shard_map/ppermute | solution.py:492
  37.4 3.1 %collective-permute-done.8.rest_3_ = bf16[48,1024]{1,0:T(8,128)(2,1)S(1)} collective-permute-done((bf16[48,1024]{1,0:T(8,128)(2,1)S(1)}, bf16[48,1024]{1,0:T(8,128)(2,1)S(1)}, u32[]{:S(2)}, u32[]{:S(2)}) %collective-permute-start.8) | collective-permute-done | bytes 98336 | tf_op jit(solution)/shard_map/ppermute | solution.py:492
  40.6 3.4 %collective-permute-done.7.rest_2_ = bf16[48,1024]{1,0:T(8,128)(2,1)S(1)} collective-permute-done((bf16[48,1024]{1,0:T(8,128)(2,1)S(1)}, bf16[48,1024]{1,0:T(8,128)(2,1)S(1)}, u32[]{:S(2)}, u32[]{:S(2)}) %collective-permute-start.7) | collective-permute-done | bytes 98336 | tf_op jit(solution)/shard_map/ppermute | solution.py:492
  44.0 0.0 collective-permute-done.6.rest_1_
  44.0 0.0 collective-permute-done.9.rest_5_.rest_1_
  44.0 0.0 collective-permute-done.10.rest_6_.rest_2_
  44.0 0.0 copy-done
  44.0 0.0 copy-done.2
  44.0 0.0 copy-done.4
  44.0 0.0 copy-done.5
  44.0 0.0 copy-done.6
  44.0 0.0 copy-done.8
  44.0 6.8 %second_step.1 = (f32[48,128]{1,0:T(8,128)S(1)}, f32[48,128]{1,0:T(8,128)S(1)}, f32[48,1024]{1,0:T(8,128)S(1)}, bf16[48,1024]{1,0:T(8,128)(2,1)S(1)}, bf16[48,10...) custom-call(s32[2]{0:T(128)S(1)} %pad_add_fusion.meta, s32[192]{0:T(256)S(1)} %copy-done.8, s32[192]{0:T(256)S(1)} %copy-done.7, ...), custom_call_target="tpu_custom_call" | custom-call | flops 905969664 | bytes 18874368 | tf_op jit(solution)/shard_map/second_step/pallas_call | solution.py:620
  50.9 2.0 %collective-permute-start.11 = (bf16[48,1024]{1,0:T(8,128)(2,1)S(1)}, bf16[48,1024]{1,0:T(8,128)(2,1)S(1)}, u32[]{:S(2)}, u32[]{:S(2)}) collective-permute-start(bf16[48,1024]{1,0:T(8,128)(2,1)S(1)} %get-tuple-element.35), channel_id=1, source_target_pairs={{0,3},{1,2},{2,1},{3,0},{4,7},{5,6},{6,5},{7,4},{8,11},{9,10},{10,... | collective-permute-start | bytes 294920 | tf_op jit(solution)/shard_map/ppermute | solution.py:492
  52.9 0.0 collective-permute-start.12
  52.9 2.4 %collective-permute-start.13 = (bf16[48,1024]{1,0:T(8,128)(2,1)S(1)}, bf16[48,1024]{1,0:T(8,128)(2,1)S(1)}, u32[]{:S(2)}, u32[]{:S(2)}) collective-permute-start(bf16[48,1024]{1,0:T(8,128)(2,1)S(1)} %get-tuple-element.37), channel_id=1, source_target_pairs={{0,1},{1,0},{2,3},{3,2},{4,5},{5,4},{6,7},{7,6},{8,9},{9,8},{10,11... | collective-permute-start | bytes 294920 | tf_op jit(solution)/shard_map/ppermute | solution.py:492
  55.3 3.1 %collective-permute-done.11.rest_0_ = bf16[48,1024]{1,0:T(8,128)(2,1)S(1)} collective-permute-done((bf16[48,1024]{1,0:T(8,128)(2,1)S(1)}, bf16[48,1024]{1,0:T(8,128)(2,1)S(1)}, u32[]{:S(2)}, u32[]{:S(2)}) %collective-permute-start.11) | collective-permute-done | bytes 98336 | tf_op jit(solution)/shard_map/ppermute | solution.py:492
  58.5 3.0 %collective-permute-done.12.rest_1_ = bf16[48,1024]{1,0:T(8,128)(2,1)S(1)} collective-permute-done((bf16[48,1024]{1,0:T(8,128)(2,1)S(1)}, bf16[48,1024]{1,0:T(8,128)(2,1)S(1)}, u32[]{:S(2)}, u32[]{:S(2)}) %collective-permute-start.12) | collective-permute-done | bytes 98336 | tf_op jit(solution)/shard_map/ppermute | solution.py:492
  61.4 0.0 collective-permute-done.13.rest_2_
  61.5 2.2 %collective-permute-start.16 = (bf16[48,1024]{1,0:T(8,128)(2,1)S(1)}, bf16[48,1024]{1,0:T(8,128)(2,1)S(1)}, u32[]{:S(2)}, u32[]{:S(2)}) collective-permute-start(bf16[48,1024]{1,0:T(8,128)(2,1)S(1)} %sum_terms.3.rest_0_), channel_id=1, source_target_pairs={{0,3},{1,2},{2,1},{3,0},{4,7},{5,6},{6,5},{7,4},{8,11},{9,10},{10,... | collective-permute-start | bytes 294920 | tf_op jit(solution)/shard_map/ppermute | solution.py:492
  63.7 0.0 collective-permute-start.15
  63.7 2.2 %collective-permute-start.14 = (bf16[48,1024]{1,0:T(8,128)(2,1)S(1)}, bf16[48,1024]{1,0:T(8,128)(2,1)S(1)}, u32[]{:S(2)}, u32[]{:S(2)}) collective-permute-start(bf16[48,1024]{1,0:T(8,128)(2,1)S(1)} %sum_terms.3.rest_0_), channel_id=1, source_target_pairs={{0,1},{1,0},{2,3},{3,2},{4,5},{5,4},{6,7},{7,6},{8,9},{9,8},{10,11... | collective-permute-start | bytes 294920 | tf_op jit(solution)/shard_map/ppermute | solution.py:492
  65.9 4.2 %write_cache.1 = bf16[48,2,256,128]{3,2,1,0:T(8,128)(2,1)} custom-call(s32[2]{0:T(128)S(1)} %pad_add_fusion.meta, s32[192]{0:T(256)S(1)} %copy-done.8, s32[192]{0:T(256)S(1)} %copy-done.7, s32[12]{0:T(128)S(1)} %get-tuple-element.21.plan, f32[48,128]{1,0:T(8,128)S(1)} %get-tuple-element.22.newkey.newkey1, ...), custom_call_target="tpu_custom_call" | custom-call | bytes 12582912 | tf_op jit(solution)/shard_map/write_cache/pallas_call | solution.py:640
  70.2 0.0 collective-permute-done.16.rest_3_
  70.2 2.2 %collective-permute-done.15.rest_2_ = bf16[48,1024]{1,0:T(8,128)(2,1)S(1)} collective-permute-done((bf16[48,1024]{1,0:T(8,128)(2,1)S(1)}, bf16[48,1024]{1,0:T(8,128)(2,1)S(1)}, u32[]{:S(2)}, u32[]{:S(2)}) %collective-permute-start.15) | collective-permute-done | bytes 98336 | tf_op jit(solution)/shard_map/ppermute | solution.py:492
  72.4 0.0 collective-permute-done.14.rest_1_
  72.4 1.3 %join.1 = bf16[48,4096]{1,0:T(8,128)(2,1)} custom-call(s32[2]{0:T(128)S(1)} %pad_add_fusion.meta, bf16[48,1024]{1,0:T(8,128)(2,1)S(1)} %sum_terms.3.rest_0_, bf16[48,1024]{1,0:T(8,128)(2,1)S(1)} %collective-permute-done.14.rest_1_, bf16[48,1024]{1,0:T(8,128)(2,1)S(1)} %collective-permute-done.15.rest_2_, bf16[48,1024]{1,0:T(8,128)(2,1)S(1)} %collective-permute-done.16.rest_3_), custom_call_target="tpu_custom_call" | custom-call | tf_op jit(solution)/shard_map/join/pallas_call | solution.py:655
  (2 shorter events, 0.0 us)
Async XLA Ops:
  0.7 10.7 %slice-start = ((s8[6291456]{0:T(1024)(128)(4,1)}), s8[4194304]{0:T(1024)(128)(4,1)S(1)}, s32[]{:S(2)}) async-start(s8[6291456]{0:T(1024)(128)(4,1)} %bitcast.6), calls=%async_computation | async-start | bytes 8388608
  0.7 10.7 %slice-start.1 = ((s8[6291456]{0:T(1024)(128)(4,1)}), s8[2097152]{0:T(1024)(128)(4,1)S(1)}, s32[]{:S(2)}) async-start(s8[6291456]{0:T(1024)(128)(4,1)} %bitcast.6), calls=%async_computation.1 | async-start | bytes 4194304
  0.7 10.7 %copy-start.7 = (s32[192]{0:T(256)S(1)}, s32[192]{0:T(256)}, u32[]{:S(2)}) copy-start(s32[192]{0:T(256)} %lengths_s.7) | copy-start | bytes 2308
  8.2 7.8 %copy-start.1 = (bf16[512,4096]{1,0:T(8,128)(2,1)S(1)}, bf16[512,4096]{1,0:T(8,128)(2,1)}, u32[]{:S(2)}) copy-start(bf16[512,4096]{1,0:T(8,128)(2,1)} %wo.3) | copy-start | bytes 12582916
  8.2 7.8 %copy-start.3 = (bf16[48,4096]{1,0:T(8,128)(2,1)S(1)}, bf16[48,4096]{1,0:T(8,128)(2,1)}, u32[]{:S(2)}) copy-start(bf16[48,4096]{1,0:T(8,128)(2,1)} %hidden.1) | copy-start | bytes 1179652
  8.3 7.8 %collective-permute-start = (bf16[2,2,272,128]{3,2,1,0:T(8,128)(2,1)S(1)}, bf16[2,2,272,128]{3,2,1,0:T(8,128)(2,1)S(1)}, u32[]{:S(2)}, u32[]{:S(2)}) collective-permute-start(bf16[2,2,272,128]{3,2,1,0:T(8,128)(2,1)S(1)} %get-tuple-element.25), channel_id=1, source_target_pairs={{0,4},{4,0},{8,12},{12,8},{1,5},{5,1},{9,13},{13,9},{2,6},{6,2},{1... | collective-permute-start | bytes 835592 | tf_op jit(solution)/shard_map/ppermute | solution.py:492
  8.8 7.2 %collective-permute-start.1 = (f32[2,1536]{1,0:T(2,128)S(1)}, f32[2,1536]{1,0:T(2,128)S(1)}, u32[]{:S(2)}, u32[]{:S(2)}) collective-permute-start(f32[2,1536]{1,0:T(2,128)S(1)} %get-tuple-element.26), channel_id=1, source_target_pairs={{0,8},{4,12},{8,0},{12,4},{1,9},{5,13},{9,1},{13,5},{2,10},{6,14},... | collective-permute-start | bytes 36872 | tf_op jit(solution)/shard_map/ppermute | solution.py:492
  11.4 4.7 %collective-permute-start.2 = (f32[2,1536]{1,0:T(2,128)S(1)}, f32[2,1536]{1,0:T(2,128)S(1)}, u32[]{:S(2)}, u32[]{:S(2)}) collective-permute-start(f32[2,1536]{1,0:T(2,128)S(1)} %get-tuple-element.27), channel_id=1, source_target_pairs={{0,12},{4,8},{8,4},{12,0},{1,13},{5,9},{9,5},{13,1},{2,14},{6,10},... | collective-permute-start | bytes 36872 | tf_op jit(solution)/shard_map/ppermute | solution.py:492
  16.1 27.9 %copy-start = (bf16[4096,512]{1,0:T(8,128)(2,1)S(1)}, bf16[4096,512]{1,0:T(8,128)(2,1)}, u32[]{:S(2)}) copy-start(bf16[4096,512]{1,0:T(8,128)(2,1)} %wq.1) | copy-start | bytes 12582916
  16.1 27.9 %copy-start.2 = (bf16[4096,2,128]{2,1,0:T(2,128)(2,1)S(1)}, bf16[4096,2,128]{2,1,0:T(2,128)(2,1)}, u32[]{:S(2)}) copy-start(bf16[4096,2,128]{2,1,0:T(2,128)(2,1)} %param.16) | copy-start | bytes 6291460
  16.1 27.9 %copy-start.4 = (f32[256,128]{1,0:T(8,128)S(1)}, f32[256,128]{1,0:T(8,128)}, u32[]{:S(2)}) copy-start(f32[256,128]{1,0:T(8,128)} %constant.12.clone.sin_hbm.sin_ref) | copy-start | bytes 393220
  16.1 27.9 %copy-start.5 = (f32[256,128]{1,0:T(8,128)S(1)}, f32[256,128]{1,0:T(8,128)}, u32[]{:S(2)}) copy-start(f32[256,128]{1,0:T(8,128)} %constant.11.clone.cos_hbm.cos_ref) | copy-start | bytes 393220
  16.1 27.9 %copy-start.6 = (f32[4096]{0:T(1024)S(1)}, f32[4096]{0:T(1024)}, u32[]{:S(2)}) copy-start(f32[4096]{0:T(1024)} %param.14) | copy-start | bytes 49156
  16.1 27.9 %copy-start.8 = (s32[192]{0:T(256)S(1)}, s32[192]{0:T(256)}, u32[]{:S(2)}) copy-start(s32[192]{0:T(256)} %source_s.3) | copy-start | bytes 2308
  18.5 25.5 %collective-permute-start.9 = (bf16[2,2,256,128]{3,2,1,0:T(8,128)(2,1)S(1)}, bf16[2,2,256,128]{3,2,1,0:T(8,128)(2,1)S(1)}, u32[]{:S(2)}, u32[]{:S(2)}) collective-permute-start(bf16[2,2,256,128]{3,2,1,0:T(8,128)(2,1)S(1)} %get-tuple-element.32), channel_id=1, source_target_pairs={{0,8},{4,12},{8,0},{12,4},{1,9},{5,13},{9,1},{13,5},{2,10},{6,14},... | collective-permute-start | bytes 786440 | tf_op jit(solution)/shard_map/ppermute | solution.py:492
  20.3 23.7 %collective-permute-start.10 = (bf16[2,2,256,128]{3,2,1,0:T(8,128)(2,1)S(1)}, bf16[2,2,256,128]{3,2,1,0:T(8,128)(2,1)S(1)}, u32[]{:S(2)}, u32[]{:S(2)}) collective-permute-start(bf16[2,2,256,128]{3,2,1,0:T(8,128)(2,1)S(1)} %get-tuple-element.33), channel_id=1, source_target_pairs={{0,12},{4,8},{8,4},{12,0},{1,13},{5,9},{9,5},{13,1},{2,14},{6,10},... | collective-permute-start | bytes 786440 | tf_op jit(solution)/shard_map/ppermute | solution.py:492
  20.3 7.6 %collective-permute-start.3 = (bf16[48,1024]{1,0:T(8,128)(2,1)S(1)}, bf16[48,1024]{1,0:T(8,128)(2,1)S(1)}, u32[]{:S(2)}, u32[]{:S(2)}) collective-permute-start(bf16[48,1024]{1,0:T(8,128)(2,1)S(1)} %get-tuple-element.29), channel_id=1, source_target_pairs={{0,3},{1,2},{2,1},{3,0},{4,7},{5,6},{6,5},{7,4},{8,11},{9,10},{10,... | collective-permute-start | bytes 294920 | tf_op jit(solution)/shard_map/ppermute | solution.py:492
  24.1 8.9 %collective-permute-start.4 = (bf16[48,1024]{1,0:T(8,128)(2,1)S(1)}, bf16[48,1024]{1,0:T(8,128)(2,1)S(1)}, u32[]{:S(2)}, u32[]{:S(2)}) collective-permute-start(bf16[48,1024]{1,0:T(8,128)(2,1)S(1)} %get-tuple-element.30), channel_id=1, source_target_pairs={{0,2},{1,3},{2,0},{3,1},{4,6},{5,7},{6,4},{7,5},{8,10},{9,11},{10,... | collective-permute-start | bytes 294920 | tf_op jit(solution)/shard_map/ppermute | solution.py:492
  24.1 8.9 %collective-permute-start.5 = (bf16[48,1024]{1,0:T(8,128)(2,1)S(1)}, bf16[48,1024]{1,0:T(8,128)(2,1)S(1)}, u32[]{:S(2)}, u32[]{:S(2)}) collective-permute-start(bf16[48,1024]{1,0:T(8,128)(2,1)S(1)} %get-tuple-element.31), channel_id=1, source_target_pairs={{0,1},{1,0},{2,3},{3,2},{4,5},{5,4},{6,7},{7,6},{8,9},{9,8},{10,11... | collective-permute-start | bytes 294920 | tf_op jit(solution)/shard_map/ppermute | solution.py:492
  33.0 7.6 %collective-permute-start.8 = (bf16[48,1024]{1,0:T(8,128)(2,1)S(1)}, bf16[48,1024]{1,0:T(8,128)(2,1)S(1)}, u32[]{:S(2)}, u32[]{:S(2)}) collective-permute-start(bf16[48,1024]{1,0:T(8,128)(2,1)S(1)} %sum_terms.2.rest_0_), channel_id=1, source_target_pairs={{0,3},{1,2},{2,1},{3,0},{4,7},{5,6},{6,5},{7,4},{8,11},{9,10},{10,... | collective-permute-start | bytes 294920 | tf_op jit(solution)/shard_map/ppermute | solution.py:492
  35.5 8.4 %collective-permute-start.7 = (bf16[48,1024]{1,0:T(8,128)(2,1)S(1)}, bf16[48,1024]{1,0:T(8,128)(2,1)S(1)}, u32[]{:S(2)}, u32[]{:S(2)}) collective-permute-start(bf16[48,1024]{1,0:T(8,128)(2,1)S(1)} %sum_terms.2.rest_0_), channel_id=1, source_target_pairs={{0,2},{1,3},{2,0},{3,1},{4,6},{5,7},{6,4},{7,5},{8,10},{9,11},{10,... | collective-permute-start | bytes 294920 | tf_op jit(solution)/shard_map/ppermute | solution.py:492
  35.5 8.4 %collective-permute-start.6 = (bf16[48,1024]{1,0:T(8,128)(2,1)S(1)}, bf16[48,1024]{1,0:T(8,128)(2,1)S(1)}, u32[]{:S(2)}, u32[]{:S(2)}) collective-permute-start(bf16[48,1024]{1,0:T(8,128)(2,1)S(1)} %sum_terms.2.rest_0_), channel_id=1, source_target_pairs={{0,1},{1,0},{2,3},{3,2},{4,5},{5,4},{6,7},{7,6},{8,9},{9,8},{10,11... | collective-permute-start | bytes 294920 | tf_op jit(solution)/shard_map/ppermute | solution.py:492
  50.9 7.6 %collective-permute-start.11 = (bf16[48,1024]{1,0:T(8,128)(2,1)S(1)}, bf16[48,1024]{1,0:T(8,128)(2,1)S(1)}, u32[]{:S(2)}, u32[]{:S(2)}) collective-permute-start(bf16[48,1024]{1,0:T(8,128)(2,1)S(1)} %get-tuple-element.35), channel_id=1, source_target_pairs={{0,3},{1,2},{2,1},{3,0},{4,7},{5,6},{6,5},{7,4},{8,11},{9,10},{10,... | collective-permute-start | bytes 294920 | tf_op jit(solution)/shard_map/ppermute | solution.py:492
  52.9 8.5 %collective-permute-start.12 = (bf16[48,1024]{1,0:T(8,128)(2,1)S(1)}, bf16[48,1024]{1,0:T(8,128)(2,1)S(1)}, u32[]{:S(2)}, u32[]{:S(2)}) collective-permute-start(bf16[48,1024]{1,0:T(8,128)(2,1)S(1)} %get-tuple-element.36), channel_id=1, source_target_pairs={{0,2},{1,3},{2,0},{3,1},{4,6},{5,7},{6,4},{7,5},{8,10},{9,11},{10,... | collective-permute-start | bytes 294920 | tf_op jit(solution)/shard_map/ppermute | solution.py:492
  52.9 8.5 %collective-permute-start.13 = (bf16[48,1024]{1,0:T(8,128)(2,1)S(1)}, bf16[48,1024]{1,0:T(8,128)(2,1)S(1)}, u32[]{:S(2)}, u32[]{:S(2)}) collective-permute-start(bf16[48,1024]{1,0:T(8,128)(2,1)S(1)} %get-tuple-element.37), channel_id=1, source_target_pairs={{0,1},{1,0},{2,3},{3,2},{4,5},{5,4},{6,7},{7,6},{8,9},{9,8},{10,11... | collective-permute-start | bytes 294920 | tf_op jit(solution)/shard_map/ppermute | solution.py:492
  61.5 8.7 %collective-permute-start.16 = (bf16[48,1024]{1,0:T(8,128)(2,1)S(1)}, bf16[48,1024]{1,0:T(8,128)(2,1)S(1)}, u32[]{:S(2)}, u32[]{:S(2)}) collective-permute-start(bf16[48,1024]{1,0:T(8,128)(2,1)S(1)} %sum_terms.3.rest_0_), channel_id=1, source_target_pairs={{0,3},{1,2},{2,1},{3,0},{4,7},{5,6},{6,5},{7,4},{8,11},{9,10},{10,... | collective-permute-start | bytes 294920 | tf_op jit(solution)/shard_map/ppermute | solution.py:492
  63.7 8.6 %collective-permute-start.15 = (bf16[48,1024]{1,0:T(8,128)(2,1)S(1)}, bf16[48,1024]{1,0:T(8,128)(2,1)S(1)}, u32[]{:S(2)}, u32[]{:S(2)}) collective-permute-start(bf16[48,1024]{1,0:T(8,128)(2,1)S(1)} %sum_terms.3.rest_0_), channel_id=1, source_target_pairs={{0,2},{1,3},{2,0},{3,1},{4,6},{5,7},{6,4},{7,5},{8,10},{9,11},{10,... | collective-permute-start | bytes 294920 | tf_op jit(solution)/shard_map/ppermute | solution.py:492
  63.7 8.6 %collective-permute-start.14 = (bf16[48,1024]{1,0:T(8,128)(2,1)S(1)}, bf16[48,1024]{1,0:T(8,128)(2,1)S(1)}, u32[]{:S(2)}, u32[]{:S(2)}) collective-permute-start(bf16[48,1024]{1,0:T(8,128)(2,1)S(1)} %sum_terms.3.rest_0_), channel_id=1, source_target_pairs={{0,1},{1,0},{2,3},{3,2},{4,5},{5,4},{6,7},{7,6},{8,9},{9,8},{10,11... | collective-permute-start | bytes 294920 | tf_op jit(solution)/shard_map/ppermute | solution.py:492

commit v5 on v4

--- a/solution.py
+++ b/solution.py
@@ -297,13 +297,30 @@
             sends[k - 1][...] = part.astype(BF16)
 
 
+def is_odd(meta):
+    return lax.rem(meta[0], 2) == 1
+
+
 def out_kernel(
     peers, peers_tp, slots, meta, lengths_s, plan, attended, wo, hidden, newkey, newvalue, box_hbm,
     cache_hbm, *rest,
 ):
     notes, rest = rest[: peers - 2], rest[peers - 2 :]
     own, sends, boxes = rest[0], rest[1:peers_tp], rest[peers_tp : peers_tp + peers - 2]
-    leaving, tail, sem, in_sem, out_sem = rest[peers_tp + peers - 2 :]
+    final_hbm, leaving, tail, sem, in_sem, out_sem, early_sem = rest[peers_tp + peers - 2 :]
+    early = [
+        pltpu.make_async_copy(
+            cache_hbm.at[pl.ds(c * CHUNK, CHUNK)], final_hbm.at[pl.ds(c * CHUNK, CHUNK)],
+            early_sem.at[c],
+        )
+        for c in range(slots // CHUNK)
+    ]
+
+    @pl.when(is_odd(meta))
+    def _():
+        for copy in early:
+            copy.start()
+
     moving = (peers - 1) * MOVE
     send_slots = [plan[moving + at] for at in range(MOVE, moving)]
     packs = [
@@ -346,6 +363,12 @@
     ]
     for out in outs:
         out.start()
+
+    @pl.when(is_odd(meta))
+    def _():
+        for copy in early:
+            copy.wait()
+
     project_out(rows.astype(BF16), wo, residual, own, sends, meta[1], peers_tp)
     for out in outs:
         out.wait()
@@ -451,8 +474,10 @@
     cache_hbm, *rest,
 ):
     box_hbm, rest = rest[: peers - 1], rest[peers - 1 :]
-    out_hbm, buffer, place, in_sem, out_sem = rest
+    _, out_hbm, buffer, place, in_sem, out_sem = rest
     low = meta[0] * slots
+    cap = cache_hbm.shape[2]
+    odd = is_odd(meta)
     cache_copies = load_slots(slots, peers, cache_hbm, box_hbm, buffer, in_sem)
     for copy in cache_copies:
         copy.start()
@@ -466,14 +491,23 @@
         for s in range(c * CHUNK, (c + 1) * CHUNK):
             at = place[s]
             length = lengths_s[source_s[low + s]]
-            first = jnp.where(at < slots, length, -1)
+            kept = at < slots
+            first = jnp.where(kept, length, -1)
             put_row(buffer, at, first, newkey1[s : s + 1, :], newvalue1[s : s + 1, :])
             put_row(buffer, at, length + 1, newkey2[s : s + 1, :], newvalue2[s : s + 1, :])
-            copy = pltpu.make_async_copy(buffer.at[at], out_hbm.at[s], out_sem.at[s])
-            copy.start()
-            outs.append(copy)
-    for copy in outs:
-        copy.wait()
+            base = pl.multiple_of(jnp.minimum((length // PIECE) * PIECE, cap - 2 * PIECE), PIECE)
+            window = (slice(None), pl.ds(base, 2 * PIECE), slice(None))
+            whole = pltpu.make_async_copy(buffer.at[at], out_hbm.at[s], out_sem.at[s])
+            part = pltpu.make_async_copy(
+                buffer.at[at].at[window], out_hbm.at[s].at[window], out_sem.at[s]
+            )
+            copied = odd & kept
+            outs.append((copied, whole, part))
+            pl.when(copied)(part.start)
+            pl.when(jnp.logical_not(copied))(whole.start)
+    for copied, whole, part in outs:
+        pl.when(copied)(part.wait)
+        pl.when(jnp.logical_not(copied))(whole.wait)
 
 
 def join_kernel(peers_tp, meta, *rest):
@@ -583,22 +617,24 @@
     own, *rest = pl.pallas_call(
         functools.partial(out_kernel, peers, peers_tp, slots),
         out_shape=sent
-        + [jax.ShapeDtypeStruct((MOVE,) + kv_cache.shape[1:], BF16)] * (others - 1),
+        + [jax.ShapeDtypeStruct((MOVE,) + kv_cache.shape[1:], BF16)] * (others - 1)
+        + [pltpu.HBM(kv_cache.shape, BF16)],
         in_specs=[SMEM] * 3 + [VMEM] * 5 + [ANY] * 2 + [VMEM] * (others - 1),
-        out_specs=[VMEM] * peers_tp + [ANY] * (others - 1),
+        out_specs=[VMEM] * peers_tp + [ANY] * (others - 1) + [HBM],
         scratch_shapes=[
             pltpu.VMEM((moving - MOVE,) + kv_cache.shape[1:], BF16),
             pltpu.VMEM((MOVE, NOTE, HD), BF16),
             dma((1,)),
             dma((moving - MOVE,)),
             dma((others - 1,)),
+            dma((slots // CHUNK,)),
         ],
         compiler_params=params(20),
         cost_estimate=cost(2 * slots * width * heads * HD, out_weight.size * 2),
         name="out_projection",
     )(meta, lengths, plan, attended, out_weight, hidden, newkey1, newvalue1, got_notes[0], kv_cache,
       *got_notes[1:])
-    sends, boxes = rest[: peers_tp - 1], rest[peers_tp - 1 :]
+    sends, boxes, final_cache = rest[: peers_tp - 1], rest[peers_tp - 1 : -1], rest[-1]
     got_boxes = got_notes[:1] + [swapped(box, "inst", peers, k + 2) for k, box in enumerate(boxes)]
 
     def summed(own, sends):
@@ -640,8 +676,9 @@
     final_cache = pl.pallas_call(
         functools.partial(cache_kernel, peers, slots),
         out_shape=jax.ShapeDtypeStruct(kv_cache.shape, BF16),
-        in_specs=[SMEM] * 4 + [VMEM] * 4 + [ANY] * peers,
-        out_specs=ANY,
+        in_specs=[SMEM] * 4 + [VMEM] * 4 + [ANY] * peers + [HBM],
+        out_specs=HBM,
+        input_output_aliases={8 + peers: 0},
         scratch_shapes=[
             pltpu.VMEM((slots + moving,) + kv_cache.shape[1:], BF16),
             pltpu.SMEM((slots,), I32),
@@ -651,7 +688,8 @@
         compiler_params=params(24),
         cost_estimate=cost(0, 2 * cache_bytes),
         name="write_cache",
-    )(meta, source, lengths, plan, newkey1, newvalue1, newkey2, newvalue2, kv_cache, *got_boxes)
+    )(meta, source, lengths, plan, newkey1, newvalue1, newkey2, newvalue2, kv_cache, *got_boxes,
+      final_cache)
     final_hidden = pl.pallas_call(
         functools.partial(join_kernel, peers_tp),
         out_shape=jax.ShapeDtypeStruct(hidden.shape, BF16),

time: 73.9 us -> 74.2 us (level)
  starting transfers between devices: 22.8 us -> 25 us
  waiting for transfers between devices: 23 us -> 21.2 us
    ppermute x17, starting transfers between devices: 22.8 us -> 25 us  [swapped(): return lax.ppermute(x, axis, [(i, i ^ k) for i in range(size)])]
    ppermute x17, waiting for transfers between devices: 23 us -> 21.2 us  [swapped(): return lax.ppermute(x, axis, [(i, i ^ k) for i in range(size)])]
where the time goes in v5:
time: 74.2 us; the launch traced here: 74.1 us
  Pallas kernels  26.9 us (36%)
  starting transfers between devices  25 us (34%)
  waiting for transfers between devices  21.2 us (29%)
  between operations  0.87 us (1%)
    ppermute x17, starting transfers between devices, swapped(): return lax.ppermute(x, axis, [(i, i ^ k) for i in range(size)])  25 us
    ppermute x17, waiting for transfers between devices, swapped(): return lax.ppermute(x, axis, [(i, i ^ k) for i in range(size)])  21.2 us
    pallas_call x1, Pallas kernels, local(): pl.pallas_call(functools.partial(first_kernel, peers, slots, heads, shard...  7.47 us
    pallas_call x1, Pallas kernels, local(): pl.pallas_call(functools.partial(second_kernel, peers, peers_tp, slots, h...  6.83 us
    pallas_call x1, Pallas kernels, local(): pl.pallas_call(functools.partial(attend_kernel, slots, heads), out_shape=...  4.56 us
    pallas_call x1, Pallas kernels, local(): pl.pallas_call(functools.partial(cache_kernel, peers, slots), out_shape=j...  4.25 us
    pallas_call x1, Pallas kernels, local(): pl.pallas_call(functools.partial(out_kernel, peers, peers_tp, slots), out...  2.42 us
  transfers between devices with their start and end apart: 17, of which 7 were waited for; matrix products, arithmetic and copies ran while one was open for 0% of the time, Pallas kernels for 12%

profile of v5, /device:TPU:0, one launch (start us, length us, event | category | flops | bytes accessed | tf_op | source)
XLA Modules:
  0.0 74.1 jit_solution(7760228275315464765)
XLA Ops:
  0.6 0.1 pad_add_fusion.meta
  0.7 0.0 copy-start
  0.7 0.0 copy-start.8
  0.7 7.5 %first_step.1 = (f32[384,128]{1,0:T(8,128)S(1)}, f32[48,128]{1,0:T(8,128)S(1)}, f32[48,128]{1,0:T(8,128)S(1)}, s32[12]{0:T(128)S(1)}, bf16[2,2,272,128]{3,2,1,0:...) custom-call(s32[2]{0:T(128)S(1)} %pad_add_fusion.meta, s32[1,192]{1,0:T(1,128)} %bitcast.11, ...), custom_call_target="tpu_custom_call" | custom-call | flops 301989888 | bytes 6291456 | tf_op jit(solution)/shard_map/first_step/pallas_call | solution.py:559
  8.2 0.0 copy-start.2
  8.2 0.0 copy-start.4
  8.2 0.5 collective-permute-start
  8.7 2.6 %collective-permute-start.1 = (f32[2,1536]{1,0:T(2,128)S(1)}, f32[2,1536]{1,0:T(2,128)S(1)}, u32[]{:S(2)}, u32[]{:S(2)}) collective-permute-start(f32[2,1536]{1,0:T(2,128)S(1)} %get-tuple-element.27), channel_id=1, source_target_pairs={{0,8},{4,12},{8,0},{12,4},{1,9},{5,13},{9,1},{13,5},{2,10},{6,14},... | collective-permute-start | bytes 36872 | tf_op jit(solution)/shard_map/ppermute | solution.py:526
  11.3 0.1 collective-permute-start.2
  11.4 0.0 copy-done
  11.4 0.0 copy-done.8
  11.4 4.6 %attention.1.attended = bf16[48,512]{1,0:T(8,128)(2,1)S(1)} custom-call(s32[2]{0:T(128)S(1)} %pad_add_fusion.meta, s32[192]{0:T(256)S(1)} %copy-done.8, f32[384,128]{1,0:T(8,128)S(1)} %get-tuple-element.25.query, f32[48,128]{1,0:T(8,128)S(1)} %get-tuple-element.23.newkey.newkey1, f32[48,128]{1,0:T(8,128)S(1)} %get-tuple-element.24.newvalue.newvalue1, ...), custom_call_target="tpu_custom_call" | custom-call | flops 25165824 | bytes 6291456 | tf_op jit(solution)/shard_map/attention/pallas_call | solution.py:600
  16.0 0.0 copy-start.1
  16.0 0.0 copy-start.3
  16.0 0.0 copy-start.5
  16.0 0.0 copy-start.6
  16.0 0.0 copy-start.7
  16.0 0.0 copy-start.9
  16.0 0.0 collective-permute-done.1.rest_0_
  16.0 0.0 collective-permute-done.2.rest_1_
  16.1 0.0 collective-permute-done.box_hbm.rest_4_.rest_0_
  16.1 0.0 copy-done.2
  16.1 0.0 copy-done.4
  16.1 2.4 %out_projection.1 = (f32[48,1024]{1,0:T(8,128)S(1)}, bf16[48,1024]{1,0:T(8,128)(2,1)S(1)}, bf16[48,1024]{1,0:T(8,128)(2,1)S(1)}, bf16[48,1024]{1,0:T(8,128)(2,1)...) custom-call(s32[2]{0:T(128)S(1)} %pad_add_fusion.meta, ...), custom_call_target="tpu_custom_call" | custom-call | flops 201326592 | bytes 4194304 | tf_op jit(solution)/shard_map/out_projection/pallas_call | solution.py:617
  18.5 1.8 %collective-permute-start.9 = (bf16[2,2,256,128]{3,2,1,0:T(8,128)(2,1)S(1)}, bf16[2,2,256,128]{3,2,1,0:T(8,128)(2,1)S(1)}, u32[]{:S(2)}, u32[]{:S(2)}) collective-permute-start(bf16[2,2,256,128]{3,2,1,0:T(8,128)(2,1)S(1)} %get-tuple-element.33), channel_id=1, source_target_pairs={{0,8},{4,12},{8,0},{12,4},{1,9},{5,13},{9,1},{13,5},{2,10},{6,14},... | collective-permute-start | bytes 786440 | tf_op jit(solution)/shard_map/ppermute | solution.py:526
  20.3 2.3 %collective-permute-start.10 = (bf16[2,2,256,128]{3,2,1,0:T(8,128)(2,1)S(1)}, bf16[2,2,256,128]{3,2,1,0:T(8,128)(2,1)S(1)}, u32[]{:S(2)}, u32[]{:S(2)}) collective-permute-start(bf16[2,2,256,128]{3,2,1,0:T(8,128)(2,1)S(1)} %get-tuple-element.34), channel_id=1, source_target_pairs={{0,12},{4,8},{8,4},{12,0},{1,13},{5,9},{9,5},{13,1},{2,14},{6,10},... | collective-permute-start | bytes 786440 | tf_op jit(solution)/shard_map/ppermute | solution.py:526
  22.6 3.8 %collective-permute-start.3 = (bf16[48,1024]{1,0:T(8,128)(2,1)S(1)}, bf16[48,1024]{1,0:T(8,128)(2,1)S(1)}, u32[]{:S(2)}, u32[]{:S(2)}) collective-permute-start(bf16[48,1024]{1,0:T(8,128)(2,1)S(1)} %get-tuple-element.30), channel_id=1, source_target_pairs={{0,3},{1,2},{2,1},{3,0},{4,7},{5,6},{6,5},{7,4},{8,11},{9,10},{10,... | collective-permute-start | bytes 294920 | tf_op jit(solution)/shard_map/ppermute | solution.py:526
  26.3 0.0 collective-permute-start.4
  26.3 0.6 collective-permute-start.5
  27.0 3.1 %collective-permute-done.3.rest_0_ = bf16[48,1024]{1,0:T(8,128)(2,1)S(1)} collective-permute-done((bf16[48,1024]{1,0:T(8,128)(2,1)S(1)}, bf16[48,1024]{1,0:T(8,128)(2,1)S(1)}, u32[]{:S(2)}, u32[]{:S(2)}) %collective-permute-start.3) | collective-permute-done | bytes 98336 | tf_op jit(solution)/shard_map/ppermute | solution.py:526
  30.1 4.6 %collective-permute-done.4.rest_1_ = bf16[48,1024]{1,0:T(8,128)(2,1)S(1)} collective-permute-done((bf16[48,1024]{1,0:T(8,128)(2,1)S(1)}, bf16[48,1024]{1,0:T(8,128)(2,1)S(1)}, u32[]{:S(2)}, u32[]{:S(2)}) %collective-permute-start.4) | collective-permute-done | bytes 98336 | tf_op jit(solution)/shard_map/ppermute | solution.py:526
  34.7 0.0 collective-permute-done.5.rest_2_
  34.7 0.1 sum_terms.2.rest_0_
  34.7 0.6 collective-permute-start.6
  35.3 2.5 %collective-permute-start.7 = (bf16[48,1024]{1,0:T(8,128)(2,1)S(1)}, bf16[48,1024]{1,0:T(8,128)(2,1)S(1)}, u32[]{:S(2)}, u32[]{:S(2)}) collective-permute-start(bf16[48,1024]{1,0:T(8,128)(2,1)S(1)} %sum_terms.2.rest_0_), channel_id=1, source_target_pairs={{0,2},{1,3},{2,0},{3,1},{4,6},{5,7},{6,4},{7,5},{8,10},{9,11},{10,... | collective-permute-start | bytes 294920 | tf_op jit(solution)/shard_map/ppermute | solution.py:526
  37.8 1.3 %collective-permute-start.8 = (bf16[48,1024]{1,0:T(8,128)(2,1)S(1)}, bf16[48,1024]{1,0:T(8,128)(2,1)S(1)}, u32[]{:S(2)}, u32[]{:S(2)}) collective-permute-start(bf16[48,1024]{1,0:T(8,128)(2,1)S(1)} %sum_terms.2.rest_0_), channel_id=1, source_target_pairs={{0,3},{1,2},{2,1},{3,0},{4,7},{5,6},{6,5},{7,4},{8,11},{9,10},{10,... | collective-permute-start | bytes 294920 | tf_op jit(solution)/shard_map/ppermute | solution.py:526
  39.2 0.5 collective-permute-done.6.rest_1_
  39.7 5.3 %collective-permute-done.7.rest_2_ = bf16[48,1024]{1,0:T(8,128)(2,1)S(1)} collective-permute-done((bf16[48,1024]{1,0:T(8,128)(2,1)S(1)}, bf16[48,1024]{1,0:T(8,128)(2,1)S(1)}, u32[]{:S(2)}, u32[]{:S(2)}) %collective-permute-start.7) | collective-permute-done | bytes 98336 | tf_op jit(solution)/shard_map/ppermute | solution.py:526
  45.0 0.0 collective-permute-done.8.rest_3_
  45.0 0.0 collective-permute-done.9.rest_5_.rest_1_
  45.0 0.0 collective-permute-done.10.rest_6_.rest_2_
  45.0 0.0 copy-done.1
  45.0 0.0 copy-done.3
  45.0 0.0 copy-done.5
  45.0 0.0 copy-done.6
  45.0 0.0 copy-done.7
  45.0 0.0 copy-done.9
  45.0 6.8 %second_step.1 = (f32[48,128]{1,0:T(8,128)S(1)}, f32[48,128]{1,0:T(8,128)S(1)}, f32[48,1024]{1,0:T(8,128)S(1)}, bf16[48,1024]{1,0:T(8,128)(2,1)S(1)}, bf16[48,10...) custom-call(s32[2]{0:T(128)S(1)} %pad_add_fusion.meta, s32[192]{0:T(256)S(1)} %copy-done.9, s32[192]{0:T(256)S(1)} %copy-done.8, ...), custom_call_target="tpu_custom_call" | custom-call | flops 905969664 | bytes 18874368 | tf_op jit(solution)/shard_map/second_step/pallas_call | solution.py:656
  51.9 2.1 %collective-permute-start.11 = (bf16[48,1024]{1,0:T(8,128)(2,1)S(1)}, bf16[48,1024]{1,0:T(8,128)(2,1)S(1)}, u32[]{:S(2)}, u32[]{:S(2)}) collective-permute-start(bf16[48,1024]{1,0:T(8,128)(2,1)S(1)} %get-tuple-element.36), channel_id=1, source_target_pairs={{0,3},{1,2},{2,1},{3,0},{4,7},{5,6},{6,5},{7,4},{8,11},{9,10},{10,... | collective-permute-start | bytes 294920 | tf_op jit(solution)/shard_map/ppermute | solution.py:526
  53.9 1.1 %collective-permute-start.12 = (bf16[48,1024]{1,0:T(8,128)(2,1)S(1)}, bf16[48,1024]{1,0:T(8,128)(2,1)S(1)}, u32[]{:S(2)}, u32[]{:S(2)}) collective-permute-start(bf16[48,1024]{1,0:T(8,128)(2,1)S(1)} %get-tuple-element.37), channel_id=1, source_target_pairs={{0,2},{1,3},{2,0},{3,1},{4,6},{5,7},{6,4},{7,5},{8,10},{9,11},{10,... | collective-permute-start | bytes 294920 | tf_op jit(solution)/shard_map/ppermute | solution.py:526
  55.0 1.3 %collective-permute-start.13 = (bf16[48,1024]{1,0:T(8,128)(2,1)S(1)}, bf16[48,1024]{1,0:T(8,128)(2,1)S(1)}, u32[]{:S(2)}, u32[]{:S(2)}) collective-permute-start(bf16[48,1024]{1,0:T(8,128)(2,1)S(1)} %get-tuple-element.38), channel_id=1, source_target_pairs={{0,1},{1,0},{2,3},{3,2},{4,5},{5,4},{6,7},{7,6},{8,9},{9,8},{10,11... | collective-permute-start | bytes 294920 | tf_op jit(solution)/shard_map/ppermute | solution.py:526
  56.3 2.3 %collective-permute-done.11.rest_0_ = bf16[48,1024]{1,0:T(8,128)(2,1)S(1)} collective-permute-done((bf16[48,1024]{1,0:T(8,128)(2,1)S(1)}, bf16[48,1024]{1,0:T(8,128)(2,1)S(1)}, u32[]{:S(2)}, u32[]{:S(2)}) %collective-permute-start.11) | collective-permute-done | bytes 98336 | tf_op jit(solution)/shard_map/ppermute | solution.py:526
  58.7 3.6 %collective-permute-done.12.rest_1_ = bf16[48,1024]{1,0:T(8,128)(2,1)S(1)} collective-permute-done((bf16[48,1024]{1,0:T(8,128)(2,1)S(1)}, bf16[48,1024]{1,0:T(8,128)(2,1)S(1)}, u32[]{:S(2)}, u32[]{:S(2)}) %collective-permute-start.12) | collective-permute-done | bytes 98336 | tf_op jit(solution)/shard_map/ppermute | solution.py:526
  62.3 0.0 collective-permute-done.13.rest_2_
  62.3 0.1 collective-permute-start.14
  62.4 2.3 %collective-permute-start.15 = (bf16[48,1024]{1,0:T(8,128)(2,1)S(1)}, bf16[48,1024]{1,0:T(8,128)(2,1)S(1)}, u32[]{:S(2)}, u32[]{:S(2)}) collective-permute-start(bf16[48,1024]{1,0:T(8,128)(2,1)S(1)} %sum_terms.3.rest_0_), channel_id=1, source_target_pairs={{0,2},{1,3},{2,0},{3,1},{4,6},{5,7},{6,4},{7,5},{8,10},{9,11},{10,... | collective-permute-start | bytes 294920 | tf_op jit(solution)/shard_map/ppermute | solution.py:526
  64.7 2.1 %collective-permute-start.16 = (bf16[48,1024]{1,0:T(8,128)(2,1)S(1)}, bf16[48,1024]{1,0:T(8,128)(2,1)S(1)}, u32[]{:S(2)}, u32[]{:S(2)}) collective-permute-start(bf16[48,1024]{1,0:T(8,128)(2,1)S(1)} %sum_terms.3.rest_0_), channel_id=1, source_target_pairs={{0,3},{1,2},{2,1},{3,0},{4,7},{5,6},{6,5},{7,4},{8,11},{9,10},{10,... | collective-permute-start | bytes 294920 | tf_op jit(solution)/shard_map/ppermute | solution.py:526
  66.8 4.2 %write_cache.1 = bf16[48,2,256,128]{3,2,1,0:T(8,128)(2,1)} custom-call(s32[2]{0:T(128)S(1)} %pad_add_fusion.meta, s32[192]{0:T(256)S(1)} %copy-done.9, s32[192]{0:T(256)S(1)} %copy-done.8, s32[12]{0:T(128)S(1)} %get-tuple-element.22.plan, f32[48,128]{1,0:T(8,128)S(1)} %get-tuple-element.23.newkey.newkey1, ...), custom_call_target="tpu_custom_call", output_to_operand_aliasing={{}: (12, {})} | custom-call | bytes 12582912 | tf_op jit(solution)/shard_map/write_cache/pallas_call | solution.py:676
  71.0 0.0 collective-permute-done.14.rest_1_
  71.0 1.7 %collective-permute-done.15.rest_2_ = bf16[48,1024]{1,0:T(8,128)(2,1)S(1)} collective-permute-done((bf16[48,1024]{1,0:T(8,128)(2,1)S(1)}, bf16[48,1024]{1,0:T(8,128)(2,1)S(1)}, u32[]{:S(2)}, u32[]{:S(2)}) %collective-permute-start.15) | collective-permute-done | bytes 98336 | tf_op jit(solution)/shard_map/ppermute | solution.py:526
  72.8 0.0 collective-permute-done.16.rest_3_
  72.8 1.3 %join.1 = bf16[48,4096]{1,0:T(8,128)(2,1)} custom-call(s32[2]{0:T(128)S(1)} %pad_add_fusion.meta, bf16[48,1024]{1,0:T(8,128)(2,1)S(1)} %sum_terms.3.rest_0_, bf16[48,1024]{1,0:T(8,128)(2,1)S(1)} %collective-permute-done.14.rest_1_, bf16[48,1024]{1,0:T(8,128)(2,1)S(1)} %collective-permute-done.15.rest_2_, bf16[48,1024]{1,0:T(8,128)(2,1)S(1)} %collective-permute-done.16.rest_3_), custom_call_target="tpu_custom_call" | custom-call | tf_op jit(solution)/shard_map/join/pallas_call | solution.py:693
  (1 shorter events, 0.0 us)
Async XLA Ops:
  0.7 10.7 %copy-start = (bf16[48,2,256,128]{3,2,1,0:T(8,128)(2,1)S(1)}, bf16[48,2,256,128]{3,2,1,0:T(8,128)(2,1)}, u32[]{:S(2)}) copy-start(bf16[48,2,256,128]{3,2,1,0:T(8,128)(2,1)} %cache_hbm.9) | copy-start | bytes 18874372
  0.7 10.7 %copy-start.8 = (s32[192]{0:T(256)S(1)}, s32[192]{0:T(256)}, u32[]{:S(2)}) copy-start(s32[192]{0:T(256)} %lengths_s.7) | copy-start | bytes 2308
  8.2 7.9 %copy-start.2 = (bf16[512,4096]{1,0:T(8,128)(2,1)S(1)}, bf16[512,4096]{1,0:T(8,128)(2,1)}, u32[]{:S(2)}) copy-start(bf16[512,4096]{1,0:T(8,128)(2,1)} %wo.3) | copy-start | bytes 12582916
  8.2 7.9 %copy-start.4 = (bf16[48,4096]{1,0:T(8,128)(2,1)S(1)}, bf16[48,4096]{1,0:T(8,128)(2,1)}, u32[]{:S(2)}) copy-start(bf16[48,4096]{1,0:T(8,128)(2,1)} %hidden.1) | copy-start | bytes 1179652
  8.2 7.8 %collective-permute-start = (bf16[2,2,272,128]{3,2,1,0:T(8,128)(2,1)S(1)}, bf16[2,2,272,128]{3,2,1,0:T(8,128)(2,1)S(1)}, u32[]{:S(2)}, u32[]{:S(2)}) collective-permute-start(bf16[2,2,272,128]{3,2,1,0:T(8,128)(2,1)S(1)} %get-tuple-element.26), channel_id=1, source_target_pairs={{0,4},{4,0},{8,12},{12,8},{1,5},{5,1},{9,13},{13,9},{2,6},{6,2},{1... | collective-permute-start | bytes 835592 | tf_op jit(solution)/shard_map/ppermute | solution.py:526
  8.7 7.3 %collective-permute-start.1 = (f32[2,1536]{1,0:T(2,128)S(1)}, f32[2,1536]{1,0:T(2,128)S(1)}, u32[]{:S(2)}, u32[]{:S(2)}) collective-permute-start(f32[2,1536]{1,0:T(2,128)S(1)} %get-tuple-element.27), channel_id=1, source_target_pairs={{0,8},{4,12},{8,0},{12,4},{1,9},{5,13},{9,1},{13,5},{2,10},{6,14},... | collective-permute-start | bytes 36872 | tf_op jit(solution)/shard_map/ppermute | solution.py:526
  11.3 4.7 %collective-permute-start.2 = (f32[2,1536]{1,0:T(2,128)S(1)}, f32[2,1536]{1,0:T(2,128)S(1)}, u32[]{:S(2)}, u32[]{:S(2)}) collective-permute-start(f32[2,1536]{1,0:T(2,128)S(1)} %get-tuple-element.28), channel_id=1, source_target_pairs={{0,12},{4,8},{8,4},{12,0},{1,13},{5,9},{9,5},{13,1},{2,14},{6,10},... | collective-permute-start | bytes 36872 | tf_op jit(solution)/shard_map/ppermute | solution.py:526
  16.0 29.0 %copy-start.1 = (bf16[4096,512]{1,0:T(8,128)(2,1)S(1)}, bf16[4096,512]{1,0:T(8,128)(2,1)}, u32[]{:S(2)}) copy-start(bf16[4096,512]{1,0:T(8,128)(2,1)} %wq.1) | copy-start | bytes 12582916
  16.0 29.0 %copy-start.3 = (bf16[4096,2,128]{2,1,0:T(2,128)(2,1)S(1)}, bf16[4096,2,128]{2,1,0:T(2,128)(2,1)}, u32[]{:S(2)}) copy-start(bf16[4096,2,128]{2,1,0:T(2,128)(2,1)} %param.16) | copy-start | bytes 6291460
  16.0 29.0 %copy-start.5 = (f32[256,128]{1,0:T(8,128)S(1)}, f32[256,128]{1,0:T(8,128)}, u32[]{:S(2)}) copy-start(f32[256,128]{1,0:T(8,128)} %constant.11.clone.cos_hbm.cos_ref) | copy-start | bytes 393220
  16.0 29.0 %copy-start.6 = (f32[256,128]{1,0:T(8,128)S(1)}, f32[256,128]{1,0:T(8,128)}, u32[]{:S(2)}) copy-start(f32[256,128]{1,0:T(8,128)} %constant.12.clone.sin_hbm.sin_ref) | copy-start | bytes 393220
  16.0 29.0 %copy-start.7 = (f32[4096]{0:T(1024)S(1)}, f32[4096]{0:T(1024)}, u32[]{:S(2)}) copy-start(f32[4096]{0:T(1024)} %param.14) | copy-start | bytes 49156
  16.0 29.0 %copy-start.9 = (s32[192]{0:T(256)S(1)}, s32[192]{0:T(256)}, u32[]{:S(2)}) copy-start(s32[192]{0:T(256)} %source_s.3) | copy-start | bytes 2308
  18.5 26.5 %collective-permute-start.9 = (bf16[2,2,256,128]{3,2,1,0:T(8,128)(2,1)S(1)}, bf16[2,2,256,128]{3,2,1,0:T(8,128)(2,1)S(1)}, u32[]{:S(2)}, u32[]{:S(2)}) collective-permute-start(bf16[2,2,256,128]{3,2,1,0:T(8,128)(2,1)S(1)} %get-tuple-element.33), channel_id=1, source_target_pairs={{0,8},{4,12},{8,0},{12,4},{1,9},{5,13},{9,1},{13,5},{2,10},{6,14},... | collective-permute-start | bytes 786440 | tf_op jit(solution)/shard_map/ppermute | solution.py:526
  20.3 24.7 %collective-permute-start.10 = (bf16[2,2,256,128]{3,2,1,0:T(8,128)(2,1)S(1)}, bf16[2,2,256,128]{3,2,1,0:T(8,128)(2,1)S(1)}, u32[]{:S(2)}, u32[]{:S(2)}) collective-permute-start(bf16[2,2,256,128]{3,2,1,0:T(8,128)(2,1)S(1)} %get-tuple-element.34), channel_id=1, source_target_pairs={{0,12},{4,8},{8,4},{12,0},{1,13},{5,9},{9,5},{13,1},{2,14},{6,10},... | collective-permute-start | bytes 786440 | tf_op jit(solution)/shard_map/ppermute | solution.py:526
  22.6 7.5 %collective-permute-start.3 = (bf16[48,1024]{1,0:T(8,128)(2,1)S(1)}, bf16[48,1024]{1,0:T(8,128)(2,1)S(1)}, u32[]{:S(2)}, u32[]{:S(2)}) collective-permute-start(bf16[48,1024]{1,0:T(8,128)(2,1)S(1)} %get-tuple-element.30), channel_id=1, source_target_pairs={{0,3},{1,2},{2,1},{3,0},{4,7},{5,6},{6,5},{7,4},{8,11},{9,10},{10,... | collective-permute-start | bytes 294920 | tf_op jit(solution)/shard_map/ppermute | solution.py:526
  26.3 8.3 %collective-permute-start.4 = (bf16[48,1024]{1,0:T(8,128)(2,1)S(1)}, bf16[48,1024]{1,0:T(8,128)(2,1)S(1)}, u32[]{:S(2)}, u32[]{:S(2)}) collective-permute-start(bf16[48,1024]{1,0:T(8,128)(2,1)S(1)} %get-tuple-element.31), channel_id=1, source_target_pairs={{0,2},{1,3},{2,0},{3,1},{4,6},{5,7},{6,4},{7,5},{8,10},{9,11},{10,... | collective-permute-start | bytes 294920 | tf_op jit(solution)/shard_map/ppermute | solution.py:526
  26.3 8.3 %collective-permute-start.5 = (bf16[48,1024]{1,0:T(8,128)(2,1)S(1)}, bf16[48,1024]{1,0:T(8,128)(2,1)S(1)}, u32[]{:S(2)}, u32[]{:S(2)}) collective-permute-start(bf16[48,1024]{1,0:T(8,128)(2,1)S(1)} %get-tuple-element.32), channel_id=1, source_target_pairs={{0,1},{1,0},{2,3},{3,2},{4,5},{5,4},{6,7},{7,6},{8,9},{9,8},{10,11... | collective-permute-start | bytes 294920 | tf_op jit(solution)/shard_map/ppermute | solution.py:526
  34.7 5.0 %collective-permute-start.6 = (bf16[48,1024]{1,0:T(8,128)(2,1)S(1)}, bf16[48,1024]{1,0:T(8,128)(2,1)S(1)}, u32[]{:S(2)}, u32[]{:S(2)}) collective-permute-start(bf16[48,1024]{1,0:T(8,128)(2,1)S(1)} %sum_terms.2.rest_0_), channel_id=1, source_target_pairs={{0,1},{1,0},{2,3},{3,2},{4,5},{5,4},{6,7},{7,6},{8,9},{9,8},{10,11... | collective-permute-start | bytes 294920 | tf_op jit(solution)/shard_map/ppermute | solution.py:526
  35.3 9.7 %collective-permute-start.7 = (bf16[48,1024]{1,0:T(8,128)(2,1)S(1)}, bf16[48,1024]{1,0:T(8,128)(2,1)S(1)}, u32[]{:S(2)}, u32[]{:S(2)}) collective-permute-start(bf16[48,1024]{1,0:T(8,128)(2,1)S(1)} %sum_terms.2.rest_0_), channel_id=1, source_target_pairs={{0,2},{1,3},{2,0},{3,1},{4,6},{5,7},{6,4},{7,5},{8,10},{9,11},{10,... | collective-permute-start | bytes 294920 | tf_op jit(solution)/shard_map/ppermute | solution.py:526
  37.8 7.1 %collective-permute-start.8 = (bf16[48,1024]{1,0:T(8,128)(2,1)S(1)}, bf16[48,1024]{1,0:T(8,128)(2,1)S(1)}, u32[]{:S(2)}, u32[]{:S(2)}) collective-permute-start(bf16[48,1024]{1,0:T(8,128)(2,1)S(1)} %sum_terms.2.rest_0_), channel_id=1, source_target_pairs={{0,3},{1,2},{2,1},{3,0},{4,7},{5,6},{6,5},{7,4},{8,11},{9,10},{10,... | collective-permute-start | bytes 294920 | tf_op jit(solution)/shard_map/ppermute | solution.py:526
  51.9 6.8 %collective-permute-start.11 = (bf16[48,1024]{1,0:T(8,128)(2,1)S(1)}, bf16[48,1024]{1,0:T(8,128)(2,1)S(1)}, u32[]{:S(2)}, u32[]{:S(2)}) collective-permute-start(bf16[48,1024]{1,0:T(8,128)(2,1)S(1)} %get-tuple-element.36), channel_id=1, source_target_pairs={{0,3},{1,2},{2,1},{3,0},{4,7},{5,6},{6,5},{7,4},{8,11},{9,10},{10,... | collective-permute-start | bytes 294920 | tf_op jit(solution)/shard_map/ppermute | solution.py:526
  53.9 8.3 %collective-permute-start.12 = (bf16[48,1024]{1,0:T(8,128)(2,1)S(1)}, bf16[48,1024]{1,0:T(8,128)(2,1)S(1)}, u32[]{:S(2)}, u32[]{:S(2)}) collective-permute-start(bf16[48,1024]{1,0:T(8,128)(2,1)S(1)} %get-tuple-element.37), channel_id=1, source_target_pairs={{0,2},{1,3},{2,0},{3,1},{4,6},{5,7},{6,4},{7,5},{8,10},{9,11},{10,... | collective-permute-start | bytes 294920 | tf_op jit(solution)/shard_map/ppermute | solution.py:526
  55.0 7.2 %collective-permute-start.13 = (bf16[48,1024]{1,0:T(8,128)(2,1)S(1)}, bf16[48,1024]{1,0:T(8,128)(2,1)S(1)}, u32[]{:S(2)}, u32[]{:S(2)}) collective-permute-start(bf16[48,1024]{1,0:T(8,128)(2,1)S(1)} %get-tuple-element.38), channel_id=1, source_target_pairs={{0,1},{1,0},{2,3},{3,2},{4,5},{5,4},{6,7},{7,6},{8,9},{9,8},{10,11... | collective-permute-start | bytes 294920 | tf_op jit(solution)/shard_map/ppermute | solution.py:526
  62.3 8.7 %collective-permute-start.14 = (bf16[48,1024]{1,0:T(8,128)(2,1)S(1)}, bf16[48,1024]{1,0:T(8,128)(2,1)S(1)}, u32[]{:S(2)}, u32[]{:S(2)}) collective-permute-start(bf16[48,1024]{1,0:T(8,128)(2,1)S(1)} %sum_terms.3.rest_0_), channel_id=1, source_target_pairs={{0,1},{1,0},{2,3},{3,2},{4,5},{5,4},{6,7},{7,6},{8,9},{9,8},{10,11... | collective-permute-start | bytes 294920 | tf_op jit(solution)/shard_map/ppermute | solution.py:526
  62.4 10.4 %collective-permute-start.15 = (bf16[48,1024]{1,0:T(8,128)(2,1)S(1)}, bf16[48,1024]{1,0:T(8,128)(2,1)S(1)}, u32[]{:S(2)}, u32[]{:S(2)}) collective-permute-start(bf16[48,1024]{1,0:T(8,128)(2,1)S(1)} %sum_terms.3.rest_0_), channel_id=1, source_target_pairs={{0,2},{1,3},{2,0},{3,1},{4,6},{5,7},{6,4},{7,5},{8,10},{9,11},{10,... | collective-permute-start | bytes 294920 | tf_op jit(solution)/shard_map/ppermute | solution.py:526
  64.7 8.1 %collective-permute-start.16 = (bf16[48,1024]{1,0:T(8,128)(2,1)S(1)}, bf16[48,1024]{1,0:T(8,128)(2,1)S(1)}, u32[]{:S(2)}, u32[]{:S(2)}) collective-permute-start(bf16[48,1024]{1,0:T(8,128)(2,1)S(1)} %sum_terms.3.rest_0_), channel_id=1, source_target_pairs={{0,3},{1,2},{2,1},{3,0},{4,7},{5,6},{6,5},{7,4},{8,11},{9,10},{10,... | collective-permute-start | bytes 294920 | tf_op jit(solution)/shard_map/ppermute | solution.py:526

commit v6 on v5

--- a/solution.py
+++ b/solution.py
@@ -15,7 +15,6 @@
 GROUP = 8
 PIECE = 16
 CHUNK = 8
-NOTE = 16
 
 F32 = jnp.float32
 BF16 = jnp.bfloat16
@@ -40,18 +39,18 @@
     angles = np.arange(positions, dtype=np.float64)[:, None] * frequency[None, :]
     cosine = np.concatenate([np.cos(angles), np.cos(angles)], axis=-1)
     sine = np.concatenate([-np.sin(angles), np.sin(angles)], axis=-1)
-    return cosine.astype(np.float32), sine.astype(np.float32)
+    return np.stack([cosine, sine]).astype(np.float32)
 
 
 def turn(x, cosine, sine):
     return x * cosine + pltpu.roll(x, HD // 2, 1) * sine
 
 
-def gather_angles(position_of, slots, cos_ref, sin_ref, cos_rows, sin_rows):
+def gather_angles(position_of, slots, table, cos_rows, sin_rows):
     for s in range(slots):
         p = position_of(s)
-        cos_rows[s : s + 1, :] = cos_ref[pl.ds(p, 1), :]
-        sin_rows[s : s + 1, :] = sin_ref[pl.ds(p, 1), :]
+        cos_rows[s : s + 1, :] = table[0, pl.ds(p, 1), :]
+        sin_rows[s : s + 1, :] = table[1, pl.ds(p, 1), :]
 
 
 def spread_normed(normed3, spread, slots, width):
@@ -67,40 +66,19 @@
     spread[:, slots:, :] = spread_all[:, 2 * HD :].reshape(blocks, slots, 2 * HD)
 
 
-def project(normed3, spread, wq, wkv, slots, width, wq_copies=(), wkv_copies=()):
-    pieces = max(len(wq_copies), 1)
-    depth = width // pieces
+def project(normed3, spread, wq, wkv, slots, width):
     query = None
     pair = None
-    for c in range(pieces):
-        for copy in wkv_copies[c : c + 1]:
-            copy.wait()
-        for b in range(c * depth // HD, (c + 1) * depth // HD):
-            part = jnp.dot(
-                spread[b], wkv[b * 2 * HD : (b + 1) * 2 * HD, :], preferred_element_type=F32
-            )
-            pair = part if pair is None else pair + part
-    for c in range(pieces):
-        for copy in wq_copies[c : c + 1]:
-            copy.wait()
-        for b in range(c * depth // (2 * HD), (c + 1) * depth // (2 * HD)):
-            block = jnp.concatenate([normed3[2 * b], normed3[2 * b + 1]], axis=1)
-            part = jnp.dot(
-                block, wq[b * 2 * HD : (b + 1) * 2 * HD, :], preferred_element_type=F32
-            )
-            query = part if query is None else query + part
+    for b in range(width // HD):
+        part = jnp.dot(
+            spread[b], wkv[b * 2 * HD : (b + 1) * 2 * HD, :], preferred_element_type=F32
+        )
+        pair = part if pair is None else pair + part
+    for b in range(width // (2 * HD)):
+        block = jnp.concatenate([normed3[2 * b], normed3[2 * b + 1]], axis=1)
+        part = jnp.dot(block, wq[b * 2 * HD : (b + 1) * 2 * HD, :], preferred_element_type=F32)
+        query = part if query is None else query + part
     return query, pair[:slots], pair[slots:]
-
-
-def weight_copies(src, dst, sem, pieces):
-    depth = src.shape[0] // pieces
-    copies = [
-        pltpu.make_async_copy(
-            src.at[pl.ds(c * depth, depth)], dst.at[pl.ds(c * depth, depth)], sem.at[c]
-        )
-        for c in range(pieces)
-    ]
-    return copies
 
 
 def put_row(cache, place, p, key_row, value_row):
@@ -147,42 +125,32 @@
             normed3[first + i] = normed[:, i * HD : (i + 1) * HD]
 
 
-def first_kernel(
-    peers, slots, heads, shard,
-    meta, source_hbm, lengths_hbm, hidden_hbm, gain_hbm, cos_hbm, sin_hbm, wq_hbm, wkv_hbm,
-    cache_hbm, query_out, newkey_out, newvalue_out, plan, *rest,
+def pack_kernel(
+    peers, slots, meta, source_hbm, lengths_hbm, gain_hbm, table_hbm, hidden_hbm, cache_hbm,
+    plan, lengths_out, gain_out, table_out, hidden_out, *rest,
 ):
-    others = peers - 1
-    moving = others * MOVE
-    box, notes = rest[0], (None,) + rest[1:others]
-    (wq, wkv, normed3, spread, cos_rows, sin_rows, leaving, hidden32, source_s, lengths_s, source_v,
-     hidden, gain, cos_ref, sin_ref, tail, small_sem, wq_sem, wkv_sem, in_sem,
-     box_sem) = rest[others:]
-    width = hidden.shape[1]
-    me, me_tp = meta[0], meta[1]
-    wq_copies = weight_copies(wq_hbm, wq, wq_sem, 4)
-    wkv_copies = weight_copies(wkv_hbm, wkv, wkv_sem, 4)
+    moving = (peers - 1) * MOVE
+    boxes, (source_s, source_v, leaving, small_sem, in_sem, out_sem) = rest[:-6], rest[-6:]
+    pairs = [
+        (source_hbm, source_v), (source_hbm, source_s), (lengths_hbm, lengths_out),
+        (gain_hbm, gain_out), (table_hbm, table_out), (hidden_hbm, hidden_out),
+    ]
     small = [
-        pltpu.make_async_copy(src, dst, small_sem.at[i])
-        for i, (src, dst) in enumerate((
-            (source_hbm, source_v), (source_hbm, source_s), (lengths_hbm, lengths_s),
-            (hidden_hbm, hidden), (gain_hbm, gain), (cos_hbm, cos_ref), (sin_hbm, sin_ref),
-        ))
-    ]
-    for copy in small + wkv_copies + wq_copies:
+        pltpu.make_async_copy(src, dst, small_sem.at[i]) for i, (src, dst) in enumerate(pairs)
+    ]
+    for copy in small:
         copy.start()
-    small[0].wait()
-    small[1].wait()
-
-    low = me * slots
+    for copy in small[:2]:
+        copy.wait()
+    low = meta[0] * slots
     src = source_v[...]
     index = lax.broadcasted_iota(I32, src.shape, 1)
     mine_goes = (src >= low) & (src < low + slots)
     mine_comes = (index >= low) & (index < low + slots)
     index_f = index.astype(F32)
-    send_slots = []
+    copies = []
     for k in range(1, peers):
-        other = jnp.bitwise_xor(me, k) * slots
+        other = jnp.bitwise_xor(meta[0], k) * slots
         sent = mine_goes & (index >= other) & (index < other + slots)
         taken = mine_comes & (src >= other) & (src < other + slots)
         for m in range(MOVE):
@@ -196,21 +164,46 @@
             known = (j >= 0) & (j < src.shape[1])
             slot = source_s[0, jnp.where(known, j, 0)] - low
             slot = jnp.where(known, slot, 0)
-            send_slots.append(slot)
             plan[at] = jnp.where((r >= 0) & (r < src.shape[1]), r - low, -1)
             plan[moving + at] = slot
-            pltpu.make_async_copy(cache_hbm.at[slot], leaving.at[at], in_sem.at[at]).start()
-
-    for copy in small[2:]:
+            copies.append(
+                pltpu.make_async_copy(cache_hbm.at[slot], leaving.at[at], in_sem.at[at])
+            )
+            copies[-1].start()
+    for copy in copies:
         copy.wait()
+    outs = []
+    for i, box in enumerate(boxes):
+        outs.append(pltpu.make_async_copy(leaving.at[pl.ds(i * MOVE, MOVE)], box, out_sem.at[i]))
+        outs[-1].start()
+    for copy in outs + small[2:]:
+        copy.wait()
+
+
+def first_kernel(
+    peers, slots, heads, shard,
+    meta, lengths_s, plan, hidden, gain, table, wq, wkv, cache_hbm, _box,
+    query_out, newkey_out, newvalue_out, *rest,
+):
+    others = peers - 1
+    moving = others * MOVE
+    notes = rest[:others]
+    normed3, spread, cos_rows, sin_rows, leaving, hidden32, in_sem = rest[others:]
+    width = hidden.shape[1]
+    low = meta[0] * slots
+    send_slots = [plan[moving + at] for at in range(moving)]
+    copies = [
+        pltpu.make_async_copy(cache_hbm.at[slot], leaving.at[at], in_sem.at[at])
+        for at, slot in enumerate(send_slots)
+    ]
+    for copy in copies:
+        copy.start()
     wide = hidden[...].astype(F32)
     hidden32[...] = wide
     norm_into(normed3, [wide], [gain[...]], [0], width)
     spread_normed(normed3, spread, slots, width)
-    gather_angles(lambda s: lengths_s[0, low + s], slots, cos_ref, sin_ref, cos_rows, sin_rows)
-    query, key, value = project(
-        normed3, spread, wq, wkv, slots, width, wq_copies, wkv_copies
-    )
+    gather_angles(lambda s: lengths_s[0, low + s], slots, table, cos_rows, sin_rows)
+    query, key, value = project(normed3, spread, wq, wkv, slots, width)
     cosine, sine = cos_rows[...], sin_rows[...]
     query_out[...] = jnp.zeros(query_out.shape, F32)
     for g in range(heads):
@@ -219,44 +212,23 @@
     newkey_out[...] = turn(key, cosine, sine).astype(BF16).astype(F32)
     newvalue_out[...] = value.astype(BF16).astype(F32)
 
+    for copy in copies:
+        copy.wait()
     positions = [lengths_s[0, low + slot] for slot in send_slots]
+    column = pl.multiple_of(meta[1] * shard, shard)
     for at, slot in enumerate(send_slots):
-        pltpu.make_async_copy(cache_hbm.at[slot], leaving.at[at], in_sem.at[at]).wait()
-        put_row(
-            leaving, at, positions[at],
-            newkey_out[pl.ds(slot, 1), :], newvalue_out[pl.ds(slot, 1), :],
-        )
-    cap = leaving.shape[2]
-    copies = [
-        pltpu.make_async_copy(
-            leaving.at[pl.ds(0, MOVE)], box.at[:, :, pl.ds(0, cap), :], box_sem.at[0]
-        )
-    ]
-    copies[0].start()
+        key_row, value_row = newkey_out[pl.ds(slot, 1), :], newvalue_out[pl.ds(slot, 1), :]
+        put_row(leaving, at, positions[at], key_row, value_row)
+        note, m = notes[at // MOVE], at % MOVE
+        note[m : m + 1, heads * HD : (heads + 1) * HD] = key_row
+        note[m : m + 1, (heads + 1) * HD : (heads + 2) * HD] = value_row
+        note[m : m + 1, (heads + 2) * HD :] = hidden32[pl.ds(slot, 1), pl.ds(column, shard)]
     rows = [query_out[pl.ds(pl.multiple_of(slot * GROUP, GROUP), GROUP), :] for slot in send_slots]
     attended = attend(leaving, list(range(moving)), positions, rows)
-    column = pl.multiple_of(me_tp * shard, shard)
-    for at, slot in enumerate(send_slots):
-        m = at % MOVE
-        residual = hidden32[pl.ds(slot, 1), pl.ds(column, shard)]
-        if at < MOVE:
-            blocks = [attended[at][g : g + 1, :] for g in range(heads)]
-            blocks += [residual[:, b * HD : (b + 1) * HD] for b in range(shard // HD)]
-            blocks += [jnp.zeros((1, HD), F32)] * (NOTE - len(blocks))
-            tail[m] = jnp.concatenate(blocks, axis=0).astype(BF16)
-            copies.append(
-                pltpu.make_async_copy(
-                    tail.at[m], box.at[m, 0, pl.ds(cap, NOTE), :], box_sem.at[1 + m]
-                )
-            )
-            copies[-1].start()
-        else:
-            note = notes[at // MOVE]
-            for g in range(heads):
-                note[m : m + 1, g * HD : (g + 1) * HD] = attended[at][g : g + 1, :]
-            note[m : m + 1, heads * HD :] = residual
-    for copy in copies:
-        copy.wait()
+    for at, got in enumerate(attended):
+        note, m = notes[at // MOVE], at % MOVE
+        for g in range(heads):
+            note[m : m + 1, g * HD : (g + 1) * HD] = got[g : g + 1, :]
 
 
 def attend_kernel(
@@ -274,7 +246,7 @@
     for c in range(slots // CHUNK):
         copy_in(c).wait()
         span = list(range(c * CHUNK, (c + 1) * CHUNK))
-        positions = [lengths_s[low + s] for s in span]
+        positions = [lengths_s[0, low + s] for s in span]
         for s, p in zip(span, positions):
             put_row(buffer, s, p, newkey[s : s + 1, :], newvalue[s : s + 1, :])
         got = attend(
@@ -302,12 +274,12 @@
 
 
 def out_kernel(
-    peers, peers_tp, slots, meta, lengths_s, plan, attended, wo, hidden, newkey, newvalue, box_hbm,
-    cache_hbm, *rest,
+    peers, peers_tp, slots, meta, plan, attended, wo, hidden, newkey, newvalue, cache_hbm, *rest,
 ):
-    notes, rest = rest[: peers - 2], rest[peers - 2 :]
-    own, sends, boxes = rest[0], rest[1:peers_tp], rest[peers_tp : peers_tp + peers - 2]
-    final_hbm, leaving, tail, sem, in_sem, out_sem, early_sem = rest[peers_tp + peers - 2 :]
+    notes, rest = rest[: peers - 1], rest[peers - 1 :]
+    own, sends, (newkey_out, newvalue_out, final_hbm, early_sem) = (
+        rest[0], rest[1:peers_tp], rest[peers_tp:]
+    )
     early = [
         pltpu.make_async_copy(
             cache_hbm.at[pl.ds(c * CHUNK, CHUNK)], final_hbm.at[pl.ds(c * CHUNK, CHUNK)],
@@ -321,48 +293,21 @@
         for copy in early:
             copy.start()
 
-    moving = (peers - 1) * MOVE
-    send_slots = [plan[moving + at] for at in range(MOVE, moving)]
-    packs = [
-        pltpu.make_async_copy(cache_hbm.at[slot], leaving.at[i], in_sem.at[i])
-        for i, slot in enumerate(send_slots)
-    ]
-    for pack in packs:
-        pack.start()
     shard = own.shape[1]
-    cap = box_hbm.shape[2] - NOTE
-    copy = pltpu.make_async_copy(box_hbm.at[:, 0, pl.ds(cap, NOTE), :], tail, sem.at[0])
-    copy.start()
-    rows = attended[...].astype(F32)
-    heads = rows.shape[1] // HD
     column = pl.multiple_of(meta[1] * shard, shard)
-    residual = hidden[:, pl.ds(column, shard)].astype(F32)
-    row_index = lax.broadcasted_iota(I32, rows.shape, 0)
-    residual_index = lax.broadcasted_iota(I32, residual.shape, 0)
-    copy.wait()
+    width = attended.shape[1]
+    parts = [
+        attended[...].astype(F32), newkey[...], newvalue[...],
+        hidden[:, pl.ds(column, shard)].astype(F32),
+    ]
+    firsts = [0, width, width + HD, width + 2 * HD, width + 2 * HD + shard]
     for at in range((peers - 1) * MOVE):
         m = at % MOVE
-        if at < MOVE:
-            blocks = tail[m].astype(F32)
-            blocks = [blocks[b : b + 1, :] for b in range(heads + shard // HD)]
-            note = jnp.concatenate(blocks, axis=1)
-        else:
-            note = notes[at // MOVE - 1][m : m + 1, :]
-        rows = jnp.where(row_index == plan[at], note[:, : heads * HD], rows)
-        residual = jnp.where(residual_index == plan[at], note[:, heads * HD :], residual)
-    for pack in packs:
-        pack.wait()
-    for i, slot in enumerate(send_slots):
-        put_row(
-            leaving, i, lengths_s[meta[0] * slots + slot],
-            newkey[pl.ds(slot, 1), :], newvalue[pl.ds(slot, 1), :],
-        )
-    outs = [
-        pltpu.make_async_copy(leaving.at[pl.ds(k * MOVE, MOVE)], out, out_sem.at[k])
-        for k, out in enumerate(boxes)
-    ]
-    for out in outs:
-        out.start()
+        note = notes[at // MOVE][m : m + 1, :]
+        for i, part in enumerate(parts):
+            hit = lax.broadcasted_iota(I32, part.shape, 0) == plan[at]
+            parts[i] = jnp.where(hit, note[:, firsts[i] : firsts[i + 1]], part)
+    rows, newkey_out[...], newvalue_out[...], residual = parts
 
     @pl.when(is_odd(meta))
     def _():
@@ -370,8 +315,6 @@
             copy.wait()
 
     project_out(rows.astype(BF16), wo, residual, own, sends, meta[1], peers_tp)
-    for out in outs:
-        out.wait()
 
 
 def sum_kernel(own, *rest):
@@ -381,15 +324,15 @@
     rest[-1][...] = total.astype(BF16)
 
 
-def load_slots(slots, peers, cache_hbm, box_hbm, buffer, in_sem):
+def load_slots(slots, peers, cache_hbm, boxes, buffer, in_sem):
     copies = []
     for c in range(slots // CHUNK):
         span = pl.ds(c * CHUNK, CHUNK)
         copies.append(pltpu.make_async_copy(cache_hbm.at[span], buffer.at[span], in_sem.at[c]))
-    for k in range(peers - 1):
+    for k, box in enumerate(boxes):
         copies.append(
             pltpu.make_async_copy(
-                box_hbm[k].at[:, :, pl.ds(0, cache_hbm.shape[2]), :],
+                box,
                 buffer.at[pl.ds(slots + k * MOVE, MOVE)],
                 in_sem.at[slots // CHUNK + k],
             )
@@ -410,7 +353,7 @@
 
 def second_kernel(
     peers, peers_tp, slots, heads,
-    meta, source_s, lengths_s, plan, gain, cos_ref, sin_ref, newkey1, newvalue1,
+    meta, source_s, lengths_s, plan, gain, table, newkey1, newvalue1,
     wq, wkv, wo, cache_hbm, *rest,
 ):
     blocks, rest = rest[:peers_tp], rest[peers_tp:]
@@ -437,8 +380,8 @@
         width,
     )
     spread_normed(normed3, spread, slots, width)
-    lengths = [lengths_s[source_s[low + s]] for s in range(slots)]
-    gather_angles(lambda s: lengths[s] + 1, slots, cos_ref, sin_ref, cos_rows, sin_rows)
+    lengths = [lengths_s[0, source_s[low + s]] for s in range(slots)]
+    gather_angles(lambda s: lengths[s] + 1, slots, table, cos_rows, sin_rows)
     query, key, value = project(normed3, spread, wq, wkv, slots, width)
     cosine, sine = cos_rows[...], sin_rows[...]
     query_rows[...] = jnp.zeros(query_rows.shape, F32)
@@ -454,8 +397,7 @@
         span = list(range(c * CHUNK, (c + 1) * CHUNK))
         places = [place[s] for s in span]
         for s, at in zip(span, places):
-            first = jnp.where(at < slots, lengths[s], -1)
-            put_row(buffer, at, first, newkey1[s : s + 1, :], newvalue1[s : s + 1, :])
+            put_row(buffer, at, lengths[s], newkey1[s : s + 1, :], newvalue1[s : s + 1, :])
             put_row(buffer, at, lengths[s] + 1, newkey[s : s + 1, :], newvalue[s : s + 1, :])
         got = attend(
             buffer, places, [lengths[s] + 1 for s in span],
@@ -490,10 +432,9 @@
         cache_copies[c].wait()
         for s in range(c * CHUNK, (c + 1) * CHUNK):
             at = place[s]
-            length = lengths_s[source_s[low + s]]
+            length = lengths_s[0, source_s[low + s]]
             kept = at < slots
-            first = jnp.where(kept, length, -1)
-            put_row(buffer, at, first, newkey1[s : s + 1, :], newvalue1[s : s + 1, :])
+            put_row(buffer, at, length, newkey1[s : s + 1, :], newvalue1[s : s + 1, :])
             put_row(buffer, at, length + 1, newkey2[s : s + 1, :], newvalue2[s : s + 1, :])
             base = pl.multiple_of(jnp.minimum((length // PIECE) * PIECE, cap - 2 * PIECE), PIECE)
             window = (slice(None), pl.ds(base, 2 * PIECE), slice(None))
@@ -527,7 +468,7 @@
 
 
 def local(
-    tables, kv_cache, hidden, lengths, source, norm_gain, query_weight, keyval_weight, out_weight
+    table, kv_cache, hidden, lengths, source, norm_gain, query_weight, keyval_weight, out_weight
 ):
     peers, peers_tp = lax.axis_size("inst"), lax.axis_size("tp")
     slots, cap = kv_cache.shape[0], kv_cache.shape[2]
@@ -537,16 +478,10 @@
     others, moving = peers - 1, (peers - 1) * MOVE
     blocks = width // HD
     meta = jnp.stack([lax.axis_index("inst"), lax.axis_index("tp")]).astype(I32)
-    gain = norm_gain.reshape(1, width)
     wkv = keyval_weight.reshape(2 * width, HD)
-    cosine, sine = (jnp.asarray(table) for table in tables)
     row32 = jax.ShapeDtypeStruct((slots, HD), F32)
-    note_width = heads * HD + shard
+    note_width = (heads + 2) * HD + shard
     dma = pltpu.SemaphoreType.DMA
-    weights = [
-        pltpu.VMEM(query_weight.shape, BF16),
-        pltpu.VMEM(wkv.shape, BF16),
-    ]
     stages = [
         pltpu.VMEM((blocks, slots, HD), BF16),
         pltpu.VMEM((blocks, 2 * slots, 2 * HD), BF16),
@@ -556,45 +491,54 @@
     flops = 2 * slots * width * (heads + 2) * HD
     cache_bytes = kv_cache.size * 2
 
-    query, newkey1, newvalue1, plan, *notes = pl.pallas_call(
-        functools.partial(first_kernel, peers, slots, heads, shard),
+    slot_shape = kv_cache.shape[1:]
+    plan, lengths, gain, table, hidden, *boxes = pl.pallas_call(
+        functools.partial(pack_kernel, peers, slots),
         out_shape=[
-            jax.ShapeDtypeStruct((slots * GROUP, HD), F32),
-            row32,
-            row32,
             jax.ShapeDtypeStruct((2 * moving,), I32),
+            jax.ShapeDtypeStruct((1, source.shape[0]), I32),
+            jax.ShapeDtypeStruct((1, width), F32),
+            jax.ShapeDtypeStruct((2, cap, HD), F32),
+            jax.ShapeDtypeStruct(hidden.shape, BF16),
         ]
-        + [jax.ShapeDtypeStruct((MOVE, 2, cap + NOTE, HD), BF16)]
-        + [jax.ShapeDtypeStruct((MOVE, note_width), F32)] * (others - 1),
-        in_specs=[SMEM] + [HBM] * 9,
-        out_specs=[VMEM] * 3 + [SMEM, ANY] + [VMEM] * (others - 1),
-        scratch_shapes=weights
-        + stages
-        + [
-            pltpu.VMEM((moving,) + kv_cache.shape[1:], BF16),
-            pltpu.VMEM((slots, width), F32),
-            pltpu.SMEM((1, source.shape[0]), I32),
+        + [jax.ShapeDtypeStruct((MOVE,) + slot_shape, BF16)] * others,
+        in_specs=[SMEM] + [HBM] * 6,
+        out_specs=[SMEM] * 2 + [VMEM] * 3 + [ANY] * others,
+        scratch_shapes=[
             pltpu.SMEM((1, source.shape[0]), I32),
             pltpu.VMEM((1, source.shape[0]), I32),
-            pltpu.VMEM(hidden.shape, BF16),
-            pltpu.VMEM((1, width), F32),
-            pltpu.VMEM(cosine.shape, F32),
-            pltpu.VMEM(cosine.shape, F32),
-            pltpu.VMEM((MOVE, NOTE, HD), BF16),
-            dma((7,)),
-            dma((4,)),
-            dma((4,)),
+            pltpu.VMEM((moving,) + slot_shape, BF16),
+            dma((6,)),
             dma((moving,)),
-            dma((1 + MOVE,)),
+            dma((others,)),
+        ],
+        compiler_params=params(10),
+        cost_estimate=cost(1, 2 * cache_bytes),
+        name="pack",
+    )(meta, *(
+        pltpu.with_memory_space_constraint(x, pltpu.HBM)
+        for x in (source.reshape(1, -1), lengths.reshape(1, -1), norm_gain.reshape(1, width),
+                  jnp.asarray(table), hidden, kv_cache)
+    ))
+    got_boxes = [swapped(box, "inst", peers, k + 1) for k, box in enumerate(boxes)]
+
+    query, newkey1, newvalue1, *notes = pl.pallas_call(
+        functools.partial(first_kernel, peers, slots, heads, shard),
+        out_shape=[jax.ShapeDtypeStruct((slots * GROUP, HD), F32), row32, row32]
+        + [jax.ShapeDtypeStruct((MOVE, note_width), F32)] * others,
+        in_specs=[SMEM] * 3 + [VMEM] * 5 + [HBM, ANY],
+        out_specs=[VMEM] * (3 + others),
+        scratch_shapes=stages
+        + [
+            pltpu.VMEM((moving,) + slot_shape, BF16),
+            pltpu.VMEM((slots, width), F32),
+            dma((moving,)),
         ],
         compiler_params=params(24),
         cost_estimate=cost(flops, (query_weight.size + wkv.size) * 2),
         name="first_step",
-    )(meta, *(
-        pltpu.with_memory_space_constraint(x, pltpu.HBM)
-        for x in (source.reshape(1, -1), lengths.reshape(1, -1), hidden, gain, cosine, sine,
-                  query_weight, wkv, kv_cache)
-    ))
+    )(meta, lengths, plan, hidden, gain, table, query_weight, wkv,
+      pltpu.with_memory_space_constraint(kv_cache, pltpu.HBM), got_boxes[0])
     got_notes = [swapped(note, "inst", peers, k + 1) for k, note in enumerate(notes)]
 
     attended = pl.pallas_call(
@@ -616,26 +560,15 @@
     sent += [jax.ShapeDtypeStruct((slots, shard), BF16)] * (peers_tp - 1)
     own, *rest = pl.pallas_call(
         functools.partial(out_kernel, peers, peers_tp, slots),
-        out_shape=sent
-        + [jax.ShapeDtypeStruct((MOVE,) + kv_cache.shape[1:], BF16)] * (others - 1)
-        + [pltpu.HBM(kv_cache.shape, BF16)],
-        in_specs=[SMEM] * 3 + [VMEM] * 5 + [ANY] * 2 + [VMEM] * (others - 1),
-        out_specs=[VMEM] * peers_tp + [ANY] * (others - 1) + [HBM],
-        scratch_shapes=[
-            pltpu.VMEM((moving - MOVE,) + kv_cache.shape[1:], BF16),
-            pltpu.VMEM((MOVE, NOTE, HD), BF16),
-            dma((1,)),
-            dma((moving - MOVE,)),
-            dma((others - 1,)),
-            dma((slots // CHUNK,)),
-        ],
+        out_shape=sent + [row32, row32, pltpu.HBM(kv_cache.shape, BF16)],
+        in_specs=[SMEM] * 2 + [VMEM] * 5 + [ANY] + [VMEM] * others,
+        out_specs=[VMEM] * (peers_tp + 2) + [HBM],
+        scratch_shapes=[dma((slots // CHUNK,))],
         compiler_params=params(20),
         cost_estimate=cost(2 * slots * width * heads * HD, out_weight.size * 2),
         name="out_projection",
-    )(meta, lengths, plan, attended, out_weight, hidden, newkey1, newvalue1, got_notes[0], kv_cache,
-      *got_notes[1:])
-    sends, boxes, final_cache = rest[: peers_tp - 1], rest[peers_tp - 1 : -1], rest[-1]
-    got_boxes = got_notes[:1] + [swapped(box, "inst", peers, k + 2) for k, box in enumerate(boxes)]
+    )(meta, plan, attended, out_weight, hidden, newkey1, newvalue1, kv_cache, *got_notes)
+    sends, (newkey1, newvalue1, final_cache) = rest[: peers_tp - 1], rest[peers_tp - 1 :]
 
     def summed(own, sends):
         got = [swapped(sends[k - 1], "tp", peers_tp, k) for k in range(peers_tp - 1, 0, -1)]
@@ -656,7 +589,7 @@
     newkey2, newvalue2, own, *sends = pl.pallas_call(
         functools.partial(second_kernel, peers, peers_tp, slots, heads),
         out_shape=[row32, row32] + sent,
-        in_specs=[SMEM] * 4 + [VMEM] * 8 + [ANY] + [VMEM] * peers_tp + [ANY] * others,
+        in_specs=[SMEM] * 4 + [VMEM] * 7 + [ANY] + [VMEM] * peers_tp + [ANY] * others,
         out_specs=[VMEM] * (2 + peers_tp),
         scratch_shapes=stages
         + [
@@ -669,7 +602,7 @@
         compiler_params=params(32),
         cost_estimate=cost(3 * flops, cache_bytes + (query_weight.size + wkv.size) * 4),
         name="second_step",
-    )(meta, source, lengths, plan, gain, cosine, sine, newkey1, newvalue1, query_weight, wkv,
+    )(meta, source, lengths, plan, gain, table, newkey1, newvalue1, query_weight, wkv,
       out_weight, kv_cache, *pieces, *got_boxes)
 
     pieces = summed(own, sends)
@@ -704,9 +637,9 @@
 
 def solution(mesh):
     def whole(kv_cache, *rest):
-        tables = angle_tables(kv_cache.shape[2])
+        table = angle_tables(kv_cache.shape[2])
         return jax.shard_map(
-            functools.partial(local, tables),
+            functools.partial(local, table),
             mesh=mesh,
             in_specs=(
                 P(("groups", "inst"), None, None, "tp"),

time: 74.2 us -> 77.8 us (1.049)
  waiting for transfers between devices: 21.2 us -> 26.5 us
  starting transfers between devices: 25 us -> 23.2 us
    ppermute x17 -> x18, waiting for transfers between devices: 21.2 us -> 26.5 us  [swapped(): return lax.ppermute(x, axis, [(i, i ^ k) for i in range(size)])]
    pallas_call x0 -> x1, Pallas kernels: none -> 4.43 us  [local(): pl.pallas_call(functools.partial(pack_kernel, peers, slots), out_shape=[j...]
    pallas_call x1, Pallas kernels: 7.47 us -> 4.09 us  [local(): pl.pallas_call(functools.partial(first_kernel, peers, slots, heads, shard...]
    ppermute x17 -> x18, starting transfers between devices: 25 us -> 23.2 us  [swapped(): return lax.ppermute(x, axis, [(i, i ^ k) for i in range(size)])]
    pallas_call x1, Pallas kernels: 2.42 us -> 1.56 us  [local(): pl.pallas_call(functools.partial(out_kernel, peers, peers_tp, slots), out...]
  transfers between devices with their start and end apart: 17 -> 18, of which waited for: 7 -> 8; matrix products, arithmetic and copies ran while one was open for 0% -> 0% of each run, Pallas kernels for 12% -> 19%
where the time goes in v6:
time: 77.8 us; the launch traced here: 77.7 us
  Pallas kernels  27 us (35%)
  waiting for transfers between devices  26.5 us (34%)
  starting transfers between devices  23.2 us (30%)
  between operations  0.8 us (1%)
    ppermute x18, waiting for transfers between devices, swapped(): return lax.ppermute(x, axis, [(i, i ^ k) for i in range(size)])  26.5 us
    ppermute x18, starting transfers between devices, swapped(): return lax.ppermute(x, axis, [(i, i ^ k) for i in range(size)])  23.2 us
    pallas_call x1, Pallas kernels, local(): pl.pallas_call(functools.partial(second_kernel, peers, peers_tp, slots, h...  6.74 us
    pallas_call x1, Pallas kernels, local(): pl.pallas_call(functools.partial(attend_kernel, slots, heads), out_shape=...  4.56 us
    pallas_call x1, Pallas kernels, local(): pl.pallas_call(functools.partial(pack_kernel, peers, slots), out_shape=[j...  4.43 us
    pallas_call x1, Pallas kernels, local(): pl.pallas_call(functools.partial(cache_kernel, peers, slots), out_shape=j...  4.25 us
    pallas_call x1, Pallas kernels, local(): pl.pallas_call(functools.partial(first_kernel, peers, slots, heads, shard...  4.09 us
    pallas_call x1, Pallas kernels, local(): pl.pallas_call(functools.partial(out_kernel, peers, peers_tp, slots), out...  1.56 us
  transfers between devices with their start and end apart: 18, of which 8 were waited for; matrix products, arithmetic and copies ran while one was open for 0% of the time, Pallas kernels for 19%

profile of v6, /device:TPU:0, one launch (start us, length us, event | category | flops | bytes accessed | tf_op | source)
XLA Modules:
  0.0 77.7 jit_solution(17793092164807025414)
XLA Ops:
  0.6 0.0 copy-start.2
  0.6 0.0 copy-start.1
  0.7 0.1 pad_add_fusion.meta
  0.7 0.0 slice-start
  0.7 4.4 %pack.1 = (s32[12]{0:T(128)S(1)}, s32[1,192]{1,0:T(1,128)S(1)}, f32[1,4096]{1,0:T(1,128)S(1)}, f32[2,256,128]{2,1,0:T(8,128)S(1)}, bf16[48,4096]{1,0:T(8,128)(2,...) custom-call(s32[2]{0:T(128)S(1)} %pad_add_fusion.meta, ...), custom_call_target="tpu_custom_call" | custom-call | flops 1 | bytes 12582912 | tf_op jit(solution)/shard_map/pack/pallas_call | solution.py:495
  5.2 0.5 collective-permute-start
  5.7 2.6 %collective-permute-start.10 = (bf16[2,2,256,128]{3,2,1,0:T(8,128)(2,1)S(1)}, bf16[2,2,256,128]{3,2,1,0:T(8,128)(2,1)S(1)}, u32[]{:S(2)}, u32[]{:S(2)}) collective-permute-start(bf16[2,2,256,128]{3,2,1,0:T(8,128)(2,1)S(1)} %get-tuple-element.47), channel_id=1, source_target_pairs={{0,8},{4,12},{8,0},{12,4},{1,9},{5,13},{9,1},{13,5},{2,10},{6,14},... | collective-permute-start | bytes 786440 | tf_op jit(solution)/shard_map/ppermute | solution.py:467
  8.3 0.1 collective-permute-start.11
  8.3 0.0 collective-permute-done._box.rest_4_.rest_0_
  8.3 0.0 copy-done.2
  8.4 0.0 copy-done.1
  8.4 0.0 slice-start.1
  8.4 4.1 %first_step.1 = (f32[384,128]{1,0:T(8,128)S(1)}, f32[48,128]{1,0:T(8,128)S(1)}, f32[48,128]{1,0:T(8,128)S(1)}, f32[2,1792]{1,0:T(2,128)S(1)}, f32[2,1792]{1,0:T(2,128)S(1)}, /*index=5*/f32[2,1792]{1,0:T(2,128)S(1)}) custom-call(s32[2]{0:T(128)S(1)} %pad_add_fusion.meta, s32[1,192]{1,0:T(1,128)S(1)} %get-tuple-element.29.lengths_s, ...), custom_call_target="tpu_custom_call" | custom-call | flops 301989888 | bytes 6291456 | tf_op jit(solution)/shard_map/first_step/pallas_call | solution.py:525
  12.5 0.0 copy-start
  12.5 0.2 collective-permute-start.1
  12.7 1.9 %collective-permute-start.2 = (f32[2,1792]{1,0:T(2,128)S(1)}, f32[2,1792]{1,0:T(2,128)S(1)}, u32[]{:S(2)}, u32[]{:S(2)}) collective-permute-start(f32[2,1792]{1,0:T(2,128)S(1)} %get-tuple-element.39), channel_id=1, source_target_pairs={{0,8},{4,12},{8,0},{12,4},{1,9},{5,13},{9,1},{13,5},{2,10},{6,14},... | collective-permute-start | bytes 43016 | tf_op jit(solution)/shard_map/ppermute | solution.py:467
  14.6 0.0 collective-permute-start.3
  14.6 0.0 slice-done
  14.6 0.0 slice-done.1
  14.6 4.6 %attention.1.attended = bf16[48,512]{1,0:T(8,128)(2,1)S(1)} custom-call(s32[2]{0:T(128)S(1)} %pad_add_fusion.meta, s32[1,192]{1,0:T(1,128)S(1)} %get-tuple-element.29.lengths_s, f32[384,128]{1,0:T(8,128)S(1)} %get-tuple-element.35.query, f32[48,128]{1,0:T(8,128)S(1)} %get-tuple-element.36.newkey, f32[48,128]{1,0:T(8,128)S(1)} %get-tuple-element.37.newvalue, ...), custom_call_target="tpu_custom_call" | custom-call | flops 25165824 | bytes 6291456 | tf_op jit(solution)/shard_map/attention/pallas_call | solution.py:544
  19.2 0.0 copy-start.3
  19.2 0.0 collective-permute-done.1.rest_0_
  19.2 2.0 %collective-permute-done.2.rest_1_ = f32[2,1792]{1,0:T(2,128)S(1)} collective-permute-done((f32[2,1792]{1,0:T(2,128)S(1)}, f32[2,1792]{1,0:T(2,128)S(1)}, u32[]{:S(2)}, u32[]{:S(2)}) %collective-permute-start.2) | collective-permute-done | bytes 14368 | tf_op jit(solution)/shard_map/ppermute | solution.py:467
  21.3 0.0 collective-permute-done.3.rest_2_
  21.3 0.0 copy-done
  21.3 1.6 %out_projection.1 = (f32[48,1024]{1,0:T(8,128)S(1)}, bf16[48,1024]{1,0:T(8,128)(2,1)S(1)}, bf16[48,1024]{1,0:T(8,128)(2,1)S(1)}, bf16[48,1024]{1,0:T(8,128)(2,1)...) custom-call(s32[2]{0:T(128)S(1)} %pad_add_fusion.meta, ...), custom_call_target="tpu_custom_call" | custom-call | flops 201326592 | bytes 4194304 | tf_op jit(solution)/shard_map/out_projection/pallas_call | solution.py:561
  22.8 3.9 %collective-permute-start.4 = (bf16[48,1024]{1,0:T(8,128)(2,1)S(1)}, bf16[48,1024]{1,0:T(8,128)(2,1)S(1)}, u32[]{:S(2)}, u32[]{:S(2)}) collective-permute-start(bf16[48,1024]{1,0:T(8,128)(2,1)S(1)} %get-tuple-element.44), channel_id=1, source_target_pairs={{0,3},{1,2},{2,1},{3,0},{4,7},{5,6},{6,5},{7,4},{8,11},{9,10},{10,... | collective-permute-start | bytes 294920 | tf_op jit(solution)/shard_map/ppermute | solution.py:467
  26.7 0.0 collective-permute-start.5
  26.7 0.6 collective-permute-start.6
  27.4 2.1 %collective-permute-done.4.rest_0_ = bf16[48,1024]{1,0:T(8,128)(2,1)S(1)} collective-permute-done((bf16[48,1024]{1,0:T(8,128)(2,1)S(1)}, bf16[48,1024]{1,0:T(8,128)(2,1)S(1)}, u32[]{:S(2)}, u32[]{:S(2)}) %collective-permute-start.4) | collective-permute-done | bytes 98336 | tf_op jit(solution)/shard_map/ppermute | solution.py:467
  29.4 6.2 %collective-permute-done.5.rest_1_ = bf16[48,1024]{1,0:T(8,128)(2,1)S(1)} collective-permute-done((bf16[48,1024]{1,0:T(8,128)(2,1)S(1)}, bf16[48,1024]{1,0:T(8,128)(2,1)S(1)}, u32[]{:S(2)}, u32[]{:S(2)}) %collective-permute-start.5) | collective-permute-done | bytes 98336 | tf_op jit(solution)/shard_map/ppermute | solution.py:467
  35.6 0.0 collective-permute-done.6.rest_2_
  35.6 0.1 sum_terms.2.rest_0_
  35.7 0.1 collective-permute-start.7
  35.8 1.0 %collective-permute-start.8 = (bf16[48,1024]{1,0:T(8,128)(2,1)S(1)}, bf16[48,1024]{1,0:T(8,128)(2,1)S(1)}, u32[]{:S(2)}, u32[]{:S(2)}) collective-permute-start(bf16[48,1024]{1,0:T(8,128)(2,1)S(1)} %sum_terms.2.rest_0_), channel_id=1, source_target_pairs={{0,2},{1,3},{2,0},{3,1},{4,6},{5,7},{6,4},{7,5},{8,10},{9,11},{10,... | collective-permute-start | bytes 294920 | tf_op jit(solution)/shard_map/ppermute | solution.py:467
  36.7 3.4 %collective-permute-start.9 = (bf16[48,1024]{1,0:T(8,128)(2,1)S(1)}, bf16[48,1024]{1,0:T(8,128)(2,1)S(1)}, u32[]{:S(2)}, u32[]{:S(2)}) collective-permute-start(bf16[48,1024]{1,0:T(8,128)(2,1)S(1)} %sum_terms.2.rest_0_), channel_id=1, source_target_pairs={{0,3},{1,2},{2,1},{3,0},{4,7},{5,6},{6,5},{7,4},{8,11},{9,10},{10,... | collective-permute-start | bytes 294920 | tf_op jit(solution)/shard_map/ppermute | solution.py:467
  40.1 0.0 collective-permute-done.10.rest_5_.rest_1_
  40.1 0.0 collective-permute-done.11.rest_6_.rest_2_
  40.1 1.7 %collective-permute-done.7.rest_1_ = bf16[48,1024]{1,0:T(8,128)(2,1)S(1)} collective-permute-done((bf16[48,1024]{1,0:T(8,128)(2,1)S(1)}, bf16[48,1024]{1,0:T(8,128)(2,1)S(1)}, u32[]{:S(2)}, u32[]{:S(2)}) %collective-permute-start.7) | collective-permute-done | bytes 98336 | tf_op jit(solution)/shard_map/ppermute | solution.py:467
  41.8 4.7 %collective-permute-done.8.rest_2_ = bf16[48,1024]{1,0:T(8,128)(2,1)S(1)} collective-permute-done((bf16[48,1024]{1,0:T(8,128)(2,1)S(1)}, bf16[48,1024]{1,0:T(8,128)(2,1)S(1)}, u32[]{:S(2)}, u32[]{:S(2)}) %collective-permute-start.8) | collective-permute-done | bytes 98336 | tf_op jit(solution)/shard_map/ppermute | solution.py:467
  46.5 0.0 collective-permute-done.9.rest_3_
  46.5 0.0 copy-done.3
  46.5 6.7 %second_step.1 = (f32[48,128]{1,0:T(8,128)S(1)}, f32[48,128]{1,0:T(8,128)S(1)}, f32[48,1024]{1,0:T(8,128)S(1)}, bf16[48,1024]{1,0:T(8,128)(2,1)S(1)}, bf16[48,10...) custom-call(s32[2]{0:T(128)S(1)} %pad_add_fusion.meta, s32[192]{0:T(256)S(1)} %copy-done.3, ...), custom_call_target="tpu_custom_call" | custom-call | flops 905969664 | bytes 18874368 | tf_op jit(solution)/shard_map/second_step/pallas_call | solution.py:589
  53.3 1.1 %collective-permute-start.12 = (bf16[48,1024]{1,0:T(8,128)(2,1)S(1)}, bf16[48,1024]{1,0:T(8,128)(2,1)S(1)}, u32[]{:S(2)}, u32[]{:S(2)}) collective-permute-start(bf16[48,1024]{1,0:T(8,128)(2,1)S(1)} %get-tuple-element.50), channel_id=1, source_target_pairs={{0,3},{1,2},{2,1},{3,0},{4,7},{5,6},{6,5},{7,4},{8,11},{9,10},{10,... | collective-permute-start | bytes 294920 | tf_op jit(solution)/shard_map/ppermute | solution.py:467
  54.4 2.7 %collective-permute-start.13 = (bf16[48,1024]{1,0:T(8,128)(2,1)S(1)}, bf16[48,1024]{1,0:T(8,128)(2,1)S(1)}, u32[]{:S(2)}, u32[]{:S(2)}) collective-permute-start(bf16[48,1024]{1,0:T(8,128)(2,1)S(1)} %get-tuple-element.51), channel_id=1, source_target_pairs={{0,2},{1,3},{2,0},{3,1},{4,6},{5,7},{6,4},{7,5},{8,10},{9,11},{10,... | collective-permute-start | bytes 294920 | tf_op jit(solution)/shard_map/ppermute | solution.py:467
  57.1 0.6 collective-permute-start.14
  57.7 2.9 %collective-permute-done.12.rest_0_ = bf16[48,1024]{1,0:T(8,128)(2,1)S(1)} collective-permute-done((bf16[48,1024]{1,0:T(8,128)(2,1)S(1)}, bf16[48,1024]{1,0:T(8,128)(2,1)S(1)}, u32[]{:S(2)}, u32[]{:S(2)}) %collective-permute-start.12) | collective-permute-done | bytes 98336 | tf_op jit(solution)/shard_map/ppermute | solution.py:467
  60.6 4.9 %collective-permute-done.13.rest_1_ = bf16[48,1024]{1,0:T(8,128)(2,1)S(1)} collective-permute-done((bf16[48,1024]{1,0:T(8,128)(2,1)S(1)}, bf16[48,1024]{1,0:T(8,128)(2,1)S(1)}, u32[]{:S(2)}, u32[]{:S(2)}) %collective-permute-start.13) | collective-permute-done | bytes 98336 | tf_op jit(solution)/shard_map/ppermute | solution.py:467
  65.5 0.0 collective-permute-done.14.rest_2_
  65.6 0.1 collective-permute-start.15
  65.6 2.8 %collective-permute-start.16 = (bf16[48,1024]{1,0:T(8,128)(2,1)S(1)}, bf16[48,1024]{1,0:T(8,128)(2,1)S(1)}, u32[]{:S(2)}, u32[]{:S(2)}) collective-permute-start(bf16[48,1024]{1,0:T(8,128)(2,1)S(1)} %sum_terms.3.rest_0_), channel_id=1, source_target_pairs={{0,2},{1,3},{2,0},{3,1},{4,6},{5,7},{6,4},{7,5},{8,10},{9,11},{10,... | collective-permute-start | bytes 294920 | tf_op jit(solution)/shard_map/ppermute | solution.py:467
  68.5 1.5 %collective-permute-start.17 = (bf16[48,1024]{1,0:T(8,128)(2,1)S(1)}, bf16[48,1024]{1,0:T(8,128)(2,1)S(1)}, u32[]{:S(2)}, u32[]{:S(2)}) collective-permute-start(bf16[48,1024]{1,0:T(8,128)(2,1)S(1)} %sum_terms.3.rest_0_), channel_id=1, source_target_pairs={{0,3},{1,2},{2,1},{3,0},{4,7},{5,6},{6,5},{7,4},{8,11},{9,10},{10,... | collective-permute-start | bytes 294920 | tf_op jit(solution)/shard_map/ppermute | solution.py:467
  70.0 4.3 %write_cache.1 = bf16[48,2,256,128]{3,2,1,0:T(8,128)(2,1)} custom-call(s32[2]{0:T(128)S(1)} %pad_add_fusion.meta, s32[192]{0:T(256)S(1)} %copy-done.3, s32[1,192]{1,0:T(1,128)S(1)} %get-tuple-element.29.lengths_s, s32[12]{0:T(128)S(1)} %get-tuple-element.30.plan, f32[48,128]{1,0:T(8,128)S(1)} %get-tuple-element.41.newkey1, ...), custom_call_target="tpu_custom_call", output_to_operand_aliasing={{}: (12, {})} | custom-call | bytes 12582912 | tf_op jit(solution)/shard_map/write_cache/pallas_call | solution.py:609
  74.3 0.0 collective-permute-done.15.rest_1_
  74.3 2.1 %collective-permute-done.16.rest_2_ = bf16[48,1024]{1,0:T(8,128)(2,1)S(1)} collective-permute-done((bf16[48,1024]{1,0:T(8,128)(2,1)S(1)}, bf16[48,1024]{1,0:T(8,128)(2,1)S(1)}, u32[]{:S(2)}, u32[]{:S(2)}) %collective-permute-start.16) | collective-permute-done | bytes 98336 | tf_op jit(solution)/shard_map/ppermute | solution.py:467
  76.4 0.0 collective-permute-done.17.rest_3_
  76.4 1.3 %join.1 = bf16[48,4096]{1,0:T(8,128)(2,1)} custom-call(s32[2]{0:T(128)S(1)} %pad_add_fusion.meta, bf16[48,1024]{1,0:T(8,128)(2,1)S(1)} %sum_terms.3.rest_0_, bf16[48,1024]{1,0:T(8,128)(2,1)S(1)} %collective-permute-done.15.rest_1_, bf16[48,1024]{1,0:T(8,128)(2,1)S(1)} %collective-permute-done.16.rest_2_, bf16[48,1024]{1,0:T(8,128)(2,1)S(1)} %collective-permute-done.17.rest_3_), custom_call_target="tpu_custom_call" | custom-call | tf_op jit(solution)/shard_map/join/pallas_call | solution.py:626
  (2 shorter events, 0.0 us)
Async XLA Ops:
  0.6 7.7 %copy-start.2 = (bf16[4096,2,128]{2,1,0:T(2,128)(2,1)S(1)}, bf16[4096,2,128]{2,1,0:T(2,128)(2,1)}, u32[]{:S(2)}) copy-start(bf16[4096,2,128]{2,1,0:T(2,128)(2,1)} %param.15) | copy-start | bytes 6291460
  0.6 7.7 %copy-start.1 = (bf16[4096,512]{1,0:T(8,128)(2,1)S(1)}, bf16[4096,512]{1,0:T(8,128)(2,1)}, u32[]{:S(2)}) copy-start(bf16[4096,512]{1,0:T(8,128)(2,1)} %wq.3) | copy-start | bytes 12582916
  0.7 13.9 %slice-start = ((s8[6291456]{0:T(1024)(128)(4,1)}), s8[4194304]{0:T(1024)(128)(4,1)S(1)}, s32[]{:S(2)}) async-start(s8[6291456]{0:T(1024)(128)(4,1)} %bitcast.6), calls=%async_computation | async-start | bytes 8388608
  5.2 3.2 %collective-permute-start = (bf16[2,2,256,128]{3,2,1,0:T(8,128)(2,1)S(1)}, bf16[2,2,256,128]{3,2,1,0:T(8,128)(2,1)S(1)}, u32[]{:S(2)}, u32[]{:S(2)}) collective-permute-start(bf16[2,2,256,128]{3,2,1,0:T(8,128)(2,1)S(1)} %get-tuple-element.34), channel_id=1, source_target_pairs={{0,4},{4,0},{8,12},{12,8},{1,5},{5,1},{9,13},{13,9},{2,6},{6,2},{1... | collective-permute-start | bytes 786440 | tf_op jit(solution)/shard_map/ppermute | solution.py:467
  5.7 34.4 %collective-permute-start.10 = (bf16[2,2,256,128]{3,2,1,0:T(8,128)(2,1)S(1)}, bf16[2,2,256,128]{3,2,1,0:T(8,128)(2,1)S(1)}, u32[]{:S(2)}, u32[]{:S(2)}) collective-permute-start(bf16[2,2,256,128]{3,2,1,0:T(8,128)(2,1)S(1)} %get-tuple-element.47), channel_id=1, source_target_pairs={{0,8},{4,12},{8,0},{12,4},{1,9},{5,13},{9,1},{13,5},{2,10},{6,14},... | collective-permute-start | bytes 786440 | tf_op jit(solution)/shard_map/ppermute | solution.py:467
  8.3 31.9 %collective-permute-start.11 = (bf16[2,2,256,128]{3,2,1,0:T(8,128)(2,1)S(1)}, bf16[2,2,256,128]{3,2,1,0:T(8,128)(2,1)S(1)}, u32[]{:S(2)}, u32[]{:S(2)}) collective-permute-start(bf16[2,2,256,128]{3,2,1,0:T(8,128)(2,1)S(1)} %get-tuple-element.48), channel_id=1, source_target_pairs={{0,12},{4,8},{8,4},{12,0},{1,13},{5,9},{9,5},{13,1},{2,14},{6,10},... | collective-permute-start | bytes 786440 | tf_op jit(solution)/shard_map/ppermute | solution.py:467
  8.4 6.3 %slice-start.1 = ((s8[6291456]{0:T(1024)(128)(4,1)}), s8[2097152]{0:T(1024)(128)(4,1)S(1)}, s32[]{:S(2)}) async-start(s8[6291456]{0:T(1024)(128)(4,1)} %bitcast.6), calls=%async_computation.1 | async-start | bytes 4194304
  12.5 8.8 %copy-start = (bf16[512,4096]{1,0:T(8,128)(2,1)S(1)}, bf16[512,4096]{1,0:T(8,128)(2,1)}, u32[]{:S(2)}) copy-start(bf16[512,4096]{1,0:T(8,128)(2,1)} %wo.3) | copy-start | bytes 12582916
  12.5 6.7 %collective-permute-start.1 = (f32[2,1792]{1,0:T(2,128)S(1)}, f32[2,1792]{1,0:T(2,128)S(1)}, u32[]{:S(2)}, u32[]{:S(2)}) collective-permute-start(f32[2,1792]{1,0:T(2,128)S(1)} %get-tuple-element.38), channel_id=1, source_target_pairs={{0,4},{4,0},{8,12},{12,8},{1,5},{5,1},{9,13},{13,9},{2,6},{6,2},{1... | collective-permute-start | bytes 43016 | tf_op jit(solution)/shard_map/ppermute | solution.py:467
  12.7 8.6 %collective-permute-start.2 = (f32[2,1792]{1,0:T(2,128)S(1)}, f32[2,1792]{1,0:T(2,128)S(1)}, u32[]{:S(2)}, u32[]{:S(2)}) collective-permute-start(f32[2,1792]{1,0:T(2,128)S(1)} %get-tuple-element.39), channel_id=1, source_target_pairs={{0,8},{4,12},{8,0},{12,4},{1,9},{5,13},{9,1},{13,5},{2,10},{6,14},... | collective-permute-start | bytes 43016 | tf_op jit(solution)/shard_map/ppermute | solution.py:467
  14.6 6.6 %collective-permute-start.3 = (f32[2,1792]{1,0:T(2,128)S(1)}, f32[2,1792]{1,0:T(2,128)S(1)}, u32[]{:S(2)}, u32[]{:S(2)}) collective-permute-start(f32[2,1792]{1,0:T(2,128)S(1)} %get-tuple-element.40), channel_id=1, source_target_pairs={{0,12},{4,8},{8,4},{12,0},{1,13},{5,9},{9,5},{13,1},{2,14},{6,10},... | collective-permute-start | bytes 43016 | tf_op jit(solution)/shard_map/ppermute | solution.py:467
  19.2 27.3 %copy-start.3 = (s32[192]{0:T(256)S(1)}, s32[192]{0:T(256)}, u32[]{:S(2)}) copy-start(s32[192]{0:T(256)} %source_s.3) | copy-start | bytes 2308
  22.8 6.6 %collective-permute-start.4 = (bf16[48,1024]{1,0:T(8,128)(2,1)S(1)}, bf16[48,1024]{1,0:T(8,128)(2,1)S(1)}, u32[]{:S(2)}, u32[]{:S(2)}) collective-permute-start(bf16[48,1024]{1,0:T(8,128)(2,1)S(1)} %get-tuple-element.44), channel_id=1, source_target_pairs={{0,3},{1,2},{2,1},{3,0},{4,7},{5,6},{6,5},{7,4},{8,11},{9,10},{10,... | collective-permute-start | bytes 294920 | tf_op jit(solution)/shard_map/ppermute | solution.py:467
  26.7 8.9 %collective-permute-start.5 = (bf16[48,1024]{1,0:T(8,128)(2,1)S(1)}, bf16[48,1024]{1,0:T(8,128)(2,1)S(1)}, u32[]{:S(2)}, u32[]{:S(2)}) collective-permute-start(bf16[48,1024]{1,0:T(8,128)(2,1)S(1)} %get-tuple-element.45), channel_id=1, source_target_pairs={{0,2},{1,3},{2,0},{3,1},{4,6},{5,7},{6,4},{7,5},{8,10},{9,11},{10,... | collective-permute-start | bytes 294920 | tf_op jit(solution)/shard_map/ppermute | solution.py:467
  26.7 8.9 %collective-permute-start.6 = (bf16[48,1024]{1,0:T(8,128)(2,1)S(1)}, bf16[48,1024]{1,0:T(8,128)(2,1)S(1)}, u32[]{:S(2)}, u32[]{:S(2)}) collective-permute-start(bf16[48,1024]{1,0:T(8,128)(2,1)S(1)} %get-tuple-element.46), channel_id=1, source_target_pairs={{0,1},{1,0},{2,3},{3,2},{4,5},{5,4},{6,7},{7,6},{8,9},{9,8},{10,11... | collective-permute-start | bytes 294920 | tf_op jit(solution)/shard_map/ppermute | solution.py:467
  35.7 6.1 %collective-permute-start.7 = (bf16[48,1024]{1,0:T(8,128)(2,1)S(1)}, bf16[48,1024]{1,0:T(8,128)(2,1)S(1)}, u32[]{:S(2)}, u32[]{:S(2)}) collective-permute-start(bf16[48,1024]{1,0:T(8,128)(2,1)S(1)} %sum_terms.2.rest_0_), channel_id=1, source_target_pairs={{0,1},{1,0},{2,3},{3,2},{4,5},{5,4},{6,7},{7,6},{8,9},{9,8},{10,11... | collective-permute-start | bytes 294920 | tf_op jit(solution)/shard_map/ppermute | solution.py:467
  35.8 10.8 %collective-permute-start.8 = (bf16[48,1024]{1,0:T(8,128)(2,1)S(1)}, bf16[48,1024]{1,0:T(8,128)(2,1)S(1)}, u32[]{:S(2)}, u32[]{:S(2)}) collective-permute-start(bf16[48,1024]{1,0:T(8,128)(2,1)S(1)} %sum_terms.2.rest_0_), channel_id=1, source_target_pairs={{0,2},{1,3},{2,0},{3,1},{4,6},{5,7},{6,4},{7,5},{8,10},{9,11},{10,... | collective-permute-start | bytes 294920 | tf_op jit(solution)/shard_map/ppermute | solution.py:467
  36.7 9.8 %collective-permute-start.9 = (bf16[48,1024]{1,0:T(8,128)(2,1)S(1)}, bf16[48,1024]{1,0:T(8,128)(2,1)S(1)}, u32[]{:S(2)}, u32[]{:S(2)}) collective-permute-start(bf16[48,1024]{1,0:T(8,128)(2,1)S(1)} %sum_terms.2.rest_0_), channel_id=1, source_target_pairs={{0,3},{1,2},{2,1},{3,0},{4,7},{5,6},{6,5},{7,4},{8,11},{9,10},{10,... | collective-permute-start | bytes 294920 | tf_op jit(solution)/shard_map/ppermute | solution.py:467
  53.3 7.3 %collective-permute-start.12 = (bf16[48,1024]{1,0:T(8,128)(2,1)S(1)}, bf16[48,1024]{1,0:T(8,128)(2,1)S(1)}, u32[]{:S(2)}, u32[]{:S(2)}) collective-permute-start(bf16[48,1024]{1,0:T(8,128)(2,1)S(1)} %get-tuple-element.50), channel_id=1, source_target_pairs={{0,3},{1,2},{2,1},{3,0},{4,7},{5,6},{6,5},{7,4},{8,11},{9,10},{10,... | collective-permute-start | bytes 294920 | tf_op jit(solution)/shard_map/ppermute | solution.py:467
  54.4 11.1 %collective-permute-start.13 = (bf16[48,1024]{1,0:T(8,128)(2,1)S(1)}, bf16[48,1024]{1,0:T(8,128)(2,1)S(1)}, u32[]{:S(2)}, u32[]{:S(2)}) collective-permute-start(bf16[48,1024]{1,0:T(8,128)(2,1)S(1)} %get-tuple-element.51), channel_id=1, source_target_pairs={{0,2},{1,3},{2,0},{3,1},{4,6},{5,7},{6,4},{7,5},{8,10},{9,11},{10,... | collective-permute-start | bytes 294920 | tf_op jit(solution)/shard_map/ppermute | solution.py:467
  57.1 8.4 %collective-permute-start.14 = (bf16[48,1024]{1,0:T(8,128)(2,1)S(1)}, bf16[48,1024]{1,0:T(8,128)(2,1)S(1)}, u32[]{:S(2)}, u32[]{:S(2)}) collective-permute-start(bf16[48,1024]{1,0:T(8,128)(2,1)S(1)} %get-tuple-element.52), channel_id=1, source_target_pairs={{0,1},{1,0},{2,3},{3,2},{4,5},{5,4},{6,7},{7,6},{8,9},{9,8},{10,11... | collective-permute-start | bytes 294920 | tf_op jit(solution)/shard_map/ppermute | solution.py:467
  65.6 8.7 %collective-permute-start.15 = (bf16[48,1024]{1,0:T(8,128)(2,1)S(1)}, bf16[48,1024]{1,0:T(8,128)(2,1)S(1)}, u32[]{:S(2)}, u32[]{:S(2)}) collective-permute-start(bf16[48,1024]{1,0:T(8,128)(2,1)S(1)} %sum_terms.3.rest_0_), channel_id=1, source_target_pairs={{0,1},{1,0},{2,3},{3,2},{4,5},{5,4},{6,7},{7,6},{8,9},{9,8},{10,11... | collective-permute-start | bytes 294920 | tf_op jit(solution)/shard_map/ppermute | solution.py:467
  65.6 10.7 %collective-permute-start.16 = (bf16[48,1024]{1,0:T(8,128)(2,1)S(1)}, bf16[48,1024]{1,0:T(8,128)(2,1)S(1)}, u32[]{:S(2)}, u32[]{:S(2)}) collective-permute-start(bf16[48,1024]{1,0:T(8,128)(2,1)S(1)} %sum_terms.3.rest_0_), channel_id=1, source_target_pairs={{0,2},{1,3},{2,0},{3,1},{4,6},{5,7},{6,4},{7,5},{8,10},{9,11},{10,... | collective-permute-start | bytes 294920 | tf_op jit(solution)/shard_map/ppermute | solution.py:467
  68.5 7.9 %collective-permute-start.17 = (bf16[48,1024]{1,0:T(8,128)(2,1)S(1)}, bf16[48,1024]{1,0:T(8,128)(2,1)S(1)}, u32[]{:S(2)}, u32[]{:S(2)}) collective-permute-start(bf16[48,1024]{1,0:T(8,128)(2,1)S(1)} %sum_terms.3.rest_0_), channel_id=1, source_target_pairs={{0,3},{1,2},{2,1},{3,0},{4,7},{5,6},{6,5},{7,4},{8,11},{9,10},{10,... | collective-permute-start | bytes 294920 | tf_op jit(solution)/shard_map/ppermute | solution.py:467

commit v7 on v4

--- a/solution.py
+++ b/solution.py
@@ -390,7 +390,7 @@
     meta, source_s, lengths_s, plan, gain, cos_ref, sin_ref, newkey1, newvalue1,
     wq, wkv, wo, cache_hbm, *rest,
 ):
-    blocks, rest = rest[:peers_tp], rest[peers_tp:]
+    blocks, rest = rest[0], rest[1:]
     box_hbm, rest = rest[: peers - 1], rest[peers - 1 :]
     newkey, newvalue, own = rest[:3]
     sends, rest = rest[3 : 2 + peers_tp], rest[2 + peers_tp :]
@@ -405,12 +405,11 @@
         copy.start()
 
     map_places(slots, peers, plan, place)
-    firsts = [jnp.bitwise_xor(me_tp, k) for k in range(peers_tp)]
     norm_into(
         normed3,
-        [block[...].astype(F32) for block in blocks],
-        [gain[:, pl.ds(pl.multiple_of(first * shard, shard), shard)] for first in firsts],
-        [first * (shard // HD) for first in firsts],
+        [blocks[k].astype(F32) for k in range(peers_tp)],
+        [gain[:, k * shard : (k + 1) * shard] for k in range(peers_tp)],
+        [k * (shard // HD) for k in range(peers_tp)],
         width,
     )
     spread_normed(normed3, spread, slots, width)
@@ -443,7 +442,7 @@
     attended = jnp.concatenate(
         [attended_rows[pl.ds(g, slots, stride=GROUP), :].astype(BF16) for g in range(heads)], axis=1
     )
-    project_out(attended, wo, blocks[0][...].astype(F32), own, sends, me_tp, peers_tp)
+    project_out(attended, wo, blocks[me_tp].astype(F32), own, sends, me_tp, peers_tp)
 
 
 def cache_kernel(
@@ -473,18 +472,6 @@
             copy.start()
             outs.append(copy)
     for copy in outs:
-        copy.wait()
-
-
-def join_kernel(peers_tp, meta, *rest):
-    blocks, out, sem = rest[:-2], rest[-2], rest[-1]
-    shard = blocks[0].shape[1]
-    copies = []
-    for k, block in enumerate(blocks):
-        column = pl.multiple_of(jnp.bitwise_xor(meta[1], k) * shard, shard)
-        copies.append(pltpu.make_async_copy(block, out.at[:, pl.ds(column, shard)], sem.at[k]))
-        copies[-1].start()
-    for copy in copies:
         copy.wait()
 
 
@@ -601,7 +588,7 @@
     sends, boxes = rest[: peers_tp - 1], rest[peers_tp - 1 :]
     got_boxes = got_notes[:1] + [swapped(box, "inst", peers, k + 2) for k, box in enumerate(boxes)]
 
-    def summed(own, sends):
+    def summed(own, sends, **gather):
         got = [swapped(sends[k - 1], "tp", peers_tp, k) for k in range(peers_tp - 1, 0, -1)]
         shard_rows = pl.pallas_call(
             sum_kernel,
@@ -611,16 +598,14 @@
             compiler_params=params(16),
             name="sum_terms",
         )(own, *got)
-        return [shard_rows] + [
-            swapped(shard_rows, "tp", peers_tp, k) for k in range(1, peers_tp)
-        ]
+        return lax.all_gather(shard_rows, "tp", **gather)
 
     pieces = summed(own, sends)
 
     newkey2, newvalue2, own, *sends = pl.pallas_call(
         functools.partial(second_kernel, peers, peers_tp, slots, heads),
         out_shape=[row32, row32] + sent,
-        in_specs=[SMEM] * 4 + [VMEM] * 8 + [ANY] + [VMEM] * peers_tp + [ANY] * others,
+        in_specs=[SMEM] * 4 + [VMEM] * 8 + [ANY, VMEM] + [ANY] * others,
         out_specs=[VMEM] * (2 + peers_tp),
         scratch_shapes=stages
         + [
@@ -634,9 +619,9 @@
         cost_estimate=cost(3 * flops, cache_bytes + (query_weight.size + wkv.size) * 4),
         name="second_step",
     )(meta, source, lengths, plan, gain, cosine, sine, newkey1, newvalue1, query_weight, wkv,
-      out_weight, kv_cache, *pieces, *got_boxes)
-
-    pieces = summed(own, sends)
+      out_weight, kv_cache, pieces, *got_boxes)
+
+    final_hidden = summed(own, sends, axis=1, tiled=True)
     final_cache = pl.pallas_call(
         functools.partial(cache_kernel, peers, slots),
         out_shape=jax.ShapeDtypeStruct(kv_cache.shape, BF16),
@@ -652,15 +637,6 @@
         cost_estimate=cost(0, 2 * cache_bytes),
         name="write_cache",
     )(meta, source, lengths, plan, newkey1, newvalue1, newkey2, newvalue2, kv_cache, *got_boxes)
-    final_hidden = pl.pallas_call(
-        functools.partial(join_kernel, peers_tp),
-        out_shape=jax.ShapeDtypeStruct(hidden.shape, BF16),
-        in_specs=[SMEM] + [ANY] * peers_tp,
-        out_specs=ANY,
-        scratch_shapes=[dma((peers_tp,))],
-        compiler_params=params(16),
-        name="join",
-    )(meta, *pieces)
     return (final_hidden, final_cache)
 
 

time: 73.9 us -> 79.1 us (1.070)
  blocking collectives: 0 us -> 28.7 us
  waiting for transfers between devices: 23 us -> 9.17 us
  starting transfers between devices: 22.8 us -> 13.9 us
  Pallas kernels: 26.9 us -> 25.5 us
    all_gather x0 -> x2, blocking collectives: none -> 28.7 us  [summed(): return lax.all_gather(shard_rows, 'tp', **gather)]
    ppermute x17 -> x11, waiting for transfers between devices: 23 us -> 9.17 us  [swapped(): return lax.ppermute(x, axis, [(i, i ^ k) for i in range(size)])]
    ppermute x17 -> x11, starting transfers between devices: 22.8 us -> 13.9 us  [swapped(): return lax.ppermute(x, axis, [(i, i ^ k) for i in range(size)])]
    pallas_call x1 -> x0, Pallas kernels: 1.32 us -> none  [local(): pl.pallas_call(functools.partial(join_kernel, peers_tp), out_shape=jax.Sh...]
  transfers between devices with their start and end apart: 17 -> 11, of which waited for: 7 -> 3; matrix products, arithmetic and copies ran while one was open for 0% -> 0% of each run, Pallas kernels for 12% -> 11%
where the time goes in v7:
time: 79.1 us; the launch traced here: 79 us
  blocking collectives  28.7 us (36%)
  Pallas kernels  25.5 us (32%)
  starting transfers between devices  13.9 us (18%)
  waiting for transfers between devices  9.17 us (12%)
  between operations  0.85 us (1%)
  local copies, waits for them, and re-layouts  0.81 us (1%)
    all_gather x2, blocking collectives, summed(): return lax.all_gather(shard_rows, 'tp', **gather)  28.7 us
    ppermute x11, starting transfers between devices, swapped(): return lax.ppermute(x, axis, [(i, i ^ k) for i in range(size)])  13.9 us
    ppermute x11, waiting for transfers between devices, swapped(): return lax.ppermute(x, axis, [(i, i ^ k) for i in range(size)])  9.17 us
    pallas_call x1, Pallas kernels, local(): pl.pallas_call(functools.partial(first_kernel, peers, slots, heads, shard...  7.51 us
    pallas_call x1, Pallas kernels, local(): pl.pallas_call(functools.partial(second_kernel, peers, peers_tp, slots, h...  6.78 us
    pallas_call x1, Pallas kernels, local(): pl.pallas_call(functools.partial(attend_kernel, slots, heads), out_shape=...  4.56 us
    pallas_call x1, Pallas kernels, local(): pl.pallas_call(functools.partial(cache_kernel, peers, slots), out_shape=j...  4.23 us
    pallas_call x1, Pallas kernels, local(): pl.pallas_call(functools.partial(out_kernel, peers, peers_tp, slots), out...  2.34 us
  transfers between devices with their start and end apart: 11, of which 3 were waited for; matrix products, arithmetic and copies ran while one was open for 0% of the time, Pallas kernels for 11%

profile of v7, /device:TPU:0, one launch (start us, length us, event | category | flops | bytes accessed | tf_op | source)
XLA Modules:
  0.0 79.0 jit_solution(5198955539858149026)
XLA Ops:
  0.6 0.1 pad_add_fusion.meta
  0.7 0.0 slice-start
  0.7 0.0 slice-start.1
  0.7 0.0 copy-start.7
  0.7 7.5 %first_step.1 = (f32[384,128]{1,0:T(8,128)S(1)}, f32[48,128]{1,0:T(8,128)S(1)}, f32[48,128]{1,0:T(8,128)S(1)}, s32[12]{0:T(128)S(1)}, bf16[2,2,272,128]{3,2,1,0:...) custom-call(s32[2]{0:T(128)S(1)} %pad_add_fusion.meta, s32[1,192]{1,0:T(1,128)} %bitcast.15, ...), custom_call_target="tpu_custom_call" | custom-call | flops 301989888 | bytes 6291456 | tf_op jit(solution)/shard_map/first_step/pallas_call | solution.py:512
  8.2 0.0 copy-start.1
  8.2 0.0 copy-start.3
  8.3 0.5 collective-permute-start
  8.8 2.6 %collective-permute-start.1 = (f32[2,1536]{1,0:T(2,128)S(1)}, f32[2,1536]{1,0:T(2,128)S(1)}, u32[]{:S(2)}, u32[]{:S(2)}) collective-permute-start(f32[2,1536]{1,0:T(2,128)S(1)} %get-tuple-element.26), channel_id=1, source_target_pairs={{0,8},{4,12},{8,0},{12,4},{1,9},{5,13},{9,1},{13,5},{2,10},{6,14},... | collective-permute-start | bytes 36872 | tf_op jit(solution)/shard_map/ppermute | solution.py:479
  11.4 0.1 collective-permute-start.2
  11.4 0.0 slice-done
  11.4 0.0 slice-done.1
  11.4 0.0 copy-done.7
  11.4 4.6 %attention.1.attended = bf16[48,512]{1,0:T(8,128)(2,1)S(1)} custom-call(s32[2]{0:T(128)S(1)} %pad_add_fusion.meta, s32[192]{0:T(256)S(1)} %copy-done.7, f32[384,128]{1,0:T(8,128)S(1)} %get-tuple-element.24.query, f32[48,128]{1,0:T(8,128)S(1)} %get-tuple-element.22.newkey.newkey1, f32[48,128]{1,0:T(8,128)S(1)} %get-tuple-element.23.newvalue.newvalue1, ...), custom_call_target="tpu_custom_call" | custom-call | flops 25165824 | bytes 6291456 | tf_op jit(solution)/shard_map/attention/pallas_call | solution.py:553
  16.0 0.0 collective-permute-done.1.rest_0_
  16.0 0.0 collective-permute-done.2.rest_1_
  16.0 0.0 collective-permute-done.box_hbm.rest_1_.rest_0_
  16.0 0.0 copy-done.1
  16.0 0.0 copy-done.3
  16.1 0.0 copy-start
  16.1 0.0 copy-start.2
  16.1 0.0 copy-start.4
  16.1 0.0 copy-start.5
  16.1 0.0 copy-start.6
  16.1 0.0 copy-start.8
  16.1 2.3 %out_projection.1 = (f32[48,1024]{1,0:T(8,128)S(1)}, bf16[48,1024]{1,0:T(8,128)(2,1)S(1)}, bf16[48,1024]{1,0:T(8,128)(2,1)S(1)}, bf16[48,1024]{1,0:T(8,128)(2,1)...) custom-call(s32[2]{0:T(128)S(1)} %pad_add_fusion.meta, s32[192]{0:T(256)S(1)} %copy-done.7, ...), custom_call_target="tpu_custom_call" | custom-call | flops 201326592 | bytes 4194304 | tf_op jit(solution)/shard_map/out_projection/pallas_call | solution.py:570
  18.5 1.8 %collective-permute-start.6 = (bf16[2,2,256,128]{3,2,1,0:T(8,128)(2,1)S(1)}, bf16[2,2,256,128]{3,2,1,0:T(8,128)(2,1)S(1)}, u32[]{:S(2)}, u32[]{:S(2)}) collective-permute-start(bf16[2,2,256,128]{3,2,1,0:T(8,128)(2,1)S(1)} %get-tuple-element.32), channel_id=1, source_target_pairs={{0,8},{4,12},{8,0},{12,4},{1,9},{5,13},{9,1},{13,5},{2,10},{6,14},... | collective-permute-start | bytes 786440 | tf_op jit(solution)/shard_map/ppermute | solution.py:479
  20.3 0.0 collective-permute-start.7
  20.3 3.7 %collective-permute-start.3 = (bf16[48,1024]{1,0:T(8,128)(2,1)S(1)}, bf16[48,1024]{1,0:T(8,128)(2,1)S(1)}, u32[]{:S(2)}, u32[]{:S(2)}) collective-permute-start(bf16[48,1024]{1,0:T(8,128)(2,1)S(1)} %get-tuple-element.29), channel_id=1, source_target_pairs={{0,3},{1,2},{2,1},{3,0},{4,7},{5,6},{6,5},{7,4},{8,11},{9,10},{10,... | collective-permute-start | bytes 294920 | tf_op jit(solution)/shard_map/ppermute | solution.py:479
  24.1 0.0 collective-permute-start.4
  24.1 0.7 collective-permute-start.5
  24.7 3.2 %collective-permute-done.3.rest_0_ = bf16[48,1024]{1,0:T(8,128)(2,1)S(1)} collective-permute-done((bf16[48,1024]{1,0:T(8,128)(2,1)S(1)}, bf16[48,1024]{1,0:T(8,128)(2,1)S(1)}, u32[]{:S(2)}, u32[]{:S(2)}) %collective-permute-start.3) | collective-permute-done | bytes 98336 | tf_op jit(solution)/shard_map/ppermute | solution.py:479
  27.9 5.0 %collective-permute-done.4.rest_1_ = bf16[48,1024]{1,0:T(8,128)(2,1)S(1)} collective-permute-done((bf16[48,1024]{1,0:T(8,128)(2,1)S(1)}, bf16[48,1024]{1,0:T(8,128)(2,1)S(1)}, u32[]{:S(2)}, u32[]{:S(2)}) %collective-permute-start.4) | collective-permute-done | bytes 98336 | tf_op jit(solution)/shard_map/ppermute | solution.py:479
  32.9 0.0 collective-permute-done.5.rest_2_
  32.9 0.1 sum_terms.2
  33.0 14.3 %all-gather = bf16[192,1024]{1,0:T(8,128)(2,1)S(1)} all-gather(bf16[48,1024]{1,0:T(8,128)(2,1)S(1)} %sum_terms.2), channel_id=2, replica_groups=mesh['groups'=2,'inst'=4,'tp'=4] {'tp'}, dimensions={0}, use_global_device_ids=true | all-gather | bytes 491520 | tf_op jit(solution)/shard_map/all_gather | solution.py:601
  47.3 0.0 collective-permute-done.6.rest_2_.rest_1_
  47.3 0.0 collective-permute-done.7.rest_3_.rest_2_
  47.3 0.0 copy-done
  47.3 0.0 copy-done.2
  47.4 0.0 copy-done.4
  47.4 0.0 copy-done.5
  47.4 0.0 copy-done.6
  47.4 0.0 copy-done.8
  47.4 6.8 %second_step.1 = (f32[48,128]{1,0:T(8,128)S(1)}, f32[48,128]{1,0:T(8,128)S(1)}, f32[48,1024]{1,0:T(8,128)S(1)}, bf16[48,1024]{1,0:T(8,128)(2,1)S(1)}, bf16[48,10...) custom-call(s32[2]{0:T(128)S(1)} %pad_add_fusion.meta, s32[192]{0:T(256)S(1)} %copy-done.8, s32[192]{0:T(256)S(1)} %copy-done.7, ...), custom_call_target="tpu_custom_call" | custom-call | flops 905969664 | bytes 18874368 | tf_op jit(solution)/shard_map/second_step/pallas_call | solution.py:605
  54.2 3.3 %collective-permute-start.8 = (bf16[48,1024]{1,0:T(8,128)(2,1)S(1)}, bf16[48,1024]{1,0:T(8,128)(2,1)S(1)}, u32[]{:S(2)}, u32[]{:S(2)}) collective-permute-start(bf16[48,1024]{1,0:T(8,128)(2,1)S(1)} %get-tuple-element.35), channel_id=1, source_target_pairs={{0,3},{1,2},{2,1},{3,0},{4,7},{5,6},{6,5},{7,4},{8,11},{9,10},{10,... | collective-permute-start | bytes 294920 | tf_op jit(solution)/shard_map/ppermute | solution.py:479
  57.5 0.0 collective-permute-start.9
  57.5 1.1 %collective-permute-start.10 = (bf16[48,1024]{1,0:T(8,128)(2,1)S(1)}, bf16[48,1024]{1,0:T(8,128)(2,1)S(1)}, u32[]{:S(2)}, u32[]{:S(2)}) collective-permute-start(bf16[48,1024]{1,0:T(8,128)(2,1)S(1)} %get-tuple-element.37), channel_id=1, source_target_pairs={{0,1},{1,0},{2,3},{3,2},{4,5},{5,4},{6,7},{7,6},{8,9},{9,8},{10,11... | collective-permute-start | bytes 294920 | tf_op jit(solution)/shard_map/ppermute | solution.py:479
  58.6 4.2 %write_cache.1 = bf16[48,2,256,128]{3,2,1,0:T(8,128)(2,1)} custom-call(s32[2]{0:T(128)S(1)} %pad_add_fusion.meta, s32[192]{0:T(256)S(1)} %copy-done.8, s32[192]{0:T(256)S(1)} %copy-done.7, s32[12]{0:T(128)S(1)} %get-tuple-element.21.plan, f32[48,128]{1,0:T(8,128)S(1)} %get-tuple-element.22.newkey.newkey1, ...), custom_call_target="tpu_custom_call" | custom-call | bytes 12582912 | tf_op jit(solution)/shard_map/write_cache/pallas_call | solution.py:625
  62.9 0.0 collective-permute-done.8.rest_0_
  62.9 0.9 %collective-permute-done.9.rest_1_ = bf16[48,1024]{1,0:T(8,128)(2,1)S(1)} collective-permute-done((bf16[48,1024]{1,0:T(8,128)(2,1)S(1)}, bf16[48,1024]{1,0:T(8,128)(2,1)S(1)}, u32[]{:S(2)}, u32[]{:S(2)}) %collective-permute-start.9) | collective-permute-done | bytes 98336 | tf_op jit(solution)/shard_map/ppermute | solution.py:479
  63.8 0.0 collective-permute-done.10.rest_2_
  63.8 0.1 sum_terms.3
  63.9 14.3 %all_gather.11 = bf16[48,4096]{1,0:T(8,128)(2,1)S(1)} all-gather(bf16[48,1024]{1,0:T(8,128)(2,1)S(1)} %sum_terms.3), channel_id=1, replica_groups=mesh['groups'=2,'inst'=4,'tp'=4] {'tp'}, dimensions={1}, use_global_device_ids=true | all-gather | bytes 491520 | tf_op jit(solution)/shard_map/all_gather | solution.py:601
  78.2 0.7 copy.13
  (1 shorter events, 0.0 us)
Async XLA Ops:
  0.7 10.7 %slice-start = ((s8[6291456]{0:T(1024)(128)(4,1)}), s8[4194304]{0:T(1024)(128)(4,1)S(1)}, s32[]{:S(2)}) async-start(s8[6291456]{0:T(1024)(128)(4,1)} %bitcast.7), calls=%async_computation | async-start | bytes 8388608
  0.7 10.7 %slice-start.1 = ((s8[6291456]{0:T(1024)(128)(4,1)}), s8[2097152]{0:T(1024)(128)(4,1)S(1)}, s32[]{:S(2)}) async-start(s8[6291456]{0:T(1024)(128)(4,1)} %bitcast.7), calls=%async_computation.1 | async-start | bytes 4194304
  0.7 10.7 %copy-start.7 = (s32[192]{0:T(256)S(1)}, s32[192]{0:T(256)}, u32[]{:S(2)}) copy-start(s32[192]{0:T(256)} %lengths_s.7) | copy-start | bytes 2308
  8.2 7.8 %copy-start.1 = (bf16[512,4096]{1,0:T(8,128)(2,1)S(1)}, bf16[512,4096]{1,0:T(8,128)(2,1)}, u32[]{:S(2)}) copy-start(bf16[512,4096]{1,0:T(8,128)(2,1)} %wo.3) | copy-start | bytes 12582916
  8.2 7.8 %copy-start.3 = (bf16[48,4096]{1,0:T(8,128)(2,1)S(1)}, bf16[48,4096]{1,0:T(8,128)(2,1)}, u32[]{:S(2)}) copy-start(bf16[48,4096]{1,0:T(8,128)(2,1)} %hidden.1) | copy-start | bytes 1179652
  8.3 7.8 %collective-permute-start = (bf16[2,2,272,128]{3,2,1,0:T(8,128)(2,1)S(1)}, bf16[2,2,272,128]{3,2,1,0:T(8,128)(2,1)S(1)}, u32[]{:S(2)}, u32[]{:S(2)}) collective-permute-start(bf16[2,2,272,128]{3,2,1,0:T(8,128)(2,1)S(1)} %get-tuple-element.25), channel_id=1, source_target_pairs={{0,4},{4,0},{8,12},{12,8},{1,5},{5,1},{9,13},{13,9},{2,6},{6,2},{1... | collective-permute-start | bytes 835592 | tf_op jit(solution)/shard_map/ppermute | solution.py:479
  8.8 7.2 %collective-permute-start.1 = (f32[2,1536]{1,0:T(2,128)S(1)}, f32[2,1536]{1,0:T(2,128)S(1)}, u32[]{:S(2)}, u32[]{:S(2)}) collective-permute-start(f32[2,1536]{1,0:T(2,128)S(1)} %get-tuple-element.26), channel_id=1, source_target_pairs={{0,8},{4,12},{8,0},{12,4},{1,9},{5,13},{9,1},{13,5},{2,10},{6,14},... | collective-permute-start | bytes 36872 | tf_op jit(solution)/shard_map/ppermute | solution.py:479
  11.4 4.7 %collective-permute-start.2 = (f32[2,1536]{1,0:T(2,128)S(1)}, f32[2,1536]{1,0:T(2,128)S(1)}, u32[]{:S(2)}, u32[]{:S(2)}) collective-permute-start(f32[2,1536]{1,0:T(2,128)S(1)} %get-tuple-element.27), channel_id=1, source_target_pairs={{0,12},{4,8},{8,4},{12,0},{1,13},{5,9},{9,5},{13,1},{2,14},{6,10},... | collective-permute-start | bytes 36872 | tf_op jit(solution)/shard_map/ppermute | solution.py:479
  16.1 31.3 %copy-start = (bf16[4096,512]{1,0:T(8,128)(2,1)S(1)}, bf16[4096,512]{1,0:T(8,128)(2,1)}, u32[]{:S(2)}) copy-start(bf16[4096,512]{1,0:T(8,128)(2,1)} %wq.1) | copy-start | bytes 12582916
  16.1 31.3 %copy-start.2 = (bf16[4096,2,128]{2,1,0:T(2,128)(2,1)S(1)}, bf16[4096,2,128]{2,1,0:T(2,128)(2,1)}, u32[]{:S(2)}) copy-start(bf16[4096,2,128]{2,1,0:T(2,128)(2,1)} %param.16) | copy-start | bytes 6291460
  16.1 31.3 %copy-start.4 = (f32[256,128]{1,0:T(8,128)S(1)}, f32[256,128]{1,0:T(8,128)}, u32[]{:S(2)}) copy-start(f32[256,128]{1,0:T(8,128)} %constant.12.clone.sin_hbm.sin_ref) | copy-start | bytes 393220
  16.1 31.3 %copy-start.5 = (f32[256,128]{1,0:T(8,128)S(1)}, f32[256,128]{1,0:T(8,128)}, u32[]{:S(2)}) copy-start(f32[256,128]{1,0:T(8,128)} %constant.11.clone.cos_hbm.cos_ref) | copy-start | bytes 393220
  16.1 31.3 %copy-start.6 = (f32[4096]{0:T(1024)S(1)}, f32[4096]{0:T(1024)}, u32[]{:S(2)}) copy-start(f32[4096]{0:T(1024)} %param.14) | copy-start | bytes 49156
  16.1 31.3 %copy-start.8 = (s32[192]{0:T(256)S(1)}, s32[192]{0:T(256)}, u32[]{:S(2)}) copy-start(s32[192]{0:T(256)} %source_s.3) | copy-start | bytes 2308
  18.5 28.9 %collective-permute-start.6 = (bf16[2,2,256,128]{3,2,1,0:T(8,128)(2,1)S(1)}, bf16[2,2,256,128]{3,2,1,0:T(8,128)(2,1)S(1)}, u32[]{:S(2)}, u32[]{:S(2)}) collective-permute-start(bf16[2,2,256,128]{3,2,1,0:T(8,128)(2,1)S(1)} %get-tuple-element.32), channel_id=1, source_target_pairs={{0,8},{4,12},{8,0},{12,4},{1,9},{5,13},{9,1},{13,5},{2,10},{6,14},... | collective-permute-start | bytes 786440 | tf_op jit(solution)/shard_map/ppermute | solution.py:479
  20.3 27.1 %collective-permute-start.7 = (bf16[2,2,256,128]{3,2,1,0:T(8,128)(2,1)S(1)}, bf16[2,2,256,128]{3,2,1,0:T(8,128)(2,1)S(1)}, u32[]{:S(2)}, u32[]{:S(2)}) collective-permute-start(bf16[2,2,256,128]{3,2,1,0:T(8,128)(2,1)S(1)} %get-tuple-element.33), channel_id=1, source_target_pairs={{0,12},{4,8},{8,4},{12,0},{1,13},{5,9},{9,5},{13,1},{2,14},{6,10},... | collective-permute-start | bytes 786440 | tf_op jit(solution)/shard_map/ppermute | solution.py:479
  20.3 7.6 %collective-permute-start.3 = (bf16[48,1024]{1,0:T(8,128)(2,1)S(1)}, bf16[48,1024]{1,0:T(8,128)(2,1)S(1)}, u32[]{:S(2)}, u32[]{:S(2)}) collective-permute-start(bf16[48,1024]{1,0:T(8,128)(2,1)S(1)} %get-tuple-element.29), channel_id=1, source_target_pairs={{0,3},{1,2},{2,1},{3,0},{4,7},{5,6},{6,5},{7,4},{8,11},{9,10},{10,... | collective-permute-start | bytes 294920 | tf_op jit(solution)/shard_map/ppermute | solution.py:479
  24.1 8.9 %collective-permute-start.4 = (bf16[48,1024]{1,0:T(8,128)(2,1)S(1)}, bf16[48,1024]{1,0:T(8,128)(2,1)S(1)}, u32[]{:S(2)}, u32[]{:S(2)}) collective-permute-start(bf16[48,1024]{1,0:T(8,128)(2,1)S(1)} %get-tuple-element.30), channel_id=1, source_target_pairs={{0,2},{1,3},{2,0},{3,1},{4,6},{5,7},{6,4},{7,5},{8,10},{9,11},{10,... | collective-permute-start | bytes 294920 | tf_op jit(solution)/shard_map/ppermute | solution.py:479
  24.1 8.9 %collective-permute-start.5 = (bf16[48,1024]{1,0:T(8,128)(2,1)S(1)}, bf16[48,1024]{1,0:T(8,128)(2,1)S(1)}, u32[]{:S(2)}, u32[]{:S(2)}) collective-permute-start(bf16[48,1024]{1,0:T(8,128)(2,1)S(1)} %get-tuple-element.31), channel_id=1, source_target_pairs={{0,1},{1,0},{2,3},{3,2},{4,5},{5,4},{6,7},{7,6},{8,9},{9,8},{10,11... | collective-permute-start | bytes 294920 | tf_op jit(solution)/shard_map/ppermute | solution.py:479
  54.2 8.7 %collective-permute-start.8 = (bf16[48,1024]{1,0:T(8,128)(2,1)S(1)}, bf16[48,1024]{1,0:T(8,128)(2,1)S(1)}, u32[]{:S(2)}, u32[]{:S(2)}) collective-permute-start(bf16[48,1024]{1,0:T(8,128)(2,1)S(1)} %get-tuple-element.35), channel_id=1, source_target_pairs={{0,3},{1,2},{2,1},{3,0},{4,7},{5,6},{6,5},{7,4},{8,11},{9,10},{10,... | collective-permute-start | bytes 294920 | tf_op jit(solution)/shard_map/ppermute | solution.py:479
  57.5 6.3 %collective-permute-start.9 = (bf16[48,1024]{1,0:T(8,128)(2,1)S(1)}, bf16[48,1024]{1,0:T(8,128)(2,1)S(1)}, u32[]{:S(2)}, u32[]{:S(2)}) collective-permute-start(bf16[48,1024]{1,0:T(8,128)(2,1)S(1)} %get-tuple-element.36), channel_id=1, source_target_pairs={{0,2},{1,3},{2,0},{3,1},{4,6},{5,7},{6,4},{7,5},{8,10},{9,11},{10,... | collective-permute-start | bytes 294920 | tf_op jit(solution)/shard_map/ppermute | solution.py:479
  57.5 6.3 %collective-permute-start.10 = (bf16[48,1024]{1,0:T(8,128)(2,1)S(1)}, bf16[48,1024]{1,0:T(8,128)(2,1)S(1)}, u32[]{:S(2)}, u32[]{:S(2)}) collective-permute-start(bf16[48,1024]{1,0:T(8,128)(2,1)S(1)} %get-tuple-element.37), channel_id=1, source_target_pairs={{0,1},{1,0},{2,3},{3,2},{4,5},{5,4},{6,7},{7,6},{8,9},{9,8},{10,11... | collective-permute-start | bytes 294920 | tf_op jit(solution)/shard_map/ppermute | solution.py:479

commit v8 on v4

--- a/solution.py
+++ b/solution.py
@@ -298,20 +298,10 @@
 
 
 def out_kernel(
-    peers, peers_tp, slots, meta, lengths_s, plan, attended, wo, hidden, newkey, newvalue, box_hbm,
-    cache_hbm, *rest,
+    peers, peers_tp, meta, plan, attended, wo, hidden, box_hbm, *rest,
 ):
     notes, rest = rest[: peers - 2], rest[peers - 2 :]
-    own, sends, boxes = rest[0], rest[1:peers_tp], rest[peers_tp : peers_tp + peers - 2]
-    leaving, tail, sem, in_sem, out_sem = rest[peers_tp + peers - 2 :]
-    moving = (peers - 1) * MOVE
-    send_slots = [plan[moving + at] for at in range(MOVE, moving)]
-    packs = [
-        pltpu.make_async_copy(cache_hbm.at[slot], leaving.at[i], in_sem.at[i])
-        for i, slot in enumerate(send_slots)
-    ]
-    for pack in packs:
-        pack.start()
+    own, sends, (tail, sem) = rest[0], rest[1:peers_tp], rest[peers_tp:]
     shard = own.shape[1]
     cap = box_hbm.shape[2] - NOTE
     copy = pltpu.make_async_copy(box_hbm.at[:, 0, pl.ds(cap, NOTE), :], tail, sem.at[0])
@@ -333,6 +323,19 @@
             note = notes[at // MOVE - 1][m : m + 1, :]
         rows = jnp.where(row_index == plan[at], note[:, : heads * HD], rows)
         residual = jnp.where(residual_index == plan[at], note[:, heads * HD :], residual)
+    project_out(rows.astype(BF16), wo, residual, own, sends, meta[1], peers_tp)
+
+
+def pack_kernel(slots, meta, lengths_s, plan, newkey, newvalue, cache_hbm, _own, *rest):
+    boxes, (leaving, in_sem, out_sem) = rest[:-3], rest[-3:]
+    moving = plan.shape[0] // 2
+    send_slots = [plan[moving + at] for at in range(MOVE, moving)]
+    packs = [
+        pltpu.make_async_copy(cache_hbm.at[slot], leaving.at[i], in_sem.at[i])
+        for i, slot in enumerate(send_slots)
+    ]
+    for pack in packs:
+        pack.start()
     for pack in packs:
         pack.wait()
     for i, slot in enumerate(send_slots):
@@ -346,7 +349,6 @@
     ]
     for out in outs:
         out.start()
-    project_out(rows.astype(BF16), wo, residual, own, sends, meta[1], peers_tp)
     for out in outs:
         out.wait()
 
@@ -580,25 +582,30 @@
 
     sent = [jax.ShapeDtypeStruct((slots, shard), F32)]
     sent += [jax.ShapeDtypeStruct((slots, shard), BF16)] * (peers_tp - 1)
-    own, *rest = pl.pallas_call(
-        functools.partial(out_kernel, peers, peers_tp, slots),
-        out_shape=sent
-        + [jax.ShapeDtypeStruct((MOVE,) + kv_cache.shape[1:], BF16)] * (others - 1),
-        in_specs=[SMEM] * 3 + [VMEM] * 5 + [ANY] * 2 + [VMEM] * (others - 1),
-        out_specs=[VMEM] * peers_tp + [ANY] * (others - 1),
+    own, *sends = pl.pallas_call(
+        functools.partial(out_kernel, peers, peers_tp),
+        out_shape=sent,
+        in_specs=[SMEM] * 2 + [VMEM] * 3 + [ANY] + [VMEM] * (others - 1),
+        out_specs=[VMEM] * peers_tp,
+        scratch_shapes=[pltpu.VMEM((MOVE, NOTE, HD), BF16), dma((1,))],
+        compiler_params=params(16),
+        cost_estimate=cost(2 * slots * width * heads * HD, out_weight.size * 2),
+        name="out_projection",
+    )(meta, plan, attended, out_weight, hidden, *got_notes)
+    boxes = pl.pallas_call(
+        functools.partial(pack_kernel, slots),
+        out_shape=[jax.ShapeDtypeStruct((MOVE,) + kv_cache.shape[1:], BF16)] * (others - 1),
+        in_specs=[SMEM] * 3 + [VMEM] * 2 + [ANY] * 2,
+        out_specs=[ANY] * (others - 1),
         scratch_shapes=[
             pltpu.VMEM((moving - MOVE,) + kv_cache.shape[1:], BF16),
-            pltpu.VMEM((MOVE, NOTE, HD), BF16),
-            dma((1,)),
             dma((moving - MOVE,)),
             dma((others - 1,)),
         ],
-        compiler_params=params(20),
-        cost_estimate=cost(2 * slots * width * heads * HD, out_weight.size * 2),
-        name="out_projection",
-    )(meta, lengths, plan, attended, out_weight, hidden, newkey1, newvalue1, got_notes[0], kv_cache,
-      *got_notes[1:])
-    sends, boxes = rest[: peers_tp - 1], rest[peers_tp - 1 :]
+        compiler_params=params(16),
+        cost_estimate=cost(1, cache_bytes),
+        name="pack",
+    )(meta, lengths, plan, newkey1, newvalue1, kv_cache, own)
     got_boxes = got_notes[:1] + [swapped(box, "inst", peers, k + 2) for k, box in enumerate(boxes)]
 
     def summed(own, sends):
@@ -611,9 +618,12 @@
             compiler_params=params(16),
             name="sum_terms",
         )(own, *got)
-        return [shard_rows] + [
-            swapped(shard_rows, "tp", peers_tp, k) for k in range(1, peers_tp)
-        ]
+        blocks = {0: shard_rows}
+        far = peers_tp // 2
+        while far:
+            blocks |= {k + far: swapped(blocks[k], "tp", peers_tp, far) for k in blocks}
+            far //= 2
+        return [blocks[k] for k in range(peers_tp)]
 
     pieces = summed(own, sends)
 

time: 73.9 us -> 71.6 us (0.969)
  starting transfers between devices: 22.8 us -> 19 us
  waiting for transfers between devices: 23 us -> 24.2 us
    ppermute x17, starting transfers between devices: 22.8 us -> 19 us  [swapped(): return lax.ppermute(x, axis, [(i, i ^ k) for i in range(size)])]
    ppermute x17, waiting for transfers between devices: 23 us -> 24.2 us  [swapped(): return lax.ppermute(x, axis, [(i, i ^ k) for i in range(size)])]
    pallas_call x1 -> x2, Pallas kernels: 2.34 us -> 2.81 us  [the longest x1 1.44 us: local(): pl.pallas_call(functools.partial(out_kernel, peers, peers_tp), out_shape=...]
  transfers between devices with their start and end apart: 17 -> 17, of which waited for: 7 -> 8; matrix products, arithmetic and copies ran while one was open for 0% -> 0% of each run, Pallas kernels for 12% -> 14%
where the time goes in v8:
time: 71.6 us; the launch traced here: 71.5 us
  Pallas kernels  27.3 us (38%)
  waiting for transfers between devices  24.2 us (34%)
  starting transfers between devices  19 us (27%)
  between operations  0.86 us (1%)
    ppermute x17, waiting for transfers between devices, swapped(): return lax.ppermute(x, axis, [(i, i ^ k) for i in range(size)])  24.2 us
    ppermute x17, starting transfers between devices, swapped(): return lax.ppermute(x, axis, [(i, i ^ k) for i in range(size)])  19 us
    pallas_call x1, Pallas kernels, local(): pl.pallas_call(functools.partial(first_kernel, peers, slots, heads, shard...  7.5 us
    pallas_call x1, Pallas kernels, local(): pl.pallas_call(functools.partial(second_kernel, peers, peers_tp, slots, h...  6.83 us
    pallas_call x1, Pallas kernels, local(): pl.pallas_call(functools.partial(attend_kernel, slots, heads), out_shape=...  4.56 us
    pallas_call x1, Pallas kernels, local(): pl.pallas_call(functools.partial(cache_kernel, peers, slots), out_shape=j...  4.23 us
    pallas_call x1, Pallas kernels, local(): pl.pallas_call(functools.partial(out_kernel, peers, peers_tp), out_shape=...  1.44 us
  transfers between devices with their start and end apart: 17, of which 8 were waited for; matrix products, arithmetic and copies ran while one was open for 0% of the time, Pallas kernels for 14%

profile of v8, /device:TPU:0, one launch (start us, length us, event | category | flops | bytes accessed | tf_op | source)
XLA Modules:
  0.0 71.5 jit_solution(10238915284758863794)
XLA Ops:
  0.6 0.1 pad_add_fusion.meta
  0.7 0.0 slice-start
  0.7 0.0 slice-start.1
  0.7 7.5 %first_step.1 = (f32[384,128]{1,0:T(8,128)S(1)}, f32[48,128]{1,0:T(8,128)S(1)}, f32[48,128]{1,0:T(8,128)S(1)}, s32[12]{0:T(128)S(1)}, bf16[2,2,272,128]{3,2,1,0:...) custom-call(s32[2]{0:T(128)S(1)} %pad_add_fusion.meta, s32[1,192]{1,0:T(1,128)} %bitcast.13, ...), custom_call_target="tpu_custom_call" | custom-call | flops 301989888 | bytes 6291456 | tf_op jit(solution)/shard_map/first_step/pallas_call | solution.py:527
  8.2 0.0 copy-start.1
  8.2 0.0 copy-start.3
  8.2 0.5 collective-permute-start
  8.8 2.6 %collective-permute-start.1 = (f32[2,1536]{1,0:T(2,128)S(1)}, f32[2,1536]{1,0:T(2,128)S(1)}, u32[]{:S(2)}, u32[]{:S(2)}) collective-permute-start(f32[2,1536]{1,0:T(2,128)S(1)} %get-tuple-element.26), channel_id=1, source_target_pairs={{0,8},{4,12},{8,0},{12,4},{1,9},{5,13},{9,1},{13,5},{2,10},{6,14},... | collective-permute-start | bytes 36872 | tf_op jit(solution)/shard_map/ppermute | solution.py:494
  11.4 0.1 collective-permute-start.2
  11.4 0.0 slice-done
  11.4 0.0 slice-done.1
  11.4 0.0 copy-done.7
  11.4 4.6 %attention.1.attended = bf16[48,512]{1,0:T(8,128)(2,1)S(1)} custom-call(s32[2]{0:T(128)S(1)} %pad_add_fusion.meta, s32[192]{0:T(256)S(1)} %copy-done.7, f32[384,128]{1,0:T(8,128)S(1)} %get-tuple-element.24.query, f32[48,128]{1,0:T(8,128)S(1)} %get-tuple-element.22.newkey.newkey1, f32[48,128]{1,0:T(8,128)S(1)} %get-tuple-element.23.newvalue.newvalue1, ...), custom_call_target="tpu_custom_call" | custom-call | flops 25165824 | bytes 6291456 | tf_op jit(solution)/shard_map/attention/pallas_call | solution.py:568
  16.0 0.0 collective-permute-done.1.rest_0_
  16.0 0.0 collective-permute-done.2.rest_1_
  16.0 0.0 collective-permute-done.box_hbm.rest_4_.rest_0_
  16.0 0.0 copy-done.1
  16.1 0.0 copy-done.3
  16.1 1.4 %out_projection.1 = (f32[48,1024]{1,0:T(8,128)S(1)}, bf16[48,1024]{1,0:T(8,128)(2,1)S(1)}, bf16[48,1024]{1,0:T(8,128)(2,1)S(1)}, bf16[48,1024]{1,0:T(8,128)(2,1)S(1)}) custom-call(s32[2]{0:T(128)S(1)} %pad_add_fusion.meta, s32[12]{0:T(128)S(1)} %get-tuple-element.21.plan, bf16[48,512]{1,0:T(8,128)(2,1)S(1)} %attention.1.attended, ...), custom_call_target="tpu_custom_call" | custom-call | flops 201326592 | bytes 4194304 | tf_op jit(solution)/shard_map/out_projection/pallas_call | solution.py:585
  17.5 0.0 copy-start
  17.5 0.0 copy-start.2
  17.5 0.0 copy-start.4
  17.5 0.0 copy-start.5
  17.6 0.0 copy-start.6
  17.6 0.0 copy-start.8
  17.6 3.9 %collective-permute-start.3 = (bf16[48,1024]{1,0:T(8,128)(2,1)S(1)}, bf16[48,1024]{1,0:T(8,128)(2,1)S(1)}, u32[]{:S(2)}, u32[]{:S(2)}) collective-permute-start(bf16[48,1024]{1,0:T(8,128)(2,1)S(1)} %get-tuple-element.29), channel_id=1, source_target_pairs={{0,3},{1,2},{2,1},{3,0},{4,7},{5,6},{6,5},{7,4},{8,11},{9,10},{10,... | collective-permute-start | bytes 294920 | tf_op jit(solution)/shard_map/ppermute | solution.py:494
  21.5 0.0 collective-permute-start.4
  21.5 0.6 collective-permute-start.5
  22.1 1.4 %pack.1 = (bf16[2,2,256,128]{3,2,1,0:T(8,128)(2,1)S(1)}, bf16[2,2,256,128]{3,2,1,0:T(8,128)(2,1)S(1)}) custom-call(s32[2]{0:T(128)S(1)} %pad_add_fusion.meta, s32[192]{0:T(256)S(1)} %copy-done.7, s32[12]{0:T(128)S(1)} %get-tuple-element.21.plan, f32[48,128]{1,0:T(8,128)S(1)} %get-tuple-element.22.newkey.newkey1, ...), custom_call_target="tpu_custom_call" | custom-call | flops 1 | bytes 6291456 | tf_op jit(solution)/shard_map/pack/pallas_call | solution.py:595
  23.5 1.7 %collective-permute-start.9 = (bf16[2,2,256,128]{3,2,1,0:T(8,128)(2,1)S(1)}, bf16[2,2,256,128]{3,2,1,0:T(8,128)(2,1)S(1)}, u32[]{:S(2)}, u32[]{:S(2)}) collective-permute-start(bf16[2,2,256,128]{3,2,1,0:T(8,128)(2,1)S(1)} %get-tuple-element.32), channel_id=1, source_target_pairs={{0,8},{4,12},{8,0},{12,4},{1,9},{5,13},{9,1},{13,5},{2,10},{6,14},... | collective-permute-start | bytes 786440 | tf_op jit(solution)/shard_map/ppermute | solution.py:494
  25.2 0.0 collective-permute-start.10
  25.2 0.0 collective-permute-done.3.rest_0_
  25.2 5.0 %collective-permute-done.4.rest_1_ = bf16[48,1024]{1,0:T(8,128)(2,1)S(1)} collective-permute-done((bf16[48,1024]{1,0:T(8,128)(2,1)S(1)}, bf16[48,1024]{1,0:T(8,128)(2,1)S(1)}, u32[]{:S(2)}, u32[]{:S(2)}) %collective-permute-start.4) | collective-permute-done | bytes 98336 | tf_op jit(solution)/shard_map/ppermute | solution.py:494
  30.2 0.0 collective-permute-done.5.rest_2_
  30.2 0.1 sum_terms.2.rest_0_
  30.3 0.1 collective-permute-start.7
  30.4 3.0 %collective-permute-start.6 = (bf16[48,1024]{1,0:T(8,128)(2,1)S(1)}, bf16[48,1024]{1,0:T(8,128)(2,1)S(1)}, u32[]{:S(2)}, u32[]{:S(2)}) collective-permute-start(bf16[48,1024]{1,0:T(8,128)(2,1)S(1)} %sum_terms.2.rest_0_), channel_id=1, source_target_pairs={{0,1},{1,0},{2,3},{3,2},{4,5},{5,4},{6,7},{7,6},{8,9},{9,8},{10,11... | collective-permute-start | bytes 294920 | tf_op jit(solution)/shard_map/ppermute | solution.py:494
  33.4 4.2 %collective-permute-done.7.rest_2_ = bf16[48,1024]{1,0:T(8,128)(2,1)S(1)} collective-permute-done((bf16[48,1024]{1,0:T(8,128)(2,1)S(1)}, bf16[48,1024]{1,0:T(8,128)(2,1)S(1)}, u32[]{:S(2)}, u32[]{:S(2)}) %collective-permute-start.7) | collective-permute-done | bytes 98336 | tf_op jit(solution)/shard_map/ppermute | solution.py:494
  37.6 0.0 collective-permute-start.8
  37.6 0.1 collective-permute-done.6.rest_1_
  37.7 0.0 collective-permute-done.9.rest_5_.rest_1_
  37.7 0.0 collective-permute-done.10.rest_6_.rest_2_
  37.7 4.5 %collective-permute-done.8.rest_3_ = bf16[48,1024]{1,0:T(8,128)(2,1)S(1)} collective-permute-done((bf16[48,1024]{1,0:T(8,128)(2,1)S(1)}, bf16[48,1024]{1,0:T(8,128)(2,1)S(1)}, u32[]{:S(2)}, u32[]{:S(2)}) %collective-permute-start.8) | collective-permute-done | bytes 98336 | tf_op jit(solution)/shard_map/ppermute | solution.py:494
  42.2 0.0 copy-done
  42.2 0.0 copy-done.2
  42.2 0.0 copy-done.4
  42.2 0.0 copy-done.5
  42.2 0.0 copy-done.6
  42.3 0.0 copy-done.8
  42.3 6.8 %second_step.1 = (f32[48,128]{1,0:T(8,128)S(1)}, f32[48,128]{1,0:T(8,128)S(1)}, f32[48,1024]{1,0:T(8,128)S(1)}, bf16[48,1024]{1,0:T(8,128)(2,1)S(1)}, bf16[48,10...) custom-call(s32[2]{0:T(128)S(1)} %pad_add_fusion.meta, s32[192]{0:T(256)S(1)} %copy-done.8, s32[192]{0:T(256)S(1)} %copy-done.7, ...), custom_call_target="tpu_custom_call" | custom-call | flops 905969664 | bytes 18874368 | tf_op jit(solution)/shard_map/second_step/pallas_call | solution.py:630
  49.1 1.5 %collective-permute-start.11 = (bf16[48,1024]{1,0:T(8,128)(2,1)S(1)}, bf16[48,1024]{1,0:T(8,128)(2,1)S(1)}, u32[]{:S(2)}, u32[]{:S(2)}) collective-permute-start(bf16[48,1024]{1,0:T(8,128)(2,1)S(1)} %get-tuple-element.35), channel_id=1, source_target_pairs={{0,3},{1,2},{2,1},{3,0},{4,7},{5,6},{6,5},{7,4},{8,11},{9,10},{10,... | collective-permute-start | bytes 294920 | tf_op jit(solution)/shard_map/ppermute | solution.py:494
  50.6 0.1 collective-permute-start.12
  50.6 2.9 %collective-permute-start.13 = (bf16[48,1024]{1,0:T(8,128)(2,1)S(1)}, bf16[48,1024]{1,0:T(8,128)(2,1)S(1)}, u32[]{:S(2)}, u32[]{:S(2)}) collective-permute-start(bf16[48,1024]{1,0:T(8,128)(2,1)S(1)} %get-tuple-element.37), channel_id=1, source_target_pairs={{0,1},{1,0},{2,3},{3,2},{4,5},{5,4},{6,7},{7,6},{8,9},{9,8},{10,11... | collective-permute-start | bytes 294920 | tf_op jit(solution)/shard_map/ppermute | solution.py:494
  53.6 2.8 %collective-permute-done.11.rest_0_ = bf16[48,1024]{1,0:T(8,128)(2,1)S(1)} collective-permute-done((bf16[48,1024]{1,0:T(8,128)(2,1)S(1)}, bf16[48,1024]{1,0:T(8,128)(2,1)S(1)}, u32[]{:S(2)}, u32[]{:S(2)}) %collective-permute-start.11) | collective-permute-done | bytes 98336 | tf_op jit(solution)/shard_map/ppermute | solution.py:494
  56.3 3.1 %collective-permute-done.12.rest_1_ = bf16[48,1024]{1,0:T(8,128)(2,1)S(1)} collective-permute-done((bf16[48,1024]{1,0:T(8,128)(2,1)S(1)}, bf16[48,1024]{1,0:T(8,128)(2,1)S(1)}, u32[]{:S(2)}, u32[]{:S(2)}) %collective-permute-start.12) | collective-permute-done | bytes 98336 | tf_op jit(solution)/shard_map/ppermute | solution.py:494
  59.4 0.0 collective-permute-done.13.rest_2_
  59.4 0.1 collective-permute-start.15
  59.5 1.9 %collective-permute-start.14 = (bf16[48,1024]{1,0:T(8,128)(2,1)S(1)}, bf16[48,1024]{1,0:T(8,128)(2,1)S(1)}, u32[]{:S(2)}, u32[]{:S(2)}) collective-permute-start(bf16[48,1024]{1,0:T(8,128)(2,1)S(1)} %sum_terms.3.rest_0_), channel_id=1, source_target_pairs={{0,1},{1,0},{2,3},{3,2},{4,5},{5,4},{6,7},{7,6},{8,9},{9,8},{10,11... | collective-permute-start | bytes 294920 | tf_op jit(solution)/shard_map/ppermute | solution.py:494
  61.4 4.1 %collective-permute-done.15.rest_2_ = bf16[48,1024]{1,0:T(8,128)(2,1)S(1)} collective-permute-done((bf16[48,1024]{1,0:T(8,128)(2,1)S(1)}, bf16[48,1024]{1,0:T(8,128)(2,1)S(1)}, u32[]{:S(2)}, u32[]{:S(2)}) %collective-permute-start.15) | collective-permute-done | bytes 98336 | tf_op jit(solution)/shard_map/ppermute | solution.py:494
  65.5 0.0 collective-permute-start.16
  65.6 4.2 %write_cache.1 = bf16[48,2,256,128]{3,2,1,0:T(8,128)(2,1)} custom-call(s32[2]{0:T(128)S(1)} %pad_add_fusion.meta, s32[192]{0:T(256)S(1)} %copy-done.8, s32[192]{0:T(256)S(1)} %copy-done.7, s32[12]{0:T(128)S(1)} %get-tuple-element.21.plan, f32[48,128]{1,0:T(8,128)S(1)} %get-tuple-element.22.newkey.newkey1, ...), custom_call_target="tpu_custom_call" | custom-call | bytes 12582912 | tf_op jit(solution)/shard_map/write_cache/pallas_call | solution.py:650
  69.8 0.0 collective-permute-done.14.rest_1_
  69.8 0.4 collective-permute-done.16.rest_3_
  70.2 1.3 %join.1 = bf16[48,4096]{1,0:T(8,128)(2,1)} custom-call(s32[2]{0:T(128)S(1)} %pad_add_fusion.meta, bf16[48,1024]{1,0:T(8,128)(2,1)S(1)} %sum_terms.3.rest_0_, bf16[48,1024]{1,0:T(8,128)(2,1)S(1)} %collective-permute-done.14.rest_1_, bf16[48,1024]{1,0:T(8,128)(2,1)S(1)} %collective-permute-done.15.rest_2_, bf16[48,1024]{1,0:T(8,128)(2,1)S(1)} %collective-permute-done.16.rest_3_), custom_call_target="tpu_custom_call" | custom-call | tf_op jit(solution)/shard_map/join/pallas_call | solution.py:665
  (3 shorter events, 0.0 us)
Async XLA Ops:
  0.7 10.7 %slice-start = ((s8[6291456]{0:T(1024)(128)(4,1)}), s8[4194304]{0:T(1024)(128)(4,1)S(1)}, s32[]{:S(2)}) async-start(s8[6291456]{0:T(1024)(128)(4,1)} %bitcast.6), calls=%async_computation | async-start | bytes 8388608
  0.7 10.7 %slice-start.1 = ((s8[6291456]{0:T(1024)(128)(4,1)}), s8[2097152]{0:T(1024)(128)(4,1)S(1)}, s32[]{:S(2)}) async-start(s8[6291456]{0:T(1024)(128)(4,1)} %bitcast.6), calls=%async_computation.1 | async-start | bytes 4194304
  0.7 10.7 %copy-start.7 = (s32[192]{0:T(256)S(1)}, s32[192]{0:T(256)}, u32[]{:S(2)}) copy-start(s32[192]{0:T(256)} %lengths_s.7) | copy-start | bytes 2308
  8.2 7.8 %copy-start.1 = (bf16[512,4096]{1,0:T(8,128)(2,1)S(1)}, bf16[512,4096]{1,0:T(8,128)(2,1)}, u32[]{:S(2)}) copy-start(bf16[512,4096]{1,0:T(8,128)(2,1)} %wo.3) | copy-start | bytes 12582916
  8.2 7.8 %copy-start.3 = (bf16[48,4096]{1,0:T(8,128)(2,1)S(1)}, bf16[48,4096]{1,0:T(8,128)(2,1)}, u32[]{:S(2)}) copy-start(bf16[48,4096]{1,0:T(8,128)(2,1)} %hidden.1) | copy-start | bytes 1179652
  8.2 7.8 %collective-permute-start = (bf16[2,2,272,128]{3,2,1,0:T(8,128)(2,1)S(1)}, bf16[2,2,272,128]{3,2,1,0:T(8,128)(2,1)S(1)}, u32[]{:S(2)}, u32[]{:S(2)}) collective-permute-start(bf16[2,2,272,128]{3,2,1,0:T(8,128)(2,1)S(1)} %get-tuple-element.25), channel_id=1, source_target_pairs={{0,4},{4,0},{8,12},{12,8},{1,5},{5,1},{9,13},{13,9},{2,6},{6,2},{1... | collective-permute-start | bytes 835592 | tf_op jit(solution)/shard_map/ppermute | solution.py:494
  8.8 7.3 %collective-permute-start.1 = (f32[2,1536]{1,0:T(2,128)S(1)}, f32[2,1536]{1,0:T(2,128)S(1)}, u32[]{:S(2)}, u32[]{:S(2)}) collective-permute-start(f32[2,1536]{1,0:T(2,128)S(1)} %get-tuple-element.26), channel_id=1, source_target_pairs={{0,8},{4,12},{8,0},{12,4},{1,9},{5,13},{9,1},{13,5},{2,10},{6,14},... | collective-permute-start | bytes 36872 | tf_op jit(solution)/shard_map/ppermute | solution.py:494
  11.4 4.7 %collective-permute-start.2 = (f32[2,1536]{1,0:T(2,128)S(1)}, f32[2,1536]{1,0:T(2,128)S(1)}, u32[]{:S(2)}, u32[]{:S(2)}) collective-permute-start(f32[2,1536]{1,0:T(2,128)S(1)} %get-tuple-element.27), channel_id=1, source_target_pairs={{0,12},{4,8},{8,4},{12,0},{1,13},{5,9},{9,5},{13,1},{2,14},{6,10},... | collective-permute-start | bytes 36872 | tf_op jit(solution)/shard_map/ppermute | solution.py:494
  17.5 24.7 %copy-start = (bf16[4096,512]{1,0:T(8,128)(2,1)S(1)}, bf16[4096,512]{1,0:T(8,128)(2,1)}, u32[]{:S(2)}) copy-start(bf16[4096,512]{1,0:T(8,128)(2,1)} %wq.1) | copy-start | bytes 12582916
  17.5 24.7 %copy-start.2 = (bf16[4096,2,128]{2,1,0:T(2,128)(2,1)S(1)}, bf16[4096,2,128]{2,1,0:T(2,128)(2,1)}, u32[]{:S(2)}) copy-start(bf16[4096,2,128]{2,1,0:T(2,128)(2,1)} %param.16) | copy-start | bytes 6291460
  17.5 24.7 %copy-start.4 = (f32[256,128]{1,0:T(8,128)S(1)}, f32[256,128]{1,0:T(8,128)}, u32[]{:S(2)}) copy-start(f32[256,128]{1,0:T(8,128)} %constant.12.clone.sin_hbm.sin_ref) | copy-start | bytes 393220
  17.5 24.7 %copy-start.5 = (f32[256,128]{1,0:T(8,128)S(1)}, f32[256,128]{1,0:T(8,128)}, u32[]{:S(2)}) copy-start(f32[256,128]{1,0:T(8,128)} %constant.11.clone.cos_hbm.cos_ref) | copy-start | bytes 393220
  17.6 24.7 %copy-start.6 = (f32[4096]{0:T(1024)S(1)}, f32[4096]{0:T(1024)}, u32[]{:S(2)}) copy-start(f32[4096]{0:T(1024)} %param.14) | copy-start | bytes 49156
  17.6 24.7 %copy-start.8 = (s32[192]{0:T(256)S(1)}, s32[192]{0:T(256)}, u32[]{:S(2)}) copy-start(s32[192]{0:T(256)} %source_s.3) | copy-start | bytes 2308
  17.6 7.6 %collective-permute-start.3 = (bf16[48,1024]{1,0:T(8,128)(2,1)S(1)}, bf16[48,1024]{1,0:T(8,128)(2,1)S(1)}, u32[]{:S(2)}, u32[]{:S(2)}) collective-permute-start(bf16[48,1024]{1,0:T(8,128)(2,1)S(1)} %get-tuple-element.29), channel_id=1, source_target_pairs={{0,3},{1,2},{2,1},{3,0},{4,7},{5,6},{6,5},{7,4},{8,11},{9,10},{10,... | collective-permute-start | bytes 294920 | tf_op jit(solution)/shard_map/ppermute | solution.py:494
  21.5 8.8 %collective-permute-start.4 = (bf16[48,1024]{1,0:T(8,128)(2,1)S(1)}, bf16[48,1024]{1,0:T(8,128)(2,1)S(1)}, u32[]{:S(2)}, u32[]{:S(2)}) collective-permute-start(bf16[48,1024]{1,0:T(8,128)(2,1)S(1)} %get-tuple-element.30), channel_id=1, source_target_pairs={{0,2},{1,3},{2,0},{3,1},{4,6},{5,7},{6,4},{7,5},{8,10},{9,11},{10,... | collective-permute-start | bytes 294920 | tf_op jit(solution)/shard_map/ppermute | solution.py:494
  21.5 8.8 %collective-permute-start.5 = (bf16[48,1024]{1,0:T(8,128)(2,1)S(1)}, bf16[48,1024]{1,0:T(8,128)(2,1)S(1)}, u32[]{:S(2)}, u32[]{:S(2)}) collective-permute-start(bf16[48,1024]{1,0:T(8,128)(2,1)S(1)} %get-tuple-element.31), channel_id=1, source_target_pairs={{0,1},{1,0},{2,3},{3,2},{4,5},{5,4},{6,7},{7,6},{8,9},{9,8},{10,11... | collective-permute-start | bytes 294920 | tf_op jit(solution)/shard_map/ppermute | solution.py:494
  23.5 14.2 %collective-permute-start.9 = (bf16[2,2,256,128]{3,2,1,0:T(8,128)(2,1)S(1)}, bf16[2,2,256,128]{3,2,1,0:T(8,128)(2,1)S(1)}, u32[]{:S(2)}, u32[]{:S(2)}) collective-permute-start(bf16[2,2,256,128]{3,2,1,0:T(8,128)(2,1)S(1)} %get-tuple-element.32), channel_id=1, source_target_pairs={{0,8},{4,12},{8,0},{12,4},{1,9},{5,13},{9,1},{13,5},{2,10},{6,14},... | collective-permute-start | bytes 786440 | tf_op jit(solution)/shard_map/ppermute | solution.py:494
  25.2 12.5 %collective-permute-start.10 = (bf16[2,2,256,128]{3,2,1,0:T(8,128)(2,1)S(1)}, bf16[2,2,256,128]{3,2,1,0:T(8,128)(2,1)S(1)}, u32[]{:S(2)}, u32[]{:S(2)}) collective-permute-start(bf16[2,2,256,128]{3,2,1,0:T(8,128)(2,1)S(1)} %get-tuple-element.33), channel_id=1, source_target_pairs={{0,12},{4,8},{8,4},{12,0},{1,13},{5,9},{9,5},{13,1},{2,14},{6,10},... | collective-permute-start | bytes 786440 | tf_op jit(solution)/shard_map/ppermute | solution.py:494
  30.3 7.3 %collective-permute-start.7 = (bf16[48,1024]{1,0:T(8,128)(2,1)S(1)}, bf16[48,1024]{1,0:T(8,128)(2,1)S(1)}, u32[]{:S(2)}, u32[]{:S(2)}) collective-permute-start(bf16[48,1024]{1,0:T(8,128)(2,1)S(1)} %sum_terms.2.rest_0_), channel_id=1, source_target_pairs={{0,2},{1,3},{2,0},{3,1},{4,6},{5,7},{6,4},{7,5},{8,10},{9,11},{10,... | collective-permute-start | bytes 294920 | tf_op jit(solution)/shard_map/ppermute | solution.py:494
  30.4 7.3 %collective-permute-start.6 = (bf16[48,1024]{1,0:T(8,128)(2,1)S(1)}, bf16[48,1024]{1,0:T(8,128)(2,1)S(1)}, u32[]{:S(2)}, u32[]{:S(2)}) collective-permute-start(bf16[48,1024]{1,0:T(8,128)(2,1)S(1)} %sum_terms.2.rest_0_), channel_id=1, source_target_pairs={{0,1},{1,0},{2,3},{3,2},{4,5},{5,4},{6,7},{7,6},{8,9},{9,8},{10,11... | collective-permute-start | bytes 294920 | tf_op jit(solution)/shard_map/ppermute | solution.py:494
  37.6 4.6 %collective-permute-start.8 = (bf16[48,1024]{1,0:T(8,128)(2,1)S(1)}, bf16[48,1024]{1,0:T(8,128)(2,1)S(1)}, u32[]{:S(2)}, u32[]{:S(2)}) collective-permute-start(bf16[48,1024]{1,0:T(8,128)(2,1)S(1)} %collective-permute-done.7.rest_2_), channel_id=1, source_target_pairs={{0,1},{1,0},{2,3},{3,2},{4,5},{5,4},{6,7},{7,6},{8,9},{9,8},{10,11... | collective-permute-start | bytes 294920 | tf_op jit(solution)/shard_map/ppermute | solution.py:494
  49.1 7.2 %collective-permute-start.11 = (bf16[48,1024]{1,0:T(8,128)(2,1)S(1)}, bf16[48,1024]{1,0:T(8,128)(2,1)S(1)}, u32[]{:S(2)}, u32[]{:S(2)}) collective-permute-start(bf16[48,1024]{1,0:T(8,128)(2,1)S(1)} %get-tuple-element.35), channel_id=1, source_target_pairs={{0,3},{1,2},{2,1},{3,0},{4,7},{5,6},{6,5},{7,4},{8,11},{9,10},{10,... | collective-permute-start | bytes 294920 | tf_op jit(solution)/shard_map/ppermute | solution.py:494
  50.6 8.8 %collective-permute-start.12 = (bf16[48,1024]{1,0:T(8,128)(2,1)S(1)}, bf16[48,1024]{1,0:T(8,128)(2,1)S(1)}, u32[]{:S(2)}, u32[]{:S(2)}) collective-permute-start(bf16[48,1024]{1,0:T(8,128)(2,1)S(1)} %get-tuple-element.36), channel_id=1, source_target_pairs={{0,2},{1,3},{2,0},{3,1},{4,6},{5,7},{6,4},{7,5},{8,10},{9,11},{10,... | collective-permute-start | bytes 294920 | tf_op jit(solution)/shard_map/ppermute | solution.py:494
  50.6 8.8 %collective-permute-start.13 = (bf16[48,1024]{1,0:T(8,128)(2,1)S(1)}, bf16[48,1024]{1,0:T(8,128)(2,1)S(1)}, u32[]{:S(2)}, u32[]{:S(2)}) collective-permute-start(bf16[48,1024]{1,0:T(8,128)(2,1)S(1)} %get-tuple-element.37), channel_id=1, source_target_pairs={{0,1},{1,0},{2,3},{3,2},{4,5},{5,4},{6,7},{7,6},{8,9},{9,8},{10,11... | collective-permute-start | bytes 294920 | tf_op jit(solution)/shard_map/ppermute | solution.py:494
  59.4 6.1 %collective-permute-start.15 = (bf16[48,1024]{1,0:T(8,128)(2,1)S(1)}, bf16[48,1024]{1,0:T(8,128)(2,1)S(1)}, u32[]{:S(2)}, u32[]{:S(2)}) collective-permute-start(bf16[48,1024]{1,0:T(8,128)(2,1)S(1)} %sum_terms.3.rest_0_), channel_id=1, source_target_pairs={{0,2},{1,3},{2,0},{3,1},{4,6},{5,7},{6,4},{7,5},{8,10},{9,11},{10,... | collective-permute-start | bytes 294920 | tf_op jit(solution)/shard_map/ppermute | solution.py:494
  59.5 10.3 %collective-permute-start.14 = (bf16[48,1024]{1,0:T(8,128)(2,1)S(1)}, bf16[48,1024]{1,0:T(8,128)(2,1)S(1)}, u32[]{:S(2)}, u32[]{:S(2)}) collective-permute-start(bf16[48,1024]{1,0:T(8,128)(2,1)S(1)} %sum_terms.3.rest_0_), channel_id=1, source_target_pairs={{0,1},{1,0},{2,3},{3,2},{4,5},{5,4},{6,7},{7,6},{8,9},{9,8},{10,11... | collective-permute-start | bytes 294920 | tf_op jit(solution)/shard_map/ppermute | solution.py:494
  65.5 4.6 %collective-permute-start.16 = (bf16[48,1024]{1,0:T(8,128)(2,1)S(1)}, bf16[48,1024]{1,0:T(8,128)(2,1)S(1)}, u32[]{:S(2)}, u32[]{:S(2)}) collective-permute-start(bf16[48,1024]{1,0:T(8,128)(2,1)S(1)} %collective-permute-done.15.rest_2_), channel_id=1, source_target_pairs={{0,1},{1,0},{2,3},{3,2},{4,5},{5,4},{6,7},{7,6},{8,9},{9,8},{10,11... | collective-permute-start | bytes 294920 | tf_op jit(solution)/shard_map/ppermute | solution.py:494

commit v9 on v8

--- a/solution.py
+++ b/solution.py
@@ -15,6 +15,7 @@
 GROUP = 8
 PIECE = 16
 CHUNK = 8
+BATCH = 16
 NOTE = 16
 
 F32 = jnp.float32
@@ -154,10 +155,10 @@
 ):
     others = peers - 1
     moving = others * MOVE
-    box, notes = rest[0], (None,) + rest[1:others]
+    cache, box, notes = rest[0], rest[1], (None,) + rest[2 : others + 1]
     (wq, wkv, normed3, spread, cos_rows, sin_rows, leaving, hidden32, source_s, lengths_s, source_v,
      hidden, gain, cos_ref, sin_ref, tail, small_sem, wq_sem, wkv_sem, in_sem,
-     box_sem) = rest[others:]
+     box_sem, cache_sem) = rest[others + 1 :]
     width = hidden.shape[1]
     me, me_tp = meta[0], meta[1]
     wq_copies = weight_copies(wq_hbm, wq, wq_sem, 4)
@@ -171,9 +172,18 @@
     ]
     for copy in small + wkv_copies + wq_copies:
         copy.start()
-    small[0].wait()
-    small[1].wait()
-
+    loads = [
+        pltpu.make_async_copy(
+            cache_hbm.at[pl.ds(c * CHUNK, CHUNK)], cache.at[pl.ds(c * CHUNK, CHUNK)], cache_sem.at[c]
+        )
+        for c in range(slots // CHUNK)
+    ]
+    for copy in small:
+        copy.wait()
+    wide = hidden[...].astype(F32)
+    hidden32[...] = wide
+    norm_into(normed3, [wide], [gain[...]], [0], width)
+    spread_normed(normed3, spread, slots, width)
     low = me * slots
     src = source_v[...]
     index = lax.broadcasted_iota(I32, src.shape, 1)
@@ -200,13 +210,9 @@
             plan[at] = jnp.where((r >= 0) & (r < src.shape[1]), r - low, -1)
             plan[moving + at] = slot
             pltpu.make_async_copy(cache_hbm.at[slot], leaving.at[at], in_sem.at[at]).start()
-
-    for copy in small[2:]:
-        copy.wait()
-    wide = hidden[...].astype(F32)
-    hidden32[...] = wide
-    norm_into(normed3, [wide], [gain[...]], [0], width)
-    spread_normed(normed3, spread, slots, width)
+    for copy in loads:
+        copy.start()
+
     gather_angles(lambda s: lengths_s[0, low + s], slots, cos_ref, sin_ref, cos_rows, sin_rows)
     query, key, value = project(
         normed3, spread, wq, wkv, slots, width, wq_copies, wkv_copies
@@ -255,35 +261,37 @@
             for g in range(heads):
                 note[m : m + 1, g * HD : (g + 1) * HD] = attended[at][g : g + 1, :]
             note[m : m + 1, heads * HD :] = residual
-    for copy in copies:
+    for copy in copies + loads:
         copy.wait()
 
 
+def attend_slots(cache, places, positions, query, attended_rows, heads):
+    slots = len(places)
+    for first in range(0, slots, BATCH):
+        span = range(first, first + BATCH)
+        got = attend(
+            cache,
+            [places[s] for s in span],
+            [positions[s] for s in span],
+            [query[s * GROUP : (s + 1) * GROUP, :] for s in span],
+        )
+        for s, rows in zip(span, got):
+            attended_rows[s * GROUP : (s + 1) * GROUP, :] = rows
+    return jnp.concatenate(
+        [attended_rows[pl.ds(g, slots, stride=GROUP), :] for g in range(heads)], axis=1
+    )
+
+
 def attend_kernel(
-    slots, heads, meta, lengths_s, query, newkey, newvalue, cache_hbm, out,
-    buffer, attended_rows, in_sem,
+    slots, heads, meta, lengths_s, query, newkey, newvalue, _, out, cache, attended_rows,
 ):
     low = meta[0] * slots
-
-    def copy_in(c):
-        span = pl.ds(c * CHUNK, CHUNK)
-        return pltpu.make_async_copy(cache_hbm.at[span], buffer.at[span], in_sem.at[c])
-
-    for c in range(slots // CHUNK):
-        copy_in(c).start()
-    for c in range(slots // CHUNK):
-        copy_in(c).wait()
-        span = list(range(c * CHUNK, (c + 1) * CHUNK))
-        positions = [lengths_s[low + s] for s in span]
-        for s, p in zip(span, positions):
-            put_row(buffer, s, p, newkey[s : s + 1, :], newvalue[s : s + 1, :])
-        got = attend(
-            buffer, span, positions, [query[s * GROUP : (s + 1) * GROUP, :] for s in span]
-        )
-        for s, rows in zip(span, got):
-            attended_rows[s * GROUP : (s + 1) * GROUP, :] = rows
-    for g in range(heads):
-        out[:, g * HD : (g + 1) * HD] = attended_rows[pl.ds(g, slots, stride=GROUP), :].astype(BF16)
+    positions = [lengths_s[low + s] for s in range(slots)]
+    for s, p in enumerate(positions):
+        put_row(cache, s, p, newkey[s : s + 1, :], newvalue[s : s + 1, :])
+    out[...] = attend_slots(
+        cache, list(range(slots)), positions, query, attended_rows, heads
+    ).astype(BF16)
 
 
 def project_out(attended, wo, residual, own, sends, me_tp, peers_tp):
@@ -326,31 +334,19 @@
     project_out(rows.astype(BF16), wo, residual, own, sends, meta[1], peers_tp)
 
 
-def pack_kernel(slots, meta, lengths_s, plan, newkey, newvalue, cache_hbm, _own, *rest):
-    boxes, (leaving, in_sem, out_sem) = rest[:-3], rest[-3:]
+def pack_kernel(plan, cache, _own, *rest):
+    boxes, out_sem = rest[:-1], rest[-1]
     moving = plan.shape[0] // 2
-    send_slots = [plan[moving + at] for at in range(MOVE, moving)]
     packs = [
-        pltpu.make_async_copy(cache_hbm.at[slot], leaving.at[i], in_sem.at[i])
-        for i, slot in enumerate(send_slots)
+        pltpu.make_async_copy(
+            cache.at[plan[moving + at]], boxes[at // MOVE - 1].at[at % MOVE], out_sem.at[at - MOVE]
+        )
+        for at in range(MOVE, moving)
     ]
     for pack in packs:
         pack.start()
     for pack in packs:
         pack.wait()
-    for i, slot in enumerate(send_slots):
-        put_row(
-            leaving, i, lengths_s[meta[0] * slots + slot],
-            newkey[pl.ds(slot, 1), :], newvalue[pl.ds(slot, 1), :],
-        )
-    outs = [
-        pltpu.make_async_copy(leaving.at[pl.ds(k * MOVE, MOVE)], out, out_sem.at[k])
-        for k, out in enumerate(boxes)
-    ]
-    for out in outs:
-        out.start()
-    for out in outs:
-        out.wait()
 
 
 def sum_kernel(own, *rest):
@@ -360,22 +356,6 @@
     rest[-1][...] = total.astype(BF16)
 
 
-def load_slots(slots, peers, cache_hbm, box_hbm, buffer, in_sem):
-    copies = []
-    for c in range(slots // CHUNK):
-        span = pl.ds(c * CHUNK, CHUNK)
-        copies.append(pltpu.make_async_copy(cache_hbm.at[span], buffer.at[span], in_sem.at[c]))
-    for k in range(peers - 1):
-        copies.append(
-            pltpu.make_async_copy(
-                box_hbm[k].at[:, :, pl.ds(0, cache_hbm.shape[2]), :],
-                buffer.at[pl.ds(slots + k * MOVE, MOVE)],
-                in_sem.at[slots // CHUNK + k],
-            )
-        )
-    return copies
-
-
 def map_places(slots, peers, plan, place):
     for s in range(slots):
         place[s] = s
@@ -389,21 +369,26 @@
 
 def second_kernel(
     peers, peers_tp, slots, heads,
-    meta, source_s, lengths_s, plan, gain, cos_ref, sin_ref, newkey1, newvalue1,
-    wq, wkv, wo, cache_hbm, *rest,
+    meta, source_s, lengths_s, plan, gain, cos_ref, sin_ref, wq, wkv, wo, _, *rest,
 ):
     blocks, rest = rest[:peers_tp], rest[peers_tp:]
     box_hbm, rest = rest[: peers - 1], rest[peers - 1 :]
-    newkey, newvalue, own = rest[:3]
-    sends, rest = rest[3 : 2 + peers_tp], rest[2 + peers_tp :]
-    (normed3, spread, cos_rows, sin_rows, buffer, query_rows, attended_rows, place,
-     in_sem) = rest
+    own, sends, cache = rest[0], rest[1:peers_tp], rest[peers_tp]
+    (normed3, spread, cos_rows, sin_rows, query_rows, attended_rows, place,
+     in_sem) = rest[peers_tp + 1 :]
     me, me_tp = meta[0], meta[1]
     low = me * slots
     width = gain.shape[1]
     shard = own.shape[1]
-    cache_copies = load_slots(slots, peers, cache_hbm, box_hbm, buffer, in_sem)
-    for copy in cache_copies[::-1]:
+    loads = [
+        pltpu.make_async_copy(
+            box.at[:, :, pl.ds(0, cache.shape[2]), :],
+            cache.at[pl.ds(slots + k * MOVE, MOVE)],
+            in_sem.at[k],
+        )
+        for k, box in enumerate(box_hbm)
+    ]
+    for copy in loads:
         copy.start()
 
     map_places(slots, peers, plan, place)
@@ -416,65 +401,37 @@
         width,
     )
     spread_normed(normed3, spread, slots, width)
-    lengths = [lengths_s[source_s[low + s]] for s in range(slots)]
-    gather_angles(lambda s: lengths[s] + 1, slots, cos_ref, sin_ref, cos_rows, sin_rows)
+    positions = [lengths_s[source_s[low + s]] + 1 for s in range(slots)]
+    gather_angles(lambda s: positions[s], slots, cos_ref, sin_ref, cos_rows, sin_rows)
     query, key, value = project(normed3, spread, wq, wkv, slots, width)
     cosine, sine = cos_rows[...], sin_rows[...]
     query_rows[...] = jnp.zeros(query_rows.shape, F32)
     for g in range(heads):
         turned = turn(query[:, g * HD : (g + 1) * HD], cosine, sine)
         query_rows[pl.ds(g, slots, stride=GROUP), :] = turned.astype(BF16).astype(F32)
-    newkey[...] = turn(key, cosine, sine).astype(BF16).astype(F32)
-    newvalue[...] = value.astype(BF16).astype(F32)
-
-    for copy in cache_copies[::-1]:
+    newkey = turn(key, cosine, sine).astype(BF16).astype(F32)
+    newvalue = value.astype(BF16).astype(F32)
+
+    for copy in loads:
         copy.wait()
-    for c in range(slots // CHUNK):
-        span = list(range(c * CHUNK, (c + 1) * CHUNK))
-        places = [place[s] for s in span]
-        for s, at in zip(span, places):
-            first = jnp.where(at < slots, lengths[s], -1)
-            put_row(buffer, at, first, newkey1[s : s + 1, :], newvalue1[s : s + 1, :])
-            put_row(buffer, at, lengths[s] + 1, newkey[s : s + 1, :], newvalue[s : s + 1, :])
-        got = attend(
-            buffer, places, [lengths[s] + 1 for s in span],
-            [query_rows[s * GROUP : (s + 1) * GROUP, :] for s in span],
-        )
-        for s, rows in zip(span, got):
-            attended_rows[s * GROUP : (s + 1) * GROUP, :] = rows
-    attended = jnp.concatenate(
-        [attended_rows[pl.ds(g, slots, stride=GROUP), :].astype(BF16) for g in range(heads)], axis=1
+    places = [place[s] for s in range(slots)]
+    for s, (at, p) in enumerate(zip(places, positions)):
+        put_row(cache, at, p, newkey[s : s + 1, :], newvalue[s : s + 1, :])
+    attended = attend_slots(cache, places, positions, query_rows, attended_rows, heads)
+    project_out(
+        attended.astype(BF16), wo, blocks[0][...].astype(F32), own, sends, me_tp, peers_tp
     )
-    project_out(attended, wo, blocks[0][...].astype(F32), own, sends, me_tp, peers_tp)
-
-
-def cache_kernel(
-    peers, slots, meta, source_s, lengths_s, plan, newkey1, newvalue1, newkey2, newvalue2,
-    cache_hbm, *rest,
-):
-    box_hbm, rest = rest[: peers - 1], rest[peers - 1 :]
-    out_hbm, buffer, place, in_sem, out_sem = rest
-    low = meta[0] * slots
-    cache_copies = load_slots(slots, peers, cache_hbm, box_hbm, buffer, in_sem)
-    for copy in cache_copies:
+
+
+def cache_kernel(peers, slots, plan, cache, out_hbm, place, out_sem):
+    map_places(slots, peers, plan, place)
+    copies = [
+        pltpu.make_async_copy(cache.at[place[s]], out_hbm.at[s], out_sem.at[s])
+        for s in range(slots)
+    ]
+    for copy in copies:
         copy.start()
-    map_places(slots, peers, plan, place)
-    chunks = slots // CHUNK
-    for copy in cache_copies[chunks:]:
-        copy.wait()
-    outs = []
-    for c in range(chunks):
-        cache_copies[c].wait()
-        for s in range(c * CHUNK, (c + 1) * CHUNK):
-            at = place[s]
-            length = lengths_s[source_s[low + s]]
-            first = jnp.where(at < slots, length, -1)
-            put_row(buffer, at, first, newkey1[s : s + 1, :], newvalue1[s : s + 1, :])
-            put_row(buffer, at, length + 1, newkey2[s : s + 1, :], newvalue2[s : s + 1, :])
-            copy = pltpu.make_async_copy(buffer.at[at], out_hbm.at[s], out_sem.at[s])
-            copy.start()
-            outs.append(copy)
-    for copy in outs:
+    for copy in copies:
         copy.wait()
 
 
@@ -523,19 +480,21 @@
     ]
     flops = 2 * slots * width * (heads + 2) * HD
     cache_bytes = kv_cache.size * 2
-
-    query, newkey1, newvalue1, plan, *notes = pl.pallas_call(
+    held = jax.ShapeDtypeStruct((slots + moving,) + kv_cache.shape[1:], BF16)
+
+    query, newkey1, newvalue1, plan, cache, *notes = pl.pallas_call(
         functools.partial(first_kernel, peers, slots, heads, shard),
         out_shape=[
             jax.ShapeDtypeStruct((slots * GROUP, HD), F32),
             row32,
             row32,
             jax.ShapeDtypeStruct((2 * moving,), I32),
+            held,
         ]
         + [jax.ShapeDtypeStruct((MOVE, 2, cap + NOTE, HD), BF16)]
         + [jax.ShapeDtypeStruct((MOVE, note_width), F32)] * (others - 1),
         in_specs=[SMEM] + [HBM] * 9,
-        out_specs=[VMEM] * 3 + [SMEM, ANY] + [VMEM] * (others - 1),
+        out_specs=[VMEM] * 3 + [SMEM, VMEM, ANY] + [VMEM] * (others - 1),
         scratch_shapes=weights
         + stages
         + [
@@ -554,6 +513,7 @@
             dma((4,)),
             dma((moving,)),
             dma((1 + MOVE,)),
+            dma((slots // CHUNK,)),
         ],
         compiler_params=params(24),
         cost_estimate=cost(flops, (query_weight.size + wkv.size) * 2),
@@ -565,20 +525,17 @@
     ))
     got_notes = [swapped(note, "inst", peers, k + 1) for k, note in enumerate(notes)]
 
-    attended = pl.pallas_call(
+    attended, cache = pl.pallas_call(
         functools.partial(attend_kernel, slots, heads),
-        out_shape=jax.ShapeDtypeStruct((slots, heads * HD), BF16),
-        in_specs=[SMEM] * 2 + [VMEM] * 3 + [ANY],
-        out_specs=VMEM,
-        scratch_shapes=[
-            pltpu.VMEM(kv_cache.shape, BF16),
-            pltpu.VMEM((slots * GROUP, HD), F32),
-            dma((slots // CHUNK,)),
-        ],
-        compiler_params=params(24),
+        out_shape=[jax.ShapeDtypeStruct((slots, heads * HD), BF16), held],
+        in_specs=[SMEM] * 2 + [VMEM] * 4,
+        out_specs=[VMEM] * 2,
+        scratch_shapes=[pltpu.VMEM((slots * GROUP, HD), F32)],
+        input_output_aliases={5: 1},
+        compiler_params=params(12),
         cost_estimate=cost(4 * slots * cap * HD * heads, cache_bytes),
         name="attention",
-    )(meta, lengths, query, newkey1, newvalue1, kv_cache)
+    )(meta, lengths, query, newkey1, newvalue1, cache)
 
     sent = [jax.ShapeDtypeStruct((slots, shard), F32)]
     sent += [jax.ShapeDtypeStruct((slots, shard), BF16)] * (peers_tp - 1)
@@ -593,22 +550,18 @@
         name="out_projection",
     )(meta, plan, attended, out_weight, hidden, *got_notes)
     boxes = pl.pallas_call(
-        functools.partial(pack_kernel, slots),
+        pack_kernel,
         out_shape=[jax.ShapeDtypeStruct((MOVE,) + kv_cache.shape[1:], BF16)] * (others - 1),
-        in_specs=[SMEM] * 3 + [VMEM] * 2 + [ANY] * 2,
+        in_specs=[SMEM, VMEM, ANY],
         out_specs=[ANY] * (others - 1),
-        scratch_shapes=[
-            pltpu.VMEM((moving - MOVE,) + kv_cache.shape[1:], BF16),
-            dma((moving - MOVE,)),
-            dma((others - 1,)),
-        ],
+        scratch_shapes=[dma((moving - MOVE,))],
         compiler_params=params(16),
-        cost_estimate=cost(1, cache_bytes),
+        cost_estimate=cost(1, 1 * cache_bytes),
         name="pack",
-    )(meta, lengths, plan, newkey1, newvalue1, kv_cache, own)
+    )(plan, cache, own)
     got_boxes = got_notes[:1] + [swapped(box, "inst", peers, k + 2) for k, box in enumerate(boxes)]
 
-    def summed(own, sends):
+    def summed(own, sends, passed_on):
         got = [swapped(sends[k - 1], "tp", peers_tp, k) for k in range(peers_tp - 1, 0, -1)]
         shard_rows = pl.pallas_call(
             sum_kernel,
@@ -619,49 +572,46 @@
             name="sum_terms",
         )(own, *got)
         blocks = {0: shard_rows}
-        far = peers_tp // 2
+        if not passed_on:
+            blocks |= {k: swapped(shard_rows, "tp", peers_tp, k) for k in range(1, peers_tp)}
+        far = peers_tp // 2 if passed_on else 0
         while far:
             blocks |= {k + far: swapped(blocks[k], "tp", peers_tp, far) for k in blocks}
             far //= 2
         return [blocks[k] for k in range(peers_tp)]
 
-    pieces = summed(own, sends)
-
-    newkey2, newvalue2, own, *sends = pl.pallas_call(
+    pieces = summed(own, sends, True)
+
+    own, *sends, cache = pl.pallas_call(
         functools.partial(second_kernel, peers, peers_tp, slots, heads),
-        out_shape=[row32, row32] + sent,
-        in_specs=[SMEM] * 4 + [VMEM] * 8 + [ANY] + [VMEM] * peers_tp + [ANY] * others,
-        out_specs=[VMEM] * (2 + peers_tp),
+        out_shape=sent + [held],
+        in_specs=[SMEM] * 4 + [VMEM] * (7 + peers_tp) + [ANY] * others,
+        out_specs=[VMEM] * (1 + peers_tp),
         scratch_shapes=stages
         + [
-            pltpu.VMEM((slots + moving,) + kv_cache.shape[1:], BF16),
             pltpu.VMEM((slots * GROUP, HD), F32),
             pltpu.VMEM((slots * GROUP, HD), F32),
             pltpu.SMEM((slots,), I32),
-            dma((slots // CHUNK + others,)),
+            dma((others,)),
         ],
-        compiler_params=params(32),
+        input_output_aliases={10: peers_tp},
+        compiler_params=params(16),
         cost_estimate=cost(3 * flops, cache_bytes + (query_weight.size + wkv.size) * 4),
         name="second_step",
-    )(meta, source, lengths, plan, gain, cosine, sine, newkey1, newvalue1, query_weight, wkv,
-      out_weight, kv_cache, *pieces, *got_boxes)
-
-    pieces = summed(own, sends)
+    )(meta, source, lengths, plan, gain, cosine, sine, query_weight, wkv, out_weight, cache,
+      *pieces, *got_boxes)
+
+    pieces = summed(own, sends, False)
     final_cache = pl.pallas_call(
         functools.partial(cache_kernel, peers, slots),
         out_shape=jax.ShapeDtypeStruct(kv_cache.shape, BF16),
-        in_specs=[SMEM] * 4 + [VMEM] * 4 + [ANY] * peers,
+        in_specs=[SMEM, VMEM],
         out_specs=ANY,
-        scratch_shapes=[
-            pltpu.VMEM((slots + moving,) + kv_cache.shape[1:], BF16),
-            pltpu.SMEM((slots,), I32),
-            dma((slots // CHUNK + others,)),
-            dma((slots,)),
-        ],
-        compiler_params=params(24),
+        scratch_shapes=[pltpu.SMEM((slots,), I32), dma((slots,))],
+        compiler_params=params(16),
         cost_estimate=cost(0, 2 * cache_bytes),
         name="write_cache",
-    )(meta, source, lengths, plan, newkey1, newvalue1, newkey2, newvalue2, kv_cache, *got_boxes)
+    )(plan, cache)
     final_hidden = pl.pallas_call(
         functools.partial(join_kernel, peers_tp),
         out_shape=jax.ShapeDtypeStruct(hidden.shape, BF16),

time: 71.6 us -> 68.3 us (0.954)
  Pallas kernels: 27.3 us -> 24.3 us
  waiting for transfers between devices: 24.2 us -> 21.7 us
  starting transfers between devices: 19 us -> 21.1 us
    ppermute x17, waiting for transfers between devices: 24.2 us -> 21.7 us  [swapped(): return lax.ppermute(x, axis, [(i, i ^ k) for i in range(size)])]
    ppermute x17, starting transfers between devices: 19 us -> 21.1 us  [swapped(): return lax.ppermute(x, axis, [(i, i ^ k) for i in range(size)])]
    pallas_call x1, Pallas kernels: 4.56 us -> 2.68 us  [local(): pl.pallas_call(functools.partial(attend_kernel, slots, heads), out_shape=...]
    pallas_call x1, Pallas kernels: 6.83 us -> 5.63 us  [local(): pl.pallas_call(functools.partial(second_kernel, peers, peers_tp, slots, h...]
    pallas_call x1, Pallas kernels: 7.5 us -> 8.23 us  [local(): pl.pallas_call(functools.partial(first_kernel, peers, slots, heads, shard...]
  transfers between devices with their start and end apart: 17 -> 17, of which waited for: 8 -> 9; matrix products, arithmetic and copies ran while one was open for 0% -> 0% of each run, Pallas kernels for 14% -> 11%
where the time goes in v9:
time: 68.3 us; the launch traced here: 68 us
  Pallas kernels  24.3 us (36%)
  waiting for transfers between devices  21.7 us (32%)
  starting transfers between devices  21.1 us (31%)
  between operations  0.81 us (1%)
    ppermute x17, waiting for transfers between devices, swapped(): return lax.ppermute(x, axis, [(i, i ^ k) for i in range(size)])  21.7 us
    ppermute x17, starting transfers between devices, swapped(): return lax.ppermute(x, axis, [(i, i ^ k) for i in range(size)])  21.1 us
    pallas_call x1, Pallas kernels, local(): pl.pallas_call(functools.partial(first_kernel, peers, slots, heads, shard...  8.23 us
    pallas_call x1, Pallas kernels, local(): pl.pallas_call(functools.partial(second_kernel, peers, peers_tp, slots, h...  5.63 us
    pallas_call x1, Pallas kernels, local(): pl.pallas_call(functools.partial(cache_kernel, peers, slots), out_shape=j...  3.61 us
    pallas_call x1, Pallas kernels, local(): pl.pallas_call(functools.partial(attend_kernel, slots, heads), out_shape=...  2.68 us
    pallas_call x1, Pallas kernels, local(): pl.pallas_call(functools.partial(out_kernel, peers, peers_tp), out_shape=...  1.43 us
  transfers between devices with their start and end apart: 17, of which 9 were waited for; matrix products, arithmetic and copies ran while one was open for 0% of the time, Pallas kernels for 11%

profile of v9, /device:TPU:0, one launch (start us, length us, event | category | flops | bytes accessed | tf_op | source)
XLA Modules:
  0.0 68.0 jit_solution(17672044803452626885)
XLA Ops:
  0.6 0.1 pad_add_fusion.meta
  0.7 0.0 copy-start.7
  0.7 8.2 %first_step.1 = (f32[384,128]{1,0:T(8,128)S(1)}, f32[48,128]{1,0:T(8,128)S(1)}, f32[48,128]{1,0:T(8,128)S(1)}, s32[12]{0:T(128)S(1)}, bf16[54,2,256,128]{3,2,1,0...) custom-call(s32[2]{0:T(128)S(1)} %pad_add_fusion.meta, ...), custom_call_target="tpu_custom_call" | custom-call | flops 301989888 | bytes 6291456 | tf_op jit(solution)/shard_map/first_step/pallas_call | solution.py:485
  8.9 0.0 copy-start.1
  9.0 0.0 copy-start.3
  9.0 0.5 collective-permute-start
  9.5 2.6 %collective-permute-start.1 = (f32[2,1536]{1,0:T(2,128)S(1)}, f32[2,1536]{1,0:T(2,128)S(1)}, u32[]{:S(2)}, u32[]{:S(2)}) collective-permute-start(f32[2,1536]{1,0:T(2,128)S(1)} %get-tuple-element.31), channel_id=1, source_target_pairs={{0,8},{4,12},{8,0},{12,4},{1,9},{5,13},{9,1},{13,5},{2,10},{6,14},... | collective-permute-start | bytes 36872 | tf_op jit(solution)/shard_map/ppermute | solution.py:451
  12.1 0.1 collective-permute-start.2
  12.2 0.0 copy-done.7
  12.2 2.7 %attention.1 = (bf16[48,512]{1,0:T(8,128)(2,1)S(1)}, bf16[54,2,256,128]{3,2,1,0:T(8,128)(2,1)S(1)}) custom-call(s32[2]{0:T(128)S(1)} %pad_add_fusion.meta, s32[192]{0:T(256)S(1)} %copy-done.7, f32[384,128]{1,0:T(8,128)S(1)} %get-tuple-element.24.query, f32[48,128]{1,0:T(8,128)S(1)} %get-tuple-element.25.newkey, ...), custom_call_target="tpu_custom_call", output_to_operand_aliasing={{1}: (5, {})} | custom-call | flops 25165824 | bytes 6291456 | tf_op jit(solution)/shard_map/attention/pallas_call | solution.py:528
  14.9 0.0 collective-permute-done.1.rest_0_
  14.9 0.3 collective-permute-done.2.rest_1_
  15.2 0.0 collective-permute-done.box_hbm.rest_4_
  15.2 0.0 copy-done.1
  15.2 0.0 copy-done.3
  15.2 0.0 copy-start
  15.3 0.0 copy-start.2
  15.3 0.0 copy-start.4
  15.3 0.0 copy-start.5
  15.3 0.0 copy-start.6
  15.3 0.0 copy-start.8
  15.3 1.4 %out_projection.1 = (f32[48,1024]{1,0:T(8,128)S(1)}, bf16[48,1024]{1,0:T(8,128)(2,1)S(1)}, bf16[48,1024]{1,0:T(8,128)(2,1)S(1)}, bf16[48,1024]{1,0:T(8,128)(2,1)S(1)}) custom-call(s32[2]{0:T(128)S(1)} %pad_add_fusion.meta, s32[12]{0:T(128)S(1)} %get-tuple-element.23.plan, bf16[48,512]{1,0:T(8,128)(2,1)S(1)} %get-tuple-element.29.attended, ...), custom_call_target="tpu_custom_call" | custom-call | flops 201326592 | bytes 4194304 | tf_op jit(solution)/shard_map/out_projection/pallas_call | solution.py:542
  16.8 3.7 %collective-permute-start.3 = (bf16[48,1024]{1,0:T(8,128)(2,1)S(1)}, bf16[48,1024]{1,0:T(8,128)(2,1)S(1)}, u32[]{:S(2)}, u32[]{:S(2)}) collective-permute-start(bf16[48,1024]{1,0:T(8,128)(2,1)S(1)} %get-tuple-element.34), channel_id=1, source_target_pairs={{0,3},{1,2},{2,1},{3,0},{4,7},{5,6},{6,5},{7,4},{8,11},{9,10},{10,... | collective-permute-start | bytes 294920 | tf_op jit(solution)/shard_map/ppermute | solution.py:451
  20.4 0.0 collective-permute-start.4
  20.4 0.8 %collective-permute-start.5 = (bf16[48,1024]{1,0:T(8,128)(2,1)S(1)}, bf16[48,1024]{1,0:T(8,128)(2,1)S(1)}, u32[]{:S(2)}, u32[]{:S(2)}) collective-permute-start(bf16[48,1024]{1,0:T(8,128)(2,1)S(1)} %get-tuple-element.36), channel_id=1, source_target_pairs={{0,1},{1,0},{2,3},{3,2},{4,5},{5,4},{6,7},{7,6},{8,9},{9,8},{10,11... | collective-permute-start | bytes 294920 | tf_op jit(solution)/shard_map/ppermute | solution.py:451
  21.2 1.3 %pack.1 = (bf16[2,2,256,128]{3,2,1,0:T(8,128)(2,1)S(1)}, bf16[2,2,256,128]{3,2,1,0:T(8,128)(2,1)S(1)}) custom-call(s32[12]{0:T(128)S(1)} %get-tuple-element.23.plan, bf16[54,2,256,128]{3,2,1,0:T(8,128)(2,1)S(1)} %get-tuple-element.28.cache._, f32[48,1024]{1,0:T(8,128)S(1)} %get-tuple-element.33.own._own), custom_call_target="tpu_custom_call" | custom-call | flops 1 | bytes 6291456 | tf_op jit(solution)/shard_map/pack/pallas_call | solution.py:552
  22.5 1.5 %collective-permute-start.9 = (bf16[2,2,256,128]{3,2,1,0:T(8,128)(2,1)S(1)}, bf16[2,2,256,128]{3,2,1,0:T(8,128)(2,1)S(1)}, u32[]{:S(2)}, u32[]{:S(2)}) collective-permute-start(bf16[2,2,256,128]{3,2,1,0:T(8,128)(2,1)S(1)} %get-tuple-element.37), channel_id=1, source_target_pairs={{0,8},{4,12},{8,0},{12,4},{1,9},{5,13},{9,1},{13,5},{2,10},{6,14},... | collective-permute-start | bytes 786440 | tf_op jit(solution)/shard_map/ppermute | solution.py:451
  24.0 0.0 collective-permute-start.10
  24.0 0.4 collective-permute-done.3.rest_0_
  24.3 4.7 %collective-permute-done.4.rest_1_ = bf16[48,1024]{1,0:T(8,128)(2,1)S(1)} collective-permute-done((bf16[48,1024]{1,0:T(8,128)(2,1)S(1)}, bf16[48,1024]{1,0:T(8,128)(2,1)S(1)}, u32[]{:S(2)}, u32[]{:S(2)}) %collective-permute-start.4) | collective-permute-done | bytes 98336 | tf_op jit(solution)/shard_map/ppermute | solution.py:451
  29.1 0.0 collective-permute-done.5.rest_2_
  29.1 0.1 sum_terms.2.rest_0_
  29.1 0.3 collective-permute-start.7
  29.4 2.8 %collective-permute-start.6 = (bf16[48,1024]{1,0:T(8,128)(2,1)S(1)}, bf16[48,1024]{1,0:T(8,128)(2,1)S(1)}, u32[]{:S(2)}, u32[]{:S(2)}) collective-permute-start(bf16[48,1024]{1,0:T(8,128)(2,1)S(1)} %sum_terms.2.rest_0_), channel_id=1, source_target_pairs={{0,1},{1,0},{2,3},{3,2},{4,5},{5,4},{6,7},{7,6},{8,9},{9,8},{10,11... | collective-permute-start | bytes 294920 | tf_op jit(solution)/shard_map/ppermute | solution.py:451
  32.2 4.1 %collective-permute-done.7.rest_2_ = bf16[48,1024]{1,0:T(8,128)(2,1)S(1)} collective-permute-done((bf16[48,1024]{1,0:T(8,128)(2,1)S(1)}, bf16[48,1024]{1,0:T(8,128)(2,1)S(1)}, u32[]{:S(2)}, u32[]{:S(2)}) %collective-permute-start.7) | collective-permute-done | bytes 98336 | tf_op jit(solution)/shard_map/ppermute | solution.py:451
  36.3 0.0 collective-permute-start.8
  36.3 0.1 collective-permute-done.6.rest_1_
  36.4 0.0 collective-permute-done.9.rest_5_
  36.4 0.0 collective-permute-done.10.rest_6_
  36.4 4.5 %collective-permute-done.8.rest_3_ = bf16[48,1024]{1,0:T(8,128)(2,1)S(1)} collective-permute-done((bf16[48,1024]{1,0:T(8,128)(2,1)S(1)}, bf16[48,1024]{1,0:T(8,128)(2,1)S(1)}, u32[]{:S(2)}, u32[]{:S(2)}) %collective-permute-start.8) | collective-permute-done | bytes 98336 | tf_op jit(solution)/shard_map/ppermute | solution.py:451
  40.9 0.0 copy-done
  40.9 0.0 copy-done.2
  40.9 0.0 copy-done.4
  40.9 0.0 copy-done.5
  40.9 0.0 copy-done.6
  40.9 0.0 copy-done.8
  40.9 5.6 %second_step.1 = (f32[48,1024]{1,0:T(8,128)S(1)}, bf16[48,1024]{1,0:T(8,128)(2,1)S(1)}, bf16[48,1024]{1,0:T(8,128)(2,1)S(1)}, bf16[48,1024]{1,0:T(8,128)(2,1)S(1)}, bf16[54,2,256,128]{3,2,1,0:T(8,128)(2,1)S(1)}) custom-call(s32[2]{0:T(128)S(1)} %pad_add_fusion.meta, s32[192]{0:T(256)S(1)} %copy-done.8, ...), custom_call_target="tpu_custom_call", output_to_operand_aliasing={{4}: (10, {})} | custom-call | flops 905969664 | bytes 18874368 | tf_op jit(solution)/shard_map/second_step/pallas_call | solution.py:585
  46.6 1.6 %collective-permute-start.11 = (bf16[48,1024]{1,0:T(8,128)(2,1)S(1)}, bf16[48,1024]{1,0:T(8,128)(2,1)S(1)}, u32[]{:S(2)}, u32[]{:S(2)}) collective-permute-start(bf16[48,1024]{1,0:T(8,128)(2,1)S(1)} %get-tuple-element.40), channel_id=1, source_target_pairs={{0,3},{1,2},{2,1},{3,0},{4,7},{5,6},{6,5},{7,4},{8,11},{9,10},{10,... | collective-permute-start | bytes 294920 | tf_op jit(solution)/shard_map/ppermute | solution.py:451
  48.2 0.0 collective-permute-start.12
  48.2 2.9 %collective-permute-start.13 = (bf16[48,1024]{1,0:T(8,128)(2,1)S(1)}, bf16[48,1024]{1,0:T(8,128)(2,1)S(1)}, u32[]{:S(2)}, u32[]{:S(2)}) collective-permute-start(bf16[48,1024]{1,0:T(8,128)(2,1)S(1)} %get-tuple-element.42), channel_id=1, source_target_pairs={{0,1},{1,0},{2,3},{3,2},{4,5},{5,4},{6,7},{7,6},{8,9},{9,8},{10,11... | collective-permute-start | bytes 294920 | tf_op jit(solution)/shard_map/ppermute | solution.py:451
  51.0 2.7 %collective-permute-done.11.rest_0_ = bf16[48,1024]{1,0:T(8,128)(2,1)S(1)} collective-permute-done((bf16[48,1024]{1,0:T(8,128)(2,1)S(1)}, bf16[48,1024]{1,0:T(8,128)(2,1)S(1)}, u32[]{:S(2)}, u32[]{:S(2)}) %collective-permute-start.11) | collective-permute-done | bytes 98336 | tf_op jit(solution)/shard_map/ppermute | solution.py:451
  53.8 3.0 %collective-permute-done.12.rest_1_ = bf16[48,1024]{1,0:T(8,128)(2,1)S(1)} collective-permute-done((bf16[48,1024]{1,0:T(8,128)(2,1)S(1)}, bf16[48,1024]{1,0:T(8,128)(2,1)S(1)}, u32[]{:S(2)}, u32[]{:S(2)}) %collective-permute-start.12) | collective-permute-done | bytes 98336 | tf_op jit(solution)/shard_map/ppermute | solution.py:451
  56.7 0.0 collective-permute-done.13.rest_2_
  56.8 1.6 %collective-permute-start.16 = (bf16[48,1024]{1,0:T(8,128)(2,1)S(1)}, bf16[48,1024]{1,0:T(8,128)(2,1)S(1)}, u32[]{:S(2)}, u32[]{:S(2)}) collective-permute-start(bf16[48,1024]{1,0:T(8,128)(2,1)S(1)} %sum_terms.3.rest_0_), channel_id=1, source_target_pairs={{0,3},{1,2},{2,1},{3,0},{4,7},{5,6},{6,5},{7,4},{8,11},{9,10},{10,... | collective-permute-start | bytes 294920 | tf_op jit(solution)/shard_map/ppermute | solution.py:451
  58.3 0.0 collective-permute-start.15
  58.3 2.9 %collective-permute-start.14 = (bf16[48,1024]{1,0:T(8,128)(2,1)S(1)}, bf16[48,1024]{1,0:T(8,128)(2,1)S(1)}, u32[]{:S(2)}, u32[]{:S(2)}) collective-permute-start(bf16[48,1024]{1,0:T(8,128)(2,1)S(1)} %sum_terms.3.rest_0_), channel_id=1, source_target_pairs={{0,1},{1,0},{2,3},{3,2},{4,5},{5,4},{6,7},{7,6},{8,9},{9,8},{10,11... | collective-permute-start | bytes 294920 | tf_op jit(solution)/shard_map/ppermute | solution.py:451
  61.2 3.6 %write_cache.1 = bf16[48,2,256,128]{3,2,1,0:T(8,128)(2,1)} custom-call(s32[12]{0:T(128)S(1)} %get-tuple-element.23.plan, bf16[54,2,256,128]{3,2,1,0:T(8,128)(2,1)S(1)} %get-tuple-element.43.cache), custom_call_target="tpu_custom_call" | custom-call | bytes 12582912 | tf_op jit(solution)/shard_map/write_cache/pallas_call | solution.py:605
  64.9 0.0 collective-permute-done.16.rest_3_
  64.9 1.9 %collective-permute-done.15.rest_2_ = bf16[48,1024]{1,0:T(8,128)(2,1)S(1)} collective-permute-done((bf16[48,1024]{1,0:T(8,128)(2,1)S(1)}, bf16[48,1024]{1,0:T(8,128)(2,1)S(1)}, u32[]{:S(2)}, u32[]{:S(2)}) %collective-permute-start.15) | collective-permute-done | bytes 98336 | tf_op jit(solution)/shard_map/ppermute | solution.py:451
  66.7 0.0 collective-permute-done.14.rest_1_
  66.7 1.3 %join.1 = bf16[48,4096]{1,0:T(8,128)(2,1)} custom-call(s32[2]{0:T(128)S(1)} %pad_add_fusion.meta, bf16[48,1024]{1,0:T(8,128)(2,1)S(1)} %sum_terms.3.rest_0_, bf16[48,1024]{1,0:T(8,128)(2,1)S(1)} %collective-permute-done.14.rest_1_, bf16[48,1024]{1,0:T(8,128)(2,1)S(1)} %collective-permute-done.15.rest_2_, bf16[48,1024]{1,0:T(8,128)(2,1)S(1)} %collective-permute-done.16.rest_3_), custom_call_target="tpu_custom_call" | custom-call | tf_op jit(solution)/shard_map/join/pallas_call | solution.py:615
  (1 shorter events, 0.0 us)
Async XLA Ops:
  0.7 11.5 %copy-start.7 = (s32[192]{0:T(256)S(1)}, s32[192]{0:T(256)}, u32[]{:S(2)}) copy-start(s32[192]{0:T(256)} %lengths_s.3) | copy-start | bytes 2308
  8.9 6.3 %copy-start.1 = (bf16[512,4096]{1,0:T(8,128)(2,1)S(1)}, bf16[512,4096]{1,0:T(8,128)(2,1)}, u32[]{:S(2)}) copy-start(bf16[512,4096]{1,0:T(8,128)(2,1)} %wo.3) | copy-start | bytes 12582916
  9.0 6.3 %copy-start.3 = (bf16[48,4096]{1,0:T(8,128)(2,1)S(1)}, bf16[48,4096]{1,0:T(8,128)(2,1)}, u32[]{:S(2)}) copy-start(bf16[48,4096]{1,0:T(8,128)(2,1)} %hidden.1) | copy-start | bytes 1179652
  9.0 6.3 %collective-permute-start = (bf16[2,2,272,128]{3,2,1,0:T(8,128)(2,1)S(1)}, bf16[2,2,272,128]{3,2,1,0:T(8,128)(2,1)S(1)}, u32[]{:S(2)}, u32[]{:S(2)}) collective-permute-start(bf16[2,2,272,128]{3,2,1,0:T(8,128)(2,1)S(1)} %get-tuple-element.30), channel_id=1, source_target_pairs={{0,4},{4,0},{8,12},{12,8},{1,5},{5,1},{9,13},{13,9},{2,6},{6,2},{1... | collective-permute-start | bytes 835592 | tf_op jit(solution)/shard_map/ppermute | solution.py:451
  9.5 5.4 %collective-permute-start.1 = (f32[2,1536]{1,0:T(2,128)S(1)}, f32[2,1536]{1,0:T(2,128)S(1)}, u32[]{:S(2)}, u32[]{:S(2)}) collective-permute-start(f32[2,1536]{1,0:T(2,128)S(1)} %get-tuple-element.31), channel_id=1, source_target_pairs={{0,8},{4,12},{8,0},{12,4},{1,9},{5,13},{9,1},{13,5},{2,10},{6,14},... | collective-permute-start | bytes 36872 | tf_op jit(solution)/shard_map/ppermute | solution.py:451
  12.1 3.1 %collective-permute-start.2 = (f32[2,1536]{1,0:T(2,128)S(1)}, f32[2,1536]{1,0:T(2,128)S(1)}, u32[]{:S(2)}, u32[]{:S(2)}) collective-permute-start(f32[2,1536]{1,0:T(2,128)S(1)} %get-tuple-element.32), channel_id=1, source_target_pairs={{0,12},{4,8},{8,4},{12,0},{1,13},{5,9},{9,5},{13,1},{2,14},{6,10},... | collective-permute-start | bytes 36872 | tf_op jit(solution)/shard_map/ppermute | solution.py:451
  15.2 25.7 %copy-start = (bf16[4096,512]{1,0:T(8,128)(2,1)S(1)}, bf16[4096,512]{1,0:T(8,128)(2,1)}, u32[]{:S(2)}) copy-start(bf16[4096,512]{1,0:T(8,128)(2,1)} %wq.1) | copy-start | bytes 12582916
  15.3 25.7 %copy-start.2 = (bf16[4096,2,128]{2,1,0:T(2,128)(2,1)S(1)}, bf16[4096,2,128]{2,1,0:T(2,128)(2,1)}, u32[]{:S(2)}) copy-start(bf16[4096,2,128]{2,1,0:T(2,128)(2,1)} %param.16) | copy-start | bytes 6291460
  15.3 25.7 %copy-start.4 = (f32[256,128]{1,0:T(8,128)S(1)}, f32[256,128]{1,0:T(8,128)}, u32[]{:S(2)}) copy-start(f32[256,128]{1,0:T(8,128)} %constant.12.clone.sin_hbm.sin_ref) | copy-start | bytes 393220
  15.3 25.6 %copy-start.5 = (f32[256,128]{1,0:T(8,128)S(1)}, f32[256,128]{1,0:T(8,128)}, u32[]{:S(2)}) copy-start(f32[256,128]{1,0:T(8,128)} %constant.11.clone.cos_hbm.cos_ref) | copy-start | bytes 393220
  15.3 25.6 %copy-start.6 = (f32[4096]{0:T(1024)S(1)}, f32[4096]{0:T(1024)}, u32[]{:S(2)}) copy-start(f32[4096]{0:T(1024)} %param.14) | copy-start | bytes 49156
  15.3 25.6 %copy-start.8 = (s32[192]{0:T(256)S(1)}, s32[192]{0:T(256)}, u32[]{:S(2)}) copy-start(s32[192]{0:T(256)} %source_s.1) | copy-start | bytes 2308
  16.8 7.6 %collective-permute-start.3 = (bf16[48,1024]{1,0:T(8,128)(2,1)S(1)}, bf16[48,1024]{1,0:T(8,128)(2,1)S(1)}, u32[]{:S(2)}, u32[]{:S(2)}) collective-permute-start(bf16[48,1024]{1,0:T(8,128)(2,1)S(1)} %get-tuple-element.34), channel_id=1, source_target_pairs={{0,3},{1,2},{2,1},{3,0},{4,7},{5,6},{6,5},{7,4},{8,11},{9,10},{10,... | collective-permute-start | bytes 294920 | tf_op jit(solution)/shard_map/ppermute | solution.py:451
  20.4 8.6 %collective-permute-start.4 = (bf16[48,1024]{1,0:T(8,128)(2,1)S(1)}, bf16[48,1024]{1,0:T(8,128)(2,1)S(1)}, u32[]{:S(2)}, u32[]{:S(2)}) collective-permute-start(bf16[48,1024]{1,0:T(8,128)(2,1)S(1)} %get-tuple-element.35), channel_id=1, source_target_pairs={{0,2},{1,3},{2,0},{3,1},{4,6},{5,7},{6,4},{7,5},{8,10},{9,11},{10,... | collective-permute-start | bytes 294920 | tf_op jit(solution)/shard_map/ppermute | solution.py:451
  20.4 8.6 %collective-permute-start.5 = (bf16[48,1024]{1,0:T(8,128)(2,1)S(1)}, bf16[48,1024]{1,0:T(8,128)(2,1)S(1)}, u32[]{:S(2)}, u32[]{:S(2)}) collective-permute-start(bf16[48,1024]{1,0:T(8,128)(2,1)S(1)} %get-tuple-element.36), channel_id=1, source_target_pairs={{0,1},{1,0},{2,3},{3,2},{4,5},{5,4},{6,7},{7,6},{8,9},{9,8},{10,11... | collective-permute-start | bytes 294920 | tf_op jit(solution)/shard_map/ppermute | solution.py:451
  22.5 13.9 %collective-permute-start.9 = (bf16[2,2,256,128]{3,2,1,0:T(8,128)(2,1)S(1)}, bf16[2,2,256,128]{3,2,1,0:T(8,128)(2,1)S(1)}, u32[]{:S(2)}, u32[]{:S(2)}) collective-permute-start(bf16[2,2,256,128]{3,2,1,0:T(8,128)(2,1)S(1)} %get-tuple-element.37), channel_id=1, source_target_pairs={{0,8},{4,12},{8,0},{12,4},{1,9},{5,13},{9,1},{13,5},{2,10},{6,14},... | collective-permute-start | bytes 786440 | tf_op jit(solution)/shard_map/ppermute | solution.py:451
  24.0 12.4 %collective-permute-start.10 = (bf16[2,2,256,128]{3,2,1,0:T(8,128)(2,1)S(1)}, bf16[2,2,256,128]{3,2,1,0:T(8,128)(2,1)S(1)}, u32[]{:S(2)}, u32[]{:S(2)}) collective-permute-start(bf16[2,2,256,128]{3,2,1,0:T(8,128)(2,1)S(1)} %get-tuple-element.38), channel_id=1, source_target_pairs={{0,12},{4,8},{8,4},{12,0},{1,13},{5,9},{9,5},{13,1},{2,14},{6,10},... | collective-permute-start | bytes 786440 | tf_op jit(solution)/shard_map/ppermute | solution.py:451
  29.1 7.2 %collective-permute-start.7 = (bf16[48,1024]{1,0:T(8,128)(2,1)S(1)}, bf16[48,1024]{1,0:T(8,128)(2,1)S(1)}, u32[]{:S(2)}, u32[]{:S(2)}) collective-permute-start(bf16[48,1024]{1,0:T(8,128)(2,1)S(1)} %sum_terms.2.rest_0_), channel_id=1, source_target_pairs={{0,2},{1,3},{2,0},{3,1},{4,6},{5,7},{6,4},{7,5},{8,10},{9,11},{10,... | collective-permute-start | bytes 294920 | tf_op jit(solution)/shard_map/ppermute | solution.py:451
  29.4 7.0 %collective-permute-start.6 = (bf16[48,1024]{1,0:T(8,128)(2,1)S(1)}, bf16[48,1024]{1,0:T(8,128)(2,1)S(1)}, u32[]{:S(2)}, u32[]{:S(2)}) collective-permute-start(bf16[48,1024]{1,0:T(8,128)(2,1)S(1)} %sum_terms.2.rest_0_), channel_id=1, source_target_pairs={{0,1},{1,0},{2,3},{3,2},{4,5},{5,4},{6,7},{7,6},{8,9},{9,8},{10,11... | collective-permute-start | bytes 294920 | tf_op jit(solution)/shard_map/ppermute | solution.py:451
  36.3 4.6 %collective-permute-start.8 = (bf16[48,1024]{1,0:T(8,128)(2,1)S(1)}, bf16[48,1024]{1,0:T(8,128)(2,1)S(1)}, u32[]{:S(2)}, u32[]{:S(2)}) collective-permute-start(bf16[48,1024]{1,0:T(8,128)(2,1)S(1)} %collective-permute-done.7.rest_2_), channel_id=1, source_target_pairs={{0,1},{1,0},{2,3},{3,2},{4,5},{5,4},{6,7},{7,6},{8,9},{9,8},{10,11... | collective-permute-start | bytes 294920 | tf_op jit(solution)/shard_map/ppermute | solution.py:451
  46.6 7.2 %collective-permute-start.11 = (bf16[48,1024]{1,0:T(8,128)(2,1)S(1)}, bf16[48,1024]{1,0:T(8,128)(2,1)S(1)}, u32[]{:S(2)}, u32[]{:S(2)}) collective-permute-start(bf16[48,1024]{1,0:T(8,128)(2,1)S(1)} %get-tuple-element.40), channel_id=1, source_target_pairs={{0,3},{1,2},{2,1},{3,0},{4,7},{5,6},{6,5},{7,4},{8,11},{9,10},{10,... | collective-permute-start | bytes 294920 | tf_op jit(solution)/shard_map/ppermute | solution.py:451
  48.2 8.6 %collective-permute-start.12 = (bf16[48,1024]{1,0:T(8,128)(2,1)S(1)}, bf16[48,1024]{1,0:T(8,128)(2,1)S(1)}, u32[]{:S(2)}, u32[]{:S(2)}) collective-permute-start(bf16[48,1024]{1,0:T(8,128)(2,1)S(1)} %get-tuple-element.41), channel_id=1, source_target_pairs={{0,2},{1,3},{2,0},{3,1},{4,6},{5,7},{6,4},{7,5},{8,10},{9,11},{10,... | collective-permute-start | bytes 294920 | tf_op jit(solution)/shard_map/ppermute | solution.py:451
  48.2 8.6 %collective-permute-start.13 = (bf16[48,1024]{1,0:T(8,128)(2,1)S(1)}, bf16[48,1024]{1,0:T(8,128)(2,1)S(1)}, u32[]{:S(2)}, u32[]{:S(2)}) collective-permute-start(bf16[48,1024]{1,0:T(8,128)(2,1)S(1)} %get-tuple-element.42), channel_id=1, source_target_pairs={{0,1},{1,0},{2,3},{3,2},{4,5},{5,4},{6,7},{7,6},{8,9},{9,8},{10,11... | collective-permute-start | bytes 294920 | tf_op jit(solution)/shard_map/ppermute | solution.py:451
  56.8 8.1 %collective-permute-start.16 = (bf16[48,1024]{1,0:T(8,128)(2,1)S(1)}, bf16[48,1024]{1,0:T(8,128)(2,1)S(1)}, u32[]{:S(2)}, u32[]{:S(2)}) collective-permute-start(bf16[48,1024]{1,0:T(8,128)(2,1)S(1)} %sum_terms.3.rest_0_), channel_id=1, source_target_pairs={{0,3},{1,2},{2,1},{3,0},{4,7},{5,6},{6,5},{7,4},{8,11},{9,10},{10,... | collective-permute-start | bytes 294920 | tf_op jit(solution)/shard_map/ppermute | solution.py:451
  58.3 8.4 %collective-permute-start.15 = (bf16[48,1024]{1,0:T(8,128)(2,1)S(1)}, bf16[48,1024]{1,0:T(8,128)(2,1)S(1)}, u32[]{:S(2)}, u32[]{:S(2)}) collective-permute-start(bf16[48,1024]{1,0:T(8,128)(2,1)S(1)} %sum_terms.3.rest_0_), channel_id=1, source_target_pairs={{0,2},{1,3},{2,0},{3,1},{4,6},{5,7},{6,4},{7,5},{8,10},{9,11},{10,... | collective-permute-start | bytes 294920 | tf_op jit(solution)/shard_map/ppermute | solution.py:451
  58.3 8.4 %collective-permute-start.14 = (bf16[48,1024]{1,0:T(8,128)(2,1)S(1)}, bf16[48,1024]{1,0:T(8,128)(2,1)S(1)}, u32[]{:S(2)}, u32[]{:S(2)}) collective-permute-start(bf16[48,1024]{1,0:T(8,128)(2,1)S(1)} %sum_terms.3.rest_0_), channel_id=1, source_target_pairs={{0,1},{1,0},{2,3},{3,2},{4,5},{5,4},{6,7},{7,6},{8,9},{9,8},{10,11... | collective-permute-start | bytes 294920 | tf_op jit(solution)/shard_map/ppermute | solution.py:451

commit v10 on v9

--- a/solution.py
+++ b/solution.py
@@ -68,29 +68,33 @@
     spread[:, slots:, :] = spread_all[:, 2 * HD :].reshape(blocks, slots, 2 * HD)
 
 
-def project(normed3, spread, wq, wkv, slots, width, wq_copies=(), wkv_copies=()):
-    pieces = max(len(wq_copies), 1)
-    depth = width // pieces
-    query = None
-    pair = None
-    for c in range(pieces):
-        for copy in wkv_copies[c : c + 1]:
-            copy.wait()
-        for b in range(c * depth // HD, (c + 1) * depth // HD):
-            part = jnp.dot(
-                spread[b], wkv[b * 2 * HD : (b + 1) * 2 * HD, :], preferred_element_type=F32
-            )
-            pair = part if pair is None else pair + part
-    for c in range(pieces):
-        for copy in wq_copies[c : c + 1]:
-            copy.wait()
-        for b in range(c * depth // (2 * HD), (c + 1) * depth // (2 * HD)):
-            block = jnp.concatenate([normed3[2 * b], normed3[2 * b + 1]], axis=1)
-            part = jnp.dot(
-                block, wq[b * 2 * HD : (b + 1) * 2 * HD, :], preferred_element_type=F32
-            )
-            query = part if query is None else query + part
-    return query, pair[:slots], pair[slots:]
+def project_from(normed3, weight, copies=()):
+    total = None
+    pairs = normed3.shape[0] // 2
+    pieces = max(len(copies), 1)
+    for b in range(pairs):
+        if copies and b % (pairs // pieces) == 0:
+            copies[b // (pairs // pieces)].wait()
+        block = jnp.concatenate([normed3[2 * b], normed3[2 * b + 1]], axis=1)
+        part = jnp.dot(
+            block, weight[b * 2 * HD : (b + 1) * 2 * HD, :], preferred_element_type=F32
+        )
+        total = part if total is None else total + part
+    return total
+
+
+def project_spread(spread, wkv, copies):
+    total = None
+    blocks = spread.shape[0]
+    for b in range(blocks):
+        if b % (blocks // len(copies)) == 0:
+            copies[b // (blocks // len(copies))].wait()
+        part = jnp.dot(
+            spread[b], wkv[b * 2 * HD : (b + 1) * 2 * HD, :], preferred_element_type=F32
+        )
+        total = part if total is None else total + part
+    slots = spread.shape[1] // 2
+    return total[:slots], total[slots:]
 
 
 def weight_copies(src, dst, sem, pieces):
@@ -166,11 +170,11 @@
     small = [
         pltpu.make_async_copy(src, dst, small_sem.at[i])
         for i, (src, dst) in enumerate((
-            (source_hbm, source_v), (source_hbm, source_s), (lengths_hbm, lengths_s),
-            (hidden_hbm, hidden), (gain_hbm, gain), (cos_hbm, cos_ref), (sin_hbm, sin_ref),
+            (source_hbm, source_v), (source_hbm, source_s), (hidden_hbm, hidden), (gain_hbm, gain),
+            (lengths_hbm, lengths_s), (cos_hbm, cos_ref), (sin_hbm, sin_ref),
         ))
     ]
-    for copy in small + wkv_copies + wq_copies:
+    for copy in small[:4] + wkv_copies + wq_copies + small[4:]:
         copy.start()
     loads = [
         pltpu.make_async_copy(
@@ -178,12 +182,9 @@
         )
         for c in range(slots // CHUNK)
     ]
-    for copy in small:
+    for copy in small[:2]:
         copy.wait()
-    wide = hidden[...].astype(F32)
-    hidden32[...] = wide
-    norm_into(normed3, [wide], [gain[...]], [0], width)
-    spread_normed(normed3, spread, slots, width)
+
     low = me * slots
     src = source_v[...]
     index = lax.broadcasted_iota(I32, src.shape, 1)
@@ -213,10 +214,17 @@
     for copy in loads:
         copy.start()
 
+    for copy in small[2:4]:
+        copy.wait()
+    wide = hidden[...].astype(F32)
+    hidden32[...] = wide
+    norm_into(normed3, [wide], [gain[...]], [0], width)
+    spread_normed(normed3, spread, slots, width)
+    for copy in small[4:]:
+        copy.wait()
     gather_angles(lambda s: lengths_s[0, low + s], slots, cos_ref, sin_ref, cos_rows, sin_rows)
-    query, key, value = project(
-        normed3, spread, wq, wkv, slots, width, wq_copies, wkv_copies
-    )
+    key, value = project_spread(spread, wkv, wkv_copies)
+    query = project_from(normed3, wq, wq_copies)
     cosine, sine = cos_rows[...], sin_rows[...]
     query_out[...] = jnp.zeros(query_out.shape, F32)
     for g in range(heads):
@@ -367,15 +375,35 @@
             place[taker] = slots + at
 
 
+def prepare_kernel(
+    peers, slots, meta, source_s, lengths_s, plan, cos_ref, sin_ref, wkv, _,
+    weight, cos_rows, sin_rows, place,
+):
+    map_places(slots, peers, plan, place)
+    low = meta[0] * slots
+    gather_angles(
+        lambda s: lengths_s[source_s[low + s]] + 1, slots, cos_ref, sin_ref, cos_rows, sin_rows
+    )
+    row = lax.broadcasted_iota(I32, (2 * HD, 2 * HD), 0)
+    col = lax.broadcasted_iota(I32, (2 * HD, 2 * HD), 1)
+    goal = jnp.where(row < HD, 2 * row, 2 * (row - HD) + 1)
+    places = jnp.where(col == goal, 1.0, 0.0).astype(BF16)
+    for b in range(weight.shape[0] // HD):
+        apart = jnp.dot(
+            places, wkv[b * 2 * HD : (b + 1) * 2 * HD, :], preferred_element_type=F32
+        ).astype(BF16)
+        weight[b * HD : (b + 1) * HD, :HD] = apart[:HD]
+        weight[b * HD : (b + 1) * HD, HD:] = apart[HD:]
+
+
 def second_kernel(
     peers, peers_tp, slots, heads,
-    meta, source_s, lengths_s, plan, gain, cos_ref, sin_ref, wq, wkv, wo, _, *rest,
+    meta, source_s, lengths_s, place, gain, cos_rows, sin_rows, wq, wkv, wo, _, *rest,
 ):
     blocks, rest = rest[:peers_tp], rest[peers_tp:]
     box_hbm, rest = rest[: peers - 1], rest[peers - 1 :]
     own, sends, cache = rest[0], rest[1:peers_tp], rest[peers_tp]
-    (normed3, spread, cos_rows, sin_rows, query_rows, attended_rows, place,
-     in_sem) = rest[peers_tp + 1 :]
+    normed3, query_rows, attended_rows, in_sem = rest[peers_tp + 1 :]
     me, me_tp = meta[0], meta[1]
     low = me * slots
     width = gain.shape[1]
@@ -391,7 +419,6 @@
     for copy in loads:
         copy.start()
 
-    map_places(slots, peers, plan, place)
     firsts = [jnp.bitwise_xor(me_tp, k) for k in range(peers_tp)]
     norm_into(
         normed3,
@@ -400,10 +427,10 @@
         [first * (shard // HD) for first in firsts],
         width,
     )
-    spread_normed(normed3, spread, slots, width)
     positions = [lengths_s[source_s[low + s]] + 1 for s in range(slots)]
-    gather_angles(lambda s: positions[s], slots, cos_ref, sin_ref, cos_rows, sin_rows)
-    query, key, value = project(normed3, spread, wq, wkv, slots, width)
+    query = project_from(normed3, wq)
+    pair = project_from(normed3, wkv)
+    key, value = pair[:, :HD], pair[:, HD:]
     cosine, sine = cos_rows[...], sin_rows[...]
     query_rows[...] = jnp.zeros(query_rows.shape, F32)
     for g in range(heads):
@@ -423,8 +450,7 @@
     )
 
 
-def cache_kernel(peers, slots, plan, cache, out_hbm, place, out_sem):
-    map_places(slots, peers, plan, place)
+def cache_kernel(slots, place, cache, out_hbm, out_sem):
     copies = [
         pltpu.make_async_copy(cache.at[place[s]], out_hbm.at[s], out_sem.at[s])
         for s in range(slots)
@@ -582,36 +608,50 @@
 
     pieces = summed(own, sends, True)
 
+    weight, cos_rows, sin_rows, place = pl.pallas_call(
+        functools.partial(prepare_kernel, peers, slots),
+        out_shape=[
+            jax.ShapeDtypeStruct((width, 2 * HD), BF16),
+            row32,
+            row32,
+            jax.ShapeDtypeStruct((slots,), I32),
+        ],
+        in_specs=[SMEM] * 4 + [VMEM] * 3 + [ANY],
+        out_specs=[VMEM] * 3 + [SMEM],
+        compiler_params=params(16),
+        cost_estimate=cost(flops, wkv.size * 4),
+        name="prepare",
+    )(meta, source, lengths, plan, cosine, sine, wkv, own)
+
     own, *sends, cache = pl.pallas_call(
         functools.partial(second_kernel, peers, peers_tp, slots, heads),
         out_shape=sent + [held],
         in_specs=[SMEM] * 4 + [VMEM] * (7 + peers_tp) + [ANY] * others,
         out_specs=[VMEM] * (1 + peers_tp),
-        scratch_shapes=stages
-        + [
+        scratch_shapes=[
+            pltpu.VMEM((blocks, slots, HD), BF16),
             pltpu.VMEM((slots * GROUP, HD), F32),
             pltpu.VMEM((slots * GROUP, HD), F32),
-            pltpu.SMEM((slots,), I32),
             dma((others,)),
         ],
         input_output_aliases={10: peers_tp},
         compiler_params=params(16),
         cost_estimate=cost(3 * flops, cache_bytes + (query_weight.size + wkv.size) * 4),
         name="second_step",
-    )(meta, source, lengths, plan, gain, cosine, sine, query_weight, wkv, out_weight, cache,
+    )(meta, source, lengths, place, gain, cos_rows, sin_rows, query_weight, weight, out_weight, cache,
       *pieces, *got_boxes)
 
     pieces = summed(own, sends, False)
     final_cache = pl.pallas_call(
-        functools.partial(cache_kernel, peers, slots),
+        functools.partial(cache_kernel, slots),
         out_shape=jax.ShapeDtypeStruct(kv_cache.shape, BF16),
         in_specs=[SMEM, VMEM],
         out_specs=ANY,
-        scratch_shapes=[pltpu.SMEM((slots,), I32), dma((slots,))],
+        scratch_shapes=[dma((slots,))],
         compiler_params=params(16),
         cost_estimate=cost(0, 2 * cache_bytes),
         name="write_cache",
-    )(plan, cache)
+    )(place, cache)
     final_hidden = pl.pallas_call(
         functools.partial(join_kernel, peers_tp),
         out_shape=jax.ShapeDtypeStruct(hidden.shape, BF16),

time: 68.3 us -> 67 us (0.981)
  waiting for transfers between devices: 21.7 us -> 19.6 us
  Pallas kernels: 24.3 us -> 25.2 us
    pallas_call x1 -> x2, Pallas kernels: 3.61 us -> 5.77 us  [the longest x1 3.58 us: local(): pl.pallas_call(functools.partial(cache_kernel, slots), out_shape=jax.Shap...]
    ppermute x17, waiting for transfers between devices: 21.7 us -> 19.6 us  [swapped(): return lax.ppermute(x, axis, [(i, i ^ k) for i in range(size)])]
    pallas_call x1, Pallas kernels: 8.23 us -> 7.14 us  [local(): pl.pallas_call(functools.partial(first_kernel, peers, slots, heads, shard...]
  transfers between devices with their start and end apart: 17 -> 17, of which waited for: 9 -> 8; matrix products, arithmetic and copies ran while one was open for 0% -> 0% of each run, Pallas kernels for 11% -> 15%
where the time goes in v10:
time: 67 us; the launch traced here: 66.9 us
  Pallas kernels  25.2 us (38%)
  starting transfers between devices  21.1 us (31%)
  waiting for transfers between devices  19.6 us (29%)
  between operations  0.83 us (1%)
    ppermute x17, starting transfers between devices, swapped(): return lax.ppermute(x, axis, [(i, i ^ k) for i in range(size)])  21.1 us
    ppermute x17, waiting for transfers between devices, swapped(): return lax.ppermute(x, axis, [(i, i ^ k) for i in range(size)])  19.6 us
    pallas_call x1, Pallas kernels, local(): pl.pallas_call(functools.partial(first_kernel, peers, slots, heads, shard...  7.14 us
    pallas_call x1, Pallas kernels, local(): pl.pallas_call(functools.partial(second_kernel, peers, peers_tp, slots, h...  5.54 us
    pallas_call x1, Pallas kernels, local(): pl.pallas_call(functools.partial(cache_kernel, slots), out_shape=jax.Shap...  3.58 us
    pallas_call x1, Pallas kernels, local(): pl.pallas_call(functools.partial(attend_kernel, slots, heads), out_shape=...  2.68 us
    pallas_call x1, Pallas kernels, local(): pl.pallas_call(functools.partial(prepare_kernel, peers, slots), out_shape...  2.19 us
    pallas_call x1, Pallas kernels, local(): pl.pallas_call(functools.partial(out_kernel, peers, peers_tp), out_shape=...  1.43 us
  transfers between devices with their start and end apart: 17, of which 8 were waited for; matrix products, arithmetic and copies ran while one was open for 0% of the time, Pallas kernels for 15%

profile of v10, /device:TPU:0, one launch (start us, length us, event | category | flops | bytes accessed | tf_op | source)
XLA Modules:
  0.0 66.9 jit_solution(7974418918900641858)
XLA Ops:
  0.6 0.1 pad_add_fusion.meta
  0.7 0.0 copy-start.7
  0.7 7.1 %first_step.1 = (f32[384,128]{1,0:T(8,128)S(1)}, f32[48,128]{1,0:T(8,128)S(1)}, f32[48,128]{1,0:T(8,128)S(1)}, s32[12]{0:T(128)S(1)}, bf16[54,2,256,128]{3,2,1,0...) custom-call(s32[2]{0:T(128)S(1)} %pad_add_fusion.meta, ...), custom_call_target="tpu_custom_call" | custom-call | flops 301989888 | bytes 6291456 | tf_op jit(solution)/shard_map/first_step/pallas_call | solution.py:511
  7.9 0.0 copy-start.1
  7.9 0.0 copy-start.3
  7.9 0.5 collective-permute-start
  8.4 2.6 %collective-permute-start.1 = (f32[2,1536]{1,0:T(2,128)S(1)}, f32[2,1536]{1,0:T(2,128)S(1)}, u32[]{:S(2)}, u32[]{:S(2)}) collective-permute-start(f32[2,1536]{1,0:T(2,128)S(1)} %get-tuple-element.34), channel_id=1, source_target_pairs={{0,8},{4,12},{8,0},{12,4},{1,9},{5,13},{9,1},{13,5},{2,10},{6,14},... | collective-permute-start | bytes 36872 | tf_op jit(solution)/shard_map/ppermute | solution.py:477
  11.0 0.1 collective-permute-start.2
  11.1 0.0 copy-done.7
  11.1 2.7 %attention.1 = (bf16[48,512]{1,0:T(8,128)(2,1)S(1)}, bf16[54,2,256,128]{3,2,1,0:T(8,128)(2,1)S(1)}) custom-call(s32[2]{0:T(128)S(1)} %pad_add_fusion.meta, s32[192]{0:T(256)S(1)} %copy-done.7, f32[384,128]{1,0:T(8,128)S(1)} %get-tuple-element.28.query, f32[48,128]{1,0:T(8,128)S(1)} %get-tuple-element.29.newkey, ...), custom_call_target="tpu_custom_call", output_to_operand_aliasing={{1}: (5, {})} | custom-call | flops 25165824 | bytes 6291456 | tf_op jit(solution)/shard_map/attention/pallas_call | solution.py:554
  13.7 0.0 collective-permute-done.1.rest_0_
  13.8 0.3 collective-permute-done.2.rest_1_
  14.1 0.0 collective-permute-done.box_hbm.rest_4_
  14.1 0.0 copy-done.1
  14.1 0.0 copy-done.3
  14.1 0.0 copy-start.2
  14.1 0.0 copy-start.4
  14.1 0.0 copy-start.5
  14.2 0.0 copy-start.8
  14.2 1.4 %out_projection.1 = (f32[48,1024]{1,0:T(8,128)S(1)}, bf16[48,1024]{1,0:T(8,128)(2,1)S(1)}, bf16[48,1024]{1,0:T(8,128)(2,1)S(1)}, bf16[48,1024]{1,0:T(8,128)(2,1)S(1)}) custom-call(s32[2]{0:T(128)S(1)} %pad_add_fusion.meta, s32[12]{0:T(128)S(1)} %get-tuple-element.27.plan, bf16[48,512]{1,0:T(8,128)(2,1)S(1)} %get-tuple-element.32.attended, ...), custom_call_target="tpu_custom_call" | custom-call | flops 201326592 | bytes 4194304 | tf_op jit(solution)/shard_map/out_projection/pallas_call | solution.py:568
  15.6 0.0 copy-start
  15.6 0.0 copy-start.6
  15.6 3.7 %collective-permute-start.3 = (bf16[48,1024]{1,0:T(8,128)(2,1)S(1)}, bf16[48,1024]{1,0:T(8,128)(2,1)S(1)}, u32[]{:S(2)}, u32[]{:S(2)}) collective-permute-start(bf16[48,1024]{1,0:T(8,128)(2,1)S(1)} %get-tuple-element.42), channel_id=1, source_target_pairs={{0,3},{1,2},{2,1},{3,0},{4,7},{5,6},{6,5},{7,4},{8,11},{9,10},{10,... | collective-permute-start | bytes 294920 | tf_op jit(solution)/shard_map/ppermute | solution.py:477
  19.3 0.0 collective-permute-start.4
  19.3 0.8 %collective-permute-start.5 = (bf16[48,1024]{1,0:T(8,128)(2,1)S(1)}, bf16[48,1024]{1,0:T(8,128)(2,1)S(1)}, u32[]{:S(2)}, u32[]{:S(2)}) collective-permute-start(bf16[48,1024]{1,0:T(8,128)(2,1)S(1)} %get-tuple-element.44), channel_id=1, source_target_pairs={{0,1},{1,0},{2,3},{3,2},{4,5},{5,4},{6,7},{7,6},{8,9},{9,8},{10,11... | collective-permute-start | bytes 294920 | tf_op jit(solution)/shard_map/ppermute | solution.py:477
  20.1 1.3 %pack.1 = (bf16[2,2,256,128]{3,2,1,0:T(8,128)(2,1)S(1)}, bf16[2,2,256,128]{3,2,1,0:T(8,128)(2,1)S(1)}) custom-call(s32[12]{0:T(128)S(1)} %get-tuple-element.27.plan, bf16[54,2,256,128]{3,2,1,0:T(8,128)(2,1)S(1)} %get-tuple-element.41.cache._, f32[48,1024]{1,0:T(8,128)S(1)} %get-tuple-element.36._.own._own), custom_call_target="tpu_custom_call" | custom-call | flops 1 | bytes 6291456 | tf_op jit(solution)/shard_map/pack/pallas_call | solution.py:578
  21.4 1.5 %collective-permute-start.9 = (bf16[2,2,256,128]{3,2,1,0:T(8,128)(2,1)S(1)}, bf16[2,2,256,128]{3,2,1,0:T(8,128)(2,1)S(1)}, u32[]{:S(2)}, u32[]{:S(2)}) collective-permute-start(bf16[2,2,256,128]{3,2,1,0:T(8,128)(2,1)S(1)} %get-tuple-element.45), channel_id=1, source_target_pairs={{0,8},{4,12},{8,0},{12,4},{1,9},{5,13},{9,1},{13,5},{2,10},{6,14},... | collective-permute-start | bytes 786440 | tf_op jit(solution)/shard_map/ppermute | solution.py:477
  22.8 0.0 collective-permute-start.10
  22.8 0.4 collective-permute-done.3.rest_0_
  23.2 4.8 %collective-permute-done.4.rest_1_ = bf16[48,1024]{1,0:T(8,128)(2,1)S(1)} collective-permute-done((bf16[48,1024]{1,0:T(8,128)(2,1)S(1)}, bf16[48,1024]{1,0:T(8,128)(2,1)S(1)}, u32[]{:S(2)}, u32[]{:S(2)}) %collective-permute-start.4) | collective-permute-done | bytes 98336 | tf_op jit(solution)/shard_map/ppermute | solution.py:477
  28.0 0.0 collective-permute-done.5.rest_2_
  28.0 0.1 sum_terms.2.rest_0_
  28.0 0.2 collective-permute-start.7
  28.3 2.9 %collective-permute-start.6 = (bf16[48,1024]{1,0:T(8,128)(2,1)S(1)}, bf16[48,1024]{1,0:T(8,128)(2,1)S(1)}, u32[]{:S(2)}, u32[]{:S(2)}) collective-permute-start(bf16[48,1024]{1,0:T(8,128)(2,1)S(1)} %sum_terms.2.rest_0_), channel_id=1, source_target_pairs={{0,1},{1,0},{2,3},{3,2},{4,5},{5,4},{6,7},{7,6},{8,9},{9,8},{10,11... | collective-permute-start | bytes 294920 | tf_op jit(solution)/shard_map/ppermute | solution.py:477
  31.1 4.1 %collective-permute-done.7.rest_2_ = bf16[48,1024]{1,0:T(8,128)(2,1)S(1)} collective-permute-done((bf16[48,1024]{1,0:T(8,128)(2,1)S(1)}, bf16[48,1024]{1,0:T(8,128)(2,1)S(1)}, u32[]{:S(2)}, u32[]{:S(2)}) %collective-permute-start.7) | collective-permute-done | bytes 98336 | tf_op jit(solution)/shard_map/ppermute | solution.py:477
  35.2 0.0 collective-permute-start.8
  35.2 0.0 copy-done.2
  35.2 0.0 copy-done.4
  35.2 0.0 copy-done.5
  35.3 0.0 copy-done.8
  35.3 2.2 %prepare.1 = (bf16[4096,256]{1,0:T(8,128)(2,1)S(1)}, f32[48,128]{1,0:T(8,128)S(1)}, f32[48,128]{1,0:T(8,128)S(1)}, s32[48]{0:T(128)S(1)}) custom-call(s32[2]{0:T(128)S(1)} %pad_add_fusion.meta, s32[192]{0:T(256)S(1)} %copy-done.8, s32[192]{0:T(256)S(1)} %copy-done.7, s32[12]{0:T(128)S(1)} %get-tuple-element.27.plan, f32[256,128]{1,0:T(8,128)S(1)} %copy-done.5, ...), custom_call_target="tpu_custom_call" | custom-call | flops 301989888 | bytes 4194304 | tf_op jit(solution)/shard_map/prepare/pallas_call | solution.py:611
  37.5 0.0 collective-permute-done.6.rest_1_
  37.5 0.0 collective-permute-done.9.rest_5_
  37.5 0.0 collective-permute-done.10.rest_6_
  37.5 2.4 %collective-permute-done.8.rest_3_ = bf16[48,1024]{1,0:T(8,128)(2,1)S(1)} collective-permute-done((bf16[48,1024]{1,0:T(8,128)(2,1)S(1)}, bf16[48,1024]{1,0:T(8,128)(2,1)S(1)}, u32[]{:S(2)}, u32[]{:S(2)}) %collective-permute-start.8) | collective-permute-done | bytes 98336 | tf_op jit(solution)/shard_map/ppermute | solution.py:477
  39.9 0.0 copy-done
  39.9 0.0 copy-done.6
  39.9 5.5 %second_step.1 = (f32[48,1024]{1,0:T(8,128)S(1)}, bf16[48,1024]{1,0:T(8,128)(2,1)S(1)}, bf16[48,1024]{1,0:T(8,128)(2,1)S(1)}, bf16[48,1024]{1,0:T(8,128)(2,1)S(1)}, bf16[54,2,256,128]{3,2,1,0:T(8,128)(2,1)S(1)}) custom-call(s32[2]{0:T(128)S(1)} %pad_add_fusion.meta, s32[192]{0:T(256)S(1)} %copy-done.8, ...), custom_call_target="tpu_custom_call", output_to_operand_aliasing={{4}: (10, {})} | custom-call | flops 905969664 | bytes 18874368 | tf_op jit(solution)/shard_map/second_step/pallas_call | solution.py:626
  45.4 1.6 %collective-permute-start.11 = (bf16[48,1024]{1,0:T(8,128)(2,1)S(1)}, bf16[48,1024]{1,0:T(8,128)(2,1)S(1)}, u32[]{:S(2)}, u32[]{:S(2)}) collective-permute-start(bf16[48,1024]{1,0:T(8,128)(2,1)S(1)} %get-tuple-element.48), channel_id=1, source_target_pairs={{0,3},{1,2},{2,1},{3,0},{4,7},{5,6},{6,5},{7,4},{8,11},{9,10},{10,... | collective-permute-start | bytes 294920 | tf_op jit(solution)/shard_map/ppermute | solution.py:477
  47.0 0.0 collective-permute-start.12
  47.0 2.9 %collective-permute-start.13 = (bf16[48,1024]{1,0:T(8,128)(2,1)S(1)}, bf16[48,1024]{1,0:T(8,128)(2,1)S(1)}, u32[]{:S(2)}, u32[]{:S(2)}) collective-permute-start(bf16[48,1024]{1,0:T(8,128)(2,1)S(1)} %get-tuple-element.50), channel_id=1, source_target_pairs={{0,1},{1,0},{2,3},{3,2},{4,5},{5,4},{6,7},{7,6},{8,9},{9,8},{10,11... | collective-permute-start | bytes 294920 | tf_op jit(solution)/shard_map/ppermute | solution.py:477
  49.9 2.7 %collective-permute-done.11.rest_0_ = bf16[48,1024]{1,0:T(8,128)(2,1)S(1)} collective-permute-done((bf16[48,1024]{1,0:T(8,128)(2,1)S(1)}, bf16[48,1024]{1,0:T(8,128)(2,1)S(1)}, u32[]{:S(2)}, u32[]{:S(2)}) %collective-permute-start.11) | collective-permute-done | bytes 98336 | tf_op jit(solution)/shard_map/ppermute | solution.py:477
  52.6 3.0 %collective-permute-done.12.rest_1_ = bf16[48,1024]{1,0:T(8,128)(2,1)S(1)} collective-permute-done((bf16[48,1024]{1,0:T(8,128)(2,1)S(1)}, bf16[48,1024]{1,0:T(8,128)(2,1)S(1)}, u32[]{:S(2)}, u32[]{:S(2)}) %collective-permute-start.12) | collective-permute-done | bytes 98336 | tf_op jit(solution)/shard_map/ppermute | solution.py:477
  55.6 0.0 collective-permute-done.13.rest_2_
  55.6 1.6 %collective-permute-start.16 = (bf16[48,1024]{1,0:T(8,128)(2,1)S(1)}, bf16[48,1024]{1,0:T(8,128)(2,1)S(1)}, u32[]{:S(2)}, u32[]{:S(2)}) collective-permute-start(bf16[48,1024]{1,0:T(8,128)(2,1)S(1)} %sum_terms.3.rest_0_), channel_id=1, source_target_pairs={{0,3},{1,2},{2,1},{3,0},{4,7},{5,6},{6,5},{7,4},{8,11},{9,10},{10,... | collective-permute-start | bytes 294920 | tf_op jit(solution)/shard_map/ppermute | solution.py:477
  57.2 0.0 collective-permute-start.15
  57.2 2.9 %collective-permute-start.14 = (bf16[48,1024]{1,0:T(8,128)(2,1)S(1)}, bf16[48,1024]{1,0:T(8,128)(2,1)S(1)}, u32[]{:S(2)}, u32[]{:S(2)}) collective-permute-start(bf16[48,1024]{1,0:T(8,128)(2,1)S(1)} %sum_terms.3.rest_0_), channel_id=1, source_target_pairs={{0,1},{1,0},{2,3},{3,2},{4,5},{5,4},{6,7},{7,6},{8,9},{9,8},{10,11... | collective-permute-start | bytes 294920 | tf_op jit(solution)/shard_map/ppermute | solution.py:477
  60.1 3.6 %write_cache.1 = bf16[48,2,256,128]{3,2,1,0:T(8,128)(2,1)} custom-call(s32[48]{0:T(128)S(1)} %get-tuple-element.37.place, bf16[54,2,256,128]{3,2,1,0:T(8,128)(2,1)S(1)} %get-tuple-element.51.cache), custom_call_target="tpu_custom_call" | custom-call | bytes 12582912 | tf_op jit(solution)/shard_map/write_cache/pallas_call | solution.py:645
  63.6 0.0 collective-permute-done.16.rest_3_
  63.7 1.9 %collective-permute-done.15.rest_2_ = bf16[48,1024]{1,0:T(8,128)(2,1)S(1)} collective-permute-done((bf16[48,1024]{1,0:T(8,128)(2,1)S(1)}, bf16[48,1024]{1,0:T(8,128)(2,1)S(1)}, u32[]{:S(2)}, u32[]{:S(2)}) %collective-permute-start.15) | collective-permute-done | bytes 98336 | tf_op jit(solution)/shard_map/ppermute | solution.py:477
  65.6 0.0 collective-permute-done.14.rest_1_
  65.6 1.3 %join.1 = bf16[48,4096]{1,0:T(8,128)(2,1)} custom-call(s32[2]{0:T(128)S(1)} %pad_add_fusion.meta, bf16[48,1024]{1,0:T(8,128)(2,1)S(1)} %sum_terms.3.rest_0_, bf16[48,1024]{1,0:T(8,128)(2,1)S(1)} %collective-permute-done.14.rest_1_, bf16[48,1024]{1,0:T(8,128)(2,1)S(1)} %collective-permute-done.15.rest_2_, bf16[48,1024]{1,0:T(8,128)(2,1)S(1)} %collective-permute-done.16.rest_3_), custom_call_target="tpu_custom_call" | custom-call | tf_op jit(solution)/shard_map/join/pallas_call | solution.py:655
  (1 shorter events, 0.0 us)
Async XLA Ops:
  0.7 10.4 %copy-start.7 = (s32[192]{0:T(256)S(1)}, s32[192]{0:T(256)}, u32[]{:S(2)}) copy-start(s32[192]{0:T(256)} %lengths_s.5) | copy-start | bytes 2308
  7.9 6.3 %copy-start.1 = (bf16[512,4096]{1,0:T(8,128)(2,1)S(1)}, bf16[512,4096]{1,0:T(8,128)(2,1)}, u32[]{:S(2)}) copy-start(bf16[512,4096]{1,0:T(8,128)(2,1)} %wo.3) | copy-start | bytes 12582916
  7.9 6.3 %copy-start.3 = (bf16[48,4096]{1,0:T(8,128)(2,1)S(1)}, bf16[48,4096]{1,0:T(8,128)(2,1)}, u32[]{:S(2)}) copy-start(bf16[48,4096]{1,0:T(8,128)(2,1)} %hidden.1) | copy-start | bytes 1179652
  7.9 6.2 %collective-permute-start = (bf16[2,2,272,128]{3,2,1,0:T(8,128)(2,1)S(1)}, bf16[2,2,272,128]{3,2,1,0:T(8,128)(2,1)S(1)}, u32[]{:S(2)}, u32[]{:S(2)}) collective-permute-start(bf16[2,2,272,128]{3,2,1,0:T(8,128)(2,1)S(1)} %get-tuple-element.33), channel_id=1, source_target_pairs={{0,4},{4,0},{8,12},{12,8},{1,5},{5,1},{9,13},{13,9},{2,6},{6,2},{1... | collective-permute-start | bytes 835592 | tf_op jit(solution)/shard_map/ppermute | solution.py:477
  8.4 5.4 %collective-permute-start.1 = (f32[2,1536]{1,0:T(2,128)S(1)}, f32[2,1536]{1,0:T(2,128)S(1)}, u32[]{:S(2)}, u32[]{:S(2)}) collective-permute-start(f32[2,1536]{1,0:T(2,128)S(1)} %get-tuple-element.34), channel_id=1, source_target_pairs={{0,8},{4,12},{8,0},{12,4},{1,9},{5,13},{9,1},{13,5},{2,10},{6,14},... | collective-permute-start | bytes 36872 | tf_op jit(solution)/shard_map/ppermute | solution.py:477
  11.0 3.1 %collective-permute-start.2 = (f32[2,1536]{1,0:T(2,128)S(1)}, f32[2,1536]{1,0:T(2,128)S(1)}, u32[]{:S(2)}, u32[]{:S(2)}) collective-permute-start(f32[2,1536]{1,0:T(2,128)S(1)} %get-tuple-element.35), channel_id=1, source_target_pairs={{0,12},{4,8},{8,4},{12,0},{1,13},{5,9},{9,5},{13,1},{2,14},{6,10},... | collective-permute-start | bytes 36872 | tf_op jit(solution)/shard_map/ppermute | solution.py:477
  14.1 21.1 %copy-start.2 = (bf16[4096,2,128]{2,1,0:T(2,128)(2,1)S(1)}, bf16[4096,2,128]{2,1,0:T(2,128)(2,1)}, u32[]{:S(2)}) copy-start(bf16[4096,2,128]{2,1,0:T(2,128)(2,1)} %param.16) | copy-start | bytes 6291460
  14.1 21.1 %copy-start.4 = (f32[256,128]{1,0:T(8,128)S(1)}, f32[256,128]{1,0:T(8,128)}, u32[]{:S(2)}) copy-start(f32[256,128]{1,0:T(8,128)} %constant.12.clone.sin_hbm.sin_ref) | copy-start | bytes 393220
  14.1 21.1 %copy-start.5 = (f32[256,128]{1,0:T(8,128)S(1)}, f32[256,128]{1,0:T(8,128)}, u32[]{:S(2)}) copy-start(f32[256,128]{1,0:T(8,128)} %constant.11.clone.cos_hbm.cos_ref) | copy-start | bytes 393220
  14.2 21.1 %copy-start.8 = (s32[192]{0:T(256)S(1)}, s32[192]{0:T(256)}, u32[]{:S(2)}) copy-start(s32[192]{0:T(256)} %source_s.3) | copy-start | bytes 2308
  15.6 24.2 %copy-start = (bf16[4096,512]{1,0:T(8,128)(2,1)S(1)}, bf16[4096,512]{1,0:T(8,128)(2,1)}, u32[]{:S(2)}) copy-start(bf16[4096,512]{1,0:T(8,128)(2,1)} %wq.1) | copy-start | bytes 12582916
  15.6 24.2 %copy-start.6 = (f32[4096]{0:T(1024)S(1)}, f32[4096]{0:T(1024)}, u32[]{:S(2)}) copy-start(f32[4096]{0:T(1024)} %param.14) | copy-start | bytes 49156
  15.6 7.6 %collective-permute-start.3 = (bf16[48,1024]{1,0:T(8,128)(2,1)S(1)}, bf16[48,1024]{1,0:T(8,128)(2,1)S(1)}, u32[]{:S(2)}, u32[]{:S(2)}) collective-permute-start(bf16[48,1024]{1,0:T(8,128)(2,1)S(1)} %get-tuple-element.42), channel_id=1, source_target_pairs={{0,3},{1,2},{2,1},{3,0},{4,7},{5,6},{6,5},{7,4},{8,11},{9,10},{10,... | collective-permute-start | bytes 294920 | tf_op jit(solution)/shard_map/ppermute | solution.py:477
  19.3 8.7 %collective-permute-start.4 = (bf16[48,1024]{1,0:T(8,128)(2,1)S(1)}, bf16[48,1024]{1,0:T(8,128)(2,1)S(1)}, u32[]{:S(2)}, u32[]{:S(2)}) collective-permute-start(bf16[48,1024]{1,0:T(8,128)(2,1)S(1)} %get-tuple-element.43), channel_id=1, source_target_pairs={{0,2},{1,3},{2,0},{3,1},{4,6},{5,7},{6,4},{7,5},{8,10},{9,11},{10,... | collective-permute-start | bytes 294920 | tf_op jit(solution)/shard_map/ppermute | solution.py:477
  19.3 8.7 %collective-permute-start.5 = (bf16[48,1024]{1,0:T(8,128)(2,1)S(1)}, bf16[48,1024]{1,0:T(8,128)(2,1)S(1)}, u32[]{:S(2)}, u32[]{:S(2)}) collective-permute-start(bf16[48,1024]{1,0:T(8,128)(2,1)S(1)} %get-tuple-element.44), channel_id=1, source_target_pairs={{0,1},{1,0},{2,3},{3,2},{4,5},{5,4},{6,7},{7,6},{8,9},{9,8},{10,11... | collective-permute-start | bytes 294920 | tf_op jit(solution)/shard_map/ppermute | solution.py:477
  21.4 16.1 %collective-permute-start.9 = (bf16[2,2,256,128]{3,2,1,0:T(8,128)(2,1)S(1)}, bf16[2,2,256,128]{3,2,1,0:T(8,128)(2,1)S(1)}, u32[]{:S(2)}, u32[]{:S(2)}) collective-permute-start(bf16[2,2,256,128]{3,2,1,0:T(8,128)(2,1)S(1)} %get-tuple-element.45), channel_id=1, source_target_pairs={{0,8},{4,12},{8,0},{12,4},{1,9},{5,13},{9,1},{13,5},{2,10},{6,14},... | collective-permute-start | bytes 786440 | tf_op jit(solution)/shard_map/ppermute | solution.py:477
  22.8 14.7 %collective-permute-start.10 = (bf16[2,2,256,128]{3,2,1,0:T(8,128)(2,1)S(1)}, bf16[2,2,256,128]{3,2,1,0:T(8,128)(2,1)S(1)}, u32[]{:S(2)}, u32[]{:S(2)}) collective-permute-start(bf16[2,2,256,128]{3,2,1,0:T(8,128)(2,1)S(1)} %get-tuple-element.46), channel_id=1, source_target_pairs={{0,12},{4,8},{8,4},{12,0},{1,13},{5,9},{9,5},{13,1},{2,14},{6,10},... | collective-permute-start | bytes 786440 | tf_op jit(solution)/shard_map/ppermute | solution.py:477
  28.0 7.2 %collective-permute-start.7 = (bf16[48,1024]{1,0:T(8,128)(2,1)S(1)}, bf16[48,1024]{1,0:T(8,128)(2,1)S(1)}, u32[]{:S(2)}, u32[]{:S(2)}) collective-permute-start(bf16[48,1024]{1,0:T(8,128)(2,1)S(1)} %sum_terms.2.rest_0_), channel_id=1, source_target_pairs={{0,2},{1,3},{2,0},{3,1},{4,6},{5,7},{6,4},{7,5},{8,10},{9,11},{10,... | collective-permute-start | bytes 294920 | tf_op jit(solution)/shard_map/ppermute | solution.py:477
  28.3 9.2 %collective-permute-start.6 = (bf16[48,1024]{1,0:T(8,128)(2,1)S(1)}, bf16[48,1024]{1,0:T(8,128)(2,1)S(1)}, u32[]{:S(2)}, u32[]{:S(2)}) collective-permute-start(bf16[48,1024]{1,0:T(8,128)(2,1)S(1)} %sum_terms.2.rest_0_), channel_id=1, source_target_pairs={{0,1},{1,0},{2,3},{3,2},{4,5},{5,4},{6,7},{7,6},{8,9},{9,8},{10,11... | collective-permute-start | bytes 294920 | tf_op jit(solution)/shard_map/ppermute | solution.py:477
  35.2 4.6 %collective-permute-start.8 = (bf16[48,1024]{1,0:T(8,128)(2,1)S(1)}, bf16[48,1024]{1,0:T(8,128)(2,1)S(1)}, u32[]{:S(2)}, u32[]{:S(2)}) collective-permute-start(bf16[48,1024]{1,0:T(8,128)(2,1)S(1)} %collective-permute-done.7.rest_2_), channel_id=1, source_target_pairs={{0,1},{1,0},{2,3},{3,2},{4,5},{5,4},{6,7},{7,6},{8,9},{9,8},{10,11... | collective-permute-start | bytes 294920 | tf_op jit(solution)/shard_map/ppermute | solution.py:477
  45.4 7.2 %collective-permute-start.11 = (bf16[48,1024]{1,0:T(8,128)(2,1)S(1)}, bf16[48,1024]{1,0:T(8,128)(2,1)S(1)}, u32[]{:S(2)}, u32[]{:S(2)}) collective-permute-start(bf16[48,1024]{1,0:T(8,128)(2,1)S(1)} %get-tuple-element.48), channel_id=1, source_target_pairs={{0,3},{1,2},{2,1},{3,0},{4,7},{5,6},{6,5},{7,4},{8,11},{9,10},{10,... | collective-permute-start | bytes 294920 | tf_op jit(solution)/shard_map/ppermute | solution.py:477
  47.0 8.6 %collective-permute-start.12 = (bf16[48,1024]{1,0:T(8,128)(2,1)S(1)}, bf16[48,1024]{1,0:T(8,128)(2,1)S(1)}, u32[]{:S(2)}, u32[]{:S(2)}) collective-permute-start(bf16[48,1024]{1,0:T(8,128)(2,1)S(1)} %get-tuple-element.49), channel_id=1, source_target_pairs={{0,2},{1,3},{2,0},{3,1},{4,6},{5,7},{6,4},{7,5},{8,10},{9,11},{10,... | collective-permute-start | bytes 294920 | tf_op jit(solution)/shard_map/ppermute | solution.py:477
  47.0 8.6 %collective-permute-start.13 = (bf16[48,1024]{1,0:T(8,128)(2,1)S(1)}, bf16[48,1024]{1,0:T(8,128)(2,1)S(1)}, u32[]{:S(2)}, u32[]{:S(2)}) collective-permute-start(bf16[48,1024]{1,0:T(8,128)(2,1)S(1)} %get-tuple-element.50), channel_id=1, source_target_pairs={{0,1},{1,0},{2,3},{3,2},{4,5},{5,4},{6,7},{7,6},{8,9},{9,8},{10,11... | collective-permute-start | bytes 294920 | tf_op jit(solution)/shard_map/ppermute | solution.py:477
  55.6 8.0 %collective-permute-start.16 = (bf16[48,1024]{1,0:T(8,128)(2,1)S(1)}, bf16[48,1024]{1,0:T(8,128)(2,1)S(1)}, u32[]{:S(2)}, u32[]{:S(2)}) collective-permute-start(bf16[48,1024]{1,0:T(8,128)(2,1)S(1)} %sum_terms.3.rest_0_), channel_id=1, source_target_pairs={{0,3},{1,2},{2,1},{3,0},{4,7},{5,6},{6,5},{7,4},{8,11},{9,10},{10,... | collective-permute-start | bytes 294920 | tf_op jit(solution)/shard_map/ppermute | solution.py:477
  57.2 8.4 %collective-permute-start.15 = (bf16[48,1024]{1,0:T(8,128)(2,1)S(1)}, bf16[48,1024]{1,0:T(8,128)(2,1)S(1)}, u32[]{:S(2)}, u32[]{:S(2)}) collective-permute-start(bf16[48,1024]{1,0:T(8,128)(2,1)S(1)} %sum_terms.3.rest_0_), channel_id=1, source_target_pairs={{0,2},{1,3},{2,0},{3,1},{4,6},{5,7},{6,4},{7,5},{8,10},{9,11},{10,... | collective-permute-start | bytes 294920 | tf_op jit(solution)/shard_map/ppermute | solution.py:477
  57.2 8.4 %collective-permute-start.14 = (bf16[48,1024]{1,0:T(8,128)(2,1)S(1)}, bf16[48,1024]{1,0:T(8,128)(2,1)S(1)}, u32[]{:S(2)}, u32[]{:S(2)}) collective-permute-start(bf16[48,1024]{1,0:T(8,128)(2,1)S(1)} %sum_terms.3.rest_0_), channel_id=1, source_target_pairs={{0,1},{1,0},{2,3},{3,2},{4,5},{5,4},{6,7},{7,6},{8,9},{9,8},{10,11... | collective-permute-start | bytes 294920 | tf_op jit(solution)/shard_map/ppermute | solution.py:477

commit v11 on v10

--- a/solution.py
+++ b/solution.py
@@ -606,7 +606,7 @@
             far //= 2
         return [blocks[k] for k in range(peers_tp)]
 
-    pieces = summed(own, sends, True)
+    pieces = summed(own, sends, False)
 
     weight, cos_rows, sin_rows, place = pl.pallas_call(
         functools.partial(prepare_kernel, peers, slots),
@@ -619,7 +619,7 @@
         in_specs=[SMEM] * 4 + [VMEM] * 3 + [ANY],
         out_specs=[VMEM] * 3 + [SMEM],
         compiler_params=params(16),
-        cost_estimate=cost(flops, wkv.size * 4),
+        cost_estimate=cost(100*flops, wkv.size * 40),
         name="prepare",
     )(meta, source, lengths, plan, cosine, sine, wkv, own)
 

time: 67 us -> 67.4 us (level)
  starting transfers between devices: 21.1 us -> 22.5 us
  waiting for transfers between devices: 19.6 us -> 18.6 us
    ppermute x17, starting transfers between devices: 21.1 us -> 22.5 us  [swapped(): return lax.ppermute(x, axis, [(i, i ^ k) for i in range(size)])]
    ppermute x17, waiting for transfers between devices: 19.6 us -> 18.6 us  [swapped(): return lax.ppermute(x, axis, [(i, i ^ k) for i in range(size)])]
where the time goes in v11:
time: 67.4 us; the launch traced here: 67.2 us
  Pallas kernels  25.3 us (38%)
  starting transfers between devices  22.5 us (33%)
  waiting for transfers between devices  18.6 us (28%)
  between operations  0.81 us (1%)
    ppermute x17, starting transfers between devices, swapped(): return lax.ppermute(x, axis, [(i, i ^ k) for i in range(size)])  22.5 us
    ppermute x17, waiting for transfers between devices, swapped(): return lax.ppermute(x, axis, [(i, i ^ k) for i in range(size)])  18.6 us
    pallas_call x1, Pallas kernels, local(): pl.pallas_call(functools.partial(first_kernel, peers, slots, heads, shard...  7.14 us
    pallas_call x1, Pallas kernels, local(): pl.pallas_call(functools.partial(second_kernel, peers, peers_tp, slots, h...  5.57 us
    pallas_call x1, Pallas kernels, local(): pl.pallas_call(functools.partial(cache_kernel, slots), out_shape=jax.Shap...  3.58 us
    pallas_call x1, Pallas kernels, local(): pl.pallas_call(functools.partial(attend_kernel, slots, heads), out_shape=...  2.68 us
    pallas_call x1, Pallas kernels, local(): pl.pallas_call(functools.partial(prepare_kernel, peers, slots), out_shape...  2.19 us
    pallas_call x1, Pallas kernels, local(): pl.pallas_call(functools.partial(out_kernel, peers, peers_tp), out_shape=...  1.43 us
  transfers between devices with their start and end apart: 17, of which 8 were waited for; matrix products, arithmetic and copies ran while one was open for 0% of the time, Pallas kernels for 15%

profile of v11, /device:TPU:0, one launch (start us, length us, event | category | flops | bytes accessed | tf_op | source)
XLA Modules:
  0.0 67.2 jit_solution(9861527760750216862)
XLA Ops:
  0.6 0.1 pad_add_fusion.meta
  0.7 0.0 copy-start.7
  0.7 7.1 %first_step.1 = (f32[384,128]{1,0:T(8,128)S(1)}, f32[48,128]{1,0:T(8,128)S(1)}, f32[48,128]{1,0:T(8,128)S(1)}, s32[12]{0:T(128)S(1)}, bf16[54,2,256,128]{3,2,1,0...) custom-call(s32[2]{0:T(128)S(1)} %pad_add_fusion.meta, ...), custom_call_target="tpu_custom_call" | custom-call | flops 301989888 | bytes 6291456 | tf_op jit(solution)/shard_map/first_step/pallas_call | solution.py:511
  7.9 0.0 copy-start.1
  7.9 0.0 copy-start.3
  7.9 0.5 collective-permute-start
  8.4 2.6 %collective-permute-start.1 = (f32[2,1536]{1,0:T(2,128)S(1)}, f32[2,1536]{1,0:T(2,128)S(1)}, u32[]{:S(2)}, u32[]{:S(2)}) collective-permute-start(f32[2,1536]{1,0:T(2,128)S(1)} %get-tuple-element.34), channel_id=1, source_target_pairs={{0,8},{4,12},{8,0},{12,4},{1,9},{5,13},{9,1},{13,5},{2,10},{6,14},... | collective-permute-start | bytes 36872 | tf_op jit(solution)/shard_map/ppermute | solution.py:477
  11.0 0.1 collective-permute-start.2
  11.1 0.0 copy-done.7
  11.1 2.7 %attention.1 = (bf16[48,512]{1,0:T(8,128)(2,1)S(1)}, bf16[54,2,256,128]{3,2,1,0:T(8,128)(2,1)S(1)}) custom-call(s32[2]{0:T(128)S(1)} %pad_add_fusion.meta, s32[192]{0:T(256)S(1)} %copy-done.7, f32[384,128]{1,0:T(8,128)S(1)} %get-tuple-element.28.query, f32[48,128]{1,0:T(8,128)S(1)} %get-tuple-element.29.newkey, ...), custom_call_target="tpu_custom_call", output_to_operand_aliasing={{1}: (5, {})} | custom-call | flops 25165824 | bytes 6291456 | tf_op jit(solution)/shard_map/attention/pallas_call | solution.py:554
  13.7 0.0 collective-permute-done.1.rest_0_
  13.8 0.3 collective-permute-done.2.rest_1_
  14.1 0.0 collective-permute-done.box_hbm.rest_4_
  14.1 0.0 copy-done.1
  14.1 0.0 copy-done.3
  14.1 0.0 copy-start.2
  14.1 0.0 copy-start.4
  14.2 0.0 copy-start.5
  14.2 0.0 copy-start.8
  14.2 1.4 %out_projection.1 = (f32[48,1024]{1,0:T(8,128)S(1)}, bf16[48,1024]{1,0:T(8,128)(2,1)S(1)}, bf16[48,1024]{1,0:T(8,128)(2,1)S(1)}, bf16[48,1024]{1,0:T(8,128)(2,1)S(1)}) custom-call(s32[2]{0:T(128)S(1)} %pad_add_fusion.meta, s32[12]{0:T(128)S(1)} %get-tuple-element.27.plan, bf16[48,512]{1,0:T(8,128)(2,1)S(1)} %get-tuple-element.32.attended, ...), custom_call_target="tpu_custom_call" | custom-call | flops 201326592 | bytes 4194304 | tf_op jit(solution)/shard_map/out_projection/pallas_call | solution.py:568
  15.6 3.7 %collective-permute-start.3 = (bf16[48,1024]{1,0:T(8,128)(2,1)S(1)}, bf16[48,1024]{1,0:T(8,128)(2,1)S(1)}, u32[]{:S(2)}, u32[]{:S(2)}) collective-permute-start(bf16[48,1024]{1,0:T(8,128)(2,1)S(1)} %get-tuple-element.42), channel_id=1, source_target_pairs={{0,3},{1,2},{2,1},{3,0},{4,7},{5,6},{6,5},{7,4},{8,11},{9,10},{10,... | collective-permute-start | bytes 294920 | tf_op jit(solution)/shard_map/ppermute | solution.py:477
  19.3 0.0 collective-permute-start.4
  19.3 0.8 %collective-permute-start.5 = (bf16[48,1024]{1,0:T(8,128)(2,1)S(1)}, bf16[48,1024]{1,0:T(8,128)(2,1)S(1)}, u32[]{:S(2)}, u32[]{:S(2)}) collective-permute-start(bf16[48,1024]{1,0:T(8,128)(2,1)S(1)} %get-tuple-element.44), channel_id=1, source_target_pairs={{0,1},{1,0},{2,3},{3,2},{4,5},{5,4},{6,7},{7,6},{8,9},{9,8},{10,11... | collective-permute-start | bytes 294920 | tf_op jit(solution)/shard_map/ppermute | solution.py:477
  20.1 1.3 %pack.1 = (bf16[2,2,256,128]{3,2,1,0:T(8,128)(2,1)S(1)}, bf16[2,2,256,128]{3,2,1,0:T(8,128)(2,1)S(1)}) custom-call(s32[12]{0:T(128)S(1)} %get-tuple-element.27.plan, bf16[54,2,256,128]{3,2,1,0:T(8,128)(2,1)S(1)} %get-tuple-element.41.cache._, f32[48,1024]{1,0:T(8,128)S(1)} %get-tuple-element.36._.own._own), custom_call_target="tpu_custom_call" | custom-call | flops 1 | bytes 6291456 | tf_op jit(solution)/shard_map/pack/pallas_call | solution.py:578
  21.3 1.5 %collective-permute-start.9 = (bf16[2,2,256,128]{3,2,1,0:T(8,128)(2,1)S(1)}, bf16[2,2,256,128]{3,2,1,0:T(8,128)(2,1)S(1)}, u32[]{:S(2)}, u32[]{:S(2)}) collective-permute-start(bf16[2,2,256,128]{3,2,1,0:T(8,128)(2,1)S(1)} %get-tuple-element.45), channel_id=1, source_target_pairs={{0,8},{4,12},{8,0},{12,4},{1,9},{5,13},{9,1},{13,5},{2,10},{6,14},... | collective-permute-start | bytes 786440 | tf_op jit(solution)/shard_map/ppermute | solution.py:477
  22.8 0.0 collective-permute-start.10
  22.8 0.4 collective-permute-done.3.rest_0_
  23.2 4.8 %collective-permute-done.4.rest_1_ = bf16[48,1024]{1,0:T(8,128)(2,1)S(1)} collective-permute-done((bf16[48,1024]{1,0:T(8,128)(2,1)S(1)}, bf16[48,1024]{1,0:T(8,128)(2,1)S(1)}, u32[]{:S(2)}, u32[]{:S(2)}) %collective-permute-start.4) | collective-permute-done | bytes 98336 | tf_op jit(solution)/shard_map/ppermute | solution.py:477
  27.9 0.0 collective-permute-done.5.rest_2_
  27.9 0.1 sum_terms.2.rest_0_
  28.0 0.0 copy-start
  28.0 0.0 copy-start.6
  28.0 2.5 %collective-permute-start.8 = (bf16[48,1024]{1,0:T(8,128)(2,1)S(1)}, bf16[48,1024]{1,0:T(8,128)(2,1)S(1)}, u32[]{:S(2)}, u32[]{:S(2)}) collective-permute-start(bf16[48,1024]{1,0:T(8,128)(2,1)S(1)} %sum_terms.2.rest_0_), channel_id=1, source_target_pairs={{0,3},{1,2},{2,1},{3,0},{4,7},{5,6},{6,5},{7,4},{8,11},{9,10},{10,... | collective-permute-start | bytes 294920 | tf_op jit(solution)/shard_map/ppermute | solution.py:477
  30.6 0.0 collective-permute-start.7
  30.6 1.9 %collective-permute-start.6 = (bf16[48,1024]{1,0:T(8,128)(2,1)S(1)}, bf16[48,1024]{1,0:T(8,128)(2,1)S(1)}, u32[]{:S(2)}, u32[]{:S(2)}) collective-permute-start(bf16[48,1024]{1,0:T(8,128)(2,1)S(1)} %sum_terms.2.rest_0_), channel_id=1, source_target_pairs={{0,1},{1,0},{2,3},{3,2},{4,5},{5,4},{6,7},{7,6},{8,9},{9,8},{10,11... | collective-permute-start | bytes 294920 | tf_op jit(solution)/shard_map/ppermute | solution.py:477
  32.5 0.0 copy-done.2
  32.5 0.0 copy-done.4
  32.5 0.0 copy-done.5
  32.5 0.0 copy-done.8
  32.5 2.2 %prepare.1 = (bf16[4096,256]{1,0:T(8,128)(2,1)S(1)}, f32[48,128]{1,0:T(8,128)S(1)}, f32[48,128]{1,0:T(8,128)S(1)}, s32[48]{0:T(128)S(1)}) custom-call(s32[2]{0:T(128)S(1)} %pad_add_fusion.meta, s32[192]{0:T(256)S(1)} %copy-done.8, s32[192]{0:T(256)S(1)} %copy-done.7, s32[12]{0:T(128)S(1)} %get-tuple-element.27.plan, f32[256,128]{1,0:T(8,128)S(1)} %copy-done.5, ...), custom_call_target="tpu_custom_call" | custom-call | flops 30198988800 | bytes 41943040 | tf_op jit(solution)/shard_map/prepare/pallas_call | solution.py:611
  34.7 0.9 %collective-permute-done.8.rest_3_ = bf16[48,1024]{1,0:T(8,128)(2,1)S(1)} collective-permute-done((bf16[48,1024]{1,0:T(8,128)(2,1)S(1)}, bf16[48,1024]{1,0:T(8,128)(2,1)S(1)}, u32[]{:S(2)}, u32[]{:S(2)}) %collective-permute-start.8) | collective-permute-done | bytes 98336 | tf_op jit(solution)/shard_map/ppermute | solution.py:477
  35.6 3.4 %collective-permute-done.7.rest_2_ = bf16[48,1024]{1,0:T(8,128)(2,1)S(1)} collective-permute-done((bf16[48,1024]{1,0:T(8,128)(2,1)S(1)}, bf16[48,1024]{1,0:T(8,128)(2,1)S(1)}, u32[]{:S(2)}, u32[]{:S(2)}) %collective-permute-start.7) | collective-permute-done | bytes 98336 | tf_op jit(solution)/shard_map/ppermute | solution.py:477
  39.0 0.0 collective-permute-done.6.rest_1_
  39.0 0.0 collective-permute-done.9.rest_5_
  39.0 0.0 collective-permute-done.10.rest_6_
  39.0 0.0 copy-done
  39.0 0.0 copy-done.6
  39.0 5.6 %second_step.1 = (f32[48,1024]{1,0:T(8,128)S(1)}, bf16[48,1024]{1,0:T(8,128)(2,1)S(1)}, bf16[48,1024]{1,0:T(8,128)(2,1)S(1)}, bf16[48,1024]{1,0:T(8,128)(2,1)S(1)}, bf16[54,2,256,128]{3,2,1,0:T(8,128)(2,1)S(1)}) custom-call(s32[2]{0:T(128)S(1)} %pad_add_fusion.meta, s32[192]{0:T(256)S(1)} %copy-done.8, ...), custom_call_target="tpu_custom_call", output_to_operand_aliasing={{4}: (10, {})} | custom-call | flops 905969664 | bytes 18874368 | tf_op jit(solution)/shard_map/second_step/pallas_call | solution.py:626
  44.6 1.8 %collective-permute-start.11 = (bf16[48,1024]{1,0:T(8,128)(2,1)S(1)}, bf16[48,1024]{1,0:T(8,128)(2,1)S(1)}, u32[]{:S(2)}, u32[]{:S(2)}) collective-permute-start(bf16[48,1024]{1,0:T(8,128)(2,1)S(1)} %get-tuple-element.48), channel_id=1, source_target_pairs={{0,3},{1,2},{2,1},{3,0},{4,7},{5,6},{6,5},{7,4},{8,11},{9,10},{10,... | collective-permute-start | bytes 294920 | tf_op jit(solution)/shard_map/ppermute | solution.py:477
  46.4 0.0 collective-permute-start.12
  46.4 2.6 %collective-permute-start.13 = (bf16[48,1024]{1,0:T(8,128)(2,1)S(1)}, bf16[48,1024]{1,0:T(8,128)(2,1)S(1)}, u32[]{:S(2)}, u32[]{:S(2)}) collective-permute-start(bf16[48,1024]{1,0:T(8,128)(2,1)S(1)} %get-tuple-element.50), channel_id=1, source_target_pairs={{0,1},{1,0},{2,3},{3,2},{4,5},{5,4},{6,7},{7,6},{8,9},{9,8},{10,11... | collective-permute-start | bytes 294920 | tf_op jit(solution)/shard_map/ppermute | solution.py:477
  49.1 3.2 %collective-permute-done.11.rest_0_ = bf16[48,1024]{1,0:T(8,128)(2,1)S(1)} collective-permute-done((bf16[48,1024]{1,0:T(8,128)(2,1)S(1)}, bf16[48,1024]{1,0:T(8,128)(2,1)S(1)}, u32[]{:S(2)}, u32[]{:S(2)}) %collective-permute-start.11) | collective-permute-done | bytes 98336 | tf_op jit(solution)/shard_map/ppermute | solution.py:477
  52.3 2.7 %collective-permute-done.12.rest_1_ = bf16[48,1024]{1,0:T(8,128)(2,1)S(1)} collective-permute-done((bf16[48,1024]{1,0:T(8,128)(2,1)S(1)}, bf16[48,1024]{1,0:T(8,128)(2,1)S(1)}, u32[]{:S(2)}, u32[]{:S(2)}) %collective-permute-start.12) | collective-permute-done | bytes 98336 | tf_op jit(solution)/shard_map/ppermute | solution.py:477
  55.0 0.0 collective-permute-done.13.rest_2_
  55.0 2.2 %collective-permute-start.16 = (bf16[48,1024]{1,0:T(8,128)(2,1)S(1)}, bf16[48,1024]{1,0:T(8,128)(2,1)S(1)}, u32[]{:S(2)}, u32[]{:S(2)}) collective-permute-start(bf16[48,1024]{1,0:T(8,128)(2,1)S(1)} %sum_terms.3.rest_0_), channel_id=1, source_target_pairs={{0,3},{1,2},{2,1},{3,0},{4,7},{5,6},{6,5},{7,4},{8,11},{9,10},{10,... | collective-permute-start | bytes 294920 | tf_op jit(solution)/shard_map/ppermute | solution.py:477
  57.3 0.0 collective-permute-start.15
  57.3 2.2 %collective-permute-start.14 = (bf16[48,1024]{1,0:T(8,128)(2,1)S(1)}, bf16[48,1024]{1,0:T(8,128)(2,1)S(1)}, u32[]{:S(2)}, u32[]{:S(2)}) collective-permute-start(bf16[48,1024]{1,0:T(8,128)(2,1)S(1)} %sum_terms.3.rest_0_), channel_id=1, source_target_pairs={{0,1},{1,0},{2,3},{3,2},{4,5},{5,4},{6,7},{7,6},{8,9},{9,8},{10,11... | collective-permute-start | bytes 294920 | tf_op jit(solution)/shard_map/ppermute | solution.py:477
  59.5 3.6 %write_cache.1 = bf16[48,2,256,128]{3,2,1,0:T(8,128)(2,1)} custom-call(s32[48]{0:T(128)S(1)} %get-tuple-element.37.place, bf16[54,2,256,128]{3,2,1,0:T(8,128)(2,1)S(1)} %get-tuple-element.51.cache), custom_call_target="tpu_custom_call" | custom-call | bytes 12582912 | tf_op jit(solution)/shard_map/write_cache/pallas_call | solution.py:645
  63.1 0.0 collective-permute-done.16.rest_3_
  63.1 2.8 %collective-permute-done.15.rest_2_ = bf16[48,1024]{1,0:T(8,128)(2,1)S(1)} collective-permute-done((bf16[48,1024]{1,0:T(8,128)(2,1)S(1)}, bf16[48,1024]{1,0:T(8,128)(2,1)S(1)}, u32[]{:S(2)}, u32[]{:S(2)}) %collective-permute-start.15) | collective-permute-done | bytes 98336 | tf_op jit(solution)/shard_map/ppermute | solution.py:477
  65.9 0.0 collective-permute-done.14.rest_1_
  65.9 1.3 %join.1 = bf16[48,4096]{1,0:T(8,128)(2,1)} custom-call(s32[2]{0:T(128)S(1)} %pad_add_fusion.meta, bf16[48,1024]{1,0:T(8,128)(2,1)S(1)} %sum_terms.3.rest_0_, bf16[48,1024]{1,0:T(8,128)(2,1)S(1)} %collective-permute-done.14.rest_1_, bf16[48,1024]{1,0:T(8,128)(2,1)S(1)} %collective-permute-done.15.rest_2_, bf16[48,1024]{1,0:T(8,128)(2,1)S(1)} %collective-permute-done.16.rest_3_), custom_call_target="tpu_custom_call" | custom-call | tf_op jit(solution)/shard_map/join/pallas_call | solution.py:655
  (1 shorter events, 0.0 us)
Async XLA Ops:
  0.7 10.4 %copy-start.7 = (s32[192]{0:T(256)S(1)}, s32[192]{0:T(256)}, u32[]{:S(2)}) copy-start(s32[192]{0:T(256)} %lengths_s.5) | copy-start | bytes 2308
  7.9 6.3 %copy-start.1 = (bf16[512,4096]{1,0:T(8,128)(2,1)S(1)}, bf16[512,4096]{1,0:T(8,128)(2,1)}, u32[]{:S(2)}) copy-start(bf16[512,4096]{1,0:T(8,128)(2,1)} %wo.3) | copy-start | bytes 12582916
  7.9 6.3 %copy-start.3 = (bf16[48,4096]{1,0:T(8,128)(2,1)S(1)}, bf16[48,4096]{1,0:T(8,128)(2,1)}, u32[]{:S(2)}) copy-start(bf16[48,4096]{1,0:T(8,128)(2,1)} %hidden.1) | copy-start | bytes 1179652
  7.9 6.2 %collective-permute-start = (bf16[2,2,272,128]{3,2,1,0:T(8,128)(2,1)S(1)}, bf16[2,2,272,128]{3,2,1,0:T(8,128)(2,1)S(1)}, u32[]{:S(2)}, u32[]{:S(2)}) collective-permute-start(bf16[2,2,272,128]{3,2,1,0:T(8,128)(2,1)S(1)} %get-tuple-element.33), channel_id=1, source_target_pairs={{0,4},{4,0},{8,12},{12,8},{1,5},{5,1},{9,13},{13,9},{2,6},{6,2},{1... | collective-permute-start | bytes 835592 | tf_op jit(solution)/shard_map/ppermute | solution.py:477
  8.4 5.4 %collective-permute-start.1 = (f32[2,1536]{1,0:T(2,128)S(1)}, f32[2,1536]{1,0:T(2,128)S(1)}, u32[]{:S(2)}, u32[]{:S(2)}) collective-permute-start(f32[2,1536]{1,0:T(2,128)S(1)} %get-tuple-element.34), channel_id=1, source_target_pairs={{0,8},{4,12},{8,0},{12,4},{1,9},{5,13},{9,1},{13,5},{2,10},{6,14},... | collective-permute-start | bytes 36872 | tf_op jit(solution)/shard_map/ppermute | solution.py:477
  11.0 3.1 %collective-permute-start.2 = (f32[2,1536]{1,0:T(2,128)S(1)}, f32[2,1536]{1,0:T(2,128)S(1)}, u32[]{:S(2)}, u32[]{:S(2)}) collective-permute-start(f32[2,1536]{1,0:T(2,128)S(1)} %get-tuple-element.35), channel_id=1, source_target_pairs={{0,12},{4,8},{8,4},{12,0},{1,13},{5,9},{9,5},{13,1},{2,14},{6,10},... | collective-permute-start | bytes 36872 | tf_op jit(solution)/shard_map/ppermute | solution.py:477
  14.1 18.4 %copy-start.2 = (bf16[4096,2,128]{2,1,0:T(2,128)(2,1)S(1)}, bf16[4096,2,128]{2,1,0:T(2,128)(2,1)}, u32[]{:S(2)}) copy-start(bf16[4096,2,128]{2,1,0:T(2,128)(2,1)} %param.16) | copy-start | bytes 6291460
  14.1 18.4 %copy-start.4 = (f32[256,128]{1,0:T(8,128)S(1)}, f32[256,128]{1,0:T(8,128)}, u32[]{:S(2)}) copy-start(f32[256,128]{1,0:T(8,128)} %constant.12.clone.sin_hbm.sin_ref) | copy-start | bytes 393220
  14.2 18.3 %copy-start.5 = (f32[256,128]{1,0:T(8,128)S(1)}, f32[256,128]{1,0:T(8,128)}, u32[]{:S(2)}) copy-start(f32[256,128]{1,0:T(8,128)} %constant.11.clone.cos_hbm.cos_ref) | copy-start | bytes 393220
  14.2 18.3 %copy-start.8 = (s32[192]{0:T(256)S(1)}, s32[192]{0:T(256)}, u32[]{:S(2)}) copy-start(s32[192]{0:T(256)} %source_s.3) | copy-start | bytes 2308
  15.6 7.6 %collective-permute-start.3 = (bf16[48,1024]{1,0:T(8,128)(2,1)S(1)}, bf16[48,1024]{1,0:T(8,128)(2,1)S(1)}, u32[]{:S(2)}, u32[]{:S(2)}) collective-permute-start(bf16[48,1024]{1,0:T(8,128)(2,1)S(1)} %get-tuple-element.42), channel_id=1, source_target_pairs={{0,3},{1,2},{2,1},{3,0},{4,7},{5,6},{6,5},{7,4},{8,11},{9,10},{10,... | collective-permute-start | bytes 294920 | tf_op jit(solution)/shard_map/ppermute | solution.py:477
  19.3 8.7 %collective-permute-start.4 = (bf16[48,1024]{1,0:T(8,128)(2,1)S(1)}, bf16[48,1024]{1,0:T(8,128)(2,1)S(1)}, u32[]{:S(2)}, u32[]{:S(2)}) collective-permute-start(bf16[48,1024]{1,0:T(8,128)(2,1)S(1)} %get-tuple-element.43), channel_id=1, source_target_pairs={{0,2},{1,3},{2,0},{3,1},{4,6},{5,7},{6,4},{7,5},{8,10},{9,11},{10,... | collective-permute-start | bytes 294920 | tf_op jit(solution)/shard_map/ppermute | solution.py:477
  19.3 8.7 %collective-permute-start.5 = (bf16[48,1024]{1,0:T(8,128)(2,1)S(1)}, bf16[48,1024]{1,0:T(8,128)(2,1)S(1)}, u32[]{:S(2)}, u32[]{:S(2)}) collective-permute-start(bf16[48,1024]{1,0:T(8,128)(2,1)S(1)} %get-tuple-element.44), channel_id=1, source_target_pairs={{0,1},{1,0},{2,3},{3,2},{4,5},{5,4},{6,7},{7,6},{8,9},{9,8},{10,11... | collective-permute-start | bytes 294920 | tf_op jit(solution)/shard_map/ppermute | solution.py:477
  21.3 17.7 %collective-permute-start.9 = (bf16[2,2,256,128]{3,2,1,0:T(8,128)(2,1)S(1)}, bf16[2,2,256,128]{3,2,1,0:T(8,128)(2,1)S(1)}, u32[]{:S(2)}, u32[]{:S(2)}) collective-permute-start(bf16[2,2,256,128]{3,2,1,0:T(8,128)(2,1)S(1)} %get-tuple-element.45), channel_id=1, source_target_pairs={{0,8},{4,12},{8,0},{12,4},{1,9},{5,13},{9,1},{13,5},{2,10},{6,14},... | collective-permute-start | bytes 786440 | tf_op jit(solution)/shard_map/ppermute | solution.py:477
  22.8 16.2 %collective-permute-start.10 = (bf16[2,2,256,128]{3,2,1,0:T(8,128)(2,1)S(1)}, bf16[2,2,256,128]{3,2,1,0:T(8,128)(2,1)S(1)}, u32[]{:S(2)}, u32[]{:S(2)}) collective-permute-start(bf16[2,2,256,128]{3,2,1,0:T(8,128)(2,1)S(1)} %get-tuple-element.46), channel_id=1, source_target_pairs={{0,12},{4,8},{8,4},{12,0},{1,13},{5,9},{9,5},{13,1},{2,14},{6,10},... | collective-permute-start | bytes 786440 | tf_op jit(solution)/shard_map/ppermute | solution.py:477
  28.0 11.0 %copy-start = (bf16[4096,512]{1,0:T(8,128)(2,1)S(1)}, bf16[4096,512]{1,0:T(8,128)(2,1)}, u32[]{:S(2)}) copy-start(bf16[4096,512]{1,0:T(8,128)(2,1)} %wq.1) | copy-start | bytes 12582916
  28.0 11.0 %copy-start.6 = (f32[4096]{0:T(1024)S(1)}, f32[4096]{0:T(1024)}, u32[]{:S(2)}) copy-start(f32[4096]{0:T(1024)} %param.14) | copy-start | bytes 49156
  28.0 7.6 %collective-permute-start.8 = (bf16[48,1024]{1,0:T(8,128)(2,1)S(1)}, bf16[48,1024]{1,0:T(8,128)(2,1)S(1)}, u32[]{:S(2)}, u32[]{:S(2)}) collective-permute-start(bf16[48,1024]{1,0:T(8,128)(2,1)S(1)} %sum_terms.2.rest_0_), channel_id=1, source_target_pairs={{0,3},{1,2},{2,1},{3,0},{4,7},{5,6},{6,5},{7,4},{8,11},{9,10},{10,... | collective-permute-start | bytes 294920 | tf_op jit(solution)/shard_map/ppermute | solution.py:477
  30.6 8.4 %collective-permute-start.7 = (bf16[48,1024]{1,0:T(8,128)(2,1)S(1)}, bf16[48,1024]{1,0:T(8,128)(2,1)S(1)}, u32[]{:S(2)}, u32[]{:S(2)}) collective-permute-start(bf16[48,1024]{1,0:T(8,128)(2,1)S(1)} %sum_terms.2.rest_0_), channel_id=1, source_target_pairs={{0,2},{1,3},{2,0},{3,1},{4,6},{5,7},{6,4},{7,5},{8,10},{9,11},{10,... | collective-permute-start | bytes 294920 | tf_op jit(solution)/shard_map/ppermute | solution.py:477
  30.6 8.4 %collective-permute-start.6 = (bf16[48,1024]{1,0:T(8,128)(2,1)S(1)}, bf16[48,1024]{1,0:T(8,128)(2,1)S(1)}, u32[]{:S(2)}, u32[]{:S(2)}) collective-permute-start(bf16[48,1024]{1,0:T(8,128)(2,1)S(1)} %sum_terms.2.rest_0_), channel_id=1, source_target_pairs={{0,1},{1,0},{2,3},{3,2},{4,5},{5,4},{6,7},{7,6},{8,9},{9,8},{10,11... | collective-permute-start | bytes 294920 | tf_op jit(solution)/shard_map/ppermute | solution.py:477
  44.6 7.7 %collective-permute-start.11 = (bf16[48,1024]{1,0:T(8,128)(2,1)S(1)}, bf16[48,1024]{1,0:T(8,128)(2,1)S(1)}, u32[]{:S(2)}, u32[]{:S(2)}) collective-permute-start(bf16[48,1024]{1,0:T(8,128)(2,1)S(1)} %get-tuple-element.48), channel_id=1, source_target_pairs={{0,3},{1,2},{2,1},{3,0},{4,7},{5,6},{6,5},{7,4},{8,11},{9,10},{10,... | collective-permute-start | bytes 294920 | tf_op jit(solution)/shard_map/ppermute | solution.py:477
  46.4 8.6 %collective-permute-start.12 = (bf16[48,1024]{1,0:T(8,128)(2,1)S(1)}, bf16[48,1024]{1,0:T(8,128)(2,1)S(1)}, u32[]{:S(2)}, u32[]{:S(2)}) collective-permute-start(bf16[48,1024]{1,0:T(8,128)(2,1)S(1)} %get-tuple-element.49), channel_id=1, source_target_pairs={{0,2},{1,3},{2,0},{3,1},{4,6},{5,7},{6,4},{7,5},{8,10},{9,11},{10,... | collective-permute-start | bytes 294920 | tf_op jit(solution)/shard_map/ppermute | solution.py:477
  46.4 8.6 %collective-permute-start.13 = (bf16[48,1024]{1,0:T(8,128)(2,1)S(1)}, bf16[48,1024]{1,0:T(8,128)(2,1)S(1)}, u32[]{:S(2)}, u32[]{:S(2)}) collective-permute-start(bf16[48,1024]{1,0:T(8,128)(2,1)S(1)} %get-tuple-element.50), channel_id=1, source_target_pairs={{0,1},{1,0},{2,3},{3,2},{4,5},{5,4},{6,7},{7,6},{8,9},{9,8},{10,11... | collective-permute-start | bytes 294920 | tf_op jit(solution)/shard_map/ppermute | solution.py:477
  55.0 8.0 %collective-permute-start.16 = (bf16[48,1024]{1,0:T(8,128)(2,1)S(1)}, bf16[48,1024]{1,0:T(8,128)(2,1)S(1)}, u32[]{:S(2)}, u32[]{:S(2)}) collective-permute-start(bf16[48,1024]{1,0:T(8,128)(2,1)S(1)} %sum_terms.3.rest_0_), channel_id=1, source_target_pairs={{0,3},{1,2},{2,1},{3,0},{4,7},{5,6},{6,5},{7,4},{8,11},{9,10},{10,... | collective-permute-start | bytes 294920 | tf_op jit(solution)/shard_map/ppermute | solution.py:477
  57.3 8.7 %collective-permute-start.15 = (bf16[48,1024]{1,0:T(8,128)(2,1)S(1)}, bf16[48,1024]{1,0:T(8,128)(2,1)S(1)}, u32[]{:S(2)}, u32[]{:S(2)}) collective-permute-start(bf16[48,1024]{1,0:T(8,128)(2,1)S(1)} %sum_terms.3.rest_0_), channel_id=1, source_target_pairs={{0,2},{1,3},{2,0},{3,1},{4,6},{5,7},{6,4},{7,5},{8,10},{9,11},{10,... | collective-permute-start | bytes 294920 | tf_op jit(solution)/shard_map/ppermute | solution.py:477
  57.3 8.7 %collective-permute-start.14 = (bf16[48,1024]{1,0:T(8,128)(2,1)S(1)}, bf16[48,1024]{1,0:T(8,128)(2,1)S(1)}, u32[]{:S(2)}, u32[]{:S(2)}) collective-permute-start(bf16[48,1024]{1,0:T(8,128)(2,1)S(1)} %sum_terms.3.rest_0_), channel_id=1, source_target_pairs={{0,1},{1,0},{2,3},{3,2},{4,5},{5,4},{6,7},{7,6},{8,9},{9,8},{10,11... | collective-permute-start | bytes 294920 | tf_op jit(solution)/shard_map/ppermute | solution.py:477

commit v12 on v11

--- a/solution.py
+++ b/solution.py
@@ -160,8 +160,8 @@
     others = peers - 1
     moving = others * MOVE
     cache, box, notes = rest[0], rest[1], (None,) + rest[2 : others + 1]
-    (wq, wkv, normed3, spread, cos_rows, sin_rows, leaving, hidden32, source_s, lengths_s, source_v,
-     hidden, gain, cos_ref, sin_ref, tail, small_sem, wq_sem, wkv_sem, in_sem,
+    (wq, wkv, normed3, spread, cos_rows, sin_rows, hidden32, source_s, lengths_s, source_v,
+     hidden, gain, cos_ref, sin_ref, small_sem, wq_sem, wkv_sem,
      box_sem, cache_sem) = rest[others + 1 :]
     width = hidden.shape[1]
     me, me_tp = meta[0], meta[1]
@@ -174,14 +174,14 @@
             (lengths_hbm, lengths_s), (cos_hbm, cos_ref), (sin_hbm, sin_ref),
         ))
     ]
-    for copy in small[:4] + wkv_copies + wq_copies + small[4:]:
-        copy.start()
     loads = [
         pltpu.make_async_copy(
             cache_hbm.at[pl.ds(c * CHUNK, CHUNK)], cache.at[pl.ds(c * CHUNK, CHUNK)], cache_sem.at[c]
         )
         for c in range(slots // CHUNK)
     ]
+    for copy in small[:4] + wkv_copies + wq_copies + small[4:] + loads:
+        copy.start()
     for copy in small[:2]:
         copy.wait()
 
@@ -210,9 +210,6 @@
             send_slots.append(slot)
             plan[at] = jnp.where((r >= 0) & (r < src.shape[1]), r - low, -1)
             plan[moving + at] = slot
-            pltpu.make_async_copy(cache_hbm.at[slot], leaving.at[at], in_sem.at[at]).start()
-    for copy in loads:
-        copy.start()
 
     for copy in small[2:4]:
         copy.wait()
@@ -234,21 +231,19 @@
     newvalue_out[...] = value.astype(BF16).astype(F32)
 
     positions = [lengths_s[0, low + slot] for slot in send_slots]
-    for at, slot in enumerate(send_slots):
-        pltpu.make_async_copy(cache_hbm.at[slot], leaving.at[at], in_sem.at[at]).wait()
-        put_row(
-            leaving, at, positions[at],
-            newkey_out[pl.ds(slot, 1), :], newvalue_out[pl.ds(slot, 1), :],
-        )
-    cap = leaving.shape[2]
+    for copy in loads:
+        copy.wait()
+    for slot, p in zip(send_slots, positions):
+        put_row(cache, slot, p, newkey_out[pl.ds(slot, 1), :], newvalue_out[pl.ds(slot, 1), :])
+    cap = cache.shape[2]
     copies = [
-        pltpu.make_async_copy(
-            leaving.at[pl.ds(0, MOVE)], box.at[:, :, pl.ds(0, cap), :], box_sem.at[0]
-        )
-    ]
-    copies[0].start()
+        pltpu.make_async_copy(cache.at[slot], box.at[m, :, pl.ds(0, cap), :], box_sem.at[m])
+        for m, slot in enumerate(send_slots[:MOVE])
+    ]
+    for copy in copies:
+        copy.start()
     rows = [query_out[pl.ds(pl.multiple_of(slot * GROUP, GROUP), GROUP), :] for slot in send_slots]
-    attended = attend(leaving, list(range(moving)), positions, rows)
+    attended = attend(cache, send_slots, positions, rows)
     column = pl.multiple_of(me_tp * shard, shard)
     for at, slot in enumerate(send_slots):
         m = at % MOVE
@@ -257,19 +252,13 @@
             blocks = [attended[at][g : g + 1, :] for g in range(heads)]
             blocks += [residual[:, b * HD : (b + 1) * HD] for b in range(shard // HD)]
             blocks += [jnp.zeros((1, HD), F32)] * (NOTE - len(blocks))
-            tail[m] = jnp.concatenate(blocks, axis=0).astype(BF16)
-            copies.append(
-                pltpu.make_async_copy(
-                    tail.at[m], box.at[m, 0, pl.ds(cap, NOTE), :], box_sem.at[1 + m]
-                )
-            )
-            copies[-1].start()
+            box[m, 0, cap : cap + NOTE, :] = jnp.concatenate(blocks, axis=0).astype(BF16)
         else:
             note = notes[at // MOVE]
             for g in range(heads):
                 note[m : m + 1, g * HD : (g + 1) * HD] = attended[at][g : g + 1, :]
             note[m : m + 1, heads * HD :] = residual
-    for copy in copies + loads:
+    for copy in copies:
         copy.wait()
 
 
@@ -520,11 +509,10 @@
         + [jax.ShapeDtypeStruct((MOVE, 2, cap + NOTE, HD), BF16)]
         + [jax.ShapeDtypeStruct((MOVE, note_width), F32)] * (others - 1),
         in_specs=[SMEM] + [HBM] * 9,
-        out_specs=[VMEM] * 3 + [SMEM, VMEM, ANY] + [VMEM] * (others - 1),
+        out_specs=[VMEM] * 3 + [SMEM] + [VMEM] * (others + 1),
         scratch_shapes=weights
         + stages
         + [
-            pltpu.VMEM((moving,) + kv_cache.shape[1:], BF16),
             pltpu.VMEM((slots, width), F32),
             pltpu.SMEM((1, source.shape[0]), I32),
             pltpu.SMEM((1, source.shape[0]), I32),
@@ -533,12 +521,10 @@
             pltpu.VMEM((1, width), F32),
             pltpu.VMEM(cosine.shape, F32),
             pltpu.VMEM(cosine.shape, F32),
-            pltpu.VMEM((MOVE, NOTE, HD), BF16),
             dma((7,)),
             dma((4,)),
             dma((4,)),
-            dma((moving,)),
-            dma((1 + MOVE,)),
+            dma((MOVE,)),
             dma((slots // CHUNK,)),
         ],
         compiler_params=params(24),

time: 67.4 us -> 68.9 us (1.022)
  Pallas kernels: 25.3 us -> 26.7 us
    pallas_call x1, Pallas kernels: 7.14 us -> 8.6 us  [local(): pl.pallas_call(functools.partial(first_kernel, peers, slots, heads, shard...]
  transfers between devices with their start and end apart: 17 -> 17, of which waited for: 8 -> 8; matrix products, arithmetic and copies ran while one was open for 0% -> 0% of each run, Pallas kernels for 15% -> 14%
where the time goes in v12:
time: 68.9 us; the launch traced here: 68.7 us
  Pallas kernels  26.7 us (39%)
  starting transfers between devices  22.5 us (33%)
  waiting for transfers between devices  18.6 us (27%)
  between operations  0.81 us (1%)
    ppermute x17, starting transfers between devices, swapped(): return lax.ppermute(x, axis, [(i, i ^ k) for i in range(size)])  22.5 us
    ppermute x17, waiting for transfers between devices, swapped(): return lax.ppermute(x, axis, [(i, i ^ k) for i in range(size)])  18.6 us
    pallas_call x1, Pallas kernels, local(): pl.pallas_call(functools.partial(first_kernel, peers, slots, heads, shard...  8.6 us
    pallas_call x1, Pallas kernels, local(): pl.pallas_call(functools.partial(second_kernel, peers, peers_tp, slots, h...  5.58 us
    pallas_call x1, Pallas kernels, local(): pl.pallas_call(functools.partial(cache_kernel, slots), out_shape=jax.Shap...  3.58 us
    pallas_call x1, Pallas kernels, local(): pl.pallas_call(functools.partial(attend_kernel, slots, heads), out_shape=...  2.68 us
    pallas_call x1, Pallas kernels, local(): pl.pallas_call(functools.partial(prepare_kernel, peers, slots), out_shape...  2.19 us
    pallas_call x1, Pallas kernels, local(): pl.pallas_call(functools.partial(out_kernel, peers, peers_tp), out_shape=...  1.43 us
  transfers between devices with their start and end apart: 17, of which 8 were waited for; matrix products, arithmetic and copies ran while one was open for 0% of the time, Pallas kernels for 14%

profile of v12, /device:TPU:0, one launch (start us, length us, event | category | flops | bytes accessed | tf_op | source)
XLA Modules:
  0.0 68.7 jit_solution(1507837328183650394)
XLA Ops:
  0.6 0.1 pad_add_fusion.meta
  0.7 0.0 copy-start.7
  0.7 8.6 %first_step.1 = (f32[384,128]{1,0:T(8,128)S(1)}, f32[48,128]{1,0:T(8,128)S(1)}, f32[48,128]{1,0:T(8,128)S(1)}, s32[12]{0:T(128)S(1)}, bf16[54,2,256,128]{3,2,1,0...) custom-call(s32[2]{0:T(128)S(1)} %pad_add_fusion.meta, ...), custom_call_target="tpu_custom_call" | custom-call | flops 301989888 | bytes 6291456 | tf_op jit(solution)/shard_map/first_step/pallas_call | solution.py:500
  9.3 0.0 copy-start.1
  9.3 0.0 copy-start.3
  9.3 0.5 collective-permute-start
  9.9 2.6 %collective-permute-start.1 = (f32[2,1536]{1,0:T(2,128)S(1)}, f32[2,1536]{1,0:T(2,128)S(1)}, u32[]{:S(2)}, u32[]{:S(2)}) collective-permute-start(f32[2,1536]{1,0:T(2,128)S(1)} %get-tuple-element.34), channel_id=1, source_target_pairs={{0,8},{4,12},{8,0},{12,4},{1,9},{5,13},{9,1},{13,5},{2,10},{6,14},... | collective-permute-start | bytes 36872 | tf_op jit(solution)/shard_map/ppermute | solution.py:466
  12.5 0.1 collective-permute-start.2
  12.5 0.0 copy-done.7
  12.5 2.7 %attention.1 = (bf16[48,512]{1,0:T(8,128)(2,1)S(1)}, bf16[54,2,256,128]{3,2,1,0:T(8,128)(2,1)S(1)}) custom-call(s32[2]{0:T(128)S(1)} %pad_add_fusion.meta, s32[192]{0:T(256)S(1)} %copy-done.7, f32[384,128]{1,0:T(8,128)S(1)} %get-tuple-element.28.query, f32[48,128]{1,0:T(8,128)S(1)} %get-tuple-element.29.newkey, ...), custom_call_target="tpu_custom_call", output_to_operand_aliasing={{1}: (5, {})} | custom-call | flops 25165824 | bytes 6291456 | tf_op jit(solution)/shard_map/attention/pallas_call | solution.py:540
  15.2 0.0 collective-permute-done.1.rest_0_
  15.2 0.3 collective-permute-done.2.rest_1_
  15.6 0.0 collective-permute-done.box_hbm.rest_4_
  15.6 0.0 copy-done.1
  15.6 0.0 copy-done.3
  15.6 0.0 copy-start.2
  15.6 0.0 copy-start.4
  15.6 0.0 copy-start.5
  15.6 0.0 copy-start.8
  15.6 1.4 %out_projection.1 = (f32[48,1024]{1,0:T(8,128)S(1)}, bf16[48,1024]{1,0:T(8,128)(2,1)S(1)}, bf16[48,1024]{1,0:T(8,128)(2,1)S(1)}, bf16[48,1024]{1,0:T(8,128)(2,1)S(1)}) custom-call(s32[2]{0:T(128)S(1)} %pad_add_fusion.meta, s32[12]{0:T(128)S(1)} %get-tuple-element.27.plan, bf16[48,512]{1,0:T(8,128)(2,1)S(1)} %get-tuple-element.32.attended, ...), custom_call_target="tpu_custom_call" | custom-call | flops 201326592 | bytes 4194304 | tf_op jit(solution)/shard_map/out_projection/pallas_call | solution.py:554
  17.1 3.7 %collective-permute-start.3 = (bf16[48,1024]{1,0:T(8,128)(2,1)S(1)}, bf16[48,1024]{1,0:T(8,128)(2,1)S(1)}, u32[]{:S(2)}, u32[]{:S(2)}) collective-permute-start(bf16[48,1024]{1,0:T(8,128)(2,1)S(1)} %get-tuple-element.42), channel_id=1, source_target_pairs={{0,3},{1,2},{2,1},{3,0},{4,7},{5,6},{6,5},{7,4},{8,11},{9,10},{10,... | collective-permute-start | bytes 294920 | tf_op jit(solution)/shard_map/ppermute | solution.py:466
  20.7 0.0 collective-permute-start.4
  20.7 0.8 %collective-permute-start.5 = (bf16[48,1024]{1,0:T(8,128)(2,1)S(1)}, bf16[48,1024]{1,0:T(8,128)(2,1)S(1)}, u32[]{:S(2)}, u32[]{:S(2)}) collective-permute-start(bf16[48,1024]{1,0:T(8,128)(2,1)S(1)} %get-tuple-element.44), channel_id=1, source_target_pairs={{0,1},{1,0},{2,3},{3,2},{4,5},{5,4},{6,7},{7,6},{8,9},{9,8},{10,11... | collective-permute-start | bytes 294920 | tf_op jit(solution)/shard_map/ppermute | solution.py:466
  21.5 1.3 %pack.1 = (bf16[2,2,256,128]{3,2,1,0:T(8,128)(2,1)S(1)}, bf16[2,2,256,128]{3,2,1,0:T(8,128)(2,1)S(1)}) custom-call(s32[12]{0:T(128)S(1)} %get-tuple-element.27.plan, bf16[54,2,256,128]{3,2,1,0:T(8,128)(2,1)S(1)} %get-tuple-element.41.cache._, f32[48,1024]{1,0:T(8,128)S(1)} %get-tuple-element.36._.own._own), custom_call_target="tpu_custom_call" | custom-call | flops 1 | bytes 6291456 | tf_op jit(solution)/shard_map/pack/pallas_call | solution.py:564
  22.8 1.5 %collective-permute-start.9 = (bf16[2,2,256,128]{3,2,1,0:T(8,128)(2,1)S(1)}, bf16[2,2,256,128]{3,2,1,0:T(8,128)(2,1)S(1)}, u32[]{:S(2)}, u32[]{:S(2)}) collective-permute-start(bf16[2,2,256,128]{3,2,1,0:T(8,128)(2,1)S(1)} %get-tuple-element.45), channel_id=1, source_target_pairs={{0,8},{4,12},{8,0},{12,4},{1,9},{5,13},{9,1},{13,5},{2,10},{6,14},... | collective-permute-start | bytes 786440 | tf_op jit(solution)/shard_map/ppermute | solution.py:466
  24.3 0.0 collective-permute-start.10
  24.3 0.4 collective-permute-done.3.rest_0_
  24.7 4.8 %collective-permute-done.4.rest_1_ = bf16[48,1024]{1,0:T(8,128)(2,1)S(1)} collective-permute-done((bf16[48,1024]{1,0:T(8,128)(2,1)S(1)}, bf16[48,1024]{1,0:T(8,128)(2,1)S(1)}, u32[]{:S(2)}, u32[]{:S(2)}) %collective-permute-start.4) | collective-permute-done | bytes 98336 | tf_op jit(solution)/shard_map/ppermute | solution.py:466
  29.4 0.0 collective-permute-done.5.rest_2_
  29.4 0.1 sum_terms.2.rest_0_
  29.5 0.0 copy-start
  29.5 0.0 copy-start.6
  29.5 2.5 %collective-permute-start.8 = (bf16[48,1024]{1,0:T(8,128)(2,1)S(1)}, bf16[48,1024]{1,0:T(8,128)(2,1)S(1)}, u32[]{:S(2)}, u32[]{:S(2)}) collective-permute-start(bf16[48,1024]{1,0:T(8,128)(2,1)S(1)} %sum_terms.2.rest_0_), channel_id=1, source_target_pairs={{0,3},{1,2},{2,1},{3,0},{4,7},{5,6},{6,5},{7,4},{8,11},{9,10},{10,... | collective-permute-start | bytes 294920 | tf_op jit(solution)/shard_map/ppermute | solution.py:466
  32.0 0.0 collective-permute-start.7
  32.0 1.9 %collective-permute-start.6 = (bf16[48,1024]{1,0:T(8,128)(2,1)S(1)}, bf16[48,1024]{1,0:T(8,128)(2,1)S(1)}, u32[]{:S(2)}, u32[]{:S(2)}) collective-permute-start(bf16[48,1024]{1,0:T(8,128)(2,1)S(1)} %sum_terms.2.rest_0_), channel_id=1, source_target_pairs={{0,1},{1,0},{2,3},{3,2},{4,5},{5,4},{6,7},{7,6},{8,9},{9,8},{10,11... | collective-permute-start | bytes 294920 | tf_op jit(solution)/shard_map/ppermute | solution.py:466
  33.9 0.0 copy-done.2
  33.9 0.0 copy-done.4
  34.0 0.0 copy-done.5
  34.0 0.0 copy-done.8
  34.0 2.2 %prepare.1 = (bf16[4096,256]{1,0:T(8,128)(2,1)S(1)}, f32[48,128]{1,0:T(8,128)S(1)}, f32[48,128]{1,0:T(8,128)S(1)}, s32[48]{0:T(128)S(1)}) custom-call(s32[2]{0:T(128)S(1)} %pad_add_fusion.meta, s32[192]{0:T(256)S(1)} %copy-done.8, s32[192]{0:T(256)S(1)} %copy-done.7, s32[12]{0:T(128)S(1)} %get-tuple-element.27.plan, f32[256,128]{1,0:T(8,128)S(1)} %copy-done.5, ...), custom_call_target="tpu_custom_call" | custom-call | flops 30198988800 | bytes 41943040 | tf_op jit(solution)/shard_map/prepare/pallas_call | solution.py:597
  36.2 0.9 %collective-permute-done.8.rest_3_ = bf16[48,1024]{1,0:T(8,128)(2,1)S(1)} collective-permute-done((bf16[48,1024]{1,0:T(8,128)(2,1)S(1)}, bf16[48,1024]{1,0:T(8,128)(2,1)S(1)}, u32[]{:S(2)}, u32[]{:S(2)}) %collective-permute-start.8) | collective-permute-done | bytes 98336 | tf_op jit(solution)/shard_map/ppermute | solution.py:466
  37.1 3.4 %collective-permute-done.7.rest_2_ = bf16[48,1024]{1,0:T(8,128)(2,1)S(1)} collective-permute-done((bf16[48,1024]{1,0:T(8,128)(2,1)S(1)}, bf16[48,1024]{1,0:T(8,128)(2,1)S(1)}, u32[]{:S(2)}, u32[]{:S(2)}) %collective-permute-start.7) | collective-permute-done | bytes 98336 | tf_op jit(solution)/shard_map/ppermute | solution.py:466
  40.4 0.0 collective-permute-done.6.rest_1_
  40.5 0.0 collective-permute-done.9.rest_5_
  40.5 0.0 collective-permute-done.10.rest_6_
  40.5 0.0 copy-done
  40.5 0.0 copy-done.6
  40.5 5.6 %second_step.1 = (f32[48,1024]{1,0:T(8,128)S(1)}, bf16[48,1024]{1,0:T(8,128)(2,1)S(1)}, bf16[48,1024]{1,0:T(8,128)(2,1)S(1)}, bf16[48,1024]{1,0:T(8,128)(2,1)S(1)}, bf16[54,2,256,128]{3,2,1,0:T(8,128)(2,1)S(1)}) custom-call(s32[2]{0:T(128)S(1)} %pad_add_fusion.meta, s32[192]{0:T(256)S(1)} %copy-done.8, ...), custom_call_target="tpu_custom_call", output_to_operand_aliasing={{4}: (10, {})} | custom-call | flops 905969664 | bytes 18874368 | tf_op jit(solution)/shard_map/second_step/pallas_call | solution.py:612
  46.1 1.8 %collective-permute-start.11 = (bf16[48,1024]{1,0:T(8,128)(2,1)S(1)}, bf16[48,1024]{1,0:T(8,128)(2,1)S(1)}, u32[]{:S(2)}, u32[]{:S(2)}) collective-permute-start(bf16[48,1024]{1,0:T(8,128)(2,1)S(1)} %get-tuple-element.48), channel_id=1, source_target_pairs={{0,3},{1,2},{2,1},{3,0},{4,7},{5,6},{6,5},{7,4},{8,11},{9,10},{10,... | collective-permute-start | bytes 294920 | tf_op jit(solution)/shard_map/ppermute | solution.py:466
  47.9 0.0 collective-permute-start.12
  47.9 2.6 %collective-permute-start.13 = (bf16[48,1024]{1,0:T(8,128)(2,1)S(1)}, bf16[48,1024]{1,0:T(8,128)(2,1)S(1)}, u32[]{:S(2)}, u32[]{:S(2)}) collective-permute-start(bf16[48,1024]{1,0:T(8,128)(2,1)S(1)} %get-tuple-element.50), channel_id=1, source_target_pairs={{0,1},{1,0},{2,3},{3,2},{4,5},{5,4},{6,7},{7,6},{8,9},{9,8},{10,11... | collective-permute-start | bytes 294920 | tf_op jit(solution)/shard_map/ppermute | solution.py:466
  50.5 3.2 %collective-permute-done.11.rest_0_ = bf16[48,1024]{1,0:T(8,128)(2,1)S(1)} collective-permute-done((bf16[48,1024]{1,0:T(8,128)(2,1)S(1)}, bf16[48,1024]{1,0:T(8,128)(2,1)S(1)}, u32[]{:S(2)}, u32[]{:S(2)}) %collective-permute-start.11) | collective-permute-done | bytes 98336 | tf_op jit(solution)/shard_map/ppermute | solution.py:466
  53.7 2.7 %collective-permute-done.12.rest_1_ = bf16[48,1024]{1,0:T(8,128)(2,1)S(1)} collective-permute-done((bf16[48,1024]{1,0:T(8,128)(2,1)S(1)}, bf16[48,1024]{1,0:T(8,128)(2,1)S(1)}, u32[]{:S(2)}, u32[]{:S(2)}) %collective-permute-start.12) | collective-permute-done | bytes 98336 | tf_op jit(solution)/shard_map/ppermute | solution.py:466
  56.4 0.0 collective-permute-done.13.rest_2_
  56.5 2.2 %collective-permute-start.16 = (bf16[48,1024]{1,0:T(8,128)(2,1)S(1)}, bf16[48,1024]{1,0:T(8,128)(2,1)S(1)}, u32[]{:S(2)}, u32[]{:S(2)}) collective-permute-start(bf16[48,1024]{1,0:T(8,128)(2,1)S(1)} %sum_terms.3.rest_0_), channel_id=1, source_target_pairs={{0,3},{1,2},{2,1},{3,0},{4,7},{5,6},{6,5},{7,4},{8,11},{9,10},{10,... | collective-permute-start | bytes 294920 | tf_op jit(solution)/shard_map/ppermute | solution.py:466
  58.7 0.0 collective-permute-start.15
  58.7 2.2 %collective-permute-start.14 = (bf16[48,1024]{1,0:T(8,128)(2,1)S(1)}, bf16[48,1024]{1,0:T(8,128)(2,1)S(1)}, u32[]{:S(2)}, u32[]{:S(2)}) collective-permute-start(bf16[48,1024]{1,0:T(8,128)(2,1)S(1)} %sum_terms.3.rest_0_), channel_id=1, source_target_pairs={{0,1},{1,0},{2,3},{3,2},{4,5},{5,4},{6,7},{7,6},{8,9},{9,8},{10,11... | collective-permute-start | bytes 294920 | tf_op jit(solution)/shard_map/ppermute | solution.py:466
  61.0 3.6 %write_cache.1 = bf16[48,2,256,128]{3,2,1,0:T(8,128)(2,1)} custom-call(s32[48]{0:T(128)S(1)} %get-tuple-element.37.place, bf16[54,2,256,128]{3,2,1,0:T(8,128)(2,1)S(1)} %get-tuple-element.51.cache), custom_call_target="tpu_custom_call" | custom-call | bytes 12582912 | tf_op jit(solution)/shard_map/write_cache/pallas_call | solution.py:631
  64.5 0.0 collective-permute-done.16.rest_3_
  64.5 2.8 %collective-permute-done.15.rest_2_ = bf16[48,1024]{1,0:T(8,128)(2,1)S(1)} collective-permute-done((bf16[48,1024]{1,0:T(8,128)(2,1)S(1)}, bf16[48,1024]{1,0:T(8,128)(2,1)S(1)}, u32[]{:S(2)}, u32[]{:S(2)}) %collective-permute-start.15) | collective-permute-done | bytes 98336 | tf_op jit(solution)/shard_map/ppermute | solution.py:466
  67.4 0.0 collective-permute-done.14.rest_1_
  67.4 1.3 %join.1 = bf16[48,4096]{1,0:T(8,128)(2,1)} custom-call(s32[2]{0:T(128)S(1)} %pad_add_fusion.meta, bf16[48,1024]{1,0:T(8,128)(2,1)S(1)} %sum_terms.3.rest_0_, bf16[48,1024]{1,0:T(8,128)(2,1)S(1)} %collective-permute-done.14.rest_1_, bf16[48,1024]{1,0:T(8,128)(2,1)S(1)} %collective-permute-done.15.rest_2_, bf16[48,1024]{1,0:T(8,128)(2,1)S(1)} %collective-permute-done.16.rest_3_), custom_call_target="tpu_custom_call" | custom-call | tf_op jit(solution)/shard_map/join/pallas_call | solution.py:641
  (1 shorter events, 0.0 us)
Async XLA Ops:
  0.7 11.8 %copy-start.7 = (s32[192]{0:T(256)S(1)}, s32[192]{0:T(256)}, u32[]{:S(2)}) copy-start(s32[192]{0:T(256)} %lengths_s.5) | copy-start | bytes 2308
  9.3 6.3 %copy-start.1 = (bf16[512,4096]{1,0:T(8,128)(2,1)S(1)}, bf16[512,4096]{1,0:T(8,128)(2,1)}, u32[]{:S(2)}) copy-start(bf16[512,4096]{1,0:T(8,128)(2,1)} %wo.3) | copy-start | bytes 12582916
  9.3 6.3 %copy-start.3 = (bf16[48,4096]{1,0:T(8,128)(2,1)S(1)}, bf16[48,4096]{1,0:T(8,128)(2,1)}, u32[]{:S(2)}) copy-start(bf16[48,4096]{1,0:T(8,128)(2,1)} %hidden.1) | copy-start | bytes 1179652
  9.3 6.2 %collective-permute-start = (bf16[2,2,272,128]{3,2,1,0:T(8,128)(2,1)S(1)}, bf16[2,2,272,128]{3,2,1,0:T(8,128)(2,1)S(1)}, u32[]{:S(2)}, u32[]{:S(2)}) collective-permute-start(bf16[2,2,272,128]{3,2,1,0:T(8,128)(2,1)S(1)} %get-tuple-element.33), channel_id=1, source_target_pairs={{0,4},{4,0},{8,12},{12,8},{1,5},{5,1},{9,13},{13,9},{2,6},{6,2},{1... | collective-permute-start | bytes 835592 | tf_op jit(solution)/shard_map/ppermute | solution.py:466
  9.9 5.4 %collective-permute-start.1 = (f32[2,1536]{1,0:T(2,128)S(1)}, f32[2,1536]{1,0:T(2,128)S(1)}, u32[]{:S(2)}, u32[]{:S(2)}) collective-permute-start(f32[2,1536]{1,0:T(2,128)S(1)} %get-tuple-element.34), channel_id=1, source_target_pairs={{0,8},{4,12},{8,0},{12,4},{1,9},{5,13},{9,1},{13,5},{2,10},{6,14},... | collective-permute-start | bytes 36872 | tf_op jit(solution)/shard_map/ppermute | solution.py:466
  12.5 3.1 %collective-permute-start.2 = (f32[2,1536]{1,0:T(2,128)S(1)}, f32[2,1536]{1,0:T(2,128)S(1)}, u32[]{:S(2)}, u32[]{:S(2)}) collective-permute-start(f32[2,1536]{1,0:T(2,128)S(1)} %get-tuple-element.35), channel_id=1, source_target_pairs={{0,12},{4,8},{8,4},{12,0},{1,13},{5,9},{9,5},{13,1},{2,14},{6,10},... | collective-permute-start | bytes 36872 | tf_op jit(solution)/shard_map/ppermute | solution.py:466
  15.6 18.4 %copy-start.2 = (bf16[4096,2,128]{2,1,0:T(2,128)(2,1)S(1)}, bf16[4096,2,128]{2,1,0:T(2,128)(2,1)}, u32[]{:S(2)}) copy-start(bf16[4096,2,128]{2,1,0:T(2,128)(2,1)} %param.16) | copy-start | bytes 6291460
  15.6 18.4 %copy-start.4 = (f32[256,128]{1,0:T(8,128)S(1)}, f32[256,128]{1,0:T(8,128)}, u32[]{:S(2)}) copy-start(f32[256,128]{1,0:T(8,128)} %constant.12.clone.sin_hbm.sin_ref) | copy-start | bytes 393220
  15.6 18.3 %copy-start.5 = (f32[256,128]{1,0:T(8,128)S(1)}, f32[256,128]{1,0:T(8,128)}, u32[]{:S(2)}) copy-start(f32[256,128]{1,0:T(8,128)} %constant.11.clone.cos_hbm.cos_ref) | copy-start | bytes 393220
  15.6 18.3 %copy-start.8 = (s32[192]{0:T(256)S(1)}, s32[192]{0:T(256)}, u32[]{:S(2)}) copy-start(s32[192]{0:T(256)} %source_s.3) | copy-start | bytes 2308
  17.1 7.6 %collective-permute-start.3 = (bf16[48,1024]{1,0:T(8,128)(2,1)S(1)}, bf16[48,1024]{1,0:T(8,128)(2,1)S(1)}, u32[]{:S(2)}, u32[]{:S(2)}) collective-permute-start(bf16[48,1024]{1,0:T(8,128)(2,1)S(1)} %get-tuple-element.42), channel_id=1, source_target_pairs={{0,3},{1,2},{2,1},{3,0},{4,7},{5,6},{6,5},{7,4},{8,11},{9,10},{10,... | collective-permute-start | bytes 294920 | tf_op jit(solution)/shard_map/ppermute | solution.py:466
  20.7 8.7 %collective-permute-start.4 = (bf16[48,1024]{1,0:T(8,128)(2,1)S(1)}, bf16[48,1024]{1,0:T(8,128)(2,1)S(1)}, u32[]{:S(2)}, u32[]{:S(2)}) collective-permute-start(bf16[48,1024]{1,0:T(8,128)(2,1)S(1)} %get-tuple-element.43), channel_id=1, source_target_pairs={{0,2},{1,3},{2,0},{3,1},{4,6},{5,7},{6,4},{7,5},{8,10},{9,11},{10,... | collective-permute-start | bytes 294920 | tf_op jit(solution)/shard_map/ppermute | solution.py:466
  20.7 8.7 %collective-permute-start.5 = (bf16[48,1024]{1,0:T(8,128)(2,1)S(1)}, bf16[48,1024]{1,0:T(8,128)(2,1)S(1)}, u32[]{:S(2)}, u32[]{:S(2)}) collective-permute-start(bf16[48,1024]{1,0:T(8,128)(2,1)S(1)} %get-tuple-element.44), channel_id=1, source_target_pairs={{0,1},{1,0},{2,3},{3,2},{4,5},{5,4},{6,7},{7,6},{8,9},{9,8},{10,11... | collective-permute-start | bytes 294920 | tf_op jit(solution)/shard_map/ppermute | solution.py:466
  22.8 17.7 %collective-permute-start.9 = (bf16[2,2,256,128]{3,2,1,0:T(8,128)(2,1)S(1)}, bf16[2,2,256,128]{3,2,1,0:T(8,128)(2,1)S(1)}, u32[]{:S(2)}, u32[]{:S(2)}) collective-permute-start(bf16[2,2,256,128]{3,2,1,0:T(8,128)(2,1)S(1)} %get-tuple-element.45), channel_id=1, source_target_pairs={{0,8},{4,12},{8,0},{12,4},{1,9},{5,13},{9,1},{13,5},{2,10},{6,14},... | collective-permute-start | bytes 786440 | tf_op jit(solution)/shard_map/ppermute | solution.py:466
  24.3 16.2 %collective-permute-start.10 = (bf16[2,2,256,128]{3,2,1,0:T(8,128)(2,1)S(1)}, bf16[2,2,256,128]{3,2,1,0:T(8,128)(2,1)S(1)}, u32[]{:S(2)}, u32[]{:S(2)}) collective-permute-start(bf16[2,2,256,128]{3,2,1,0:T(8,128)(2,1)S(1)} %get-tuple-element.46), channel_id=1, source_target_pairs={{0,12},{4,8},{8,4},{12,0},{1,13},{5,9},{9,5},{13,1},{2,14},{6,10},... | collective-permute-start | bytes 786440 | tf_op jit(solution)/shard_map/ppermute | solution.py:466
  29.5 11.0 %copy-start = (bf16[4096,512]{1,0:T(8,128)(2,1)S(1)}, bf16[4096,512]{1,0:T(8,128)(2,1)}, u32[]{:S(2)}) copy-start(bf16[4096,512]{1,0:T(8,128)(2,1)} %wq.1) | copy-start | bytes 12582916
  29.5 11.0 %copy-start.6 = (f32[4096]{0:T(1024)S(1)}, f32[4096]{0:T(1024)}, u32[]{:S(2)}) copy-start(f32[4096]{0:T(1024)} %param.14) | copy-start | bytes 49156
  29.5 7.6 %collective-permute-start.8 = (bf16[48,1024]{1,0:T(8,128)(2,1)S(1)}, bf16[48,1024]{1,0:T(8,128)(2,1)S(1)}, u32[]{:S(2)}, u32[]{:S(2)}) collective-permute-start(bf16[48,1024]{1,0:T(8,128)(2,1)S(1)} %sum_terms.2.rest_0_), channel_id=1, source_target_pairs={{0,3},{1,2},{2,1},{3,0},{4,7},{5,6},{6,5},{7,4},{8,11},{9,10},{10,... | collective-permute-start | bytes 294920 | tf_op jit(solution)/shard_map/ppermute | solution.py:466
  32.0 8.4 %collective-permute-start.7 = (bf16[48,1024]{1,0:T(8,128)(2,1)S(1)}, bf16[48,1024]{1,0:T(8,128)(2,1)S(1)}, u32[]{:S(2)}, u32[]{:S(2)}) collective-permute-start(bf16[48,1024]{1,0:T(8,128)(2,1)S(1)} %sum_terms.2.rest_0_), channel_id=1, source_target_pairs={{0,2},{1,3},{2,0},{3,1},{4,6},{5,7},{6,4},{7,5},{8,10},{9,11},{10,... | collective-permute-start | bytes 294920 | tf_op jit(solution)/shard_map/ppermute | solution.py:466
  32.0 8.4 %collective-permute-start.6 = (bf16[48,1024]{1,0:T(8,128)(2,1)S(1)}, bf16[48,1024]{1,0:T(8,128)(2,1)S(1)}, u32[]{:S(2)}, u32[]{:S(2)}) collective-permute-start(bf16[48,1024]{1,0:T(8,128)(2,1)S(1)} %sum_terms.2.rest_0_), channel_id=1, source_target_pairs={{0,1},{1,0},{2,3},{3,2},{4,5},{5,4},{6,7},{7,6},{8,9},{9,8},{10,11... | collective-permute-start | bytes 294920 | tf_op jit(solution)/shard_map/ppermute | solution.py:466
  46.1 7.7 %collective-permute-start.11 = (bf16[48,1024]{1,0:T(8,128)(2,1)S(1)}, bf16[48,1024]{1,0:T(8,128)(2,1)S(1)}, u32[]{:S(2)}, u32[]{:S(2)}) collective-permute-start(bf16[48,1024]{1,0:T(8,128)(2,1)S(1)} %get-tuple-element.48), channel_id=1, source_target_pairs={{0,3},{1,2},{2,1},{3,0},{4,7},{5,6},{6,5},{7,4},{8,11},{9,10},{10,... | collective-permute-start | bytes 294920 | tf_op jit(solution)/shard_map/ppermute | solution.py:466
  47.9 8.6 %collective-permute-start.12 = (bf16[48,1024]{1,0:T(8,128)(2,1)S(1)}, bf16[48,1024]{1,0:T(8,128)(2,1)S(1)}, u32[]{:S(2)}, u32[]{:S(2)}) collective-permute-start(bf16[48,1024]{1,0:T(8,128)(2,1)S(1)} %get-tuple-element.49), channel_id=1, source_target_pairs={{0,2},{1,3},{2,0},{3,1},{4,6},{5,7},{6,4},{7,5},{8,10},{9,11},{10,... | collective-permute-start | bytes 294920 | tf_op jit(solution)/shard_map/ppermute | solution.py:466
  47.9 8.6 %collective-permute-start.13 = (bf16[48,1024]{1,0:T(8,128)(2,1)S(1)}, bf16[48,1024]{1,0:T(8,128)(2,1)S(1)}, u32[]{:S(2)}, u32[]{:S(2)}) collective-permute-start(bf16[48,1024]{1,0:T(8,128)(2,1)S(1)} %get-tuple-element.50), channel_id=1, source_target_pairs={{0,1},{1,0},{2,3},{3,2},{4,5},{5,4},{6,7},{7,6},{8,9},{9,8},{10,11... | collective-permute-start | bytes 294920 | tf_op jit(solution)/shard_map/ppermute | solution.py:466
  56.5 8.0 %collective-permute-start.16 = (bf16[48,1024]{1,0:T(8,128)(2,1)S(1)}, bf16[48,1024]{1,0:T(8,128)(2,1)S(1)}, u32[]{:S(2)}, u32[]{:S(2)}) collective-permute-start(bf16[48,1024]{1,0:T(8,128)(2,1)S(1)} %sum_terms.3.rest_0_), channel_id=1, source_target_pairs={{0,3},{1,2},{2,1},{3,0},{4,7},{5,6},{6,5},{7,4},{8,11},{9,10},{10,... | collective-permute-start | bytes 294920 | tf_op jit(solution)/shard_map/ppermute | solution.py:466
  58.7 8.7 %collective-permute-start.15 = (bf16[48,1024]{1,0:T(8,128)(2,1)S(1)}, bf16[48,1024]{1,0:T(8,128)(2,1)S(1)}, u32[]{:S(2)}, u32[]{:S(2)}) collective-permute-start(bf16[48,1024]{1,0:T(8,128)(2,1)S(1)} %sum_terms.3.rest_0_), channel_id=1, source_target_pairs={{0,2},{1,3},{2,0},{3,1},{4,6},{5,7},{6,4},{7,5},{8,10},{9,11},{10,... | collective-permute-start | bytes 294920 | tf_op jit(solution)/shard_map/ppermute | solution.py:466
  58.7 8.7 %collective-permute-start.14 = (bf16[48,1024]{1,0:T(8,128)(2,1)S(1)}, bf16[48,1024]{1,0:T(8,128)(2,1)S(1)}, u32[]{:S(2)}, u32[]{:S(2)}) collective-permute-start(bf16[48,1024]{1,0:T(8,128)(2,1)S(1)} %sum_terms.3.rest_0_), channel_id=1, source_target_pairs={{0,1},{1,0},{2,3},{3,2},{4,5},{5,4},{6,7},{7,6},{8,9},{9,8},{10,11... | collective-permute-start | bytes 294920 | tf_op jit(solution)/shard_map/ppermute | solution.py:466

commit v13 on v11

--- a/solution.py
+++ b/solution.py
@@ -152,6 +152,15 @@
             normed3[first + i] = normed[:, i * HD : (i + 1) * HD]
 
 
+def cache_copies(cache_hbm, cache, sem, first, last):
+    return [
+        pltpu.make_async_copy(
+            cache_hbm.at[pl.ds(at, CHUNK)], cache.at[pl.ds(at, CHUNK)], sem.at[i]
+        )
+        for i, at in enumerate(range(first, last, CHUNK))
+    ]
+
+
 def first_kernel(
     peers, slots, heads, shard,
     meta, source_hbm, lengths_hbm, hidden_hbm, gain_hbm, cos_hbm, sin_hbm, wq_hbm, wkv_hbm,
@@ -161,7 +170,7 @@
     moving = others * MOVE
     cache, box, notes = rest[0], rest[1], (None,) + rest[2 : others + 1]
     (wq, wkv, normed3, spread, cos_rows, sin_rows, leaving, hidden32, source_s, lengths_s, source_v,
-     hidden, gain, cos_ref, sin_ref, tail, small_sem, wq_sem, wkv_sem, in_sem,
+     hidden, gain, cos_ref, sin_ref, small_sem, wq_sem, wkv_sem, in_sem,
      box_sem, cache_sem) = rest[others + 1 :]
     width = hidden.shape[1]
     me, me_tp = meta[0], meta[1]
@@ -176,12 +185,7 @@
     ]
     for copy in small[:4] + wkv_copies + wq_copies + small[4:]:
         copy.start()
-    loads = [
-        pltpu.make_async_copy(
-            cache_hbm.at[pl.ds(c * CHUNK, CHUNK)], cache.at[pl.ds(c * CHUNK, CHUNK)], cache_sem.at[c]
-        )
-        for c in range(slots // CHUNK)
-    ]
+    loads = cache_copies(cache_hbm, cache, cache_sem, 0, slots - BATCH)
     for copy in small[:2]:
         copy.wait()
 
@@ -257,13 +261,7 @@
             blocks = [attended[at][g : g + 1, :] for g in range(heads)]
             blocks += [residual[:, b * HD : (b + 1) * HD] for b in range(shard // HD)]
             blocks += [jnp.zeros((1, HD), F32)] * (NOTE - len(blocks))
-            tail[m] = jnp.concatenate(blocks, axis=0).astype(BF16)
-            copies.append(
-                pltpu.make_async_copy(
-                    tail.at[m], box.at[m, 0, pl.ds(cap, NOTE), :], box_sem.at[1 + m]
-                )
-            )
-            copies[-1].start()
+            box[m, 0, cap : cap + NOTE, :] = jnp.concatenate(blocks, axis=0).astype(BF16)
         else:
             note = notes[at // MOVE]
             for g in range(heads):
@@ -273,10 +271,9 @@
         copy.wait()
 
 
-def attend_slots(cache, places, positions, query, attended_rows, heads):
-    slots = len(places)
-    for first in range(0, slots, BATCH):
-        span = range(first, first + BATCH)
+def attend_slots(cache, places, positions, query, attended_rows, first, last):
+    for start in range(first, last, BATCH):
+        span = range(start, start + BATCH)
         got = attend(
             cache,
             [places[s] for s in span],
@@ -285,21 +282,32 @@
         )
         for s, rows in zip(span, got):
             attended_rows[s * GROUP : (s + 1) * GROUP, :] = rows
+
+
+def side_by_side(attended_rows, slots, heads):
     return jnp.concatenate(
         [attended_rows[pl.ds(g, slots, stride=GROUP), :] for g in range(heads)], axis=1
-    )
+    ).astype(BF16)
 
 
 def attend_kernel(
-    slots, heads, meta, lengths_s, query, newkey, newvalue, _, out, cache, attended_rows,
+    slots, heads, meta, lengths_s, query, newkey, newvalue, cache_hbm, _,
+    out, cache, attended_rows, in_sem,
 ):
     low = meta[0] * slots
+    early = slots - BATCH
+    loads = cache_copies(cache_hbm, cache, in_sem, early, slots)
+    for copy in loads:
+        copy.start()
     positions = [lengths_s[low + s] for s in range(slots)]
-    for s, p in enumerate(positions):
-        put_row(cache, s, p, newkey[s : s + 1, :], newvalue[s : s + 1, :])
-    out[...] = attend_slots(
-        cache, list(range(slots)), positions, query, attended_rows, heads
-    ).astype(BF16)
+    for first, last in ((0, early), (early, slots)):
+        if first:
+            for copy in loads:
+                copy.wait()
+        for s in range(first, last):
+            put_row(cache, s, positions[s], newkey[s : s + 1, :], newvalue[s : s + 1, :])
+        attend_slots(cache, list(range(slots)), positions, query, attended_rows, first, last)
+    out[...] = side_by_side(attended_rows, slots, heads)
 
 
 def project_out(attended, wo, residual, own, sends, me_tp, peers_tp):
@@ -444,10 +452,9 @@
     places = [place[s] for s in range(slots)]
     for s, (at, p) in enumerate(zip(places, positions)):
         put_row(cache, at, p, newkey[s : s + 1, :], newvalue[s : s + 1, :])
-    attended = attend_slots(cache, places, positions, query_rows, attended_rows, heads)
-    project_out(
-        attended.astype(BF16), wo, blocks[0][...].astype(F32), own, sends, me_tp, peers_tp
-    )
+    attend_slots(cache, places, positions, query_rows, attended_rows, 0, slots)
+    attended = side_by_side(attended_rows, slots, heads)
+    project_out(attended, wo, blocks[0][...].astype(F32), own, sends, me_tp, peers_tp)
 
 
 def cache_kernel(slots, place, cache, out_hbm, out_sem):
@@ -520,7 +527,7 @@
         + [jax.ShapeDtypeStruct((MOVE, 2, cap + NOTE, HD), BF16)]
         + [jax.ShapeDtypeStruct((MOVE, note_width), F32)] * (others - 1),
         in_specs=[SMEM] + [HBM] * 9,
-        out_specs=[VMEM] * 3 + [SMEM, VMEM, ANY] + [VMEM] * (others - 1),
+        out_specs=[VMEM] * 3 + [SMEM] + [VMEM] * (others + 1),
         scratch_shapes=weights
         + stages
         + [
@@ -533,13 +540,12 @@
             pltpu.VMEM((1, width), F32),
             pltpu.VMEM(cosine.shape, F32),
             pltpu.VMEM(cosine.shape, F32),
-            pltpu.VMEM((MOVE, NOTE, HD), BF16),
             dma((7,)),
             dma((4,)),
             dma((4,)),
             dma((moving,)),
-            dma((1 + MOVE,)),
-            dma((slots // CHUNK,)),
+            dma((1,)),
+            dma(((slots - BATCH) // CHUNK,)),
         ],
         compiler_params=params(24),
         cost_estimate=cost(flops, (query_weight.size + wkv.size) * 2),
@@ -554,14 +560,15 @@
     attended, cache = pl.pallas_call(
         functools.partial(attend_kernel, slots, heads),
         out_shape=[jax.ShapeDtypeStruct((slots, heads * HD), BF16), held],
-        in_specs=[SMEM] * 2 + [VMEM] * 4,
+        in_specs=[SMEM] * 2 + [VMEM] * 3 + [HBM, VMEM],
         out_specs=[VMEM] * 2,
-        scratch_shapes=[pltpu.VMEM((slots * GROUP, HD), F32)],
-        input_output_aliases={5: 1},
+        scratch_shapes=[pltpu.VMEM((slots * GROUP, HD), F32), dma((BATCH // CHUNK,))],
+        input_output_aliases={6: 1},
         compiler_params=params(12),
         cost_estimate=cost(4 * slots * cap * HD * heads, cache_bytes),
         name="attention",
-    )(meta, lengths, query, newkey1, newvalue1, cache)
+    )(meta, lengths, query, newkey1, newvalue1,
+      pltpu.with_memory_space_constraint(kv_cache, pltpu.HBM), cache)
 
     sent = [jax.ShapeDtypeStruct((slots, shard), F32)]
     sent += [jax.ShapeDtypeStruct((slots, shard), BF16)] * (peers_tp - 1)

time: 67.4 us -> 67.8 us (level)
  transfers between devices with their start and end apart: 17 -> 17, of which waited for: 8 -> 6; matrix products, arithmetic and copies ran while one was open for 0% -> 0% of each run, Pallas kernels for 15% -> 15%
where the time goes in v13:
time: 67.8 us; the launch traced here: 67.7 us
  Pallas kernels  25.6 us (38%)
  starting transfers between devices  22.8 us (34%)
  waiting for transfers between devices  18.3 us (27%)
  between operations  0.83 us (1%)
    ppermute x17, starting transfers between devices, swapped(): return lax.ppermute(x, axis, [(i, i ^ k) for i in range(size)])  22.8 us
    ppermute x17, waiting for transfers between devices, swapped(): return lax.ppermute(x, axis, [(i, i ^ k) for i in range(size)])  18.3 us
    pallas_call x1, Pallas kernels, local(): pl.pallas_call(functools.partial(first_kernel, peers, slots, heads, shard...  6.97 us
    pallas_call x1, Pallas kernels, local(): pl.pallas_call(functools.partial(second_kernel, peers, peers_tp, slots, h...  5.58 us
    pallas_call x1, Pallas kernels, local(): pl.pallas_call(functools.partial(cache_kernel, slots), out_shape=jax.Shap...  3.58 us
    pallas_call x1, Pallas kernels, local(): pl.pallas_call(functools.partial(attend_kernel, slots, heads), out_shape=...  3.17 us
    pallas_call x1, Pallas kernels, local(): pl.pallas_call(functools.partial(prepare_kernel, peers, slots), out_shape...  2.19 us
    pallas_call x1, Pallas kernels, local(): pl.pallas_call(functools.partial(out_kernel, peers, peers_tp), out_shape=...  1.43 us
  transfers between devices with their start and end apart: 17, of which 6 were waited for; matrix products, arithmetic and copies ran while one was open for 0% of the time, Pallas kernels for 15%

profile of v13, /device:TPU:0, one launch (start us, length us, event | category | flops | bytes accessed | tf_op | source)
XLA Modules:
  0.0 67.7 jit_solution(8582506716068132807)
XLA Ops:
  0.6 0.1 pad_add_fusion.meta
  0.7 0.0 copy-start.7
  0.7 7.0 %first_step.1 = (f32[384,128]{1,0:T(8,128)S(1)}, f32[48,128]{1,0:T(8,128)S(1)}, f32[48,128]{1,0:T(8,128)S(1)}, s32[12]{0:T(128)S(1)}, bf16[54,2,256,128]{3,2,1,0...) custom-call(s32[2]{0:T(128)S(1)} %pad_add_fusion.meta, ...), custom_call_target="tpu_custom_call" | custom-call | flops 301989888 | bytes 6291456 | tf_op jit(solution)/shard_map/first_step/pallas_call | solution.py:518
  7.7 0.5 collective-permute-start
  8.2 2.6 %collective-permute-start.1 = (f32[2,1536]{1,0:T(2,128)S(1)}, f32[2,1536]{1,0:T(2,128)S(1)}, u32[]{:S(2)}, u32[]{:S(2)}) collective-permute-start(f32[2,1536]{1,0:T(2,128)S(1)} %get-tuple-element.34), channel_id=1, source_target_pairs={{0,8},{4,12},{8,0},{12,4},{1,9},{5,13},{9,1},{13,5},{2,10},{6,14},... | collective-permute-start | bytes 36872 | tf_op jit(solution)/shard_map/ppermute | solution.py:484
  10.8 0.1 collective-permute-start.2
  10.9 0.0 copy-done.7
  10.9 0.0 copy-start.1
  10.9 0.0 copy-start.3
  10.9 3.2 %attention.1 = (bf16[48,512]{1,0:T(8,128)(2,1)S(1)}, bf16[54,2,256,128]{3,2,1,0:T(8,128)(2,1)S(1)}) custom-call(s32[2]{0:T(128)S(1)} %pad_add_fusion.meta, s32[192]{0:T(256)S(1)} %copy-done.7, f32[384,128]{1,0:T(8,128)S(1)} %get-tuple-element.28.query, f32[48,128]{1,0:T(8,128)S(1)} %get-tuple-element.29.newkey, ...), custom_call_target="tpu_custom_call", output_to_operand_aliasing={{1}: (6, {})} | custom-call | flops 25165824 | bytes 6291456 | tf_op jit(solution)/shard_map/attention/pallas_call | solution.py:560
  14.1 0.0 collective-permute-done.1.rest_0_
  14.1 0.0 collective-permute-done.2.rest_1_
  14.1 0.0 collective-permute-done.box_hbm.rest_4_
  14.1 0.0 copy-done.1
  14.1 0.0 copy-done.3
  14.1 0.0 copy-start.2
  14.1 0.0 copy-start.4
  14.1 0.0 copy-start.5
  14.1 0.0 copy-start.8
  14.2 1.4 %out_projection.1 = (f32[48,1024]{1,0:T(8,128)S(1)}, bf16[48,1024]{1,0:T(8,128)(2,1)S(1)}, bf16[48,1024]{1,0:T(8,128)(2,1)S(1)}, bf16[48,1024]{1,0:T(8,128)(2,1)S(1)}) custom-call(s32[2]{0:T(128)S(1)} %pad_add_fusion.meta, s32[12]{0:T(128)S(1)} %get-tuple-element.27.plan, bf16[48,512]{1,0:T(8,128)(2,1)S(1)} %get-tuple-element.32.attended, ...), custom_call_target="tpu_custom_call" | custom-call | flops 201326592 | bytes 4194304 | tf_op jit(solution)/shard_map/out_projection/pallas_call | solution.py:575
  15.6 3.9 %collective-permute-start.3 = (bf16[48,1024]{1,0:T(8,128)(2,1)S(1)}, bf16[48,1024]{1,0:T(8,128)(2,1)S(1)}, u32[]{:S(2)}, u32[]{:S(2)}) collective-permute-start(bf16[48,1024]{1,0:T(8,128)(2,1)S(1)} %get-tuple-element.42), channel_id=1, source_target_pairs={{0,3},{1,2},{2,1},{3,0},{4,7},{5,6},{6,5},{7,4},{8,11},{9,10},{10,... | collective-permute-start | bytes 294920 | tf_op jit(solution)/shard_map/ppermute | solution.py:484
  19.5 0.0 collective-permute-start.4
  19.5 0.6 collective-permute-start.5
  20.1 1.3 %pack.1 = (bf16[2,2,256,128]{3,2,1,0:T(8,128)(2,1)S(1)}, bf16[2,2,256,128]{3,2,1,0:T(8,128)(2,1)S(1)}) custom-call(s32[12]{0:T(128)S(1)} %get-tuple-element.27.plan, bf16[54,2,256,128]{3,2,1,0:T(8,128)(2,1)S(1)} %get-tuple-element.41.cache._, f32[48,1024]{1,0:T(8,128)S(1)} %get-tuple-element.36._.own._own), custom_call_target="tpu_custom_call" | custom-call | flops 1 | bytes 6291456 | tf_op jit(solution)/shard_map/pack/pallas_call | solution.py:585
  21.4 1.7 %collective-permute-start.9 = (bf16[2,2,256,128]{3,2,1,0:T(8,128)(2,1)S(1)}, bf16[2,2,256,128]{3,2,1,0:T(8,128)(2,1)S(1)}, u32[]{:S(2)}, u32[]{:S(2)}) collective-permute-start(bf16[2,2,256,128]{3,2,1,0:T(8,128)(2,1)S(1)} %get-tuple-element.45), channel_id=1, source_target_pairs={{0,8},{4,12},{8,0},{12,4},{1,9},{5,13},{9,1},{13,5},{2,10},{6,14},... | collective-permute-start | bytes 786440 | tf_op jit(solution)/shard_map/ppermute | solution.py:484
  23.1 0.0 collective-permute-start.10
  23.1 0.0 collective-permute-done.3.rest_0_
  23.1 5.1 %collective-permute-done.4.rest_1_ = bf16[48,1024]{1,0:T(8,128)(2,1)S(1)} collective-permute-done((bf16[48,1024]{1,0:T(8,128)(2,1)S(1)}, bf16[48,1024]{1,0:T(8,128)(2,1)S(1)}, u32[]{:S(2)}, u32[]{:S(2)}) %collective-permute-start.4) | collective-permute-done | bytes 98336 | tf_op jit(solution)/shard_map/ppermute | solution.py:484
  28.2 0.0 collective-permute-done.5.rest_2_
  28.2 0.1 sum_terms.2.rest_0_
  28.3 0.0 copy-start
  28.3 0.0 copy-start.6
  28.3 2.5 %collective-permute-start.8 = (bf16[48,1024]{1,0:T(8,128)(2,1)S(1)}, bf16[48,1024]{1,0:T(8,128)(2,1)S(1)}, u32[]{:S(2)}, u32[]{:S(2)}) collective-permute-start(bf16[48,1024]{1,0:T(8,128)(2,1)S(1)} %sum_terms.2.rest_0_), channel_id=1, source_target_pairs={{0,3},{1,2},{2,1},{3,0},{4,7},{5,6},{6,5},{7,4},{8,11},{9,10},{10,... | collective-permute-start | bytes 294920 | tf_op jit(solution)/shard_map/ppermute | solution.py:484
  30.9 0.0 collective-permute-start.7
  30.9 1.9 %collective-permute-start.6 = (bf16[48,1024]{1,0:T(8,128)(2,1)S(1)}, bf16[48,1024]{1,0:T(8,128)(2,1)S(1)}, u32[]{:S(2)}, u32[]{:S(2)}) collective-permute-start(bf16[48,1024]{1,0:T(8,128)(2,1)S(1)} %sum_terms.2.rest_0_), channel_id=1, source_target_pairs={{0,1},{1,0},{2,3},{3,2},{4,5},{5,4},{6,7},{7,6},{8,9},{9,8},{10,11... | collective-permute-start | bytes 294920 | tf_op jit(solution)/shard_map/ppermute | solution.py:484
  32.8 0.0 copy-done.2
  32.8 0.0 copy-done.4
  32.8 0.0 copy-done.5
  32.8 0.0 copy-done.8
  32.8 2.2 %prepare.1 = (bf16[4096,256]{1,0:T(8,128)(2,1)S(1)}, f32[48,128]{1,0:T(8,128)S(1)}, f32[48,128]{1,0:T(8,128)S(1)}, s32[48]{0:T(128)S(1)}) custom-call(s32[2]{0:T(128)S(1)} %pad_add_fusion.meta, s32[192]{0:T(256)S(1)} %copy-done.8, s32[192]{0:T(256)S(1)} %copy-done.7, s32[12]{0:T(128)S(1)} %get-tuple-element.27.plan, f32[256,128]{1,0:T(8,128)S(1)} %copy-done.5, ...), custom_call_target="tpu_custom_call" | custom-call | flops 30198988800 | bytes 41943040 | tf_op jit(solution)/shard_map/prepare/pallas_call | solution.py:618
  35.0 0.9 %collective-permute-done.8.rest_3_ = bf16[48,1024]{1,0:T(8,128)(2,1)S(1)} collective-permute-done((bf16[48,1024]{1,0:T(8,128)(2,1)S(1)}, bf16[48,1024]{1,0:T(8,128)(2,1)S(1)}, u32[]{:S(2)}, u32[]{:S(2)}) %collective-permute-start.8) | collective-permute-done | bytes 98336 | tf_op jit(solution)/shard_map/ppermute | solution.py:484
  35.9 3.4 %collective-permute-done.7.rest_2_ = bf16[48,1024]{1,0:T(8,128)(2,1)S(1)} collective-permute-done((bf16[48,1024]{1,0:T(8,128)(2,1)S(1)}, bf16[48,1024]{1,0:T(8,128)(2,1)S(1)}, u32[]{:S(2)}, u32[]{:S(2)}) %collective-permute-start.7) | collective-permute-done | bytes 98336 | tf_op jit(solution)/shard_map/ppermute | solution.py:484
  39.3 0.0 collective-permute-done.6.rest_1_
  39.3 0.0 collective-permute-done.9.rest_5_
  39.3 0.0 collective-permute-done.10.rest_6_
  39.3 0.0 copy-done
  39.3 0.0 copy-done.6
  39.3 5.6 %second_step.1 = (f32[48,1024]{1,0:T(8,128)S(1)}, bf16[48,1024]{1,0:T(8,128)(2,1)S(1)}, bf16[48,1024]{1,0:T(8,128)(2,1)S(1)}, bf16[48,1024]{1,0:T(8,128)(2,1)S(1)}, bf16[54,2,256,128]{3,2,1,0:T(8,128)(2,1)S(1)}) custom-call(s32[2]{0:T(128)S(1)} %pad_add_fusion.meta, s32[192]{0:T(256)S(1)} %copy-done.8, ...), custom_call_target="tpu_custom_call", output_to_operand_aliasing={{4}: (10, {})} | custom-call | flops 905969664 | bytes 18874368 | tf_op jit(solution)/shard_map/second_step/pallas_call | solution.py:633
  44.9 1.9 %collective-permute-start.11 = (bf16[48,1024]{1,0:T(8,128)(2,1)S(1)}, bf16[48,1024]{1,0:T(8,128)(2,1)S(1)}, u32[]{:S(2)}, u32[]{:S(2)}) collective-permute-start(bf16[48,1024]{1,0:T(8,128)(2,1)S(1)} %get-tuple-element.48), channel_id=1, source_target_pairs={{0,3},{1,2},{2,1},{3,0},{4,7},{5,6},{6,5},{7,4},{8,11},{9,10},{10,... | collective-permute-start | bytes 294920 | tf_op jit(solution)/shard_map/ppermute | solution.py:484
  46.8 0.0 collective-permute-start.12
  46.8 2.6 %collective-permute-start.13 = (bf16[48,1024]{1,0:T(8,128)(2,1)S(1)}, bf16[48,1024]{1,0:T(8,128)(2,1)S(1)}, u32[]{:S(2)}, u32[]{:S(2)}) collective-permute-start(bf16[48,1024]{1,0:T(8,128)(2,1)S(1)} %get-tuple-element.50), channel_id=1, source_target_pairs={{0,1},{1,0},{2,3},{3,2},{4,5},{5,4},{6,7},{7,6},{8,9},{9,8},{10,11... | collective-permute-start | bytes 294920 | tf_op jit(solution)/shard_map/ppermute | solution.py:484
  49.4 3.2 %collective-permute-done.11.rest_0_ = bf16[48,1024]{1,0:T(8,128)(2,1)S(1)} collective-permute-done((bf16[48,1024]{1,0:T(8,128)(2,1)S(1)}, bf16[48,1024]{1,0:T(8,128)(2,1)S(1)}, u32[]{:S(2)}, u32[]{:S(2)}) %collective-permute-start.11) | collective-permute-done | bytes 98336 | tf_op jit(solution)/shard_map/ppermute | solution.py:484
  52.6 2.9 %collective-permute-done.12.rest_1_ = bf16[48,1024]{1,0:T(8,128)(2,1)S(1)} collective-permute-done((bf16[48,1024]{1,0:T(8,128)(2,1)S(1)}, bf16[48,1024]{1,0:T(8,128)(2,1)S(1)}, u32[]{:S(2)}, u32[]{:S(2)}) %collective-permute-start.12) | collective-permute-done | bytes 98336 | tf_op jit(solution)/shard_map/ppermute | solution.py:484
  55.4 0.0 collective-permute-done.13.rest_2_
  55.5 2.2 %collective-permute-start.16 = (bf16[48,1024]{1,0:T(8,128)(2,1)S(1)}, bf16[48,1024]{1,0:T(8,128)(2,1)S(1)}, u32[]{:S(2)}, u32[]{:S(2)}) collective-permute-start(bf16[48,1024]{1,0:T(8,128)(2,1)S(1)} %sum_terms.3.rest_0_), channel_id=1, source_target_pairs={{0,3},{1,2},{2,1},{3,0},{4,7},{5,6},{6,5},{7,4},{8,11},{9,10},{10,... | collective-permute-start | bytes 294920 | tf_op jit(solution)/shard_map/ppermute | solution.py:484
  57.6 0.0 collective-permute-start.15
  57.6 2.3 %collective-permute-start.14 = (bf16[48,1024]{1,0:T(8,128)(2,1)S(1)}, bf16[48,1024]{1,0:T(8,128)(2,1)S(1)}, u32[]{:S(2)}, u32[]{:S(2)}) collective-permute-start(bf16[48,1024]{1,0:T(8,128)(2,1)S(1)} %sum_terms.3.rest_0_), channel_id=1, source_target_pairs={{0,1},{1,0},{2,3},{3,2},{4,5},{5,4},{6,7},{7,6},{8,9},{9,8},{10,11... | collective-permute-start | bytes 294920 | tf_op jit(solution)/shard_map/ppermute | solution.py:484
  59.9 3.6 %write_cache.1 = bf16[48,2,256,128]{3,2,1,0:T(8,128)(2,1)} custom-call(s32[48]{0:T(128)S(1)} %get-tuple-element.37.place, bf16[54,2,256,128]{3,2,1,0:T(8,128)(2,1)S(1)} %get-tuple-element.51.cache), custom_call_target="tpu_custom_call" | custom-call | bytes 12582912 | tf_op jit(solution)/shard_map/write_cache/pallas_call | solution.py:652
  63.5 0.0 collective-permute-done.16.rest_3_
  63.5 2.8 %collective-permute-done.15.rest_2_ = bf16[48,1024]{1,0:T(8,128)(2,1)S(1)} collective-permute-done((bf16[48,1024]{1,0:T(8,128)(2,1)S(1)}, bf16[48,1024]{1,0:T(8,128)(2,1)S(1)}, u32[]{:S(2)}, u32[]{:S(2)}) %collective-permute-start.15) | collective-permute-done | bytes 98336 | tf_op jit(solution)/shard_map/ppermute | solution.py:484
  66.3 0.0 collective-permute-done.14.rest_1_
  66.3 1.3 %join.1 = bf16[48,4096]{1,0:T(8,128)(2,1)} custom-call(s32[2]{0:T(128)S(1)} %pad_add_fusion.meta, bf16[48,1024]{1,0:T(8,128)(2,1)S(1)} %sum_terms.3.rest_0_, bf16[48,1024]{1,0:T(8,128)(2,1)S(1)} %collective-permute-done.14.rest_1_, bf16[48,1024]{1,0:T(8,128)(2,1)S(1)} %collective-permute-done.15.rest_2_, bf16[48,1024]{1,0:T(8,128)(2,1)S(1)} %collective-permute-done.16.rest_3_), custom_call_target="tpu_custom_call" | custom-call | tf_op jit(solution)/shard_map/join/pallas_call | solution.py:662
  (1 shorter events, 0.0 us)
Async XLA Ops:
  0.7 10.2 %copy-start.7 = (s32[192]{0:T(256)S(1)}, s32[192]{0:T(256)}, u32[]{:S(2)}) copy-start(s32[192]{0:T(256)} %lengths_s.5) | copy-start | bytes 2308
  7.7 6.4 %collective-permute-start = (bf16[2,2,272,128]{3,2,1,0:T(8,128)(2,1)S(1)}, bf16[2,2,272,128]{3,2,1,0:T(8,128)(2,1)S(1)}, u32[]{:S(2)}, u32[]{:S(2)}) collective-permute-start(bf16[2,2,272,128]{3,2,1,0:T(8,128)(2,1)S(1)} %get-tuple-element.33), channel_id=1, source_target_pairs={{0,4},{4,0},{8,12},{12,8},{1,5},{5,1},{9,13},{13,9},{2,6},{6,2},{1... | collective-permute-start | bytes 835592 | tf_op jit(solution)/shard_map/ppermute | solution.py:484
  8.2 5.9 %collective-permute-start.1 = (f32[2,1536]{1,0:T(2,128)S(1)}, f32[2,1536]{1,0:T(2,128)S(1)}, u32[]{:S(2)}, u32[]{:S(2)}) collective-permute-start(f32[2,1536]{1,0:T(2,128)S(1)} %get-tuple-element.34), channel_id=1, source_target_pairs={{0,8},{4,12},{8,0},{12,4},{1,9},{5,13},{9,1},{13,5},{2,10},{6,14},... | collective-permute-start | bytes 36872 | tf_op jit(solution)/shard_map/ppermute | solution.py:484
  10.8 3.3 %collective-permute-start.2 = (f32[2,1536]{1,0:T(2,128)S(1)}, f32[2,1536]{1,0:T(2,128)S(1)}, u32[]{:S(2)}, u32[]{:S(2)}) collective-permute-start(f32[2,1536]{1,0:T(2,128)S(1)} %get-tuple-element.35), channel_id=1, source_target_pairs={{0,12},{4,8},{8,4},{12,0},{1,13},{5,9},{9,5},{13,1},{2,14},{6,10},... | collective-permute-start | bytes 36872 | tf_op jit(solution)/shard_map/ppermute | solution.py:484
  10.9 3.2 %copy-start.1 = (bf16[512,4096]{1,0:T(8,128)(2,1)S(1)}, bf16[512,4096]{1,0:T(8,128)(2,1)}, u32[]{:S(2)}) copy-start(bf16[512,4096]{1,0:T(8,128)(2,1)} %wo.3) | copy-start | bytes 12582916
  10.9 3.2 %copy-start.3 = (bf16[48,4096]{1,0:T(8,128)(2,1)S(1)}, bf16[48,4096]{1,0:T(8,128)(2,1)}, u32[]{:S(2)}) copy-start(bf16[48,4096]{1,0:T(8,128)(2,1)} %hidden.1) | copy-start | bytes 1179652
  14.1 18.7 %copy-start.2 = (bf16[4096,2,128]{2,1,0:T(2,128)(2,1)S(1)}, bf16[4096,2,128]{2,1,0:T(2,128)(2,1)}, u32[]{:S(2)}) copy-start(bf16[4096,2,128]{2,1,0:T(2,128)(2,1)} %param.16) | copy-start | bytes 6291460
  14.1 18.7 %copy-start.4 = (f32[256,128]{1,0:T(8,128)S(1)}, f32[256,128]{1,0:T(8,128)}, u32[]{:S(2)}) copy-start(f32[256,128]{1,0:T(8,128)} %constant.12.clone.sin_hbm.sin_ref) | copy-start | bytes 393220
  14.1 18.7 %copy-start.5 = (f32[256,128]{1,0:T(8,128)S(1)}, f32[256,128]{1,0:T(8,128)}, u32[]{:S(2)}) copy-start(f32[256,128]{1,0:T(8,128)} %constant.11.clone.cos_hbm.cos_ref) | copy-start | bytes 393220
  14.1 18.7 %copy-start.8 = (s32[192]{0:T(256)S(1)}, s32[192]{0:T(256)}, u32[]{:S(2)}) copy-start(s32[192]{0:T(256)} %source_s.3) | copy-start | bytes 2308
  15.6 7.5 %collective-permute-start.3 = (bf16[48,1024]{1,0:T(8,128)(2,1)S(1)}, bf16[48,1024]{1,0:T(8,128)(2,1)S(1)}, u32[]{:S(2)}, u32[]{:S(2)}) collective-permute-start(bf16[48,1024]{1,0:T(8,128)(2,1)S(1)} %get-tuple-element.42), channel_id=1, source_target_pairs={{0,3},{1,2},{2,1},{3,0},{4,7},{5,6},{6,5},{7,4},{8,11},{9,10},{10,... | collective-permute-start | bytes 294920 | tf_op jit(solution)/shard_map/ppermute | solution.py:484
  19.5 8.8 %collective-permute-start.4 = (bf16[48,1024]{1,0:T(8,128)(2,1)S(1)}, bf16[48,1024]{1,0:T(8,128)(2,1)S(1)}, u32[]{:S(2)}, u32[]{:S(2)}) collective-permute-start(bf16[48,1024]{1,0:T(8,128)(2,1)S(1)} %get-tuple-element.43), channel_id=1, source_target_pairs={{0,2},{1,3},{2,0},{3,1},{4,6},{5,7},{6,4},{7,5},{8,10},{9,11},{10,... | collective-permute-start | bytes 294920 | tf_op jit(solution)/shard_map/ppermute | solution.py:484
  19.5 8.8 %collective-permute-start.5 = (bf16[48,1024]{1,0:T(8,128)(2,1)S(1)}, bf16[48,1024]{1,0:T(8,128)(2,1)S(1)}, u32[]{:S(2)}, u32[]{:S(2)}) collective-permute-start(bf16[48,1024]{1,0:T(8,128)(2,1)S(1)} %get-tuple-element.44), channel_id=1, source_target_pairs={{0,1},{1,0},{2,3},{3,2},{4,5},{5,4},{6,7},{7,6},{8,9},{9,8},{10,11... | collective-permute-start | bytes 294920 | tf_op jit(solution)/shard_map/ppermute | solution.py:484
  21.4 17.9 %collective-permute-start.9 = (bf16[2,2,256,128]{3,2,1,0:T(8,128)(2,1)S(1)}, bf16[2,2,256,128]{3,2,1,0:T(8,128)(2,1)S(1)}, u32[]{:S(2)}, u32[]{:S(2)}) collective-permute-start(bf16[2,2,256,128]{3,2,1,0:T(8,128)(2,1)S(1)} %get-tuple-element.45), channel_id=1, source_target_pairs={{0,8},{4,12},{8,0},{12,4},{1,9},{5,13},{9,1},{13,5},{2,10},{6,14},... | collective-permute-start | bytes 786440 | tf_op jit(solution)/shard_map/ppermute | solution.py:484
  23.1 16.2 %collective-permute-start.10 = (bf16[2,2,256,128]{3,2,1,0:T(8,128)(2,1)S(1)}, bf16[2,2,256,128]{3,2,1,0:T(8,128)(2,1)S(1)}, u32[]{:S(2)}, u32[]{:S(2)}) collective-permute-start(bf16[2,2,256,128]{3,2,1,0:T(8,128)(2,1)S(1)} %get-tuple-element.46), channel_id=1, source_target_pairs={{0,12},{4,8},{8,4},{12,0},{1,13},{5,9},{9,5},{13,1},{2,14},{6,10},... | collective-permute-start | bytes 786440 | tf_op jit(solution)/shard_map/ppermute | solution.py:484
  28.3 11.0 %copy-start = (bf16[4096,512]{1,0:T(8,128)(2,1)S(1)}, bf16[4096,512]{1,0:T(8,128)(2,1)}, u32[]{:S(2)}) copy-start(bf16[4096,512]{1,0:T(8,128)(2,1)} %wq.1) | copy-start | bytes 12582916
  28.3 11.0 %copy-start.6 = (f32[4096]{0:T(1024)S(1)}, f32[4096]{0:T(1024)}, u32[]{:S(2)}) copy-start(f32[4096]{0:T(1024)} %param.14) | copy-start | bytes 49156
  28.3 7.6 %collective-permute-start.8 = (bf16[48,1024]{1,0:T(8,128)(2,1)S(1)}, bf16[48,1024]{1,0:T(8,128)(2,1)S(1)}, u32[]{:S(2)}, u32[]{:S(2)}) collective-permute-start(bf16[48,1024]{1,0:T(8,128)(2,1)S(1)} %sum_terms.2.rest_0_), channel_id=1, source_target_pairs={{0,3},{1,2},{2,1},{3,0},{4,7},{5,6},{6,5},{7,4},{8,11},{9,10},{10,... | collective-permute-start | bytes 294920 | tf_op jit(solution)/shard_map/ppermute | solution.py:484
  30.9 8.4 %collective-permute-start.7 = (bf16[48,1024]{1,0:T(8,128)(2,1)S(1)}, bf16[48,1024]{1,0:T(8,128)(2,1)S(1)}, u32[]{:S(2)}, u32[]{:S(2)}) collective-permute-start(bf16[48,1024]{1,0:T(8,128)(2,1)S(1)} %sum_terms.2.rest_0_), channel_id=1, source_target_pairs={{0,2},{1,3},{2,0},{3,1},{4,6},{5,7},{6,4},{7,5},{8,10},{9,11},{10,... | collective-permute-start | bytes 294920 | tf_op jit(solution)/shard_map/ppermute | solution.py:484
  30.9 8.4 %collective-permute-start.6 = (bf16[48,1024]{1,0:T(8,128)(2,1)S(1)}, bf16[48,1024]{1,0:T(8,128)(2,1)S(1)}, u32[]{:S(2)}, u32[]{:S(2)}) collective-permute-start(bf16[48,1024]{1,0:T(8,128)(2,1)S(1)} %sum_terms.2.rest_0_), channel_id=1, source_target_pairs={{0,1},{1,0},{2,3},{3,2},{4,5},{5,4},{6,7},{7,6},{8,9},{9,8},{10,11... | collective-permute-start | bytes 294920 | tf_op jit(solution)/shard_map/ppermute | solution.py:484
  44.9 7.6 %collective-permute-start.11 = (bf16[48,1024]{1,0:T(8,128)(2,1)S(1)}, bf16[48,1024]{1,0:T(8,128)(2,1)S(1)}, u32[]{:S(2)}, u32[]{:S(2)}) collective-permute-start(bf16[48,1024]{1,0:T(8,128)(2,1)S(1)} %get-tuple-element.48), channel_id=1, source_target_pairs={{0,3},{1,2},{2,1},{3,0},{4,7},{5,6},{6,5},{7,4},{8,11},{9,10},{10,... | collective-permute-start | bytes 294920 | tf_op jit(solution)/shard_map/ppermute | solution.py:484
  46.8 8.6 %collective-permute-start.12 = (bf16[48,1024]{1,0:T(8,128)(2,1)S(1)}, bf16[48,1024]{1,0:T(8,128)(2,1)S(1)}, u32[]{:S(2)}, u32[]{:S(2)}) collective-permute-start(bf16[48,1024]{1,0:T(8,128)(2,1)S(1)} %get-tuple-element.49), channel_id=1, source_target_pairs={{0,2},{1,3},{2,0},{3,1},{4,6},{5,7},{6,4},{7,5},{8,10},{9,11},{10,... | collective-permute-start | bytes 294920 | tf_op jit(solution)/shard_map/ppermute | solution.py:484
  46.8 8.6 %collective-permute-start.13 = (bf16[48,1024]{1,0:T(8,128)(2,1)S(1)}, bf16[48,1024]{1,0:T(8,128)(2,1)S(1)}, u32[]{:S(2)}, u32[]{:S(2)}) collective-permute-start(bf16[48,1024]{1,0:T(8,128)(2,1)S(1)} %get-tuple-element.50), channel_id=1, source_target_pairs={{0,1},{1,0},{2,3},{3,2},{4,5},{5,4},{6,7},{7,6},{8,9},{9,8},{10,11... | collective-permute-start | bytes 294920 | tf_op jit(solution)/shard_map/ppermute | solution.py:484
  55.5 8.0 %collective-permute-start.16 = (bf16[48,1024]{1,0:T(8,128)(2,1)S(1)}, bf16[48,1024]{1,0:T(8,128)(2,1)S(1)}, u32[]{:S(2)}, u32[]{:S(2)}) collective-permute-start(bf16[48,1024]{1,0:T(8,128)(2,1)S(1)} %sum_terms.3.rest_0_), channel_id=1, source_target_pairs={{0,3},{1,2},{2,1},{3,0},{4,7},{5,6},{6,5},{7,4},{8,11},{9,10},{10,... | collective-permute-start | bytes 294920 | tf_op jit(solution)/shard_map/ppermute | solution.py:484
  57.6 8.7 %collective-permute-start.15 = (bf16[48,1024]{1,0:T(8,128)(2,1)S(1)}, bf16[48,1024]{1,0:T(8,128)(2,1)S(1)}, u32[]{:S(2)}, u32[]{:S(2)}) collective-permute-start(bf16[48,1024]{1,0:T(8,128)(2,1)S(1)} %sum_terms.3.rest_0_), channel_id=1, source_target_pairs={{0,2},{1,3},{2,0},{3,1},{4,6},{5,7},{6,4},{7,5},{8,10},{9,11},{10,... | collective-permute-start | bytes 294920 | tf_op jit(solution)/shard_map/ppermute | solution.py:484
  57.6 8.7 %collective-permute-start.14 = (bf16[48,1024]{1,0:T(8,128)(2,1)S(1)}, bf16[48,1024]{1,0:T(8,128)(2,1)S(1)}, u32[]{:S(2)}, u32[]{:S(2)}) collective-permute-start(bf16[48,1024]{1,0:T(8,128)(2,1)S(1)} %sum_terms.3.rest_0_), channel_id=1, source_target_pairs={{0,1},{1,0},{2,3},{3,2},{4,5},{5,4},{6,7},{7,6},{8,9},{9,8},{10,11... | collective-permute-start | bytes 294920 | tf_op jit(solution)/shard_map/ppermute | solution.py:484

commit v14 on v11

--- a/solution.py
+++ b/solution.py
@@ -152,6 +152,28 @@
             normed3[first + i] = normed[:, i * HD : (i + 1) * HD]
 
 
+def plan_moves(me, peers, slots, source):
+    moving = (peers - 1) * MOVE
+    shape = (2 * moving, source.shape[1])
+    row = lax.broadcasted_iota(I32, shape, 0)
+    index = lax.broadcasted_iota(I32, shape, 1)
+    leaves = row < moving
+    at = jnp.where(leaves, row, row - moving)
+    other = jnp.bitwise_xor(me, at // MOVE + 1)
+    here, there = me * slots, other * slots
+    src = jnp.broadcast_to(source, shape)
+    came, went = jnp.where(leaves, here, there), jnp.where(leaves, there, here)
+    moved = (src >= came) & (src < came + slots) & (index >= went) & (index < went + slots)
+    sign = jnp.where(at % MOVE == 0, -1.0, 1.0)
+    index_f = index.astype(F32)
+    best = jnp.max(jnp.where(moved, sign * index_f, -1e6), axis=1, keepdims=True)
+    hit = moved & (sign * index_f == best)
+    result = jnp.where(leaves, src, index) - here
+    found = jnp.sum(jnp.where(hit, result.astype(F32), 0.0), axis=1, keepdims=True)
+    none = jnp.where(leaves[:, :1], 0.0, -1.0)
+    return jnp.where(best > -1e6, found, none).astype(I32)
+
+
 def first_kernel(
     peers, slots, heads, shard,
     meta, source_hbm, lengths_hbm, hidden_hbm, gain_hbm, cos_hbm, sin_hbm, wq_hbm, wkv_hbm,
@@ -160,8 +182,8 @@
     others = peers - 1
     moving = others * MOVE
     cache, box, notes = rest[0], rest[1], (None,) + rest[2 : others + 1]
-    (wq, wkv, normed3, spread, cos_rows, sin_rows, leaving, hidden32, source_s, lengths_s, source_v,
-     hidden, gain, cos_ref, sin_ref, tail, small_sem, wq_sem, wkv_sem, in_sem,
+    (wq, wkv, normed3, spread, cos_rows, sin_rows, leaving, hidden32, lengths_s, source_v,
+     hidden, gain, cos_ref, sin_ref, small_sem, wq_sem, wkv_sem, in_sem,
      box_sem, cache_sem) = rest[others + 1 :]
     width = hidden.shape[1]
     me, me_tp = meta[0], meta[1]
@@ -170,11 +192,11 @@
     small = [
         pltpu.make_async_copy(src, dst, small_sem.at[i])
         for i, (src, dst) in enumerate((
-            (source_hbm, source_v), (source_hbm, source_s), (hidden_hbm, hidden), (gain_hbm, gain),
-            (lengths_hbm, lengths_s), (cos_hbm, cos_ref), (sin_hbm, sin_ref),
+            (source_hbm, source_v), (hidden_hbm, hidden), (gain_hbm, gain), (lengths_hbm, lengths_s),
+            (cos_hbm, cos_ref), (sin_hbm, sin_ref),
         ))
     ]
-    for copy in small[:4] + wkv_copies + wq_copies + small[4:]:
+    for copy in small[:3] + wkv_copies + wq_copies + small[3:]:
         copy.start()
     loads = [
         pltpu.make_async_copy(
@@ -182,45 +204,24 @@
         )
         for c in range(slots // CHUNK)
     ]
-    for copy in small[:2]:
+    for copy in small[:3]:
         copy.wait()
-
     low = me * slots
-    src = source_v[...]
-    index = lax.broadcasted_iota(I32, src.shape, 1)
-    mine_goes = (src >= low) & (src < low + slots)
-    mine_comes = (index >= low) & (index < low + slots)
-    index_f = index.astype(F32)
-    send_slots = []
-    for k in range(1, peers):
-        other = jnp.bitwise_xor(me, k) * slots
-        sent = mine_goes & (index >= other) & (index < other + slots)
-        taken = mine_comes & (src >= other) & (src < other + slots)
-        for m in range(MOVE):
-            at = (k - 1) * MOVE + m
-            if m == 0:
-                j = jnp.min(jnp.where(sent, index_f, 1e6)).astype(I32)
-                r = jnp.min(jnp.where(taken, index_f, 1e6)).astype(I32)
-            else:
-                j = jnp.max(jnp.where(sent, index_f, -1.0)).astype(I32)
-                r = jnp.max(jnp.where(taken, index_f, -1.0)).astype(I32)
-            known = (j >= 0) & (j < src.shape[1])
-            slot = source_s[0, jnp.where(known, j, 0)] - low
-            slot = jnp.where(known, slot, 0)
-            send_slots.append(slot)
-            plan[at] = jnp.where((r >= 0) & (r < src.shape[1]), r - low, -1)
-            plan[moving + at] = slot
-            pltpu.make_async_copy(cache_hbm.at[slot], leaving.at[at], in_sem.at[at]).start()
-    for copy in loads:
-        copy.start()
-
-    for copy in small[2:4]:
-        copy.wait()
+    moves = plan_moves(me, peers, slots, source_v[...])
     wide = hidden[...].astype(F32)
     hidden32[...] = wide
     norm_into(normed3, [wide], [gain[...]], [0], width)
     spread_normed(normed3, spread, slots, width)
-    for copy in small[4:]:
+    send_slots = []
+    for at in range(moving):
+        slot = moves[at, 0]
+        send_slots.append(slot)
+        plan[moving + at] = slot
+        plan[at] = moves[moving + at, 0]
+        pltpu.make_async_copy(cache_hbm.at[slot], leaving.at[at], in_sem.at[at]).start()
+    for copy in loads:
+        copy.start()
+    for copy in small[3:]:
         copy.wait()
     gather_angles(lambda s: lengths_s[0, low + s], slots, cos_ref, sin_ref, cos_rows, sin_rows)
     key, value = project_spread(spread, wkv, wkv_copies)
@@ -257,13 +258,7 @@
             blocks = [attended[at][g : g + 1, :] for g in range(heads)]
             blocks += [residual[:, b * HD : (b + 1) * HD] for b in range(shard // HD)]
             blocks += [jnp.zeros((1, HD), F32)] * (NOTE - len(blocks))
-            tail[m] = jnp.concatenate(blocks, axis=0).astype(BF16)
-            copies.append(
-                pltpu.make_async_copy(
-                    tail.at[m], box.at[m, 0, pl.ds(cap, NOTE), :], box_sem.at[1 + m]
-                )
-            )
-            copies[-1].start()
+            box[m, 0, cap : cap + NOTE, :] = jnp.concatenate(blocks, axis=0).astype(BF16)
         else:
             note = notes[at // MOVE]
             for g in range(heads):
@@ -520,25 +515,23 @@
         + [jax.ShapeDtypeStruct((MOVE, 2, cap + NOTE, HD), BF16)]
         + [jax.ShapeDtypeStruct((MOVE, note_width), F32)] * (others - 1),
         in_specs=[SMEM] + [HBM] * 9,
-        out_specs=[VMEM] * 3 + [SMEM, VMEM, ANY] + [VMEM] * (others - 1),
+        out_specs=[VMEM] * 3 + [SMEM] + [VMEM] * (others + 1),
         scratch_shapes=weights
         + stages
         + [
             pltpu.VMEM((moving,) + kv_cache.shape[1:], BF16),
             pltpu.VMEM((slots, width), F32),
             pltpu.SMEM((1, source.shape[0]), I32),
-            pltpu.SMEM((1, source.shape[0]), I32),
             pltpu.VMEM((1, source.shape[0]), I32),
             pltpu.VMEM(hidden.shape, BF16),
             pltpu.VMEM((1, width), F32),
             pltpu.VMEM(cosine.shape, F32),
             pltpu.VMEM(cosine.shape, F32),
-            pltpu.VMEM((MOVE, NOTE, HD), BF16),
-            dma((7,)),
+            dma((6,)),
             dma((4,)),
             dma((4,)),
             dma((moving,)),
-            dma((1 + MOVE,)),
+            dma((1,)),
             dma((slots // CHUNK,)),
         ],
         compiler_params=params(24),

time: 67.4 us -> 67.2 us (level)
  no operation moved by 1% of the time
where the time goes in v14:
time: 67.2 us; the launch traced here: 67.1 us
  Pallas kernels  25.1 us (37%)
  starting transfers between devices  22.5 us (33%)
  waiting for transfers between devices  18.5 us (28%)
  between operations  0.81 us (1%)
    ppermute x17, starting transfers between devices, swapped(): return lax.ppermute(x, axis, [(i, i ^ k) for i in range(size)])  22.5 us
    ppermute x17, waiting for transfers between devices, swapped(): return lax.ppermute(x, axis, [(i, i ^ k) for i in range(size)])  18.5 us
    pallas_call x1, Pallas kernels, local(): pl.pallas_call(functools.partial(first_kernel, peers, slots, heads, shard...  6.98 us
    pallas_call x1, Pallas kernels, local(): pl.pallas_call(functools.partial(second_kernel, peers, peers_tp, slots, h...  5.58 us
    pallas_call x1, Pallas kernels, local(): pl.pallas_call(functools.partial(cache_kernel, slots), out_shape=jax.Shap...  3.58 us
    pallas_call x1, Pallas kernels, local(): pl.pallas_call(functools.partial(attend_kernel, slots, heads), out_shape=...  2.68 us
    pallas_call x1, Pallas kernels, local(): pl.pallas_call(functools.partial(prepare_kernel, peers, slots), out_shape...  2.2 us
    pallas_call x1, Pallas kernels, local(): pl.pallas_call(functools.partial(out_kernel, peers, peers_tp), out_shape=...  1.43 us
  transfers between devices with their start and end apart: 17, of which 8 were waited for; matrix products, arithmetic and copies ran while one was open for 0% of the time, Pallas kernels for 15%

profile of v14, /device:TPU:0, one launch (start us, length us, event | category | flops | bytes accessed | tf_op | source)
XLA Modules:
  0.0 67.1 jit_solution(17071875131044059141)
XLA Ops:
  0.6 0.1 pad_add_fusion.meta
  0.7 0.0 copy-start.7
  0.7 7.0 %first_step.1 = (f32[384,128]{1,0:T(8,128)S(1)}, f32[48,128]{1,0:T(8,128)S(1)}, f32[48,128]{1,0:T(8,128)S(1)}, s32[12]{0:T(128)S(1)}, bf16[54,2,256,128]{3,2,1,0...) custom-call(s32[2]{0:T(128)S(1)} %pad_add_fusion.meta, ...), custom_call_target="tpu_custom_call" | custom-call | flops 301989888 | bytes 6291456 | tf_op jit(solution)/shard_map/first_step/pallas_call | solution.py:506
  7.7 0.0 copy-start.1
  7.7 0.0 copy-start.3
  7.7 0.5 collective-permute-start
  8.2 2.6 %collective-permute-start.1 = (f32[2,1536]{1,0:T(2,128)S(1)}, f32[2,1536]{1,0:T(2,128)S(1)}, u32[]{:S(2)}, u32[]{:S(2)}) collective-permute-start(f32[2,1536]{1,0:T(2,128)S(1)} %get-tuple-element.34), channel_id=1, source_target_pairs={{0,8},{4,12},{8,0},{12,4},{1,9},{5,13},{9,1},{13,5},{2,10},{6,14},... | collective-permute-start | bytes 36872 | tf_op jit(solution)/shard_map/ppermute | solution.py:472
  10.8 0.1 collective-permute-start.2
  10.9 0.0 copy-done.7
  10.9 2.7 %attention.1 = (bf16[48,512]{1,0:T(8,128)(2,1)S(1)}, bf16[54,2,256,128]{3,2,1,0:T(8,128)(2,1)S(1)}) custom-call(s32[2]{0:T(128)S(1)} %pad_add_fusion.meta, s32[192]{0:T(256)S(1)} %copy-done.7, f32[384,128]{1,0:T(8,128)S(1)} %get-tuple-element.28.query, f32[48,128]{1,0:T(8,128)S(1)} %get-tuple-element.29.newkey, ...), custom_call_target="tpu_custom_call", output_to_operand_aliasing={{1}: (5, {})} | custom-call | flops 25165824 | bytes 6291456 | tf_op jit(solution)/shard_map/attention/pallas_call | solution.py:547
  13.6 0.0 collective-permute-done.1.rest_0_
  13.6 0.3 collective-permute-done.2.rest_1_
  14.0 0.0 collective-permute-done.box_hbm.rest_4_
  14.0 0.0 copy-done.1
  14.0 0.0 copy-done.3
  14.0 0.0 copy-start.2
  14.0 0.0 copy-start.4
  14.0 0.0 copy-start.5
  14.0 0.0 copy-start.8
  14.0 1.4 %out_projection.1 = (f32[48,1024]{1,0:T(8,128)S(1)}, bf16[48,1024]{1,0:T(8,128)(2,1)S(1)}, bf16[48,1024]{1,0:T(8,128)(2,1)S(1)}, bf16[48,1024]{1,0:T(8,128)(2,1)S(1)}) custom-call(s32[2]{0:T(128)S(1)} %pad_add_fusion.meta, s32[12]{0:T(128)S(1)} %get-tuple-element.27.plan, bf16[48,512]{1,0:T(8,128)(2,1)S(1)} %get-tuple-element.32.attended, ...), custom_call_target="tpu_custom_call" | custom-call | flops 201326592 | bytes 4194304 | tf_op jit(solution)/shard_map/out_projection/pallas_call | solution.py:561
  15.5 3.7 %collective-permute-start.3 = (bf16[48,1024]{1,0:T(8,128)(2,1)S(1)}, bf16[48,1024]{1,0:T(8,128)(2,1)S(1)}, u32[]{:S(2)}, u32[]{:S(2)}) collective-permute-start(bf16[48,1024]{1,0:T(8,128)(2,1)S(1)} %get-tuple-element.42), channel_id=1, source_target_pairs={{0,3},{1,2},{2,1},{3,0},{4,7},{5,6},{6,5},{7,4},{8,11},{9,10},{10,... | collective-permute-start | bytes 294920 | tf_op jit(solution)/shard_map/ppermute | solution.py:472
  19.1 0.0 collective-permute-start.4
  19.1 0.8 %collective-permute-start.5 = (bf16[48,1024]{1,0:T(8,128)(2,1)S(1)}, bf16[48,1024]{1,0:T(8,128)(2,1)S(1)}, u32[]{:S(2)}, u32[]{:S(2)}) collective-permute-start(bf16[48,1024]{1,0:T(8,128)(2,1)S(1)} %get-tuple-element.44), channel_id=1, source_target_pairs={{0,1},{1,0},{2,3},{3,2},{4,5},{5,4},{6,7},{7,6},{8,9},{9,8},{10,11... | collective-permute-start | bytes 294920 | tf_op jit(solution)/shard_map/ppermute | solution.py:472
  19.9 1.3 %pack.1 = (bf16[2,2,256,128]{3,2,1,0:T(8,128)(2,1)S(1)}, bf16[2,2,256,128]{3,2,1,0:T(8,128)(2,1)S(1)}) custom-call(s32[12]{0:T(128)S(1)} %get-tuple-element.27.plan, bf16[54,2,256,128]{3,2,1,0:T(8,128)(2,1)S(1)} %get-tuple-element.41.cache._, f32[48,1024]{1,0:T(8,128)S(1)} %get-tuple-element.36._.own._own), custom_call_target="tpu_custom_call" | custom-call | flops 1 | bytes 6291456 | tf_op jit(solution)/shard_map/pack/pallas_call | solution.py:571
  21.2 1.5 %collective-permute-start.9 = (bf16[2,2,256,128]{3,2,1,0:T(8,128)(2,1)S(1)}, bf16[2,2,256,128]{3,2,1,0:T(8,128)(2,1)S(1)}, u32[]{:S(2)}, u32[]{:S(2)}) collective-permute-start(bf16[2,2,256,128]{3,2,1,0:T(8,128)(2,1)S(1)} %get-tuple-element.45), channel_id=1, source_target_pairs={{0,8},{4,12},{8,0},{12,4},{1,9},{5,13},{9,1},{13,5},{2,10},{6,14},... | collective-permute-start | bytes 786440 | tf_op jit(solution)/shard_map/ppermute | solution.py:472
  22.7 0.0 collective-permute-start.10
  22.7 0.4 collective-permute-done.3.rest_0_
  23.0 4.7 %collective-permute-done.4.rest_1_ = bf16[48,1024]{1,0:T(8,128)(2,1)S(1)} collective-permute-done((bf16[48,1024]{1,0:T(8,128)(2,1)S(1)}, bf16[48,1024]{1,0:T(8,128)(2,1)S(1)}, u32[]{:S(2)}, u32[]{:S(2)}) %collective-permute-start.4) | collective-permute-done | bytes 98336 | tf_op jit(solution)/shard_map/ppermute | solution.py:472
  27.8 0.0 collective-permute-done.5.rest_2_
  27.8 0.1 sum_terms.2.rest_0_
  27.8 0.0 copy-start
  27.9 0.0 copy-start.6
  27.9 2.5 %collective-permute-start.8 = (bf16[48,1024]{1,0:T(8,128)(2,1)S(1)}, bf16[48,1024]{1,0:T(8,128)(2,1)S(1)}, u32[]{:S(2)}, u32[]{:S(2)}) collective-permute-start(bf16[48,1024]{1,0:T(8,128)(2,1)S(1)} %sum_terms.2.rest_0_), channel_id=1, source_target_pairs={{0,3},{1,2},{2,1},{3,0},{4,7},{5,6},{6,5},{7,4},{8,11},{9,10},{10,... | collective-permute-start | bytes 294920 | tf_op jit(solution)/shard_map/ppermute | solution.py:472
  30.4 0.0 collective-permute-start.7
  30.4 1.9 %collective-permute-start.6 = (bf16[48,1024]{1,0:T(8,128)(2,1)S(1)}, bf16[48,1024]{1,0:T(8,128)(2,1)S(1)}, u32[]{:S(2)}, u32[]{:S(2)}) collective-permute-start(bf16[48,1024]{1,0:T(8,128)(2,1)S(1)} %sum_terms.2.rest_0_), channel_id=1, source_target_pairs={{0,1},{1,0},{2,3},{3,2},{4,5},{5,4},{6,7},{7,6},{8,9},{9,8},{10,11... | collective-permute-start | bytes 294920 | tf_op jit(solution)/shard_map/ppermute | solution.py:472
  32.3 0.0 copy-done.2
  32.3 0.0 copy-done.4
  32.3 0.0 copy-done.5
  32.3 0.0 copy-done.8
  32.3 2.2 %prepare.1 = (bf16[4096,256]{1,0:T(8,128)(2,1)S(1)}, f32[48,128]{1,0:T(8,128)S(1)}, f32[48,128]{1,0:T(8,128)S(1)}, s32[48]{0:T(128)S(1)}) custom-call(s32[2]{0:T(128)S(1)} %pad_add_fusion.meta, s32[192]{0:T(256)S(1)} %copy-done.8, s32[192]{0:T(256)S(1)} %copy-done.7, s32[12]{0:T(128)S(1)} %get-tuple-element.27.plan, f32[256,128]{1,0:T(8,128)S(1)} %copy-done.5, ...), custom_call_target="tpu_custom_call" | custom-call | flops 30198988800 | bytes 41943040 | tf_op jit(solution)/shard_map/prepare/pallas_call | solution.py:604
  34.5 0.9 %collective-permute-done.8.rest_3_ = bf16[48,1024]{1,0:T(8,128)(2,1)S(1)} collective-permute-done((bf16[48,1024]{1,0:T(8,128)(2,1)S(1)}, bf16[48,1024]{1,0:T(8,128)(2,1)S(1)}, u32[]{:S(2)}, u32[]{:S(2)}) %collective-permute-start.8) | collective-permute-done | bytes 98336 | tf_op jit(solution)/shard_map/ppermute | solution.py:472
  35.5 3.4 %collective-permute-done.7.rest_2_ = bf16[48,1024]{1,0:T(8,128)(2,1)S(1)} collective-permute-done((bf16[48,1024]{1,0:T(8,128)(2,1)S(1)}, bf16[48,1024]{1,0:T(8,128)(2,1)S(1)}, u32[]{:S(2)}, u32[]{:S(2)}) %collective-permute-start.7) | collective-permute-done | bytes 98336 | tf_op jit(solution)/shard_map/ppermute | solution.py:472
  38.8 0.0 collective-permute-done.6.rest_1_
  38.8 0.0 collective-permute-done.9.rest_5_
  38.8 0.0 collective-permute-done.10.rest_6_
  38.8 0.0 copy-done
  38.9 0.0 copy-done.6
  38.9 5.6 %second_step.1 = (f32[48,1024]{1,0:T(8,128)S(1)}, bf16[48,1024]{1,0:T(8,128)(2,1)S(1)}, bf16[48,1024]{1,0:T(8,128)(2,1)S(1)}, bf16[48,1024]{1,0:T(8,128)(2,1)S(1)}, bf16[54,2,256,128]{3,2,1,0:T(8,128)(2,1)S(1)}) custom-call(s32[2]{0:T(128)S(1)} %pad_add_fusion.meta, s32[192]{0:T(256)S(1)} %copy-done.8, ...), custom_call_target="tpu_custom_call", output_to_operand_aliasing={{4}: (10, {})} | custom-call | flops 905969664 | bytes 18874368 | tf_op jit(solution)/shard_map/second_step/pallas_call | solution.py:619
  44.4 1.8 %collective-permute-start.11 = (bf16[48,1024]{1,0:T(8,128)(2,1)S(1)}, bf16[48,1024]{1,0:T(8,128)(2,1)S(1)}, u32[]{:S(2)}, u32[]{:S(2)}) collective-permute-start(bf16[48,1024]{1,0:T(8,128)(2,1)S(1)} %get-tuple-element.48), channel_id=1, source_target_pairs={{0,3},{1,2},{2,1},{3,0},{4,7},{5,6},{6,5},{7,4},{8,11},{9,10},{10,... | collective-permute-start | bytes 294920 | tf_op jit(solution)/shard_map/ppermute | solution.py:472
  46.3 0.0 collective-permute-start.12
  46.3 2.6 %collective-permute-start.13 = (bf16[48,1024]{1,0:T(8,128)(2,1)S(1)}, bf16[48,1024]{1,0:T(8,128)(2,1)S(1)}, u32[]{:S(2)}, u32[]{:S(2)}) collective-permute-start(bf16[48,1024]{1,0:T(8,128)(2,1)S(1)} %get-tuple-element.50), channel_id=1, source_target_pairs={{0,1},{1,0},{2,3},{3,2},{4,5},{5,4},{6,7},{7,6},{8,9},{9,8},{10,11... | collective-permute-start | bytes 294920 | tf_op jit(solution)/shard_map/ppermute | solution.py:472
  48.9 3.2 %collective-permute-done.11.rest_0_ = bf16[48,1024]{1,0:T(8,128)(2,1)S(1)} collective-permute-done((bf16[48,1024]{1,0:T(8,128)(2,1)S(1)}, bf16[48,1024]{1,0:T(8,128)(2,1)S(1)}, u32[]{:S(2)}, u32[]{:S(2)}) %collective-permute-start.11) | collective-permute-done | bytes 98336 | tf_op jit(solution)/shard_map/ppermute | solution.py:472
  52.1 2.7 %collective-permute-done.12.rest_1_ = bf16[48,1024]{1,0:T(8,128)(2,1)S(1)} collective-permute-done((bf16[48,1024]{1,0:T(8,128)(2,1)S(1)}, bf16[48,1024]{1,0:T(8,128)(2,1)S(1)}, u32[]{:S(2)}, u32[]{:S(2)}) %collective-permute-start.12) | collective-permute-done | bytes 98336 | tf_op jit(solution)/shard_map/ppermute | solution.py:472
  54.8 0.0 collective-permute-done.13.rest_2_
  54.9 2.2 %collective-permute-start.16 = (bf16[48,1024]{1,0:T(8,128)(2,1)S(1)}, bf16[48,1024]{1,0:T(8,128)(2,1)S(1)}, u32[]{:S(2)}, u32[]{:S(2)}) collective-permute-start(bf16[48,1024]{1,0:T(8,128)(2,1)S(1)} %sum_terms.3.rest_0_), channel_id=1, source_target_pairs={{0,3},{1,2},{2,1},{3,0},{4,7},{5,6},{6,5},{7,4},{8,11},{9,10},{10,... | collective-permute-start | bytes 294920 | tf_op jit(solution)/shard_map/ppermute | solution.py:472
  57.1 0.0 collective-permute-start.15
  57.1 2.2 %collective-permute-start.14 = (bf16[48,1024]{1,0:T(8,128)(2,1)S(1)}, bf16[48,1024]{1,0:T(8,128)(2,1)S(1)}, u32[]{:S(2)}, u32[]{:S(2)}) collective-permute-start(bf16[48,1024]{1,0:T(8,128)(2,1)S(1)} %sum_terms.3.rest_0_), channel_id=1, source_target_pairs={{0,1},{1,0},{2,3},{3,2},{4,5},{5,4},{6,7},{7,6},{8,9},{9,8},{10,11... | collective-permute-start | bytes 294920 | tf_op jit(solution)/shard_map/ppermute | solution.py:472
  59.3 3.6 %write_cache.1 = bf16[48,2,256,128]{3,2,1,0:T(8,128)(2,1)} custom-call(s32[48]{0:T(128)S(1)} %get-tuple-element.37.place, bf16[54,2,256,128]{3,2,1,0:T(8,128)(2,1)S(1)} %get-tuple-element.51.cache), custom_call_target="tpu_custom_call" | custom-call | bytes 12582912 | tf_op jit(solution)/shard_map/write_cache/pallas_call | solution.py:638
  62.9 0.0 collective-permute-done.16.rest_3_
  62.9 2.8 %collective-permute-done.15.rest_2_ = bf16[48,1024]{1,0:T(8,128)(2,1)S(1)} collective-permute-done((bf16[48,1024]{1,0:T(8,128)(2,1)S(1)}, bf16[48,1024]{1,0:T(8,128)(2,1)S(1)}, u32[]{:S(2)}, u32[]{:S(2)}) %collective-permute-start.15) | collective-permute-done | bytes 98336 | tf_op jit(solution)/shard_map/ppermute | solution.py:472
  65.8 0.0 collective-permute-done.14.rest_1_
  65.8 1.3 %join.1 = bf16[48,4096]{1,0:T(8,128)(2,1)} custom-call(s32[2]{0:T(128)S(1)} %pad_add_fusion.meta, bf16[48,1024]{1,0:T(8,128)(2,1)S(1)} %sum_terms.3.rest_0_, bf16[48,1024]{1,0:T(8,128)(2,1)S(1)} %collective-permute-done.14.rest_1_, bf16[48,1024]{1,0:T(8,128)(2,1)S(1)} %collective-permute-done.15.rest_2_, bf16[48,1024]{1,0:T(8,128)(2,1)S(1)} %collective-permute-done.16.rest_3_), custom_call_target="tpu_custom_call" | custom-call | tf_op jit(solution)/shard_map/join/pallas_call | solution.py:648
  (1 shorter events, 0.0 us)
Async XLA Ops:
  0.7 10.2 %copy-start.7 = (s32[192]{0:T(256)S(1)}, s32[192]{0:T(256)}, u32[]{:S(2)}) copy-start(s32[192]{0:T(256)} %lengths_s.5) | copy-start | bytes 2308
  7.7 6.3 %copy-start.1 = (bf16[512,4096]{1,0:T(8,128)(2,1)S(1)}, bf16[512,4096]{1,0:T(8,128)(2,1)}, u32[]{:S(2)}) copy-start(bf16[512,4096]{1,0:T(8,128)(2,1)} %wo.3) | copy-start | bytes 12582916
  7.7 6.3 %copy-start.3 = (bf16[48,4096]{1,0:T(8,128)(2,1)S(1)}, bf16[48,4096]{1,0:T(8,128)(2,1)}, u32[]{:S(2)}) copy-start(bf16[48,4096]{1,0:T(8,128)(2,1)} %hidden.1) | copy-start | bytes 1179652
  7.7 6.2 %collective-permute-start = (bf16[2,2,272,128]{3,2,1,0:T(8,128)(2,1)S(1)}, bf16[2,2,272,128]{3,2,1,0:T(8,128)(2,1)S(1)}, u32[]{:S(2)}, u32[]{:S(2)}) collective-permute-start(bf16[2,2,272,128]{3,2,1,0:T(8,128)(2,1)S(1)} %get-tuple-element.33), channel_id=1, source_target_pairs={{0,4},{4,0},{8,12},{12,8},{1,5},{5,1},{9,13},{13,9},{2,6},{6,2},{1... | collective-permute-start | bytes 835592 | tf_op jit(solution)/shard_map/ppermute | solution.py:472
  8.2 5.4 %collective-permute-start.1 = (f32[2,1536]{1,0:T(2,128)S(1)}, f32[2,1536]{1,0:T(2,128)S(1)}, u32[]{:S(2)}, u32[]{:S(2)}) collective-permute-start(f32[2,1536]{1,0:T(2,128)S(1)} %get-tuple-element.34), channel_id=1, source_target_pairs={{0,8},{4,12},{8,0},{12,4},{1,9},{5,13},{9,1},{13,5},{2,10},{6,14},... | collective-permute-start | bytes 36872 | tf_op jit(solution)/shard_map/ppermute | solution.py:472
  10.8 3.1 %collective-permute-start.2 = (f32[2,1536]{1,0:T(2,128)S(1)}, f32[2,1536]{1,0:T(2,128)S(1)}, u32[]{:S(2)}, u32[]{:S(2)}) collective-permute-start(f32[2,1536]{1,0:T(2,128)S(1)} %get-tuple-element.35), channel_id=1, source_target_pairs={{0,12},{4,8},{8,4},{12,0},{1,13},{5,9},{9,5},{13,1},{2,14},{6,10},... | collective-permute-start | bytes 36872 | tf_op jit(solution)/shard_map/ppermute | solution.py:472
  14.0 18.4 %copy-start.2 = (bf16[4096,2,128]{2,1,0:T(2,128)(2,1)S(1)}, bf16[4096,2,128]{2,1,0:T(2,128)(2,1)}, u32[]{:S(2)}) copy-start(bf16[4096,2,128]{2,1,0:T(2,128)(2,1)} %param.16) | copy-start | bytes 6291460
  14.0 18.3 %copy-start.4 = (f32[256,128]{1,0:T(8,128)S(1)}, f32[256,128]{1,0:T(8,128)}, u32[]{:S(2)}) copy-start(f32[256,128]{1,0:T(8,128)} %constant.12.clone.sin_hbm.sin_ref) | copy-start | bytes 393220
  14.0 18.3 %copy-start.5 = (f32[256,128]{1,0:T(8,128)S(1)}, f32[256,128]{1,0:T(8,128)}, u32[]{:S(2)}) copy-start(f32[256,128]{1,0:T(8,128)} %constant.11.clone.cos_hbm.cos_ref) | copy-start | bytes 393220
  14.0 18.3 %copy-start.8 = (s32[192]{0:T(256)S(1)}, s32[192]{0:T(256)}, u32[]{:S(2)}) copy-start(s32[192]{0:T(256)} %source_s.3) | copy-start | bytes 2308
  15.5 7.6 %collective-permute-start.3 = (bf16[48,1024]{1,0:T(8,128)(2,1)S(1)}, bf16[48,1024]{1,0:T(8,128)(2,1)S(1)}, u32[]{:S(2)}, u32[]{:S(2)}) collective-permute-start(bf16[48,1024]{1,0:T(8,128)(2,1)S(1)} %get-tuple-element.42), channel_id=1, source_target_pairs={{0,3},{1,2},{2,1},{3,0},{4,7},{5,6},{6,5},{7,4},{8,11},{9,10},{10,... | collective-permute-start | bytes 294920 | tf_op jit(solution)/shard_map/ppermute | solution.py:472
  19.1 8.7 %collective-permute-start.4 = (bf16[48,1024]{1,0:T(8,128)(2,1)S(1)}, bf16[48,1024]{1,0:T(8,128)(2,1)S(1)}, u32[]{:S(2)}, u32[]{:S(2)}) collective-permute-start(bf16[48,1024]{1,0:T(8,128)(2,1)S(1)} %get-tuple-element.43), channel_id=1, source_target_pairs={{0,2},{1,3},{2,0},{3,1},{4,6},{5,7},{6,4},{7,5},{8,10},{9,11},{10,... | collective-permute-start | bytes 294920 | tf_op jit(solution)/shard_map/ppermute | solution.py:472
  19.1 8.7 %collective-permute-start.5 = (bf16[48,1024]{1,0:T(8,128)(2,1)S(1)}, bf16[48,1024]{1,0:T(8,128)(2,1)S(1)}, u32[]{:S(2)}, u32[]{:S(2)}) collective-permute-start(bf16[48,1024]{1,0:T(8,128)(2,1)S(1)} %get-tuple-element.44), channel_id=1, source_target_pairs={{0,1},{1,0},{2,3},{3,2},{4,5},{5,4},{6,7},{7,6},{8,9},{9,8},{10,11... | collective-permute-start | bytes 294920 | tf_op jit(solution)/shard_map/ppermute | solution.py:472
  21.2 17.7 %collective-permute-start.9 = (bf16[2,2,256,128]{3,2,1,0:T(8,128)(2,1)S(1)}, bf16[2,2,256,128]{3,2,1,0:T(8,128)(2,1)S(1)}, u32[]{:S(2)}, u32[]{:S(2)}) collective-permute-start(bf16[2,2,256,128]{3,2,1,0:T(8,128)(2,1)S(1)} %get-tuple-element.45), channel_id=1, source_target_pairs={{0,8},{4,12},{8,0},{12,4},{1,9},{5,13},{9,1},{13,5},{2,10},{6,14},... | collective-permute-start | bytes 786440 | tf_op jit(solution)/shard_map/ppermute | solution.py:472
  22.7 16.2 %collective-permute-start.10 = (bf16[2,2,256,128]{3,2,1,0:T(8,128)(2,1)S(1)}, bf16[2,2,256,128]{3,2,1,0:T(8,128)(2,1)S(1)}, u32[]{:S(2)}, u32[]{:S(2)}) collective-permute-start(bf16[2,2,256,128]{3,2,1,0:T(8,128)(2,1)S(1)} %get-tuple-element.46), channel_id=1, source_target_pairs={{0,12},{4,8},{8,4},{12,0},{1,13},{5,9},{9,5},{13,1},{2,14},{6,10},... | collective-permute-start | bytes 786440 | tf_op jit(solution)/shard_map/ppermute | solution.py:472
  27.8 11.0 %copy-start = (bf16[4096,512]{1,0:T(8,128)(2,1)S(1)}, bf16[4096,512]{1,0:T(8,128)(2,1)}, u32[]{:S(2)}) copy-start(bf16[4096,512]{1,0:T(8,128)(2,1)} %wq.1) | copy-start | bytes 12582916
  27.9 11.0 %copy-start.6 = (f32[4096]{0:T(1024)S(1)}, f32[4096]{0:T(1024)}, u32[]{:S(2)}) copy-start(f32[4096]{0:T(1024)} %param.14) | copy-start | bytes 49156
  27.9 7.6 %collective-permute-start.8 = (bf16[48,1024]{1,0:T(8,128)(2,1)S(1)}, bf16[48,1024]{1,0:T(8,128)(2,1)S(1)}, u32[]{:S(2)}, u32[]{:S(2)}) collective-permute-start(bf16[48,1024]{1,0:T(8,128)(2,1)S(1)} %sum_terms.2.rest_0_), channel_id=1, source_target_pairs={{0,3},{1,2},{2,1},{3,0},{4,7},{5,6},{6,5},{7,4},{8,11},{9,10},{10,... | collective-permute-start | bytes 294920 | tf_op jit(solution)/shard_map/ppermute | solution.py:472
  30.4 8.4 %collective-permute-start.7 = (bf16[48,1024]{1,0:T(8,128)(2,1)S(1)}, bf16[48,1024]{1,0:T(8,128)(2,1)S(1)}, u32[]{:S(2)}, u32[]{:S(2)}) collective-permute-start(bf16[48,1024]{1,0:T(8,128)(2,1)S(1)} %sum_terms.2.rest_0_), channel_id=1, source_target_pairs={{0,2},{1,3},{2,0},{3,1},{4,6},{5,7},{6,4},{7,5},{8,10},{9,11},{10,... | collective-permute-start | bytes 294920 | tf_op jit(solution)/shard_map/ppermute | solution.py:472
  30.4 8.4 %collective-permute-start.6 = (bf16[48,1024]{1,0:T(8,128)(2,1)S(1)}, bf16[48,1024]{1,0:T(8,128)(2,1)S(1)}, u32[]{:S(2)}, u32[]{:S(2)}) collective-permute-start(bf16[48,1024]{1,0:T(8,128)(2,1)S(1)} %sum_terms.2.rest_0_), channel_id=1, source_target_pairs={{0,1},{1,0},{2,3},{3,2},{4,5},{5,4},{6,7},{7,6},{8,9},{9,8},{10,11... | collective-permute-start | bytes 294920 | tf_op jit(solution)/shard_map/ppermute | solution.py:472
  44.4 7.7 %collective-permute-start.11 = (bf16[48,1024]{1,0:T(8,128)(2,1)S(1)}, bf16[48,1024]{1,0:T(8,128)(2,1)S(1)}, u32[]{:S(2)}, u32[]{:S(2)}) collective-permute-start(bf16[48,1024]{1,0:T(8,128)(2,1)S(1)} %get-tuple-element.48), channel_id=1, source_target_pairs={{0,3},{1,2},{2,1},{3,0},{4,7},{5,6},{6,5},{7,4},{8,11},{9,10},{10,... | collective-permute-start | bytes 294920 | tf_op jit(solution)/shard_map/ppermute | solution.py:472
  46.3 8.6 %collective-permute-start.12 = (bf16[48,1024]{1,0:T(8,128)(2,1)S(1)}, bf16[48,1024]{1,0:T(8,128)(2,1)S(1)}, u32[]{:S(2)}, u32[]{:S(2)}) collective-permute-start(bf16[48,1024]{1,0:T(8,128)(2,1)S(1)} %get-tuple-element.49), channel_id=1, source_target_pairs={{0,2},{1,3},{2,0},{3,1},{4,6},{5,7},{6,4},{7,5},{8,10},{9,11},{10,... | collective-permute-start | bytes 294920 | tf_op jit(solution)/shard_map/ppermute | solution.py:472
  46.3 8.6 %collective-permute-start.13 = (bf16[48,1024]{1,0:T(8,128)(2,1)S(1)}, bf16[48,1024]{1,0:T(8,128)(2,1)S(1)}, u32[]{:S(2)}, u32[]{:S(2)}) collective-permute-start(bf16[48,1024]{1,0:T(8,128)(2,1)S(1)} %get-tuple-element.50), channel_id=1, source_target_pairs={{0,1},{1,0},{2,3},{3,2},{4,5},{5,4},{6,7},{7,6},{8,9},{9,8},{10,11... | collective-permute-start | bytes 294920 | tf_op jit(solution)/shard_map/ppermute | solution.py:472
  54.9 8.0 %collective-permute-start.16 = (bf16[48,1024]{1,0:T(8,128)(2,1)S(1)}, bf16[48,1024]{1,0:T(8,128)(2,1)S(1)}, u32[]{:S(2)}, u32[]{:S(2)}) collective-permute-start(bf16[48,1024]{1,0:T(8,128)(2,1)S(1)} %sum_terms.3.rest_0_), channel_id=1, source_target_pairs={{0,3},{1,2},{2,1},{3,0},{4,7},{5,6},{6,5},{7,4},{8,11},{9,10},{10,... | collective-permute-start | bytes 294920 | tf_op jit(solution)/shard_map/ppermute | solution.py:472
  57.1 8.7 %collective-permute-start.15 = (bf16[48,1024]{1,0:T(8,128)(2,1)S(1)}, bf16[48,1024]{1,0:T(8,128)(2,1)S(1)}, u32[]{:S(2)}, u32[]{:S(2)}) collective-permute-start(bf16[48,1024]{1,0:T(8,128)(2,1)S(1)} %sum_terms.3.rest_0_), channel_id=1, source_target_pairs={{0,2},{1,3},{2,0},{3,1},{4,6},{5,7},{6,4},{7,5},{8,10},{9,11},{10,... | collective-permute-start | bytes 294920 | tf_op jit(solution)/shard_map/ppermute | solution.py:472
  57.1 8.7 %collective-permute-start.14 = (bf16[48,1024]{1,0:T(8,128)(2,1)S(1)}, bf16[48,1024]{1,0:T(8,128)(2,1)S(1)}, u32[]{:S(2)}, u32[]{:S(2)}) collective-permute-start(bf16[48,1024]{1,0:T(8,128)(2,1)S(1)} %sum_terms.3.rest_0_), channel_id=1, source_target_pairs={{0,1},{1,0},{2,3},{3,2},{4,5},{5,4},{6,7},{7,6},{8,9},{9,8},{10,11... | collective-permute-start | bytes 294920 | tf_op jit(solution)/shard_map/ppermute | solution.py:472

commit v15 on v14

--- a/solution.py
+++ b/solution.py
@@ -150,6 +150,15 @@
         normed = (piece * factor * gain).astype(BF16)
         for i in range(piece.shape[1] // HD):
             normed3[first + i] = normed[:, i * HD : (i + 1) * HD]
+
+
+def cache_copies(cache_hbm, cache, sem, first, last):
+    return [
+        pltpu.make_async_copy(
+            cache_hbm.at[pl.ds(at, CHUNK)], cache.at[pl.ds(at, CHUNK)], sem.at[i]
+        )
+        for i, at in enumerate(range(first, last, CHUNK))
+    ]
 
 
 def plan_moves(me, peers, slots, source):
@@ -198,12 +207,7 @@
     ]
     for copy in small[:3] + wkv_copies + wq_copies + small[3:]:
         copy.start()
-    loads = [
-        pltpu.make_async_copy(
-            cache_hbm.at[pl.ds(c * CHUNK, CHUNK)], cache.at[pl.ds(c * CHUNK, CHUNK)], cache_sem.at[c]
-        )
-        for c in range(slots // CHUNK)
-    ]
+    loads = cache_copies(cache_hbm, cache, cache_sem, 0, slots - BATCH)
     for copy in small[:3]:
         copy.wait()
     low = me * slots
@@ -268,10 +272,9 @@
         copy.wait()
 
 
-def attend_slots(cache, places, positions, query, attended_rows, heads):
-    slots = len(places)
-    for first in range(0, slots, BATCH):
-        span = range(first, first + BATCH)
+def attend_slots(cache, places, positions, query, attended_rows, first, last):
+    for start in range(first, last, BATCH):
+        span = range(start, start + BATCH)
         got = attend(
             cache,
             [places[s] for s in span],
@@ -280,21 +283,32 @@
         )
         for s, rows in zip(span, got):
             attended_rows[s * GROUP : (s + 1) * GROUP, :] = rows
+
+
+def side_by_side(attended_rows, slots, heads):
     return jnp.concatenate(
         [attended_rows[pl.ds(g, slots, stride=GROUP), :] for g in range(heads)], axis=1
-    )
+    ).astype(BF16)
 
 
 def attend_kernel(
-    slots, heads, meta, lengths_s, query, newkey, newvalue, _, out, cache, attended_rows,
+    slots, heads, meta, lengths_s, query, newkey, newvalue, cache_hbm, _,
+    out, cache, attended_rows, in_sem,
 ):
     low = meta[0] * slots
+    early = slots - BATCH
+    loads = cache_copies(cache_hbm, cache, in_sem, early, slots)
+    for copy in loads:
+        copy.start()
     positions = [lengths_s[low + s] for s in range(slots)]
-    for s, p in enumerate(positions):
-        put_row(cache, s, p, newkey[s : s + 1, :], newvalue[s : s + 1, :])
-    out[...] = attend_slots(
-        cache, list(range(slots)), positions, query, attended_rows, heads
-    ).astype(BF16)
+    for first, last in ((0, early), (early, slots)):
+        if first:
+            for copy in loads:
+                copy.wait()
+        for s in range(first, last):
+            put_row(cache, s, positions[s], newkey[s : s + 1, :], newvalue[s : s + 1, :])
+        attend_slots(cache, list(range(slots)), positions, query, attended_rows, first, last)
+    out[...] = side_by_side(attended_rows, slots, heads)
 
 
 def project_out(attended, wo, residual, own, sends, me_tp, peers_tp):
@@ -439,10 +453,9 @@
     places = [place[s] for s in range(slots)]
     for s, (at, p) in enumerate(zip(places, positions)):
         put_row(cache, at, p, newkey[s : s + 1, :], newvalue[s : s + 1, :])
-    attended = attend_slots(cache, places, positions, query_rows, attended_rows, heads)
-    project_out(
-        attended.astype(BF16), wo, blocks[0][...].astype(F32), own, sends, me_tp, peers_tp
-    )
+    attend_slots(cache, places, positions, query_rows, attended_rows, 0, slots)
+    attended = side_by_side(attended_rows, slots, heads)
+    project_out(attended, wo, blocks[0][...].astype(F32), own, sends, me_tp, peers_tp)
 
 
 def cache_kernel(slots, place, cache, out_hbm, out_sem):
@@ -532,7 +545,7 @@
             dma((4,)),
             dma((moving,)),
             dma((1,)),
-            dma((slots // CHUNK,)),
+            dma(((slots - BATCH) // CHUNK,)),
         ],
         compiler_params=params(24),
         cost_estimate=cost(flops, (query_weight.size + wkv.size) * 2),
@@ -547,14 +560,15 @@
     attended, cache = pl.pallas_call(
         functools.partial(attend_kernel, slots, heads),
         out_shape=[jax.ShapeDtypeStruct((slots, heads * HD), BF16), held],
-        in_specs=[SMEM] * 2 + [VMEM] * 4,
+        in_specs=[SMEM] * 2 + [VMEM] * 3 + [HBM, VMEM],
         out_specs=[VMEM] * 2,
-        scratch_shapes=[pltpu.VMEM((slots * GROUP, HD), F32)],
-        input_output_aliases={5: 1},
+        scratch_shapes=[pltpu.VMEM((slots * GROUP, HD), F32), dma((BATCH // CHUNK,))],
+        input_output_aliases={6: 1},
         compiler_params=params(12),
         cost_estimate=cost(4 * slots * cap * HD * heads, cache_bytes),
         name="attention",
-    )(meta, lengths, query, newkey1, newvalue1, cache)
+    )(meta, lengths, query, newkey1, newvalue1,
+      pltpu.with_memory_space_constraint(kv_cache, pltpu.HBM), cache)
 
     sent = [jax.ShapeDtypeStruct((slots, shard), F32)]
     sent += [jax.ShapeDtypeStruct((slots, shard), BF16)] * (peers_tp - 1)

time: 67.2 us -> 67.8 us (level)
  transfers between devices with their start and end apart: 17 -> 17, of which waited for: 8 -> 6; matrix products, arithmetic and copies ran while one was open for 0% -> 0% of each run, Pallas kernels for 15% -> 15%
where the time goes in v15:
time: 67.8 us; the launch traced here: 67.6 us
  Pallas kernels  25.6 us (38%)
  starting transfers between devices  22.8 us (34%)
  waiting for transfers between devices  18.3 us (27%)
  between operations  0.83 us (1%)
    ppermute x17, starting transfers between devices, swapped(): return lax.ppermute(x, axis, [(i, i ^ k) for i in range(size)])  22.8 us
    ppermute x17, waiting for transfers between devices, swapped(): return lax.ppermute(x, axis, [(i, i ^ k) for i in range(size)])  18.3 us
    pallas_call x1, Pallas kernels, local(): pl.pallas_call(functools.partial(first_kernel, peers, slots, heads, shard...  6.96 us
    pallas_call x1, Pallas kernels, local(): pl.pallas_call(functools.partial(second_kernel, peers, peers_tp, slots, h...  5.58 us
    pallas_call x1, Pallas kernels, local(): pl.pallas_call(functools.partial(cache_kernel, slots), out_shape=jax.Shap...  3.58 us
    pallas_call x1, Pallas kernels, local(): pl.pallas_call(functools.partial(attend_kernel, slots, heads), out_shape=...  3.17 us
    pallas_call x1, Pallas kernels, local(): pl.pallas_call(functools.partial(prepare_kernel, peers, slots), out_shape...  2.19 us
    pallas_call x1, Pallas kernels, local(): pl.pallas_call(functools.partial(out_kernel, peers, peers_tp), out_shape=...  1.43 us
  transfers between devices with their start and end apart: 17, of which 6 were waited for; matrix products, arithmetic and copies ran while one was open for 0% of the time, Pallas kernels for 15%

profile of v15, /device:TPU:0, one launch (start us, length us, event | category | flops | bytes accessed | tf_op | source)
XLA Modules:
  0.0 67.6 jit_solution(14821397811143892980)
XLA Ops:
  0.6 0.1 pad_add_fusion.meta
  0.7 0.0 copy-start.7
  0.7 7.0 %first_step.1 = (f32[384,128]{1,0:T(8,128)S(1)}, f32[48,128]{1,0:T(8,128)S(1)}, f32[48,128]{1,0:T(8,128)S(1)}, s32[12]{0:T(128)S(1)}, bf16[54,2,256,128]{3,2,1,0...) custom-call(s32[2]{0:T(128)S(1)} %pad_add_fusion.meta, ...), custom_call_target="tpu_custom_call" | custom-call | flops 301989888 | bytes 6291456 | tf_op jit(solution)/shard_map/first_step/pallas_call | solution.py:519
  7.7 0.5 collective-permute-start
  8.2 2.6 %collective-permute-start.1 = (f32[2,1536]{1,0:T(2,128)S(1)}, f32[2,1536]{1,0:T(2,128)S(1)}, u32[]{:S(2)}, u32[]{:S(2)}) collective-permute-start(f32[2,1536]{1,0:T(2,128)S(1)} %get-tuple-element.34), channel_id=1, source_target_pairs={{0,8},{4,12},{8,0},{12,4},{1,9},{5,13},{9,1},{13,5},{2,10},{6,14},... | collective-permute-start | bytes 36872 | tf_op jit(solution)/shard_map/ppermute | solution.py:485
  10.8 0.1 collective-permute-start.2
  10.9 0.0 copy-done.7
  10.9 0.0 copy-start.1
  10.9 0.0 copy-start.3
  10.9 3.2 %attention.1 = (bf16[48,512]{1,0:T(8,128)(2,1)S(1)}, bf16[54,2,256,128]{3,2,1,0:T(8,128)(2,1)S(1)}) custom-call(s32[2]{0:T(128)S(1)} %pad_add_fusion.meta, s32[192]{0:T(256)S(1)} %copy-done.7, f32[384,128]{1,0:T(8,128)S(1)} %get-tuple-element.28.query, f32[48,128]{1,0:T(8,128)S(1)} %get-tuple-element.29.newkey, ...), custom_call_target="tpu_custom_call", output_to_operand_aliasing={{1}: (6, {})} | custom-call | flops 25165824 | bytes 6291456 | tf_op jit(solution)/shard_map/attention/pallas_call | solution.py:560
  14.0 0.0 collective-permute-done.1.rest_0_
  14.1 0.0 collective-permute-done.2.rest_1_
  14.1 0.0 collective-permute-done.box_hbm.rest_4_
  14.1 0.0 copy-done.1
  14.1 0.0 copy-done.3
  14.1 0.0 copy-start.2
  14.1 0.0 copy-start.4
  14.1 0.0 copy-start.5
  14.1 0.0 copy-start.8
  14.1 1.4 %out_projection.1 = (f32[48,1024]{1,0:T(8,128)S(1)}, bf16[48,1024]{1,0:T(8,128)(2,1)S(1)}, bf16[48,1024]{1,0:T(8,128)(2,1)S(1)}, bf16[48,1024]{1,0:T(8,128)(2,1)S(1)}) custom-call(s32[2]{0:T(128)S(1)} %pad_add_fusion.meta, s32[12]{0:T(128)S(1)} %get-tuple-element.27.plan, bf16[48,512]{1,0:T(8,128)(2,1)S(1)} %get-tuple-element.32.attended, ...), custom_call_target="tpu_custom_call" | custom-call | flops 201326592 | bytes 4194304 | tf_op jit(solution)/shard_map/out_projection/pallas_call | solution.py:575
  15.6 3.9 %collective-permute-start.3 = (bf16[48,1024]{1,0:T(8,128)(2,1)S(1)}, bf16[48,1024]{1,0:T(8,128)(2,1)S(1)}, u32[]{:S(2)}, u32[]{:S(2)}) collective-permute-start(bf16[48,1024]{1,0:T(8,128)(2,1)S(1)} %get-tuple-element.42), channel_id=1, source_target_pairs={{0,3},{1,2},{2,1},{3,0},{4,7},{5,6},{6,5},{7,4},{8,11},{9,10},{10,... | collective-permute-start | bytes 294920 | tf_op jit(solution)/shard_map/ppermute | solution.py:485
  19.5 0.0 collective-permute-start.4
  19.5 0.6 collective-permute-start.5
  20.1 1.3 %pack.1 = (bf16[2,2,256,128]{3,2,1,0:T(8,128)(2,1)S(1)}, bf16[2,2,256,128]{3,2,1,0:T(8,128)(2,1)S(1)}) custom-call(s32[12]{0:T(128)S(1)} %get-tuple-element.27.plan, bf16[54,2,256,128]{3,2,1,0:T(8,128)(2,1)S(1)} %get-tuple-element.41.cache._, f32[48,1024]{1,0:T(8,128)S(1)} %get-tuple-element.36._.own._own), custom_call_target="tpu_custom_call" | custom-call | flops 1 | bytes 6291456 | tf_op jit(solution)/shard_map/pack/pallas_call | solution.py:585
  21.4 1.7 %collective-permute-start.9 = (bf16[2,2,256,128]{3,2,1,0:T(8,128)(2,1)S(1)}, bf16[2,2,256,128]{3,2,1,0:T(8,128)(2,1)S(1)}, u32[]{:S(2)}, u32[]{:S(2)}) collective-permute-start(bf16[2,2,256,128]{3,2,1,0:T(8,128)(2,1)S(1)} %get-tuple-element.45), channel_id=1, source_target_pairs={{0,8},{4,12},{8,0},{12,4},{1,9},{5,13},{9,1},{13,5},{2,10},{6,14},... | collective-permute-start | bytes 786440 | tf_op jit(solution)/shard_map/ppermute | solution.py:485
  23.1 0.0 collective-permute-start.10
  23.1 0.0 collective-permute-done.3.rest_0_
  23.1 5.1 %collective-permute-done.4.rest_1_ = bf16[48,1024]{1,0:T(8,128)(2,1)S(1)} collective-permute-done((bf16[48,1024]{1,0:T(8,128)(2,1)S(1)}, bf16[48,1024]{1,0:T(8,128)(2,1)S(1)}, u32[]{:S(2)}, u32[]{:S(2)}) %collective-permute-start.4) | collective-permute-done | bytes 98336 | tf_op jit(solution)/shard_map/ppermute | solution.py:485
  28.2 0.0 collective-permute-done.5.rest_2_
  28.2 0.1 sum_terms.2.rest_0_
  28.3 0.0 copy-start
  28.3 0.0 copy-start.6
  28.3 2.5 %collective-permute-start.8 = (bf16[48,1024]{1,0:T(8,128)(2,1)S(1)}, bf16[48,1024]{1,0:T(8,128)(2,1)S(1)}, u32[]{:S(2)}, u32[]{:S(2)}) collective-permute-start(bf16[48,1024]{1,0:T(8,128)(2,1)S(1)} %sum_terms.2.rest_0_), channel_id=1, source_target_pairs={{0,3},{1,2},{2,1},{3,0},{4,7},{5,6},{6,5},{7,4},{8,11},{9,10},{10,... | collective-permute-start | bytes 294920 | tf_op jit(solution)/shard_map/ppermute | solution.py:485
  30.9 0.0 collective-permute-start.7
  30.9 1.9 %collective-permute-start.6 = (bf16[48,1024]{1,0:T(8,128)(2,1)S(1)}, bf16[48,1024]{1,0:T(8,128)(2,1)S(1)}, u32[]{:S(2)}, u32[]{:S(2)}) collective-permute-start(bf16[48,1024]{1,0:T(8,128)(2,1)S(1)} %sum_terms.2.rest_0_), channel_id=1, source_target_pairs={{0,1},{1,0},{2,3},{3,2},{4,5},{5,4},{6,7},{7,6},{8,9},{9,8},{10,11... | collective-permute-start | bytes 294920 | tf_op jit(solution)/shard_map/ppermute | solution.py:485
  32.8 0.0 copy-done.2
  32.8 0.0 copy-done.4
  32.8 0.0 copy-done.5
  32.8 0.0 copy-done.8
  32.8 2.2 %prepare.1 = (bf16[4096,256]{1,0:T(8,128)(2,1)S(1)}, f32[48,128]{1,0:T(8,128)S(1)}, f32[48,128]{1,0:T(8,128)S(1)}, s32[48]{0:T(128)S(1)}) custom-call(s32[2]{0:T(128)S(1)} %pad_add_fusion.meta, s32[192]{0:T(256)S(1)} %copy-done.8, s32[192]{0:T(256)S(1)} %copy-done.7, s32[12]{0:T(128)S(1)} %get-tuple-element.27.plan, f32[256,128]{1,0:T(8,128)S(1)} %copy-done.5, ...), custom_call_target="tpu_custom_call" | custom-call | flops 30198988800 | bytes 41943040 | tf_op jit(solution)/shard_map/prepare/pallas_call | solution.py:618
  35.0 0.9 %collective-permute-done.8.rest_3_ = bf16[48,1024]{1,0:T(8,128)(2,1)S(1)} collective-permute-done((bf16[48,1024]{1,0:T(8,128)(2,1)S(1)}, bf16[48,1024]{1,0:T(8,128)(2,1)S(1)}, u32[]{:S(2)}, u32[]{:S(2)}) %collective-permute-start.8) | collective-permute-done | bytes 98336 | tf_op jit(solution)/shard_map/ppermute | solution.py:485
  35.9 3.4 %collective-permute-done.7.rest_2_ = bf16[48,1024]{1,0:T(8,128)(2,1)S(1)} collective-permute-done((bf16[48,1024]{1,0:T(8,128)(2,1)S(1)}, bf16[48,1024]{1,0:T(8,128)(2,1)S(1)}, u32[]{:S(2)}, u32[]{:S(2)}) %collective-permute-start.7) | collective-permute-done | bytes 98336 | tf_op jit(solution)/shard_map/ppermute | solution.py:485
  39.3 0.0 collective-permute-done.6.rest_1_
  39.3 0.0 collective-permute-done.9.rest_5_
  39.3 0.0 collective-permute-done.10.rest_6_
  39.3 0.0 copy-done
  39.3 0.0 copy-done.6
  39.3 5.6 %second_step.1 = (f32[48,1024]{1,0:T(8,128)S(1)}, bf16[48,1024]{1,0:T(8,128)(2,1)S(1)}, bf16[48,1024]{1,0:T(8,128)(2,1)S(1)}, bf16[48,1024]{1,0:T(8,128)(2,1)S(1)}, bf16[54,2,256,128]{3,2,1,0:T(8,128)(2,1)S(1)}) custom-call(s32[2]{0:T(128)S(1)} %pad_add_fusion.meta, s32[192]{0:T(256)S(1)} %copy-done.8, ...), custom_call_target="tpu_custom_call", output_to_operand_aliasing={{4}: (10, {})} | custom-call | flops 905969664 | bytes 18874368 | tf_op jit(solution)/shard_map/second_step/pallas_call | solution.py:633
  44.9 1.9 %collective-permute-start.11 = (bf16[48,1024]{1,0:T(8,128)(2,1)S(1)}, bf16[48,1024]{1,0:T(8,128)(2,1)S(1)}, u32[]{:S(2)}, u32[]{:S(2)}) collective-permute-start(bf16[48,1024]{1,0:T(8,128)(2,1)S(1)} %get-tuple-element.48), channel_id=1, source_target_pairs={{0,3},{1,2},{2,1},{3,0},{4,7},{5,6},{6,5},{7,4},{8,11},{9,10},{10,... | collective-permute-start | bytes 294920 | tf_op jit(solution)/shard_map/ppermute | solution.py:485
  46.8 0.0 collective-permute-start.12
  46.8 2.6 %collective-permute-start.13 = (bf16[48,1024]{1,0:T(8,128)(2,1)S(1)}, bf16[48,1024]{1,0:T(8,128)(2,1)S(1)}, u32[]{:S(2)}, u32[]{:S(2)}) collective-permute-start(bf16[48,1024]{1,0:T(8,128)(2,1)S(1)} %get-tuple-element.50), channel_id=1, source_target_pairs={{0,1},{1,0},{2,3},{3,2},{4,5},{5,4},{6,7},{7,6},{8,9},{9,8},{10,11... | collective-permute-start | bytes 294920 | tf_op jit(solution)/shard_map/ppermute | solution.py:485
  49.3 3.2 %collective-permute-done.11.rest_0_ = bf16[48,1024]{1,0:T(8,128)(2,1)S(1)} collective-permute-done((bf16[48,1024]{1,0:T(8,128)(2,1)S(1)}, bf16[48,1024]{1,0:T(8,128)(2,1)S(1)}, u32[]{:S(2)}, u32[]{:S(2)}) %collective-permute-start.11) | collective-permute-done | bytes 98336 | tf_op jit(solution)/shard_map/ppermute | solution.py:485
  52.5 2.9 %collective-permute-done.12.rest_1_ = bf16[48,1024]{1,0:T(8,128)(2,1)S(1)} collective-permute-done((bf16[48,1024]{1,0:T(8,128)(2,1)S(1)}, bf16[48,1024]{1,0:T(8,128)(2,1)S(1)}, u32[]{:S(2)}, u32[]{:S(2)}) %collective-permute-start.12) | collective-permute-done | bytes 98336 | tf_op jit(solution)/shard_map/ppermute | solution.py:485
  55.4 0.0 collective-permute-done.13.rest_2_
  55.4 2.2 %collective-permute-start.16 = (bf16[48,1024]{1,0:T(8,128)(2,1)S(1)}, bf16[48,1024]{1,0:T(8,128)(2,1)S(1)}, u32[]{:S(2)}, u32[]{:S(2)}) collective-permute-start(bf16[48,1024]{1,0:T(8,128)(2,1)S(1)} %sum_terms.3.rest_0_), channel_id=1, source_target_pairs={{0,3},{1,2},{2,1},{3,0},{4,7},{5,6},{6,5},{7,4},{8,11},{9,10},{10,... | collective-permute-start | bytes 294920 | tf_op jit(solution)/shard_map/ppermute | solution.py:485
  57.6 0.0 collective-permute-start.15
  57.6 2.3 %collective-permute-start.14 = (bf16[48,1024]{1,0:T(8,128)(2,1)S(1)}, bf16[48,1024]{1,0:T(8,128)(2,1)S(1)}, u32[]{:S(2)}, u32[]{:S(2)}) collective-permute-start(bf16[48,1024]{1,0:T(8,128)(2,1)S(1)} %sum_terms.3.rest_0_), channel_id=1, source_target_pairs={{0,1},{1,0},{2,3},{3,2},{4,5},{5,4},{6,7},{7,6},{8,9},{9,8},{10,11... | collective-permute-start | bytes 294920 | tf_op jit(solution)/shard_map/ppermute | solution.py:485
  59.9 3.6 %write_cache.1 = bf16[48,2,256,128]{3,2,1,0:T(8,128)(2,1)} custom-call(s32[48]{0:T(128)S(1)} %get-tuple-element.37.place, bf16[54,2,256,128]{3,2,1,0:T(8,128)(2,1)S(1)} %get-tuple-element.51.cache), custom_call_target="tpu_custom_call" | custom-call | bytes 12582912 | tf_op jit(solution)/shard_map/write_cache/pallas_call | solution.py:652
  63.5 0.0 collective-permute-done.16.rest_3_
  63.5 2.8 %collective-permute-done.15.rest_2_ = bf16[48,1024]{1,0:T(8,128)(2,1)S(1)} collective-permute-done((bf16[48,1024]{1,0:T(8,128)(2,1)S(1)}, bf16[48,1024]{1,0:T(8,128)(2,1)S(1)}, u32[]{:S(2)}, u32[]{:S(2)}) %collective-permute-start.15) | collective-permute-done | bytes 98336 | tf_op jit(solution)/shard_map/ppermute | solution.py:485
  66.3 0.0 collective-permute-done.14.rest_1_
  66.3 1.3 %join.1 = bf16[48,4096]{1,0:T(8,128)(2,1)} custom-call(s32[2]{0:T(128)S(1)} %pad_add_fusion.meta, bf16[48,1024]{1,0:T(8,128)(2,1)S(1)} %sum_terms.3.rest_0_, bf16[48,1024]{1,0:T(8,128)(2,1)S(1)} %collective-permute-done.14.rest_1_, bf16[48,1024]{1,0:T(8,128)(2,1)S(1)} %collective-permute-done.15.rest_2_, bf16[48,1024]{1,0:T(8,128)(2,1)S(1)} %collective-permute-done.16.rest_3_), custom_call_target="tpu_custom_call" | custom-call | tf_op jit(solution)/shard_map/join/pallas_call | solution.py:662
  (1 shorter events, 0.0 us)
Async XLA Ops:
  0.7 10.2 %copy-start.7 = (s32[192]{0:T(256)S(1)}, s32[192]{0:T(256)}, u32[]{:S(2)}) copy-start(s32[192]{0:T(256)} %lengths_s.5) | copy-start | bytes 2308
  7.7 6.4 %collective-permute-start = (bf16[2,2,272,128]{3,2,1,0:T(8,128)(2,1)S(1)}, bf16[2,2,272,128]{3,2,1,0:T(8,128)(2,1)S(1)}, u32[]{:S(2)}, u32[]{:S(2)}) collective-permute-start(bf16[2,2,272,128]{3,2,1,0:T(8,128)(2,1)S(1)} %get-tuple-element.33), channel_id=1, source_target_pairs={{0,4},{4,0},{8,12},{12,8},{1,5},{5,1},{9,13},{13,9},{2,6},{6,2},{1... | collective-permute-start | bytes 835592 | tf_op jit(solution)/shard_map/ppermute | solution.py:485
  8.2 5.9 %collective-permute-start.1 = (f32[2,1536]{1,0:T(2,128)S(1)}, f32[2,1536]{1,0:T(2,128)S(1)}, u32[]{:S(2)}, u32[]{:S(2)}) collective-permute-start(f32[2,1536]{1,0:T(2,128)S(1)} %get-tuple-element.34), channel_id=1, source_target_pairs={{0,8},{4,12},{8,0},{12,4},{1,9},{5,13},{9,1},{13,5},{2,10},{6,14},... | collective-permute-start | bytes 36872 | tf_op jit(solution)/shard_map/ppermute | solution.py:485
  10.8 3.3 %collective-permute-start.2 = (f32[2,1536]{1,0:T(2,128)S(1)}, f32[2,1536]{1,0:T(2,128)S(1)}, u32[]{:S(2)}, u32[]{:S(2)}) collective-permute-start(f32[2,1536]{1,0:T(2,128)S(1)} %get-tuple-element.35), channel_id=1, source_target_pairs={{0,12},{4,8},{8,4},{12,0},{1,13},{5,9},{9,5},{13,1},{2,14},{6,10},... | collective-permute-start | bytes 36872 | tf_op jit(solution)/shard_map/ppermute | solution.py:485
  10.9 3.2 %copy-start.1 = (bf16[512,4096]{1,0:T(8,128)(2,1)S(1)}, bf16[512,4096]{1,0:T(8,128)(2,1)}, u32[]{:S(2)}) copy-start(bf16[512,4096]{1,0:T(8,128)(2,1)} %wo.3) | copy-start | bytes 12582916
  10.9 3.2 %copy-start.3 = (bf16[48,4096]{1,0:T(8,128)(2,1)S(1)}, bf16[48,4096]{1,0:T(8,128)(2,1)}, u32[]{:S(2)}) copy-start(bf16[48,4096]{1,0:T(8,128)(2,1)} %hidden.1) | copy-start | bytes 1179652
  14.1 18.7 %copy-start.2 = (bf16[4096,2,128]{2,1,0:T(2,128)(2,1)S(1)}, bf16[4096,2,128]{2,1,0:T(2,128)(2,1)}, u32[]{:S(2)}) copy-start(bf16[4096,2,128]{2,1,0:T(2,128)(2,1)} %param.16) | copy-start | bytes 6291460
  14.1 18.7 %copy-start.4 = (f32[256,128]{1,0:T(8,128)S(1)}, f32[256,128]{1,0:T(8,128)}, u32[]{:S(2)}) copy-start(f32[256,128]{1,0:T(8,128)} %constant.12.clone.sin_hbm.sin_ref) | copy-start | bytes 393220
  14.1 18.7 %copy-start.5 = (f32[256,128]{1,0:T(8,128)S(1)}, f32[256,128]{1,0:T(8,128)}, u32[]{:S(2)}) copy-start(f32[256,128]{1,0:T(8,128)} %constant.11.clone.cos_hbm.cos_ref) | copy-start | bytes 393220
  14.1 18.6 %copy-start.8 = (s32[192]{0:T(256)S(1)}, s32[192]{0:T(256)}, u32[]{:S(2)}) copy-start(s32[192]{0:T(256)} %source_s.3) | copy-start | bytes 2308
  15.6 7.5 %collective-permute-start.3 = (bf16[48,1024]{1,0:T(8,128)(2,1)S(1)}, bf16[48,1024]{1,0:T(8,128)(2,1)S(1)}, u32[]{:S(2)}, u32[]{:S(2)}) collective-permute-start(bf16[48,1024]{1,0:T(8,128)(2,1)S(1)} %get-tuple-element.42), channel_id=1, source_target_pairs={{0,3},{1,2},{2,1},{3,0},{4,7},{5,6},{6,5},{7,4},{8,11},{9,10},{10,... | collective-permute-start | bytes 294920 | tf_op jit(solution)/shard_map/ppermute | solution.py:485
  19.5 8.8 %collective-permute-start.4 = (bf16[48,1024]{1,0:T(8,128)(2,1)S(1)}, bf16[48,1024]{1,0:T(8,128)(2,1)S(1)}, u32[]{:S(2)}, u32[]{:S(2)}) collective-permute-start(bf16[48,1024]{1,0:T(8,128)(2,1)S(1)} %get-tuple-element.43), channel_id=1, source_target_pairs={{0,2},{1,3},{2,0},{3,1},{4,6},{5,7},{6,4},{7,5},{8,10},{9,11},{10,... | collective-permute-start | bytes 294920 | tf_op jit(solution)/shard_map/ppermute | solution.py:485
  19.5 8.8 %collective-permute-start.5 = (bf16[48,1024]{1,0:T(8,128)(2,1)S(1)}, bf16[48,1024]{1,0:T(8,128)(2,1)S(1)}, u32[]{:S(2)}, u32[]{:S(2)}) collective-permute-start(bf16[48,1024]{1,0:T(8,128)(2,1)S(1)} %get-tuple-element.44), channel_id=1, source_target_pairs={{0,1},{1,0},{2,3},{3,2},{4,5},{5,4},{6,7},{7,6},{8,9},{9,8},{10,11... | collective-permute-start | bytes 294920 | tf_op jit(solution)/shard_map/ppermute | solution.py:485
  21.4 17.9 %collective-permute-start.9 = (bf16[2,2,256,128]{3,2,1,0:T(8,128)(2,1)S(1)}, bf16[2,2,256,128]{3,2,1,0:T(8,128)(2,1)S(1)}, u32[]{:S(2)}, u32[]{:S(2)}) collective-permute-start(bf16[2,2,256,128]{3,2,1,0:T(8,128)(2,1)S(1)} %get-tuple-element.45), channel_id=1, source_target_pairs={{0,8},{4,12},{8,0},{12,4},{1,9},{5,13},{9,1},{13,5},{2,10},{6,14},... | collective-permute-start | bytes 786440 | tf_op jit(solution)/shard_map/ppermute | solution.py:485
  23.1 16.2 %collective-permute-start.10 = (bf16[2,2,256,128]{3,2,1,0:T(8,128)(2,1)S(1)}, bf16[2,2,256,128]{3,2,1,0:T(8,128)(2,1)S(1)}, u32[]{:S(2)}, u32[]{:S(2)}) collective-permute-start(bf16[2,2,256,128]{3,2,1,0:T(8,128)(2,1)S(1)} %get-tuple-element.46), channel_id=1, source_target_pairs={{0,12},{4,8},{8,4},{12,0},{1,13},{5,9},{9,5},{13,1},{2,14},{6,10},... | collective-permute-start | bytes 786440 | tf_op jit(solution)/shard_map/ppermute | solution.py:485
  28.3 11.0 %copy-start = (bf16[4096,512]{1,0:T(8,128)(2,1)S(1)}, bf16[4096,512]{1,0:T(8,128)(2,1)}, u32[]{:S(2)}) copy-start(bf16[4096,512]{1,0:T(8,128)(2,1)} %wq.1) | copy-start | bytes 12582916
  28.3 11.0 %copy-start.6 = (f32[4096]{0:T(1024)S(1)}, f32[4096]{0:T(1024)}, u32[]{:S(2)}) copy-start(f32[4096]{0:T(1024)} %param.14) | copy-start | bytes 49156
  28.3 7.6 %collective-permute-start.8 = (bf16[48,1024]{1,0:T(8,128)(2,1)S(1)}, bf16[48,1024]{1,0:T(8,128)(2,1)S(1)}, u32[]{:S(2)}, u32[]{:S(2)}) collective-permute-start(bf16[48,1024]{1,0:T(8,128)(2,1)S(1)} %sum_terms.2.rest_0_), channel_id=1, source_target_pairs={{0,3},{1,2},{2,1},{3,0},{4,7},{5,6},{6,5},{7,4},{8,11},{9,10},{10,... | collective-permute-start | bytes 294920 | tf_op jit(solution)/shard_map/ppermute | solution.py:485
  30.9 8.4 %collective-permute-start.7 = (bf16[48,1024]{1,0:T(8,128)(2,1)S(1)}, bf16[48,1024]{1,0:T(8,128)(2,1)S(1)}, u32[]{:S(2)}, u32[]{:S(2)}) collective-permute-start(bf16[48,1024]{1,0:T(8,128)(2,1)S(1)} %sum_terms.2.rest_0_), channel_id=1, source_target_pairs={{0,2},{1,3},{2,0},{3,1},{4,6},{5,7},{6,4},{7,5},{8,10},{9,11},{10,... | collective-permute-start | bytes 294920 | tf_op jit(solution)/shard_map/ppermute | solution.py:485
  30.9 8.4 %collective-permute-start.6 = (bf16[48,1024]{1,0:T(8,128)(2,1)S(1)}, bf16[48,1024]{1,0:T(8,128)(2,1)S(1)}, u32[]{:S(2)}, u32[]{:S(2)}) collective-permute-start(bf16[48,1024]{1,0:T(8,128)(2,1)S(1)} %sum_terms.2.rest_0_), channel_id=1, source_target_pairs={{0,1},{1,0},{2,3},{3,2},{4,5},{5,4},{6,7},{7,6},{8,9},{9,8},{10,11... | collective-permute-start | bytes 294920 | tf_op jit(solution)/shard_map/ppermute | solution.py:485
  44.9 7.6 %collective-permute-start.11 = (bf16[48,1024]{1,0:T(8,128)(2,1)S(1)}, bf16[48,1024]{1,0:T(8,128)(2,1)S(1)}, u32[]{:S(2)}, u32[]{:S(2)}) collective-permute-start(bf16[48,1024]{1,0:T(8,128)(2,1)S(1)} %get-tuple-element.48), channel_id=1, source_target_pairs={{0,3},{1,2},{2,1},{3,0},{4,7},{5,6},{6,5},{7,4},{8,11},{9,10},{10,... | collective-permute-start | bytes 294920 | tf_op jit(solution)/shard_map/ppermute | solution.py:485
  46.8 8.6 %collective-permute-start.12 = (bf16[48,1024]{1,0:T(8,128)(2,1)S(1)}, bf16[48,1024]{1,0:T(8,128)(2,1)S(1)}, u32[]{:S(2)}, u32[]{:S(2)}) collective-permute-start(bf16[48,1024]{1,0:T(8,128)(2,1)S(1)} %get-tuple-element.49), channel_id=1, source_target_pairs={{0,2},{1,3},{2,0},{3,1},{4,6},{5,7},{6,4},{7,5},{8,10},{9,11},{10,... | collective-permute-start | bytes 294920 | tf_op jit(solution)/shard_map/ppermute | solution.py:485
  46.8 8.6 %collective-permute-start.13 = (bf16[48,1024]{1,0:T(8,128)(2,1)S(1)}, bf16[48,1024]{1,0:T(8,128)(2,1)S(1)}, u32[]{:S(2)}, u32[]{:S(2)}) collective-permute-start(bf16[48,1024]{1,0:T(8,128)(2,1)S(1)} %get-tuple-element.50), channel_id=1, source_target_pairs={{0,1},{1,0},{2,3},{3,2},{4,5},{5,4},{6,7},{7,6},{8,9},{9,8},{10,11... | collective-permute-start | bytes 294920 | tf_op jit(solution)/shard_map/ppermute | solution.py:485
  55.4 8.0 %collective-permute-start.16 = (bf16[48,1024]{1,0:T(8,128)(2,1)S(1)}, bf16[48,1024]{1,0:T(8,128)(2,1)S(1)}, u32[]{:S(2)}, u32[]{:S(2)}) collective-permute-start(bf16[48,1024]{1,0:T(8,128)(2,1)S(1)} %sum_terms.3.rest_0_), channel_id=1, source_target_pairs={{0,3},{1,2},{2,1},{3,0},{4,7},{5,6},{6,5},{7,4},{8,11},{9,10},{10,... | collective-permute-start | bytes 294920 | tf_op jit(solution)/shard_map/ppermute | solution.py:485
  57.6 8.7 %collective-permute-start.15 = (bf16[48,1024]{1,0:T(8,128)(2,1)S(1)}, bf16[48,1024]{1,0:T(8,128)(2,1)S(1)}, u32[]{:S(2)}, u32[]{:S(2)}) collective-permute-start(bf16[48,1024]{1,0:T(8,128)(2,1)S(1)} %sum_terms.3.rest_0_), channel_id=1, source_target_pairs={{0,2},{1,3},{2,0},{3,1},{4,6},{5,7},{6,4},{7,5},{8,10},{9,11},{10,... | collective-permute-start | bytes 294920 | tf_op jit(solution)/shard_map/ppermute | solution.py:485
  57.6 8.7 %collective-permute-start.14 = (bf16[48,1024]{1,0:T(8,128)(2,1)S(1)}, bf16[48,1024]{1,0:T(8,128)(2,1)S(1)}, u32[]{:S(2)}, u32[]{:S(2)}) collective-permute-start(bf16[48,1024]{1,0:T(8,128)(2,1)S(1)} %sum_terms.3.rest_0_), channel_id=1, source_target_pairs={{0,1},{1,0},{2,3},{3,2},{4,5},{5,4},{6,7},{7,6},{8,9},{9,8},{10,11... | collective-permute-start | bytes 294920 | tf_op jit(solution)/shard_map/ppermute | solution.py:485

commit v16 on v14

--- a/solution.py
+++ b/solution.py
@@ -68,13 +68,9 @@
     spread[:, slots:, :] = spread_all[:, 2 * HD :].reshape(blocks, slots, 2 * HD)
 
 
-def project_from(normed3, weight, copies=()):
+def project_from(normed3, weight):
     total = None
-    pairs = normed3.shape[0] // 2
-    pieces = max(len(copies), 1)
-    for b in range(pairs):
-        if copies and b % (pairs // pieces) == 0:
-            copies[b // (pairs // pieces)].wait()
+    for b in range(normed3.shape[0] // 2):
         block = jnp.concatenate([normed3[2 * b], normed3[2 * b + 1]], axis=1)
         part = jnp.dot(
             block, weight[b * 2 * HD : (b + 1) * 2 * HD, :], preferred_element_type=F32
@@ -83,12 +79,9 @@
     return total
 
 
-def project_spread(spread, wkv, copies):
+def project_spread(spread, wkv):
     total = None
-    blocks = spread.shape[0]
-    for b in range(blocks):
-        if b % (blocks // len(copies)) == 0:
-            copies[b // (blocks // len(copies))].wait()
+    for b in range(spread.shape[0]):
         part = jnp.dot(
             spread[b], wkv[b * 2 * HD : (b + 1) * 2 * HD, :], preferred_element_type=F32
         )
@@ -221,11 +214,11 @@
         pltpu.make_async_copy(cache_hbm.at[slot], leaving.at[at], in_sem.at[at]).start()
     for copy in loads:
         copy.start()
-    for copy in small[3:]:
+    for copy in small[3:] + wkv_copies + wq_copies:
         copy.wait()
     gather_angles(lambda s: lengths_s[0, low + s], slots, cos_ref, sin_ref, cos_rows, sin_rows)
-    key, value = project_spread(spread, wkv, wkv_copies)
-    query = project_from(normed3, wq, wq_copies)
+    key, value = project_spread(spread, wkv)
+    query = project_from(normed3, wq)
     cosine, sine = cos_rows[...], sin_rows[...]
     query_out[...] = jnp.zeros(query_out.shape, F32)
     for g in range(heads):

time: 67.2 us -> 66.9 us (level)
  no operation moved by 1% of the time
where the time goes in v16:
time: 66.9 us; the launch traced here: 66.8 us
  Pallas kernels  24.8 us (37%)
  starting transfers between devices  22.5 us (34%)
  waiting for transfers between devices  18.6 us (28%)
  between operations  0.81 us (1%)
    ppermute x17, starting transfers between devices, swapped(): return lax.ppermute(x, axis, [(i, i ^ k) for i in range(size)])  22.5 us
    ppermute x17, waiting for transfers between devices, swapped(): return lax.ppermute(x, axis, [(i, i ^ k) for i in range(size)])  18.6 us
    pallas_call x1, Pallas kernels, local(): pl.pallas_call(functools.partial(first_kernel, peers, slots, heads, shard...  6.64 us
    pallas_call x1, Pallas kernels, local(): pl.pallas_call(functools.partial(second_kernel, peers, peers_tp, slots, h...  5.57 us
    pallas_call x1, Pallas kernels, local(): pl.pallas_call(functools.partial(cache_kernel, slots), out_shape=jax.Shap...  3.58 us
    pallas_call x1, Pallas kernels, local(): pl.pallas_call(functools.partial(attend_kernel, slots, heads), out_shape=...  2.68 us
    pallas_call x1, Pallas kernels, local(): pl.pallas_call(functools.partial(prepare_kernel, peers, slots), out_shape...  2.2 us
    pallas_call x1, Pallas kernels, local(): pl.pallas_call(functools.partial(out_kernel, peers, peers_tp), out_shape=...  1.43 us
  transfers between devices with their start and end apart: 17, of which 8 were waited for; matrix products, arithmetic and copies ran while one was open for 0% of the time, Pallas kernels for 15%

profile of v16, /device:TPU:0, one launch (start us, length us, event | category | flops | bytes accessed | tf_op | source)
XLA Modules:
  0.0 66.8 jit_solution(11347675245196771110)
XLA Ops:
  0.6 0.1 pad_add_fusion.meta
  0.7 0.0 copy-start.7
  0.7 6.6 %first_step.1 = (f32[384,128]{1,0:T(8,128)S(1)}, f32[48,128]{1,0:T(8,128)S(1)}, f32[48,128]{1,0:T(8,128)S(1)}, s32[12]{0:T(128)S(1)}, bf16[54,2,256,128]{3,2,1,0...) custom-call(s32[2]{0:T(128)S(1)} %pad_add_fusion.meta, ...), custom_call_target="tpu_custom_call" | custom-call | flops 301989888 | bytes 6291456 | tf_op jit(solution)/shard_map/first_step/pallas_call | solution.py:499
  7.4 0.0 copy-start.1
  7.4 0.0 copy-start.3
  7.4 0.5 collective-permute-start
  7.9 2.6 %collective-permute-start.1 = (f32[2,1536]{1,0:T(2,128)S(1)}, f32[2,1536]{1,0:T(2,128)S(1)}, u32[]{:S(2)}, u32[]{:S(2)}) collective-permute-start(f32[2,1536]{1,0:T(2,128)S(1)} %get-tuple-element.34), channel_id=1, source_target_pairs={{0,8},{4,12},{8,0},{12,4},{1,9},{5,13},{9,1},{13,5},{2,10},{6,14},... | collective-permute-start | bytes 36872 | tf_op jit(solution)/shard_map/ppermute | solution.py:465
  10.5 0.1 collective-permute-start.2
  10.6 0.0 copy-done.7
  10.6 2.7 %attention.1 = (bf16[48,512]{1,0:T(8,128)(2,1)S(1)}, bf16[54,2,256,128]{3,2,1,0:T(8,128)(2,1)S(1)}) custom-call(s32[2]{0:T(128)S(1)} %pad_add_fusion.meta, s32[192]{0:T(256)S(1)} %copy-done.7, f32[384,128]{1,0:T(8,128)S(1)} %get-tuple-element.28.query, f32[48,128]{1,0:T(8,128)S(1)} %get-tuple-element.29.newkey, ...), custom_call_target="tpu_custom_call", output_to_operand_aliasing={{1}: (5, {})} | custom-call | flops 25165824 | bytes 6291456 | tf_op jit(solution)/shard_map/attention/pallas_call | solution.py:540
  13.3 0.0 collective-permute-done.1.rest_0_
  13.3 0.3 collective-permute-done.2.rest_1_
  13.6 0.0 collective-permute-done.box_hbm.rest_4_
  13.6 0.0 copy-done.1
  13.6 0.0 copy-done.3
  13.6 0.0 copy-start.2
  13.6 0.0 copy-start.4
  13.7 0.0 copy-start.5
  13.7 0.0 copy-start.8
  13.7 1.4 %out_projection.1 = (f32[48,1024]{1,0:T(8,128)S(1)}, bf16[48,1024]{1,0:T(8,128)(2,1)S(1)}, bf16[48,1024]{1,0:T(8,128)(2,1)S(1)}, bf16[48,1024]{1,0:T(8,128)(2,1)S(1)}) custom-call(s32[2]{0:T(128)S(1)} %pad_add_fusion.meta, s32[12]{0:T(128)S(1)} %get-tuple-element.27.plan, bf16[48,512]{1,0:T(8,128)(2,1)S(1)} %get-tuple-element.32.attended, ...), custom_call_target="tpu_custom_call" | custom-call | flops 201326592 | bytes 4194304 | tf_op jit(solution)/shard_map/out_projection/pallas_call | solution.py:554
  15.1 3.7 %collective-permute-start.3 = (bf16[48,1024]{1,0:T(8,128)(2,1)S(1)}, bf16[48,1024]{1,0:T(8,128)(2,1)S(1)}, u32[]{:S(2)}, u32[]{:S(2)}) collective-permute-start(bf16[48,1024]{1,0:T(8,128)(2,1)S(1)} %get-tuple-element.42), channel_id=1, source_target_pairs={{0,3},{1,2},{2,1},{3,0},{4,7},{5,6},{6,5},{7,4},{8,11},{9,10},{10,... | collective-permute-start | bytes 294920 | tf_op jit(solution)/shard_map/ppermute | solution.py:465
  18.8 0.0 collective-permute-start.4
  18.8 0.8 %collective-permute-start.5 = (bf16[48,1024]{1,0:T(8,128)(2,1)S(1)}, bf16[48,1024]{1,0:T(8,128)(2,1)S(1)}, u32[]{:S(2)}, u32[]{:S(2)}) collective-permute-start(bf16[48,1024]{1,0:T(8,128)(2,1)S(1)} %get-tuple-element.44), channel_id=1, source_target_pairs={{0,1},{1,0},{2,3},{3,2},{4,5},{5,4},{6,7},{7,6},{8,9},{9,8},{10,11... | collective-permute-start | bytes 294920 | tf_op jit(solution)/shard_map/ppermute | solution.py:465
  19.6 1.3 %pack.1 = (bf16[2,2,256,128]{3,2,1,0:T(8,128)(2,1)S(1)}, bf16[2,2,256,128]{3,2,1,0:T(8,128)(2,1)S(1)}) custom-call(s32[12]{0:T(128)S(1)} %get-tuple-element.27.plan, bf16[54,2,256,128]{3,2,1,0:T(8,128)(2,1)S(1)} %get-tuple-element.41.cache._, f32[48,1024]{1,0:T(8,128)S(1)} %get-tuple-element.36._.own._own), custom_call_target="tpu_custom_call" | custom-call | flops 1 | bytes 6291456 | tf_op jit(solution)/shard_map/pack/pallas_call | solution.py:564
  20.8 1.5 %collective-permute-start.9 = (bf16[2,2,256,128]{3,2,1,0:T(8,128)(2,1)S(1)}, bf16[2,2,256,128]{3,2,1,0:T(8,128)(2,1)S(1)}, u32[]{:S(2)}, u32[]{:S(2)}) collective-permute-start(bf16[2,2,256,128]{3,2,1,0:T(8,128)(2,1)S(1)} %get-tuple-element.45), channel_id=1, source_target_pairs={{0,8},{4,12},{8,0},{12,4},{1,9},{5,13},{9,1},{13,5},{2,10},{6,14},... | collective-permute-start | bytes 786440 | tf_op jit(solution)/shard_map/ppermute | solution.py:465
  22.3 0.0 collective-permute-start.10
  22.3 0.4 collective-permute-done.3.rest_0_
  22.7 4.8 %collective-permute-done.4.rest_1_ = bf16[48,1024]{1,0:T(8,128)(2,1)S(1)} collective-permute-done((bf16[48,1024]{1,0:T(8,128)(2,1)S(1)}, bf16[48,1024]{1,0:T(8,128)(2,1)S(1)}, u32[]{:S(2)}, u32[]{:S(2)}) %collective-permute-start.4) | collective-permute-done | bytes 98336 | tf_op jit(solution)/shard_map/ppermute | solution.py:465
  27.5 0.0 collective-permute-done.5.rest_2_
  27.5 0.1 sum_terms.2.rest_0_
  27.5 0.0 copy-start
  27.5 0.0 copy-start.6
  27.5 2.5 %collective-permute-start.8 = (bf16[48,1024]{1,0:T(8,128)(2,1)S(1)}, bf16[48,1024]{1,0:T(8,128)(2,1)S(1)}, u32[]{:S(2)}, u32[]{:S(2)}) collective-permute-start(bf16[48,1024]{1,0:T(8,128)(2,1)S(1)} %sum_terms.2.rest_0_), channel_id=1, source_target_pairs={{0,3},{1,2},{2,1},{3,0},{4,7},{5,6},{6,5},{7,4},{8,11},{9,10},{10,... | collective-permute-start | bytes 294920 | tf_op jit(solution)/shard_map/ppermute | solution.py:465
  30.1 0.0 collective-permute-start.7
  30.1 1.9 %collective-permute-start.6 = (bf16[48,1024]{1,0:T(8,128)(2,1)S(1)}, bf16[48,1024]{1,0:T(8,128)(2,1)S(1)}, u32[]{:S(2)}, u32[]{:S(2)}) collective-permute-start(bf16[48,1024]{1,0:T(8,128)(2,1)S(1)} %sum_terms.2.rest_0_), channel_id=1, source_target_pairs={{0,1},{1,0},{2,3},{3,2},{4,5},{5,4},{6,7},{7,6},{8,9},{9,8},{10,11... | collective-permute-start | bytes 294920 | tf_op jit(solution)/shard_map/ppermute | solution.py:465
  32.0 0.0 copy-done.2
  32.0 0.0 copy-done.4
  32.0 0.0 copy-done.5
  32.0 0.0 copy-done.8
  32.0 2.2 %prepare.1 = (bf16[4096,256]{1,0:T(8,128)(2,1)S(1)}, f32[48,128]{1,0:T(8,128)S(1)}, f32[48,128]{1,0:T(8,128)S(1)}, s32[48]{0:T(128)S(1)}) custom-call(s32[2]{0:T(128)S(1)} %pad_add_fusion.meta, s32[192]{0:T(256)S(1)} %copy-done.8, s32[192]{0:T(256)S(1)} %copy-done.7, s32[12]{0:T(128)S(1)} %get-tuple-element.27.plan, f32[256,128]{1,0:T(8,128)S(1)} %copy-done.5, ...), custom_call_target="tpu_custom_call" | custom-call | flops 30198988800 | bytes 41943040 | tf_op jit(solution)/shard_map/prepare/pallas_call | solution.py:597
  34.2 0.9 %collective-permute-done.8.rest_3_ = bf16[48,1024]{1,0:T(8,128)(2,1)S(1)} collective-permute-done((bf16[48,1024]{1,0:T(8,128)(2,1)S(1)}, bf16[48,1024]{1,0:T(8,128)(2,1)S(1)}, u32[]{:S(2)}, u32[]{:S(2)}) %collective-permute-start.8) | collective-permute-done | bytes 98336 | tf_op jit(solution)/shard_map/ppermute | solution.py:465
  35.1 3.4 %collective-permute-done.7.rest_2_ = bf16[48,1024]{1,0:T(8,128)(2,1)S(1)} collective-permute-done((bf16[48,1024]{1,0:T(8,128)(2,1)S(1)}, bf16[48,1024]{1,0:T(8,128)(2,1)S(1)}, u32[]{:S(2)}, u32[]{:S(2)}) %collective-permute-start.7) | collective-permute-done | bytes 98336 | tf_op jit(solution)/shard_map/ppermute | solution.py:465
  38.5 0.0 collective-permute-done.6.rest_1_
  38.5 0.0 collective-permute-done.9.rest_5_
  38.5 0.0 collective-permute-done.10.rest_6_
  38.5 0.0 copy-done
  38.5 0.0 copy-done.6
  38.5 5.6 %second_step.1 = (f32[48,1024]{1,0:T(8,128)S(1)}, bf16[48,1024]{1,0:T(8,128)(2,1)S(1)}, bf16[48,1024]{1,0:T(8,128)(2,1)S(1)}, bf16[48,1024]{1,0:T(8,128)(2,1)S(1)}, bf16[54,2,256,128]{3,2,1,0:T(8,128)(2,1)S(1)}) custom-call(s32[2]{0:T(128)S(1)} %pad_add_fusion.meta, s32[192]{0:T(256)S(1)} %copy-done.8, ...), custom_call_target="tpu_custom_call", output_to_operand_aliasing={{4}: (10, {})} | custom-call | flops 905969664 | bytes 18874368 | tf_op jit(solution)/shard_map/second_step/pallas_call | solution.py:612
  44.1 1.8 %collective-permute-start.11 = (bf16[48,1024]{1,0:T(8,128)(2,1)S(1)}, bf16[48,1024]{1,0:T(8,128)(2,1)S(1)}, u32[]{:S(2)}, u32[]{:S(2)}) collective-permute-start(bf16[48,1024]{1,0:T(8,128)(2,1)S(1)} %get-tuple-element.48), channel_id=1, source_target_pairs={{0,3},{1,2},{2,1},{3,0},{4,7},{5,6},{6,5},{7,4},{8,11},{9,10},{10,... | collective-permute-start | bytes 294920 | tf_op jit(solution)/shard_map/ppermute | solution.py:465
  45.9 0.0 collective-permute-start.12
  45.9 2.6 %collective-permute-start.13 = (bf16[48,1024]{1,0:T(8,128)(2,1)S(1)}, bf16[48,1024]{1,0:T(8,128)(2,1)S(1)}, u32[]{:S(2)}, u32[]{:S(2)}) collective-permute-start(bf16[48,1024]{1,0:T(8,128)(2,1)S(1)} %get-tuple-element.50), channel_id=1, source_target_pairs={{0,1},{1,0},{2,3},{3,2},{4,5},{5,4},{6,7},{7,6},{8,9},{9,8},{10,11... | collective-permute-start | bytes 294920 | tf_op jit(solution)/shard_map/ppermute | solution.py:465
  48.6 3.2 %collective-permute-done.11.rest_0_ = bf16[48,1024]{1,0:T(8,128)(2,1)S(1)} collective-permute-done((bf16[48,1024]{1,0:T(8,128)(2,1)S(1)}, bf16[48,1024]{1,0:T(8,128)(2,1)S(1)}, u32[]{:S(2)}, u32[]{:S(2)}) %collective-permute-start.11) | collective-permute-done | bytes 98336 | tf_op jit(solution)/shard_map/ppermute | solution.py:465
  51.8 2.7 %collective-permute-done.12.rest_1_ = bf16[48,1024]{1,0:T(8,128)(2,1)S(1)} collective-permute-done((bf16[48,1024]{1,0:T(8,128)(2,1)S(1)}, bf16[48,1024]{1,0:T(8,128)(2,1)S(1)}, u32[]{:S(2)}, u32[]{:S(2)}) %collective-permute-start.12) | collective-permute-done | bytes 98336 | tf_op jit(solution)/shard_map/ppermute | solution.py:465
  54.5 0.0 collective-permute-done.13.rest_2_
  54.5 2.2 %collective-permute-start.16 = (bf16[48,1024]{1,0:T(8,128)(2,1)S(1)}, bf16[48,1024]{1,0:T(8,128)(2,1)S(1)}, u32[]{:S(2)}, u32[]{:S(2)}) collective-permute-start(bf16[48,1024]{1,0:T(8,128)(2,1)S(1)} %sum_terms.3.rest_0_), channel_id=1, source_target_pairs={{0,3},{1,2},{2,1},{3,0},{4,7},{5,6},{6,5},{7,4},{8,11},{9,10},{10,... | collective-permute-start | bytes 294920 | tf_op jit(solution)/shard_map/ppermute | solution.py:465
  56.8 0.0 collective-permute-start.15
  56.8 2.2 %collective-permute-start.14 = (bf16[48,1024]{1,0:T(8,128)(2,1)S(1)}, bf16[48,1024]{1,0:T(8,128)(2,1)S(1)}, u32[]{:S(2)}, u32[]{:S(2)}) collective-permute-start(bf16[48,1024]{1,0:T(8,128)(2,1)S(1)} %sum_terms.3.rest_0_), channel_id=1, source_target_pairs={{0,1},{1,0},{2,3},{3,2},{4,5},{5,4},{6,7},{7,6},{8,9},{9,8},{10,11... | collective-permute-start | bytes 294920 | tf_op jit(solution)/shard_map/ppermute | solution.py:465
  59.0 3.6 %write_cache.1 = bf16[48,2,256,128]{3,2,1,0:T(8,128)(2,1)} custom-call(s32[48]{0:T(128)S(1)} %get-tuple-element.37.place, bf16[54,2,256,128]{3,2,1,0:T(8,128)(2,1)S(1)} %get-tuple-element.51.cache), custom_call_target="tpu_custom_call" | custom-call | bytes 12582912 | tf_op jit(solution)/shard_map/write_cache/pallas_call | solution.py:631
  62.6 0.0 collective-permute-done.16.rest_3_
  62.6 2.8 %collective-permute-done.15.rest_2_ = bf16[48,1024]{1,0:T(8,128)(2,1)S(1)} collective-permute-done((bf16[48,1024]{1,0:T(8,128)(2,1)S(1)}, bf16[48,1024]{1,0:T(8,128)(2,1)S(1)}, u32[]{:S(2)}, u32[]{:S(2)}) %collective-permute-start.15) | collective-permute-done | bytes 98336 | tf_op jit(solution)/shard_map/ppermute | solution.py:465
  65.4 0.0 collective-permute-done.14.rest_1_
  65.4 1.3 %join.1 = bf16[48,4096]{1,0:T(8,128)(2,1)} custom-call(s32[2]{0:T(128)S(1)} %pad_add_fusion.meta, bf16[48,1024]{1,0:T(8,128)(2,1)S(1)} %sum_terms.3.rest_0_, bf16[48,1024]{1,0:T(8,128)(2,1)S(1)} %collective-permute-done.14.rest_1_, bf16[48,1024]{1,0:T(8,128)(2,1)S(1)} %collective-permute-done.15.rest_2_, bf16[48,1024]{1,0:T(8,128)(2,1)S(1)} %collective-permute-done.16.rest_3_), custom_call_target="tpu_custom_call" | custom-call | tf_op jit(solution)/shard_map/join/pallas_call | solution.py:641
  (1 shorter events, 0.0 us)
Async XLA Ops:
  0.7 9.9 %copy-start.7 = (s32[192]{0:T(256)S(1)}, s32[192]{0:T(256)}, u32[]{:S(2)}) copy-start(s32[192]{0:T(256)} %lengths_s.5) | copy-start | bytes 2308
  7.4 6.3 %copy-start.1 = (bf16[512,4096]{1,0:T(8,128)(2,1)S(1)}, bf16[512,4096]{1,0:T(8,128)(2,1)}, u32[]{:S(2)}) copy-start(bf16[512,4096]{1,0:T(8,128)(2,1)} %wo.3) | copy-start | bytes 12582916
  7.4 6.3 %copy-start.3 = (bf16[48,4096]{1,0:T(8,128)(2,1)S(1)}, bf16[48,4096]{1,0:T(8,128)(2,1)}, u32[]{:S(2)}) copy-start(bf16[48,4096]{1,0:T(8,128)(2,1)} %hidden.1) | copy-start | bytes 1179652
  7.4 6.2 %collective-permute-start = (bf16[2,2,272,128]{3,2,1,0:T(8,128)(2,1)S(1)}, bf16[2,2,272,128]{3,2,1,0:T(8,128)(2,1)S(1)}, u32[]{:S(2)}, u32[]{:S(2)}) collective-permute-start(bf16[2,2,272,128]{3,2,1,0:T(8,128)(2,1)S(1)} %get-tuple-element.33), channel_id=1, source_target_pairs={{0,4},{4,0},{8,12},{12,8},{1,5},{5,1},{9,13},{13,9},{2,6},{6,2},{1... | collective-permute-start | bytes 835592 | tf_op jit(solution)/shard_map/ppermute | solution.py:465
  7.9 5.4 %collective-permute-start.1 = (f32[2,1536]{1,0:T(2,128)S(1)}, f32[2,1536]{1,0:T(2,128)S(1)}, u32[]{:S(2)}, u32[]{:S(2)}) collective-permute-start(f32[2,1536]{1,0:T(2,128)S(1)} %get-tuple-element.34), channel_id=1, source_target_pairs={{0,8},{4,12},{8,0},{12,4},{1,9},{5,13},{9,1},{13,5},{2,10},{6,14},... | collective-permute-start | bytes 36872 | tf_op jit(solution)/shard_map/ppermute | solution.py:465
  10.5 3.1 %collective-permute-start.2 = (f32[2,1536]{1,0:T(2,128)S(1)}, f32[2,1536]{1,0:T(2,128)S(1)}, u32[]{:S(2)}, u32[]{:S(2)}) collective-permute-start(f32[2,1536]{1,0:T(2,128)S(1)} %get-tuple-element.35), channel_id=1, source_target_pairs={{0,12},{4,8},{8,4},{12,0},{1,13},{5,9},{9,5},{13,1},{2,14},{6,10},... | collective-permute-start | bytes 36872 | tf_op jit(solution)/shard_map/ppermute | solution.py:465
  13.6 18.4 %copy-start.2 = (bf16[4096,2,128]{2,1,0:T(2,128)(2,1)S(1)}, bf16[4096,2,128]{2,1,0:T(2,128)(2,1)}, u32[]{:S(2)}) copy-start(bf16[4096,2,128]{2,1,0:T(2,128)(2,1)} %param.16) | copy-start | bytes 6291460
  13.6 18.4 %copy-start.4 = (f32[256,128]{1,0:T(8,128)S(1)}, f32[256,128]{1,0:T(8,128)}, u32[]{:S(2)}) copy-start(f32[256,128]{1,0:T(8,128)} %constant.12.clone.sin_hbm.sin_ref) | copy-start | bytes 393220
  13.7 18.3 %copy-start.5 = (f32[256,128]{1,0:T(8,128)S(1)}, f32[256,128]{1,0:T(8,128)}, u32[]{:S(2)}) copy-start(f32[256,128]{1,0:T(8,128)} %constant.11.clone.cos_hbm.cos_ref) | copy-start | bytes 393220
  13.7 18.3 %copy-start.8 = (s32[192]{0:T(256)S(1)}, s32[192]{0:T(256)}, u32[]{:S(2)}) copy-start(s32[192]{0:T(256)} %source_s.3) | copy-start | bytes 2308
  15.1 7.6 %collective-permute-start.3 = (bf16[48,1024]{1,0:T(8,128)(2,1)S(1)}, bf16[48,1024]{1,0:T(8,128)(2,1)S(1)}, u32[]{:S(2)}, u32[]{:S(2)}) collective-permute-start(bf16[48,1024]{1,0:T(8,128)(2,1)S(1)} %get-tuple-element.42), channel_id=1, source_target_pairs={{0,3},{1,2},{2,1},{3,0},{4,7},{5,6},{6,5},{7,4},{8,11},{9,10},{10,... | collective-permute-start | bytes 294920 | tf_op jit(solution)/shard_map/ppermute | solution.py:465
  18.8 8.7 %collective-permute-start.4 = (bf16[48,1024]{1,0:T(8,128)(2,1)S(1)}, bf16[48,1024]{1,0:T(8,128)(2,1)S(1)}, u32[]{:S(2)}, u32[]{:S(2)}) collective-permute-start(bf16[48,1024]{1,0:T(8,128)(2,1)S(1)} %get-tuple-element.43), channel_id=1, source_target_pairs={{0,2},{1,3},{2,0},{3,1},{4,6},{5,7},{6,4},{7,5},{8,10},{9,11},{10,... | collective-permute-start | bytes 294920 | tf_op jit(solution)/shard_map/ppermute | solution.py:465
  18.8 8.7 %collective-permute-start.5 = (bf16[48,1024]{1,0:T(8,128)(2,1)S(1)}, bf16[48,1024]{1,0:T(8,128)(2,1)S(1)}, u32[]{:S(2)}, u32[]{:S(2)}) collective-permute-start(bf16[48,1024]{1,0:T(8,128)(2,1)S(1)} %get-tuple-element.44), channel_id=1, source_target_pairs={{0,1},{1,0},{2,3},{3,2},{4,5},{5,4},{6,7},{7,6},{8,9},{9,8},{10,11... | collective-permute-start | bytes 294920 | tf_op jit(solution)/shard_map/ppermute | solution.py:465
  20.8 17.7 %collective-permute-start.9 = (bf16[2,2,256,128]{3,2,1,0:T(8,128)(2,1)S(1)}, bf16[2,2,256,128]{3,2,1,0:T(8,128)(2,1)S(1)}, u32[]{:S(2)}, u32[]{:S(2)}) collective-permute-start(bf16[2,2,256,128]{3,2,1,0:T(8,128)(2,1)S(1)} %get-tuple-element.45), channel_id=1, source_target_pairs={{0,8},{4,12},{8,0},{12,4},{1,9},{5,13},{9,1},{13,5},{2,10},{6,14},... | collective-permute-start | bytes 786440 | tf_op jit(solution)/shard_map/ppermute | solution.py:465
  22.3 16.2 %collective-permute-start.10 = (bf16[2,2,256,128]{3,2,1,0:T(8,128)(2,1)S(1)}, bf16[2,2,256,128]{3,2,1,0:T(8,128)(2,1)S(1)}, u32[]{:S(2)}, u32[]{:S(2)}) collective-permute-start(bf16[2,2,256,128]{3,2,1,0:T(8,128)(2,1)S(1)} %get-tuple-element.46), channel_id=1, source_target_pairs={{0,12},{4,8},{8,4},{12,0},{1,13},{5,9},{9,5},{13,1},{2,14},{6,10},... | collective-permute-start | bytes 786440 | tf_op jit(solution)/shard_map/ppermute | solution.py:465
  27.5 11.0 %copy-start = (bf16[4096,512]{1,0:T(8,128)(2,1)S(1)}, bf16[4096,512]{1,0:T(8,128)(2,1)}, u32[]{:S(2)}) copy-start(bf16[4096,512]{1,0:T(8,128)(2,1)} %wq.1) | copy-start | bytes 12582916
  27.5 11.0 %copy-start.6 = (f32[4096]{0:T(1024)S(1)}, f32[4096]{0:T(1024)}, u32[]{:S(2)}) copy-start(f32[4096]{0:T(1024)} %param.14) | copy-start | bytes 49156
  27.5 7.6 %collective-permute-start.8 = (bf16[48,1024]{1,0:T(8,128)(2,1)S(1)}, bf16[48,1024]{1,0:T(8,128)(2,1)S(1)}, u32[]{:S(2)}, u32[]{:S(2)}) collective-permute-start(bf16[48,1024]{1,0:T(8,128)(2,1)S(1)} %sum_terms.2.rest_0_), channel_id=1, source_target_pairs={{0,3},{1,2},{2,1},{3,0},{4,7},{5,6},{6,5},{7,4},{8,11},{9,10},{10,... | collective-permute-start | bytes 294920 | tf_op jit(solution)/shard_map/ppermute | solution.py:465
  30.1 8.4 %collective-permute-start.7 = (bf16[48,1024]{1,0:T(8,128)(2,1)S(1)}, bf16[48,1024]{1,0:T(8,128)(2,1)S(1)}, u32[]{:S(2)}, u32[]{:S(2)}) collective-permute-start(bf16[48,1024]{1,0:T(8,128)(2,1)S(1)} %sum_terms.2.rest_0_), channel_id=1, source_target_pairs={{0,2},{1,3},{2,0},{3,1},{4,6},{5,7},{6,4},{7,5},{8,10},{9,11},{10,... | collective-permute-start | bytes 294920 | tf_op jit(solution)/shard_map/ppermute | solution.py:465
  30.1 8.4 %collective-permute-start.6 = (bf16[48,1024]{1,0:T(8,128)(2,1)S(1)}, bf16[48,1024]{1,0:T(8,128)(2,1)S(1)}, u32[]{:S(2)}, u32[]{:S(2)}) collective-permute-start(bf16[48,1024]{1,0:T(8,128)(2,1)S(1)} %sum_terms.2.rest_0_), channel_id=1, source_target_pairs={{0,1},{1,0},{2,3},{3,2},{4,5},{5,4},{6,7},{7,6},{8,9},{9,8},{10,11... | collective-permute-start | bytes 294920 | tf_op jit(solution)/shard_map/ppermute | solution.py:465
  44.1 7.7 %collective-permute-start.11 = (bf16[48,1024]{1,0:T(8,128)(2,1)S(1)}, bf16[48,1024]{1,0:T(8,128)(2,1)S(1)}, u32[]{:S(2)}, u32[]{:S(2)}) collective-permute-start(bf16[48,1024]{1,0:T(8,128)(2,1)S(1)} %get-tuple-element.48), channel_id=1, source_target_pairs={{0,3},{1,2},{2,1},{3,0},{4,7},{5,6},{6,5},{7,4},{8,11},{9,10},{10,... | collective-permute-start | bytes 294920 | tf_op jit(solution)/shard_map/ppermute | solution.py:465
  45.9 8.6 %collective-permute-start.12 = (bf16[48,1024]{1,0:T(8,128)(2,1)S(1)}, bf16[48,1024]{1,0:T(8,128)(2,1)S(1)}, u32[]{:S(2)}, u32[]{:S(2)}) collective-permute-start(bf16[48,1024]{1,0:T(8,128)(2,1)S(1)} %get-tuple-element.49), channel_id=1, source_target_pairs={{0,2},{1,3},{2,0},{3,1},{4,6},{5,7},{6,4},{7,5},{8,10},{9,11},{10,... | collective-permute-start | bytes 294920 | tf_op jit(solution)/shard_map/ppermute | solution.py:465
  45.9 8.6 %collective-permute-start.13 = (bf16[48,1024]{1,0:T(8,128)(2,1)S(1)}, bf16[48,1024]{1,0:T(8,128)(2,1)S(1)}, u32[]{:S(2)}, u32[]{:S(2)}) collective-permute-start(bf16[48,1024]{1,0:T(8,128)(2,1)S(1)} %get-tuple-element.50), channel_id=1, source_target_pairs={{0,1},{1,0},{2,3},{3,2},{4,5},{5,4},{6,7},{7,6},{8,9},{9,8},{10,11... | collective-permute-start | bytes 294920 | tf_op jit(solution)/shard_map/ppermute | solution.py:465
  54.5 8.0 %collective-permute-start.16 = (bf16[48,1024]{1,0:T(8,128)(2,1)S(1)}, bf16[48,1024]{1,0:T(8,128)(2,1)S(1)}, u32[]{:S(2)}, u32[]{:S(2)}) collective-permute-start(bf16[48,1024]{1,0:T(8,128)(2,1)S(1)} %sum_terms.3.rest_0_), channel_id=1, source_target_pairs={{0,3},{1,2},{2,1},{3,0},{4,7},{5,6},{6,5},{7,4},{8,11},{9,10},{10,... | collective-permute-start | bytes 294920 | tf_op jit(solution)/shard_map/ppermute | solution.py:465
  56.8 8.7 %collective-permute-start.15 = (bf16[48,1024]{1,0:T(8,128)(2,1)S(1)}, bf16[48,1024]{1,0:T(8,128)(2,1)S(1)}, u32[]{:S(2)}, u32[]{:S(2)}) collective-permute-start(bf16[48,1024]{1,0:T(8,128)(2,1)S(1)} %sum_terms.3.rest_0_), channel_id=1, source_target_pairs={{0,2},{1,3},{2,0},{3,1},{4,6},{5,7},{6,4},{7,5},{8,10},{9,11},{10,... | collective-permute-start | bytes 294920 | tf_op jit(solution)/shard_map/ppermute | solution.py:465
  56.8 8.7 %collective-permute-start.14 = (bf16[48,1024]{1,0:T(8,128)(2,1)S(1)}, bf16[48,1024]{1,0:T(8,128)(2,1)S(1)}, u32[]{:S(2)}, u32[]{:S(2)}) collective-permute-start(bf16[48,1024]{1,0:T(8,128)(2,1)S(1)} %sum_terms.3.rest_0_), channel_id=1, source_target_pairs={{0,1},{1,0},{2,3},{3,2},{4,5},{5,4},{6,7},{7,6},{8,9},{9,8},{10,11... | collective-permute-start | bytes 294920 | tf_op jit(solution)/shard_map/ppermute | solution.py:465

commit v17 on v16

--- a/solution.py
+++ b/solution.py
@@ -205,16 +205,19 @@
     hidden32[...] = wide
     norm_into(normed3, [wide], [gain[...]], [0], width)
     spread_normed(normed3, spread, slots, width)
-    send_slots = []
-    for at in range(moving):
-        slot = moves[at, 0]
-        send_slots.append(slot)
+    send_slots = [moves[at, 0] for at in range(moving)]
+    fetches = [
+        pltpu.make_async_copy(cache_hbm.at[slot], leaving.at[at], in_sem.at[at])
+        for at, slot in enumerate(send_slots)
+    ]
+    for copy in fetches:
+        copy.start()
+    for at, slot in enumerate(send_slots):
         plan[moving + at] = slot
         plan[at] = moves[moving + at, 0]
-        pltpu.make_async_copy(cache_hbm.at[slot], leaving.at[at], in_sem.at[at]).start()
     for copy in loads:
         copy.start()
-    for copy in small[3:] + wkv_copies + wq_copies:
+    for copy in small[3:] + wkv_copies + wq_copies + fetches:
         copy.wait()
     gather_angles(lambda s: lengths_s[0, low + s], slots, cos_ref, sin_ref, cos_rows, sin_rows)
     key, value = project_spread(spread, wkv)
@@ -229,7 +232,6 @@
 
     positions = [lengths_s[0, low + slot] for slot in send_slots]
     for at, slot in enumerate(send_slots):
-        pltpu.make_async_copy(cache_hbm.at[slot], leaving.at[at], in_sem.at[at]).wait()
         put_row(
             leaving, at, positions[at],
             newkey_out[pl.ds(slot, 1), :], newvalue_out[pl.ds(slot, 1), :],
@@ -302,25 +304,22 @@
 
 
 def out_kernel(
-    peers, peers_tp, meta, plan, attended, wo, hidden, box_hbm, *rest,
+    peers, peers_tp, meta, plan, attended, wo, hidden, box, *rest,
 ):
     notes, rest = rest[: peers - 2], rest[peers - 2 :]
-    own, sends, (tail, sem) = rest[0], rest[1:peers_tp], rest[peers_tp:]
+    own, sends = rest[0], rest[1:peers_tp]
     shard = own.shape[1]
-    cap = box_hbm.shape[2] - NOTE
-    copy = pltpu.make_async_copy(box_hbm.at[:, 0, pl.ds(cap, NOTE), :], tail, sem.at[0])
-    copy.start()
+    cap = box.shape[2] - NOTE
     rows = attended[...].astype(F32)
     heads = rows.shape[1] // HD
     column = pl.multiple_of(meta[1] * shard, shard)
     residual = hidden[:, pl.ds(column, shard)].astype(F32)
     row_index = lax.broadcasted_iota(I32, rows.shape, 0)
     residual_index = lax.broadcasted_iota(I32, residual.shape, 0)
-    copy.wait()
     for at in range((peers - 1) * MOVE):
         m = at % MOVE
         if at < MOVE:
-            blocks = tail[m].astype(F32)
+            blocks = box[m, 0, cap : cap + NOTE, :].astype(F32)
             blocks = [blocks[b : b + 1, :] for b in range(heads + shard // HD)]
             note = jnp.concatenate(blocks, axis=1)
         else:
@@ -416,6 +415,8 @@
         width,
     )
     positions = [lengths_s[source_s[low + s]] + 1 for s in range(slots)]
+    for copy in loads:
+        copy.wait()
     query = project_from(normed3, wq)
     pair = project_from(normed3, wkv)
     key, value = pair[:, :HD], pair[:, HD:]
@@ -427,8 +428,6 @@
     newkey = turn(key, cosine, sine).astype(BF16).astype(F32)
     newvalue = value.astype(BF16).astype(F32)
 
-    for copy in loads:
-        copy.wait()
     places = [place[s] for s in range(slots)]
     for s, (at, p) in enumerate(zip(places, positions)):
         put_row(cache, at, p, newkey[s : s + 1, :], newvalue[s : s + 1, :])
@@ -554,9 +553,8 @@
     own, *sends = pl.pallas_call(
         functools.partial(out_kernel, peers, peers_tp),
         out_shape=sent,
-        in_specs=[SMEM] * 2 + [VMEM] * 3 + [ANY] + [VMEM] * (others - 1),
+        in_specs=[SMEM] * 2 + [VMEM] * (3 + others),
         out_specs=[VMEM] * peers_tp,
-        scratch_shapes=[pltpu.VMEM((MOVE, NOTE, HD), BF16), dma((1,))],
         compiler_params=params(16),
         cost_estimate=cost(2 * slots * width * heads * HD, out_weight.size * 2),
         name="out_projection",

time: 66.9 us -> 66.9 us (level)
  no operation moved by 1% of the time
where the time goes in v17:
time: 66.9 us; the launch traced here: 66.7 us
  Pallas kernels  24.7 us (37%)
  starting transfers between devices  22.5 us (34%)
  waiting for transfers between devices  18.6 us (28%)
  between operations  0.81 us (1%)
    ppermute x17, starting transfers between devices, swapped(): return lax.ppermute(x, axis, [(i, i ^ k) for i in range(size)])  22.5 us
    ppermute x17, waiting for transfers between devices, swapped(): return lax.ppermute(x, axis, [(i, i ^ k) for i in range(size)])  18.6 us
    pallas_call x1, Pallas kernels, local(): pl.pallas_call(functools.partial(first_kernel, peers, slots, heads, shard...  6.67 us
    pallas_call x1, Pallas kernels, local(): pl.pallas_call(functools.partial(second_kernel, peers, peers_tp, slots, h...  5.55 us
    pallas_call x1, Pallas kernels, local(): pl.pallas_call(functools.partial(cache_kernel, slots), out_shape=jax.Shap...  3.58 us
    pallas_call x1, Pallas kernels, local(): pl.pallas_call(functools.partial(attend_kernel, slots, heads), out_shape=...  2.68 us
    pallas_call x1, Pallas kernels, local(): pl.pallas_call(functools.partial(prepare_kernel, peers, slots), out_shape...  2.19 us
    pallas_call x1, Pallas kernels, local(): pl.pallas_call(functools.partial(out_kernel, peers, peers_tp), out_shape=...  1.4 us
  transfers between devices with their start and end apart: 17, of which 8 were waited for; matrix products, arithmetic and copies ran while one was open for 0% of the time, Pallas kernels for 15%

profile of v17, /device:TPU:0, one launch (start us, length us, event | category | flops | bytes accessed | tf_op | source)
XLA Modules:
  0.0 66.7 jit_solution(11275247854612110573)
XLA Ops:
  0.6 0.1 pad_add_fusion.meta
  0.7 0.0 copy-start.7
  0.7 6.7 %first_step.1 = (f32[384,128]{1,0:T(8,128)S(1)}, f32[48,128]{1,0:T(8,128)S(1)}, f32[48,128]{1,0:T(8,128)S(1)}, s32[12]{0:T(128)S(1)}, bf16[54,2,256,128]{3,2,1,0...) custom-call(s32[2]{0:T(128)S(1)} %pad_add_fusion.meta, ...), custom_call_target="tpu_custom_call" | custom-call | flops 301989888 | bytes 6291456 | tf_op jit(solution)/shard_map/first_step/pallas_call | solution.py:498
  7.4 0.0 copy-start.1
  7.4 0.0 copy-start.3
  7.4 0.5 collective-permute-start
  7.9 2.6 %collective-permute-start.1 = (f32[2,1536]{1,0:T(2,128)S(1)}, f32[2,1536]{1,0:T(2,128)S(1)}, u32[]{:S(2)}, u32[]{:S(2)}) collective-permute-start(f32[2,1536]{1,0:T(2,128)S(1)} %get-tuple-element.34), channel_id=1, source_target_pairs={{0,8},{4,12},{8,0},{12,4},{1,9},{5,13},{9,1},{13,5},{2,10},{6,14},... | collective-permute-start | bytes 36872 | tf_op jit(solution)/shard_map/ppermute | solution.py:464
  10.5 0.1 collective-permute-start.2
  10.6 0.0 copy-done.7
  10.6 2.7 %attention.1 = (bf16[48,512]{1,0:T(8,128)(2,1)S(1)}, bf16[54,2,256,128]{3,2,1,0:T(8,128)(2,1)S(1)}) custom-call(s32[2]{0:T(128)S(1)} %pad_add_fusion.meta, s32[192]{0:T(256)S(1)} %copy-done.7, f32[384,128]{1,0:T(8,128)S(1)} %get-tuple-element.28.query, f32[48,128]{1,0:T(8,128)S(1)} %get-tuple-element.29.newkey, ...), custom_call_target="tpu_custom_call", output_to_operand_aliasing={{1}: (5, {})} | custom-call | flops 25165824 | bytes 6291456 | tf_op jit(solution)/shard_map/attention/pallas_call | solution.py:539
  13.3 0.0 collective-permute-done.1.rest_0_
  13.3 0.3 collective-permute-done.2.rest_1_
  13.6 0.0 collective-permute-done.box.rest_4_
  13.7 0.0 copy-done.1
  13.7 0.0 copy-done.3
  13.7 0.0 copy-start.2
  13.7 0.0 copy-start.4
  13.7 0.0 copy-start.5
  13.7 0.0 copy-start.8
  13.7 1.4 %out_projection.1 = (f32[48,1024]{1,0:T(8,128)S(1)}, bf16[48,1024]{1,0:T(8,128)(2,1)S(1)}, bf16[48,1024]{1,0:T(8,128)(2,1)S(1)}, bf16[48,1024]{1,0:T(8,128)(2,1)S(1)}) custom-call(s32[2]{0:T(128)S(1)} %pad_add_fusion.meta, s32[12]{0:T(128)S(1)} %get-tuple-element.27.plan, bf16[48,512]{1,0:T(8,128)(2,1)S(1)} %get-tuple-element.32.attended, ...), custom_call_target="tpu_custom_call" | custom-call | flops 201326592 | bytes 4194304 | tf_op jit(solution)/shard_map/out_projection/pallas_call | solution.py:553
  15.1 3.7 %collective-permute-start.3 = (bf16[48,1024]{1,0:T(8,128)(2,1)S(1)}, bf16[48,1024]{1,0:T(8,128)(2,1)S(1)}, u32[]{:S(2)}, u32[]{:S(2)}) collective-permute-start(bf16[48,1024]{1,0:T(8,128)(2,1)S(1)} %get-tuple-element.42), channel_id=1, source_target_pairs={{0,3},{1,2},{2,1},{3,0},{4,7},{5,6},{6,5},{7,4},{8,11},{9,10},{10,... | collective-permute-start | bytes 294920 | tf_op jit(solution)/shard_map/ppermute | solution.py:464
  18.8 0.0 collective-permute-start.4
  18.8 0.8 %collective-permute-start.5 = (bf16[48,1024]{1,0:T(8,128)(2,1)S(1)}, bf16[48,1024]{1,0:T(8,128)(2,1)S(1)}, u32[]{:S(2)}, u32[]{:S(2)}) collective-permute-start(bf16[48,1024]{1,0:T(8,128)(2,1)S(1)} %get-tuple-element.44), channel_id=1, source_target_pairs={{0,1},{1,0},{2,3},{3,2},{4,5},{5,4},{6,7},{7,6},{8,9},{9,8},{10,11... | collective-permute-start | bytes 294920 | tf_op jit(solution)/shard_map/ppermute | solution.py:464
  19.6 1.3 %pack.1 = (bf16[2,2,256,128]{3,2,1,0:T(8,128)(2,1)S(1)}, bf16[2,2,256,128]{3,2,1,0:T(8,128)(2,1)S(1)}) custom-call(s32[12]{0:T(128)S(1)} %get-tuple-element.27.plan, bf16[54,2,256,128]{3,2,1,0:T(8,128)(2,1)S(1)} %get-tuple-element.41.cache._, f32[48,1024]{1,0:T(8,128)S(1)} %get-tuple-element.36._.own._own), custom_call_target="tpu_custom_call" | custom-call | flops 1 | bytes 6291456 | tf_op jit(solution)/shard_map/pack/pallas_call | solution.py:562
  20.8 1.5 %collective-permute-start.9 = (bf16[2,2,256,128]{3,2,1,0:T(8,128)(2,1)S(1)}, bf16[2,2,256,128]{3,2,1,0:T(8,128)(2,1)S(1)}, u32[]{:S(2)}, u32[]{:S(2)}) collective-permute-start(bf16[2,2,256,128]{3,2,1,0:T(8,128)(2,1)S(1)} %get-tuple-element.45), channel_id=1, source_target_pairs={{0,8},{4,12},{8,0},{12,4},{1,9},{5,13},{9,1},{13,5},{2,10},{6,14},... | collective-permute-start | bytes 786440 | tf_op jit(solution)/shard_map/ppermute | solution.py:464
  22.3 0.0 collective-permute-start.10
  22.3 0.4 collective-permute-done.3.rest_0_
  22.7 4.7 %collective-permute-done.4.rest_1_ = bf16[48,1024]{1,0:T(8,128)(2,1)S(1)} collective-permute-done((bf16[48,1024]{1,0:T(8,128)(2,1)S(1)}, bf16[48,1024]{1,0:T(8,128)(2,1)S(1)}, u32[]{:S(2)}, u32[]{:S(2)}) %collective-permute-start.4) | collective-permute-done | bytes 98336 | tf_op jit(solution)/shard_map/ppermute | solution.py:464
  27.4 0.0 collective-permute-done.5.rest_2_
  27.5 0.1 sum_terms.2.rest_0_
  27.5 0.0 copy-start
  27.5 0.0 copy-start.6
  27.5 2.5 %collective-permute-start.8 = (bf16[48,1024]{1,0:T(8,128)(2,1)S(1)}, bf16[48,1024]{1,0:T(8,128)(2,1)S(1)}, u32[]{:S(2)}, u32[]{:S(2)}) collective-permute-start(bf16[48,1024]{1,0:T(8,128)(2,1)S(1)} %sum_terms.2.rest_0_), channel_id=1, source_target_pairs={{0,3},{1,2},{2,1},{3,0},{4,7},{5,6},{6,5},{7,4},{8,11},{9,10},{10,... | collective-permute-start | bytes 294920 | tf_op jit(solution)/shard_map/ppermute | solution.py:464
  30.1 0.0 collective-permute-start.7
  30.1 1.9 %collective-permute-start.6 = (bf16[48,1024]{1,0:T(8,128)(2,1)S(1)}, bf16[48,1024]{1,0:T(8,128)(2,1)S(1)}, u32[]{:S(2)}, u32[]{:S(2)}) collective-permute-start(bf16[48,1024]{1,0:T(8,128)(2,1)S(1)} %sum_terms.2.rest_0_), channel_id=1, source_target_pairs={{0,1},{1,0},{2,3},{3,2},{4,5},{5,4},{6,7},{7,6},{8,9},{9,8},{10,11... | collective-permute-start | bytes 294920 | tf_op jit(solution)/shard_map/ppermute | solution.py:464
  32.0 0.0 copy-done.2
  32.0 0.0 copy-done.4
  32.0 0.0 copy-done.5
  32.0 0.0 copy-done.8
  32.0 2.2 %prepare.1 = (bf16[4096,256]{1,0:T(8,128)(2,1)S(1)}, f32[48,128]{1,0:T(8,128)S(1)}, f32[48,128]{1,0:T(8,128)S(1)}, s32[48]{0:T(128)S(1)}) custom-call(s32[2]{0:T(128)S(1)} %pad_add_fusion.meta, s32[192]{0:T(256)S(1)} %copy-done.8, s32[192]{0:T(256)S(1)} %copy-done.7, s32[12]{0:T(128)S(1)} %get-tuple-element.27.plan, f32[256,128]{1,0:T(8,128)S(1)} %copy-done.5, ...), custom_call_target="tpu_custom_call" | custom-call | flops 30198988800 | bytes 41943040 | tf_op jit(solution)/shard_map/prepare/pallas_call | solution.py:595
  34.2 0.9 %collective-permute-done.8.rest_3_ = bf16[48,1024]{1,0:T(8,128)(2,1)S(1)} collective-permute-done((bf16[48,1024]{1,0:T(8,128)(2,1)S(1)}, bf16[48,1024]{1,0:T(8,128)(2,1)S(1)}, u32[]{:S(2)}, u32[]{:S(2)}) %collective-permute-start.8) | collective-permute-done | bytes 98336 | tf_op jit(solution)/shard_map/ppermute | solution.py:464
  35.1 3.4 %collective-permute-done.7.rest_2_ = bf16[48,1024]{1,0:T(8,128)(2,1)S(1)} collective-permute-done((bf16[48,1024]{1,0:T(8,128)(2,1)S(1)}, bf16[48,1024]{1,0:T(8,128)(2,1)S(1)}, u32[]{:S(2)}, u32[]{:S(2)}) %collective-permute-start.7) | collective-permute-done | bytes 98336 | tf_op jit(solution)/shard_map/ppermute | solution.py:464
  38.5 0.0 collective-permute-done.6.rest_1_
  38.5 0.0 collective-permute-done.9.rest_5_
  38.5 0.0 collective-permute-done.10.rest_6_
  38.5 0.0 copy-done
  38.5 0.0 copy-done.6
  38.5 5.5 %second_step.1 = (f32[48,1024]{1,0:T(8,128)S(1)}, bf16[48,1024]{1,0:T(8,128)(2,1)S(1)}, bf16[48,1024]{1,0:T(8,128)(2,1)S(1)}, bf16[48,1024]{1,0:T(8,128)(2,1)S(1)}, bf16[54,2,256,128]{3,2,1,0:T(8,128)(2,1)S(1)}) custom-call(s32[2]{0:T(128)S(1)} %pad_add_fusion.meta, s32[192]{0:T(256)S(1)} %copy-done.8, ...), custom_call_target="tpu_custom_call", output_to_operand_aliasing={{4}: (10, {})} | custom-call | flops 905969664 | bytes 18874368 | tf_op jit(solution)/shard_map/second_step/pallas_call | solution.py:610
  44.1 1.8 %collective-permute-start.11 = (bf16[48,1024]{1,0:T(8,128)(2,1)S(1)}, bf16[48,1024]{1,0:T(8,128)(2,1)S(1)}, u32[]{:S(2)}, u32[]{:S(2)}) collective-permute-start(bf16[48,1024]{1,0:T(8,128)(2,1)S(1)} %get-tuple-element.48), channel_id=1, source_target_pairs={{0,3},{1,2},{2,1},{3,0},{4,7},{5,6},{6,5},{7,4},{8,11},{9,10},{10,... | collective-permute-start | bytes 294920 | tf_op jit(solution)/shard_map/ppermute | solution.py:464
  45.9 0.0 collective-permute-start.12
  45.9 2.6 %collective-permute-start.13 = (bf16[48,1024]{1,0:T(8,128)(2,1)S(1)}, bf16[48,1024]{1,0:T(8,128)(2,1)S(1)}, u32[]{:S(2)}, u32[]{:S(2)}) collective-permute-start(bf16[48,1024]{1,0:T(8,128)(2,1)S(1)} %get-tuple-element.50), channel_id=1, source_target_pairs={{0,1},{1,0},{2,3},{3,2},{4,5},{5,4},{6,7},{7,6},{8,9},{9,8},{10,11... | collective-permute-start | bytes 294920 | tf_op jit(solution)/shard_map/ppermute | solution.py:464
  48.5 3.2 %collective-permute-done.11.rest_0_ = bf16[48,1024]{1,0:T(8,128)(2,1)S(1)} collective-permute-done((bf16[48,1024]{1,0:T(8,128)(2,1)S(1)}, bf16[48,1024]{1,0:T(8,128)(2,1)S(1)}, u32[]{:S(2)}, u32[]{:S(2)}) %collective-permute-start.11) | collective-permute-done | bytes 98336 | tf_op jit(solution)/shard_map/ppermute | solution.py:464
  51.7 2.7 %collective-permute-done.12.rest_1_ = bf16[48,1024]{1,0:T(8,128)(2,1)S(1)} collective-permute-done((bf16[48,1024]{1,0:T(8,128)(2,1)S(1)}, bf16[48,1024]{1,0:T(8,128)(2,1)S(1)}, u32[]{:S(2)}, u32[]{:S(2)}) %collective-permute-start.12) | collective-permute-done | bytes 98336 | tf_op jit(solution)/shard_map/ppermute | solution.py:464
  54.5 0.0 collective-permute-done.13.rest_2_
  54.5 2.2 %collective-permute-start.16 = (bf16[48,1024]{1,0:T(8,128)(2,1)S(1)}, bf16[48,1024]{1,0:T(8,128)(2,1)S(1)}, u32[]{:S(2)}, u32[]{:S(2)}) collective-permute-start(bf16[48,1024]{1,0:T(8,128)(2,1)S(1)} %sum_terms.3.rest_0_), channel_id=1, source_target_pairs={{0,3},{1,2},{2,1},{3,0},{4,7},{5,6},{6,5},{7,4},{8,11},{9,10},{10,... | collective-permute-start | bytes 294920 | tf_op jit(solution)/shard_map/ppermute | solution.py:464
  56.7 0.0 collective-permute-start.15
  56.7 2.2 %collective-permute-start.14 = (bf16[48,1024]{1,0:T(8,128)(2,1)S(1)}, bf16[48,1024]{1,0:T(8,128)(2,1)S(1)}, u32[]{:S(2)}, u32[]{:S(2)}) collective-permute-start(bf16[48,1024]{1,0:T(8,128)(2,1)S(1)} %sum_terms.3.rest_0_), channel_id=1, source_target_pairs={{0,1},{1,0},{2,3},{3,2},{4,5},{5,4},{6,7},{7,6},{8,9},{9,8},{10,11... | collective-permute-start | bytes 294920 | tf_op jit(solution)/shard_map/ppermute | solution.py:464
  59.0 3.6 %write_cache.1 = bf16[48,2,256,128]{3,2,1,0:T(8,128)(2,1)} custom-call(s32[48]{0:T(128)S(1)} %get-tuple-element.37.place, bf16[54,2,256,128]{3,2,1,0:T(8,128)(2,1)S(1)} %get-tuple-element.51.cache), custom_call_target="tpu_custom_call" | custom-call | bytes 12582912 | tf_op jit(solution)/shard_map/write_cache/pallas_call | solution.py:629
  62.5 0.0 collective-permute-done.16.rest_3_
  62.6 2.8 %collective-permute-done.15.rest_2_ = bf16[48,1024]{1,0:T(8,128)(2,1)S(1)} collective-permute-done((bf16[48,1024]{1,0:T(8,128)(2,1)S(1)}, bf16[48,1024]{1,0:T(8,128)(2,1)S(1)}, u32[]{:S(2)}, u32[]{:S(2)}) %collective-permute-start.15) | collective-permute-done | bytes 98336 | tf_op jit(solution)/shard_map/ppermute | solution.py:464
  65.4 0.0 collective-permute-done.14.rest_1_
  65.4 1.3 %join.1 = bf16[48,4096]{1,0:T(8,128)(2,1)} custom-call(s32[2]{0:T(128)S(1)} %pad_add_fusion.meta, bf16[48,1024]{1,0:T(8,128)(2,1)S(1)} %sum_terms.3.rest_0_, bf16[48,1024]{1,0:T(8,128)(2,1)S(1)} %collective-permute-done.14.rest_1_, bf16[48,1024]{1,0:T(8,128)(2,1)S(1)} %collective-permute-done.15.rest_2_, bf16[48,1024]{1,0:T(8,128)(2,1)S(1)} %collective-permute-done.16.rest_3_), custom_call_target="tpu_custom_call" | custom-call | tf_op jit(solution)/shard_map/join/pallas_call | solution.py:639
  (1 shorter events, 0.0 us)
Async XLA Ops:
  0.7 9.9 %copy-start.7 = (s32[192]{0:T(256)S(1)}, s32[192]{0:T(256)}, u32[]{:S(2)}) copy-start(s32[192]{0:T(256)} %lengths_s.5) | copy-start | bytes 2308
  7.4 6.3 %copy-start.1 = (bf16[512,4096]{1,0:T(8,128)(2,1)S(1)}, bf16[512,4096]{1,0:T(8,128)(2,1)}, u32[]{:S(2)}) copy-start(bf16[512,4096]{1,0:T(8,128)(2,1)} %wo.3) | copy-start | bytes 12582916
  7.4 6.3 %copy-start.3 = (bf16[48,4096]{1,0:T(8,128)(2,1)S(1)}, bf16[48,4096]{1,0:T(8,128)(2,1)}, u32[]{:S(2)}) copy-start(bf16[48,4096]{1,0:T(8,128)(2,1)} %hidden.1) | copy-start | bytes 1179652
  7.4 6.2 %collective-permute-start = (bf16[2,2,272,128]{3,2,1,0:T(8,128)(2,1)S(1)}, bf16[2,2,272,128]{3,2,1,0:T(8,128)(2,1)S(1)}, u32[]{:S(2)}, u32[]{:S(2)}) collective-permute-start(bf16[2,2,272,128]{3,2,1,0:T(8,128)(2,1)S(1)} %get-tuple-element.33), channel_id=1, source_target_pairs={{0,4},{4,0},{8,12},{12,8},{1,5},{5,1},{9,13},{13,9},{2,6},{6,2},{1... | collective-permute-start | bytes 835592 | tf_op jit(solution)/shard_map/ppermute | solution.py:464
  7.9 5.4 %collective-permute-start.1 = (f32[2,1536]{1,0:T(2,128)S(1)}, f32[2,1536]{1,0:T(2,128)S(1)}, u32[]{:S(2)}, u32[]{:S(2)}) collective-permute-start(f32[2,1536]{1,0:T(2,128)S(1)} %get-tuple-element.34), channel_id=1, source_target_pairs={{0,8},{4,12},{8,0},{12,4},{1,9},{5,13},{9,1},{13,5},{2,10},{6,14},... | collective-permute-start | bytes 36872 | tf_op jit(solution)/shard_map/ppermute | solution.py:464
  10.5 3.1 %collective-permute-start.2 = (f32[2,1536]{1,0:T(2,128)S(1)}, f32[2,1536]{1,0:T(2,128)S(1)}, u32[]{:S(2)}, u32[]{:S(2)}) collective-permute-start(f32[2,1536]{1,0:T(2,128)S(1)} %get-tuple-element.35), channel_id=1, source_target_pairs={{0,12},{4,8},{8,4},{12,0},{1,13},{5,9},{9,5},{13,1},{2,14},{6,10},... | collective-permute-start | bytes 36872 | tf_op jit(solution)/shard_map/ppermute | solution.py:464
  13.7 18.3 %copy-start.2 = (bf16[4096,2,128]{2,1,0:T(2,128)(2,1)S(1)}, bf16[4096,2,128]{2,1,0:T(2,128)(2,1)}, u32[]{:S(2)}) copy-start(bf16[4096,2,128]{2,1,0:T(2,128)(2,1)} %param.16) | copy-start | bytes 6291460
  13.7 18.3 %copy-start.4 = (f32[256,128]{1,0:T(8,128)S(1)}, f32[256,128]{1,0:T(8,128)}, u32[]{:S(2)}) copy-start(f32[256,128]{1,0:T(8,128)} %constant.12.clone.sin_hbm.sin_ref) | copy-start | bytes 393220
  13.7 18.3 %copy-start.5 = (f32[256,128]{1,0:T(8,128)S(1)}, f32[256,128]{1,0:T(8,128)}, u32[]{:S(2)}) copy-start(f32[256,128]{1,0:T(8,128)} %constant.11.clone.cos_hbm.cos_ref) | copy-start | bytes 393220
  13.7 18.3 %copy-start.8 = (s32[192]{0:T(256)S(1)}, s32[192]{0:T(256)}, u32[]{:S(2)}) copy-start(s32[192]{0:T(256)} %source_s.3) | copy-start | bytes 2308
  15.1 7.6 %collective-permute-start.3 = (bf16[48,1024]{1,0:T(8,128)(2,1)S(1)}, bf16[48,1024]{1,0:T(8,128)(2,1)S(1)}, u32[]{:S(2)}, u32[]{:S(2)}) collective-permute-start(bf16[48,1024]{1,0:T(8,128)(2,1)S(1)} %get-tuple-element.42), channel_id=1, source_target_pairs={{0,3},{1,2},{2,1},{3,0},{4,7},{5,6},{6,5},{7,4},{8,11},{9,10},{10,... | collective-permute-start | bytes 294920 | tf_op jit(solution)/shard_map/ppermute | solution.py:464
  18.8 8.7 %collective-permute-start.4 = (bf16[48,1024]{1,0:T(8,128)(2,1)S(1)}, bf16[48,1024]{1,0:T(8,128)(2,1)S(1)}, u32[]{:S(2)}, u32[]{:S(2)}) collective-permute-start(bf16[48,1024]{1,0:T(8,128)(2,1)S(1)} %get-tuple-element.43), channel_id=1, source_target_pairs={{0,2},{1,3},{2,0},{3,1},{4,6},{5,7},{6,4},{7,5},{8,10},{9,11},{10,... | collective-permute-start | bytes 294920 | tf_op jit(solution)/shard_map/ppermute | solution.py:464
  18.8 8.7 %collective-permute-start.5 = (bf16[48,1024]{1,0:T(8,128)(2,1)S(1)}, bf16[48,1024]{1,0:T(8,128)(2,1)S(1)}, u32[]{:S(2)}, u32[]{:S(2)}) collective-permute-start(bf16[48,1024]{1,0:T(8,128)(2,1)S(1)} %get-tuple-element.44), channel_id=1, source_target_pairs={{0,1},{1,0},{2,3},{3,2},{4,5},{5,4},{6,7},{7,6},{8,9},{9,8},{10,11... | collective-permute-start | bytes 294920 | tf_op jit(solution)/shard_map/ppermute | solution.py:464
  20.8 17.7 %collective-permute-start.9 = (bf16[2,2,256,128]{3,2,1,0:T(8,128)(2,1)S(1)}, bf16[2,2,256,128]{3,2,1,0:T(8,128)(2,1)S(1)}, u32[]{:S(2)}, u32[]{:S(2)}) collective-permute-start(bf16[2,2,256,128]{3,2,1,0:T(8,128)(2,1)S(1)} %get-tuple-element.45), channel_id=1, source_target_pairs={{0,8},{4,12},{8,0},{12,4},{1,9},{5,13},{9,1},{13,5},{2,10},{6,14},... | collective-permute-start | bytes 786440 | tf_op jit(solution)/shard_map/ppermute | solution.py:464
  22.3 16.2 %collective-permute-start.10 = (bf16[2,2,256,128]{3,2,1,0:T(8,128)(2,1)S(1)}, bf16[2,2,256,128]{3,2,1,0:T(8,128)(2,1)S(1)}, u32[]{:S(2)}, u32[]{:S(2)}) collective-permute-start(bf16[2,2,256,128]{3,2,1,0:T(8,128)(2,1)S(1)} %get-tuple-element.46), channel_id=1, source_target_pairs={{0,12},{4,8},{8,4},{12,0},{1,13},{5,9},{9,5},{13,1},{2,14},{6,10},... | collective-permute-start | bytes 786440 | tf_op jit(solution)/shard_map/ppermute | solution.py:464
  27.5 11.0 %copy-start = (bf16[4096,512]{1,0:T(8,128)(2,1)S(1)}, bf16[4096,512]{1,0:T(8,128)(2,1)}, u32[]{:S(2)}) copy-start(bf16[4096,512]{1,0:T(8,128)(2,1)} %wq.1) | copy-start | bytes 12582916
  27.5 11.0 %copy-start.6 = (f32[4096]{0:T(1024)S(1)}, f32[4096]{0:T(1024)}, u32[]{:S(2)}) copy-start(f32[4096]{0:T(1024)} %param.14) | copy-start | bytes 49156
  27.5 7.6 %collective-permute-start.8 = (bf16[48,1024]{1,0:T(8,128)(2,1)S(1)}, bf16[48,1024]{1,0:T(8,128)(2,1)S(1)}, u32[]{:S(2)}, u32[]{:S(2)}) collective-permute-start(bf16[48,1024]{1,0:T(8,128)(2,1)S(1)} %sum_terms.2.rest_0_), channel_id=1, source_target_pairs={{0,3},{1,2},{2,1},{3,0},{4,7},{5,6},{6,5},{7,4},{8,11},{9,10},{10,... | collective-permute-start | bytes 294920 | tf_op jit(solution)/shard_map/ppermute | solution.py:464
  30.1 8.4 %collective-permute-start.7 = (bf16[48,1024]{1,0:T(8,128)(2,1)S(1)}, bf16[48,1024]{1,0:T(8,128)(2,1)S(1)}, u32[]{:S(2)}, u32[]{:S(2)}) collective-permute-start(bf16[48,1024]{1,0:T(8,128)(2,1)S(1)} %sum_terms.2.rest_0_), channel_id=1, source_target_pairs={{0,2},{1,3},{2,0},{3,1},{4,6},{5,7},{6,4},{7,5},{8,10},{9,11},{10,... | collective-permute-start | bytes 294920 | tf_op jit(solution)/shard_map/ppermute | solution.py:464
  30.1 8.4 %collective-permute-start.6 = (bf16[48,1024]{1,0:T(8,128)(2,1)S(1)}, bf16[48,1024]{1,0:T(8,128)(2,1)S(1)}, u32[]{:S(2)}, u32[]{:S(2)}) collective-permute-start(bf16[48,1024]{1,0:T(8,128)(2,1)S(1)} %sum_terms.2.rest_0_), channel_id=1, source_target_pairs={{0,1},{1,0},{2,3},{3,2},{4,5},{5,4},{6,7},{7,6},{8,9},{9,8},{10,11... | collective-permute-start | bytes 294920 | tf_op jit(solution)/shard_map/ppermute | solution.py:464
  44.1 7.7 %collective-permute-start.11 = (bf16[48,1024]{1,0:T(8,128)(2,1)S(1)}, bf16[48,1024]{1,0:T(8,128)(2,1)S(1)}, u32[]{:S(2)}, u32[]{:S(2)}) collective-permute-start(bf16[48,1024]{1,0:T(8,128)(2,1)S(1)} %get-tuple-element.48), channel_id=1, source_target_pairs={{0,3},{1,2},{2,1},{3,0},{4,7},{5,6},{6,5},{7,4},{8,11},{9,10},{10,... | collective-permute-start | bytes 294920 | tf_op jit(solution)/shard_map/ppermute | solution.py:464
  45.9 8.6 %collective-permute-start.12 = (bf16[48,1024]{1,0:T(8,128)(2,1)S(1)}, bf16[48,1024]{1,0:T(8,128)(2,1)S(1)}, u32[]{:S(2)}, u32[]{:S(2)}) collective-permute-start(bf16[48,1024]{1,0:T(8,128)(2,1)S(1)} %get-tuple-element.49), channel_id=1, source_target_pairs={{0,2},{1,3},{2,0},{3,1},{4,6},{5,7},{6,4},{7,5},{8,10},{9,11},{10,... | collective-permute-start | bytes 294920 | tf_op jit(solution)/shard_map/ppermute | solution.py:464
  45.9 8.6 %collective-permute-start.13 = (bf16[48,1024]{1,0:T(8,128)(2,1)S(1)}, bf16[48,1024]{1,0:T(8,128)(2,1)S(1)}, u32[]{:S(2)}, u32[]{:S(2)}) collective-permute-start(bf16[48,1024]{1,0:T(8,128)(2,1)S(1)} %get-tuple-element.50), channel_id=1, source_target_pairs={{0,1},{1,0},{2,3},{3,2},{4,5},{5,4},{6,7},{7,6},{8,9},{9,8},{10,11... | collective-permute-start | bytes 294920 | tf_op jit(solution)/shard_map/ppermute | solution.py:464
  54.5 8.0 %collective-permute-start.16 = (bf16[48,1024]{1,0:T(8,128)(2,1)S(1)}, bf16[48,1024]{1,0:T(8,128)(2,1)S(1)}, u32[]{:S(2)}, u32[]{:S(2)}) collective-permute-start(bf16[48,1024]{1,0:T(8,128)(2,1)S(1)} %sum_terms.3.rest_0_), channel_id=1, source_target_pairs={{0,3},{1,2},{2,1},{3,0},{4,7},{5,6},{6,5},{7,4},{8,11},{9,10},{10,... | collective-permute-start | bytes 294920 | tf_op jit(solution)/shard_map/ppermute | solution.py:464
  56.7 8.7 %collective-permute-start.15 = (bf16[48,1024]{1,0:T(8,128)(2,1)S(1)}, bf16[48,1024]{1,0:T(8,128)(2,1)S(1)}, u32[]{:S(2)}, u32[]{:S(2)}) collective-permute-start(bf16[48,1024]{1,0:T(8,128)(2,1)S(1)} %sum_terms.3.rest_0_), channel_id=1, source_target_pairs={{0,2},{1,3},{2,0},{3,1},{4,6},{5,7},{6,4},{7,5},{8,10},{9,11},{10,... | collective-permute-start | bytes 294920 | tf_op jit(solution)/shard_map/ppermute | solution.py:464
  56.7 8.7 %collective-permute-start.14 = (bf16[48,1024]{1,0:T(8,128)(2,1)S(1)}, bf16[48,1024]{1,0:T(8,128)(2,1)S(1)}, u32[]{:S(2)}, u32[]{:S(2)}) collective-permute-start(bf16[48,1024]{1,0:T(8,128)(2,1)S(1)} %sum_terms.3.rest_0_), channel_id=1, source_target_pairs={{0,1},{1,0},{2,3},{3,2},{4,5},{5,4},{6,7},{7,6},{8,9},{9,8},{10,11... | collective-permute-start | bytes 294920 | tf_op jit(solution)/shard_map/ppermute | solution.py:464

commit v18 on v17

--- a/solution.py
+++ b/solution.py
@@ -105,8 +105,9 @@
     base = pl.multiple_of((jnp.maximum(p, 0) // PIECE) * PIECE, PIECE)
     hit = lax.broadcasted_iota(I32, (PIECE, HD), 0) + base == p
     for which, new in ((0, key_row), (1, value_row)):
-        old = cache[place, which, pl.ds(base, PIECE), :].astype(F32)
-        cache[place, which, pl.ds(base, PIECE), :] = jnp.where(hit, new, old).astype(BF16)
+        old = cache[place, which, pl.ds(base, PIECE), :]
+        new = jnp.broadcast_to(new, old.shape).astype(BF16)
+        cache[place, which, pl.ds(base, PIECE), :] = jnp.where(hit, new, old)
 
 
 def attend(cache, places, positions, query_rows):
@@ -221,21 +222,20 @@
         copy.wait()
     gather_angles(lambda s: lengths_s[0, low + s], slots, cos_ref, sin_ref, cos_rows, sin_rows)
     key, value = project_spread(spread, wkv)
-    query = project_from(normed3, wq)
     cosine, sine = cos_rows[...], sin_rows[...]
-    query_out[...] = jnp.zeros(query_out.shape, F32)
-    for g in range(heads):
-        turned = turn(query[:, g * HD : (g + 1) * HD], cosine, sine)
-        query_out[pl.ds(g, slots, stride=GROUP), :] = turned.astype(BF16).astype(F32)
     newkey_out[...] = turn(key, cosine, sine).astype(BF16).astype(F32)
     newvalue_out[...] = value.astype(BF16).astype(F32)
-
     positions = [lengths_s[0, low + slot] for slot in send_slots]
     for at, slot in enumerate(send_slots):
         put_row(
             leaving, at, positions[at],
             newkey_out[pl.ds(slot, 1), :], newvalue_out[pl.ds(slot, 1), :],
         )
+    query = project_from(normed3, wq)
+    query_out[...] = jnp.zeros(query_out.shape, F32)
+    for g in range(heads):
+        turned = turn(query[:, g * HD : (g + 1) * HD], cosine, sine)
+        query_out[pl.ds(g, slots, stride=GROUP), :] = turned.astype(BF16).astype(F32)
     cap = leaving.shape[2]
     copies = [
         pltpu.make_async_copy(
@@ -417,20 +417,18 @@
     positions = [lengths_s[source_s[low + s]] + 1 for s in range(slots)]
     for copy in loads:
         copy.wait()
+    pair = project_from(normed3, wkv)
+    cosine, sine = cos_rows[...], sin_rows[...]
+    newkey = turn(pair[:, :HD], cosine, sine).astype(BF16).astype(F32)
+    newvalue = pair[:, HD:].astype(BF16).astype(F32)
+    places = [place[s] for s in range(slots)]
+    for s, (at, p) in enumerate(zip(places, positions)):
+        put_row(cache, at, p, newkey[s : s + 1, :], newvalue[s : s + 1, :])
     query = project_from(normed3, wq)
-    pair = project_from(normed3, wkv)
-    key, value = pair[:, :HD], pair[:, HD:]
-    cosine, sine = cos_rows[...], sin_rows[...]
     query_rows[...] = jnp.zeros(query_rows.shape, F32)
     for g in range(heads):
         turned = turn(query[:, g * HD : (g + 1) * HD], cosine, sine)
         query_rows[pl.ds(g, slots, stride=GROUP), :] = turned.astype(BF16).astype(F32)
-    newkey = turn(key, cosine, sine).astype(BF16).astype(F32)
-    newvalue = value.astype(BF16).astype(F32)
-
-    places = [place[s] for s in range(slots)]
-    for s, (at, p) in enumerate(zip(places, positions)):
-        put_row(cache, at, p, newkey[s : s + 1, :], newvalue[s : s + 1, :])
     attended = attend_slots(cache, places, positions, query_rows, attended_rows, heads)
     project_out(
         attended.astype(BF16), wo, blocks[0][...].astype(F32), own, sends, me_tp, peers_tp

time: 66.9 us -> 66.4 us (level)
  no operation moved by 1% of the time
where the time goes in v18:
time: 66.4 us; the launch traced here: 66.3 us
  Pallas kernels  24.4 us (37%)
  starting transfers between devices  22.4 us (34%)
  waiting for transfers between devices  18.6 us (28%)
  between operations  0.81 us (1%)
    ppermute x17, starting transfers between devices, swapped(): return lax.ppermute(x, axis, [(i, i ^ k) for i in range(size)])  22.4 us
    ppermute x17, waiting for transfers between devices, swapped(): return lax.ppermute(x, axis, [(i, i ^ k) for i in range(size)])  18.6 us
    pallas_call x1, Pallas kernels, local(): pl.pallas_call(functools.partial(first_kernel, peers, slots, heads, shard...  6.67 us
    pallas_call x1, Pallas kernels, local(): pl.pallas_call(functools.partial(second_kernel, peers, peers_tp, slots, h...  5.2 us
    pallas_call x1, Pallas kernels, local(): pl.pallas_call(functools.partial(cache_kernel, slots), out_shape=jax.Shap...  3.58 us
    pallas_call x1, Pallas kernels, local(): pl.pallas_call(functools.partial(attend_kernel, slots, heads), out_shape=...  2.65 us
    pallas_call x1, Pallas kernels, local(): pl.pallas_call(functools.partial(prepare_kernel, peers, slots), out_shape...  2.19 us
    pallas_call x1, Pallas kernels, local(): pl.pallas_call(functools.partial(out_kernel, peers, peers_tp), out_shape=...  1.4 us
  transfers between devices with their start and end apart: 17, of which 8 were waited for; matrix products, arithmetic and copies ran while one was open for 0% of the time, Pallas kernels for 15%

profile of v18, /device:TPU:0, one launch (start us, length us, event | category | flops | bytes accessed | tf_op | source)
XLA Modules:
  0.0 66.3 jit_solution(1725907247654215113)
XLA Ops:
  0.6 0.1 pad_add_fusion.meta
  0.7 0.0 copy-start.7
  0.7 6.7 %first_step.1 = (f32[384,128]{1,0:T(8,128)S(1)}, f32[48,128]{1,0:T(8,128)S(1)}, f32[48,128]{1,0:T(8,128)S(1)}, s32[12]{0:T(128)S(1)}, bf16[54,2,256,128]{3,2,1,0...) custom-call(s32[2]{0:T(128)S(1)} %pad_add_fusion.meta, ...), custom_call_target="tpu_custom_call" | custom-call | flops 301989888 | bytes 6291456 | tf_op jit(solution)/shard_map/first_step/pallas_call | solution.py:496
  7.4 0.0 copy-start.1
  7.4 0.0 copy-start.3
  7.4 0.5 collective-permute-start
  7.9 2.6 %collective-permute-start.1 = (f32[2,1536]{1,0:T(2,128)S(1)}, f32[2,1536]{1,0:T(2,128)S(1)}, u32[]{:S(2)}, u32[]{:S(2)}) collective-permute-start(f32[2,1536]{1,0:T(2,128)S(1)} %get-tuple-element.34), channel_id=1, source_target_pairs={{0,8},{4,12},{8,0},{12,4},{1,9},{5,13},{9,1},{13,5},{2,10},{6,14},... | collective-permute-start | bytes 36872 | tf_op jit(solution)/shard_map/ppermute | solution.py:462
  10.5 0.1 collective-permute-start.2
  10.6 0.0 copy-done.7
  10.6 2.6 %attention.1 = (bf16[48,512]{1,0:T(8,128)(2,1)S(1)}, bf16[54,2,256,128]{3,2,1,0:T(8,128)(2,1)S(1)}) custom-call(s32[2]{0:T(128)S(1)} %pad_add_fusion.meta, s32[192]{0:T(256)S(1)} %copy-done.7, f32[384,128]{1,0:T(8,128)S(1)} %get-tuple-element.28.query, f32[48,128]{1,0:T(8,128)S(1)} %get-tuple-element.29.newkey, ...), custom_call_target="tpu_custom_call", output_to_operand_aliasing={{1}: (5, {})} | custom-call | flops 25165824 | bytes 6291456 | tf_op jit(solution)/shard_map/attention/pallas_call | solution.py:537
  13.2 0.0 collective-permute-done.1.rest_0_
  13.3 0.4 collective-permute-done.2.rest_1_
  13.6 0.0 collective-permute-done.box.rest_4_
  13.6 0.0 copy-done.1
  13.6 0.0 copy-done.3
  13.7 0.0 copy-start.2
  13.7 0.0 copy-start.4
  13.7 0.0 copy-start.5
  13.7 0.0 copy-start.8
  13.7 1.4 %out_projection.1 = (f32[48,1024]{1,0:T(8,128)S(1)}, bf16[48,1024]{1,0:T(8,128)(2,1)S(1)}, bf16[48,1024]{1,0:T(8,128)(2,1)S(1)}, bf16[48,1024]{1,0:T(8,128)(2,1)S(1)}) custom-call(s32[2]{0:T(128)S(1)} %pad_add_fusion.meta, s32[12]{0:T(128)S(1)} %get-tuple-element.27.plan, bf16[48,512]{1,0:T(8,128)(2,1)S(1)} %get-tuple-element.32.attended, ...), custom_call_target="tpu_custom_call" | custom-call | flops 201326592 | bytes 4194304 | tf_op jit(solution)/shard_map/out_projection/pallas_call | solution.py:551
  15.1 3.7 %collective-permute-start.3 = (bf16[48,1024]{1,0:T(8,128)(2,1)S(1)}, bf16[48,1024]{1,0:T(8,128)(2,1)S(1)}, u32[]{:S(2)}, u32[]{:S(2)}) collective-permute-start(bf16[48,1024]{1,0:T(8,128)(2,1)S(1)} %get-tuple-element.42), channel_id=1, source_target_pairs={{0,3},{1,2},{2,1},{3,0},{4,7},{5,6},{6,5},{7,4},{8,11},{9,10},{10,... | collective-permute-start | bytes 294920 | tf_op jit(solution)/shard_map/ppermute | solution.py:462
  18.8 0.0 collective-permute-start.4
  18.8 0.8 %collective-permute-start.5 = (bf16[48,1024]{1,0:T(8,128)(2,1)S(1)}, bf16[48,1024]{1,0:T(8,128)(2,1)S(1)}, u32[]{:S(2)}, u32[]{:S(2)}) collective-permute-start(bf16[48,1024]{1,0:T(8,128)(2,1)S(1)} %get-tuple-element.44), channel_id=1, source_target_pairs={{0,1},{1,0},{2,3},{3,2},{4,5},{5,4},{6,7},{7,6},{8,9},{9,8},{10,11... | collective-permute-start | bytes 294920 | tf_op jit(solution)/shard_map/ppermute | solution.py:462
  19.6 1.3 %pack.1 = (bf16[2,2,256,128]{3,2,1,0:T(8,128)(2,1)S(1)}, bf16[2,2,256,128]{3,2,1,0:T(8,128)(2,1)S(1)}) custom-call(s32[12]{0:T(128)S(1)} %get-tuple-element.27.plan, bf16[54,2,256,128]{3,2,1,0:T(8,128)(2,1)S(1)} %get-tuple-element.41.cache._, f32[48,1024]{1,0:T(8,128)S(1)} %get-tuple-element.36._.own._own), custom_call_target="tpu_custom_call" | custom-call | flops 1 | bytes 6291456 | tf_op jit(solution)/shard_map/pack/pallas_call | solution.py:560
  20.8 1.4 %collective-permute-start.9 = (bf16[2,2,256,128]{3,2,1,0:T(8,128)(2,1)S(1)}, bf16[2,2,256,128]{3,2,1,0:T(8,128)(2,1)S(1)}, u32[]{:S(2)}, u32[]{:S(2)}) collective-permute-start(bf16[2,2,256,128]{3,2,1,0:T(8,128)(2,1)S(1)} %get-tuple-element.45), channel_id=1, source_target_pairs={{0,8},{4,12},{8,0},{12,4},{1,9},{5,13},{9,1},{13,5},{2,10},{6,14},... | collective-permute-start | bytes 786440 | tf_op jit(solution)/shard_map/ppermute | solution.py:462
  22.3 0.0 collective-permute-start.10
  22.3 0.4 collective-permute-done.3.rest_0_
  22.7 4.7 %collective-permute-done.4.rest_1_ = bf16[48,1024]{1,0:T(8,128)(2,1)S(1)} collective-permute-done((bf16[48,1024]{1,0:T(8,128)(2,1)S(1)}, bf16[48,1024]{1,0:T(8,128)(2,1)S(1)}, u32[]{:S(2)}, u32[]{:S(2)}) %collective-permute-start.4) | collective-permute-done | bytes 98336 | tf_op jit(solution)/shard_map/ppermute | solution.py:462
  27.4 0.0 collective-permute-done.5.rest_2_
  27.4 0.1 sum_terms.2.rest_0_
  27.5 0.0 copy-start
  27.5 0.0 copy-start.6
  27.5 2.5 %collective-permute-start.8 = (bf16[48,1024]{1,0:T(8,128)(2,1)S(1)}, bf16[48,1024]{1,0:T(8,128)(2,1)S(1)}, u32[]{:S(2)}, u32[]{:S(2)}) collective-permute-start(bf16[48,1024]{1,0:T(8,128)(2,1)S(1)} %sum_terms.2.rest_0_), channel_id=1, source_target_pairs={{0,3},{1,2},{2,1},{3,0},{4,7},{5,6},{6,5},{7,4},{8,11},{9,10},{10,... | collective-permute-start | bytes 294920 | tf_op jit(solution)/shard_map/ppermute | solution.py:462
  30.0 0.0 collective-permute-start.7
  30.0 1.9 %collective-permute-start.6 = (bf16[48,1024]{1,0:T(8,128)(2,1)S(1)}, bf16[48,1024]{1,0:T(8,128)(2,1)S(1)}, u32[]{:S(2)}, u32[]{:S(2)}) collective-permute-start(bf16[48,1024]{1,0:T(8,128)(2,1)S(1)} %sum_terms.2.rest_0_), channel_id=1, source_target_pairs={{0,1},{1,0},{2,3},{3,2},{4,5},{5,4},{6,7},{7,6},{8,9},{9,8},{10,11... | collective-permute-start | bytes 294920 | tf_op jit(solution)/shard_map/ppermute | solution.py:462
  32.0 0.0 copy-done.2
  32.0 0.0 copy-done.4
  32.0 0.0 copy-done.5
  32.0 0.0 copy-done.8
  32.0 2.2 %prepare.1 = (bf16[4096,256]{1,0:T(8,128)(2,1)S(1)}, f32[48,128]{1,0:T(8,128)S(1)}, f32[48,128]{1,0:T(8,128)S(1)}, s32[48]{0:T(128)S(1)}) custom-call(s32[2]{0:T(128)S(1)} %pad_add_fusion.meta, s32[192]{0:T(256)S(1)} %copy-done.8, s32[192]{0:T(256)S(1)} %copy-done.7, s32[12]{0:T(128)S(1)} %get-tuple-element.27.plan, f32[256,128]{1,0:T(8,128)S(1)} %copy-done.5, ...), custom_call_target="tpu_custom_call" | custom-call | flops 30198988800 | bytes 41943040 | tf_op jit(solution)/shard_map/prepare/pallas_call | solution.py:593
  34.2 0.9 %collective-permute-done.8.rest_3_ = bf16[48,1024]{1,0:T(8,128)(2,1)S(1)} collective-permute-done((bf16[48,1024]{1,0:T(8,128)(2,1)S(1)}, bf16[48,1024]{1,0:T(8,128)(2,1)S(1)}, u32[]{:S(2)}, u32[]{:S(2)}) %collective-permute-start.8) | collective-permute-done | bytes 98336 | tf_op jit(solution)/shard_map/ppermute | solution.py:462
  35.1 3.4 %collective-permute-done.7.rest_2_ = bf16[48,1024]{1,0:T(8,128)(2,1)S(1)} collective-permute-done((bf16[48,1024]{1,0:T(8,128)(2,1)S(1)}, bf16[48,1024]{1,0:T(8,128)(2,1)S(1)}, u32[]{:S(2)}, u32[]{:S(2)}) %collective-permute-start.7) | collective-permute-done | bytes 98336 | tf_op jit(solution)/shard_map/ppermute | solution.py:462
  38.5 0.0 collective-permute-done.6.rest_1_
  38.5 0.0 collective-permute-done.9.rest_5_
  38.5 0.0 collective-permute-done.10.rest_6_
  38.5 0.0 copy-done
  38.5 0.0 copy-done.6
  38.5 5.2 %second_step.1 = (f32[48,1024]{1,0:T(8,128)S(1)}, bf16[48,1024]{1,0:T(8,128)(2,1)S(1)}, bf16[48,1024]{1,0:T(8,128)(2,1)S(1)}, bf16[48,1024]{1,0:T(8,128)(2,1)S(1)}, bf16[54,2,256,128]{3,2,1,0:T(8,128)(2,1)S(1)}) custom-call(s32[2]{0:T(128)S(1)} %pad_add_fusion.meta, s32[192]{0:T(256)S(1)} %copy-done.8, ...), custom_call_target="tpu_custom_call", output_to_operand_aliasing={{4}: (10, {})} | custom-call | flops 905969664 | bytes 18874368 | tf_op jit(solution)/shard_map/second_step/pallas_call | solution.py:608
  43.7 1.8 %collective-permute-start.11 = (bf16[48,1024]{1,0:T(8,128)(2,1)S(1)}, bf16[48,1024]{1,0:T(8,128)(2,1)S(1)}, u32[]{:S(2)}, u32[]{:S(2)}) collective-permute-start(bf16[48,1024]{1,0:T(8,128)(2,1)S(1)} %get-tuple-element.48), channel_id=1, source_target_pairs={{0,3},{1,2},{2,1},{3,0},{4,7},{5,6},{6,5},{7,4},{8,11},{9,10},{10,... | collective-permute-start | bytes 294920 | tf_op jit(solution)/shard_map/ppermute | solution.py:462
  45.5 0.0 collective-permute-start.12
  45.5 2.7 %collective-permute-start.13 = (bf16[48,1024]{1,0:T(8,128)(2,1)S(1)}, bf16[48,1024]{1,0:T(8,128)(2,1)S(1)}, u32[]{:S(2)}, u32[]{:S(2)}) collective-permute-start(bf16[48,1024]{1,0:T(8,128)(2,1)S(1)} %get-tuple-element.50), channel_id=1, source_target_pairs={{0,1},{1,0},{2,3},{3,2},{4,5},{5,4},{6,7},{7,6},{8,9},{9,8},{10,11... | collective-permute-start | bytes 294920 | tf_op jit(solution)/shard_map/ppermute | solution.py:462
  48.2 3.2 %collective-permute-done.11.rest_0_ = bf16[48,1024]{1,0:T(8,128)(2,1)S(1)} collective-permute-done((bf16[48,1024]{1,0:T(8,128)(2,1)S(1)}, bf16[48,1024]{1,0:T(8,128)(2,1)S(1)}, u32[]{:S(2)}, u32[]{:S(2)}) %collective-permute-start.11) | collective-permute-done | bytes 98336 | tf_op jit(solution)/shard_map/ppermute | solution.py:462
  51.4 2.7 %collective-permute-done.12.rest_1_ = bf16[48,1024]{1,0:T(8,128)(2,1)S(1)} collective-permute-done((bf16[48,1024]{1,0:T(8,128)(2,1)S(1)}, bf16[48,1024]{1,0:T(8,128)(2,1)S(1)}, u32[]{:S(2)}, u32[]{:S(2)}) %collective-permute-start.12) | collective-permute-done | bytes 98336 | tf_op jit(solution)/shard_map/ppermute | solution.py:462
  54.0 0.0 collective-permute-done.13.rest_2_
  54.1 2.2 %collective-permute-start.16 = (bf16[48,1024]{1,0:T(8,128)(2,1)S(1)}, bf16[48,1024]{1,0:T(8,128)(2,1)S(1)}, u32[]{:S(2)}, u32[]{:S(2)}) collective-permute-start(bf16[48,1024]{1,0:T(8,128)(2,1)S(1)} %sum_terms.3.rest_0_), channel_id=1, source_target_pairs={{0,3},{1,2},{2,1},{3,0},{4,7},{5,6},{6,5},{7,4},{8,11},{9,10},{10,... | collective-permute-start | bytes 294920 | tf_op jit(solution)/shard_map/ppermute | solution.py:462
  56.3 0.0 collective-permute-start.15
  56.3 2.2 %collective-permute-start.14 = (bf16[48,1024]{1,0:T(8,128)(2,1)S(1)}, bf16[48,1024]{1,0:T(8,128)(2,1)S(1)}, u32[]{:S(2)}, u32[]{:S(2)}) collective-permute-start(bf16[48,1024]{1,0:T(8,128)(2,1)S(1)} %sum_terms.3.rest_0_), channel_id=1, source_target_pairs={{0,1},{1,0},{2,3},{3,2},{4,5},{5,4},{6,7},{7,6},{8,9},{9,8},{10,11... | collective-permute-start | bytes 294920 | tf_op jit(solution)/shard_map/ppermute | solution.py:462
  58.6 3.6 %write_cache.1 = bf16[48,2,256,128]{3,2,1,0:T(8,128)(2,1)} custom-call(s32[48]{0:T(128)S(1)} %get-tuple-element.37.place, bf16[54,2,256,128]{3,2,1,0:T(8,128)(2,1)S(1)} %get-tuple-element.51.cache), custom_call_target="tpu_custom_call" | custom-call | bytes 12582912 | tf_op jit(solution)/shard_map/write_cache/pallas_call | solution.py:627
  62.1 0.0 collective-permute-done.16.rest_3_
  62.1 2.8 %collective-permute-done.15.rest_2_ = bf16[48,1024]{1,0:T(8,128)(2,1)S(1)} collective-permute-done((bf16[48,1024]{1,0:T(8,128)(2,1)S(1)}, bf16[48,1024]{1,0:T(8,128)(2,1)S(1)}, u32[]{:S(2)}, u32[]{:S(2)}) %collective-permute-start.15) | collective-permute-done | bytes 98336 | tf_op jit(solution)/shard_map/ppermute | solution.py:462
  65.0 0.0 collective-permute-done.14.rest_1_
  65.0 1.3 %join.1 = bf16[48,4096]{1,0:T(8,128)(2,1)} custom-call(s32[2]{0:T(128)S(1)} %pad_add_fusion.meta, bf16[48,1024]{1,0:T(8,128)(2,1)S(1)} %sum_terms.3.rest_0_, bf16[48,1024]{1,0:T(8,128)(2,1)S(1)} %collective-permute-done.14.rest_1_, bf16[48,1024]{1,0:T(8,128)(2,1)S(1)} %collective-permute-done.15.rest_2_, bf16[48,1024]{1,0:T(8,128)(2,1)S(1)} %collective-permute-done.16.rest_3_), custom_call_target="tpu_custom_call" | custom-call | tf_op jit(solution)/shard_map/join/pallas_call | solution.py:637
  (1 shorter events, 0.0 us)
Async XLA Ops:
  0.7 9.9 %copy-start.7 = (s32[192]{0:T(256)S(1)}, s32[192]{0:T(256)}, u32[]{:S(2)}) copy-start(s32[192]{0:T(256)} %lengths_s.5) | copy-start | bytes 2308
  7.4 6.3 %copy-start.1 = (bf16[512,4096]{1,0:T(8,128)(2,1)S(1)}, bf16[512,4096]{1,0:T(8,128)(2,1)}, u32[]{:S(2)}) copy-start(bf16[512,4096]{1,0:T(8,128)(2,1)} %wo.3) | copy-start | bytes 12582916
  7.4 6.2 %copy-start.3 = (bf16[48,4096]{1,0:T(8,128)(2,1)S(1)}, bf16[48,4096]{1,0:T(8,128)(2,1)}, u32[]{:S(2)}) copy-start(bf16[48,4096]{1,0:T(8,128)(2,1)} %hidden.1) | copy-start | bytes 1179652
  7.4 6.2 %collective-permute-start = (bf16[2,2,272,128]{3,2,1,0:T(8,128)(2,1)S(1)}, bf16[2,2,272,128]{3,2,1,0:T(8,128)(2,1)S(1)}, u32[]{:S(2)}, u32[]{:S(2)}) collective-permute-start(bf16[2,2,272,128]{3,2,1,0:T(8,128)(2,1)S(1)} %get-tuple-element.33), channel_id=1, source_target_pairs={{0,4},{4,0},{8,12},{12,8},{1,5},{5,1},{9,13},{13,9},{2,6},{6,2},{1... | collective-permute-start | bytes 835592 | tf_op jit(solution)/shard_map/ppermute | solution.py:462
  7.9 5.3 %collective-permute-start.1 = (f32[2,1536]{1,0:T(2,128)S(1)}, f32[2,1536]{1,0:T(2,128)S(1)}, u32[]{:S(2)}, u32[]{:S(2)}) collective-permute-start(f32[2,1536]{1,0:T(2,128)S(1)} %get-tuple-element.34), channel_id=1, source_target_pairs={{0,8},{4,12},{8,0},{12,4},{1,9},{5,13},{9,1},{13,5},{2,10},{6,14},... | collective-permute-start | bytes 36872 | tf_op jit(solution)/shard_map/ppermute | solution.py:462
  10.5 3.1 %collective-permute-start.2 = (f32[2,1536]{1,0:T(2,128)S(1)}, f32[2,1536]{1,0:T(2,128)S(1)}, u32[]{:S(2)}, u32[]{:S(2)}) collective-permute-start(f32[2,1536]{1,0:T(2,128)S(1)} %get-tuple-element.35), channel_id=1, source_target_pairs={{0,12},{4,8},{8,4},{12,0},{1,13},{5,9},{9,5},{13,1},{2,14},{6,10},... | collective-permute-start | bytes 36872 | tf_op jit(solution)/shard_map/ppermute | solution.py:462
  13.7 18.3 %copy-start.2 = (bf16[4096,2,128]{2,1,0:T(2,128)(2,1)S(1)}, bf16[4096,2,128]{2,1,0:T(2,128)(2,1)}, u32[]{:S(2)}) copy-start(bf16[4096,2,128]{2,1,0:T(2,128)(2,1)} %param.16) | copy-start | bytes 6291460
  13.7 18.3 %copy-start.4 = (f32[256,128]{1,0:T(8,128)S(1)}, f32[256,128]{1,0:T(8,128)}, u32[]{:S(2)}) copy-start(f32[256,128]{1,0:T(8,128)} %constant.12.clone.sin_hbm.sin_ref) | copy-start | bytes 393220
  13.7 18.3 %copy-start.5 = (f32[256,128]{1,0:T(8,128)S(1)}, f32[256,128]{1,0:T(8,128)}, u32[]{:S(2)}) copy-start(f32[256,128]{1,0:T(8,128)} %constant.11.clone.cos_hbm.cos_ref) | copy-start | bytes 393220
  13.7 18.3 %copy-start.8 = (s32[192]{0:T(256)S(1)}, s32[192]{0:T(256)}, u32[]{:S(2)}) copy-start(s32[192]{0:T(256)} %source_s.3) | copy-start | bytes 2308
  15.1 7.6 %collective-permute-start.3 = (bf16[48,1024]{1,0:T(8,128)(2,1)S(1)}, bf16[48,1024]{1,0:T(8,128)(2,1)S(1)}, u32[]{:S(2)}, u32[]{:S(2)}) collective-permute-start(bf16[48,1024]{1,0:T(8,128)(2,1)S(1)} %get-tuple-element.42), channel_id=1, source_target_pairs={{0,3},{1,2},{2,1},{3,0},{4,7},{5,6},{6,5},{7,4},{8,11},{9,10},{10,... | collective-permute-start | bytes 294920 | tf_op jit(solution)/shard_map/ppermute | solution.py:462
  18.8 8.6 %collective-permute-start.4 = (bf16[48,1024]{1,0:T(8,128)(2,1)S(1)}, bf16[48,1024]{1,0:T(8,128)(2,1)S(1)}, u32[]{:S(2)}, u32[]{:S(2)}) collective-permute-start(bf16[48,1024]{1,0:T(8,128)(2,1)S(1)} %get-tuple-element.43), channel_id=1, source_target_pairs={{0,2},{1,3},{2,0},{3,1},{4,6},{5,7},{6,4},{7,5},{8,10},{9,11},{10,... | collective-permute-start | bytes 294920 | tf_op jit(solution)/shard_map/ppermute | solution.py:462
  18.8 8.6 %collective-permute-start.5 = (bf16[48,1024]{1,0:T(8,128)(2,1)S(1)}, bf16[48,1024]{1,0:T(8,128)(2,1)S(1)}, u32[]{:S(2)}, u32[]{:S(2)}) collective-permute-start(bf16[48,1024]{1,0:T(8,128)(2,1)S(1)} %get-tuple-element.44), channel_id=1, source_target_pairs={{0,1},{1,0},{2,3},{3,2},{4,5},{5,4},{6,7},{7,6},{8,9},{9,8},{10,11... | collective-permute-start | bytes 294920 | tf_op jit(solution)/shard_map/ppermute | solution.py:462
  20.8 17.6 %collective-permute-start.9 = (bf16[2,2,256,128]{3,2,1,0:T(8,128)(2,1)S(1)}, bf16[2,2,256,128]{3,2,1,0:T(8,128)(2,1)S(1)}, u32[]{:S(2)}, u32[]{:S(2)}) collective-permute-start(bf16[2,2,256,128]{3,2,1,0:T(8,128)(2,1)S(1)} %get-tuple-element.45), channel_id=1, source_target_pairs={{0,8},{4,12},{8,0},{12,4},{1,9},{5,13},{9,1},{13,5},{2,10},{6,14},... | collective-permute-start | bytes 786440 | tf_op jit(solution)/shard_map/ppermute | solution.py:462
  22.3 16.2 %collective-permute-start.10 = (bf16[2,2,256,128]{3,2,1,0:T(8,128)(2,1)S(1)}, bf16[2,2,256,128]{3,2,1,0:T(8,128)(2,1)S(1)}, u32[]{:S(2)}, u32[]{:S(2)}) collective-permute-start(bf16[2,2,256,128]{3,2,1,0:T(8,128)(2,1)S(1)} %get-tuple-element.46), channel_id=1, source_target_pairs={{0,12},{4,8},{8,4},{12,0},{1,13},{5,9},{9,5},{13,1},{2,14},{6,10},... | collective-permute-start | bytes 786440 | tf_op jit(solution)/shard_map/ppermute | solution.py:462
  27.5 11.0 %copy-start = (bf16[4096,512]{1,0:T(8,128)(2,1)S(1)}, bf16[4096,512]{1,0:T(8,128)(2,1)}, u32[]{:S(2)}) copy-start(bf16[4096,512]{1,0:T(8,128)(2,1)} %wq.1) | copy-start | bytes 12582916
  27.5 11.0 %copy-start.6 = (f32[4096]{0:T(1024)S(1)}, f32[4096]{0:T(1024)}, u32[]{:S(2)}) copy-start(f32[4096]{0:T(1024)} %param.14) | copy-start | bytes 49156
  27.5 7.6 %collective-permute-start.8 = (bf16[48,1024]{1,0:T(8,128)(2,1)S(1)}, bf16[48,1024]{1,0:T(8,128)(2,1)S(1)}, u32[]{:S(2)}, u32[]{:S(2)}) collective-permute-start(bf16[48,1024]{1,0:T(8,128)(2,1)S(1)} %sum_terms.2.rest_0_), channel_id=1, source_target_pairs={{0,3},{1,2},{2,1},{3,0},{4,7},{5,6},{6,5},{7,4},{8,11},{9,10},{10,... | collective-permute-start | bytes 294920 | tf_op jit(solution)/shard_map/ppermute | solution.py:462
  30.0 8.4 %collective-permute-start.7 = (bf16[48,1024]{1,0:T(8,128)(2,1)S(1)}, bf16[48,1024]{1,0:T(8,128)(2,1)S(1)}, u32[]{:S(2)}, u32[]{:S(2)}) collective-permute-start(bf16[48,1024]{1,0:T(8,128)(2,1)S(1)} %sum_terms.2.rest_0_), channel_id=1, source_target_pairs={{0,2},{1,3},{2,0},{3,1},{4,6},{5,7},{6,4},{7,5},{8,10},{9,11},{10,... | collective-permute-start | bytes 294920 | tf_op jit(solution)/shard_map/ppermute | solution.py:462
  30.0 8.4 %collective-permute-start.6 = (bf16[48,1024]{1,0:T(8,128)(2,1)S(1)}, bf16[48,1024]{1,0:T(8,128)(2,1)S(1)}, u32[]{:S(2)}, u32[]{:S(2)}) collective-permute-start(bf16[48,1024]{1,0:T(8,128)(2,1)S(1)} %sum_terms.2.rest_0_), channel_id=1, source_target_pairs={{0,1},{1,0},{2,3},{3,2},{4,5},{5,4},{6,7},{7,6},{8,9},{9,8},{10,11... | collective-permute-start | bytes 294920 | tf_op jit(solution)/shard_map/ppermute | solution.py:462
  43.7 7.7 %collective-permute-start.11 = (bf16[48,1024]{1,0:T(8,128)(2,1)S(1)}, bf16[48,1024]{1,0:T(8,128)(2,1)S(1)}, u32[]{:S(2)}, u32[]{:S(2)}) collective-permute-start(bf16[48,1024]{1,0:T(8,128)(2,1)S(1)} %get-tuple-element.48), channel_id=1, source_target_pairs={{0,3},{1,2},{2,1},{3,0},{4,7},{5,6},{6,5},{7,4},{8,11},{9,10},{10,... | collective-permute-start | bytes 294920 | tf_op jit(solution)/shard_map/ppermute | solution.py:462
  45.5 8.6 %collective-permute-start.12 = (bf16[48,1024]{1,0:T(8,128)(2,1)S(1)}, bf16[48,1024]{1,0:T(8,128)(2,1)S(1)}, u32[]{:S(2)}, u32[]{:S(2)}) collective-permute-start(bf16[48,1024]{1,0:T(8,128)(2,1)S(1)} %get-tuple-element.49), channel_id=1, source_target_pairs={{0,2},{1,3},{2,0},{3,1},{4,6},{5,7},{6,4},{7,5},{8,10},{9,11},{10,... | collective-permute-start | bytes 294920 | tf_op jit(solution)/shard_map/ppermute | solution.py:462
  45.5 8.6 %collective-permute-start.13 = (bf16[48,1024]{1,0:T(8,128)(2,1)S(1)}, bf16[48,1024]{1,0:T(8,128)(2,1)S(1)}, u32[]{:S(2)}, u32[]{:S(2)}) collective-permute-start(bf16[48,1024]{1,0:T(8,128)(2,1)S(1)} %get-tuple-element.50), channel_id=1, source_target_pairs={{0,1},{1,0},{2,3},{3,2},{4,5},{5,4},{6,7},{7,6},{8,9},{9,8},{10,11... | collective-permute-start | bytes 294920 | tf_op jit(solution)/shard_map/ppermute | solution.py:462
  54.1 8.0 %collective-permute-start.16 = (bf16[48,1024]{1,0:T(8,128)(2,1)S(1)}, bf16[48,1024]{1,0:T(8,128)(2,1)S(1)}, u32[]{:S(2)}, u32[]{:S(2)}) collective-permute-start(bf16[48,1024]{1,0:T(8,128)(2,1)S(1)} %sum_terms.3.rest_0_), channel_id=1, source_target_pairs={{0,3},{1,2},{2,1},{3,0},{4,7},{5,6},{6,5},{7,4},{8,11},{9,10},{10,... | collective-permute-start | bytes 294920 | tf_op jit(solution)/shard_map/ppermute | solution.py:462
  56.3 8.7 %collective-permute-start.15 = (bf16[48,1024]{1,0:T(8,128)(2,1)S(1)}, bf16[48,1024]{1,0:T(8,128)(2,1)S(1)}, u32[]{:S(2)}, u32[]{:S(2)}) collective-permute-start(bf16[48,1024]{1,0:T(8,128)(2,1)S(1)} %sum_terms.3.rest_0_), channel_id=1, source_target_pairs={{0,2},{1,3},{2,0},{3,1},{4,6},{5,7},{6,4},{7,5},{8,10},{9,11},{10,... | collective-permute-start | bytes 294920 | tf_op jit(solution)/shard_map/ppermute | solution.py:462
  56.3 8.7 %collective-permute-start.14 = (bf16[48,1024]{1,0:T(8,128)(2,1)S(1)}, bf16[48,1024]{1,0:T(8,128)(2,1)S(1)}, u32[]{:S(2)}, u32[]{:S(2)}) collective-permute-start(bf16[48,1024]{1,0:T(8,128)(2,1)S(1)} %sum_terms.3.rest_0_), channel_id=1, source_target_pairs={{0,1},{1,0},{2,3},{3,2},{4,5},{5,4},{6,7},{7,6},{8,9},{9,8},{10,11... | collective-permute-start | bytes 294920 | tf_op jit(solution)/shard_map/ppermute | solution.py:462

commit v19 on v18

--- a/solution.py
+++ b/solution.py
@@ -292,23 +292,27 @@
     ).astype(BF16)
 
 
-def project_out(attended, wo, residual, own, sends, me_tp, peers_tp):
-    shard = own.shape[1]
-    for k in list(range(peers_tp - 1, 0, -1)) + [0]:
+def project_out(attended, wo, sends, me_tp):
+    for k in range(len(sends), 0, -1):
+        shard = sends[k - 1].shape[1]
         column = pl.multiple_of(jnp.bitwise_xor(me_tp, k) * shard, shard)
         part = jnp.dot(attended, wo[:, pl.ds(column, shard)], preferred_element_type=F32)
-        if k == 0:
-            own[...] = residual + part
-        else:
-            sends[k - 1][...] = part.astype(BF16)
+        sends[k - 1][...] = part.astype(BF16)
+
+
+def own_kernel(meta, attended, wo, residual, own):
+    shard = own.shape[1]
+    column = pl.multiple_of(meta[1] * shard, shard)
+    part = jnp.dot(attended[...], wo[:, pl.ds(column, shard)], preferred_element_type=F32)
+    own[...] = residual[...].astype(F32) + part
 
 
 def out_kernel(
     peers, peers_tp, meta, plan, attended, wo, hidden, box, *rest,
 ):
     notes, rest = rest[: peers - 2], rest[peers - 2 :]
-    own, sends = rest[0], rest[1:peers_tp]
-    shard = own.shape[1]
+    residual_out, rows_out, sends = rest[0], rest[1], rest[2:]
+    shard = residual_out.shape[1]
     cap = box.shape[2] - NOTE
     rows = attended[...].astype(F32)
     heads = rows.shape[1] // HD
@@ -326,7 +330,9 @@
             note = notes[at // MOVE - 1][m : m + 1, :]
         rows = jnp.where(row_index == plan[at], note[:, : heads * HD], rows)
         residual = jnp.where(residual_index == plan[at], note[:, heads * HD :], residual)
-    project_out(rows.astype(BF16), wo, residual, own, sends, meta[1], peers_tp)
+    residual_out[...] = residual
+    rows_out[...] = rows.astype(BF16)
+    project_out(rows.astype(BF16), wo, sends, meta[1])
 
 
 def pack_kernel(plan, cache, _own, *rest):
@@ -389,12 +395,12 @@
 ):
     blocks, rest = rest[:peers_tp], rest[peers_tp:]
     box_hbm, rest = rest[: peers - 1], rest[peers - 1 :]
-    own, sends, cache = rest[0], rest[1:peers_tp], rest[peers_tp]
+    attended_out, sends, cache = rest[0], rest[1:peers_tp], rest[peers_tp]
     normed3, query_rows, attended_rows, in_sem = rest[peers_tp + 1 :]
     me, me_tp = meta[0], meta[1]
     low = me * slots
     width = gain.shape[1]
-    shard = own.shape[1]
+    shard = blocks[0].shape[1]
     loads = [
         pltpu.make_async_copy(
             box.at[:, :, pl.ds(0, cache.shape[2]), :],
@@ -430,9 +436,8 @@
         turned = turn(query[:, g * HD : (g + 1) * HD], cosine, sine)
         query_rows[pl.ds(g, slots, stride=GROUP), :] = turned.astype(BF16).astype(F32)
     attended = attend_slots(cache, places, positions, query_rows, attended_rows, heads)
-    project_out(
-        attended.astype(BF16), wo, blocks[0][...].astype(F32), own, sends, me_tp, peers_tp
-    )
+    attended_out[...] = attended.astype(BF16)
+    project_out(attended.astype(BF16), wo, sends, me_tp)
 
 
 def cache_kernel(slots, place, cache, out_hbm, out_sem):
@@ -546,17 +551,31 @@
         name="attention",
     )(meta, lengths, query, newkey1, newvalue1, cache)
 
-    sent = [jax.ShapeDtypeStruct((slots, shard), F32)]
-    sent += [jax.ShapeDtypeStruct((slots, shard), BF16)] * (peers_tp - 1)
-    own, *sends = pl.pallas_call(
+    own32 = jax.ShapeDtypeStruct((slots, shard), F32)
+    rows16 = jax.ShapeDtypeStruct((slots, heads * HD), BF16)
+    sent = [jax.ShapeDtypeStruct((slots, shard), BF16)] * (peers_tp - 1)
+
+    def own_term(rows, residual):
+        return pl.pallas_call(
+            own_kernel,
+            out_shape=own32,
+            in_specs=[SMEM] + [VMEM] * 3,
+            out_specs=VMEM,
+            compiler_params=params(16),
+            cost_estimate=cost(2 * slots * shard * heads * HD, out_weight.size // 2),
+            name="own_term",
+        )(meta, rows, out_weight, residual)
+
+    residual, rows, *sends = pl.pallas_call(
         functools.partial(out_kernel, peers, peers_tp),
-        out_shape=sent,
+        out_shape=[own32, rows16] + sent,
         in_specs=[SMEM] * 2 + [VMEM] * (3 + others),
-        out_specs=[VMEM] * peers_tp,
+        out_specs=[VMEM] * (1 + peers_tp),
         compiler_params=params(16),
         cost_estimate=cost(2 * slots * width * heads * HD, out_weight.size * 2),
         name="out_projection",
     )(meta, plan, attended, out_weight, hidden, *got_notes)
+    own = own_term(rows, residual)
     boxes = pl.pallas_call(
         pack_kernel,
         out_shape=[jax.ShapeDtypeStruct((MOVE,) + kv_cache.shape[1:], BF16)] * (others - 1),
@@ -566,7 +585,7 @@
         compiler_params=params(16),
         cost_estimate=cost(1, 1 * cache_bytes),
         name="pack",
-    )(plan, cache, own)
+    )(plan, cache, rows)
     got_boxes = got_notes[:1] + [swapped(box, "inst", peers, k + 2) for k, box in enumerate(boxes)]
 
     def summed(own, sends, passed_on):
@@ -603,11 +622,11 @@
         compiler_params=params(16),
         cost_estimate=cost(100*flops, wkv.size * 40),
         name="prepare",
-    )(meta, source, lengths, plan, cosine, sine, wkv, own)
-
-    own, *sends, cache = pl.pallas_call(
+    )(meta, source, lengths, plan, cosine, sine, wkv, rows)
+
+    rows, *sends, cache = pl.pallas_call(
         functools.partial(second_kernel, peers, peers_tp, slots, heads),
-        out_shape=sent + [held],
+        out_shape=[rows16] + sent + [held],
         in_specs=[SMEM] * 4 + [VMEM] * (7 + peers_tp) + [ANY] * others,
         out_specs=[VMEM] * (1 + peers_tp),
         scratch_shapes=[
@@ -622,6 +641,7 @@
         name="second_step",
     )(meta, source, lengths, place, gain, cos_rows, sin_rows, query_weight, weight, out_weight, cache,
       *pieces, *got_boxes)
+    own = own_term(rows, pieces[0])
 
     pieces = summed(own, sends, False)
     final_cache = pl.pallas_call(

time: 66.4 us -> 66.1 us (level)
  waiting for transfers between devices: 18.6 us -> 16.9 us
  Pallas kernels: 24.4 us -> 25.7 us
    ppermute x17, waiting for transfers between devices: 18.6 us -> 16.9 us  [swapped(): return lax.ppermute(x, axis, [(i, i ^ k) for i in range(size)])]
    pallas_call x0 -> x2, Pallas kernels: none -> 1.67 us  [own_term(): pl.pallas_call(own_kernel, out_shape=own32, in_specs=[SMEM] + [VMEM] * 3,...]
  transfers between devices with their start and end apart: 17 -> 17, of which waited for: 8 -> 7; matrix products, arithmetic and copies ran while one was open for 0% -> 0% of each run, Pallas kernels for 15% -> 17%
where the time goes in v19:
time: 66.1 us; the launch traced here: 66 us
  Pallas kernels  25.7 us (39%)
  starting transfers between devices  22.4 us (34%)
  waiting for transfers between devices  16.9 us (26%)
  between operations  0.84 us (1%)
    ppermute x17, starting transfers between devices, swapped(): return lax.ppermute(x, axis, [(i, i ^ k) for i in range(size)])  22.4 us
    ppermute x17, waiting for transfers between devices, swapped(): return lax.ppermute(x, axis, [(i, i ^ k) for i in range(size)])  16.9 us
    pallas_call x1, Pallas kernels, local(): pl.pallas_call(functools.partial(first_kernel, peers, slots, heads, shard...  6.67 us
    pallas_call x1, Pallas kernels, local(): pl.pallas_call(functools.partial(second_kernel, peers, peers_tp, slots, h...  5.02 us
    pallas_call x1, Pallas kernels, local(): pl.pallas_call(functools.partial(cache_kernel, slots), out_shape=jax.Shap...  3.58 us
    pallas_call x1, Pallas kernels, local(): pl.pallas_call(functools.partial(attend_kernel, slots, heads), out_shape=...  2.65 us
    pallas_call x1, Pallas kernels, local(): pl.pallas_call(functools.partial(prepare_kernel, peers, slots), out_shape...  2.19 us
    pallas_call x2, Pallas kernels, own_term(): pl.pallas_call(own_kernel, out_shape=own32, in_specs=[SMEM] + [VMEM] * 3,...  1.67 us
  transfers between devices with their start and end apart: 17, of which 7 were waited for; matrix products, arithmetic and copies ran while one was open for 0% of the time, Pallas kernels for 17%

profile of v19, /device:TPU:0, one launch (start us, length us, event | category | flops | bytes accessed | tf_op | source)
XLA Modules:
  0.0 66.0 jit_solution(9080935273508697192)
XLA Ops:
  0.6 0.1 pad_add_fusion.meta
  0.7 6.7 %first_step.1 = (f32[384,128]{1,0:T(8,128)S(1)}, f32[48,128]{1,0:T(8,128)S(1)}, f32[48,128]{1,0:T(8,128)S(1)}, s32[12]{0:T(128)S(1)}, bf16[54,2,256,128]{3,2,1,0...) custom-call(s32[2]{0:T(128)S(1)} %pad_add_fusion.meta, ...), custom_call_target="tpu_custom_call" | custom-call | flops 301989888 | bytes 6291456 | tf_op jit(solution)/shard_map/first_step/pallas_call | solution.py:501
  7.4 0.0 copy-start
  7.4 0.0 copy-start.3
  7.4 0.6 collective-permute-start
  8.0 2.5 %collective-permute-start.1 = (f32[2,1536]{1,0:T(2,128)S(1)}, f32[2,1536]{1,0:T(2,128)S(1)}, u32[]{:S(2)}, u32[]{:S(2)}) collective-permute-start(f32[2,1536]{1,0:T(2,128)S(1)} %get-tuple-element.35), channel_id=1, source_target_pairs={{0,8},{4,12},{8,0},{12,4},{1,9},{5,13},{9,1},{13,5},{2,10},{6,14},... | collective-permute-start | bytes 36872 | tf_op jit(solution)/shard_map/ppermute | solution.py:467
  10.5 0.1 collective-permute-start.2
  10.6 0.0 copy-done.7
  10.6 2.6 %attention.1 = (bf16[48,512]{1,0:T(8,128)(2,1)S(1)}, bf16[54,2,256,128]{3,2,1,0:T(8,128)(2,1)S(1)}) custom-call(s32[2]{0:T(128)S(1)} %pad_add_fusion.meta, s32[192]{0:T(256)S(1)} %copy-done.7, f32[384,128]{1,0:T(8,128)S(1)} %get-tuple-element.29.query, f32[48,128]{1,0:T(8,128)S(1)} %get-tuple-element.30.newkey, ...), custom_call_target="tpu_custom_call", output_to_operand_aliasing={{1}: (5, {})} | custom-call | flops 25165824 | bytes 6291456 | tf_op jit(solution)/shard_map/attention/pallas_call | solution.py:542
  13.2 0.0 collective-permute-done.1.rest_0_
  13.3 0.4 collective-permute-done.2.rest_1_
  13.6 0.0 collective-permute-done.box.rest_4_
  13.6 0.0 copy-done
  13.7 0.0 copy-done.3
  13.7 1.3 %out_projection.1 = (f32[48,1024]{1,0:T(8,128)S(1)}, bf16[48,512]{1,0:T(8,128)(2,1)S(1)}, bf16[48,1024]{1,0:T(8,128)(2,1)S(1)}, bf16[48,1024]{1,0:T(8,128)(2,1)S(1)}, bf16[48,1024]{1,0:T(8,128)(2,1)S(1)}) custom-call(s32[2]{0:T(128)S(1)} %pad_add_fusion.meta, s32[12]{0:T(128)S(1)} %get-tuple-element.28.plan, bf16[48,512]{1,0:T(8,128)(2,1)S(1)} %get-tuple-element.33.attended, ...), custom_call_target="tpu_custom_call" | custom-call | flops 201326592 | bytes 4194304 | tf_op jit(solution)/shard_map/out_projection/pallas_call | solution.py:569
  14.9 0.0 copy-start.2
  14.9 0.0 copy-start.4
  14.9 0.0 copy-start.5
  15.0 0.0 copy-start.8
  15.0 3.7 %collective-permute-start.3 = (bf16[48,1024]{1,0:T(8,128)(2,1)S(1)}, bf16[48,1024]{1,0:T(8,128)(2,1)S(1)}, u32[]{:S(2)}, u32[]{:S(2)}) collective-permute-start(bf16[48,1024]{1,0:T(8,128)(2,1)S(1)} %get-tuple-element.44), channel_id=1, source_target_pairs={{0,3},{1,2},{2,1},{3,0},{4,7},{5,6},{6,5},{7,4},{8,11},{9,10},{10,... | collective-permute-start | bytes 294920 | tf_op jit(solution)/shard_map/ppermute | solution.py:467
  18.6 0.0 collective-permute-start.4
  18.6 0.8 %collective-permute-start.5 = (bf16[48,1024]{1,0:T(8,128)(2,1)S(1)}, bf16[48,1024]{1,0:T(8,128)(2,1)S(1)}, u32[]{:S(2)}, u32[]{:S(2)}) collective-permute-start(bf16[48,1024]{1,0:T(8,128)(2,1)S(1)} %get-tuple-element.46), channel_id=1, source_target_pairs={{0,1},{1,0},{2,3},{3,2},{4,5},{5,4},{6,7},{7,6},{8,9},{9,8},{10,11... | collective-permute-start | bytes 294920 | tf_op jit(solution)/shard_map/ppermute | solution.py:467
  19.4 1.3 %pack.1 = (bf16[2,2,256,128]{3,2,1,0:T(8,128)(2,1)S(1)}, bf16[2,2,256,128]{3,2,1,0:T(8,128)(2,1)S(1)}) custom-call(s32[12]{0:T(128)S(1)} %get-tuple-element.28.plan, bf16[54,2,256,128]{3,2,1,0:T(8,128)(2,1)S(1)} %get-tuple-element.42.cache._, bf16[48,512]{1,0:T(8,128)(2,1)S(1)} %get-tuple-element.37._.attended._own), custom_call_target="tpu_custom_call" | custom-call | flops 1 | bytes 6291456 | tf_op jit(solution)/shard_map/pack/pallas_call | solution.py:579
  20.7 1.4 %collective-permute-start.9 = (bf16[2,2,256,128]{3,2,1,0:T(8,128)(2,1)S(1)}, bf16[2,2,256,128]{3,2,1,0:T(8,128)(2,1)S(1)}, u32[]{:S(2)}, u32[]{:S(2)}) collective-permute-start(bf16[2,2,256,128]{3,2,1,0:T(8,128)(2,1)S(1)} %get-tuple-element.47), channel_id=1, source_target_pairs={{0,8},{4,12},{8,0},{12,4},{1,9},{5,13},{9,1},{13,5},{2,10},{6,14},... | collective-permute-start | bytes 786440 | tf_op jit(solution)/shard_map/ppermute | solution.py:467
  22.1 0.0 collective-permute-start.10
  22.1 0.8 %own_term.2.own = f32[48,1024]{1,0:T(8,128)S(1)} custom-call(s32[2]{0:T(128)S(1)} %pad_add_fusion.meta, bf16[48,512]{1,0:T(8,128)(2,1)S(1)} %get-tuple-element.37._.attended._own, bf16[512,4096]{1,0:T(8,128)(2,1)S(1)} %copy-done, f32[48,1024]{1,0:T(8,128)S(1)} %get-tuple-element.43.residual), custom_call_target="tpu_custom_call" | custom-call | flops 50331648 | bytes 1048576 | tf_op jit(solution)/shard_map/own_term/pallas_call | solution.py:559
  23.0 0.0 collective-permute-done.3.rest_0_
  23.0 4.3 %collective-permute-done.4.rest_1_ = bf16[48,1024]{1,0:T(8,128)(2,1)S(1)} collective-permute-done((bf16[48,1024]{1,0:T(8,128)(2,1)S(1)}, bf16[48,1024]{1,0:T(8,128)(2,1)S(1)}, u32[]{:S(2)}, u32[]{:S(2)}) %collective-permute-start.4) | collective-permute-done | bytes 98336 | tf_op jit(solution)/shard_map/ppermute | solution.py:467
  27.3 0.0 collective-permute-done.5.rest_2_
  27.3 0.1 sum_terms.2.rest_0_.residual
  27.3 0.0 copy-start.1
  27.3 0.0 copy-start.6
  27.4 2.5 %collective-permute-start.8 = (bf16[48,1024]{1,0:T(8,128)(2,1)S(1)}, bf16[48,1024]{1,0:T(8,128)(2,1)S(1)}, u32[]{:S(2)}, u32[]{:S(2)}) collective-permute-start(bf16[48,1024]{1,0:T(8,128)(2,1)S(1)} %sum_terms.2.rest_0_.residual), channel_id=1, source_target_pairs={{0,3},{1,2},{2,1},{3,0},{4,7},{5,6},{6,5},{7,4},{8,11},{9,10},{10,... | collective-permute-start | bytes 294920 | tf_op jit(solution)/shard_map/ppermute | solution.py:467
  29.9 0.0 collective-permute-start.7
  29.9 1.9 %collective-permute-start.6 = (bf16[48,1024]{1,0:T(8,128)(2,1)S(1)}, bf16[48,1024]{1,0:T(8,128)(2,1)S(1)}, u32[]{:S(2)}, u32[]{:S(2)}) collective-permute-start(bf16[48,1024]{1,0:T(8,128)(2,1)S(1)} %sum_terms.2.rest_0_.residual), channel_id=1, source_target_pairs={{0,1},{1,0},{2,3},{3,2},{4,5},{5,4},{6,7},{7,6},{8,9},{9,8},{10,11... | collective-permute-start | bytes 294920 | tf_op jit(solution)/shard_map/ppermute | solution.py:467
  31.8 0.0 copy-done.2
  31.8 0.0 copy-done.4
  31.8 0.0 copy-done.5
  31.8 0.0 copy-done.8
  31.8 2.2 %prepare.1 = (bf16[4096,256]{1,0:T(8,128)(2,1)S(1)}, f32[48,128]{1,0:T(8,128)S(1)}, f32[48,128]{1,0:T(8,128)S(1)}, s32[48]{0:T(128)S(1)}) custom-call(s32[2]{0:T(128)S(1)} %pad_add_fusion.meta, s32[192]{0:T(256)S(1)} %copy-done.8, s32[192]{0:T(256)S(1)} %copy-done.7, s32[12]{0:T(128)S(1)} %get-tuple-element.28.plan, f32[256,128]{1,0:T(8,128)S(1)} %copy-done.5, ...), custom_call_target="tpu_custom_call" | custom-call | flops 30198988800 | bytes 41943040 | tf_op jit(solution)/shard_map/prepare/pallas_call | solution.py:612
  34.0 0.9 %collective-permute-done.8.rest_3_ = bf16[48,1024]{1,0:T(8,128)(2,1)S(1)} collective-permute-done((bf16[48,1024]{1,0:T(8,128)(2,1)S(1)}, bf16[48,1024]{1,0:T(8,128)(2,1)S(1)}, u32[]{:S(2)}, u32[]{:S(2)}) %collective-permute-start.8) | collective-permute-done | bytes 98336 | tf_op jit(solution)/shard_map/ppermute | solution.py:467
  35.0 3.4 %collective-permute-done.7.rest_2_ = bf16[48,1024]{1,0:T(8,128)(2,1)S(1)} collective-permute-done((bf16[48,1024]{1,0:T(8,128)(2,1)S(1)}, bf16[48,1024]{1,0:T(8,128)(2,1)S(1)}, u32[]{:S(2)}, u32[]{:S(2)}) %collective-permute-start.7) | collective-permute-done | bytes 98336 | tf_op jit(solution)/shard_map/ppermute | solution.py:467
  38.3 0.0 collective-permute-done.6.rest_1_
  38.3 0.0 collective-permute-done.9.rest_5_
  38.3 0.0 collective-permute-done.10.rest_6_
  38.3 0.0 copy-done.1
  38.3 0.0 copy-done.6
  38.4 5.0 %second_step.1 = (bf16[48,512]{1,0:T(8,128)(2,1)S(1)}, bf16[48,1024]{1,0:T(8,128)(2,1)S(1)}, bf16[48,1024]{1,0:T(8,128)(2,1)S(1)}, bf16[48,1024]{1,0:T(8,128)(2,1)S(1)}, bf16[54,2,256,128]{3,2,1,0:T(8,128)(2,1)S(1)}) custom-call(s32[2]{0:T(128)S(1)} %pad_add_fusion.meta, s32[192]{0:T(256)S(1)} %copy-done.8, ...), custom_call_target="tpu_custom_call", output_to_operand_aliasing={{4}: (10, {})} | custom-call | flops 905969664 | bytes 18874368 | tf_op jit(solution)/shard_map/second_step/pallas_call | solution.py:627
  43.4 1.8 %collective-permute-start.11 = (bf16[48,1024]{1,0:T(8,128)(2,1)S(1)}, bf16[48,1024]{1,0:T(8,128)(2,1)S(1)}, u32[]{:S(2)}, u32[]{:S(2)}) collective-permute-start(bf16[48,1024]{1,0:T(8,128)(2,1)S(1)} %get-tuple-element.50), channel_id=1, source_target_pairs={{0,3},{1,2},{2,1},{3,0},{4,7},{5,6},{6,5},{7,4},{8,11},{9,10},{10,... | collective-permute-start | bytes 294920 | tf_op jit(solution)/shard_map/ppermute | solution.py:467
  45.2 0.0 collective-permute-start.12
  45.2 2.7 %collective-permute-start.13 = (bf16[48,1024]{1,0:T(8,128)(2,1)S(1)}, bf16[48,1024]{1,0:T(8,128)(2,1)S(1)}, u32[]{:S(2)}, u32[]{:S(2)}) collective-permute-start(bf16[48,1024]{1,0:T(8,128)(2,1)S(1)} %get-tuple-element.52), channel_id=1, source_target_pairs={{0,1},{1,0},{2,3},{3,2},{4,5},{5,4},{6,7},{7,6},{8,9},{9,8},{10,11... | collective-permute-start | bytes 294920 | tf_op jit(solution)/shard_map/ppermute | solution.py:467
  47.8 0.8 %own_term.3.own = f32[48,1024]{1,0:T(8,128)S(1)} custom-call(s32[2]{0:T(128)S(1)} %pad_add_fusion.meta, bf16[48,512]{1,0:T(8,128)(2,1)S(1)} %get-tuple-element.49.attended, bf16[512,4096]{1,0:T(8,128)(2,1)S(1)} %copy-done, bf16[48,1024]{1,0:T(8,128)(2,1)S(1)} %sum_terms.2.rest_0_.residual), custom_call_target="tpu_custom_call" | custom-call | flops 50331648 | bytes 1048576 | tf_op jit(solution)/shard_map/own_term/pallas_call | solution.py:559
  48.7 2.4 %collective-permute-done.11.rest_0_ = bf16[48,1024]{1,0:T(8,128)(2,1)S(1)} collective-permute-done((bf16[48,1024]{1,0:T(8,128)(2,1)S(1)}, bf16[48,1024]{1,0:T(8,128)(2,1)S(1)}, u32[]{:S(2)}, u32[]{:S(2)}) %collective-permute-start.11) | collective-permute-done | bytes 98336 | tf_op jit(solution)/shard_map/ppermute | solution.py:467
  51.0 2.7 %collective-permute-done.12.rest_1_ = bf16[48,1024]{1,0:T(8,128)(2,1)S(1)} collective-permute-done((bf16[48,1024]{1,0:T(8,128)(2,1)S(1)}, bf16[48,1024]{1,0:T(8,128)(2,1)S(1)}, u32[]{:S(2)}, u32[]{:S(2)}) %collective-permute-start.12) | collective-permute-done | bytes 98336 | tf_op jit(solution)/shard_map/ppermute | solution.py:467
  53.7 0.0 collective-permute-done.13.rest_2_
  53.7 0.1 sum_terms.3.rest_0_
  53.8 2.2 %collective-permute-start.16 = (bf16[48,1024]{1,0:T(8,128)(2,1)S(1)}, bf16[48,1024]{1,0:T(8,128)(2,1)S(1)}, u32[]{:S(2)}, u32[]{:S(2)}) collective-permute-start(bf16[48,1024]{1,0:T(8,128)(2,1)S(1)} %sum_terms.3.rest_0_), channel_id=1, source_target_pairs={{0,3},{1,2},{2,1},{3,0},{4,7},{5,6},{6,5},{7,4},{8,11},{9,10},{10,... | collective-permute-start | bytes 294920 | tf_op jit(solution)/shard_map/ppermute | solution.py:467
  56.0 0.0 collective-permute-start.15
  56.0 2.2 %collective-permute-start.14 = (bf16[48,1024]{1,0:T(8,128)(2,1)S(1)}, bf16[48,1024]{1,0:T(8,128)(2,1)S(1)}, u32[]{:S(2)}, u32[]{:S(2)}) collective-permute-start(bf16[48,1024]{1,0:T(8,128)(2,1)S(1)} %sum_terms.3.rest_0_), channel_id=1, source_target_pairs={{0,1},{1,0},{2,3},{3,2},{4,5},{5,4},{6,7},{7,6},{8,9},{9,8},{10,11... | collective-permute-start | bytes 294920 | tf_op jit(solution)/shard_map/ppermute | solution.py:467
  58.2 3.6 %write_cache.1 = bf16[48,2,256,128]{3,2,1,0:T(8,128)(2,1)} custom-call(s32[48]{0:T(128)S(1)} %get-tuple-element.38.place, bf16[54,2,256,128]{3,2,1,0:T(8,128)(2,1)S(1)} %get-tuple-element.53.cache), custom_call_target="tpu_custom_call" | custom-call | bytes 12582912 | tf_op jit(solution)/shard_map/write_cache/pallas_call | solution.py:647
  61.8 0.0 collective-permute-done.16.rest_3_
  61.8 2.8 %collective-permute-done.15.rest_2_ = bf16[48,1024]{1,0:T(8,128)(2,1)S(1)} collective-permute-done((bf16[48,1024]{1,0:T(8,128)(2,1)S(1)}, bf16[48,1024]{1,0:T(8,128)(2,1)S(1)}, u32[]{:S(2)}, u32[]{:S(2)}) %collective-permute-start.15) | collective-permute-done | bytes 98336 | tf_op jit(solution)/shard_map/ppermute | solution.py:467
  64.7 0.0 collective-permute-done.14.rest_1_
  64.7 1.3 %join.1 = bf16[48,4096]{1,0:T(8,128)(2,1)} custom-call(s32[2]{0:T(128)S(1)} %pad_add_fusion.meta, bf16[48,1024]{1,0:T(8,128)(2,1)S(1)} %sum_terms.3.rest_0_, bf16[48,1024]{1,0:T(8,128)(2,1)S(1)} %collective-permute-done.14.rest_1_, bf16[48,1024]{1,0:T(8,128)(2,1)S(1)} %collective-permute-done.15.rest_2_, bf16[48,1024]{1,0:T(8,128)(2,1)S(1)} %collective-permute-done.16.rest_3_), custom_call_target="tpu_custom_call" | custom-call | tf_op jit(solution)/shard_map/join/pallas_call | solution.py:657
  (1 shorter events, 0.0 us)
Async XLA Ops:
  0.7 9.9 %copy-start.7 = (s32[192]{0:T(256)S(1)}, s32[192]{0:T(256)}, u32[]{:S(2)}) copy-start(s32[192]{0:T(256)} %lengths_s.5) | copy-start | bytes 2308
  7.4 6.3 %copy-start = (bf16[512,4096]{1,0:T(8,128)(2,1)S(1)}, bf16[512,4096]{1,0:T(8,128)(2,1)}, u32[]{:S(2)}) copy-start(bf16[512,4096]{1,0:T(8,128)(2,1)} %wo.7) | copy-start | bytes 12582916
  7.4 6.2 %copy-start.3 = (bf16[48,4096]{1,0:T(8,128)(2,1)S(1)}, bf16[48,4096]{1,0:T(8,128)(2,1)}, u32[]{:S(2)}) copy-start(bf16[48,4096]{1,0:T(8,128)(2,1)} %hidden.1) | copy-start | bytes 1179652
  7.4 6.2 %collective-permute-start = (bf16[2,2,272,128]{3,2,1,0:T(8,128)(2,1)S(1)}, bf16[2,2,272,128]{3,2,1,0:T(8,128)(2,1)S(1)}, u32[]{:S(2)}, u32[]{:S(2)}) collective-permute-start(bf16[2,2,272,128]{3,2,1,0:T(8,128)(2,1)S(1)} %get-tuple-element.34), channel_id=1, source_target_pairs={{0,4},{4,0},{8,12},{12,8},{1,5},{5,1},{9,13},{13,9},{2,6},{6,2},{1... | collective-permute-start | bytes 835592 | tf_op jit(solution)/shard_map/ppermute | solution.py:467
  8.0 5.3 %collective-permute-start.1 = (f32[2,1536]{1,0:T(2,128)S(1)}, f32[2,1536]{1,0:T(2,128)S(1)}, u32[]{:S(2)}, u32[]{:S(2)}) collective-permute-start(f32[2,1536]{1,0:T(2,128)S(1)} %get-tuple-element.35), channel_id=1, source_target_pairs={{0,8},{4,12},{8,0},{12,4},{1,9},{5,13},{9,1},{13,5},{2,10},{6,14},... | collective-permute-start | bytes 36872 | tf_op jit(solution)/shard_map/ppermute | solution.py:467
  10.5 3.1 %collective-permute-start.2 = (f32[2,1536]{1,0:T(2,128)S(1)}, f32[2,1536]{1,0:T(2,128)S(1)}, u32[]{:S(2)}, u32[]{:S(2)}) collective-permute-start(f32[2,1536]{1,0:T(2,128)S(1)} %get-tuple-element.36), channel_id=1, source_target_pairs={{0,12},{4,8},{8,4},{12,0},{1,13},{5,9},{9,5},{13,1},{2,14},{6,10},... | collective-permute-start | bytes 36872 | tf_op jit(solution)/shard_map/ppermute | solution.py:467
  14.9 16.9 %copy-start.2 = (bf16[4096,2,128]{2,1,0:T(2,128)(2,1)S(1)}, bf16[4096,2,128]{2,1,0:T(2,128)(2,1)}, u32[]{:S(2)}) copy-start(bf16[4096,2,128]{2,1,0:T(2,128)(2,1)} %param.16) | copy-start | bytes 6291460
  14.9 16.9 %copy-start.4 = (f32[256,128]{1,0:T(8,128)S(1)}, f32[256,128]{1,0:T(8,128)}, u32[]{:S(2)}) copy-start(f32[256,128]{1,0:T(8,128)} %constant.12.clone.sin_hbm.sin_ref) | copy-start | bytes 393220
  14.9 16.9 %copy-start.5 = (f32[256,128]{1,0:T(8,128)S(1)}, f32[256,128]{1,0:T(8,128)}, u32[]{:S(2)}) copy-start(f32[256,128]{1,0:T(8,128)} %constant.11.clone.cos_hbm.cos_ref) | copy-start | bytes 393220
  15.0 16.9 %copy-start.8 = (s32[192]{0:T(256)S(1)}, s32[192]{0:T(256)}, u32[]{:S(2)}) copy-start(s32[192]{0:T(256)} %source_s.3) | copy-start | bytes 2308
  15.0 8.0 %collective-permute-start.3 = (bf16[48,1024]{1,0:T(8,128)(2,1)S(1)}, bf16[48,1024]{1,0:T(8,128)(2,1)S(1)}, u32[]{:S(2)}, u32[]{:S(2)}) collective-permute-start(bf16[48,1024]{1,0:T(8,128)(2,1)S(1)} %get-tuple-element.44), channel_id=1, source_target_pairs={{0,3},{1,2},{2,1},{3,0},{4,7},{5,6},{6,5},{7,4},{8,11},{9,10},{10,... | collective-permute-start | bytes 294920 | tf_op jit(solution)/shard_map/ppermute | solution.py:467
  18.6 8.6 %collective-permute-start.4 = (bf16[48,1024]{1,0:T(8,128)(2,1)S(1)}, bf16[48,1024]{1,0:T(8,128)(2,1)S(1)}, u32[]{:S(2)}, u32[]{:S(2)}) collective-permute-start(bf16[48,1024]{1,0:T(8,128)(2,1)S(1)} %get-tuple-element.45), channel_id=1, source_target_pairs={{0,2},{1,3},{2,0},{3,1},{4,6},{5,7},{6,4},{7,5},{8,10},{9,11},{10,... | collective-permute-start | bytes 294920 | tf_op jit(solution)/shard_map/ppermute | solution.py:467
  18.6 8.6 %collective-permute-start.5 = (bf16[48,1024]{1,0:T(8,128)(2,1)S(1)}, bf16[48,1024]{1,0:T(8,128)(2,1)S(1)}, u32[]{:S(2)}, u32[]{:S(2)}) collective-permute-start(bf16[48,1024]{1,0:T(8,128)(2,1)S(1)} %get-tuple-element.46), channel_id=1, source_target_pairs={{0,1},{1,0},{2,3},{3,2},{4,5},{5,4},{6,7},{7,6},{8,9},{9,8},{10,11... | collective-permute-start | bytes 294920 | tf_op jit(solution)/shard_map/ppermute | solution.py:467
  20.7 17.6 %collective-permute-start.9 = (bf16[2,2,256,128]{3,2,1,0:T(8,128)(2,1)S(1)}, bf16[2,2,256,128]{3,2,1,0:T(8,128)(2,1)S(1)}, u32[]{:S(2)}, u32[]{:S(2)}) collective-permute-start(bf16[2,2,256,128]{3,2,1,0:T(8,128)(2,1)S(1)} %get-tuple-element.47), channel_id=1, source_target_pairs={{0,8},{4,12},{8,0},{12,4},{1,9},{5,13},{9,1},{13,5},{2,10},{6,14},... | collective-permute-start | bytes 786440 | tf_op jit(solution)/shard_map/ppermute | solution.py:467
  22.1 16.2 %collective-permute-start.10 = (bf16[2,2,256,128]{3,2,1,0:T(8,128)(2,1)S(1)}, bf16[2,2,256,128]{3,2,1,0:T(8,128)(2,1)S(1)}, u32[]{:S(2)}, u32[]{:S(2)}) collective-permute-start(bf16[2,2,256,128]{3,2,1,0:T(8,128)(2,1)S(1)} %get-tuple-element.48), channel_id=1, source_target_pairs={{0,12},{4,8},{8,4},{12,0},{1,13},{5,9},{9,5},{13,1},{2,14},{6,10},... | collective-permute-start | bytes 786440 | tf_op jit(solution)/shard_map/ppermute | solution.py:467
  27.3 11.0 %copy-start.1 = (bf16[4096,512]{1,0:T(8,128)(2,1)S(1)}, bf16[4096,512]{1,0:T(8,128)(2,1)}, u32[]{:S(2)}) copy-start(bf16[4096,512]{1,0:T(8,128)(2,1)} %wq.1) | copy-start | bytes 12582916
  27.3 11.0 %copy-start.6 = (f32[4096]{0:T(1024)S(1)}, f32[4096]{0:T(1024)}, u32[]{:S(2)}) copy-start(f32[4096]{0:T(1024)} %param.14) | copy-start | bytes 49156
  27.4 7.6 %collective-permute-start.8 = (bf16[48,1024]{1,0:T(8,128)(2,1)S(1)}, bf16[48,1024]{1,0:T(8,128)(2,1)S(1)}, u32[]{:S(2)}, u32[]{:S(2)}) collective-permute-start(bf16[48,1024]{1,0:T(8,128)(2,1)S(1)} %sum_terms.2.rest_0_.residual), channel_id=1, source_target_pairs={{0,3},{1,2},{2,1},{3,0},{4,7},{5,6},{6,5},{7,4},{8,11},{9,10},{10,... | collective-permute-start | bytes 294920 | tf_op jit(solution)/shard_map/ppermute | solution.py:467
  29.9 8.4 %collective-permute-start.7 = (bf16[48,1024]{1,0:T(8,128)(2,1)S(1)}, bf16[48,1024]{1,0:T(8,128)(2,1)S(1)}, u32[]{:S(2)}, u32[]{:S(2)}) collective-permute-start(bf16[48,1024]{1,0:T(8,128)(2,1)S(1)} %sum_terms.2.rest_0_.residual), channel_id=1, source_target_pairs={{0,2},{1,3},{2,0},{3,1},{4,6},{5,7},{6,4},{7,5},{8,10},{9,11},{10,... | collective-permute-start | bytes 294920 | tf_op jit(solution)/shard_map/ppermute | solution.py:467
  29.9 8.4 %collective-permute-start.6 = (bf16[48,1024]{1,0:T(8,128)(2,1)S(1)}, bf16[48,1024]{1,0:T(8,128)(2,1)S(1)}, u32[]{:S(2)}, u32[]{:S(2)}) collective-permute-start(bf16[48,1024]{1,0:T(8,128)(2,1)S(1)} %sum_terms.2.rest_0_.residual), channel_id=1, source_target_pairs={{0,1},{1,0},{2,3},{3,2},{4,5},{5,4},{6,7},{7,6},{8,9},{9,8},{10,11... | collective-permute-start | bytes 294920 | tf_op jit(solution)/shard_map/ppermute | solution.py:467
  43.4 7.7 %collective-permute-start.11 = (bf16[48,1024]{1,0:T(8,128)(2,1)S(1)}, bf16[48,1024]{1,0:T(8,128)(2,1)S(1)}, u32[]{:S(2)}, u32[]{:S(2)}) collective-permute-start(bf16[48,1024]{1,0:T(8,128)(2,1)S(1)} %get-tuple-element.50), channel_id=1, source_target_pairs={{0,3},{1,2},{2,1},{3,0},{4,7},{5,6},{6,5},{7,4},{8,11},{9,10},{10,... | collective-permute-start | bytes 294920 | tf_op jit(solution)/shard_map/ppermute | solution.py:467
  45.2 8.6 %collective-permute-start.12 = (bf16[48,1024]{1,0:T(8,128)(2,1)S(1)}, bf16[48,1024]{1,0:T(8,128)(2,1)S(1)}, u32[]{:S(2)}, u32[]{:S(2)}) collective-permute-start(bf16[48,1024]{1,0:T(8,128)(2,1)S(1)} %get-tuple-element.51), channel_id=1, source_target_pairs={{0,2},{1,3},{2,0},{3,1},{4,6},{5,7},{6,4},{7,5},{8,10},{9,11},{10,... | collective-permute-start | bytes 294920 | tf_op jit(solution)/shard_map/ppermute | solution.py:467
  45.2 8.6 %collective-permute-start.13 = (bf16[48,1024]{1,0:T(8,128)(2,1)S(1)}, bf16[48,1024]{1,0:T(8,128)(2,1)S(1)}, u32[]{:S(2)}, u32[]{:S(2)}) collective-permute-start(bf16[48,1024]{1,0:T(8,128)(2,1)S(1)} %get-tuple-element.52), channel_id=1, source_target_pairs={{0,1},{1,0},{2,3},{3,2},{4,5},{5,4},{6,7},{7,6},{8,9},{9,8},{10,11... | collective-permute-start | bytes 294920 | tf_op jit(solution)/shard_map/ppermute | solution.py:467
  53.8 8.0 %collective-permute-start.16 = (bf16[48,1024]{1,0:T(8,128)(2,1)S(1)}, bf16[48,1024]{1,0:T(8,128)(2,1)S(1)}, u32[]{:S(2)}, u32[]{:S(2)}) collective-permute-start(bf16[48,1024]{1,0:T(8,128)(2,1)S(1)} %sum_terms.3.rest_0_), channel_id=1, source_target_pairs={{0,3},{1,2},{2,1},{3,0},{4,7},{5,6},{6,5},{7,4},{8,11},{9,10},{10,... | collective-permute-start | bytes 294920 | tf_op jit(solution)/shard_map/ppermute | solution.py:467
  56.0 8.7 %collective-permute-start.15 = (bf16[48,1024]{1,0:T(8,128)(2,1)S(1)}, bf16[48,1024]{1,0:T(8,128)(2,1)S(1)}, u32[]{:S(2)}, u32[]{:S(2)}) collective-permute-start(bf16[48,1024]{1,0:T(8,128)(2,1)S(1)} %sum_terms.3.rest_0_), channel_id=1, source_target_pairs={{0,2},{1,3},{2,0},{3,1},{4,6},{5,7},{6,4},{7,5},{8,10},{9,11},{10,... | collective-permute-start | bytes 294920 | tf_op jit(solution)/shard_map/ppermute | solution.py:467
  56.0 8.7 %collective-permute-start.14 = (bf16[48,1024]{1,0:T(8,128)(2,1)S(1)}, bf16[48,1024]{1,0:T(8,128)(2,1)S(1)}, u32[]{:S(2)}, u32[]{:S(2)}) collective-permute-start(bf16[48,1024]{1,0:T(8,128)(2,1)S(1)} %sum_terms.3.rest_0_), channel_id=1, source_target_pairs={{0,1},{1,0},{2,3},{3,2},{4,5},{5,4},{6,7},{7,6},{8,9},{9,8},{10,11... | collective-permute-start | bytes 294920 | tf_op jit(solution)/shard_map/ppermute | solution.py:467

commit v20 on v19

--- a/solution.py
+++ b/solution.py
@@ -15,7 +15,7 @@
 GROUP = 8
 PIECE = 16
 CHUNK = 8
-BATCH = 16
+BATCH = 24
 NOTE = 16
 
 F32 = jnp.float32
@@ -374,9 +374,10 @@
 ):
     map_places(slots, peers, plan, place)
     low = meta[0] * slots
-    gather_angles(
-        lambda s: lengths_s[source_s[low + s]] + 1, slots, cos_ref, sin_ref, cos_rows, sin_rows
-    )
+    positions = [lengths_s[source_s[low + s]] + 1 for s in range(slots)]
+    for s, p in enumerate(positions):
+        place[slots + s] = p
+    gather_angles(lambda s: positions[s], slots, cos_ref, sin_ref, cos_rows, sin_rows)
     row = lax.broadcasted_iota(I32, (2 * HD, 2 * HD), 0)
     col = lax.broadcasted_iota(I32, (2 * HD, 2 * HD), 1)
     goal = jnp.where(row < HD, 2 * row, 2 * (row - HD) + 1)
@@ -391,14 +392,13 @@
 
 def second_kernel(
     peers, peers_tp, slots, heads,
-    meta, source_s, lengths_s, place, gain, cos_rows, sin_rows, wq, wkv, wo, _, *rest,
+    meta, place, gain, cos_rows, sin_rows, wq, wkv, wo, _, *rest,
 ):
     blocks, rest = rest[:peers_tp], rest[peers_tp:]
     box_hbm, rest = rest[: peers - 1], rest[peers - 1 :]
     attended_out, sends, cache = rest[0], rest[1:peers_tp], rest[peers_tp]
     normed3, query_rows, attended_rows, in_sem = rest[peers_tp + 1 :]
-    me, me_tp = meta[0], meta[1]
-    low = me * slots
+    me_tp = meta[1]
     width = gain.shape[1]
     shard = blocks[0].shape[1]
     loads = [
@@ -420,7 +420,7 @@
         [first * (shard // HD) for first in firsts],
         width,
     )
-    positions = [lengths_s[source_s[low + s]] + 1 for s in range(slots)]
+    positions = [place[slots + s] for s in range(slots)]
     for copy in loads:
         copy.wait()
     pair = project_from(normed3, wkv)
@@ -615,7 +615,7 @@
             jax.ShapeDtypeStruct((width, 2 * HD), BF16),
             row32,
             row32,
-            jax.ShapeDtypeStruct((slots,), I32),
+            jax.ShapeDtypeStruct((2 * slots,), I32),
         ],
         in_specs=[SMEM] * 4 + [VMEM] * 3 + [ANY],
         out_specs=[VMEM] * 3 + [SMEM],
@@ -627,7 +627,7 @@
     rows, *sends, cache = pl.pallas_call(
         functools.partial(second_kernel, peers, peers_tp, slots, heads),
         out_shape=[rows16] + sent + [held],
-        in_specs=[SMEM] * 4 + [VMEM] * (7 + peers_tp) + [ANY] * others,
+        in_specs=[SMEM] * 2 + [VMEM] * (7 + peers_tp) + [ANY] * others,
         out_specs=[VMEM] * (1 + peers_tp),
         scratch_shapes=[
             pltpu.VMEM((blocks, slots, HD), BF16),
@@ -635,11 +635,11 @@
             pltpu.VMEM((slots * GROUP, HD), F32),
             dma((others,)),
         ],
-        input_output_aliases={10: peers_tp},
+        input_output_aliases={8: peers_tp},
         compiler_params=params(16),
         cost_estimate=cost(3 * flops, cache_bytes + (query_weight.size + wkv.size) * 4),
         name="second_step",
-    )(meta, source, lengths, place, gain, cos_rows, sin_rows, query_weight, weight, out_weight, cache,
+    )(meta, place, gain, cos_rows, sin_rows, query_weight, weight, out_weight, cache,
       *pieces, *got_boxes)
     own = own_term(rows, pieces[0])
 

time: 66.1 us -> 65.7 us (level)
  no operation moved by 1% of the time
where the time goes in v20:
time: 65.7 us; the launch traced here: 65.6 us
  Pallas kernels  25.4 us (39%)
  starting transfers between devices  22.2 us (34%)
  waiting for transfers between devices  17.1 us (26%)
  between operations  0.84 us (1%)
    ppermute x17, starting transfers between devices, swapped(): return lax.ppermute(x, axis, [(i, i ^ k) for i in range(size)])  22.2 us
    ppermute x17, waiting for transfers between devices, swapped(): return lax.ppermute(x, axis, [(i, i ^ k) for i in range(size)])  17.1 us
    pallas_call x1, Pallas kernels, local(): pl.pallas_call(functools.partial(first_kernel, peers, slots, heads, shard...  6.67 us
    pallas_call x1, Pallas kernels, local(): pl.pallas_call(functools.partial(second_kernel, peers, peers_tp, slots, h...  4.7 us
    pallas_call x1, Pallas kernels, local(): pl.pallas_call(functools.partial(cache_kernel, slots), out_shape=jax.Shap...  3.58 us
    pallas_call x1, Pallas kernels, local(): pl.pallas_call(functools.partial(prepare_kernel, peers, slots), out_shape...  2.47 us
    pallas_call x1, Pallas kernels, local(): pl.pallas_call(functools.partial(attend_kernel, slots, heads), out_shape=...  2.36 us
    pallas_call x2, Pallas kernels, own_term(): pl.pallas_call(own_kernel, out_shape=own32, in_specs=[SMEM] + [VMEM] * 3,...  1.69 us
  transfers between devices with their start and end apart: 17, of which 7 were waited for; matrix products, arithmetic and copies ran while one was open for 0% of the time, Pallas kernels for 17%

profile of v20, /device:TPU:0, one launch (start us, length us, event | category | flops | bytes accessed | tf_op | source)
XLA Modules:
  0.0 65.6 jit_solution(7809874036238231566)
XLA Ops:
  0.6 0.1 pad_add_fusion.meta
  0.7 6.7 %first_step.1 = (f32[384,128]{1,0:T(8,128)S(1)}, f32[48,128]{1,0:T(8,128)S(1)}, f32[48,128]{1,0:T(8,128)S(1)}, s32[12]{0:T(128)S(1)}, bf16[54,2,256,128]{3,2,1,0...) custom-call(s32[2]{0:T(128)S(1)} %pad_add_fusion.meta, ...), custom_call_target="tpu_custom_call" | custom-call | flops 301989888 | bytes 6291456 | tf_op jit(solution)/shard_map/first_step/pallas_call | solution.py:501
  7.4 0.0 copy-start
  7.4 0.0 copy-start.3
  7.4 0.5 collective-permute-start
  7.9 2.6 %collective-permute-start.1 = (f32[2,1536]{1,0:T(2,128)S(1)}, f32[2,1536]{1,0:T(2,128)S(1)}, u32[]{:S(2)}, u32[]{:S(2)}) collective-permute-start(f32[2,1536]{1,0:T(2,128)S(1)} %get-tuple-element.35), channel_id=1, source_target_pairs={{0,8},{4,12},{8,0},{12,4},{1,9},{5,13},{9,1},{13,5},{2,10},{6,14},... | collective-permute-start | bytes 36872 | tf_op jit(solution)/shard_map/ppermute | solution.py:467
  10.5 0.1 collective-permute-start.2
  10.6 0.0 copy-done.7
  10.6 2.4 %attention.1 = (bf16[48,512]{1,0:T(8,128)(2,1)S(1)}, bf16[54,2,256,128]{3,2,1,0:T(8,128)(2,1)S(1)}) custom-call(s32[2]{0:T(128)S(1)} %pad_add_fusion.meta, s32[192]{0:T(256)S(1)} %copy-done.7, f32[384,128]{1,0:T(8,128)S(1)} %get-tuple-element.29.query, f32[48,128]{1,0:T(8,128)S(1)} %get-tuple-element.30.newkey, ...), custom_call_target="tpu_custom_call", output_to_operand_aliasing={{1}: (5, {})} | custom-call | flops 25165824 | bytes 6291456 | tf_op jit(solution)/shard_map/attention/pallas_call | solution.py:542
  13.0 0.0 collective-permute-done.1.rest_0_
  13.0 0.7 %collective-permute-done.2.rest_1_ = f32[2,1536]{1,0:T(2,128)S(1)} collective-permute-done((f32[2,1536]{1,0:T(2,128)S(1)}, f32[2,1536]{1,0:T(2,128)S(1)}, u32[]{:S(2)}, u32[]{:S(2)}) %collective-permute-start.2) | collective-permute-done | bytes 12320 | tf_op jit(solution)/shard_map/ppermute | solution.py:467
  13.6 0.0 collective-permute-done.box.rest_4_
  13.6 0.0 copy-done
  13.7 0.0 copy-done.3
  13.7 1.3 %out_projection.1 = (f32[48,1024]{1,0:T(8,128)S(1)}, bf16[48,512]{1,0:T(8,128)(2,1)S(1)}, bf16[48,1024]{1,0:T(8,128)(2,1)S(1)}, bf16[48,1024]{1,0:T(8,128)(2,1)S(1)}, bf16[48,1024]{1,0:T(8,128)(2,1)S(1)}) custom-call(s32[2]{0:T(128)S(1)} %pad_add_fusion.meta, s32[12]{0:T(128)S(1)} %get-tuple-element.28.plan, bf16[48,512]{1,0:T(8,128)(2,1)S(1)} %get-tuple-element.33.attended, ...), custom_call_target="tpu_custom_call" | custom-call | flops 201326592 | bytes 4194304 | tf_op jit(solution)/shard_map/out_projection/pallas_call | solution.py:569
  14.9 0.0 copy-start.2
  14.9 0.0 copy-start.4
  15.0 0.0 copy-start.5
  15.0 0.0 copy-start.8
  15.0 3.7 %collective-permute-start.3 = (bf16[48,1024]{1,0:T(8,128)(2,1)S(1)}, bf16[48,1024]{1,0:T(8,128)(2,1)S(1)}, u32[]{:S(2)}, u32[]{:S(2)}) collective-permute-start(bf16[48,1024]{1,0:T(8,128)(2,1)S(1)} %get-tuple-element.44), channel_id=1, source_target_pairs={{0,3},{1,2},{2,1},{3,0},{4,7},{5,6},{6,5},{7,4},{8,11},{9,10},{10,... | collective-permute-start | bytes 294920 | tf_op jit(solution)/shard_map/ppermute | solution.py:467
  18.6 0.0 collective-permute-start.4
  18.7 0.8 %collective-permute-start.5 = (bf16[48,1024]{1,0:T(8,128)(2,1)S(1)}, bf16[48,1024]{1,0:T(8,128)(2,1)S(1)}, u32[]{:S(2)}, u32[]{:S(2)}) collective-permute-start(bf16[48,1024]{1,0:T(8,128)(2,1)S(1)} %get-tuple-element.46), channel_id=1, source_target_pairs={{0,1},{1,0},{2,3},{3,2},{4,5},{5,4},{6,7},{7,6},{8,9},{9,8},{10,11... | collective-permute-start | bytes 294920 | tf_op jit(solution)/shard_map/ppermute | solution.py:467
  19.4 1.3 %pack.1 = (bf16[2,2,256,128]{3,2,1,0:T(8,128)(2,1)S(1)}, bf16[2,2,256,128]{3,2,1,0:T(8,128)(2,1)S(1)}) custom-call(s32[12]{0:T(128)S(1)} %get-tuple-element.28.plan, bf16[54,2,256,128]{3,2,1,0:T(8,128)(2,1)S(1)} %get-tuple-element.42.cache._, bf16[48,512]{1,0:T(8,128)(2,1)S(1)} %get-tuple-element.37._.attended._own), custom_call_target="tpu_custom_call" | custom-call | flops 1 | bytes 6291456 | tf_op jit(solution)/shard_map/pack/pallas_call | solution.py:579
  20.7 1.2 %collective-permute-start.9 = (bf16[2,2,256,128]{3,2,1,0:T(8,128)(2,1)S(1)}, bf16[2,2,256,128]{3,2,1,0:T(8,128)(2,1)S(1)}, u32[]{:S(2)}, u32[]{:S(2)}) collective-permute-start(bf16[2,2,256,128]{3,2,1,0:T(8,128)(2,1)S(1)} %get-tuple-element.47), channel_id=1, source_target_pairs={{0,8},{4,12},{8,0},{12,4},{1,9},{5,13},{9,1},{13,5},{2,10},{6,14},... | collective-permute-start | bytes 786440 | tf_op jit(solution)/shard_map/ppermute | solution.py:467
  21.9 0.0 collective-permute-start.10
  21.9 0.8 %own_term.2.own = f32[48,1024]{1,0:T(8,128)S(1)} custom-call(s32[2]{0:T(128)S(1)} %pad_add_fusion.meta, bf16[48,512]{1,0:T(8,128)(2,1)S(1)} %get-tuple-element.37._.attended._own, bf16[512,4096]{1,0:T(8,128)(2,1)S(1)} %copy-done, f32[48,1024]{1,0:T(8,128)S(1)} %get-tuple-element.43.residual), custom_call_target="tpu_custom_call" | custom-call | flops 50331648 | bytes 1048576 | tf_op jit(solution)/shard_map/own_term/pallas_call | solution.py:559
  22.7 0.0 collective-permute-done.3.rest_0_
  22.7 4.5 %collective-permute-done.4.rest_1_ = bf16[48,1024]{1,0:T(8,128)(2,1)S(1)} collective-permute-done((bf16[48,1024]{1,0:T(8,128)(2,1)S(1)}, bf16[48,1024]{1,0:T(8,128)(2,1)S(1)}, u32[]{:S(2)}, u32[]{:S(2)}) %collective-permute-start.4) | collective-permute-done | bytes 98336 | tf_op jit(solution)/shard_map/ppermute | solution.py:467
  27.2 0.0 collective-permute-done.5.rest_2_
  27.2 0.1 sum_terms.2.rest_0_.residual
  27.3 0.0 copy-start.1
  27.3 0.0 copy-start.6
  27.3 2.5 %collective-permute-start.8 = (bf16[48,1024]{1,0:T(8,128)(2,1)S(1)}, bf16[48,1024]{1,0:T(8,128)(2,1)S(1)}, u32[]{:S(2)}, u32[]{:S(2)}) collective-permute-start(bf16[48,1024]{1,0:T(8,128)(2,1)S(1)} %sum_terms.2.rest_0_.residual), channel_id=1, source_target_pairs={{0,3},{1,2},{2,1},{3,0},{4,7},{5,6},{6,5},{7,4},{8,11},{9,10},{10,... | collective-permute-start | bytes 294920 | tf_op jit(solution)/shard_map/ppermute | solution.py:467
  29.9 0.0 collective-permute-start.7
  29.9 1.9 %collective-permute-start.6 = (bf16[48,1024]{1,0:T(8,128)(2,1)S(1)}, bf16[48,1024]{1,0:T(8,128)(2,1)S(1)}, u32[]{:S(2)}, u32[]{:S(2)}) collective-permute-start(bf16[48,1024]{1,0:T(8,128)(2,1)S(1)} %sum_terms.2.rest_0_.residual), channel_id=1, source_target_pairs={{0,1},{1,0},{2,3},{3,2},{4,5},{5,4},{6,7},{7,6},{8,9},{9,8},{10,11... | collective-permute-start | bytes 294920 | tf_op jit(solution)/shard_map/ppermute | solution.py:467
  31.8 0.0 copy-done.2
  31.8 0.0 copy-done.4
  31.8 0.0 copy-done.5
  31.8 0.0 copy-done.8
  31.8 2.5 %prepare.1 = (bf16[4096,256]{1,0:T(8,128)(2,1)S(1)}, f32[48,128]{1,0:T(8,128)S(1)}, f32[48,128]{1,0:T(8,128)S(1)}, s32[96]{0:T(128)S(1)}) custom-call(s32[2]{0:T(128)S(1)} %pad_add_fusion.meta, s32[192]{0:T(256)S(1)} %copy-done.8, s32[192]{0:T(256)S(1)} %copy-done.7, s32[12]{0:T(128)S(1)} %get-tuple-element.28.plan, f32[256,128]{1,0:T(8,128)S(1)} %copy-done.5, ...), custom_call_target="tpu_custom_call" | custom-call | flops 30198988800 | bytes 41943040 | tf_op jit(solution)/shard_map/prepare/pallas_call | solution.py:612
  34.3 0.6 collective-permute-done.8.rest_3_
  34.9 3.4 %collective-permute-done.7.rest_2_ = bf16[48,1024]{1,0:T(8,128)(2,1)S(1)} collective-permute-done((bf16[48,1024]{1,0:T(8,128)(2,1)S(1)}, bf16[48,1024]{1,0:T(8,128)(2,1)S(1)}, u32[]{:S(2)}, u32[]{:S(2)}) %collective-permute-start.7) | collective-permute-done | bytes 98336 | tf_op jit(solution)/shard_map/ppermute | solution.py:467
  38.3 0.0 collective-permute-done.6.rest_1_
  38.3 0.0 collective-permute-done.9.rest_5_
  38.3 0.0 collective-permute-done.10.rest_6_
  38.3 0.0 copy-done.1
  38.3 0.0 copy-done.6
  38.3 4.7 %second_step.1 = (bf16[48,512]{1,0:T(8,128)(2,1)S(1)}, bf16[48,1024]{1,0:T(8,128)(2,1)S(1)}, bf16[48,1024]{1,0:T(8,128)(2,1)S(1)}, bf16[48,1024]{1,0:T(8,128)(2,1)S(1)}, bf16[54,2,256,128]{3,2,1,0:T(8,128)(2,1)S(1)}) custom-call(s32[2]{0:T(128)S(1)} %pad_add_fusion.meta, s32[96]{0:T(128)S(1)} %get-tuple-element.38.place, ...), custom_call_target="tpu_custom_call", output_to_operand_aliasing={{4}: (8, {})} | custom-call | flops 905969664 | bytes 18874368 | tf_op jit(solution)/shard_map/second_step/pallas_call | solution.py:627
  43.0 1.7 %collective-permute-start.11 = (bf16[48,1024]{1,0:T(8,128)(2,1)S(1)}, bf16[48,1024]{1,0:T(8,128)(2,1)S(1)}, u32[]{:S(2)}, u32[]{:S(2)}) collective-permute-start(bf16[48,1024]{1,0:T(8,128)(2,1)S(1)} %get-tuple-element.50), channel_id=1, source_target_pairs={{0,3},{1,2},{2,1},{3,0},{4,7},{5,6},{6,5},{7,4},{8,11},{9,10},{10,... | collective-permute-start | bytes 294920 | tf_op jit(solution)/shard_map/ppermute | solution.py:467
  44.8 0.0 collective-permute-start.12
  44.8 2.7 %collective-permute-start.13 = (bf16[48,1024]{1,0:T(8,128)(2,1)S(1)}, bf16[48,1024]{1,0:T(8,128)(2,1)S(1)}, u32[]{:S(2)}, u32[]{:S(2)}) collective-permute-start(bf16[48,1024]{1,0:T(8,128)(2,1)S(1)} %get-tuple-element.52), channel_id=1, source_target_pairs={{0,1},{1,0},{2,3},{3,2},{4,5},{5,4},{6,7},{7,6},{8,9},{9,8},{10,11... | collective-permute-start | bytes 294920 | tf_op jit(solution)/shard_map/ppermute | solution.py:467
  47.5 0.8 %own_term.3.own = f32[48,1024]{1,0:T(8,128)S(1)} custom-call(s32[2]{0:T(128)S(1)} %pad_add_fusion.meta, bf16[48,512]{1,0:T(8,128)(2,1)S(1)} %get-tuple-element.49.attended, bf16[512,4096]{1,0:T(8,128)(2,1)S(1)} %copy-done, bf16[48,1024]{1,0:T(8,128)(2,1)S(1)} %sum_terms.2.rest_0_.residual), custom_call_target="tpu_custom_call" | custom-call | flops 50331648 | bytes 1048576 | tf_op jit(solution)/shard_map/own_term/pallas_call | solution.py:559
  48.3 2.4 %collective-permute-done.11.rest_0_ = bf16[48,1024]{1,0:T(8,128)(2,1)S(1)} collective-permute-done((bf16[48,1024]{1,0:T(8,128)(2,1)S(1)}, bf16[48,1024]{1,0:T(8,128)(2,1)S(1)}, u32[]{:S(2)}, u32[]{:S(2)}) %collective-permute-start.11) | collective-permute-done | bytes 98336 | tf_op jit(solution)/shard_map/ppermute | solution.py:467
  50.7 2.6 %collective-permute-done.12.rest_1_ = bf16[48,1024]{1,0:T(8,128)(2,1)S(1)} collective-permute-done((bf16[48,1024]{1,0:T(8,128)(2,1)S(1)}, bf16[48,1024]{1,0:T(8,128)(2,1)S(1)}, u32[]{:S(2)}, u32[]{:S(2)}) %collective-permute-start.12) | collective-permute-done | bytes 98336 | tf_op jit(solution)/shard_map/ppermute | solution.py:467
  53.3 0.0 collective-permute-done.13.rest_2_
  53.3 0.1 sum_terms.3.rest_0_
  53.4 2.2 %collective-permute-start.16 = (bf16[48,1024]{1,0:T(8,128)(2,1)S(1)}, bf16[48,1024]{1,0:T(8,128)(2,1)S(1)}, u32[]{:S(2)}, u32[]{:S(2)}) collective-permute-start(bf16[48,1024]{1,0:T(8,128)(2,1)S(1)} %sum_terms.3.rest_0_), channel_id=1, source_target_pairs={{0,3},{1,2},{2,1},{3,0},{4,7},{5,6},{6,5},{7,4},{8,11},{9,10},{10,... | collective-permute-start | bytes 294920 | tf_op jit(solution)/shard_map/ppermute | solution.py:467
  55.6 0.0 collective-permute-start.15
  55.6 2.2 %collective-permute-start.14 = (bf16[48,1024]{1,0:T(8,128)(2,1)S(1)}, bf16[48,1024]{1,0:T(8,128)(2,1)S(1)}, u32[]{:S(2)}, u32[]{:S(2)}) collective-permute-start(bf16[48,1024]{1,0:T(8,128)(2,1)S(1)} %sum_terms.3.rest_0_), channel_id=1, source_target_pairs={{0,1},{1,0},{2,3},{3,2},{4,5},{5,4},{6,7},{7,6},{8,9},{9,8},{10,11... | collective-permute-start | bytes 294920 | tf_op jit(solution)/shard_map/ppermute | solution.py:467
  57.8 3.6 %write_cache.1 = bf16[48,2,256,128]{3,2,1,0:T(8,128)(2,1)} custom-call(s32[96]{0:T(128)S(1)} %get-tuple-element.38.place, bf16[54,2,256,128]{3,2,1,0:T(8,128)(2,1)S(1)} %get-tuple-element.53.cache), custom_call_target="tpu_custom_call" | custom-call | bytes 12582912 | tf_op jit(solution)/shard_map/write_cache/pallas_call | solution.py:647
  61.4 0.0 collective-permute-done.16.rest_3_
  61.4 2.8 %collective-permute-done.15.rest_2_ = bf16[48,1024]{1,0:T(8,128)(2,1)S(1)} collective-permute-done((bf16[48,1024]{1,0:T(8,128)(2,1)S(1)}, bf16[48,1024]{1,0:T(8,128)(2,1)S(1)}, u32[]{:S(2)}, u32[]{:S(2)}) %collective-permute-start.15) | collective-permute-done | bytes 98336 | tf_op jit(solution)/shard_map/ppermute | solution.py:467
  64.3 0.0 collective-permute-done.14.rest_1_
  64.3 1.3 %join.1 = bf16[48,4096]{1,0:T(8,128)(2,1)} custom-call(s32[2]{0:T(128)S(1)} %pad_add_fusion.meta, bf16[48,1024]{1,0:T(8,128)(2,1)S(1)} %sum_terms.3.rest_0_, bf16[48,1024]{1,0:T(8,128)(2,1)S(1)} %collective-permute-done.14.rest_1_, bf16[48,1024]{1,0:T(8,128)(2,1)S(1)} %collective-permute-done.15.rest_2_, bf16[48,1024]{1,0:T(8,128)(2,1)S(1)} %collective-permute-done.16.rest_3_), custom_call_target="tpu_custom_call" | custom-call | tf_op jit(solution)/shard_map/join/pallas_call | solution.py:657
  (1 shorter events, 0.0 us)
Async XLA Ops:
  0.7 9.9 %copy-start.7 = (s32[192]{0:T(256)S(1)}, s32[192]{0:T(256)}, u32[]{:S(2)}) copy-start(s32[192]{0:T(256)} %lengths_s.3) | copy-start | bytes 2308
  7.4 6.3 %copy-start = (bf16[512,4096]{1,0:T(8,128)(2,1)S(1)}, bf16[512,4096]{1,0:T(8,128)(2,1)}, u32[]{:S(2)}) copy-start(bf16[512,4096]{1,0:T(8,128)(2,1)} %wo.7) | copy-start | bytes 12582916
  7.4 6.3 %copy-start.3 = (bf16[48,4096]{1,0:T(8,128)(2,1)S(1)}, bf16[48,4096]{1,0:T(8,128)(2,1)}, u32[]{:S(2)}) copy-start(bf16[48,4096]{1,0:T(8,128)(2,1)} %hidden.1) | copy-start | bytes 1179652
  7.4 6.2 %collective-permute-start = (bf16[2,2,272,128]{3,2,1,0:T(8,128)(2,1)S(1)}, bf16[2,2,272,128]{3,2,1,0:T(8,128)(2,1)S(1)}, u32[]{:S(2)}, u32[]{:S(2)}) collective-permute-start(bf16[2,2,272,128]{3,2,1,0:T(8,128)(2,1)S(1)} %get-tuple-element.34), channel_id=1, source_target_pairs={{0,4},{4,0},{8,12},{12,8},{1,5},{5,1},{9,13},{13,9},{2,6},{6,2},{1... | collective-permute-start | bytes 835592 | tf_op jit(solution)/shard_map/ppermute | solution.py:467
  7.9 5.0 %collective-permute-start.1 = (f32[2,1536]{1,0:T(2,128)S(1)}, f32[2,1536]{1,0:T(2,128)S(1)}, u32[]{:S(2)}, u32[]{:S(2)}) collective-permute-start(f32[2,1536]{1,0:T(2,128)S(1)} %get-tuple-element.35), channel_id=1, source_target_pairs={{0,8},{4,12},{8,0},{12,4},{1,9},{5,13},{9,1},{13,5},{2,10},{6,14},... | collective-permute-start | bytes 36872 | tf_op jit(solution)/shard_map/ppermute | solution.py:467
  10.5 3.1 %collective-permute-start.2 = (f32[2,1536]{1,0:T(2,128)S(1)}, f32[2,1536]{1,0:T(2,128)S(1)}, u32[]{:S(2)}, u32[]{:S(2)}) collective-permute-start(f32[2,1536]{1,0:T(2,128)S(1)} %get-tuple-element.36), channel_id=1, source_target_pairs={{0,12},{4,8},{8,4},{12,0},{1,13},{5,9},{9,5},{13,1},{2,14},{6,10},... | collective-permute-start | bytes 36872 | tf_op jit(solution)/shard_map/ppermute | solution.py:467
  14.9 16.9 %copy-start.2 = (bf16[4096,2,128]{2,1,0:T(2,128)(2,1)S(1)}, bf16[4096,2,128]{2,1,0:T(2,128)(2,1)}, u32[]{:S(2)}) copy-start(bf16[4096,2,128]{2,1,0:T(2,128)(2,1)} %param.16) | copy-start | bytes 6291460
  14.9 16.8 %copy-start.4 = (f32[256,128]{1,0:T(8,128)S(1)}, f32[256,128]{1,0:T(8,128)}, u32[]{:S(2)}) copy-start(f32[256,128]{1,0:T(8,128)} %constant.12.clone.sin_hbm.sin_ref) | copy-start | bytes 393220
  15.0 16.8 %copy-start.5 = (f32[256,128]{1,0:T(8,128)S(1)}, f32[256,128]{1,0:T(8,128)}, u32[]{:S(2)}) copy-start(f32[256,128]{1,0:T(8,128)} %constant.11.clone.cos_hbm.cos_ref) | copy-start | bytes 393220
  15.0 16.8 %copy-start.8 = (s32[192]{0:T(256)S(1)}, s32[192]{0:T(256)}, u32[]{:S(2)}) copy-start(s32[192]{0:T(256)} %source_s.1) | copy-start | bytes 2308
  15.0 7.7 %collective-permute-start.3 = (bf16[48,1024]{1,0:T(8,128)(2,1)S(1)}, bf16[48,1024]{1,0:T(8,128)(2,1)S(1)}, u32[]{:S(2)}, u32[]{:S(2)}) collective-permute-start(bf16[48,1024]{1,0:T(8,128)(2,1)S(1)} %get-tuple-element.44), channel_id=1, source_target_pairs={{0,3},{1,2},{2,1},{3,0},{4,7},{5,6},{6,5},{7,4},{8,11},{9,10},{10,... | collective-permute-start | bytes 294920 | tf_op jit(solution)/shard_map/ppermute | solution.py:467
  18.6 8.6 %collective-permute-start.4 = (bf16[48,1024]{1,0:T(8,128)(2,1)S(1)}, bf16[48,1024]{1,0:T(8,128)(2,1)S(1)}, u32[]{:S(2)}, u32[]{:S(2)}) collective-permute-start(bf16[48,1024]{1,0:T(8,128)(2,1)S(1)} %get-tuple-element.45), channel_id=1, source_target_pairs={{0,2},{1,3},{2,0},{3,1},{4,6},{5,7},{6,4},{7,5},{8,10},{9,11},{10,... | collective-permute-start | bytes 294920 | tf_op jit(solution)/shard_map/ppermute | solution.py:467
  18.7 8.6 %collective-permute-start.5 = (bf16[48,1024]{1,0:T(8,128)(2,1)S(1)}, bf16[48,1024]{1,0:T(8,128)(2,1)S(1)}, u32[]{:S(2)}, u32[]{:S(2)}) collective-permute-start(bf16[48,1024]{1,0:T(8,128)(2,1)S(1)} %get-tuple-element.46), channel_id=1, source_target_pairs={{0,1},{1,0},{2,3},{3,2},{4,5},{5,4},{6,7},{7,6},{8,9},{9,8},{10,11... | collective-permute-start | bytes 294920 | tf_op jit(solution)/shard_map/ppermute | solution.py:467
  20.7 17.6 %collective-permute-start.9 = (bf16[2,2,256,128]{3,2,1,0:T(8,128)(2,1)S(1)}, bf16[2,2,256,128]{3,2,1,0:T(8,128)(2,1)S(1)}, u32[]{:S(2)}, u32[]{:S(2)}) collective-permute-start(bf16[2,2,256,128]{3,2,1,0:T(8,128)(2,1)S(1)} %get-tuple-element.47), channel_id=1, source_target_pairs={{0,8},{4,12},{8,0},{12,4},{1,9},{5,13},{9,1},{13,5},{2,10},{6,14},... | collective-permute-start | bytes 786440 | tf_op jit(solution)/shard_map/ppermute | solution.py:467
  21.9 16.4 %collective-permute-start.10 = (bf16[2,2,256,128]{3,2,1,0:T(8,128)(2,1)S(1)}, bf16[2,2,256,128]{3,2,1,0:T(8,128)(2,1)S(1)}, u32[]{:S(2)}, u32[]{:S(2)}) collective-permute-start(bf16[2,2,256,128]{3,2,1,0:T(8,128)(2,1)S(1)} %get-tuple-element.48), channel_id=1, source_target_pairs={{0,12},{4,8},{8,4},{12,0},{1,13},{5,9},{9,5},{13,1},{2,14},{6,10},... | collective-permute-start | bytes 786440 | tf_op jit(solution)/shard_map/ppermute | solution.py:467
  27.3 11.0 %copy-start.1 = (bf16[4096,512]{1,0:T(8,128)(2,1)S(1)}, bf16[4096,512]{1,0:T(8,128)(2,1)}, u32[]{:S(2)}) copy-start(bf16[4096,512]{1,0:T(8,128)(2,1)} %wq.1) | copy-start | bytes 12582916
  27.3 11.0 %copy-start.6 = (f32[4096]{0:T(1024)S(1)}, f32[4096]{0:T(1024)}, u32[]{:S(2)}) copy-start(f32[4096]{0:T(1024)} %param.14) | copy-start | bytes 49156
  27.3 7.6 %collective-permute-start.8 = (bf16[48,1024]{1,0:T(8,128)(2,1)S(1)}, bf16[48,1024]{1,0:T(8,128)(2,1)S(1)}, u32[]{:S(2)}, u32[]{:S(2)}) collective-permute-start(bf16[48,1024]{1,0:T(8,128)(2,1)S(1)} %sum_terms.2.rest_0_.residual), channel_id=1, source_target_pairs={{0,3},{1,2},{2,1},{3,0},{4,7},{5,6},{6,5},{7,4},{8,11},{9,10},{10,... | collective-permute-start | bytes 294920 | tf_op jit(solution)/shard_map/ppermute | solution.py:467
  29.9 8.4 %collective-permute-start.7 = (bf16[48,1024]{1,0:T(8,128)(2,1)S(1)}, bf16[48,1024]{1,0:T(8,128)(2,1)S(1)}, u32[]{:S(2)}, u32[]{:S(2)}) collective-permute-start(bf16[48,1024]{1,0:T(8,128)(2,1)S(1)} %sum_terms.2.rest_0_.residual), channel_id=1, source_target_pairs={{0,2},{1,3},{2,0},{3,1},{4,6},{5,7},{6,4},{7,5},{8,10},{9,11},{10,... | collective-permute-start | bytes 294920 | tf_op jit(solution)/shard_map/ppermute | solution.py:467
  29.9 8.4 %collective-permute-start.6 = (bf16[48,1024]{1,0:T(8,128)(2,1)S(1)}, bf16[48,1024]{1,0:T(8,128)(2,1)S(1)}, u32[]{:S(2)}, u32[]{:S(2)}) collective-permute-start(bf16[48,1024]{1,0:T(8,128)(2,1)S(1)} %sum_terms.2.rest_0_.residual), channel_id=1, source_target_pairs={{0,1},{1,0},{2,3},{3,2},{4,5},{5,4},{6,7},{7,6},{8,9},{9,8},{10,11... | collective-permute-start | bytes 294920 | tf_op jit(solution)/shard_map/ppermute | solution.py:467
  43.0 7.7 %collective-permute-start.11 = (bf16[48,1024]{1,0:T(8,128)(2,1)S(1)}, bf16[48,1024]{1,0:T(8,128)(2,1)S(1)}, u32[]{:S(2)}, u32[]{:S(2)}) collective-permute-start(bf16[48,1024]{1,0:T(8,128)(2,1)S(1)} %get-tuple-element.50), channel_id=1, source_target_pairs={{0,3},{1,2},{2,1},{3,0},{4,7},{5,6},{6,5},{7,4},{8,11},{9,10},{10,... | collective-permute-start | bytes 294920 | tf_op jit(solution)/shard_map/ppermute | solution.py:467
  44.8 8.6 %collective-permute-start.12 = (bf16[48,1024]{1,0:T(8,128)(2,1)S(1)}, bf16[48,1024]{1,0:T(8,128)(2,1)S(1)}, u32[]{:S(2)}, u32[]{:S(2)}) collective-permute-start(bf16[48,1024]{1,0:T(8,128)(2,1)S(1)} %get-tuple-element.51), channel_id=1, source_target_pairs={{0,2},{1,3},{2,0},{3,1},{4,6},{5,7},{6,4},{7,5},{8,10},{9,11},{10,... | collective-permute-start | bytes 294920 | tf_op jit(solution)/shard_map/ppermute | solution.py:467
  44.8 8.6 %collective-permute-start.13 = (bf16[48,1024]{1,0:T(8,128)(2,1)S(1)}, bf16[48,1024]{1,0:T(8,128)(2,1)S(1)}, u32[]{:S(2)}, u32[]{:S(2)}) collective-permute-start(bf16[48,1024]{1,0:T(8,128)(2,1)S(1)} %get-tuple-element.52), channel_id=1, source_target_pairs={{0,1},{1,0},{2,3},{3,2},{4,5},{5,4},{6,7},{7,6},{8,9},{9,8},{10,11... | collective-permute-start | bytes 294920 | tf_op jit(solution)/shard_map/ppermute | solution.py:467
  53.4 8.0 %collective-permute-start.16 = (bf16[48,1024]{1,0:T(8,128)(2,1)S(1)}, bf16[48,1024]{1,0:T(8,128)(2,1)S(1)}, u32[]{:S(2)}, u32[]{:S(2)}) collective-permute-start(bf16[48,1024]{1,0:T(8,128)(2,1)S(1)} %sum_terms.3.rest_0_), channel_id=1, source_target_pairs={{0,3},{1,2},{2,1},{3,0},{4,7},{5,6},{6,5},{7,4},{8,11},{9,10},{10,... | collective-permute-start | bytes 294920 | tf_op jit(solution)/shard_map/ppermute | solution.py:467
  55.6 8.7 %collective-permute-start.15 = (bf16[48,1024]{1,0:T(8,128)(2,1)S(1)}, bf16[48,1024]{1,0:T(8,128)(2,1)S(1)}, u32[]{:S(2)}, u32[]{:S(2)}) collective-permute-start(bf16[48,1024]{1,0:T(8,128)(2,1)S(1)} %sum_terms.3.rest_0_), channel_id=1, source_target_pairs={{0,2},{1,3},{2,0},{3,1},{4,6},{5,7},{6,4},{7,5},{8,10},{9,11},{10,... | collective-permute-start | bytes 294920 | tf_op jit(solution)/shard_map/ppermute | solution.py:467
  55.6 8.7 %collective-permute-start.14 = (bf16[48,1024]{1,0:T(8,128)(2,1)S(1)}, bf16[48,1024]{1,0:T(8,128)(2,1)S(1)}, u32[]{:S(2)}, u32[]{:S(2)}) collective-permute-start(bf16[48,1024]{1,0:T(8,128)(2,1)S(1)} %sum_terms.3.rest_0_), channel_id=1, source_target_pairs={{0,1},{1,0},{2,3},{3,2},{4,5},{5,4},{6,7},{7,6},{8,9},{9,8},{10,11... | collective-permute-start | bytes 294920 | tf_op jit(solution)/shard_map/ppermute | solution.py:467

commit v21 on v20

--- a/solution.py
+++ b/solution.py
@@ -15,7 +15,7 @@
 GROUP = 8
 PIECE = 16
 CHUNK = 8
-BATCH = 24
+BATCH = 48
 NOTE = 16
 
 F32 = jnp.float32

time: 65.7 us -> 65.6 us (level)
  no operation moved by 1% of the time
where the time goes in v21:
time: 65.6 us; the launch traced here: 65.4 us
  Pallas kernels  25.1 us (38%)
  starting transfers between devices  22 us (34%)
  waiting for transfers between devices  17.4 us (27%)
  between operations  0.83 us (1%)
    ppermute x17, starting transfers between devices, swapped(): return lax.ppermute(x, axis, [(i, i ^ k) for i in range(size)])  22 us
    ppermute x17, waiting for transfers between devices, swapped(): return lax.ppermute(x, axis, [(i, i ^ k) for i in range(size)])  17.4 us
    pallas_call x1, Pallas kernels, local(): pl.pallas_call(functools.partial(first_kernel, peers, slots, heads, shard...  6.67 us
    pallas_call x1, Pallas kernels, local(): pl.pallas_call(functools.partial(second_kernel, peers, peers_tp, slots, h...  4.54 us
    pallas_call x1, Pallas kernels, local(): pl.pallas_call(functools.partial(cache_kernel, slots), out_shape=jax.Shap...  3.58 us
    pallas_call x1, Pallas kernels, local(): pl.pallas_call(functools.partial(prepare_kernel, peers, slots), out_shape...  2.47 us
    pallas_call x1, Pallas kernels, local(): pl.pallas_call(functools.partial(attend_kernel, slots, heads), out_shape=...  2.21 us
    pallas_call x2, Pallas kernels, own_term(): pl.pallas_call(own_kernel, out_shape=own32, in_specs=[SMEM] + [VMEM] * 3,...  1.69 us
  transfers between devices with their start and end apart: 17, of which 7 were waited for; matrix products, arithmetic and copies ran while one was open for 0% of the time, Pallas kernels for 17%

profile of v21, /device:TPU:0, one launch (start us, length us, event | category | flops | bytes accessed | tf_op | source)
XLA Modules:
  0.0 65.4 jit_solution(18038112415703373548)
XLA Ops:
  0.6 0.1 pad_add_fusion.meta
  0.7 6.7 %first_step.1 = (f32[384,128]{1,0:T(8,128)S(1)}, f32[48,128]{1,0:T(8,128)S(1)}, f32[48,128]{1,0:T(8,128)S(1)}, s32[12]{0:T(128)S(1)}, bf16[54,2,256,128]{3,2,1,0...) custom-call(s32[2]{0:T(128)S(1)} %pad_add_fusion.meta, ...), custom_call_target="tpu_custom_call" | custom-call | flops 301989888 | bytes 6291456 | tf_op jit(solution)/shard_map/first_step/pallas_call | solution.py:501
  7.4 0.0 copy-start
  7.4 0.0 copy-start.3
  7.4 0.5 collective-permute-start
  7.9 2.6 %collective-permute-start.1 = (f32[2,1536]{1,0:T(2,128)S(1)}, f32[2,1536]{1,0:T(2,128)S(1)}, u32[]{:S(2)}, u32[]{:S(2)}) collective-permute-start(f32[2,1536]{1,0:T(2,128)S(1)} %get-tuple-element.35), channel_id=1, source_target_pairs={{0,8},{4,12},{8,0},{12,4},{1,9},{5,13},{9,1},{13,5},{2,10},{6,14},... | collective-permute-start | bytes 36872 | tf_op jit(solution)/shard_map/ppermute | solution.py:467
  10.5 0.1 collective-permute-start.2
  10.6 0.0 copy-done.7
  10.6 2.2 %attention.1 = (bf16[48,512]{1,0:T(8,128)(2,1)S(1)}, bf16[54,2,256,128]{3,2,1,0:T(8,128)(2,1)S(1)}) custom-call(s32[2]{0:T(128)S(1)} %pad_add_fusion.meta, s32[192]{0:T(256)S(1)} %copy-done.7, f32[384,128]{1,0:T(8,128)S(1)} %get-tuple-element.29.query, f32[48,128]{1,0:T(8,128)S(1)} %get-tuple-element.30.newkey, ...), custom_call_target="tpu_custom_call", output_to_operand_aliasing={{1}: (5, {})} | custom-call | flops 25165824 | bytes 6291456 | tf_op jit(solution)/shard_map/attention/pallas_call | solution.py:542
  12.8 0.0 collective-permute-done.1.rest_0_
  12.8 0.8 %collective-permute-done.2.rest_1_ = f32[2,1536]{1,0:T(2,128)S(1)} collective-permute-done((f32[2,1536]{1,0:T(2,128)S(1)}, f32[2,1536]{1,0:T(2,128)S(1)}, u32[]{:S(2)}, u32[]{:S(2)}) %collective-permute-start.2) | collective-permute-done | bytes 12320 | tf_op jit(solution)/shard_map/ppermute | solution.py:467
  13.6 0.0 collective-permute-done.box.rest_4_
  13.6 0.0 copy-done
  13.7 0.0 copy-done.3
  13.7 1.3 %out_projection.1 = (f32[48,1024]{1,0:T(8,128)S(1)}, bf16[48,512]{1,0:T(8,128)(2,1)S(1)}, bf16[48,1024]{1,0:T(8,128)(2,1)S(1)}, bf16[48,1024]{1,0:T(8,128)(2,1)S(1)}, bf16[48,1024]{1,0:T(8,128)(2,1)S(1)}) custom-call(s32[2]{0:T(128)S(1)} %pad_add_fusion.meta, s32[12]{0:T(128)S(1)} %get-tuple-element.28.plan, bf16[48,512]{1,0:T(8,128)(2,1)S(1)} %get-tuple-element.33.attended, ...), custom_call_target="tpu_custom_call" | custom-call | flops 201326592 | bytes 4194304 | tf_op jit(solution)/shard_map/out_projection/pallas_call | solution.py:569
  14.9 0.0 copy-start.2
  14.9 0.0 copy-start.4
  15.0 0.0 copy-start.5
  15.0 0.0 copy-start.8
  15.0 3.7 %collective-permute-start.3 = (bf16[48,1024]{1,0:T(8,128)(2,1)S(1)}, bf16[48,1024]{1,0:T(8,128)(2,1)S(1)}, u32[]{:S(2)}, u32[]{:S(2)}) collective-permute-start(bf16[48,1024]{1,0:T(8,128)(2,1)S(1)} %get-tuple-element.44), channel_id=1, source_target_pairs={{0,3},{1,2},{2,1},{3,0},{4,7},{5,6},{6,5},{7,4},{8,11},{9,10},{10,... | collective-permute-start | bytes 294920 | tf_op jit(solution)/shard_map/ppermute | solution.py:467
  18.6 0.0 collective-permute-start.4
  18.7 0.8 %collective-permute-start.5 = (bf16[48,1024]{1,0:T(8,128)(2,1)S(1)}, bf16[48,1024]{1,0:T(8,128)(2,1)S(1)}, u32[]{:S(2)}, u32[]{:S(2)}) collective-permute-start(bf16[48,1024]{1,0:T(8,128)(2,1)S(1)} %get-tuple-element.46), channel_id=1, source_target_pairs={{0,1},{1,0},{2,3},{3,2},{4,5},{5,4},{6,7},{7,6},{8,9},{9,8},{10,11... | collective-permute-start | bytes 294920 | tf_op jit(solution)/shard_map/ppermute | solution.py:467
  19.4 1.3 %pack.1 = (bf16[2,2,256,128]{3,2,1,0:T(8,128)(2,1)S(1)}, bf16[2,2,256,128]{3,2,1,0:T(8,128)(2,1)S(1)}) custom-call(s32[12]{0:T(128)S(1)} %get-tuple-element.28.plan, bf16[54,2,256,128]{3,2,1,0:T(8,128)(2,1)S(1)} %get-tuple-element.42.cache._, bf16[48,512]{1,0:T(8,128)(2,1)S(1)} %get-tuple-element.37._.attended._own), custom_call_target="tpu_custom_call" | custom-call | flops 1 | bytes 6291456 | tf_op jit(solution)/shard_map/pack/pallas_call | solution.py:579
  20.7 1.0 %collective-permute-start.9 = (bf16[2,2,256,128]{3,2,1,0:T(8,128)(2,1)S(1)}, bf16[2,2,256,128]{3,2,1,0:T(8,128)(2,1)S(1)}, u32[]{:S(2)}, u32[]{:S(2)}) collective-permute-start(bf16[2,2,256,128]{3,2,1,0:T(8,128)(2,1)S(1)} %get-tuple-element.47), channel_id=1, source_target_pairs={{0,8},{4,12},{8,0},{12,4},{1,9},{5,13},{9,1},{13,5},{2,10},{6,14},... | collective-permute-start | bytes 786440 | tf_op jit(solution)/shard_map/ppermute | solution.py:467
  21.7 0.0 collective-permute-start.10
  21.7 0.8 %own_term.2.own = f32[48,1024]{1,0:T(8,128)S(1)} custom-call(s32[2]{0:T(128)S(1)} %pad_add_fusion.meta, bf16[48,512]{1,0:T(8,128)(2,1)S(1)} %get-tuple-element.37._.attended._own, bf16[512,4096]{1,0:T(8,128)(2,1)S(1)} %copy-done, f32[48,1024]{1,0:T(8,128)S(1)} %get-tuple-element.43.residual), custom_call_target="tpu_custom_call" | custom-call | flops 50331648 | bytes 1048576 | tf_op jit(solution)/shard_map/own_term/pallas_call | solution.py:559
  22.6 0.0 collective-permute-done.3.rest_0_
  22.6 4.7 %collective-permute-done.4.rest_1_ = bf16[48,1024]{1,0:T(8,128)(2,1)S(1)} collective-permute-done((bf16[48,1024]{1,0:T(8,128)(2,1)S(1)}, bf16[48,1024]{1,0:T(8,128)(2,1)S(1)}, u32[]{:S(2)}, u32[]{:S(2)}) %collective-permute-start.4) | collective-permute-done | bytes 98336 | tf_op jit(solution)/shard_map/ppermute | solution.py:467
  27.2 0.0 collective-permute-done.5.rest_2_
  27.2 0.1 sum_terms.2.rest_0_.residual
  27.3 0.0 copy-start.1
  27.3 0.0 copy-start.6
  27.3 2.5 %collective-permute-start.8 = (bf16[48,1024]{1,0:T(8,128)(2,1)S(1)}, bf16[48,1024]{1,0:T(8,128)(2,1)S(1)}, u32[]{:S(2)}, u32[]{:S(2)}) collective-permute-start(bf16[48,1024]{1,0:T(8,128)(2,1)S(1)} %sum_terms.2.rest_0_.residual), channel_id=1, source_target_pairs={{0,3},{1,2},{2,1},{3,0},{4,7},{5,6},{6,5},{7,4},{8,11},{9,10},{10,... | collective-permute-start | bytes 294920 | tf_op jit(solution)/shard_map/ppermute | solution.py:467
  29.9 0.0 collective-permute-start.7
  29.9 1.9 %collective-permute-start.6 = (bf16[48,1024]{1,0:T(8,128)(2,1)S(1)}, bf16[48,1024]{1,0:T(8,128)(2,1)S(1)}, u32[]{:S(2)}, u32[]{:S(2)}) collective-permute-start(bf16[48,1024]{1,0:T(8,128)(2,1)S(1)} %sum_terms.2.rest_0_.residual), channel_id=1, source_target_pairs={{0,1},{1,0},{2,3},{3,2},{4,5},{5,4},{6,7},{7,6},{8,9},{9,8},{10,11... | collective-permute-start | bytes 294920 | tf_op jit(solution)/shard_map/ppermute | solution.py:467
  31.8 0.0 copy-done.2
  31.8 0.0 copy-done.4
  31.8 0.0 copy-done.5
  31.8 0.0 copy-done.8
  31.8 2.5 %prepare.1 = (bf16[4096,256]{1,0:T(8,128)(2,1)S(1)}, f32[48,128]{1,0:T(8,128)S(1)}, f32[48,128]{1,0:T(8,128)S(1)}, s32[96]{0:T(128)S(1)}) custom-call(s32[2]{0:T(128)S(1)} %pad_add_fusion.meta, s32[192]{0:T(256)S(1)} %copy-done.8, s32[192]{0:T(256)S(1)} %copy-done.7, s32[12]{0:T(128)S(1)} %get-tuple-element.28.plan, f32[256,128]{1,0:T(8,128)S(1)} %copy-done.5, ...), custom_call_target="tpu_custom_call" | custom-call | flops 30198988800 | bytes 41943040 | tf_op jit(solution)/shard_map/prepare/pallas_call | solution.py:612
  34.3 0.6 collective-permute-done.8.rest_3_
  34.9 3.4 %collective-permute-done.7.rest_2_ = bf16[48,1024]{1,0:T(8,128)(2,1)S(1)} collective-permute-done((bf16[48,1024]{1,0:T(8,128)(2,1)S(1)}, bf16[48,1024]{1,0:T(8,128)(2,1)S(1)}, u32[]{:S(2)}, u32[]{:S(2)}) %collective-permute-start.7) | collective-permute-done | bytes 98336 | tf_op jit(solution)/shard_map/ppermute | solution.py:467
  38.3 0.0 collective-permute-done.6.rest_1_
  38.3 0.0 collective-permute-done.9.rest_5_
  38.3 0.0 collective-permute-done.10.rest_6_
  38.3 0.0 copy-done.1
  38.3 0.0 copy-done.6
  38.3 4.5 %second_step.1 = (bf16[48,512]{1,0:T(8,128)(2,1)S(1)}, bf16[48,1024]{1,0:T(8,128)(2,1)S(1)}, bf16[48,1024]{1,0:T(8,128)(2,1)S(1)}, bf16[48,1024]{1,0:T(8,128)(2,1)S(1)}, bf16[54,2,256,128]{3,2,1,0:T(8,128)(2,1)S(1)}) custom-call(s32[2]{0:T(128)S(1)} %pad_add_fusion.meta, s32[96]{0:T(128)S(1)} %get-tuple-element.38.place, ...), custom_call_target="tpu_custom_call", output_to_operand_aliasing={{4}: (8, {})} | custom-call | flops 905969664 | bytes 18874368 | tf_op jit(solution)/shard_map/second_step/pallas_call | solution.py:627
  42.9 1.7 %collective-permute-start.11 = (bf16[48,1024]{1,0:T(8,128)(2,1)S(1)}, bf16[48,1024]{1,0:T(8,128)(2,1)S(1)}, u32[]{:S(2)}, u32[]{:S(2)}) collective-permute-start(bf16[48,1024]{1,0:T(8,128)(2,1)S(1)} %get-tuple-element.50), channel_id=1, source_target_pairs={{0,3},{1,2},{2,1},{3,0},{4,7},{5,6},{6,5},{7,4},{8,11},{9,10},{10,... | collective-permute-start | bytes 294920 | tf_op jit(solution)/shard_map/ppermute | solution.py:467
  44.6 0.0 collective-permute-start.12
  44.6 2.7 %collective-permute-start.13 = (bf16[48,1024]{1,0:T(8,128)(2,1)S(1)}, bf16[48,1024]{1,0:T(8,128)(2,1)S(1)}, u32[]{:S(2)}, u32[]{:S(2)}) collective-permute-start(bf16[48,1024]{1,0:T(8,128)(2,1)S(1)} %get-tuple-element.52), channel_id=1, source_target_pairs={{0,1},{1,0},{2,3},{3,2},{4,5},{5,4},{6,7},{7,6},{8,9},{9,8},{10,11... | collective-permute-start | bytes 294920 | tf_op jit(solution)/shard_map/ppermute | solution.py:467
  47.3 0.8 %own_term.3.own = f32[48,1024]{1,0:T(8,128)S(1)} custom-call(s32[2]{0:T(128)S(1)} %pad_add_fusion.meta, bf16[48,512]{1,0:T(8,128)(2,1)S(1)} %get-tuple-element.49.attended, bf16[512,4096]{1,0:T(8,128)(2,1)S(1)} %copy-done, bf16[48,1024]{1,0:T(8,128)(2,1)S(1)} %sum_terms.2.rest_0_.residual), custom_call_target="tpu_custom_call" | custom-call | flops 50331648 | bytes 1048576 | tf_op jit(solution)/shard_map/own_term/pallas_call | solution.py:559
  48.2 2.4 %collective-permute-done.11.rest_0_ = bf16[48,1024]{1,0:T(8,128)(2,1)S(1)} collective-permute-done((bf16[48,1024]{1,0:T(8,128)(2,1)S(1)}, bf16[48,1024]{1,0:T(8,128)(2,1)S(1)}, u32[]{:S(2)}, u32[]{:S(2)}) %collective-permute-start.11) | collective-permute-done | bytes 98336 | tf_op jit(solution)/shard_map/ppermute | solution.py:467
  50.5 2.6 %collective-permute-done.12.rest_1_ = bf16[48,1024]{1,0:T(8,128)(2,1)S(1)} collective-permute-done((bf16[48,1024]{1,0:T(8,128)(2,1)S(1)}, bf16[48,1024]{1,0:T(8,128)(2,1)S(1)}, u32[]{:S(2)}, u32[]{:S(2)}) %collective-permute-start.12) | collective-permute-done | bytes 98336 | tf_op jit(solution)/shard_map/ppermute | solution.py:467
  53.2 0.0 collective-permute-done.13.rest_2_
  53.2 0.1 sum_terms.3.rest_0_
  53.2 2.2 %collective-permute-start.16 = (bf16[48,1024]{1,0:T(8,128)(2,1)S(1)}, bf16[48,1024]{1,0:T(8,128)(2,1)S(1)}, u32[]{:S(2)}, u32[]{:S(2)}) collective-permute-start(bf16[48,1024]{1,0:T(8,128)(2,1)S(1)} %sum_terms.3.rest_0_), channel_id=1, source_target_pairs={{0,3},{1,2},{2,1},{3,0},{4,7},{5,6},{6,5},{7,4},{8,11},{9,10},{10,... | collective-permute-start | bytes 294920 | tf_op jit(solution)/shard_map/ppermute | solution.py:467
  55.5 0.0 collective-permute-start.15
  55.5 2.2 %collective-permute-start.14 = (bf16[48,1024]{1,0:T(8,128)(2,1)S(1)}, bf16[48,1024]{1,0:T(8,128)(2,1)S(1)}, u32[]{:S(2)}, u32[]{:S(2)}) collective-permute-start(bf16[48,1024]{1,0:T(8,128)(2,1)S(1)} %sum_terms.3.rest_0_), channel_id=1, source_target_pairs={{0,1},{1,0},{2,3},{3,2},{4,5},{5,4},{6,7},{7,6},{8,9},{9,8},{10,11... | collective-permute-start | bytes 294920 | tf_op jit(solution)/shard_map/ppermute | solution.py:467
  57.7 3.6 %write_cache.1 = bf16[48,2,256,128]{3,2,1,0:T(8,128)(2,1)} custom-call(s32[96]{0:T(128)S(1)} %get-tuple-element.38.place, bf16[54,2,256,128]{3,2,1,0:T(8,128)(2,1)S(1)} %get-tuple-element.53.cache), custom_call_target="tpu_custom_call" | custom-call | bytes 12582912 | tf_op jit(solution)/shard_map/write_cache/pallas_call | solution.py:647
  61.3 0.0 collective-permute-done.16.rest_3_
  61.3 2.8 %collective-permute-done.15.rest_2_ = bf16[48,1024]{1,0:T(8,128)(2,1)S(1)} collective-permute-done((bf16[48,1024]{1,0:T(8,128)(2,1)S(1)}, bf16[48,1024]{1,0:T(8,128)(2,1)S(1)}, u32[]{:S(2)}, u32[]{:S(2)}) %collective-permute-start.15) | collective-permute-done | bytes 98336 | tf_op jit(solution)/shard_map/ppermute | solution.py:467
  64.1 0.0 collective-permute-done.14.rest_1_
  64.1 1.3 %join.1 = bf16[48,4096]{1,0:T(8,128)(2,1)} custom-call(s32[2]{0:T(128)S(1)} %pad_add_fusion.meta, bf16[48,1024]{1,0:T(8,128)(2,1)S(1)} %sum_terms.3.rest_0_, bf16[48,1024]{1,0:T(8,128)(2,1)S(1)} %collective-permute-done.14.rest_1_, bf16[48,1024]{1,0:T(8,128)(2,1)S(1)} %collective-permute-done.15.rest_2_, bf16[48,1024]{1,0:T(8,128)(2,1)S(1)} %collective-permute-done.16.rest_3_), custom_call_target="tpu_custom_call" | custom-call | tf_op jit(solution)/shard_map/join/pallas_call | solution.py:657
  (1 shorter events, 0.0 us)
Async XLA Ops:
  0.7 9.9 %copy-start.7 = (s32[192]{0:T(256)S(1)}, s32[192]{0:T(256)}, u32[]{:S(2)}) copy-start(s32[192]{0:T(256)} %lengths_s.3) | copy-start | bytes 2308
  7.4 6.3 %copy-start = (bf16[512,4096]{1,0:T(8,128)(2,1)S(1)}, bf16[512,4096]{1,0:T(8,128)(2,1)}, u32[]{:S(2)}) copy-start(bf16[512,4096]{1,0:T(8,128)(2,1)} %wo.7) | copy-start | bytes 12582916
  7.4 6.3 %copy-start.3 = (bf16[48,4096]{1,0:T(8,128)(2,1)S(1)}, bf16[48,4096]{1,0:T(8,128)(2,1)}, u32[]{:S(2)}) copy-start(bf16[48,4096]{1,0:T(8,128)(2,1)} %hidden.1) | copy-start | bytes 1179652
  7.4 6.2 %collective-permute-start = (bf16[2,2,272,128]{3,2,1,0:T(8,128)(2,1)S(1)}, bf16[2,2,272,128]{3,2,1,0:T(8,128)(2,1)S(1)}, u32[]{:S(2)}, u32[]{:S(2)}) collective-permute-start(bf16[2,2,272,128]{3,2,1,0:T(8,128)(2,1)S(1)} %get-tuple-element.34), channel_id=1, source_target_pairs={{0,4},{4,0},{8,12},{12,8},{1,5},{5,1},{9,13},{13,9},{2,6},{6,2},{1... | collective-permute-start | bytes 835592 | tf_op jit(solution)/shard_map/ppermute | solution.py:467
  7.9 4.9 %collective-permute-start.1 = (f32[2,1536]{1,0:T(2,128)S(1)}, f32[2,1536]{1,0:T(2,128)S(1)}, u32[]{:S(2)}, u32[]{:S(2)}) collective-permute-start(f32[2,1536]{1,0:T(2,128)S(1)} %get-tuple-element.35), channel_id=1, source_target_pairs={{0,8},{4,12},{8,0},{12,4},{1,9},{5,13},{9,1},{13,5},{2,10},{6,14},... | collective-permute-start | bytes 36872 | tf_op jit(solution)/shard_map/ppermute | solution.py:467
  10.5 3.1 %collective-permute-start.2 = (f32[2,1536]{1,0:T(2,128)S(1)}, f32[2,1536]{1,0:T(2,128)S(1)}, u32[]{:S(2)}, u32[]{:S(2)}) collective-permute-start(f32[2,1536]{1,0:T(2,128)S(1)} %get-tuple-element.36), channel_id=1, source_target_pairs={{0,12},{4,8},{8,4},{12,0},{1,13},{5,9},{9,5},{13,1},{2,14},{6,10},... | collective-permute-start | bytes 36872 | tf_op jit(solution)/shard_map/ppermute | solution.py:467
  14.9 16.9 %copy-start.2 = (bf16[4096,2,128]{2,1,0:T(2,128)(2,1)S(1)}, bf16[4096,2,128]{2,1,0:T(2,128)(2,1)}, u32[]{:S(2)}) copy-start(bf16[4096,2,128]{2,1,0:T(2,128)(2,1)} %param.16) | copy-start | bytes 6291460
  14.9 16.8 %copy-start.4 = (f32[256,128]{1,0:T(8,128)S(1)}, f32[256,128]{1,0:T(8,128)}, u32[]{:S(2)}) copy-start(f32[256,128]{1,0:T(8,128)} %constant.12.clone.sin_hbm.sin_ref) | copy-start | bytes 393220
  15.0 16.8 %copy-start.5 = (f32[256,128]{1,0:T(8,128)S(1)}, f32[256,128]{1,0:T(8,128)}, u32[]{:S(2)}) copy-start(f32[256,128]{1,0:T(8,128)} %constant.11.clone.cos_hbm.cos_ref) | copy-start | bytes 393220
  15.0 16.8 %copy-start.8 = (s32[192]{0:T(256)S(1)}, s32[192]{0:T(256)}, u32[]{:S(2)}) copy-start(s32[192]{0:T(256)} %source_s.1) | copy-start | bytes 2308
  15.0 7.6 %collective-permute-start.3 = (bf16[48,1024]{1,0:T(8,128)(2,1)S(1)}, bf16[48,1024]{1,0:T(8,128)(2,1)S(1)}, u32[]{:S(2)}, u32[]{:S(2)}) collective-permute-start(bf16[48,1024]{1,0:T(8,128)(2,1)S(1)} %get-tuple-element.44), channel_id=1, source_target_pairs={{0,3},{1,2},{2,1},{3,0},{4,7},{5,6},{6,5},{7,4},{8,11},{9,10},{10,... | collective-permute-start | bytes 294920 | tf_op jit(solution)/shard_map/ppermute | solution.py:467
  18.6 8.6 %collective-permute-start.4 = (bf16[48,1024]{1,0:T(8,128)(2,1)S(1)}, bf16[48,1024]{1,0:T(8,128)(2,1)S(1)}, u32[]{:S(2)}, u32[]{:S(2)}) collective-permute-start(bf16[48,1024]{1,0:T(8,128)(2,1)S(1)} %get-tuple-element.45), channel_id=1, source_target_pairs={{0,2},{1,3},{2,0},{3,1},{4,6},{5,7},{6,4},{7,5},{8,10},{9,11},{10,... | collective-permute-start | bytes 294920 | tf_op jit(solution)/shard_map/ppermute | solution.py:467
  18.7 8.6 %collective-permute-start.5 = (bf16[48,1024]{1,0:T(8,128)(2,1)S(1)}, bf16[48,1024]{1,0:T(8,128)(2,1)S(1)}, u32[]{:S(2)}, u32[]{:S(2)}) collective-permute-start(bf16[48,1024]{1,0:T(8,128)(2,1)S(1)} %get-tuple-element.46), channel_id=1, source_target_pairs={{0,1},{1,0},{2,3},{3,2},{4,5},{5,4},{6,7},{7,6},{8,9},{9,8},{10,11... | collective-permute-start | bytes 294920 | tf_op jit(solution)/shard_map/ppermute | solution.py:467
  20.7 17.6 %collective-permute-start.9 = (bf16[2,2,256,128]{3,2,1,0:T(8,128)(2,1)S(1)}, bf16[2,2,256,128]{3,2,1,0:T(8,128)(2,1)S(1)}, u32[]{:S(2)}, u32[]{:S(2)}) collective-permute-start(bf16[2,2,256,128]{3,2,1,0:T(8,128)(2,1)S(1)} %get-tuple-element.47), channel_id=1, source_target_pairs={{0,8},{4,12},{8,0},{12,4},{1,9},{5,13},{9,1},{13,5},{2,10},{6,14},... | collective-permute-start | bytes 786440 | tf_op jit(solution)/shard_map/ppermute | solution.py:467
  21.7 16.6 %collective-permute-start.10 = (bf16[2,2,256,128]{3,2,1,0:T(8,128)(2,1)S(1)}, bf16[2,2,256,128]{3,2,1,0:T(8,128)(2,1)S(1)}, u32[]{:S(2)}, u32[]{:S(2)}) collective-permute-start(bf16[2,2,256,128]{3,2,1,0:T(8,128)(2,1)S(1)} %get-tuple-element.48), channel_id=1, source_target_pairs={{0,12},{4,8},{8,4},{12,0},{1,13},{5,9},{9,5},{13,1},{2,14},{6,10},... | collective-permute-start | bytes 786440 | tf_op jit(solution)/shard_map/ppermute | solution.py:467
  27.3 11.0 %copy-start.1 = (bf16[4096,512]{1,0:T(8,128)(2,1)S(1)}, bf16[4096,512]{1,0:T(8,128)(2,1)}, u32[]{:S(2)}) copy-start(bf16[4096,512]{1,0:T(8,128)(2,1)} %wq.1) | copy-start | bytes 12582916
  27.3 11.0 %copy-start.6 = (f32[4096]{0:T(1024)S(1)}, f32[4096]{0:T(1024)}, u32[]{:S(2)}) copy-start(f32[4096]{0:T(1024)} %param.14) | copy-start | bytes 49156
  27.3 7.6 %collective-permute-start.8 = (bf16[48,1024]{1,0:T(8,128)(2,1)S(1)}, bf16[48,1024]{1,0:T(8,128)(2,1)S(1)}, u32[]{:S(2)}, u32[]{:S(2)}) collective-permute-start(bf16[48,1024]{1,0:T(8,128)(2,1)S(1)} %sum_terms.2.rest_0_.residual), channel_id=1, source_target_pairs={{0,3},{1,2},{2,1},{3,0},{4,7},{5,6},{6,5},{7,4},{8,11},{9,10},{10,... | collective-permute-start | bytes 294920 | tf_op jit(solution)/shard_map/ppermute | solution.py:467
  29.9 8.4 %collective-permute-start.7 = (bf16[48,1024]{1,0:T(8,128)(2,1)S(1)}, bf16[48,1024]{1,0:T(8,128)(2,1)S(1)}, u32[]{:S(2)}, u32[]{:S(2)}) collective-permute-start(bf16[48,1024]{1,0:T(8,128)(2,1)S(1)} %sum_terms.2.rest_0_.residual), channel_id=1, source_target_pairs={{0,2},{1,3},{2,0},{3,1},{4,6},{5,7},{6,4},{7,5},{8,10},{9,11},{10,... | collective-permute-start | bytes 294920 | tf_op jit(solution)/shard_map/ppermute | solution.py:467
  29.9 8.4 %collective-permute-start.6 = (bf16[48,1024]{1,0:T(8,128)(2,1)S(1)}, bf16[48,1024]{1,0:T(8,128)(2,1)S(1)}, u32[]{:S(2)}, u32[]{:S(2)}) collective-permute-start(bf16[48,1024]{1,0:T(8,128)(2,1)S(1)} %sum_terms.2.rest_0_.residual), channel_id=1, source_target_pairs={{0,1},{1,0},{2,3},{3,2},{4,5},{5,4},{6,7},{7,6},{8,9},{9,8},{10,11... | collective-permute-start | bytes 294920 | tf_op jit(solution)/shard_map/ppermute | solution.py:467
  42.9 7.7 %collective-permute-start.11 = (bf16[48,1024]{1,0:T(8,128)(2,1)S(1)}, bf16[48,1024]{1,0:T(8,128)(2,1)S(1)}, u32[]{:S(2)}, u32[]{:S(2)}) collective-permute-start(bf16[48,1024]{1,0:T(8,128)(2,1)S(1)} %get-tuple-element.50), channel_id=1, source_target_pairs={{0,3},{1,2},{2,1},{3,0},{4,7},{5,6},{6,5},{7,4},{8,11},{9,10},{10,... | collective-permute-start | bytes 294920 | tf_op jit(solution)/shard_map/ppermute | solution.py:467
  44.6 8.6 %collective-permute-start.12 = (bf16[48,1024]{1,0:T(8,128)(2,1)S(1)}, bf16[48,1024]{1,0:T(8,128)(2,1)S(1)}, u32[]{:S(2)}, u32[]{:S(2)}) collective-permute-start(bf16[48,1024]{1,0:T(8,128)(2,1)S(1)} %get-tuple-element.51), channel_id=1, source_target_pairs={{0,2},{1,3},{2,0},{3,1},{4,6},{5,7},{6,4},{7,5},{8,10},{9,11},{10,... | collective-permute-start | bytes 294920 | tf_op jit(solution)/shard_map/ppermute | solution.py:467
  44.6 8.6 %collective-permute-start.13 = (bf16[48,1024]{1,0:T(8,128)(2,1)S(1)}, bf16[48,1024]{1,0:T(8,128)(2,1)S(1)}, u32[]{:S(2)}, u32[]{:S(2)}) collective-permute-start(bf16[48,1024]{1,0:T(8,128)(2,1)S(1)} %get-tuple-element.52), channel_id=1, source_target_pairs={{0,1},{1,0},{2,3},{3,2},{4,5},{5,4},{6,7},{7,6},{8,9},{9,8},{10,11... | collective-permute-start | bytes 294920 | tf_op jit(solution)/shard_map/ppermute | solution.py:467
  53.2 8.0 %collective-permute-start.16 = (bf16[48,1024]{1,0:T(8,128)(2,1)S(1)}, bf16[48,1024]{1,0:T(8,128)(2,1)S(1)}, u32[]{:S(2)}, u32[]{:S(2)}) collective-permute-start(bf16[48,1024]{1,0:T(8,128)(2,1)S(1)} %sum_terms.3.rest_0_), channel_id=1, source_target_pairs={{0,3},{1,2},{2,1},{3,0},{4,7},{5,6},{6,5},{7,4},{8,11},{9,10},{10,... | collective-permute-start | bytes 294920 | tf_op jit(solution)/shard_map/ppermute | solution.py:467
  55.5 8.7 %collective-permute-start.15 = (bf16[48,1024]{1,0:T(8,128)(2,1)S(1)}, bf16[48,1024]{1,0:T(8,128)(2,1)S(1)}, u32[]{:S(2)}, u32[]{:S(2)}) collective-permute-start(bf16[48,1024]{1,0:T(8,128)(2,1)S(1)} %sum_terms.3.rest_0_), channel_id=1, source_target_pairs={{0,2},{1,3},{2,0},{3,1},{4,6},{5,7},{6,4},{7,5},{8,10},{9,11},{10,... | collective-permute-start | bytes 294920 | tf_op jit(solution)/shard_map/ppermute | solution.py:467
  55.5 8.7 %collective-permute-start.14 = (bf16[48,1024]{1,0:T(8,128)(2,1)S(1)}, bf16[48,1024]{1,0:T(8,128)(2,1)S(1)}, u32[]{:S(2)}, u32[]{:S(2)}) collective-permute-start(bf16[48,1024]{1,0:T(8,128)(2,1)S(1)} %sum_terms.3.rest_0_), channel_id=1, source_target_pairs={{0,1},{1,0},{2,3},{3,2},{4,5},{5,4},{6,7},{7,6},{8,9},{9,8},{10,11... | collective-permute-start | bytes 294920 | tf_op jit(solution)/shard_map/ppermute | solution.py:467
